TPU v7x, 32 devices: a whole 2x2x4 slice. The times are simulated.
32 devices in a mesh: groups: 2 (over y), latent: 8 (over z, x), layer: 2 (over core).
Axes of the slice: x: 2, y: 2, z: 4, core: 2. Of those that a mesh axis runs over, the one named last changes fastest.
Arguments:
- residual_in: bfloat16 [2, 1024, 2048], P('layer', 'groups', 'latent'), parts along dimension 1, may hold values from -6 to 6
- targets: bfloat16 [2, 1024, 2048], P('layer', 'groups', 'latent'), parts along dimension 1, may hold values from -6 to 6
- enc_weight: bfloat16 [2, 2048, 1024], P('layer', None, 'latent'), may hold values from -0.125 to 0.125
- enc_bias: float32 [2, 1024], P('layer', 'latent'), may hold values from -3 to 3
- dec_same: bfloat16 [2, 1024, 2048], P('layer', 'latent'), may hold values from -0.25 to 0.25
- dec_cross: bfloat16 [1024, 2048], P('latent', 'layer'), may hold values from -0.25 to 0.25
Outputs:
- grad_encoder: float32 [4, 2048, 1024], P(('groups', 'layer'), None, 'latent'), parts along dimension 0
- grad_bias: float32 [4, 1024], P(('groups', 'layer'), 'latent'), parts along dimension 0
- grad_same: float32 [4, 1024, 2048], P(('groups', 'layer'), 'latent'), parts along dimension 0
- grad_cross: float32 [2048, 2048], P(('groups', 'latent'), 'layer'), parts along dimension 0
There are 2 independent parts, one for each index of `groups`. A program takes and returns all parts, laid end to end along the dimension named above; an argument that names none is the same for every part. Nothing has to cross between parts.
All inputs are finite; a program needn't handle non-finite values.
Results may differ from a plain program's by a relative error of at most 0.004.
Values may be sent and summed in bfloat16 or wider, within the bound.
No kernel may reach another device: no remote copies, remote signals or barrier semaphores. Data moves between devices by JAX's collectives and lax.ppermute only.
A program may use at most 64 MiB of HBM per device.

v0:
```python
import math

import jax
import jax.numpy as jnp
from jax import lax
from jax.sharding import PartitionSpec as P


def passed_along(shard, axis, by):
    size = lax.axis_size(axis)
    pairs = [(i, i + by) for i in range(size) if 0 <= i + by < size]
    return lax.ppermute(shard, axis, pairs)


def shards(residual_in, targets, enc_weight, enc_bias, dec_same, dec_cross):
    is_first = lax.axis_index("layer") == 0
    rows_count = residual_in.shape[1]
    err_scale = 1.0 / math.sqrt(rows_count)
    over_rows = (((0,), (0,)), ((), ()))
    over_cols = (((1,), (1,)), ((), ()))
    inputs = lax.all_gather(residual_in[0], "latent", axis=1, tiled=True)
    preact = jnp.dot(inputs, enc_weight[0], preferred_element_type=jnp.float32) + enc_bias[0]
    codes_now = jnp.maximum(preact, 0.0).astype(jnp.bfloat16)
    earlier = passed_along(codes_now, "layer", 1)
    cross_full = lax.all_gather(dec_cross, "layer", axis=1, tiled=True)
    own_dec = dec_same[0]
    full_width = own_dec.shape[1]
    half_width = full_width // 2
    partial_value = jnp.dot(codes_now, own_dec, preferred_element_type=jnp.float32) + jnp.dot(
        earlier, cross_full, preferred_element_type=jnp.float32
    )
    recon_full = lax.psum(partial_value, "latent")
    wanted = lax.all_gather(targets[0], "latent", axis=1, tiled=True)
    errors = ((recon_full - wanted.astype(jnp.float32)) * err_scale).astype(jnp.bfloat16)
    grad_same = lax.dot_general(codes_now, errors, over_rows, preferred_element_type=jnp.float32)
    back_own = lax.dot_general(errors, own_dec, over_cols, preferred_element_type=jnp.float32)
    grad_full = lax.dot_general(earlier, errors, over_rows, preferred_element_type=jnp.float32)
    returned = passed_along(grad_full[:, :half_width], "layer", -1)
    grad_cross = jnp.where(is_first, returned, grad_full[:, half_width:])
    back_cross = lax.dot_general(errors, cross_full, over_cols, preferred_element_type=jnp.float32)
    from_next = passed_along(back_cross, "layer", -1)
    grad_codes = back_own + from_next
    grad_pre = jnp.where(preact > 0, grad_codes, 0.0).astype(jnp.bfloat16)
    grad_enc = lax.dot_general(inputs, grad_pre, over_rows, preferred_element_type=jnp.float32)
    grad_bias = jnp.sum(grad_pre.astype(jnp.float32), axis=0)
    return (grad_enc[None], grad_bias[None], grad_same[None], grad_cross)


def solution(mesh):
    placed = (
        P("layer", "groups", "latent"),
        P("layer", "groups", "latent"),
        P("layer", None, "latent"),
        P("layer", "latent"),
        P("layer", "latent", None),
        P("latent", "layer"),
    )
    return jax.shard_map(
        shards,
        mesh=mesh,
        in_specs=placed,
        out_specs=(
            P(("groups", "layer"), None, "latent"),
            P(("groups", "layer"), "latent"),
            P(("groups", "layer"), "latent", None),
            P(("groups", "latent"), "layer"),
        ),
        check_vma=False,
    )
```

profile of v0, /device:TPU:0, one launch (start us, length us, event | category | flops | bytes accessed | tf_op | source)
XLA Modules:
  0.0 293.8 jit_solution(17187593080569776878)
XLA Ops:
  7.2 0.0 copy-start
  7.2 0.0 all-gather.5.cloned.1.call-start
  7.2 0.7 all-gather.5.cloned.1.call-update
  7.9 0.0 all-gather.7.cloned.1.call-start
  8.0 0.7 all-gather.7.cloned.1.call-update
  8.7 0.0 all-reduce.2.cloned.1.call-start
  8.7 2.5 all_gather.10
  11.2 52.7 %all-gather.5.cloned.1.call-done = bf16[1,512,2048]{2,1,0:T(8,128)(2,1)} async-done(((bf16[1,512,256]{2,1,0:T(8,128)(2,1)}), bf16[1,512,2048]{2,1,0:T(8,128)(2,1)}) %all-gather.5.cloned.1.call-update) | async-done | bytes 2097168 | tf_op jit(solution)/shard_map/all_gather | solution.py:21
  63.9 2.5 maximum_convert_fusion
  66.3 1.3 collective-permute-start
  67.7 0.0 copy-done
  67.7 0.7 fusion.11
  68.4 0.3 collective-permute-done
  68.6 2.7 convolution_add_fusion
  71.3 0.0 all-reduce.2.cloned.1.call-update
  71.3 43.9 %all-gather.7.cloned.1.call-done = bf16[1,512,2048]{2,1,0:T(8,128)(2,1)} async-done(((bf16[1,512,256]{2,1,0:T(8,128)(2,1)}), bf16[1,512,2048]{2,1,0:T(8,128)(2,1)}) %all-gather.7.cloned.1.call-update) | async-done | bytes 2097168 | tf_op jit(solution)/shard_map/all_gather | solution.py:33
  115.2 158.2 %all-reduce.2.cloned.1.call-done = f32[512,2048]{1,0:T(8,128)} async-done(((f32[512,2048]{1,0:T(8,128)}), f32[512,2048]{1,0:T(8,128)}) %all-reduce.2.cloned.1.call-update) | async-done | bytes 4194320 | tf_op jit(solution)/shard_map/psum | solution.py:32
  273.4 3.6 %fusion.1 = bf16[512,2048]{1,0:T(8,128)(2,1)S(1)} fusion(f32[512,2048]{1,0:T(8,128)} %all-reduce.2.cloned.1.call-done, bf16[1,512,2048]{2,1,0:T(8,128)(2,1)} %all-gather.7.cloned.1.call-done), kind=kLoop, calls=%fused_computation.2 | loop fusion | flops 4194304 | bytes 8388608 | tf_op jit(solution)/shard_map/convert_element_type | solution.py:34
  277.0 0.7 fusion.14
  277.7 1.3 collective-permute-start.1
  279.0 0.5 fusion.15
  279.5 0.8 slice.8
  280.3 1.3 collective-permute-start.2
  281.6 1.4 convolution_bitcast_fusion
  283.0 0.0 copy-start.1
  283.0 0.0 collective-permute-done.1
  283.0 1.3 convert_reduce_fusion
  284.3 0.3 copy-done.1
  284.6 0.5 convolution_bitcast_fusion.1
  285.1 1.3 copy.10
  286.4 0.0 collective-permute-done.2
  286.4 0.9 slice_select_fusion
Async XLA Ops:
  7.2 60.5 %copy-start = (bf16[1,128,2048]{2,1,0:T(8,128)(2,1)S(1)}, bf16[1,128,2048]{2,1,0:T(8,128)(2,1)}, u32[]{:S(2)}) copy-start(bf16[1,128,2048]{2,1,0:T(8,128)(2,1)} %param.10) | copy-start | bytes 1572868
  7.2 56.7 %all-gather.5.cloned.1.call-start = ((), (), s32[]{:S(2)}) async-start(), calls=%async_computation.1 | async-start | bytes 2359296 | tf_op jit(solution)/shard_map/all_gather | solution.py:21
  7.9 107.3 %all-gather.7.cloned.1.call-start = ((), (), s32[]{:S(2)}) async-start(), calls=%async_computation.2 | async-start | bytes 2359296 | tf_op jit(solution)/shard_map/all_gather | solution.py:33
  8.7 264.7 %all-reduce.2.cloned.1.call-start = ((), (), s32[]{:S(2)}) async-start(), calls=%async_computation | async-start | bytes 8388608 | tf_op jit(solution)/shard_map/psum | solution.py:32
  66.3 2.3 collective-permute-start
  277.7 5.3 %collective-permute-start.1 = (f32[512,128]{1,0:T(8,128)S(1)}, f32[512,128]{1,0:T(8,128)S(1)}, u32[]{:S(2)}, u32[]{:S(2)}) collective-permute-start(f32[512,128]{1,0:T(8,128)S(1)} %fusion.14), channel_id=1, source_target_pairs={{1,0},{3,2},{5,4},{7,6},{9,8},{11,10},{13,12},{15,14},{17,16},{19,... | collective-permute-start | bytes 786440 | tf_op jit(solution)/shard_map/ppermute | solution.py:12
  280.3 6.1 %collective-permute-start.2 = (f32[128,1024]{1,0:T(8,128)}, f32[128,1024]{1,0:T(8,128)S(1)}, u32[]{:S(2)}, u32[]{:S(2)}) collective-permute-start(f32[128,1024]{1,0:T(8,128)} %slice.8), channel_id=1, source_target_pairs={{1,0},{3,2},{5,4},{7,6},{9,8},{11,10},{13,12},{15,14},{17,16},{19,... | collective-permute-start | bytes 1572872 | tf_op jit(solution)/shard_map/ppermute | solution.py:12
  283.0 1.6 copy-start.1
Sparse Core Ops, SparseCore 0:
  10.1 53.7 all-gather.4
  65.9 49.2 all-gather.6
  118.9 154.4 all-reduce.1
where the time goes:
time: 295 us; the launch traced here: 294 us
  waiting for transfers between devices  256 us (87%)
  between operations  13.8 us (5%)
  matrix products  10.2 us (3%)
  other arithmetic  4.43 us (2%)
  starting transfers between devices  3.98 us (1%)
    psum x1, waiting for transfers between devices, shards(): recon_full = lax.psum(partial_value, 'latent')  158 us
    all_gather x1, waiting for transfers between devices, shards(): inputs = lax.all_gather(residual_in[0], 'latent', axis=1, tiled=True)  52.7 us
    all_gather x1, waiting for transfers between devices, shards(): wanted = lax.all_gather(targets[0], 'latent', axis=1, tiled=True)  43.9 us
  transfers between devices with their start and end apart: 6, of which 4 were waited for; matrix products, arithmetic and copies ran while one was open for 4% of the time, Pallas kernels for 0%

commit v1 on v0

v1 whole, which is shorter than its diff:
```python
import math

import jax
import jax.numpy as jnp
from jax import lax
from jax.sharding import PartitionSpec as P

F32 = jnp.float32
BF16 = jnp.bfloat16
OVER_ROWS = (((0,), (0,)), ((), ()))
OVER_COLS = (((1,), (1,)), ((), ()))
RING_LIMIT = 16


def passed_along(shard, axis, by):
    size = lax.axis_size(axis)
    pairs = [(i, i + by) for i in range(size) if 0 <= i + by < size]
    return lax.ppermute(shard, axis, pairs)


def matmul(a, b, dims=(((1,), (0,)), ((), ()))):
    return lax.dot_general(a, b, dims, preferred_element_type=F32)


def ring_member(place, size):
    place = lax.rem(place + 2 * size, size)
    return jnp.where(place < size // 2, 2 * place, 2 * (size - 1 - place) + 1)


def ring_place(member, size):
    return jnp.where(member % 2 == 0, member // 2, size - 1 - member // 2)


def ring_pairs(size, by):
    order = [2 * p if p < size // 2 else 2 * (size - 1 - p) + 1 for p in range(size)]
    return [(order[p], order[(p + by) % size]) for p in range(size)]


def hop(shard, size, by):
    return lax.ppermute(shard, "latent", ring_pairs(size, by))


def ring_gather(shard, size):
    half = shard.shape[0] // 2
    found = [(0, shard)]
    ahead = behind = shard
    for step in range(1, size // 2):
        ahead, behind = hop(ahead, size, 1), hop(behind, size, -1)
        found += [(-step, ahead), (step, behind)]
    top, bottom = hop(ahead[:half], size, 1), hop(behind[half:], size, -1)
    found.append((size // 2, jnp.concatenate([top, bottom], axis=0)))
    return found


def ring_reduce(partial_of, rows, size):
    half = rows // 2
    far = partial_of(size // 2)
    ahead = hop(far[:half].astype(BF16), size, 1)
    behind = hop(far[half:].astype(BF16), size, -1)
    for step in range(size // 2 - 1, 0, -1):
        plus, minus = partial_of(step), partial_of(-step)
        if step == size // 2 - 1:
            plus = jnp.concatenate([plus[:half] + ahead.astype(F32), plus[half:]], axis=0)
            minus = jnp.concatenate([minus[:half], minus[half:] + behind.astype(F32)], axis=0)
        else:
            plus, minus = plus + ahead.astype(F32), minus + behind.astype(F32)
        ahead, behind = hop(plus.astype(BF16), size, 1), hop(minus.astype(BF16), size, -1)
    return partial_of(0) + (ahead.astype(F32) + behind.astype(F32))


def ring_shards(residual_in, targets, enc_weight, enc_bias, dec_same, dec_cross):
    size = lax.axis_size("latent")
    place = ring_place(lax.axis_index("latent"), size)
    is_first = lax.axis_index("layer") == 0
    rows, wide = residual_in.shape[1:]
    full_width = dec_same.shape[2]
    half_width = full_width // 2
    err_scale = 1.0 / math.sqrt(rows)

    def start_of(offset):
        return ring_member(place + offset, size) * wide

    cross_full = lax.all_gather(dec_cross, "layer", axis=1, tiled=True)
    own_dec = dec_same[0]
    inputs = ring_gather(residual_in[0], size)
    preact = enc_bias
    for offset, shard in inputs:
        preact = preact + matmul(shard, lax.dynamic_slice_in_dim(enc_weight[0], start_of(offset), wide, 0))
    codes_now = jnp.maximum(preact, 0.0).astype(BF16)
    earlier = passed_along(codes_now, "layer", 1)

    def columns(array, offset):
        return lax.dynamic_slice_in_dim(array, start_of(offset), wide, 1)

    def partial_of(offset):
        return matmul(codes_now, columns(own_dec, offset)) + matmul(earlier, columns(cross_full, offset))

    recon = ring_reduce(partial_of, rows, size)
    own_errors = ((recon - targets[0].astype(F32)) * err_scale).astype(BF16)
    found = ring_gather(own_errors, size)
    errors = jnp.zeros((rows, full_width), BF16)
    for offset, shard in found:
        errors = lax.dynamic_update_slice_in_dim(errors, shard, start_of(offset), 1)
    back_cross = matmul(errors, cross_full, OVER_COLS)
    from_next = passed_along(back_cross, "layer", -1)
    grad_full = matmul(earlier, errors, OVER_ROWS)
    returned = passed_along(grad_full[:, :half_width], "layer", -1)
    grad_same = matmul(codes_now, errors, OVER_ROWS)
    grad_cross = jnp.where(is_first, returned, grad_full[:, half_width:])
    grad_codes = matmul(errors, own_dec, OVER_COLS) + from_next
    grad_pre = jnp.where(preact > 0, grad_codes, 0.0).astype(BF16)
    grad_enc = jnp.zeros(enc_weight.shape[1:], F32)
    for offset, shard in inputs:
        grad_enc = lax.dynamic_update_slice_in_dim(grad_enc, matmul(shard, grad_pre, OVER_ROWS), start_of(offset), 0)
    grad_bias = jnp.sum(grad_pre.astype(F32), axis=0)
    return (grad_enc[None], grad_bias[None], grad_same[None], grad_cross)


def wide_shards(residual_in, targets, enc_weight, enc_bias, dec_same, dec_cross):
    is_first = lax.axis_index("layer") == 0
    err_scale = 1.0 / math.sqrt(residual_in.shape[1])
    inputs = lax.all_gather(residual_in[0], "latent", axis=1, tiled=True)
    preact = matmul(inputs, enc_weight[0]) + enc_bias[0]
    codes_now = jnp.maximum(preact, 0.0).astype(BF16)
    earlier = passed_along(codes_now, "layer", 1)
    cross_full = lax.all_gather(dec_cross, "layer", axis=1, tiled=True)
    own_dec = dec_same[0]
    half_width = own_dec.shape[1] // 2
    recon_full = lax.psum(matmul(codes_now, own_dec) + matmul(earlier, cross_full), "latent")
    wanted = lax.all_gather(targets[0], "latent", axis=1, tiled=True)
    errors = ((recon_full - wanted.astype(F32)) * err_scale).astype(BF16)
    grad_same = matmul(codes_now, errors, OVER_ROWS)
    grad_full = matmul(earlier, errors, OVER_ROWS)
    returned = passed_along(grad_full[:, :half_width], "layer", -1)
    grad_cross = jnp.where(is_first, returned, grad_full[:, half_width:])
    from_next = passed_along(matmul(errors, cross_full, OVER_COLS), "layer", -1)
    grad_codes = matmul(errors, own_dec, OVER_COLS) + from_next
    grad_pre = jnp.where(preact > 0, grad_codes, 0.0).astype(BF16)
    grad_enc = matmul(inputs, grad_pre, OVER_ROWS)
    grad_bias = jnp.sum(grad_pre.astype(F32), axis=0)
    return (grad_enc[None], grad_bias[None], grad_same[None], grad_cross)


def solution(mesh):
    size = mesh.shape["latent"]
    placed = (
        P("layer", "groups", "latent"),
        P("layer", "groups", "latent"),
        P("layer", None, "latent"),
        P("layer", "latent"),
        P("layer", "latent", None),
        P("latent", "layer"),
    )
    return jax.shard_map(
        ring_shards if size % 2 == 0 and size <= RING_LIMIT else wide_shards,
        mesh=mesh,
        in_specs=placed,
        out_specs=(
            P(("groups", "layer"), None, "latent"),
            P(("groups", "layer"), "latent"),
            P(("groups", "layer"), "latent", None),
            P(("groups", "latent"), "layer"),
        ),
        check_vma=False,
    )
```

time: 295 us -> 115 us (0.39)
  waiting for transfers between devices: 256 us -> 51.5 us
  starting transfers between devices: 3.98 us -> 30 us
  between operations: 13.8 us -> 1.29 us
  local copies, waits for them, and re-layouts: 2.48 us -> 11.6 us
  matrix products: 10.2 us -> 15.6 us
    psum x1 -> x0, waiting for transfers between devices: 158 us -> none  [shards(): recon_full = lax.psum(partial_value, 'latent')]
    all_gather x2 -> x0, waiting for transfers between devices: 96.6 us -> none  [the longest x1 52.7 us: shards(): inputs = lax.all_gather(residual_in[0], 'latent', axis=1, tiled=True)]
    ppermute x0 -> x24, waiting for transfers between devices: none -> 51.5 us  [hop(): return lax.ppermute(shard, 'latent', ring_pairs(size, by))]
    ppermute x0 -> x24, starting transfers between devices: none -> 26.1 us  [hop(): return lax.ppermute(shard, 'latent', ring_pairs(size, by))]
    dynamic_update_slice x0 -> x13, local copies, waits for them, and re-layouts: none -> 8.61 us  [the longest x7 4.66 us: ring_shards(): lax.dynamic_update_slice_in_dim(grad_enc, matmul(shard, grad_pre, OVER_RO...]
    dot_general x8 -> x36, matrix products: 10.2 us -> 15.6 us  [matmul(): return lax.dot_general(a, b, dims, preferred_element_type=F32)]
    convert_element_type x1 -> x0, other arithmetic: 3.58 us -> none  [shards(): ((recon_full - wanted.astype(jnp.float32)) * err_scale).astype(jnp.bfloat16)]
  transfers between devices with their start and end apart: 6 -> 27, of which waited for: 4 -> 16; matrix products, arithmetic and copies ran while one was open for 4% -> 21% of each run, Pallas kernels for 0% -> 0%
where the time goes in v1:
time: 115 us; the launch traced here: 114 us
  waiting for transfers between devices  51.5 us (45%)
  starting transfers between devices  30 us (26%)
  matrix products  15.6 us (14%)
  local copies, waits for them, and re-layouts  11.6 us (10%)
  blocking collectives  2.38 us (2%)
  other arithmetic  2.02 us (2%)
  between operations  1.29 us (1%)
    ppermute x24, waiting for transfers between devices, hop(): return lax.ppermute(shard, 'latent', ring_pairs(size, by))  51.5 us
    ppermute x24, starting transfers between devices, hop(): return lax.ppermute(shard, 'latent', ring_pairs(size, by))  26.1 us
    dot_general x36, matrix products, matmul(): return lax.dot_general(a, b, dims, preferred_element_type=F32)  15.6 us
    dynamic_update_slice x7, local copies, waits for them, and re-layouts, ring_shards(): lax.dynamic_update_slice_in_dim(grad_enc, matmul(shard, grad_pre, OVER_RO...  4.66 us
    dynamic_update_slice x6, local copies, waits for them, and re-layouts, ring_shards(): errors = lax.dynamic_update_slice_in_dim(errors, shard, start_of(offset), 1)  3.95 us
    ppermute x3, starting transfers between devices, passed_along(): return lax.ppermute(shard, axis, pairs)  3.86 us
    all_gather x1, blocking collectives, ring_shards(): cross_full = lax.all_gather(dec_cross, 'layer', axis=1, tiled=True)  2.38 us
  transfers between devices with their start and end apart: 27, of which 16 were waited for; matrix products, arithmetic and copies ran while one was open for 21% of the time, Pallas kernels for 0%

profile of v1, /device:TPU:0, one launch (start us, length us, event | category | flops | bytes accessed | tf_op | source)
XLA Modules:
  0.0 114.4 jit_solution(9193177946357374619)
XLA Ops:
  0.6 3.0 %collective-permute-start.1 = (bf16[512,256]{1,0:T(8,128)(2,1)}, bf16[512,256]{1,0:T(8,128)(2,1)S(1)}, u32[]{:S(2)}, u32[]{:S(2)}) collective-permute-start(bf16[512,256]{1,0:T(8,128)(2,1)} %bitcast.148), channel_id=1, source_target_pairs={{0,2},{4,0},{8,4},{12,8},{14,12},{10,14},{6,10},{2,6},{1,3},{5,1},... | collective-permute-start | bytes 786440 | tf_op jit(solution)/shard_map/ppermute | solution.py:40
  3.8 2.4 %all_gather.3 = bf16[128,2048]{1,0:T(8,128)(2,1)S(1)} all-gather(bf16[128,1024]{1,0:T(8,128)(2,1)} %param.11), channel_id=1, replica_groups=mesh['groups'=2,'latent'=8,'layer'=2] {'layer'}, dimensions={1}, use_global_device_ids=true | all-gather | bytes 786432 | tf_op jit(solution)/shard_map/all_gather | solution.py:83
  7.4 2.8 %collective-permute-done.1 = bf16[512,256]{1,0:T(8,128)(2,1)S(1)} collective-permute-done((bf16[512,256]{1,0:T(8,128)(2,1)}, bf16[512,256]{1,0:T(8,128)(2,1)S(1)}, u32[]{:S(2)}, u32[]{:S(2)}) %collective-permute-start.1) | collective-permute-done | bytes 262176 | tf_op jit(solution)/shard_map/ppermute | solution.py:40
  10.2 1.7 %collective-permute-start.3 = (bf16[512,256]{1,0:T(8,128)(2,1)S(1)}, bf16[512,256]{1,0:T(8,128)(2,1)S(1)}, u32[]{:S(2)}, u32[]{:S(2)}) collective-permute-start(bf16[512,256]{1,0:T(8,128)(2,1)S(1)} %collective-permute-done.1), channel_id=1, source_target_pairs={{0,2},{4,0},{8,4},{12,8},{14,12},{10,14},{6,10},{2,6},{1,3},{5,1},... | collective-permute-start | bytes 786440 | tf_op jit(solution)/shard_map/ppermute | solution.py:40
  14.4 3.3 %collective-permute-done.3 = bf16[512,256]{1,0:T(8,128)(2,1)S(1)} collective-permute-done((bf16[512,256]{1,0:T(8,128)(2,1)S(1)}, bf16[512,256]{1,0:T(8,128)(2,1)S(1)}, u32[]{:S(2)}, u32[]{:S(2)}) %collective-permute-start.3) | collective-permute-done | bytes 262176 | tf_op jit(solution)/shard_map/ppermute | solution.py:40
  17.7 1.3 %collective-permute-start.5 = (bf16[512,256]{1,0:T(8,128)(2,1)S(1)}, bf16[512,256]{1,0:T(8,128)(2,1)S(1)}, u32[]{:S(2)}, u32[]{:S(2)}) collective-permute-start(bf16[512,256]{1,0:T(8,128)(2,1)S(1)} %collective-permute-done.3), channel_id=1, source_target_pairs={{0,2},{4,0},{8,4},{12,8},{14,12},{10,14},{6,10},{2,6},{1,3},{5,1},... | collective-permute-start | bytes 786440 | tf_op jit(solution)/shard_map/ppermute | solution.py:40
  20.3 5.6 %collective-permute-done.4 = bf16[512,256]{1,0:T(8,128)(2,1)S(1)} collective-permute-done((bf16[512,256]{1,0:T(8,128)(2,1)S(1)}, bf16[512,256]{1,0:T(8,128)(2,1)S(1)}, u32[]{:S(2)}, u32[]{:S(2)}) %collective-permute-start.4) | collective-permute-done | bytes 262176 | tf_op jit(solution)/shard_map/ppermute | solution.py:40
  26.3 1.7 %collective-permute-start.7 = (bf16[256,256]{1,0:T(8,128)(2,1)S(1)}, bf16[256,256]{1,0:T(8,128)(2,1)S(1)}, u32[]{:S(2)}, u32[]{:S(2)}) collective-permute-start(bf16[256,256]{1,0:T(8,128)(2,1)S(1)} %slice.53), channel_id=1, source_target_pairs={{0,2},{4,0},{8,4},{12,8},{14,12},{10,14},{6,10},{2,6},{1,3},{5,1},... | collective-permute-start | bytes 393224 | tf_op jit(solution)/shard_map/ppermute | solution.py:40
  28.3 2.6 %collective-permute-done.6 = bf16[256,256]{1,0:T(8,128)(2,1)S(1)} collective-permute-done((bf16[256,256]{1,0:T(8,128)(2,1)S(1)}, bf16[256,256]{1,0:T(8,128)(2,1)S(1)}, u32[]{:S(2)}, u32[]{:S(2)}) %collective-permute-start.6) | collective-permute-done | bytes 131104 | tf_op jit(solution)/shard_map/ppermute | solution.py:40
  32.6 1.3 %collective-permute-start.8 = (bf16[512,128]{0,1:T(8,128)(2,1)S(1)}, bf16[512,128]{0,1:T(8,128)(2,1)S(1)}, u32[]{:S(2)}, u32[]{:S(2)}) collective-permute-start(bf16[512,128]{0,1:T(8,128)(2,1)S(1)} %get-tuple-element.8), channel_id=1, source_target_pairs={{0,1},{2,3},{4,5},{6,7},{8,9},{10,11},{12,13},{14,15},{16,17},{18,... | collective-permute-start | bytes 393224 | tf_op jit(solution)/shard_map/ppermute | solution.py:18
  35.4 1.8 %collective-permute-start.9 = (bf16[256,256]{1,0:T(8,128)(2,1)S(1)}, bf16[256,256]{1,0:T(8,128)(2,1)S(1)}, u32[]{:S(2)}, u32[]{:S(2)}) collective-permute-start(bf16[256,256]{1,0:T(8,128)(2,1)S(1)} %get-tuple-element.6), channel_id=1, source_target_pairs={{0,4},{4,8},{8,12},{12,14},{14,10},{10,6},{6,2},{2,0},{1,5},{5,9},... | collective-permute-start | bytes 393224 | tf_op jit(solution)/shard_map/ppermute | solution.py:40
  38.1 2.8 %collective-permute-done.9 = bf16[256,256]{1,0:T(8,128)(2,1)S(1)} collective-permute-done((bf16[256,256]{1,0:T(8,128)(2,1)S(1)}, bf16[256,256]{1,0:T(8,128)(2,1)S(1)}, u32[]{:S(2)}, u32[]{:S(2)}) %collective-permute-start.9) | collective-permute-done | bytes 131104 | tf_op jit(solution)/shard_map/ppermute | solution.py:40
  41.0 1.8 %collective-permute-start.10 = (bf16[512,256]{1,0:T(8,128)(2,1)S(1)}, bf16[512,256]{1,0:T(8,128)(2,1)S(1)}, u32[]{:S(2)}, u32[]{:S(2)}) collective-permute-start(bf16[512,256]{1,0:T(8,128)(2,1)S(1)} %pad_maximum_fusion), channel_id=1, source_target_pairs={{0,4},{4,8},{8,12},{12,14},{14,10},{10,6},{6,2},{2,0},{1,5},{5,9},... | collective-permute-start | bytes 786440 | tf_op jit(solution)/shard_map/ppermute | solution.py:40
  43.4 5.0 %collective-permute-done.10 = bf16[512,256]{1,0:T(8,128)(2,1)S(1)} collective-permute-done((bf16[512,256]{1,0:T(8,128)(2,1)S(1)}, bf16[512,256]{1,0:T(8,128)(2,1)S(1)}, u32[]{:S(2)}, u32[]{:S(2)}) %collective-permute-start.10) | collective-permute-done | bytes 262176 | tf_op jit(solution)/shard_map/ppermute | solution.py:40
  48.7 1.8 %collective-permute-start.11 = (bf16[512,256]{1,0:T(8,128)(2,1)S(1)}, bf16[512,256]{1,0:T(8,128)(2,1)S(1)}, u32[]{:S(2)}, u32[]{:S(2)}) collective-permute-start(bf16[512,256]{1,0:T(8,128)(2,1)S(1)} %fusion.9), channel_id=1, source_target_pairs={{0,4},{4,8},{8,12},{12,14},{14,10},{10,6},{6,2},{2,0},{1,5},{5,9},... | collective-permute-start | bytes 786440 | tf_op jit(solution)/shard_map/ppermute | solution.py:40
  51.3 3.9 %collective-permute-done.11 = bf16[512,256]{1,0:T(8,128)(2,1)S(1)} collective-permute-done((bf16[512,256]{1,0:T(8,128)(2,1)S(1)}, bf16[512,256]{1,0:T(8,128)(2,1)S(1)}, u32[]{:S(2)}, u32[]{:S(2)}) %collective-permute-start.11) | collective-permute-done | bytes 262176 | tf_op jit(solution)/shard_map/ppermute | solution.py:40
  55.4 1.8 %collective-permute-start.12 = (bf16[512,256]{1,0:T(8,128)(2,1)S(1)}, bf16[512,256]{1,0:T(8,128)(2,1)S(1)}, u32[]{:S(2)}, u32[]{:S(2)}) collective-permute-start(bf16[512,256]{1,0:T(8,128)(2,1)S(1)} %fusion.10), channel_id=1, source_target_pairs={{0,4},{4,8},{8,12},{12,14},{14,10},{10,6},{6,2},{2,0},{1,5},{5,9},... | collective-permute-start | bytes 786440 | tf_op jit(solution)/shard_map/ppermute | solution.py:40
  58.1 3.8 %collective-permute-done.12 = bf16[512,256]{1,0:T(8,128)(2,1)S(1)} collective-permute-done((bf16[512,256]{1,0:T(8,128)(2,1)S(1)}, bf16[512,256]{1,0:T(8,128)(2,1)S(1)}, u32[]{:S(2)}, u32[]{:S(2)}) %collective-permute-start.12) | collective-permute-done | bytes 262176 | tf_op jit(solution)/shard_map/ppermute | solution.py:40
  61.9 2.1 %collective-permute-done.16 = bf16[512,256]{1,0:T(8,128)(2,1)S(1)} collective-permute-done((bf16[512,256]{1,0:T(8,128)(2,1)S(1)}, bf16[512,256]{1,0:T(8,128)(2,1)S(1)}, u32[]{:S(2)}, u32[]{:S(2)}) %collective-permute-start.16) | collective-permute-done | bytes 262176 | tf_op jit(solution)/shard_map/ppermute | solution.py:40
  64.5 1.6 %collective-permute-start.17 = (bf16[512,256]{1,0:T(8,128)(2,1)S(1)}, bf16[512,256]{1,0:T(8,128)(2,1)}, u32[]{:S(2)}, u32[]{:S(2)}) collective-permute-start(bf16[512,256]{1,0:T(8,128)(2,1)S(1)} %get-tuple-element.11), channel_id=1, source_target_pairs={{0,4},{4,8},{8,12},{12,14},{14,10},{10,6},{6,2},{2,0},{1,5},{5,9},... | collective-permute-start | bytes 786440 | tf_op jit(solution)/shard_map/ppermute | solution.py:40
  66.6 6.5 %collective-permute-done.17 = bf16[512,256]{1,0:T(8,128)(2,1)} collective-permute-done((bf16[512,256]{1,0:T(8,128)(2,1)S(1)}, bf16[512,256]{1,0:T(8,128)(2,1)}, u32[]{:S(2)}, u32[]{:S(2)}) %collective-permute-start.17) | collective-permute-done | bytes 262176 | tf_op jit(solution)/shard_map/ppermute | solution.py:40
  73.1 1.6 %collective-permute-start.19 = (bf16[512,256]{1,0:T(8,128)(2,1)}, bf16[512,256]{1,0:T(8,128)(2,1)}, u32[]{:S(2)}, u32[]{:S(2)}) collective-permute-start(bf16[512,256]{1,0:T(8,128)(2,1)} %collective-permute-done.17), channel_id=1, source_target_pairs={{0,4},{4,8},{8,12},{12,14},{14,10},{10,6},{6,2},{2,0},{1,5},{5,9},... | collective-permute-start | bytes 786440 | tf_op jit(solution)/shard_map/ppermute | solution.py:40
  76.4 6.0 %collective-permute-done.19 = bf16[512,256]{1,0:T(8,128)(2,1)} collective-permute-done((bf16[512,256]{1,0:T(8,128)(2,1)}, bf16[512,256]{1,0:T(8,128)(2,1)}, u32[]{:S(2)}, u32[]{:S(2)}) %collective-permute-start.19) | collective-permute-done | bytes 262176 | tf_op jit(solution)/shard_map/ppermute | solution.py:40
  82.5 1.6 %collective-permute-start.21 = (bf16[512,256]{1,0:T(8,128)(2,1)}, bf16[512,256]{1,0:T(8,128)(2,1)S(1)}, u32[]{:S(2)}, u32[]{:S(2)}) collective-permute-start(bf16[512,256]{1,0:T(8,128)(2,1)} %collective-permute-done.19), channel_id=1, source_target_pairs={{0,4},{4,8},{8,12},{12,14},{14,10},{10,6},{6,2},{2,0},{1,5},{5,9},... | collective-permute-start | bytes 786440 | tf_op jit(solution)/shard_map/ppermute | solution.py:40
  87.5 1.9 %collective-permute-done.21 = bf16[512,256]{1,0:T(8,128)(2,1)S(1)} collective-permute-done((bf16[512,256]{1,0:T(8,128)(2,1)}, bf16[512,256]{1,0:T(8,128)(2,1)S(1)}, u32[]{:S(2)}, u32[]{:S(2)}) %collective-permute-start.21) | collective-permute-done | bytes 262176 | tf_op jit(solution)/shard_map/ppermute | solution.py:40
  89.4 1.6 %collective-permute-start.23 = (bf16[256,256]{1,0:T(8,128)(2,1)S(1)}, bf16[256,256]{1,0:T(8,128)(2,1)S(1)}, u32[]{:S(2)}, u32[]{:S(2)}) collective-permute-start(bf16[256,256]{1,0:T(8,128)(2,1)S(1)} %slice.60), channel_id=1, source_target_pairs={{0,4},{4,8},{8,12},{12,14},{14,10},{10,6},{6,2},{2,0},{1,5},{5,9},... | collective-permute-start | bytes 393224 | tf_op jit(solution)/shard_map/ppermute | solution.py:40
  91.6 2.8 %collective-permute-done.23 = bf16[256,256]{1,0:T(8,128)(2,1)S(1)} collective-permute-done((bf16[256,256]{1,0:T(8,128)(2,1)S(1)}, bf16[256,256]{1,0:T(8,128)(2,1)S(1)}, u32[]{:S(2)}, u32[]{:S(2)}) %collective-permute-start.23) | collective-permute-done | bytes 131104 | tf_op jit(solution)/shard_map/ppermute | solution.py:40
  94.4 1.6 %collective-permute-done.24 = bf16[256,256]{1,0:T(8,128)(2,1)S(1)} collective-permute-done((bf16[256,256]{1,0:T(8,128)(2,1)S(1)}, bf16[256,256]{1,0:T(8,128)(2,1)S(1)}, u32[]{:S(2)}, u32[]{:S(2)}) %collective-permute-start.24) | collective-permute-done | bytes 131104 | tf_op jit(solution)/shard_map/ppermute | solution.py:40
  96.9 1.3 %collective-permute-start.25 = (f32[512,128]{0,1:T(8,128)S(1)}, f32[512,128]{0,1:T(8,128)S(1)}, u32[]{:S(2)}, u32[]{:S(2)}) collective-permute-start(f32[512,128]{0,1:T(8,128)S(1)} %fusion.101), channel_id=1, source_target_pairs={{1,0},{3,2},{5,4},{7,6},{9,8},{11,10},{13,12},{15,14},{17,16},{19,... | collective-permute-start | bytes 786440 | tf_op jit(solution)/shard_map/ppermute | solution.py:18
  100.8 1.4 %convolution_bitcast_fusion = f32[1,128,2048]{2,1,0:T(8,128)} fusion(bf16[512,128]{0,1:T(8,128)(2,1)S(1)} %get-tuple-element.8, bf16[512,2048]{1,0:T(8,128)(2,1)S(1)} %maximum_dynamic-update-slice_fusion), kind=kOutput, calls=%fused_computation | convolution fusion | flops 268435456 | bytes 3276800 | tf_op jit(solution)/shard_map/dot_general | solution.py:22
  102.3 1.4 %convert_reduce_fusion = (f32[128]{0:T(128)}, bf16[512,128]{0,1:T(8,128)(2,1)S(1)}) fusion(f32[512,128]{0,1:T(8,128)S(1)} %copy-done.3, f32[512,128]{0,1:T(8,128)S(1)} %collective-permute-done.25, bf16[512,2048]{1,0:T(8,128)(2,1)S(1)} %maximum_dynamic-update-slice_fusion, bf16[1,128,2048]{2,1,0:T(8,128)(2,1)S(1)} %copy-done), kind=kOutput, calls=%fused_computation.52 | convolution fusion | flops 268828544 | bytes 3277312 | tf_op jit(solution)/shard_map/dot_general | solution.py:22
  112.5 1.9 %slice_select_fusion = f32[128,1024]{1,0:T(8,128)} fusion(f32[128,1024]{1,0:T(8,128)} %collective-permute-done.26, f32[128,2048]{1,0:T(8,128)S(1)} %copy-done.2, pred[]{:T(512)S(6)} %eq.9), kind=kLoop, calls=%fused_computation.41 | loop fusion | flops 131072 | bytes 1572865 | tf_op jit(solution)/shard_map/jit(_where)/select_n | solution.py:109
  (139 shorter events, 31.4 us)
Async XLA Ops:
  0.6 33.2 %copy-start = (bf16[1,128,2048]{2,1,0:T(8,128)(2,1)S(1)}, bf16[1,128,2048]{2,1,0:T(8,128)(2,1)}, u32[]{:S(2)}) copy-start(bf16[1,128,2048]{2,1,0:T(8,128)(2,1)} %param.10) | copy-start | bytes 1572868
  0.6 9.6 %collective-permute-start.1 = (bf16[512,256]{1,0:T(8,128)(2,1)}, bf16[512,256]{1,0:T(8,128)(2,1)S(1)}, u32[]{:S(2)}, u32[]{:S(2)}) collective-permute-start(bf16[512,256]{1,0:T(8,128)(2,1)} %bitcast.148), channel_id=1, source_target_pairs={{0,2},{4,0},{8,4},{12,8},{14,12},{10,14},{6,10},{2,6},{1,3},{5,1},... | collective-permute-start | bytes 786440 | tf_op jit(solution)/shard_map/ppermute | solution.py:40
  3.6 8.3 %collective-permute-start = (bf16[512,256]{1,0:T(8,128)(2,1)}, bf16[512,256]{1,0:T(8,128)(2,1)S(1)}, u32[]{:S(2)}, u32[]{:S(2)}) collective-permute-start(bf16[512,256]{1,0:T(8,128)(2,1)} %bitcast.149), channel_id=1, source_target_pairs={{0,4},{4,8},{8,12},{12,14},{14,10},{10,6},{6,2},{2,0},{1,5},{5,9},... | collective-permute-start | bytes 786440 | tf_op jit(solution)/shard_map/ppermute | solution.py:40
  6.2 13.7 %copy-start.19 = (bf16[1,2048,128]{2,1,0:T(8,128)(2,1)S(1)}, bf16[1,2048,128]{2,1,0:T(8,128)(2,1)}, u32[]{:S(2)}) copy-start(bf16[1,2048,128]{2,1,0:T(8,128)(2,1)} %param.8) | copy-start | bytes 1572868
  10.2 7.5 %collective-permute-start.3 = (bf16[512,256]{1,0:T(8,128)(2,1)S(1)}, bf16[512,256]{1,0:T(8,128)(2,1)S(1)}, u32[]{:S(2)}, u32[]{:S(2)}) collective-permute-start(bf16[512,256]{1,0:T(8,128)(2,1)S(1)} %collective-permute-done.1), channel_id=1, source_target_pairs={{0,2},{4,0},{8,4},{12,8},{14,12},{10,14},{6,10},{2,6},{1,3},{5,1},... | collective-permute-start | bytes 786440 | tf_op jit(solution)/shard_map/ppermute | solution.py:40
  11.9 7.2 %collective-permute-start.2 = (bf16[512,256]{1,0:T(8,128)(2,1)S(1)}, bf16[512,256]{1,0:T(8,128)(2,1)S(1)}, u32[]{:S(2)}, u32[]{:S(2)}) collective-permute-start(bf16[512,256]{1,0:T(8,128)(2,1)S(1)} %collective-permute-done), channel_id=1, source_target_pairs={{0,4},{4,8},{8,12},{12,14},{14,10},{10,6},{6,2},{2,0},{1,5},{5,9},... | collective-permute-start | bytes 786440 | tf_op jit(solution)/shard_map/ppermute | solution.py:40
  17.7 14.8 %copy-start.13 = (bf16[512,256]{1,0:T(8,128)(2,1)}, bf16[512,256]{1,0:T(8,128)(2,1)S(1)}, u32[]{:S(2)}) copy-start(bf16[512,256]{1,0:T(8,128)(2,1)S(1)} %collective-permute-done.3) | copy-start | bytes 786436
  17.7 8.6 %collective-permute-start.5 = (bf16[512,256]{1,0:T(8,128)(2,1)S(1)}, bf16[512,256]{1,0:T(8,128)(2,1)S(1)}, u32[]{:S(2)}, u32[]{:S(2)}) collective-permute-start(bf16[512,256]{1,0:T(8,128)(2,1)S(1)} %collective-permute-done.3), channel_id=1, source_target_pairs={{0,2},{4,0},{8,4},{12,8},{14,12},{10,14},{6,10},{2,6},{1,3},{5,1},... | collective-permute-start | bytes 786440 | tf_op jit(solution)/shard_map/ppermute | solution.py:40
  19.1 13.5 %copy-start.17 = (bf16[512,256]{1,0:T(8,128)(2,1)}, bf16[512,256]{1,0:T(8,128)(2,1)S(1)}, u32[]{:S(2)}) copy-start(bf16[512,256]{1,0:T(8,128)(2,1)S(1)} %collective-permute-done.2) | copy-start | bytes 786436
  19.1 6.8 %collective-permute-start.4 = (bf16[512,256]{1,0:T(8,128)(2,1)S(1)}, bf16[512,256]{1,0:T(8,128)(2,1)S(1)}, u32[]{:S(2)}, u32[]{:S(2)}) collective-permute-start(bf16[512,256]{1,0:T(8,128)(2,1)S(1)} %collective-permute-done.2), channel_id=1, source_target_pairs={{0,4},{4,8},{8,12},{12,14},{14,10},{10,6},{6,2},{2,0},{1,5},{5,9},... | collective-permute-start | bytes 786440 | tf_op jit(solution)/shard_map/ppermute | solution.py:40
  25.9 5.0 %collective-permute-start.6 = (bf16[256,256]{1,0:T(8,128)(2,1)S(1)}, bf16[256,256]{1,0:T(8,128)(2,1)S(1)}, u32[]{:S(2)}, u32[]{:S(2)}) collective-permute-start(bf16[256,256]{1,0:T(8,128)(2,1)S(1)} %slice.52), channel_id=1, source_target_pairs={{0,4},{4,8},{8,12},{12,14},{14,10},{10,6},{6,2},{2,0},{1,5},{5,9},... | collective-permute-start | bytes 393224 | tf_op jit(solution)/shard_map/ppermute | solution.py:40
  26.3 5.0 %collective-permute-start.7 = (bf16[256,256]{1,0:T(8,128)(2,1)S(1)}, bf16[256,256]{1,0:T(8,128)(2,1)S(1)}, u32[]{:S(2)}, u32[]{:S(2)}) collective-permute-start(bf16[256,256]{1,0:T(8,128)(2,1)S(1)} %slice.53), channel_id=1, source_target_pairs={{0,2},{4,0},{8,4},{12,8},{14,12},{10,14},{6,10},{2,6},{1,3},{5,1},... | collective-permute-start | bytes 393224 | tf_op jit(solution)/shard_map/ppermute | solution.py:40
  32.6 2.6 %collective-permute-start.8 = (bf16[512,128]{0,1:T(8,128)(2,1)S(1)}, bf16[512,128]{0,1:T(8,128)(2,1)S(1)}, u32[]{:S(2)}, u32[]{:S(2)}) collective-permute-start(bf16[512,128]{0,1:T(8,128)(2,1)S(1)} %get-tuple-element.8), channel_id=1, source_target_pairs={{0,1},{2,3},{4,5},{6,7},{8,9},{10,11},{12,13},{14,15},{16,17},{18,... | collective-permute-start | bytes 393224 | tf_op jit(solution)/shard_map/ppermute | solution.py:18
  35.4 5.5 %collective-permute-start.9 = (bf16[256,256]{1,0:T(8,128)(2,1)S(1)}, bf16[256,256]{1,0:T(8,128)(2,1)S(1)}, u32[]{:S(2)}, u32[]{:S(2)}) collective-permute-start(bf16[256,256]{1,0:T(8,128)(2,1)S(1)} %get-tuple-element.6), channel_id=1, source_target_pairs={{0,4},{4,8},{8,12},{12,14},{14,10},{10,6},{6,2},{2,0},{1,5},{5,9},... | collective-permute-start | bytes 393224 | tf_op jit(solution)/shard_map/ppermute | solution.py:40
  37.5 5.3 %collective-permute-start.13 = (bf16[256,256]{1,0:T(8,128)(2,1)S(1)}, bf16[256,256]{1,0:T(8,128)(2,1)S(1)}, u32[]{:S(2)}, u32[]{:S(2)}) collective-permute-start(bf16[256,256]{1,0:T(8,128)(2,1)S(1)} %get-tuple-element.7), channel_id=1, source_target_pairs={{0,2},{4,0},{8,4},{12,8},{14,12},{10,14},{6,10},{2,6},{1,3},{5,1},... | collective-permute-start | bytes 393224 | tf_op jit(solution)/shard_map/ppermute | solution.py:40
  41.0 7.4 %collective-permute-start.10 = (bf16[512,256]{1,0:T(8,128)(2,1)S(1)}, bf16[512,256]{1,0:T(8,128)(2,1)S(1)}, u32[]{:S(2)}, u32[]{:S(2)}) collective-permute-start(bf16[512,256]{1,0:T(8,128)(2,1)S(1)} %pad_maximum_fusion), channel_id=1, source_target_pairs={{0,4},{4,8},{8,12},{12,14},{14,10},{10,6},{6,2},{2,0},{1,5},{5,9},... | collective-permute-start | bytes 786440 | tf_op jit(solution)/shard_map/ppermute | solution.py:40
  42.8 7.6 %collective-permute-start.14 = (bf16[512,256]{1,0:T(8,128)(2,1)S(1)}, bf16[512,256]{1,0:T(8,128)(2,1)S(1)}, u32[]{:S(2)}, u32[]{:S(2)}) collective-permute-start(bf16[512,256]{1,0:T(8,128)(2,1)S(1)} %pad_maximum_fusion.1), channel_id=1, source_target_pairs={{0,2},{4,0},{8,4},{12,8},{14,12},{10,14},{6,10},{2,6},{1,3},{5,1},... | collective-permute-start | bytes 786440 | tf_op jit(solution)/shard_map/ppermute | solution.py:40
  48.7 6.5 %collective-permute-start.11 = (bf16[512,256]{1,0:T(8,128)(2,1)S(1)}, bf16[512,256]{1,0:T(8,128)(2,1)S(1)}, u32[]{:S(2)}, u32[]{:S(2)}) collective-permute-start(bf16[512,256]{1,0:T(8,128)(2,1)S(1)} %fusion.9), channel_id=1, source_target_pairs={{0,4},{4,8},{8,12},{12,14},{14,10},{10,6},{6,2},{2,0},{1,5},{5,9},... | collective-permute-start | bytes 786440 | tf_op jit(solution)/shard_map/ppermute | solution.py:40
  50.7 6.5 %collective-permute-start.15 = (bf16[512,256]{1,0:T(8,128)(2,1)S(1)}, bf16[512,256]{1,0:T(8,128)(2,1)S(1)}, u32[]{:S(2)}, u32[]{:S(2)}) collective-permute-start(bf16[512,256]{1,0:T(8,128)(2,1)S(1)} %fusion.7), channel_id=1, source_target_pairs={{0,2},{4,0},{8,4},{12,8},{14,12},{10,14},{6,10},{2,6},{1,3},{5,1},... | collective-permute-start | bytes 786440 | tf_op jit(solution)/shard_map/ppermute | solution.py:40
  55.4 8.8 %copy-start.20 = (bf16[1,512,256]{2,1,0:T(8,128)(2,1)S(1)}, bf16[1,512,256]{2,1,0:T(8,128)(2,1)}, u32[]{:S(2)}) copy-start(bf16[1,512,256]{2,1,0:T(8,128)(2,1)} %param.7) | copy-start | bytes 786436
  55.4 6.4 %collective-permute-start.12 = (bf16[512,256]{1,0:T(8,128)(2,1)S(1)}, bf16[512,256]{1,0:T(8,128)(2,1)S(1)}, u32[]{:S(2)}, u32[]{:S(2)}) collective-permute-start(bf16[512,256]{1,0:T(8,128)(2,1)S(1)} %fusion.10), channel_id=1, source_target_pairs={{0,4},{4,8},{8,12},{12,14},{14,10},{10,6},{6,2},{2,0},{1,5},{5,9},... | collective-permute-start | bytes 786440 | tf_op jit(solution)/shard_map/ppermute | solution.py:40
  57.5 6.4 %collective-permute-start.16 = (bf16[512,256]{1,0:T(8,128)(2,1)S(1)}, bf16[512,256]{1,0:T(8,128)(2,1)S(1)}, u32[]{:S(2)}, u32[]{:S(2)}) collective-permute-start(bf16[512,256]{1,0:T(8,128)(2,1)S(1)} %fusion.8), channel_id=1, source_target_pairs={{0,2},{4,0},{8,4},{12,8},{14,12},{10,14},{6,10},{2,6},{1,3},{5,1},... | collective-permute-start | bytes 786440 | tf_op jit(solution)/shard_map/ppermute | solution.py:40
  64.5 8.6 %collective-permute-start.17 = (bf16[512,256]{1,0:T(8,128)(2,1)S(1)}, bf16[512,256]{1,0:T(8,128)(2,1)}, u32[]{:S(2)}, u32[]{:S(2)}) collective-permute-start(bf16[512,256]{1,0:T(8,128)(2,1)S(1)} %get-tuple-element.11), channel_id=1, source_target_pairs={{0,4},{4,8},{8,12},{12,14},{14,10},{10,6},{6,2},{2,0},{1,5},{5,9},... | collective-permute-start | bytes 786440 | tf_op jit(solution)/shard_map/ppermute | solution.py:40
  66.1 8.9 %collective-permute-start.18 = (bf16[512,256]{1,0:T(8,128)(2,1)S(1)}, bf16[512,256]{1,0:T(8,128)(2,1)}, u32[]{:S(2)}, u32[]{:S(2)}) collective-permute-start(bf16[512,256]{1,0:T(8,128)(2,1)S(1)} %get-tuple-element.11), channel_id=1, source_target_pairs={{0,2},{4,0},{8,4},{12,8},{14,12},{10,14},{6,10},{2,6},{1,3},{5,1},... | collective-permute-start | bytes 786440 | tf_op jit(solution)/shard_map/ppermute | solution.py:40
  73.1 9.4 %collective-permute-start.19 = (bf16[512,256]{1,0:T(8,128)(2,1)}, bf16[512,256]{1,0:T(8,128)(2,1)}, u32[]{:S(2)}, u32[]{:S(2)}) collective-permute-start(bf16[512,256]{1,0:T(8,128)(2,1)} %collective-permute-done.17), channel_id=1, source_target_pairs={{0,4},{4,8},{8,12},{12,14},{14,10},{10,6},{6,2},{2,0},{1,5},{5,9},... | collective-permute-start | bytes 786440 | tf_op jit(solution)/shard_map/ppermute | solution.py:40
  75.0 9.0 %collective-permute-start.20 = (bf16[512,256]{1,0:T(8,128)(2,1)}, bf16[512,256]{1,0:T(8,128)(2,1)}, u32[]{:S(2)}, u32[]{:S(2)}) collective-permute-start(bf16[512,256]{1,0:T(8,128)(2,1)} %collective-permute-done.18), channel_id=1, source_target_pairs={{0,2},{4,0},{8,4},{12,8},{14,12},{10,14},{6,10},{2,6},{1,3},{5,1},... | collective-permute-start | bytes 786440 | tf_op jit(solution)/shard_map/ppermute | solution.py:40
  82.5 6.9 %collective-permute-start.21 = (bf16[512,256]{1,0:T(8,128)(2,1)}, bf16[512,256]{1,0:T(8,128)(2,1)S(1)}, u32[]{:S(2)}, u32[]{:S(2)}) collective-permute-start(bf16[512,256]{1,0:T(8,128)(2,1)} %collective-permute-done.19), channel_id=1, source_target_pairs={{0,4},{4,8},{8,12},{12,14},{14,10},{10,6},{6,2},{2,0},{1,5},{5,9},... | collective-permute-start | bytes 786440 | tf_op jit(solution)/shard_map/ppermute | solution.py:40
  84.1 6.9 %collective-permute-start.22 = (bf16[512,256]{1,0:T(8,128)(2,1)}, bf16[512,256]{1,0:T(8,128)(2,1)S(1)}, u32[]{:S(2)}, u32[]{:S(2)}) collective-permute-start(bf16[512,256]{1,0:T(8,128)(2,1)} %collective-permute-done.20), channel_id=1, source_target_pairs={{0,2},{4,0},{8,4},{12,8},{14,12},{10,14},{6,10},{2,6},{1,3},{5,1},... | collective-permute-start | bytes 786440 | tf_op jit(solution)/shard_map/ppermute | solution.py:40
  89.4 5.0 %collective-permute-start.23 = (bf16[256,256]{1,0:T(8,128)(2,1)S(1)}, bf16[256,256]{1,0:T(8,128)(2,1)S(1)}, u32[]{:S(2)}, u32[]{:S(2)}) collective-permute-start(bf16[256,256]{1,0:T(8,128)(2,1)S(1)} %slice.60), channel_id=1, source_target_pairs={{0,4},{4,8},{8,12},{12,14},{14,10},{10,6},{6,2},{2,0},{1,5},{5,9},... | collective-permute-start | bytes 393224 | tf_op jit(solution)/shard_map/ppermute | solution.py:40
  91.0 5.0 %collective-permute-start.24 = (bf16[256,256]{1,0:T(8,128)(2,1)S(1)}, bf16[256,256]{1,0:T(8,128)(2,1)S(1)}, u32[]{:S(2)}, u32[]{:S(2)}) collective-permute-start(bf16[256,256]{1,0:T(8,128)(2,1)S(1)} %slice.61), channel_id=1, source_target_pairs={{0,2},{4,0},{8,4},{12,8},{14,12},{10,14},{6,10},{2,6},{1,3},{5,1},... | collective-permute-start | bytes 393224 | tf_op jit(solution)/shard_map/ppermute | solution.py:40
  96.9 5.3 %collective-permute-start.25 = (f32[512,128]{0,1:T(8,128)S(1)}, f32[512,128]{0,1:T(8,128)S(1)}, u32[]{:S(2)}, u32[]{:S(2)}) collective-permute-start(f32[512,128]{0,1:T(8,128)S(1)} %fusion.101), channel_id=1, source_target_pairs={{1,0},{3,2},{5,4},{7,6},{9,8},{11,10},{13,12},{15,14},{17,16},{19,... | collective-permute-start | bytes 786440 | tf_op jit(solution)/shard_map/ppermute | solution.py:18
  99.5 13.0 %collective-permute-start.26 = (f32[128,1024]{1,0:T(8,128)}, f32[128,1024]{1,0:T(8,128)}, u32[]{:S(2)}, u32[]{:S(2)}) collective-permute-start(f32[128,1024]{1,0:T(8,128)} %slice.62), channel_id=1, source_target_pairs={{1,0},{3,2},{5,4},{7,6},{9,8},{11,10},{13,12},{15,14},{17,16},{19,... | collective-permute-start | bytes 1572872 | tf_op jit(solution)/shard_map/ppermute | solution.py:18
  (16 other events, 59.9 us)

commit v2 on v1

v2 whole, which is shorter than its diff:
```python
import functools
import math

import jax
import jax.numpy as jnp
from jax import lax
from jax.experimental import pallas as pl
from jax.experimental.pallas import tpu as pltpu
from jax.sharding import PartitionSpec as P

F32 = jnp.float32
BF16 = jnp.bfloat16
OVER_ROWS = (((0,), (0,)), ((), ()))
OVER_COLS = (((1,), (1,)), ((), ()))
RING_LIMIT = 16
VMEM_BYTES = 24 * 1024 * 1024
ENC_PIECES = 4


def passed_along(shard, axis, by):
    size = lax.axis_size(axis)
    pairs = [(i, i + by) for i in range(size) if 0 <= i + by < size]
    return lax.ppermute(shard, axis, pairs)


def matmul(a, b, dims=(((1,), (0,)), ((), ()))):
    return lax.dot_general(a, b, dims, preferred_element_type=F32)


def ring_member(place, size):
    place = lax.rem(place + 2 * size, size)
    return jnp.where(place < size // 2, 2 * place, 2 * (size - 1 - place) + 1)


def ring_place(member, size):
    return jnp.where(member % 2 == 0, member // 2, size - 1 - member // 2)


def ring_pairs(size, by):
    order = [2 * p if p < size // 2 else 2 * (size - 1 - p) + 1 for p in range(size)]
    return [(order[p], order[(p + by) % size]) for p in range(size)]


def hop(shard, size, by):
    return lax.ppermute(shard, "latent", ring_pairs(size, by))


def ring_gather(parts, size):
    found = [[(0, part)] for part in parts]
    ahead, behind = list(parts), list(parts)
    for step in range(1, size // 2):
        for chain in range(2):
            ahead[chain] = hop(ahead[chain], size, 1)
            behind[chain] = hop(behind[chain], size, -1)
            found[chain] += [(-step, ahead[chain]), (step, behind[chain])]
    found[0].append((size // 2, hop(ahead[0], size, 1)))
    found[1].append((size // 2, hop(behind[1], size, -1)))
    return found


def ring_reduce(partial_of, size):
    far = [partial_of(chain, size // 2).astype(BF16) for chain in range(2)]
    ahead = [hop(far[0], size, 1), None]
    behind = [None, hop(far[1], size, -1)]
    for step in range(size // 2 - 1, 0, -1):
        for chain in range(2):
            plus, minus = partial_of(chain, step), partial_of(chain, -step)
            if ahead[chain] is not None:
                plus = plus + ahead[chain].astype(F32)
            if behind[chain] is not None:
                minus = minus + behind[chain].astype(F32)
            ahead[chain] = hop(plus.astype(BF16), size, 1)
            behind[chain] = hop(minus.astype(BF16), size, -1)
    totals = []
    for chain in range(2):
        total = partial_of(chain, 0)
        for arrived in (ahead[chain], behind[chain]):
            if arrived is not None:
                total = total + arrived.astype(F32)
        totals.append(total)
    return totals


def call(kernel, outs, flops, operands, grid=(), out_specs=None, scratch=(), in_vmem=None):
    whole = pl.BlockSpec(memory_space=pltpu.VMEM)
    return pl.pallas_call(
        kernel,
        out_shape=outs,
        grid=grid,
        in_specs=[pl.BlockSpec(memory_space=pltpu.SMEM)] + [whole] * (len(operands) - 1),
        out_specs=out_specs if out_specs is not None else [whole] * len(outs),
        scratch_shapes=list(scratch),
        compiler_params=pltpu.CompilerParams(vmem_limit_bytes=VMEM_BYTES),
        cost_estimate=pl.CostEstimate(flops=flops, bytes_accessed=1 << 20, transcendentals=0),
    )(*operands)


def encode_kernel(starts, *refs):
    *shards, weight, bias, preact, codes = refs
    wide = shards[0].shape[1]
    total = jnp.broadcast_to(bias[...], preact.shape)
    for k, shard in enumerate(shards):
        block = weight[0, pl.ds(pl.multiple_of(starts[k], wide), wide), :]
        total = total + jnp.dot(shard[...], block, preferred_element_type=F32)
    preact[...] = total
    codes[...] = jnp.maximum(total, 0.0).astype(BF16)


def turn_kernel(starts, *refs):
    *shards, turned = refs
    rows, wide = shards[0].shape
    for k in range(len(shards) // 2):
        at = pl.ds(pl.multiple_of(starts[k], wide), wide)
        for chain in range(2):
            turned[at, chain * rows:(chain + 1) * rows] = shards[2 * k + chain][...].T


def back_kernel(starts, *refs):
    *shards, own_dec, cross, back_own, back_cross = refs
    wide = shards[0].shape[1]
    for source, target in ((cross, back_cross), (own_dec, back_own)):
        total = None
        for k, shard in enumerate(shards):
            block = source[:, pl.ds(pl.multiple_of(starts[k], wide), wide)]
            term = lax.dot_general(shard[...], block, OVER_COLS, preferred_element_type=F32)
            total = term if total is None else total + term
        target[...] = total


def outer_kernel(starts, *refs):
    *shards, codes_0, codes_1, earlier_0, earlier_1, same, low, high, errors, turned, turned_earlier = refs
    rows, wide = shards[0].shape
    size = len(shards) // 2

    for chain, (codes, earlier) in enumerate(((codes_0, earlier_0), (codes_1, earlier_1))):
        turned[:, chain * rows:(chain + 1) * rows] = codes[...].T
        turned_earlier[:, chain * rows:(chain + 1) * rows] = earlier[...].T
    for k in range(size):
        at = pl.ds(pl.multiple_of(starts[k], wide), wide)
        for chain in range(2):
            errors[chain * rows:(chain + 1) * rows, at] = shards[2 * k + chain][...]
    half = size // 2
    for k in range(size):
        block = errors[:, k * wide:(k + 1) * wide]
        target = low if k < half else high
        at = (k % half) * wide
        target[:, at:at + wide] = jnp.dot(turned_earlier[...], block, preferred_element_type=F32)
        same[0, :, k * wide:(k + 1) * wide] = jnp.dot(turned[...], block, preferred_element_type=F32)


def enc_kernel(first, turned, pre_0, pre_1, own_0, own_1, next_0, next_1, grad, bias, grad_pre):
    rows = pre_0.shape[0]

    @pl.when(pl.program_id(0) == 0)
    def _():
        total = 0.0
        for chain, (pre, own, later) in enumerate(((pre_0, own_0, next_0), (pre_1, own_1, next_1))):
            value = jnp.where(pre[...] > 0, own[...] + later[...], 0.0).astype(BF16)
            grad_pre[chain * rows:(chain + 1) * rows, :] = value
            total = total + jnp.sum(value.astype(F32), axis=0, keepdims=True)
        bias[...] = total

    height = grad.shape[1]
    at = pl.multiple_of(pl.program_id(0) * height, height)
    grad[0] = jnp.dot(turned[pl.ds(at, height), :], grad_pre[...], preferred_element_type=F32)


def ring_shards(residual_in, targets, enc_weight, enc_bias, dec_same, dec_cross):
    size = lax.axis_size("latent")
    place = ring_place(lax.axis_index("latent"), size)
    is_first = lax.axis_index("layer") == 0
    rows, wide = residual_in.shape[1:]
    deep, lat = enc_weight.shape[1:]
    half = rows // 2
    half_width = deep // 2
    err_scale = 1.0 / math.sqrt(rows)
    shape = jax.ShapeDtypeStruct
    work = 2 * rows * deep * lat

    def start_of(offset):
        return ring_member(place + offset, size) * wide

    def halves(array):
        return [array[:half], array[half:]]

    own_dec = dec_same[0]
    inputs = ring_gather(halves(residual_in[0]), size)
    offsets = [offset for offset, _ in inputs[0]]
    starts = jnp.stack([start_of(offset) for offset in offsets]).astype(jnp.int32)
    cross_full = lax.all_gather(dec_cross, "layer", axis=1, tiled=True)

    preacts, codes, earlier = [], [], []
    for chain in range(2):
        preact, now = call(
            encode_kernel,
            [shape((half, lat), F32), shape((half, lat), BF16)],
            work // 2,
            [starts] + [shard for _, shard in inputs[chain]] + [enc_weight, enc_bias],
        )
        preacts.append(preact)
        codes.append(now)
        earlier.append(passed_along(now, "layer", 1))
    both = [shard for pair in zip(*inputs) for _, shard in pair]
    turned = call(turn_kernel, [shape((deep, rows), BF16)], 0, [starts] + both)[0]

    def columns(array, offset):
        return lax.dynamic_slice_in_dim(array, start_of(offset), wide, 1)

    def partial_of(chain, offset):
        return matmul(codes[chain], columns(own_dec, offset)) + matmul(earlier[chain], columns(cross_full, offset))

    recon = ring_reduce(partial_of, size)
    own_errors = [
        ((total - wanted.astype(F32)) * err_scale).astype(BF16) for total, wanted in zip(recon, halves(targets[0]))
    ]
    errors = ring_gather(own_errors, size)
    back_own, from_next = [], []
    for chain in range(2):
        own, cross = call(
            back_kernel,
            [shape((half, lat), F32), shape((half, lat), F32)],
            work,
            [starts] + [shard for _, shard in errors[chain]] + [own_dec, cross_full],
        )
        back_own.append(own)
        from_next.append(passed_along(cross, "layer", -1))
    both = [shard for pair in zip(*errors) for _, shard in pair]
    grad_same, low, high = call(
        outer_kernel,
        [shape((1, lat, deep), F32), shape((lat, half_width), F32), shape((lat, half_width), F32)],
        2 * work,
        [starts] + both + codes + earlier,
        scratch=[pltpu.VMEM((rows, deep), BF16), pltpu.VMEM((lat, rows), BF16), pltpu.VMEM((lat, rows), BF16)],
    )
    returned = passed_along(low, "layer", -1)
    pieces = ENC_PIECES
    grad_enc, grad_bias = call(
        enc_kernel,
        [shape((1, deep, lat), F32), shape((1, lat), F32)],
        work,
        [starts, turned] + preacts + back_own + from_next,
        grid=(pieces,),
        out_specs=[
            pl.BlockSpec((1, deep // pieces, lat), lambda i: (0, i, 0)),
            pl.BlockSpec((1, lat), lambda i: (0, 0)),
        ],
        scratch=[pltpu.VMEM((rows, lat), BF16)],
    )
    grad_cross = jnp.where(is_first, returned, high)
    return (grad_enc, grad_bias, grad_same, grad_cross)


def wide_shards(residual_in, targets, enc_weight, enc_bias, dec_same, dec_cross):
    is_first = lax.axis_index("layer") == 0
    err_scale = 1.0 / math.sqrt(residual_in.shape[1])
    inputs = lax.all_gather(residual_in[0], "latent", axis=1, tiled=True)
    preact = matmul(inputs, enc_weight[0]) + enc_bias[0]
    codes_now = jnp.maximum(preact, 0.0).astype(BF16)
    earlier = passed_along(codes_now, "layer", 1)
    cross_full = lax.all_gather(dec_cross, "layer", axis=1, tiled=True)
    own_dec = dec_same[0]
    half_width = own_dec.shape[1] // 2
    recon_full = lax.psum(matmul(codes_now, own_dec) + matmul(earlier, cross_full), "latent")
    wanted = lax.all_gather(targets[0], "latent", axis=1, tiled=True)
    errors = ((recon_full - wanted.astype(F32)) * err_scale).astype(BF16)
    grad_same = matmul(codes_now, errors, OVER_ROWS)
    grad_full = matmul(earlier, errors, OVER_ROWS)
    returned = passed_along(grad_full[:, :half_width], "layer", -1)
    grad_cross = jnp.where(is_first, returned, grad_full[:, half_width:])
    from_next = passed_along(matmul(errors, cross_full, OVER_COLS), "layer", -1)
    grad_codes = matmul(errors, own_dec, OVER_COLS) + from_next
    grad_pre = jnp.where(preact > 0, grad_codes, 0.0).astype(BF16)
    grad_enc = matmul(inputs, grad_pre, OVER_ROWS)
    grad_bias = jnp.sum(grad_pre.astype(F32), axis=0)
    return (grad_enc[None], grad_bias[None], grad_same[None], grad_cross)


def solution(mesh):
    size = mesh.shape["latent"]
    placed = (
        P("layer", "groups", "latent"),
        P("layer", "groups", "latent"),
        P("layer", None, "latent"),
        P("layer", "latent"),
        P("layer", "latent", None),
        P("latent", "layer"),
    )
    return jax.shard_map(
        ring_shards if size % 2 == 0 and size <= RING_LIMIT else wide_shards,
        mesh=mesh,
        in_specs=placed,
        out_specs=(
            P(("groups", "layer"), None, "latent"),
            P(("groups", "layer"), "latent"),
            P(("groups", "layer"), "latent", None),
            P(("groups", "latent"), "layer"),
        ),
        check_vma=False,
    )
```

time: 115 us -> 111 us (0.965)
  waiting for transfers between devices: 51.5 us -> 24.5 us
  starting transfers between devices: 30 us -> 55.9 us
  Pallas kernels: 0 us -> 13.7 us
  matrix products: 15.6 us -> 5.67 us
  local copies, waits for them, and re-layouts: 11.6 us -> 4.89 us
    ppermute x24 -> x42, waiting for transfers between devices: 51.5 us -> 22.7 us  [hop(): return lax.ppermute(shard, 'latent', ring_pairs(size, by))]
    ppermute x24 -> x42, starting transfers between devices: 26.1 us -> 48.8 us  [hop(): return lax.ppermute(shard, 'latent', ring_pairs(size, by))]
    pallas_call x0 -> x7, Pallas kernels: none -> 13.7 us  [call(): pl.pallas_call(kernel, out_shape=outs, grid=grid, in_specs=[pl.BlockSpec(...]
    dot_general x36 -> x32, matrix products: 15.6 us -> 5.67 us  [matmul(): return lax.dot_general(a, b, dims, preferred_element_type=F32)]
    dynamic_update_slice x13 -> x0, local copies, waits for them, and re-layouts: 8.61 us -> none  [the longest x7 4.66 us: ring_shards(): lax.dynamic_update_slice_in_dim(grad_enc, matmul(shard, grad_pre, OVER_RO...]
    unnamed x43 -> x44, local copies, waits for them, and re-layouts: 0.14 us -> 3.77 us
    ppermute x3 -> x5, starting transfers between devices: 3.86 us -> 7.17 us  [passed_along(): return lax.ppermute(shard, axis, pairs)]
    broadcast_in_dim x9 -> x0, local copies, waits for them, and re-layouts: 1.9 us -> none  [the longest x8 1.66 us: ring_shards(): return (grad_enc[None], grad_bias[None], grad_same[None], grad_cross)]
  transfers between devices with their start and end apart: 27 -> 47, of which waited for: 16 -> 21; matrix products, arithmetic and copies ran while one was open for 21% -> 5% of each run, Pallas kernels for 0% -> 10%
where the time goes in v2:
time: 111 us; the launch traced here: 110 us
  starting transfers between devices  55.9 us (50%)
  waiting for transfers between devices  24.5 us (22%)
  Pallas kernels  13.7 us (12%)
  matrix products  5.67 us (5%)
  local copies, waits for them, and re-layouts  4.89 us (4%)
  blocking collectives  2.39 us (2%)
  other arithmetic  1.89 us (2%)
  between operations  1.21 us (1%)
    ppermute x42, starting transfers between devices, hop(): return lax.ppermute(shard, 'latent', ring_pairs(size, by))  48.8 us
    ppermute x42, waiting for transfers between devices, hop(): return lax.ppermute(shard, 'latent', ring_pairs(size, by))  22.7 us
    pallas_call x7, Pallas kernels, call(): pl.pallas_call(kernel, out_shape=outs, grid=grid, in_specs=[pl.BlockSpec(...  13.7 us
    ppermute x5, starting transfers between devices, passed_along(): return lax.ppermute(shard, axis, pairs)  7.17 us
    dot_general x32, matrix products, matmul(): return lax.dot_general(a, b, dims, preferred_element_type=F32)  5.67 us
    unnamed x44, local copies, waits for them, and re-layouts  3.77 us
    all_gather x1, blocking collectives, ring_shards(): cross_full = lax.all_gather(dec_cross, 'layer', axis=1, tiled=True)  2.39 us
  transfers between devices with their start and end apart: 47, of which 21 were waited for; matrix products, arithmetic and copies ran while one was open for 5% of the time, Pallas kernels for 10%

profile of v2, /device:TPU:0, one launch (start us, length us, event | category | flops | bytes accessed | tf_op | source)
XLA Modules:
  0.0 110.2 jit_solution(4153561305669246231)
XLA Ops:
  1.7 3.1 %collective-permute-start = (bf16[256,256]{1,0:T(8,128)(2,1)S(1)}, bf16[256,256]{1,0:T(8,128)(2,1)S(1)}, u32[]{:S(2)}, u32[]{:S(2)}) collective-permute-start(bf16[256,256]{1,0:T(8,128)(2,1)S(1)} %get-tuple-element.31.refs_0_), channel_id=1, source_target_pairs={{0,4},{4,8},{8,12},{12,14},{14,10},{10,6},{6,2},{2,0},{1,5},{5,9},... | collective-permute-start | bytes 393224 | tf_op jit(solution)/shard_map/ppermute | solution.py:45
  4.8 1.9 %collective-permute-start.2 = (bf16[256,256]{1,0:T(8,128)(2,1)S(1)}, bf16[256,256]{1,0:T(8,128)(2,1)S(1)}, u32[]{:S(2)}, u32[]{:S(2)}) collective-permute-start(bf16[256,256]{1,0:T(8,128)(2,1)S(1)} %get-tuple-element.31.refs_0_), channel_id=1, source_target_pairs={{0,2},{4,0},{8,4},{12,8},{14,12},{10,14},{6,10},{2,6},{1,3},{5,1},... | collective-permute-start | bytes 393224 | tf_op jit(solution)/shard_map/ppermute | solution.py:45
  6.7 1.5 %collective-permute-done.refs_2_.refs_1_ = bf16[256,256]{1,0:T(8,128)(2,1)S(1)} collective-permute-done((bf16[256,256]{1,0:T(8,128)(2,1)S(1)}, bf16[256,256]{1,0:T(8,128)(2,1)S(1)}, u32[]{:S(2)}, u32[]{:S(2)}) %collective-permute-start) | collective-permute-done | bytes 131104 | tf_op jit(solution)/shard_map/ppermute | solution.py:45
  8.2 1.8 %collective-permute-start.4 = (bf16[256,256]{1,0:T(8,128)(2,1)S(1)}, bf16[256,256]{1,0:T(8,128)(2,1)S(1)}, u32[]{:S(2)}, u32[]{:S(2)}) collective-permute-start(bf16[256,256]{1,0:T(8,128)(2,1)S(1)} %collective-permute-done.refs_2_.refs_1_), channel_id=1, source_target_pairs={{0,4},{4,8},{8,12},{12,14},{14,10},{10,6},{6,2},{2,0},{1,5},{5,9},... | collective-permute-start | bytes 393224 | tf_op jit(solution)/shard_map/ppermute | solution.py:45
  10.0 1.6 %collective-permute-start.1 = (bf16[256,256]{1,0:T(8,128)(2,1)S(1)}, bf16[256,256]{1,0:T(8,128)(2,1)S(1)}, u32[]{:S(2)}, u32[]{:S(2)}) collective-permute-start(bf16[256,256]{1,0:T(8,128)(2,1)S(1)} %get-tuple-element.30.refs_1_.refs_0_), channel_id=1, source_target_pairs={{0,4},{4,8},{8,12},{12,14},{14,10},{10,6},{6,2},{2,0},{1,5},{5,9},... | collective-permute-start | bytes 393224 | tf_op jit(solution)/shard_map/ppermute | solution.py:45
  14.3 1.5 %collective-permute-start.8 = (bf16[256,256]{1,0:T(8,128)(2,1)S(1)}, bf16[256,256]{1,0:T(8,128)(2,1)S(1)}, u32[]{:S(2)}, u32[]{:S(2)}) collective-permute-start(bf16[256,256]{1,0:T(8,128)(2,1)S(1)} %collective-permute-done.4.refs_6_.refs_3_), channel_id=1, source_target_pairs={{0,4},{4,8},{8,12},{12,14},{14,10},{10,6},{6,2},{2,0},{1,5},{5,9},... | collective-permute-start | bytes 393224 | tf_op jit(solution)/shard_map/ppermute | solution.py:45
  17.1 1.5 %collective-permute-start.5 = (bf16[256,256]{1,0:T(8,128)(2,1)S(1)}, bf16[256,256]{1,0:T(8,128)(2,1)S(1)}, u32[]{:S(2)}, u32[]{:S(2)}) collective-permute-start(bf16[256,256]{1,0:T(8,128)(2,1)S(1)} %collective-permute-done.1.refs_3_.refs_1_), channel_id=1, source_target_pairs={{0,4},{4,8},{8,12},{12,14},{14,10},{10,6},{6,2},{2,0},{1,5},{5,9},... | collective-permute-start | bytes 393224 | tf_op jit(solution)/shard_map/ppermute | solution.py:45
  19.1 1.5 %collective-permute-start.10 = (bf16[256,256]{1,0:T(8,128)(2,1)S(1)}, bf16[256,256]{1,0:T(8,128)(2,1)S(1)}, u32[]{:S(2)}, u32[]{:S(2)}) collective-permute-start(bf16[256,256]{1,0:T(8,128)(2,1)S(1)} %collective-permute-done.6.refs_8_.refs_4_), channel_id=1, source_target_pairs={{0,2},{4,0},{8,4},{12,8},{14,12},{10,14},{6,10},{2,6},{1,3},{5,1},... | collective-permute-start | bytes 393224 | tf_op jit(solution)/shard_map/ppermute | solution.py:45
  21.6 1.9 %collective-permute-done.5.refs_7_.refs_3_ = bf16[256,256]{1,0:T(8,128)(2,1)S(1)} collective-permute-done((bf16[256,256]{1,0:T(8,128)(2,1)S(1)}, bf16[256,256]{1,0:T(8,128)(2,1)S(1)}, u32[]{:S(2)}, u32[]{:S(2)}) %collective-permute-start.5) | collective-permute-done | bytes 131104 | tf_op jit(solution)/shard_map/ppermute | solution.py:45
  23.5 1.5 %collective-permute-start.9 = (bf16[256,256]{1,0:T(8,128)(2,1)S(1)}, bf16[256,256]{1,0:T(8,128)(2,1)}, u32[]{:S(2)}, u32[]{:S(2)}) collective-permute-start(bf16[256,256]{1,0:T(8,128)(2,1)S(1)} %collective-permute-done.5.refs_7_.refs_3_), channel_id=1, source_target_pairs={{0,4},{4,8},{8,12},{12,14},{14,10},{10,6},{6,2},{2,0},{1,5},{5,9},... | collective-permute-start | bytes 393224 | tf_op jit(solution)/shard_map/ppermute | solution.py:45
  31.1 2.4 %all_gather.3.refs_9_ = bf16[128,2048]{1,0:T(8,128)(2,1)S(1)} all-gather(bf16[128,1024]{1,0:T(8,128)(2,1)} %param.11), channel_id=1, replica_groups=mesh['groups'=2,'latent'=8,'layer'=2] {'layer'}, dimensions={1}, use_global_device_ids=true | all-gather | bytes 786432 | tf_op jit(solution)/shard_map/all_gather | solution.py:190
  34.9 2.0 %collective-permute-start.29 = (bf16[256,128]{1,0:T(8,128)(2,1)S(1)}, bf16[256,128]{1,0:T(8,128)(2,1)S(1)}, u32[]{:S(2)}, u32[]{:S(2)}) collective-permute-start(bf16[256,128]{1,0:T(8,128)(2,1)S(1)} %get-tuple-element.21.refs_17_), channel_id=1, source_target_pairs={{0,1},{2,3},{4,5},{6,7},{8,9},{10,11},{12,13},{14,15},{16,17},{18,... | collective-permute-start | bytes 196616 | tf_op jit(solution)/shard_map/ppermute | solution.py:23
  48.5 1.4 %collective-permute-start.31 = (bf16[256,256]{1,0:T(8,128)(2,1)S(1)}, bf16[256,256]{1,0:T(8,128)(2,1)S(1)}, u32[]{:S(2)}, u32[]{:S(2)}) collective-permute-start(bf16[256,256]{1,0:T(8,128)(2,1)S(1)} %fusion.26), channel_id=1, source_target_pairs={{0,4},{4,8},{8,12},{12,14},{14,10},{10,6},{6,2},{2,0},{1,5},{5,9},... | collective-permute-start | bytes 393224 | tf_op jit(solution)/shard_map/ppermute | solution.py:45
  50.0 1.5 %collective-permute-done.20 = bf16[256,256]{1,0:T(8,128)(2,1)S(1)} collective-permute-done((bf16[256,256]{1,0:T(8,128)(2,1)S(1)}, bf16[256,256]{1,0:T(8,128)(2,1)S(1)}, u32[]{:S(2)}, u32[]{:S(2)}) %collective-permute-start.20) | collective-permute-done | bytes 131104 | tf_op jit(solution)/shard_map/ppermute | solution.py:45
  52.4 1.6 %collective-permute-start.17 = (bf16[256,256]{1,0:T(8,128)(2,1)S(1)}, bf16[256,256]{1,0:T(8,128)(2,1)S(1)}, u32[]{:S(2)}, u32[]{:S(2)}) collective-permute-start(bf16[256,256]{1,0:T(8,128)(2,1)S(1)} %fusion.19), channel_id=1, source_target_pairs={{0,4},{4,8},{8,12},{12,14},{14,10},{10,6},{6,2},{2,0},{1,5},{5,9},... | collective-permute-start | bytes 393224 | tf_op jit(solution)/shard_map/ppermute | solution.py:45
  55.2 1.4 %collective-permute-start.32 = (bf16[256,256]{1,0:T(8,128)(2,1)S(1)}, bf16[256,256]{1,0:T(8,128)(2,1)S(1)}, u32[]{:S(2)}, u32[]{:S(2)}) collective-permute-start(bf16[256,256]{1,0:T(8,128)(2,1)S(1)} %fusion.25), channel_id=1, source_target_pairs={{0,4},{4,8},{8,12},{12,14},{14,10},{10,6},{6,2},{2,0},{1,5},{5,9},... | collective-permute-start | bytes 393224 | tf_op jit(solution)/shard_map/ppermute | solution.py:45
  56.6 1.8 %collective-permute-done.17 = bf16[256,256]{1,0:T(8,128)(2,1)S(1)} collective-permute-done((bf16[256,256]{1,0:T(8,128)(2,1)S(1)}, bf16[256,256]{1,0:T(8,128)(2,1)S(1)}, u32[]{:S(2)}, u32[]{:S(2)}) %collective-permute-start.17) | collective-permute-done | bytes 131104 | tf_op jit(solution)/shard_map/ppermute | solution.py:45
  58.6 1.7 %collective-permute-start.18 = (bf16[256,256]{1,0:T(8,128)(2,1)S(1)}, bf16[256,256]{1,0:T(8,128)(2,1)S(1)}, u32[]{:S(2)}, u32[]{:S(2)}) collective-permute-start(bf16[256,256]{1,0:T(8,128)(2,1)S(1)} %fusion.18), channel_id=1, source_target_pairs={{0,4},{4,8},{8,12},{12,14},{14,10},{10,6},{6,2},{2,0},{1,5},{5,9},... | collective-permute-start | bytes 393224 | tf_op jit(solution)/shard_map/ppermute | solution.py:45
  61.5 3.0 %collective-permute-done.18 = bf16[256,256]{1,0:T(8,128)(2,1)S(1)} collective-permute-done((bf16[256,256]{1,0:T(8,128)(2,1)S(1)}, bf16[256,256]{1,0:T(8,128)(2,1)S(1)}, u32[]{:S(2)}, u32[]{:S(2)}) %collective-permute-start.18) | collective-permute-done | bytes 131104 | tf_op jit(solution)/shard_map/ppermute | solution.py:45
  64.8 1.9 %collective-permute-start.22 = (bf16[256,256]{1,0:T(8,128)(2,1)S(1)}, bf16[256,256]{1,0:T(8,128)(2,1)S(1)}, u32[]{:S(2)}, u32[]{:S(2)}) collective-permute-start(bf16[256,256]{1,0:T(8,128)(2,1)S(1)} %fusion.32.refs_0_), channel_id=1, source_target_pairs={{0,4},{4,8},{8,12},{12,14},{14,10},{10,6},{6,2},{2,0},{1,5},{5,9},... | collective-permute-start | bytes 393224 | tf_op jit(solution)/shard_map/ppermute | solution.py:45
  68.1 1.6 %collective-permute-start.23 = (bf16[256,256]{1,0:T(8,128)(2,1)S(1)}, bf16[256,256]{1,0:T(8,128)(2,1)S(1)}, u32[]{:S(2)}, u32[]{:S(2)}) collective-permute-start(bf16[256,256]{1,0:T(8,128)(2,1)S(1)} %fusion.32.refs_0_), channel_id=1, source_target_pairs={{0,2},{4,0},{8,4},{12,8},{14,12},{10,14},{6,10},{2,6},{1,3},{5,1},... | collective-permute-start | bytes 393224 | tf_op jit(solution)/shard_map/ppermute | solution.py:45
  70.2 1.5 %collective-permute-start.24 = (bf16[256,256]{1,0:T(8,128)(2,1)S(1)}, bf16[256,256]{1,0:T(8,128)(2,1)S(1)}, u32[]{:S(2)}, u32[]{:S(2)}) collective-permute-start(bf16[256,256]{1,0:T(8,128)(2,1)S(1)} %collective-permute-done.22.refs_1_.refs_2_), channel_id=1, source_target_pairs={{0,4},{4,8},{8,12},{12,14},{14,10},{10,6},{6,2},{2,0},{1,5},{5,9},... | collective-permute-start | bytes 393224 | tf_op jit(solution)/shard_map/ppermute | solution.py:45
  75.6 1.5 %collective-permute-start.25 = (bf16[256,256]{1,0:T(8,128)(2,1)S(1)}, bf16[256,256]{1,0:T(8,128)(2,1)S(1)}, u32[]{:S(2)}, u32[]{:S(2)}) collective-permute-start(bf16[256,256]{1,0:T(8,128)(2,1)S(1)} %collective-permute-done.23.refs_2_.refs_4_), channel_id=1, source_target_pairs={{0,2},{4,0},{8,4},{12,8},{14,12},{10,14},{6,10},{2,6},{1,3},{5,1},... | collective-permute-start | bytes 393224 | tf_op jit(solution)/shard_map/ppermute | solution.py:45
  77.6 1.6 %collective-permute-start.26 = (bf16[256,256]{1,0:T(8,128)(2,1)S(1)}, bf16[256,256]{1,0:T(8,128)(2,1)S(1)}, u32[]{:S(2)}, u32[]{:S(2)}) collective-permute-start(bf16[256,256]{1,0:T(8,128)(2,1)S(1)} %collective-permute-done.24.refs_3_.refs_6_), channel_id=1, source_target_pairs={{0,4},{4,8},{8,12},{12,14},{14,10},{10,6},{6,2},{2,0},{1,5},{5,9},... | collective-permute-start | bytes 393224 | tf_op jit(solution)/shard_map/ppermute | solution.py:45
  83.4 1.5 %collective-permute-start.28 = (bf16[256,256]{1,0:T(8,128)(2,1)S(1)}, bf16[256,256]{1,0:T(8,128)(2,1)S(1)}, u32[]{:S(2)}, u32[]{:S(2)}) collective-permute-start(bf16[256,256]{1,0:T(8,128)(2,1)S(1)} %collective-permute-done.26.refs_5_.refs_10_), channel_id=1, source_target_pairs={{0,4},{4,8},{8,12},{12,14},{14,10},{10,6},{6,2},{2,0},{1,5},{5,9},... | collective-permute-start | bytes 393224 | tf_op jit(solution)/shard_map/ppermute | solution.py:45
  89.8 2.5 %shard_map.99 = (f32[1,128,2048]{2,1,0:T(8,128)}, f32[128,1024]{1,0:T(8,128)}, f32[128,1024]{1,0:T(8,128)S(1)}) custom-call(s32[8]{0:T(128)S(1)} %stack.35.starts.first, bf16[256,256]{1,0:T(8,128)(2,1)S(1)} %fusion.32.refs_0_, bf16[256,256]{1,0:T(8,128)(2,1)S(1)} %fusion.33.refs_0_.refs_1_, bf16[256,256]{1,0:T(8,128)(2,1)S(1)} %collective-permute-done.22.refs_1_.refs_2_, ...), custom_call_target="tpu_custom_call" | custom-call | flops 536870912 | bytes 1048576 | tf_op jit(solution)/shard_map/pallas_call | solution.py:86
  93.7 1.9 %shard_map.96 = (f32[256,128]{1,0:T(8,128)S(1)}, f32[256,128]{1,0:T(8,128)}) custom-call(s32[8]{0:T(128)S(1)} %stack.35.starts.first, bf16[256,256]{1,0:T(8,128)(2,1)S(1)} %fusion.32.refs_0_, bf16[256,256]{1,0:T(8,128)(2,1)S(1)} %collective-permute-done.22.refs_1_.refs_2_, bf16[256,256]{1,0:T(8,128)(2,1)S(1)} %collective-permute-done.23.refs_2_.refs_4_, ...), custom_call_target="tpu_custom_call" | custom-call | flops 268435456 | bytes 1048576 | tf_op jit(solution)/shard_map/pallas_call | solution.py:86
  97.5 1.9 %shard_map.97 = (f32[256,128]{1,0:T(8,128)S(1)}, f32[256,128]{1,0:T(8,128)}) custom-call(s32[8]{0:T(128)S(1)} %stack.35.starts.first, bf16[256,256]{1,0:T(8,128)(2,1)S(1)} %fusion.33.refs_0_.refs_1_, bf16[256,256]{1,0:T(8,128)(2,1)S(1)} %collective-permute-done.37.refs_1_.refs_3_, bf16[256,256]{1,0:T(8,128)(2,1)S(1)} %collective-permute-done.38.refs_2_.refs_5_, ...), custom_call_target="tpu_custom_call" | custom-call | flops 268435456 | bytes 1048576 | tf_op jit(solution)/shard_map/pallas_call | solution.py:86
  101.5 1.6 %shard_map.93.turned = bf16[2048,512]{1,0:T(8,128)(2,1)S(1)} custom-call(s32[8]{0:T(128)S(1)} %stack.35.starts.first, bf16[256,256]{1,0:T(8,128)(2,1)S(1)} %get-tuple-element.31.refs_0_, bf16[256,256]{1,0:T(8,128)(2,1)S(1)} %get-tuple-element.30.refs_1_.refs_0_, bf16[256,256]{1,0:T(8,128)(2,1)S(1)} %collective-permute-done.refs_2_.refs_1_, ...), custom_call_target="tpu_custom_call" | custom-call | bytes 1048576 | tf_op jit(solution)/shard_map/pallas_call | solution.py:86
  103.1 1.8 %collective-permute-done.45.next_1 = f32[256,128]{1,0:T(8,128)S(1)} collective-permute-done((f32[256,128]{1,0:T(8,128)}, f32[256,128]{1,0:T(8,128)S(1)}, u32[]{:S(2)}, u32[]{:S(2)}) %collective-permute-start.45) | collective-permute-done | bytes 131104 | tf_op jit(solution)/shard_map/ppermute | solution.py:23
  105.0 3.3 %shard_map.98 = (f32[1,2048,128]{2,1,0:T(8,128)}, f32[1,128]{1,0:T(1,128)}) custom-call(s32[8]{0:T(128)S(1)} %stack.35.starts.first, bf16[2048,512]{1,0:T(8,128)(2,1)S(1)} %shard_map.93.turned, f32[256,128]{1,0:T(8,128)S(1)} %copy-done.12, f32[256,128]{1,0:T(8,128)S(1)} %copy-done.14, f32[256,128]{1,0:T(8,128)S(1)} %copy-done.16, f32[256,128]{1,0:T(8,128)S(1)} %copy-done.18, ...), custom_call_target="tpu_custom_call" | custom-call | flops 268435456 | bytes 1048576 | tf_op jit(solution)/shard_map/pallas_call | solution.py:86
  108.3 1.9 %broadcast_select_fusion = f32[128,1024]{1,0:T(8,128)} fusion(f32[128,1024]{1,0:T(8,128)} %collective-permute-done.46, f32[128,1024]{1,0:T(8,128)S(1)} %get-tuple-element.29, pred[]{:T(512)S(6)} %eq.9), kind=kLoop, calls=%fused_computation.50 | loop fusion | flops 131072 | bytes 1572865 | tf_op jit(solution)/shard_map/jit(_where)/select_n | solution.py:249
  (149 shorter events, 49.6 us)
Async XLA Ops:
  1.7 6.5 %collective-permute-start = (bf16[256,256]{1,0:T(8,128)(2,1)S(1)}, bf16[256,256]{1,0:T(8,128)(2,1)S(1)}, u32[]{:S(2)}, u32[]{:S(2)}) collective-permute-start(bf16[256,256]{1,0:T(8,128)(2,1)S(1)} %get-tuple-element.31.refs_0_), channel_id=1, source_target_pairs={{0,4},{4,8},{8,12},{12,14},{14,10},{10,6},{6,2},{2,0},{1,5},{5,9},... | collective-permute-start | bytes 393224 | tf_op jit(solution)/shard_map/ppermute | solution.py:45
  4.8 6.8 %collective-permute-start.3 = (bf16[256,256]{1,0:T(8,128)(2,1)S(1)}, bf16[256,256]{1,0:T(8,128)(2,1)S(1)}, u32[]{:S(2)}, u32[]{:S(2)}) collective-permute-start(bf16[256,256]{1,0:T(8,128)(2,1)S(1)} %get-tuple-element.30.refs_1_.refs_0_), channel_id=1, source_target_pairs={{0,2},{4,0},{8,4},{12,8},{14,12},{10,14},{6,10},{2,6},{1,3},{5,1},... | collective-permute-start | bytes 393224 | tf_op jit(solution)/shard_map/ppermute | solution.py:45
  4.8 7.8 %collective-permute-start.2 = (bf16[256,256]{1,0:T(8,128)(2,1)S(1)}, bf16[256,256]{1,0:T(8,128)(2,1)S(1)}, u32[]{:S(2)}, u32[]{:S(2)}) collective-permute-start(bf16[256,256]{1,0:T(8,128)(2,1)S(1)} %get-tuple-element.31.refs_0_), channel_id=1, source_target_pairs={{0,2},{4,0},{8,4},{12,8},{14,12},{10,14},{6,10},{2,6},{1,3},{5,1},... | collective-permute-start | bytes 393224 | tf_op jit(solution)/shard_map/ppermute | solution.py:45
  8.2 6.1 %collective-permute-start.4 = (bf16[256,256]{1,0:T(8,128)(2,1)S(1)}, bf16[256,256]{1,0:T(8,128)(2,1)S(1)}, u32[]{:S(2)}, u32[]{:S(2)}) collective-permute-start(bf16[256,256]{1,0:T(8,128)(2,1)S(1)} %collective-permute-done.refs_2_.refs_1_), channel_id=1, source_target_pairs={{0,4},{4,8},{8,12},{12,14},{14,10},{10,6},{6,2},{2,0},{1,5},{5,9},... | collective-permute-start | bytes 393224 | tf_op jit(solution)/shard_map/ppermute | solution.py:45
  10.0 7.1 %collective-permute-start.1 = (bf16[256,256]{1,0:T(8,128)(2,1)S(1)}, bf16[256,256]{1,0:T(8,128)(2,1)S(1)}, u32[]{:S(2)}, u32[]{:S(2)}) collective-permute-start(bf16[256,256]{1,0:T(8,128)(2,1)S(1)} %get-tuple-element.30.refs_1_.refs_0_), channel_id=1, source_target_pairs={{0,4},{4,8},{8,12},{12,14},{14,10},{10,6},{6,2},{2,0},{1,5},{5,9},... | collective-permute-start | bytes 393224 | tf_op jit(solution)/shard_map/ppermute | solution.py:45
  11.6 7.0 %collective-permute-start.7 = (bf16[256,256]{1,0:T(8,128)(2,1)S(1)}, bf16[256,256]{1,0:T(8,128)(2,1)S(1)}, u32[]{:S(2)}, u32[]{:S(2)}) collective-permute-start(bf16[256,256]{1,0:T(8,128)(2,1)S(1)} %collective-permute-done.3.refs_5_.refs_2_), channel_id=1, source_target_pairs={{0,2},{4,0},{8,4},{12,8},{14,12},{10,14},{6,10},{2,6},{1,3},{5,1},... | collective-permute-start | bytes 393224 | tf_op jit(solution)/shard_map/ppermute | solution.py:45
  12.5 6.6 %collective-permute-start.6 = (bf16[256,256]{1,0:T(8,128)(2,1)S(1)}, bf16[256,256]{1,0:T(8,128)(2,1)S(1)}, u32[]{:S(2)}, u32[]{:S(2)}) collective-permute-start(bf16[256,256]{1,0:T(8,128)(2,1)S(1)} %collective-permute-done.2.refs_4_.refs_2_), channel_id=1, source_target_pairs={{0,2},{4,0},{8,4},{12,8},{14,12},{10,14},{6,10},{2,6},{1,3},{5,1},... | collective-permute-start | bytes 393224 | tf_op jit(solution)/shard_map/ppermute | solution.py:45
  14.3 6.3 %collective-permute-start.8 = (bf16[256,256]{1,0:T(8,128)(2,1)S(1)}, bf16[256,256]{1,0:T(8,128)(2,1)S(1)}, u32[]{:S(2)}, u32[]{:S(2)}) collective-permute-start(bf16[256,256]{1,0:T(8,128)(2,1)S(1)} %collective-permute-done.4.refs_6_.refs_3_), channel_id=1, source_target_pairs={{0,4},{4,8},{8,12},{12,14},{14,10},{10,6},{6,2},{2,0},{1,5},{5,9},... | collective-permute-start | bytes 393224 | tf_op jit(solution)/shard_map/ppermute | solution.py:45
  17.1 6.4 %collective-permute-start.5 = (bf16[256,256]{1,0:T(8,128)(2,1)S(1)}, bf16[256,256]{1,0:T(8,128)(2,1)S(1)}, u32[]{:S(2)}, u32[]{:S(2)}) collective-permute-start(bf16[256,256]{1,0:T(8,128)(2,1)S(1)} %collective-permute-done.1.refs_3_.refs_1_), channel_id=1, source_target_pairs={{0,4},{4,8},{8,12},{12,14},{14,10},{10,6},{6,2},{2,0},{1,5},{5,9},... | collective-permute-start | bytes 393224 | tf_op jit(solution)/shard_map/ppermute | solution.py:45
  18.6 6.4 %collective-permute-start.11 = (bf16[256,256]{1,0:T(8,128)(2,1)S(1)}, bf16[256,256]{1,0:T(8,128)(2,1)S(1)}, u32[]{:S(2)}, u32[]{:S(2)}) collective-permute-start(bf16[256,256]{1,0:T(8,128)(2,1)S(1)} %collective-permute-done.7.refs_9_.refs_4_), channel_id=1, source_target_pairs={{0,2},{4,0},{8,4},{12,8},{14,12},{10,14},{6,10},{2,6},{1,3},{5,1},... | collective-permute-start | bytes 393224 | tf_op jit(solution)/shard_map/ppermute | solution.py:45
  19.1 7.3 %collective-permute-start.10 = (bf16[256,256]{1,0:T(8,128)(2,1)S(1)}, bf16[256,256]{1,0:T(8,128)(2,1)S(1)}, u32[]{:S(2)}, u32[]{:S(2)}) collective-permute-start(bf16[256,256]{1,0:T(8,128)(2,1)S(1)} %collective-permute-done.6.refs_8_.refs_4_), channel_id=1, source_target_pairs={{0,2},{4,0},{8,4},{12,8},{14,12},{10,14},{6,10},{2,6},{1,3},{5,1},... | collective-permute-start | bytes 393224 | tf_op jit(solution)/shard_map/ppermute | solution.py:45
  23.5 10.0 %collective-permute-start.9 = (bf16[256,256]{1,0:T(8,128)(2,1)S(1)}, bf16[256,256]{1,0:T(8,128)(2,1)}, u32[]{:S(2)}, u32[]{:S(2)}) collective-permute-start(bf16[256,256]{1,0:T(8,128)(2,1)S(1)} %collective-permute-done.5.refs_7_.refs_3_), channel_id=1, source_target_pairs={{0,4},{4,8},{8,12},{12,14},{14,10},{10,6},{6,2},{2,0},{1,5},{5,9},... | collective-permute-start | bytes 393224 | tf_op jit(solution)/shard_map/ppermute | solution.py:45
  25.0 8.5 %collective-permute-start.13 = (bf16[256,256]{1,0:T(8,128)(2,1)S(1)}, bf16[256,256]{1,0:T(8,128)(2,1)}, u32[]{:S(2)}, u32[]{:S(2)}) collective-permute-start(bf16[256,256]{1,0:T(8,128)(2,1)S(1)} %collective-permute-done.11.refs_13_.refs_6_), channel_id=1, source_target_pairs={{0,2},{4,0},{8,4},{12,8},{14,12},{10,14},{6,10},{2,6},{1,3},{5,1},... | collective-permute-start | bytes 393224 | tf_op jit(solution)/shard_map/ppermute | solution.py:45
  29.8 7.2 %collective-permute-start.14 = (bf16[256,128]{1,0:T(8,128)(2,1)S(1)}, bf16[256,128]{1,0:T(8,128)(2,1)S(1)}, u32[]{:S(2)}, u32[]{:S(2)}) collective-permute-start(bf16[256,128]{1,0:T(8,128)(2,1)S(1)} %get-tuple-element.19.refs_16_), channel_id=1, source_target_pairs={{0,1},{2,3},{4,5},{6,7},{8,9},{10,11},{12,13},{14,15},{16,17},{18,... | collective-permute-start | bytes 196616 | tf_op jit(solution)/shard_map/ppermute | solution.py:23
  37.4 7.5 %collective-permute-start.19 = (bf16[256,256]{1,0:T(8,128)(2,1)S(1)}, bf16[256,256]{1,0:T(8,128)(2,1)S(1)}, u32[]{:S(2)}, u32[]{:S(2)}) collective-permute-start(bf16[256,256]{1,0:T(8,128)(2,1)S(1)} %fusion.24), channel_id=1, source_target_pairs={{0,2},{4,0},{8,4},{12,8},{14,12},{10,14},{6,10},{2,6},{1,3},{5,1},... | collective-permute-start | bytes 393224 | tf_op jit(solution)/shard_map/ppermute | solution.py:45
  38.5 7.4 %collective-permute-start.15 = (bf16[256,256]{1,0:T(8,128)(2,1)S(1)}, bf16[256,256]{1,0:T(8,128)(2,1)S(1)}, u32[]{:S(2)}, u32[]{:S(2)}) collective-permute-start(bf16[256,256]{1,0:T(8,128)(2,1)S(1)} %fusion.21), channel_id=1, source_target_pairs={{0,4},{4,8},{8,12},{12,14},{14,10},{10,6},{6,2},{2,0},{1,5},{5,9},... | collective-permute-start | bytes 393224 | tf_op jit(solution)/shard_map/ppermute | solution.py:45
  40.3 7.2 %collective-permute-start.33 = (bf16[256,256]{1,0:T(8,128)(2,1)S(1)}, bf16[256,256]{1,0:T(8,128)(2,1)S(1)}, u32[]{:S(2)}, u32[]{:S(2)}) collective-permute-start(bf16[256,256]{1,0:T(8,128)(2,1)S(1)} %fusion.31), channel_id=1, source_target_pairs={{0,2},{4,0},{8,4},{12,8},{14,12},{10,14},{6,10},{2,6},{1,3},{5,1},... | collective-permute-start | bytes 393224 | tf_op jit(solution)/shard_map/ppermute | solution.py:45
  41.3 7.0 %collective-permute-start.30 = (bf16[256,256]{1,0:T(8,128)(2,1)S(1)}, bf16[256,256]{1,0:T(8,128)(2,1)S(1)}, u32[]{:S(2)}, u32[]{:S(2)}) collective-permute-start(bf16[256,256]{1,0:T(8,128)(2,1)S(1)} %fusion.27), channel_id=1, source_target_pairs={{0,4},{4,8},{8,12},{12,14},{14,10},{10,6},{6,2},{2,0},{1,5},{5,9},... | collective-permute-start | bytes 393224 | tf_op jit(solution)/shard_map/ppermute | solution.py:45
  45.1 6.3 %collective-permute-start.20 = (bf16[256,256]{1,0:T(8,128)(2,1)S(1)}, bf16[256,256]{1,0:T(8,128)(2,1)S(1)}, u32[]{:S(2)}, u32[]{:S(2)}) collective-permute-start(bf16[256,256]{1,0:T(8,128)(2,1)S(1)} %fusion.23), channel_id=1, source_target_pairs={{0,2},{4,0},{8,4},{12,8},{14,12},{10,14},{6,10},{2,6},{1,3},{5,1},... | collective-permute-start | bytes 393224 | tf_op jit(solution)/shard_map/ppermute | solution.py:45
  46.0 6.2 %collective-permute-start.16 = (bf16[256,256]{1,0:T(8,128)(2,1)S(1)}, bf16[256,256]{1,0:T(8,128)(2,1)S(1)}, u32[]{:S(2)}, u32[]{:S(2)}) collective-permute-start(bf16[256,256]{1,0:T(8,128)(2,1)S(1)} %fusion.20), channel_id=1, source_target_pairs={{0,4},{4,8},{8,12},{12,14},{14,10},{10,6},{6,2},{2,0},{1,5},{5,9},... | collective-permute-start | bytes 393224 | tf_op jit(solution)/shard_map/ppermute | solution.py:45
  47.6 6.5 %collective-permute-start.34 = (bf16[256,256]{1,0:T(8,128)(2,1)S(1)}, bf16[256,256]{1,0:T(8,128)(2,1)S(1)}, u32[]{:S(2)}, u32[]{:S(2)}) collective-permute-start(bf16[256,256]{1,0:T(8,128)(2,1)S(1)} %fusion.30), channel_id=1, source_target_pairs={{0,2},{4,0},{8,4},{12,8},{14,12},{10,14},{6,10},{2,6},{1,3},{5,1},... | collective-permute-start | bytes 393224 | tf_op jit(solution)/shard_map/ppermute | solution.py:45
  48.5 6.5 %collective-permute-start.31 = (bf16[256,256]{1,0:T(8,128)(2,1)S(1)}, bf16[256,256]{1,0:T(8,128)(2,1)S(1)}, u32[]{:S(2)}, u32[]{:S(2)}) collective-permute-start(bf16[256,256]{1,0:T(8,128)(2,1)S(1)} %fusion.26), channel_id=1, source_target_pairs={{0,4},{4,8},{8,12},{12,14},{14,10},{10,6},{6,2},{2,0},{1,5},{5,9},... | collective-permute-start | bytes 393224 | tf_op jit(solution)/shard_map/ppermute | solution.py:45
  51.6 9.9 %collective-permute-start.21 = (bf16[256,256]{1,0:T(8,128)(2,1)S(1)}, bf16[256,256]{1,0:T(8,128)(2,1)S(1)}, u32[]{:S(2)}, u32[]{:S(2)}) collective-permute-start(bf16[256,256]{1,0:T(8,128)(2,1)S(1)} %fusion.22), channel_id=1, source_target_pairs={{0,2},{4,0},{8,4},{12,8},{14,12},{10,14},{6,10},{2,6},{1,3},{5,1},... | collective-permute-start | bytes 393224 | tf_op jit(solution)/shard_map/ppermute | solution.py:45
  54.3 6.2 %collective-permute-start.35 = (bf16[256,256]{1,0:T(8,128)(2,1)S(1)}, bf16[256,256]{1,0:T(8,128)(2,1)S(1)}, u32[]{:S(2)}, u32[]{:S(2)}) collective-permute-start(bf16[256,256]{1,0:T(8,128)(2,1)S(1)} %fusion.29), channel_id=1, source_target_pairs={{0,2},{4,0},{8,4},{12,8},{14,12},{10,14},{6,10},{2,6},{1,3},{5,1},... | collective-permute-start | bytes 393224 | tf_op jit(solution)/shard_map/ppermute | solution.py:45
  55.2 11.6 %collective-permute-start.32 = (bf16[256,256]{1,0:T(8,128)(2,1)S(1)}, bf16[256,256]{1,0:T(8,128)(2,1)S(1)}, u32[]{:S(2)}, u32[]{:S(2)}) collective-permute-start(bf16[256,256]{1,0:T(8,128)(2,1)S(1)} %fusion.25), channel_id=1, source_target_pairs={{0,4},{4,8},{8,12},{12,14},{14,10},{10,6},{6,2},{2,0},{1,5},{5,9},... | collective-permute-start | bytes 393224 | tf_op jit(solution)/shard_map/ppermute | solution.py:45
  60.7 6.4 %collective-permute-start.36 = (bf16[256,256]{1,0:T(8,128)(2,1)S(1)}, bf16[256,256]{1,0:T(8,128)(2,1)S(1)}, u32[]{:S(2)}, u32[]{:S(2)}) collective-permute-start(bf16[256,256]{1,0:T(8,128)(2,1)S(1)} %fusion.28), channel_id=1, source_target_pairs={{0,2},{4,0},{8,4},{12,8},{14,12},{10,14},{6,10},{2,6},{1,3},{5,1},... | collective-permute-start | bytes 393224 | tf_op jit(solution)/shard_map/ppermute | solution.py:45
  68.1 7.4 %collective-permute-start.23 = (bf16[256,256]{1,0:T(8,128)(2,1)S(1)}, bf16[256,256]{1,0:T(8,128)(2,1)S(1)}, u32[]{:S(2)}, u32[]{:S(2)}) collective-permute-start(bf16[256,256]{1,0:T(8,128)(2,1)S(1)} %fusion.32.refs_0_), channel_id=1, source_target_pairs={{0,2},{4,0},{8,4},{12,8},{14,12},{10,14},{6,10},{2,6},{1,3},{5,1},... | collective-permute-start | bytes 393224 | tf_op jit(solution)/shard_map/ppermute | solution.py:45
  69.8 7.3 %collective-permute-start.37 = (bf16[256,256]{1,0:T(8,128)(2,1)S(1)}, bf16[256,256]{1,0:T(8,128)(2,1)S(1)}, u32[]{:S(2)}, u32[]{:S(2)}) collective-permute-start(bf16[256,256]{1,0:T(8,128)(2,1)S(1)} %fusion.33.refs_0_.refs_1_), channel_id=1, source_target_pairs={{0,4},{4,8},{8,12},{12,14},{14,10},{10,6},{6,2},{2,0},{1,5},{5,9},... | collective-permute-start | bytes 393224 | tf_op jit(solution)/shard_map/ppermute | solution.py:45
  70.2 7.4 %collective-permute-start.24 = (bf16[256,256]{1,0:T(8,128)(2,1)S(1)}, bf16[256,256]{1,0:T(8,128)(2,1)S(1)}, u32[]{:S(2)}, u32[]{:S(2)}) collective-permute-start(bf16[256,256]{1,0:T(8,128)(2,1)S(1)} %collective-permute-done.22.refs_1_.refs_2_), channel_id=1, source_target_pairs={{0,4},{4,8},{8,12},{12,14},{14,10},{10,6},{6,2},{2,0},{1,5},{5,9},... | collective-permute-start | bytes 393224 | tf_op jit(solution)/shard_map/ppermute | solution.py:45
  72.8 6.4 %collective-permute-start.40 = (bf16[256,256]{1,0:T(8,128)(2,1)S(1)}, bf16[256,256]{1,0:T(8,128)(2,1)S(1)}, u32[]{:S(2)}, u32[]{:S(2)}) collective-permute-start(bf16[256,256]{1,0:T(8,128)(2,1)S(1)} %collective-permute-done.38.refs_2_.refs_5_), channel_id=1, source_target_pairs={{0,2},{4,0},{8,4},{12,8},{14,12},{10,14},{6,10},{2,6},{1,3},{5,1},... | collective-permute-start | bytes 393224 | tf_op jit(solution)/shard_map/ppermute | solution.py:45
  92.4 15.9 %collective-permute-start.46 = (f32[128,1024]{1,0:T(8,128)}, f32[128,1024]{1,0:T(8,128)}, u32[]{:S(2)}, u32[]{:S(2)}) collective-permute-start(f32[128,1024]{1,0:T(8,128)} %get-tuple-element.28), channel_id=1, source_target_pairs={{1,0},{3,2},{5,4},{7,6},{9,8},{11,10},{13,12},{15,14},{17,16},{19,... | collective-permute-start | bytes 1572872 | tf_op jit(solution)/shard_map/ppermute | solution.py:23
  96.3 6.9 %collective-permute-start.44 = (f32[256,128]{1,0:T(8,128)}, f32[256,128]{1,0:T(8,128)}, u32[]{:S(2)}, u32[]{:S(2)}) collective-permute-start(f32[256,128]{1,0:T(8,128)} %get-tuple-element.23), channel_id=1, source_target_pairs={{1,0},{3,2},{5,4},{7,6},{9,8},{11,10},{13,12},{15,14},{17,16},{19,... | collective-permute-start | bytes 393224 | tf_op jit(solution)/shard_map/ppermute | solution.py:23
  (37 other events, 280.8 us)

commit v3 on v0

v3 whole, which is shorter than its diff:
```python
import functools
import math

import jax
import jax.numpy as jnp
from jax import lax
from jax.experimental import pallas as pl
from jax.experimental.pallas import tpu as pltpu
from jax.sharding import PartitionSpec as P

F32 = jnp.float32
BF16 = jnp.bfloat16
OVER_ROWS = (((0,), (0,)), ((), ()))
OVER_COLS = (((1,), (1,)), ((), ()))
RING_LIMIT = 16
VMEM_BYTES = 24 * 1024 * 1024
PIECES = 8


def passed_along(shard, axis, by):
    size = lax.axis_size(axis)
    pairs = [(i, i + by) for i in range(size) if 0 <= i + by < size]
    return lax.ppermute(shard, axis, pairs)


def matmul(a, b, dims=(((1,), (0,)), ((), ()))):
    return lax.dot_general(a, b, dims, preferred_element_type=F32)


def ring_order(size):
    return [2 * p if p < size // 2 else 2 * (size - 1 - p) + 1 for p in range(size)]


def ring_member(place, size):
    place = lax.rem(place + 2 * size, size)
    return jnp.where(place < size // 2, 2 * place, 2 * (size - 1 - place) + 1)


def ring_place(member, size):
    return jnp.where(member % 2 == 0, member // 2, size - 1 - member // 2)


def hop(shard, way):
    size, layers = lax.axis_size("latent"), lax.axis_size("layer")
    order = ring_order(size)
    pairs = []
    for p in range(size):
        for layer in range(layers):
            by = way if layer % 2 == 0 else -way
            pairs.append((order[p] * layers + layer, order[(p + by) % size] * layers + layer))
    return lax.ppermute(shard, ("latent", "layer"), pairs)


def after(value, *others):
    return lax.optimization_barrier((value,) + others)[0]


def call(kernel, outs, flops, operands, spaces=None, out_spaces=None, scratch=(), aliases=None):
    def spec(space):
        return pl.BlockSpec(memory_space=space)

    spaces = spaces or [pltpu.VMEM] * (len(operands) - 1)
    out_spaces = out_spaces or [pltpu.VMEM] * len(outs)
    size = sum(math.prod(x.shape) * x.dtype.itemsize for x in list(operands) + list(outs))
    return pl.pallas_call(
        kernel,
        out_shape=outs,
        in_specs=[spec(pltpu.SMEM)] + [spec(space) for space in spaces],
        out_specs=[spec(space) for space in out_spaces],
        scratch_shapes=list(scratch),
        input_output_aliases=aliases or {},
        compiler_params=pltpu.CompilerParams(vmem_limit_bytes=VMEM_BYTES),
        cost_estimate=pl.CostEstimate(flops=flops, bytes_accessed=size, transcendentals=0),
    )(*operands)


def block_of(starts, slot, wide):
    return pl.ds(pl.multiple_of(starts[slot], wide), wide)


def encode_kernel(slots, last, starts, *refs):
    shards, (weight, before, *outs) = refs[:len(slots)], refs[len(slots):]
    total = jnp.broadcast_to(before[...], outs[0].shape)
    for slot, shard in zip(slots, shards):
        block = weight[0, block_of(starts, slot, shard.shape[1]), :]
        total = total + jnp.dot(shard[...], block, preferred_element_type=F32)
    outs[0][...] = total
    if last:
        outs[1][...] = jnp.maximum(total, 0.0).astype(BF16)


def turn_kernel(starts, *refs):
    *shards, turned = refs
    for slot, shard in enumerate(shards):
        turned[block_of(starts, slot, shard.shape[1]), :] = shard[...].T


def spread_kernel(slots, starts, codes, earlier, own_dec, cross, *outs):
    *partials, codes_t, earlier_t = outs
    both = jnp.concatenate([codes[...], earlier[...]], axis=1)
    for slot, partial in zip(slots, partials):
        at = block_of(starts, slot, partial.shape[1])
        block = jnp.concatenate([own_dec[0, :, at], cross[:, at]], axis=0)
        partial[...] = jnp.dot(both, block, preferred_element_type=F32).astype(partial.dtype)
    codes_t[...] = codes[...].T
    earlier_t[...] = earlier[...].T


def back_kernel(slots, first, starts, *refs):
    count = len(slots)
    shards, (codes_t, earlier_t, own_dec, cross), refs = refs[:count], refs[count:count + 4], refs[count + 4:]
    if not first:
        own_before, next_before = refs[:2]
        refs = refs[5:]
    back_own, back_next, same, low, high, stage, sems = refs
    wide = shards[0].shape[1]
    half_width = low.shape[1]
    own_total = 0.0 if first else own_before[...]
    next_total = 0.0 if first else next_before[...]
    for i, (slot, shard) in enumerate(zip(slots, shards)):
        start = pl.multiple_of(starts[slot], wide)
        error = shard[...]
        stage[0, i] = jnp.dot(codes_t[...], error, preferred_element_type=F32)
        pltpu.make_async_copy(stage.at[0, i], same.at[0, :, pl.ds(start, wide)], sems.at[0, i]).start()
        stage[1, i] = jnp.dot(earlier_t[...], error, preferred_element_type=F32)

        @pl.when(start < half_width)
        def _():
            pltpu.make_async_copy(stage.at[1, i], low.at[:, pl.ds(start, wide)], sems.at[1, i]).start()

        @pl.when(start >= half_width)
        def _():
            there = pl.multiple_of(start - half_width, wide)
            pltpu.make_async_copy(stage.at[1, i], high.at[:, pl.ds(there, wide)], sems.at[1, i]).start()

        at = pl.ds(start, wide)
        next_total = next_total + lax.dot_general(error, cross[:, at], OVER_COLS, preferred_element_type=F32)
        own_total = own_total + lax.dot_general(error, own_dec[0, :, at], OVER_COLS, preferred_element_type=F32)
    back_own[...] = own_total
    back_next[...] = next_total
    for i in range(count):
        pltpu.make_async_copy(stage.at[0, i], same.at[0, :, pl.ds(0, wide)], sems.at[0, i]).wait()
        pltpu.make_async_copy(stage.at[1, i], low.at[:, pl.ds(0, wide)], sems.at[1, i]).wait()


def finish_kernel(starts, turned, preact, back_own, from_next, returned, high, grad, bias, cross, stage, sems, cross_sem):
    pieces, height = stage.shape[:2]
    first = starts[starts.shape[0] - 1] == 0

    @pl.when(first)
    def _():
        pltpu.make_async_copy(returned, cross, cross_sem).start()

    @pl.when(jnp.logical_not(first))
    def _():
        pltpu.make_async_copy(high, cross, cross_sem).start()

    value = jnp.where(preact[...] > 0, back_own[...] + from_next[...], 0.0).astype(BF16)
    for i in range(pieces):
        rows = pl.ds(i * height, height)
        stage[i] = jnp.dot(turned[rows, :], value, preferred_element_type=F32)
        pltpu.make_async_copy(stage.at[i], grad.at[0, rows, :], sems.at[i]).start()
    bias[...] = jnp.sum(value.astype(F32), axis=0, keepdims=True)
    for i in range(pieces):
        pltpu.make_async_copy(stage.at[i], grad.at[0, pl.ds(i * height, height), :], sems.at[i]).wait()
    pltpu.make_async_copy(high, cross, cross_sem).wait()


def ring_shards(residual_in, targets, enc_weight, enc_bias, dec_same, dec_cross):
    size = lax.axis_size("latent")
    reach = size // 2
    place = ring_place(lax.axis_index("latent"), size)
    layer = lax.axis_index("layer")
    sign = jnp.where(layer % 2 == 0, 1, -1)
    rows, wide = residual_in.shape[1:]
    deep, lat = enc_weight.shape[1:]
    half_width = deep // 2
    err_scale = 1.0 / math.sqrt(rows)
    shape = jax.ShapeDtypeStruct
    unit = 2 * rows * wide * lat

    slot_p = {s: 2 * s - 1 for s in range(1, reach)}
    slot_q = {s: 2 * s for s in range(1, reach)}
    far = size - 1
    slot_p[reach] = far
    offsets = [0] * size
    for s in range(1, reach + 1):
        offsets[slot_p[s]] = -s
        if s < reach:
            offsets[slot_q[s]] = s
    starts = jnp.stack([ring_member(place + sign * offset, size) * wide for offset in offsets] + [layer])
    starts = starts.astype(jnp.int32)

    own = residual_in[0]
    inputs = [own] + [None] * (size - 1)
    inputs[slot_p[1]] = hop(own, 1)
    cross_full = lax.all_gather(dec_cross, "layer", axis=1, tiled=True)
    if reach > 1:
        inputs[slot_q[1]] = hop(after(own, cross_full), -1)
    for s in range(2, reach + 1):
        inputs[slot_p[s]] = hop(inputs[slot_p[s - 1]], 1)
        if s < reach:
            inputs[slot_q[s]] = hop(inputs[slot_q[s - 1]], -1)

    early = tuple(range(size - 1))
    part = call(
        functools.partial(encode_kernel, early, False),
        [shape((rows, lat), F32)],
        unit * len(early),
        [starts] + inputs[:-1] + [enc_weight, enc_bias],
    )[0]
    preact, codes = call(
        functools.partial(encode_kernel, (far,), True),
        [shape((rows, lat), F32), shape((rows, lat), BF16)],
        unit,
        [starts, inputs[far], enc_weight, part],
    )
    earlier = passed_along(codes, "layer", 1)

    def columns(array, slot):
        return lax.dynamic_slice_in_dim(array, starts[slot], wide, 1)

    message = (matmul(codes, columns(dec_same[0], far)) + matmul(earlier, columns(cross_full, far))).astype(BF16)
    ahead = hop(message, 1)
    spread = tuple([slot_p[s] for s in range(reach - 1, 0, -1)] + [slot_q[s] for s in range(reach - 1, 0, -1)] + [0])
    *partials, codes_t, earlier_t = call(
        functools.partial(spread_kernel, spread),
        [shape((rows, wide), BF16 if slot == slot_p.get(reach - 1) else F32) for slot in spread]
        + [shape((lat, rows), BF16)] * 2,
        2 * unit * len(spread),
        [starts, codes, earlier, dec_same, cross_full],
    )
    partial = dict(zip(spread, partials))
    turned = call(turn_kernel, [shape((deep, rows), BF16)], unit, [starts] + inputs)[0]
    total = partial[0]
    behind = None
    for s in range(reach - 1, 0, -1):
        going = partial[slot_p[s]]
        if behind is not None:
            going = (going + behind.astype(F32)).astype(BF16)
        behind = hop(going, -1)
        going = (partial[slot_q[s]] + ahead.astype(F32)).astype(BF16)
        if s == 1:
            going = after(going, turned)
        ahead = hop(going, 1)
    total = total + ahead.astype(F32)
    if behind is not None:
        total = total + behind.astype(F32)
    own_errors = ((total - targets[0].astype(F32)) * err_scale).astype(BF16)

    def back(slots, shards, before):
        count = len(slots)
        acc = shape((rows, lat), F32)
        outs = [acc, acc, shape((1, lat, deep), F32), shape((lat, half_width), F32), shape((lat, half_width), F32)]
        operands = [starts] + list(shards) + [codes_t, earlier_t, dec_same, cross_full]
        aliases = {}
        if before is not None:
            aliases = {len(operands) + 2 + i: 2 + i for i in range(3)}
            operands += list(before)
        spaces = [pltpu.VMEM] * (count + 4) + ([] if before is None else [pltpu.VMEM] * 2 + [pl.ANY] * 3)
        return call(
            functools.partial(back_kernel, slots, before is None),
            outs,
            4 * unit * count,
            operands,
            spaces=spaces,
            out_spaces=[pltpu.VMEM] * 2 + [pl.ANY] * 3,
            scratch=[pltpu.VMEM((2, count, lat, wide), F32), pltpu.SemaphoreType.DMA((2, count))],
            aliases=aliases,
        )

    ahead = hop(own_errors, 1)
    done = back((0,), [own_errors], None)
    if reach > 1:
        behind = hop(after(own_errors, done[0]), -1)
    pending = []
    for s in range(1, reach):
        pending += [(slot_p[s], ahead), (slot_q[s], behind)]
        following = after(ahead, done[0])
        if s % 2 == 0 or s == reach - 1:
            done = back(tuple(slot for slot, _ in pending), [shard for _, shard in pending], done)
            pending = []
        ahead = hop(following, 1)
        if s < reach - 1:
            behind = hop(behind, -1)
    back_own, back_next, grad_same, low, high = back((far,), [ahead], done)
    from_next = passed_along(back_next, "layer", -1)
    returned = passed_along(low, "layer", -1)
    height = deep // PIECES
    grad_enc, grad_bias, grad_cross = call(
        finish_kernel,
        [shape((1, deep, lat), F32), shape((1, lat), F32), shape((lat, half_width), F32)],
        unit * size,
        [starts, turned, preact, back_own, from_next, returned, high],
        spaces=[pltpu.VMEM] * 4 + [pl.ANY] * 2,
        out_spaces=[pl.ANY, pltpu.VMEM, pl.ANY],
        scratch=[
            pltpu.VMEM((PIECES, height, lat), F32),
            pltpu.SemaphoreType.DMA((PIECES,)),
            pltpu.SemaphoreType.DMA,
        ],
    )
    return (grad_enc, grad_bias, grad_same, grad_cross)


def wide_shards(residual_in, targets, enc_weight, enc_bias, dec_same, dec_cross):
    is_first = lax.axis_index("layer") == 0
    err_scale = 1.0 / math.sqrt(residual_in.shape[1])
    inputs = lax.all_gather(residual_in[0], "latent", axis=1, tiled=True)
    preact = matmul(inputs, enc_weight[0]) + enc_bias[0]
    codes_now = jnp.maximum(preact, 0.0).astype(BF16)
    earlier = passed_along(codes_now, "layer", 1)
    cross_full = lax.all_gather(dec_cross, "layer", axis=1, tiled=True)
    own_dec = dec_same[0]
    half_width = own_dec.shape[1] // 2
    recon_full = lax.psum(matmul(codes_now, own_dec) + matmul(earlier, cross_full), "latent")
    wanted = lax.all_gather(targets[0], "latent", axis=1, tiled=True)
    errors = ((recon_full - wanted.astype(F32)) * err_scale).astype(BF16)
    grad_same = matmul(codes_now, errors, OVER_ROWS)
    grad_full = matmul(earlier, errors, OVER_ROWS)
    returned = passed_along(grad_full[:, :half_width], "layer", -1)
    grad_cross = jnp.where(is_first, returned, grad_full[:, half_width:])
    from_next = passed_along(matmul(errors, cross_full, OVER_COLS), "layer", -1)
    grad_codes = matmul(errors, own_dec, OVER_COLS) + from_next
    grad_pre = jnp.where(preact > 0, grad_codes, 0.0).astype(BF16)
    grad_enc = matmul(inputs, grad_pre, OVER_ROWS)
    grad_bias = jnp.sum(grad_pre.astype(F32), axis=0)
    return (grad_enc[None], grad_bias[None], grad_same[None], grad_cross)


def solution(mesh):
    size = mesh.shape["latent"]
    placed = (
        P("layer", "groups", "latent"),
        P("layer", "groups", "latent"),
        P("layer", None, "latent"),
        P("layer", "latent"),
        P("layer", "latent", None),
        P("latent", "layer"),
    )
    return jax.shard_map(
        ring_shards if size % 2 == 0 and size <= RING_LIMIT else wide_shards,
        mesh=mesh,
        in_specs=placed,
        out_specs=(
            P(("groups", "layer"), None, "latent"),
            P(("groups", "layer"), "latent"),
            P(("groups", "layer"), "latent", None),
            P(("groups", "latent"), "layer"),
        ),
        check_vma=False,
    )
```

time: 295 us -> 112 us (0.38)
  waiting for transfers between devices: 256 us -> 58.6 us
  starting transfers between devices: 3.98 us -> 31.8 us
  Pallas kernels: 0 us -> 14.5 us
  between operations: 13.8 us -> 0.83 us
  matrix products: 10.2 us -> 0.42 us
  other arithmetic: 4.43 us -> 0.46 us
    psum x1 -> x0, waiting for transfers between devices: 158 us -> none  [shards(): recon_full = lax.psum(partial_value, 'latent')]
    all_gather x2 -> x0, waiting for transfers between devices: 96.6 us -> none  [the longest x1 52.7 us: shards(): inputs = lax.all_gather(residual_in[0], 'latent', axis=1, tiled=True)]
    ppermute x0 -> x21, waiting for transfers between devices: none -> 55.5 us  [hop(): return lax.ppermute(shard, ('latent', 'layer'), pairs)]
    ppermute x0 -> x21, starting transfers between devices: none -> 27.9 us  [hop(): return lax.ppermute(shard, ('latent', 'layer'), pairs)]
    pallas_call x0 -> x9, Pallas kernels: none -> 14.5 us  [call(): pl.pallas_call(kernel, out_shape=outs, in_specs=[spec(pltpu.SMEM)] + [spe...]
    dot_general x8 -> x2, matrix products: 10.2 us -> 0.42 us  [matmul(): return lax.dot_general(a, b, dims, preferred_element_type=F32)]
    convert_element_type x1 -> x6, other arithmetic: 3.58 us -> 0.46 us  [the longest x3 0.17 us: ring_shards(): going = (partial[slot_q[s]] + ahead.astype(F32)).astype(BF16)]
  transfers between devices with their start and end apart: 6 -> 24, of which waited for: 4 -> 18; matrix products, arithmetic and copies ran while one was open for 4% -> 0% of each run, Pallas kernels for 0% -> 9%
where the time goes in v3:
time: 112 us
  waiting for transfers between devices  58.6 us (52%)
  starting transfers between devices  31.8 us (28%)
  Pallas kernels  14.5 us (13%)
  local copies, waits for them, and re-layouts  2.75 us (2%)
  blocking collectives  2.38 us (2%)
    ppermute x21, waiting for transfers between devices, hop(): return lax.ppermute(shard, ('latent', 'layer'), pairs)  55.5 us
    ppermute x21, starting transfers between devices, hop(): return lax.ppermute(shard, ('latent', 'layer'), pairs)  27.9 us
    pallas_call x9, Pallas kernels, call(): pl.pallas_call(kernel, out_shape=outs, in_specs=[spec(pltpu.SMEM)] + [spe...  14.5 us
    ppermute x3, starting transfers between devices, passed_along(): return lax.ppermute(shard, axis, pairs)  3.88 us
    ppermute x3, waiting for transfers between devices, passed_along(): return lax.ppermute(shard, axis, pairs)  3.12 us
    unnamed x12, local copies, waits for them, and re-layouts  2.66 us
    all_gather x1, blocking collectives, ring_shards(): cross_full = lax.all_gather(dec_cross, 'layer', axis=1, tiled=True)  2.38 us
  transfers between devices with their start and end apart: 24, of which 18 were waited for; matrix products, arithmetic and copies ran while one was open for 0% of the time, Pallas kernels for 9%

profile of v3, /device:TPU:0, one launch (start us, length us, event | category | flops | bytes accessed | tf_op | source)
XLA Modules:
  0.0 111.7 jit_solution(8859327019612085474)
XLA Ops:
  0.6 3.1 %collective-permute-start = (bf16[512,256]{1,0:T(8,128)(2,1)}, bf16[512,256]{1,0:T(8,128)(2,1)S(1)}, u32[]{:S(2)}, u32[]{:S(2)}) collective-permute-start(bf16[512,256]{1,0:T(8,128)(2,1)} %bitcast.18), channel_id=1, source_target_pairs={{0,4},{1,3},{4,8},{5,1},{8,12},{9,5},{12,14},{13,9},{14,10},{15,13... | collective-permute-start | bytes 786440 | tf_op jit(solution)/shard_map/ppermute | solution.py:51
  3.7 2.4 %all_gather.3.cross.refs_4_.refs_7_.refs_5_ = bf16[128,2048]{1,0:T(8,128)(2,1)S(1)} all-gather(bf16[128,1024]{1,0:T(8,128)(2,1)} %param.11), channel_id=1, replica_groups=mesh['groups'=2,'latent'=8,'layer'=2] {'layer'}, dimensions={1}, use_global_device_ids=true | all-gather | bytes 786432 | tf_op jit(solution)/shard_map/all_gather | solution.py:197
  6.8 1.4 %collective-permute-done.refs_1_ = bf16[512,256]{1,0:T(8,128)(2,1)S(1)} collective-permute-done((bf16[512,256]{1,0:T(8,128)(2,1)}, bf16[512,256]{1,0:T(8,128)(2,1)S(1)}, u32[]{:S(2)}, u32[]{:S(2)}) %collective-permute-start) | collective-permute-done | bytes 262176 | tf_op jit(solution)/shard_map/ppermute | solution.py:51
  8.2 2.1 %collective-permute-start.2 = (bf16[512,256]{1,0:T(8,128)(2,1)S(1)}, bf16[512,256]{1,0:T(8,128)(2,1)S(1)}, u32[]{:S(2)}, u32[]{:S(2)}) collective-permute-start(bf16[512,256]{1,0:T(8,128)(2,1)S(1)} %collective-permute-done.refs_1_), channel_id=1, source_target_pairs={{0,4},{1,3},{4,8},{5,1},{8,12},{9,5},{12,14},{13,9},{14,10},{15,13... | collective-permute-start | bytes 786440 | tf_op jit(solution)/shard_map/ppermute | solution.py:51
  10.3 4.9 %collective-permute-done.1.refs_2_ = bf16[512,256]{1,0:T(8,128)(2,1)S(1)} collective-permute-done((bf16[512,256]{1,0:T(8,128)(2,1)}, bf16[512,256]{1,0:T(8,128)(2,1)S(1)}, u32[]{:S(2)}, u32[]{:S(2)}) %collective-permute-start.1) | collective-permute-done | bytes 262176 | tf_op jit(solution)/shard_map/ppermute | solution.py:51
  15.2 2.0 %collective-permute-start.4 = (bf16[512,256]{1,0:T(8,128)(2,1)S(1)}, bf16[512,256]{1,0:T(8,128)(2,1)S(1)}, u32[]{:S(2)}, u32[]{:S(2)}) collective-permute-start(bf16[512,256]{1,0:T(8,128)(2,1)S(1)} %collective-permute-done.2.refs_3_), channel_id=1, source_target_pairs={{0,4},{1,3},{4,8},{5,1},{8,12},{9,5},{12,14},{13,9},{14,10},{15,13... | collective-permute-start | bytes 786440 | tf_op jit(solution)/shard_map/ppermute | solution.py:51
  17.2 6.4 %collective-permute-done.3.refs_4_ = bf16[512,256]{1,0:T(8,128)(2,1)S(1)} collective-permute-done((bf16[512,256]{1,0:T(8,128)(2,1)S(1)}, bf16[512,256]{1,0:T(8,128)(2,1)S(1)}, u32[]{:S(2)}, u32[]{:S(2)}) %collective-permute-start.3) | collective-permute-done | bytes 262176 | tf_op jit(solution)/shard_map/ppermute | solution.py:51
  24.3 1.3 %collective-permute-start.6 = (bf16[512,256]{1,0:T(8,128)(2,1)S(1)}, bf16[512,256]{1,0:T(8,128)(2,1)S(1)}, u32[]{:S(2)}, u32[]{:S(2)}) collective-permute-start(bf16[512,256]{1,0:T(8,128)(2,1)S(1)} %collective-permute-done.4.refs_5_), channel_id=1, source_target_pairs={{0,4},{1,3},{4,8},{5,1},{8,12},{9,5},{12,14},{13,9},{14,10},{15,13... | collective-permute-start | bytes 786440 | tf_op jit(solution)/shard_map/ppermute | solution.py:51
  25.8 5.8 %collective-permute-done.5.refs_6_ = bf16[512,256]{1,0:T(8,128)(2,1)S(1)} collective-permute-done((bf16[512,256]{1,0:T(8,128)(2,1)S(1)}, bf16[512,256]{1,0:T(8,128)(2,1)S(1)}, u32[]{:S(2)}, u32[]{:S(2)}) %collective-permute-start.5) | collective-permute-done | bytes 262176 | tf_op jit(solution)/shard_map/ppermute | solution.py:51
  36.1 1.3 %collective-permute-start.7 = (bf16[512,128]{1,0:T(8,128)(2,1)S(1)}, bf16[512,128]{1,0:T(8,128)(2,1)S(1)}, u32[]{:S(2)}, u32[]{:S(2)}) collective-permute-start(bf16[512,128]{1,0:T(8,128)(2,1)S(1)} %get-tuple-element.46.codes), channel_id=1, source_target_pairs={{0,1},{2,3},{4,5},{6,7},{8,9},{10,11},{12,13},{14,15},{16,17},{18,... | collective-permute-start | bytes 393224 | tf_op jit(solution)/shard_map/ppermute | solution.py:23
  38.9 1.8 %collective-permute-start.8 = (bf16[512,256]{1,0:T(8,128)(2,1)S(1)}, bf16[512,256]{1,0:T(8,128)(2,1)S(1)}, u32[]{:S(2)}, u32[]{:S(2)}) collective-permute-start(bf16[512,256]{1,0:T(8,128)(2,1)S(1)} %fusion), channel_id=1, source_target_pairs={{0,4},{1,3},{4,8},{5,1},{8,12},{9,5},{12,14},{13,9},{14,10},{15,13... | collective-permute-start | bytes 786440 | tf_op jit(solution)/shard_map/ppermute | solution.py:51
  42.2 4.6 %collective-permute-done.8 = bf16[512,256]{1,0:T(8,128)(2,1)S(1)} collective-permute-done((bf16[512,256]{1,0:T(8,128)(2,1)S(1)}, bf16[512,256]{1,0:T(8,128)(2,1)S(1)}, u32[]{:S(2)}, u32[]{:S(2)}) %collective-permute-start.8) | collective-permute-done | bytes 262176 | tf_op jit(solution)/shard_map/ppermute | solution.py:51
  46.9 2.5 %collective-permute-start.9 = (bf16[512,256]{1,0:T(8,128)(2,1)S(1)}, bf16[512,256]{1,0:T(8,128)(2,1)S(1)}, u32[]{:S(2)}, u32[]{:S(2)}) collective-permute-start(bf16[512,256]{1,0:T(8,128)(2,1)S(1)} %add_convert_fusion.4), channel_id=1, source_target_pairs={{0,4},{1,3},{4,8},{5,1},{8,12},{9,5},{12,14},{13,9},{14,10},{15,13... | collective-permute-start | bytes 786440 | tf_op jit(solution)/shard_map/ppermute | solution.py:51
  49.5 6.3 %collective-permute-done.9 = bf16[512,256]{1,0:T(8,128)(2,1)S(1)} collective-permute-done((bf16[512,256]{1,0:T(8,128)(2,1)S(1)}, bf16[512,256]{1,0:T(8,128)(2,1)S(1)}, u32[]{:S(2)}, u32[]{:S(2)}) %collective-permute-start.9) | collective-permute-done | bytes 262176 | tf_op jit(solution)/shard_map/ppermute | solution.py:51
  55.9 2.5 %collective-permute-start.10 = (bf16[512,256]{1,0:T(8,128)(2,1)S(1)}, bf16[512,256]{1,0:T(8,128)(2,1)S(1)}, u32[]{:S(2)}, u32[]{:S(2)}) collective-permute-start(bf16[512,256]{1,0:T(8,128)(2,1)S(1)} %add_convert_fusion.3), channel_id=1, source_target_pairs={{0,4},{1,3},{4,8},{5,1},{8,12},{9,5},{12,14},{13,9},{14,10},{15,13... | collective-permute-start | bytes 786440 | tf_op jit(solution)/shard_map/ppermute | solution.py:51
  59.7 4.8 %collective-permute-done.10 = bf16[512,256]{1,0:T(8,128)(2,1)S(1)} collective-permute-done((bf16[512,256]{1,0:T(8,128)(2,1)S(1)}, bf16[512,256]{1,0:T(8,128)(2,1)S(1)}, u32[]{:S(2)}, u32[]{:S(2)}) %collective-permute-start.10) | collective-permute-done | bytes 262176 | tf_op jit(solution)/shard_map/ppermute | solution.py:51
  64.6 2.0 %collective-permute-start.11 = (bf16[512,256]{1,0:T(8,128)(2,1)S(1)}, bf16[512,256]{1,0:T(8,128)(2,1)S(1)}, u32[]{:S(2)}, u32[]{:S(2)}) collective-permute-start(bf16[512,256]{1,0:T(8,128)(2,1)S(1)} %add_convert_fusion.2), channel_id=1, source_target_pairs={{0,4},{1,3},{4,8},{5,1},{8,12},{9,5},{12,14},{13,9},{14,10},{15,13... | collective-permute-start | bytes 786440 | tf_op jit(solution)/shard_map/ppermute | solution.py:51
  66.9 5.8 %collective-permute-done.11 = bf16[512,256]{1,0:T(8,128)(2,1)S(1)} collective-permute-done((bf16[512,256]{1,0:T(8,128)(2,1)S(1)}, bf16[512,256]{1,0:T(8,128)(2,1)S(1)}, u32[]{:S(2)}, u32[]{:S(2)}) %collective-permute-start.11) | collective-permute-done | bytes 262176 | tf_op jit(solution)/shard_map/ppermute | solution.py:51
  72.8 2.5 %collective-permute-start.15 = (bf16[512,256]{1,0:T(8,128)(2,1)S(1)}, bf16[512,256]{1,0:T(8,128)(2,1)S(1)}, u32[]{:S(2)}, u32[]{:S(2)}) collective-permute-start(bf16[512,256]{1,0:T(8,128)(2,1)S(1)} %fusion.2.refs_0_), channel_id=1, source_target_pairs={{0,4},{1,3},{4,8},{5,1},{8,12},{9,5},{12,14},{13,9},{14,10},{15,13... | collective-permute-start | bytes 786440 | tf_op jit(solution)/shard_map/ppermute | solution.py:51
  75.3 1.4 %shard_map.97 = (f32[512,128]{1,0:T(8,128)S(1)}, f32[512,128]{1,0:T(8,128)S(1)}, f32[1,128,2048]{2,1,0:T(8,128)}, f32[128,1024]{1,0:T(8,128)S(1)}, f32[128,1024]{1,0:T(8,128)S(1)}) custom-call(s32[9]{0:T(128)S(1)} %stack.39.starts, bf16[512,256]{1,0:T(8,128)(2,1)S(1)} %fusion.2.refs_0_, bf16[128,512]{1,0:T(8,128)(2,1)S(1)} %get-tuple-element.55.refs_1_.refs_4_.refs_2_, ...), custom_call_target="tpu_custom_call" | custom-call | flops 134217728 | bytes 4194340 | tf_op jit(solution)/shard_map/pallas_call | solution.py:65
  76.8 5.0 %collective-permute-done.15.refs_0_ = bf16[512,256]{1,0:T(8,128)(2,1)S(1)} collective-permute-done((bf16[512,256]{1,0:T(8,128)(2,1)S(1)}, bf16[512,256]{1,0:T(8,128)(2,1)S(1)}, u32[]{:S(2)}, u32[]{:S(2)}) %collective-permute-start.15) | collective-permute-done | bytes 262176 | tf_op jit(solution)/shard_map/ppermute | solution.py:51
  81.9 2.0 %collective-permute-start.16 = (bf16[512,256]{1,0:T(8,128)(2,1)S(1)}, bf16[512,256]{1,0:T(8,128)(2,1)S(1)}, u32[]{:S(2)}, u32[]{:S(2)}) collective-permute-start(bf16[512,256]{1,0:T(8,128)(2,1)S(1)} %collective-permute-done.15.refs_0_), channel_id=1, source_target_pairs={{0,4},{1,3},{4,8},{5,1},{8,12},{9,5},{12,14},{13,9},{14,10},{15,13... | collective-permute-start | bytes 786440 | tf_op jit(solution)/shard_map/ppermute | solution.py:51
  84.6 5.5 %collective-permute-done.16.refs_2_ = bf16[512,256]{1,0:T(8,128)(2,1)S(1)} collective-permute-done((bf16[512,256]{1,0:T(8,128)(2,1)S(1)}, bf16[512,256]{1,0:T(8,128)(2,1)S(1)}, u32[]{:S(2)}, u32[]{:S(2)}) %collective-permute-start.16) | collective-permute-done | bytes 262176 | tf_op jit(solution)/shard_map/ppermute | solution.py:51
  90.1 1.5 %collective-permute-start.17 = (bf16[512,256]{1,0:T(8,128)(2,1)S(1)}, bf16[512,256]{1,0:T(8,128)(2,1)S(1)}, u32[]{:S(2)}, u32[]{:S(2)}) collective-permute-start(bf16[512,256]{1,0:T(8,128)(2,1)S(1)} %collective-permute-done.16.refs_2_), channel_id=1, source_target_pairs={{0,4},{1,3},{4,8},{5,1},{8,12},{9,5},{12,14},{13,9},{14,10},{15,13... | collective-permute-start | bytes 786440 | tf_op jit(solution)/shard_map/ppermute | solution.py:51
  92.9 2.7 %shard_map.98 = (f32[512,128]{1,0:T(8,128)S(1)}, f32[512,128]{1,0:T(8,128)S(1)}, f32[1,128,2048]{2,1,0:T(8,128)}, f32[128,1024]{1,0:T(8,128)S(1)}, f32[128,1024]{1,0:T(8,128)S(1)}) custom-call(s32[9]{0:T(128)S(1)} %stack.39.starts, ...), custom_call_target="tpu_custom_call", output_to_operand_aliasing={{2}: (11, {}), {3}: (12, {}), {4}: (13, {})} | custom-call | flops 536870912 | bytes 7602212 | tf_op jit(solution)/shard_map/pallas_call | solution.py:65
  96.4 1.5 %collective-permute-start.20 = (bf16[512,256]{1,0:T(8,128)(2,1)S(1)}, bf16[512,256]{1,0:T(8,128)(2,1)S(1)}, u32[]{:S(2)}, u32[]{:S(2)}) collective-permute-start(bf16[512,256]{1,0:T(8,128)(2,1)S(1)} %collective-permute-done.17.refs_0_), channel_id=1, source_target_pairs={{0,4},{1,3},{4,8},{5,1},{8,12},{9,5},{12,14},{13,9},{14,10},{15,13... | collective-permute-start | bytes 786440 | tf_op jit(solution)/shard_map/ppermute | solution.py:51
  98.7 1.9 %shard_map.99 = (f32[512,128]{1,0:T(8,128)S(1)}, f32[512,128]{1,0:T(8,128)S(1)}, f32[1,128,2048]{2,1,0:T(8,128)}, f32[128,1024]{1,0:T(8,128)S(1)}, f32[128,1024]{1,0:T(8,128)S(1)}) custom-call(s32[9]{0:T(128)S(1)} %stack.39.starts, ...), custom_call_target="tpu_custom_call", output_to_operand_aliasing={{2}: (9, {}), {3}: (10, {}), {4}: (11, {})} | custom-call | flops 268435456 | bytes 7077924 | tf_op jit(solution)/shard_map/pallas_call | solution.py:65
  100.6 2.2 %collective-permute-done.20.refs_0_ = bf16[512,256]{1,0:T(8,128)(2,1)S(1)} collective-permute-done((bf16[512,256]{1,0:T(8,128)(2,1)S(1)}, bf16[512,256]{1,0:T(8,128)(2,1)S(1)}, u32[]{:S(2)}, u32[]{:S(2)}) %collective-permute-start.20) | collective-permute-done | bytes 262176 | tf_op jit(solution)/shard_map/ppermute | solution.py:51
  102.8 1.5 %shard_map.100 = (f32[512,128]{1,0:T(8,128)S(1)}, f32[512,128]{1,0:T(8,128)S(1)}, f32[1,128,2048]{2,1,0:T(8,128)}, f32[128,1024]{1,0:T(8,128)S(1)}, f32[128,1024]{1,0:T(8,128)S(1)}) custom-call(s32[9]{0:T(128)S(1)} %stack.39.starts, ...), custom_call_target="tpu_custom_call", output_to_operand_aliasing={{2}: (8, {}), {3}: (9, {}), {4}: (10, {})} | custom-call | flops 134217728 | bytes 6815780 | tf_op jit(solution)/shard_map/pallas_call | solution.py:65
  104.3 1.3 %collective-permute-start.23 = (f32[128,1024]{1,0:T(8,128)S(1)}, f32[128,1024]{1,0:T(8,128)S(1)}, u32[]{:S(2)}, u32[]{:S(2)}) collective-permute-start(f32[128,1024]{1,0:T(8,128)S(1)} %get-tuple-element.78), channel_id=1, source_target_pairs={{1,0},{3,2},{5,4},{7,6},{9,8},{11,10},{13,12},{15,14},{17,16},{19,... | collective-permute-start | bytes 1572872 | tf_op jit(solution)/shard_map/ppermute | solution.py:23
  106.9 2.2 %collective-permute-done.22.from_next = f32[512,128]{1,0:T(8,128)S(1)} collective-permute-done((f32[512,128]{1,0:T(8,128)S(1)}, f32[512,128]{1,0:T(8,128)S(1)}, u32[]{:S(2)}, u32[]{:S(2)}) %collective-permute-start.22) | collective-permute-done | bytes 262176 | tf_op jit(solution)/shard_map/ppermute | solution.py:23
  109.1 2.7 %shard_map.101 = (f32[1,2048,128]{2,1,0:T(8,128)}, f32[1,128]{1,0:T(1,128)}, f32[128,1024]{1,0:T(8,128)}) custom-call(s32[9]{0:T(128)S(1)} %stack.39.starts, bf16[2048,512]{1,0:T(8,128)(2,1)S(1)} %shard_map.93.turned, f32[512,128]{1,0:T(8,128)S(1)} %get-tuple-element.45.preact, f32[512,128]{1,0:T(8,128)S(1)} %get-tuple-element.76.back_own, ...), custom_call_target="tpu_custom_call" | custom-call | flops 268435456 | bytes 5505572 | tf_op jit(solution)/shard_map/pallas_call | solution.py:65
  (47 shorter events, 16.0 us)
Async XLA Ops:
  0.6 7.6 %collective-permute-start = (bf16[512,256]{1,0:T(8,128)(2,1)}, bf16[512,256]{1,0:T(8,128)(2,1)S(1)}, u32[]{:S(2)}, u32[]{:S(2)}) collective-permute-start(bf16[512,256]{1,0:T(8,128)(2,1)} %bitcast.18), channel_id=1, source_target_pairs={{0,4},{1,3},{4,8},{5,1},{8,12},{9,5},{12,14},{13,9},{14,10},{15,13... | collective-permute-start | bytes 786440 | tf_op jit(solution)/shard_map/ppermute | solution.py:51
  6.1 9.1 %collective-permute-start.1 = (bf16[512,256]{1,0:T(8,128)(2,1)}, bf16[512,256]{1,0:T(8,128)(2,1)S(1)}, u32[]{:S(2)}, u32[]{:S(2)}) collective-permute-start(bf16[512,256]{1,0:T(8,128)(2,1)} %bitcast.19), channel_id=1, source_target_pairs={{0,2},{1,5},{4,0},{5,9},{8,4},{9,13},{12,8},{13,15},{14,12},{15,11... | collective-permute-start | bytes 786440 | tf_op jit(solution)/shard_map/ppermute | solution.py:51
  8.2 7.0 %collective-permute-start.2 = (bf16[512,256]{1,0:T(8,128)(2,1)S(1)}, bf16[512,256]{1,0:T(8,128)(2,1)S(1)}, u32[]{:S(2)}, u32[]{:S(2)}) collective-permute-start(bf16[512,256]{1,0:T(8,128)(2,1)S(1)} %collective-permute-done.refs_1_), channel_id=1, source_target_pairs={{0,4},{1,3},{4,8},{5,1},{8,12},{9,5},{12,14},{13,9},{14,10},{15,13... | collective-permute-start | bytes 786440 | tf_op jit(solution)/shard_map/ppermute | solution.py:51
  15.2 8.4 %collective-permute-start.3 = (bf16[512,256]{1,0:T(8,128)(2,1)S(1)}, bf16[512,256]{1,0:T(8,128)(2,1)S(1)}, u32[]{:S(2)}, u32[]{:S(2)}) collective-permute-start(bf16[512,256]{1,0:T(8,128)(2,1)S(1)} %collective-permute-done.1.refs_2_), channel_id=1, source_target_pairs={{0,2},{1,5},{4,0},{5,9},{8,4},{9,13},{12,8},{13,15},{14,12},{15,11... | collective-permute-start | bytes 786440 | tf_op jit(solution)/shard_map/ppermute | solution.py:51
  15.2 9.1 %collective-permute-start.4 = (bf16[512,256]{1,0:T(8,128)(2,1)S(1)}, bf16[512,256]{1,0:T(8,128)(2,1)S(1)}, u32[]{:S(2)}, u32[]{:S(2)}) collective-permute-start(bf16[512,256]{1,0:T(8,128)(2,1)S(1)} %collective-permute-done.2.refs_3_), channel_id=1, source_target_pairs={{0,4},{1,3},{4,8},{5,1},{8,12},{9,5},{12,14},{13,9},{14,10},{15,13... | collective-permute-start | bytes 786440 | tf_op jit(solution)/shard_map/ppermute | solution.py:51
  23.6 7.9 %collective-permute-start.5 = (bf16[512,256]{1,0:T(8,128)(2,1)S(1)}, bf16[512,256]{1,0:T(8,128)(2,1)S(1)}, u32[]{:S(2)}, u32[]{:S(2)}) collective-permute-start(bf16[512,256]{1,0:T(8,128)(2,1)S(1)} %collective-permute-done.3.refs_4_), channel_id=1, source_target_pairs={{0,2},{1,5},{4,0},{5,9},{8,4},{9,13},{12,8},{13,15},{14,12},{15,11... | collective-permute-start | bytes 786440 | tf_op jit(solution)/shard_map/ppermute | solution.py:51
  24.3 11.0 %collective-permute-start.6 = (bf16[512,256]{1,0:T(8,128)(2,1)S(1)}, bf16[512,256]{1,0:T(8,128)(2,1)S(1)}, u32[]{:S(2)}, u32[]{:S(2)}) collective-permute-start(bf16[512,256]{1,0:T(8,128)(2,1)S(1)} %collective-permute-done.4.refs_5_), channel_id=1, source_target_pairs={{0,4},{1,3},{4,8},{5,1},{8,12},{9,5},{12,14},{13,9},{14,10},{15,13... | collective-permute-start | bytes 786440 | tf_op jit(solution)/shard_map/ppermute | solution.py:51
  25.8 12.9 %copy-start = (bf16[1,128,2048]{2,1,0:T(8,128)(2,1)S(1)}, bf16[1,128,2048]{2,1,0:T(8,128)(2,1)}, u32[]{:S(2)}) copy-start(bf16[1,128,2048]{2,1,0:T(8,128)(2,1)} %refs_3_.3) | copy-start | bytes 1572868
  31.5 1.0 copy-start.1
  32.6 0.9 copy-start.2
  33.5 0.7 copy-start.4
  36.1 2.3 %collective-permute-start.7 = (bf16[512,128]{1,0:T(8,128)(2,1)S(1)}, bf16[512,128]{1,0:T(8,128)(2,1)S(1)}, u32[]{:S(2)}, u32[]{:S(2)}) collective-permute-start(bf16[512,128]{1,0:T(8,128)(2,1)S(1)} %get-tuple-element.46.codes), channel_id=1, source_target_pairs={{0,1},{2,3},{4,5},{6,7},{8,9},{10,11},{12,13},{14,15},{16,17},{18,... | collective-permute-start | bytes 393224 | tf_op jit(solution)/shard_map/ppermute | solution.py:23
  38.9 19.6 %copy-start.3 = (bf16[1,512,256]{2,1,0:T(8,128)(2,1)S(1)}, bf16[1,512,256]{2,1,0:T(8,128)(2,1)}, u32[]{:S(2)}) copy-start(bf16[1,512,256]{2,1,0:T(8,128)(2,1)} %param.6) | copy-start | bytes 786436
  38.9 7.9 %collective-permute-start.8 = (bf16[512,256]{1,0:T(8,128)(2,1)S(1)}, bf16[512,256]{1,0:T(8,128)(2,1)S(1)}, u32[]{:S(2)}, u32[]{:S(2)}) collective-permute-start(bf16[512,256]{1,0:T(8,128)(2,1)S(1)} %fusion), channel_id=1, source_target_pairs={{0,4},{1,3},{4,8},{5,1},{8,12},{9,5},{12,14},{13,9},{14,10},{15,13... | collective-permute-start | bytes 786440 | tf_op jit(solution)/shard_map/ppermute | solution.py:51
  41.9 7.5 %collective-permute-start.12 = (bf16[512,256]{1,0:T(8,128)(2,1)S(1)}, bf16[512,256]{1,0:T(8,128)(2,1)S(1)}, u32[]{:S(2)}, u32[]{:S(2)}) collective-permute-start(bf16[512,256]{1,0:T(8,128)(2,1)S(1)} %get-tuple-element.54), channel_id=1, source_target_pairs={{0,2},{1,5},{4,0},{5,9},{8,4},{9,13},{12,8},{13,15},{14,12},{15,11... | collective-permute-start | bytes 786440 | tf_op jit(solution)/shard_map/ppermute | solution.py:51
  46.9 9.0 %collective-permute-start.9 = (bf16[512,256]{1,0:T(8,128)(2,1)S(1)}, bf16[512,256]{1,0:T(8,128)(2,1)S(1)}, u32[]{:S(2)}, u32[]{:S(2)}) collective-permute-start(bf16[512,256]{1,0:T(8,128)(2,1)S(1)} %add_convert_fusion.4), channel_id=1, source_target_pairs={{0,4},{1,3},{4,8},{5,1},{8,12},{9,5},{12,14},{13,9},{14,10},{15,13... | collective-permute-start | bytes 786440 | tf_op jit(solution)/shard_map/ppermute | solution.py:51
  49.5 10.1 %collective-permute-start.13 = (bf16[512,256]{1,0:T(8,128)(2,1)S(1)}, bf16[512,256]{1,0:T(8,128)(2,1)S(1)}, u32[]{:S(2)}, u32[]{:S(2)}) collective-permute-start(bf16[512,256]{1,0:T(8,128)(2,1)S(1)} %add_convert_fusion.1), channel_id=1, source_target_pairs={{0,2},{1,5},{4,0},{5,9},{8,4},{9,13},{12,8},{13,15},{14,12},{15,11... | collective-permute-start | bytes 786440 | tf_op jit(solution)/shard_map/ppermute | solution.py:51
  55.9 8.7 %collective-permute-start.10 = (bf16[512,256]{1,0:T(8,128)(2,1)S(1)}, bf16[512,256]{1,0:T(8,128)(2,1)S(1)}, u32[]{:S(2)}, u32[]{:S(2)}) collective-permute-start(bf16[512,256]{1,0:T(8,128)(2,1)S(1)} %add_convert_fusion.3), channel_id=1, source_target_pairs={{0,4},{1,3},{4,8},{5,1},{8,12},{9,5},{12,14},{13,9},{14,10},{15,13... | collective-permute-start | bytes 786440 | tf_op jit(solution)/shard_map/ppermute | solution.py:51
  59.6 13.1 %copy-start.5 = (bf16[1,512,256]{2,1,0:T(8,128)(2,1)S(1)}, bf16[1,512,256]{2,1,0:T(8,128)(2,1)}, u32[]{:S(2)}) copy-start(bf16[1,512,256]{2,1,0:T(8,128)(2,1)} %param.7) | copy-start | bytes 786436
  59.7 7.2 %collective-permute-start.14 = (bf16[512,256]{1,0:T(8,128)(2,1)S(1)}, bf16[512,256]{1,0:T(8,128)(2,1)S(1)}, u32[]{:S(2)}, u32[]{:S(2)}) collective-permute-start(bf16[512,256]{1,0:T(8,128)(2,1)S(1)} %add_convert_fusion), channel_id=1, source_target_pairs={{0,2},{1,5},{4,0},{5,9},{8,4},{9,13},{12,8},{13,15},{14,12},{15,11... | collective-permute-start | bytes 786440 | tf_op jit(solution)/shard_map/ppermute | solution.py:51
  64.6 8.0 %collective-permute-start.11 = (bf16[512,256]{1,0:T(8,128)(2,1)S(1)}, bf16[512,256]{1,0:T(8,128)(2,1)S(1)}, u32[]{:S(2)}, u32[]{:S(2)}) collective-permute-start(bf16[512,256]{1,0:T(8,128)(2,1)S(1)} %add_convert_fusion.2), channel_id=1, source_target_pairs={{0,4},{1,3},{4,8},{5,1},{8,12},{9,5},{12,14},{13,9},{14,10},{15,13... | collective-permute-start | bytes 786440 | tf_op jit(solution)/shard_map/ppermute | solution.py:51
  72.8 9.1 %collective-permute-start.15 = (bf16[512,256]{1,0:T(8,128)(2,1)S(1)}, bf16[512,256]{1,0:T(8,128)(2,1)S(1)}, u32[]{:S(2)}, u32[]{:S(2)}) collective-permute-start(bf16[512,256]{1,0:T(8,128)(2,1)S(1)} %fusion.2.refs_0_), channel_id=1, source_target_pairs={{0,4},{1,3},{4,8},{5,1},{8,12},{9,5},{12,14},{13,9},{14,10},{15,13... | collective-permute-start | bytes 786440 | tf_op jit(solution)/shard_map/ppermute | solution.py:51
  76.8 7.3 %collective-permute-start.18 = (bf16[512,256]{1,0:T(8,128)(2,1)S(1)}, bf16[512,256]{1,0:T(8,128)(2,1)S(1)}, u32[]{:S(2)}, u32[]{:S(2)}) collective-permute-start(bf16[512,256]{1,0:T(8,128)(2,1)S(1)} %fusion.2.refs_0_), channel_id=1, source_target_pairs={{0,2},{1,5},{4,0},{5,9},{8,4},{9,13},{12,8},{13,15},{14,12},{15,11... | collective-permute-start | bytes 786440 | tf_op jit(solution)/shard_map/ppermute | solution.py:51
  81.9 8.2 %collective-permute-start.16 = (bf16[512,256]{1,0:T(8,128)(2,1)S(1)}, bf16[512,256]{1,0:T(8,128)(2,1)S(1)}, u32[]{:S(2)}, u32[]{:S(2)}) collective-permute-start(bf16[512,256]{1,0:T(8,128)(2,1)S(1)} %collective-permute-done.15.refs_0_), channel_id=1, source_target_pairs={{0,4},{1,3},{4,8},{5,1},{8,12},{9,5},{12,14},{13,9},{14,10},{15,13... | collective-permute-start | bytes 786440 | tf_op jit(solution)/shard_map/ppermute | solution.py:51
  84.0 8.3 %collective-permute-start.19 = (bf16[512,256]{1,0:T(8,128)(2,1)S(1)}, bf16[512,256]{1,0:T(8,128)(2,1)S(1)}, u32[]{:S(2)}, u32[]{:S(2)}) collective-permute-start(bf16[512,256]{1,0:T(8,128)(2,1)S(1)} %collective-permute-done.18.refs_1_), channel_id=1, source_target_pairs={{0,2},{1,5},{4,0},{5,9},{8,4},{9,13},{12,8},{13,15},{14,12},{15,11... | collective-permute-start | bytes 786440 | tf_op jit(solution)/shard_map/ppermute | solution.py:51
  90.1 6.4 %collective-permute-start.17 = (bf16[512,256]{1,0:T(8,128)(2,1)S(1)}, bf16[512,256]{1,0:T(8,128)(2,1)S(1)}, u32[]{:S(2)}, u32[]{:S(2)}) collective-permute-start(bf16[512,256]{1,0:T(8,128)(2,1)S(1)} %collective-permute-done.16.refs_2_), channel_id=1, source_target_pairs={{0,4},{1,3},{4,8},{5,1},{8,12},{9,5},{12,14},{13,9},{14,10},{15,13... | collective-permute-start | bytes 786440 | tf_op jit(solution)/shard_map/ppermute | solution.py:51
  92.4 6.4 %collective-permute-start.21 = (bf16[512,256]{1,0:T(8,128)(2,1)S(1)}, bf16[512,256]{1,0:T(8,128)(2,1)S(1)}, u32[]{:S(2)}, u32[]{:S(2)}) collective-permute-start(bf16[512,256]{1,0:T(8,128)(2,1)S(1)} %collective-permute-done.19.refs_3_), channel_id=1, source_target_pairs={{0,2},{1,5},{4,0},{5,9},{8,4},{9,13},{12,8},{13,15},{14,12},{15,11... | collective-permute-start | bytes 786440 | tf_op jit(solution)/shard_map/ppermute | solution.py:51
  96.4 6.4 %collective-permute-start.20 = (bf16[512,256]{1,0:T(8,128)(2,1)S(1)}, bf16[512,256]{1,0:T(8,128)(2,1)S(1)}, u32[]{:S(2)}, u32[]{:S(2)}) collective-permute-start(bf16[512,256]{1,0:T(8,128)(2,1)S(1)} %collective-permute-done.17.refs_0_), channel_id=1, source_target_pairs={{0,4},{1,3},{4,8},{5,1},{8,12},{9,5},{12,14},{13,9},{14,10},{15,13... | collective-permute-start | bytes 786440 | tf_op jit(solution)/shard_map/ppermute | solution.py:51
  104.3 4.8 %collective-permute-start.23 = (f32[128,1024]{1,0:T(8,128)S(1)}, f32[128,1024]{1,0:T(8,128)S(1)}, u32[]{:S(2)}, u32[]{:S(2)}) collective-permute-start(f32[128,1024]{1,0:T(8,128)S(1)} %get-tuple-element.78), channel_id=1, source_target_pairs={{1,0},{3,2},{5,4},{7,6},{9,8},{11,10},{13,12},{15,14},{17,16},{19,... | collective-permute-start | bytes 1572872 | tf_op jit(solution)/shard_map/ppermute | solution.py:23
  105.6 3.5 %collective-permute-start.22 = (f32[512,128]{1,0:T(8,128)S(1)}, f32[512,128]{1,0:T(8,128)S(1)}, u32[]{:S(2)}, u32[]{:S(2)}) collective-permute-start(f32[512,128]{1,0:T(8,128)S(1)} %get-tuple-element.77), channel_id=1, source_target_pairs={{1,0},{3,2},{5,4},{7,6},{9,8},{11,10},{13,12},{15,14},{17,16},{19,... | collective-permute-start | bytes 786440 | tf_op jit(solution)/shard_map/ppermute | solution.py:23

commit v4 on v3

--- a/solution.py
+++ b/solution.py
@@ -15,6 +15,7 @@
 RING_LIMIT = 16
 VMEM_BYTES = 24 * 1024 * 1024
 PIECES = 8
+GATHER_BYTES = 512 * 1024
 
 
 def passed_along(shard, axis, by):
@@ -78,21 +79,20 @@
     return pl.ds(pl.multiple_of(starts[slot], wide), wide)
 
 
-def encode_kernel(slots, last, starts, *refs):
-    shards, (weight, before, *outs) = refs[:len(slots)], refs[len(slots):]
-    total = jnp.broadcast_to(before[...], outs[0].shape)
-    for slot, shard in zip(slots, shards):
-        block = weight[0, block_of(starts, slot, shard.shape[1]), :]
-        total = total + jnp.dot(shard[...], block, preferred_element_type=F32)
-    outs[0][...] = total
-    if last:
-        outs[1][...] = jnp.maximum(total, 0.0).astype(BF16)
+def encode_kernel(starts, *refs):
+    *shards, weight, bias, preact, codes = refs
+    height = shards[0].shape[0]
+    for i, shard in enumerate(shards):
+        total = bias[...] + jnp.dot(shard[...], weight[0], preferred_element_type=F32)
+        preact[i * height:(i + 1) * height, :] = total
+        codes[i * height:(i + 1) * height, :] = jnp.maximum(total, 0.0).astype(BF16)
 
 
 def turn_kernel(starts, *refs):
     *shards, turned = refs
-    for slot, shard in enumerate(shards):
-        turned[block_of(starts, slot, shard.shape[1]), :] = shard[...].T
+    height = shards[0].shape[0]
+    for i, shard in enumerate(shards):
+        turned[:, i * height:(i + 1) * height] = shard[...].T
 
 
 def spread_kernel(slots, starts, codes, earlier, own_dec, cross, *outs):
@@ -191,29 +191,17 @@
     starts = jnp.stack([ring_member(place + sign * offset, size) * wide for offset in offsets] + [layer])
     starts = starts.astype(jnp.int32)
 
-    own = residual_in[0]
-    inputs = [own] + [None] * (size - 1)
-    inputs[slot_p[1]] = hop(own, 1)
     cross_full = lax.all_gather(dec_cross, "layer", axis=1, tiled=True)
-    if reach > 1:
-        inputs[slot_q[1]] = hop(after(own, cross_full), -1)
-    for s in range(2, reach + 1):
-        inputs[slot_p[s]] = hop(inputs[slot_p[s - 1]], 1)
-        if s < reach:
-            inputs[slot_q[s]] = hop(inputs[slot_q[s - 1]], -1)
-
-    early = tuple(range(size - 1))
-    part = call(
-        functools.partial(encode_kernel, early, False),
-        [shape((rows, lat), F32)],
-        unit * len(early),
-        [starts] + inputs[:-1] + [enc_weight, enc_bias],
-    )[0]
+    count = rows * wide * size * 2 // GATHER_BYTES
+    height = rows // count
+    inputs = [
+        lax.all_gather(residual_in[0, i * height:(i + 1) * height], "latent", axis=1, tiled=True) for i in range(count)
+    ]
     preact, codes = call(
-        functools.partial(encode_kernel, (far,), True),
+        encode_kernel,
         [shape((rows, lat), F32), shape((rows, lat), BF16)],
-        unit,
-        [starts, inputs[far], enc_weight, part],
+        unit * size,
+        [starts] + inputs + [enc_weight, enc_bias],
     )
     earlier = passed_along(codes, "layer", 1)
 

time: 112 us -> 207 us (1.85)
  blocking collectives: 2.38 us -> 130 us
  waiting for transfers between devices: 58.6 us -> 42.2 us
  starting transfers between devices: 31.8 us -> 18.3 us
    all_gather x0 -> x4, blocking collectives: none -> 127 us  [ring_shards(): lax.all_gather(residual_in[0, i * height:(i + 1) * height], 'latent', axi...]
    ppermute x21 -> x14, waiting for transfers between devices: 55.5 us -> 40 us  [hop(): return lax.ppermute(shard, ('latent', 'layer'), pairs)]
    ppermute x21 -> x14, starting transfers between devices: 27.9 us -> 14.5 us  [hop(): return lax.ppermute(shard, ('latent', 'layer'), pairs)]
    unnamed x12 -> x8, local copies, waits for them, and re-layouts: 2.66 us -> 0.02 us
    pallas_call x9 -> x8, Pallas kernels: 14.5 us -> 13.8 us  [call(): pl.pallas_call(kernel, out_shape=outs, in_specs=[spec(pltpu.SMEM)] + [spe...]
  transfers between devices with their start and end apart: 24 -> 17, of which waited for: 18 -> 13; matrix products, arithmetic and copies ran while one was open for 0% -> 0% of each run, Pallas kernels for 9% -> 4%
where the time goes in v4:
time: 207 us
  blocking collectives  130 us (63%)
  waiting for transfers between devices  42.2 us (20%)
  starting transfers between devices  18.3 us (9%)
  Pallas kernels  13.8 us (7%)
    all_gather x4, blocking collectives, ring_shards(): lax.all_gather(residual_in[0, i * height:(i + 1) * height], 'latent', axi...  127 us
    ppermute x14, waiting for transfers between devices, hop(): return lax.ppermute(shard, ('latent', 'layer'), pairs)  40 us
    ppermute x14, starting transfers between devices, hop(): return lax.ppermute(shard, ('latent', 'layer'), pairs)  14.5 us
    pallas_call x8, Pallas kernels, call(): pl.pallas_call(kernel, out_shape=outs, in_specs=[spec(pltpu.SMEM)] + [spe...  13.8 us
  transfers between devices with their start and end apart: 17, of which 13 were waited for; matrix products, arithmetic and copies ran while one was open for 0% of the time, Pallas kernels for 4%

profile of v4, /device:TPU:0, one launch (start us, length us, event | category | flops | bytes accessed | tf_op | source)
XLA Modules:
  0.0 206.9 jit_solution(7927194900643036708)
XLA Ops:
  1.8 33.0 %all-gather.1 = bf16[1,128,2048]{2,1,0:T(8,128)(2,1)S(1)} all-gather(bf16[1,128,256]{2,1,0:T(8,128)(2,1)S(1)} %get-tuple-element.83), channel_id=3, replica_groups=mesh['groups'=2,'latent'=8,'layer'=2] {'latent'}, dimensions={2}, use_global_device_ids=true | all-gather | bytes 589824 | tf_op jit(solution)/shard_map/all_gather | solution.py:198
  34.8 31.4 %all-gather.2 = bf16[1,128,2048]{2,1,0:T(8,128)(2,1)S(1)} all-gather(bf16[1,128,256]{2,1,0:T(8,128)(2,1)S(1)} %get-tuple-element.85), channel_id=4, replica_groups=mesh['groups'=2,'latent'=8,'layer'=2] {'latent'}, dimensions={2}, use_global_device_ids=true | all-gather | bytes 589824 | tf_op jit(solution)/shard_map/all_gather | solution.py:198
  66.2 31.7 %all-gather.3 = bf16[1,128,2048]{2,1,0:T(8,128)(2,1)S(1)} all-gather(bf16[1,128,256]{2,1,0:T(8,128)(2,1)S(1)} %get-tuple-element.82), channel_id=5, replica_groups=mesh['groups'=2,'latent'=8,'layer'=2] {'latent'}, dimensions={2}, use_global_device_ids=true | all-gather | bytes 589824 | tf_op jit(solution)/shard_map/all_gather | solution.py:198
  97.9 31.2 %all-gather = bf16[1,128,2048]{2,1,0:T(8,128)(2,1)S(1)} all-gather(bf16[1,128,256]{2,1,0:T(8,128)(2,1)S(1)} %get-tuple-element.84), channel_id=2, replica_groups=mesh['groups'=2,'latent'=8,'layer'=2] {'latent'}, dimensions={2}, use_global_device_ids=true | all-gather | bytes 589824 | tf_op jit(solution)/shard_map/all_gather | solution.py:198
  129.1 1.2 shard_map.94
  130.4 1.3 collective-permute-start
  131.9 2.4 %all_gather.19.cross.refs_4_.refs_7_.refs_5_ = bf16[128,2048]{1,0:T(8,128)(2,1)S(1)} all-gather(bf16[128,1024]{1,0:T(8,128)(2,1)} %param.11), channel_id=1, replica_groups=mesh['groups'=2,'latent'=8,'layer'=2] {'layer'}, dimensions={1}, use_global_device_ids=true | all-gather | bytes 786432 | tf_op jit(solution)/shard_map/all_gather | solution.py:194
  134.6 1.2 shard_map.95
  135.8 2.1 collective-permute-start.5
  137.9 4.0 %collective-permute-done.1 = bf16[512,256]{1,0:T(8,128)(2,1)S(1)} collective-permute-done((bf16[512,256]{1,0:T(8,128)(2,1)S(1)}, bf16[512,256]{1,0:T(8,128)(2,1)S(1)}, u32[]{:S(2)}, u32[]{:S(2)}) %collective-permute-start.1) | collective-permute-done | bytes 262176 | tf_op jit(solution)/shard_map/ppermute | solution.py:52
  143.0 2.4 %collective-permute-start.6 = (bf16[512,256]{1,0:T(8,128)(2,1)S(1)}, bf16[512,256]{1,0:T(8,128)(2,1)S(1)}, u32[]{:S(2)}, u32[]{:S(2)}) collective-permute-start(bf16[512,256]{1,0:T(8,128)(2,1)S(1)} %add_convert_fusion.1), channel_id=1, source_target_pairs={{0,2},{1,5},{4,0},{5,9},{8,4},{9,13},{12,8},{13,15},{14,12},{15,11... | collective-permute-start | bytes 786440 | tf_op jit(solution)/shard_map/ppermute | solution.py:52
  145.4 6.5 %collective-permute-done.2 = bf16[512,256]{1,0:T(8,128)(2,1)S(1)} collective-permute-done((bf16[512,256]{1,0:T(8,128)(2,1)S(1)}, bf16[512,256]{1,0:T(8,128)(2,1)S(1)}, u32[]{:S(2)}, u32[]{:S(2)}) %collective-permute-start.2) | collective-permute-done | bytes 262176 | tf_op jit(solution)/shard_map/ppermute | solution.py:52
  152.1 1.1 shard_map.93.turned
  153.3 2.1 collective-permute-start.7
  155.3 4.6 %collective-permute-done.3 = bf16[512,256]{1,0:T(8,128)(2,1)S(1)} collective-permute-done((bf16[512,256]{1,0:T(8,128)(2,1)S(1)}, bf16[512,256]{1,0:T(8,128)(2,1)S(1)}, u32[]{:S(2)}, u32[]{:S(2)}) %collective-permute-start.3) | collective-permute-done | bytes 262176 | tf_op jit(solution)/shard_map/ppermute | solution.py:52
  160.8 6.4 %collective-permute-done.4 = bf16[512,256]{1,0:T(8,128)(2,1)S(1)} collective-permute-done((bf16[512,256]{1,0:T(8,128)(2,1)S(1)}, bf16[512,256]{1,0:T(8,128)(2,1)S(1)}, u32[]{:S(2)}, u32[]{:S(2)}) %collective-permute-start.4) | collective-permute-done | bytes 262176 | tf_op jit(solution)/shard_map/ppermute | solution.py:52
  167.4 1.4 shard_map.96
  168.9 2.1 collective-permute-start.11
  171.0 5.0 %collective-permute-done.8.refs_0_ = bf16[512,256]{1,0:T(8,128)(2,1)S(1)} collective-permute-done((bf16[512,256]{1,0:T(8,128)(2,1)S(1)}, bf16[512,256]{1,0:T(8,128)(2,1)S(1)}, u32[]{:S(2)}, u32[]{:S(2)}) %collective-permute-start.8) | collective-permute-done | bytes 262176 | tf_op jit(solution)/shard_map/ppermute | solution.py:52
  176.0 1.4 collective-permute-done.11.refs_1_
  177.4 2.5 %collective-permute-start.12 = (bf16[512,256]{1,0:T(8,128)(2,1)S(1)}, bf16[512,256]{1,0:T(8,128)(2,1)S(1)}, u32[]{:S(2)}, u32[]{:S(2)}) collective-permute-start(bf16[512,256]{1,0:T(8,128)(2,1)S(1)} %collective-permute-done.11.refs_1_), channel_id=1, source_target_pairs={{0,2},{1,5},{4,0},{5,9},{8,4},{9,13},{12,8},{13,15},{14,12},{15,11... | collective-permute-start | bytes 786440 | tf_op jit(solution)/shard_map/ppermute | solution.py:52
  179.8 4.8 %collective-permute-done.9.refs_2_ = bf16[512,256]{1,0:T(8,128)(2,1)S(1)} collective-permute-done((bf16[512,256]{1,0:T(8,128)(2,1)S(1)}, bf16[512,256]{1,0:T(8,128)(2,1)S(1)}, u32[]{:S(2)}, u32[]{:S(2)}) %collective-permute-start.9) | collective-permute-done | bytes 262176 | tf_op jit(solution)/shard_map/ppermute | solution.py:52
  184.9 1.4 collective-permute-done.12.refs_3_
  186.4 2.5 %collective-permute-start.14 = (bf16[512,256]{1,0:T(8,128)(2,1)S(1)}, bf16[512,256]{1,0:T(8,128)(2,1)S(1)}, u32[]{:S(2)}, u32[]{:S(2)}) collective-permute-start(bf16[512,256]{1,0:T(8,128)(2,1)S(1)} %collective-permute-done.12.refs_3_), channel_id=1, source_target_pairs={{0,2},{1,5},{4,0},{5,9},{8,4},{9,13},{12,8},{13,15},{14,12},{15,11... | collective-permute-start | bytes 786440 | tf_op jit(solution)/shard_map/ppermute | solution.py:52
  188.8 2.7 %shard_map.97 = (f32[512,128]{1,0:T(8,128)S(1)}, f32[512,128]{1,0:T(8,128)S(1)}, f32[1,128,2048]{2,1,0:T(8,128)}, f32[128,1024]{1,0:T(8,128)S(1)}, f32[128,1024]{1,0:T(8,128)S(1)}) custom-call(s32[9]{0:T(128)S(1)} %stack.39.starts, ...), custom_call_target="tpu_custom_call", output_to_operand_aliasing={{2}: (11, {}), {3}: (12, {}), {4}: (13, {})} | custom-call | flops 536870912 | bytes 7602212 | tf_op jit(solution)/shard_map/pallas_call | solution.py:66
  192.7 1.9 shard_map.98
  194.6 3.4 %collective-permute-done.13.refs_0_ = bf16[512,256]{1,0:T(8,128)(2,1)S(1)} collective-permute-done((bf16[512,256]{1,0:T(8,128)(2,1)S(1)}, bf16[512,256]{1,0:T(8,128)(2,1)S(1)}, u32[]{:S(2)}, u32[]{:S(2)}) %collective-permute-start.13) | collective-permute-done | bytes 262176 | tf_op jit(solution)/shard_map/ppermute | solution.py:52
  198.0 1.5 shard_map.99
  199.5 1.3 collective-permute-start.16
  200.8 1.3 collective-permute-start.15
  202.1 2.2 %collective-permute-done.15.from_next = f32[512,128]{1,0:T(8,128)S(1)} collective-permute-done((f32[512,128]{1,0:T(8,128)S(1)}, f32[512,128]{1,0:T(8,128)S(1)}, u32[]{:S(2)}, u32[]{:S(2)}) %collective-permute-start.15) | collective-permute-done | bytes 262176 | tf_op jit(solution)/shard_map/ppermute | solution.py:24
  204.3 2.7 %shard_map.100 = (f32[1,2048,128]{2,1,0:T(8,128)}, f32[1,128]{1,0:T(1,128)}, f32[128,1024]{1,0:T(8,128)}) custom-call(s32[9]{0:T(128)S(1)} %stack.39.starts, bf16[2048,512]{1,0:T(8,128)(2,1)S(1)} %shard_map.93.turned, f32[512,128]{1,0:T(8,128)S(1)} %get-tuple-element.43.preact, f32[512,128]{1,0:T(8,128)S(1)} %get-tuple-element.74.back_own, ...), custom_call_target="tpu_custom_call" | custom-call | flops 268435456 | bytes 5505572 | tf_op jit(solution)/shard_map/pallas_call | solution.py:66
  (33 shorter events, 5.4 us)
Async XLA Ops:
  0.6 128.5 %copy-start.1 = (bf16[1,2048,128]{2,1,0:T(8,128)(2,1)S(1)}, bf16[1,2048,128]{2,1,0:T(8,128)(2,1)}, u32[]{:S(2)}) copy-start(bf16[1,2048,128]{2,1,0:T(8,128)(2,1)} %refs_4_.2) | copy-start | bytes 1572868
  0.6 128.5 %copy-start.2 = (f32[1,128]{1,0:T(1,128)S(1)}, f32[1,128]{1,0:T(1,128)}, u32[]{:S(2)}) copy-start(f32[1,128]{1,0:T(1,128)} %refs_5_.1) | copy-start | bytes 1540
  34.8 96.9 %copy-start = (bf16[1,128,2048]{2,1,0:T(8,128)(2,1)S(1)}, bf16[1,128,2048]{2,1,0:T(8,128)(2,1)}, u32[]{:S(2)}) copy-start(bf16[1,128,2048]{2,1,0:T(8,128)(2,1)} %refs_3_.3) | copy-start | bytes 1572868
  130.4 3.9 %collective-permute-start = (bf16[512,128]{1,0:T(8,128)(2,1)S(1)}, bf16[512,128]{1,0:T(8,128)(2,1)S(1)}, u32[]{:S(2)}, u32[]{:S(2)}) collective-permute-start(bf16[512,128]{1,0:T(8,128)(2,1)S(1)} %get-tuple-element.44.codes), channel_id=1, source_target_pairs={{0,1},{2,3},{4,5},{6,7},{8,9},{10,11},{12,13},{14,15},{16,17},{18,... | collective-permute-start | bytes 393224 | tf_op jit(solution)/shard_map/ppermute | solution.py:24
  134.5 7.3 %collective-permute-start.1 = (bf16[512,256]{1,0:T(8,128)(2,1)S(1)}, bf16[512,256]{1,0:T(8,128)(2,1)S(1)}, u32[]{:S(2)}, u32[]{:S(2)}) collective-permute-start(bf16[512,256]{1,0:T(8,128)(2,1)S(1)} %fusion), channel_id=1, source_target_pairs={{0,4},{1,3},{4,8},{5,1},{8,12},{9,5},{12,14},{13,9},{14,10},{15,13... | collective-permute-start | bytes 786440 | tf_op jit(solution)/shard_map/ppermute | solution.py:52
  135.8 7.1 %collective-permute-start.5 = (bf16[512,256]{1,0:T(8,128)(2,1)S(1)}, bf16[512,256]{1,0:T(8,128)(2,1)S(1)}, u32[]{:S(2)}, u32[]{:S(2)}) collective-permute-start(bf16[512,256]{1,0:T(8,128)(2,1)S(1)} %get-tuple-element.52), channel_id=1, source_target_pairs={{0,2},{1,5},{4,0},{5,9},{8,4},{9,13},{12,8},{13,15},{14,12},{15,11... | collective-permute-start | bytes 786440 | tf_op jit(solution)/shard_map/ppermute | solution.py:52
  142.0 10.0 %collective-permute-start.2 = (bf16[512,256]{1,0:T(8,128)(2,1)S(1)}, bf16[512,256]{1,0:T(8,128)(2,1)S(1)}, u32[]{:S(2)}, u32[]{:S(2)}) collective-permute-start(bf16[512,256]{1,0:T(8,128)(2,1)S(1)} %add_convert_fusion.4), channel_id=1, source_target_pairs={{0,4},{1,3},{4,8},{5,1},{8,12},{9,5},{12,14},{13,9},{14,10},{15,13... | collective-permute-start | bytes 786440 | tf_op jit(solution)/shard_map/ppermute | solution.py:52
  143.0 10.2 %collective-permute-start.6 = (bf16[512,256]{1,0:T(8,128)(2,1)S(1)}, bf16[512,256]{1,0:T(8,128)(2,1)S(1)}, u32[]{:S(2)}, u32[]{:S(2)}) collective-permute-start(bf16[512,256]{1,0:T(8,128)(2,1)S(1)} %add_convert_fusion.1), channel_id=1, source_target_pairs={{0,2},{1,5},{4,0},{5,9},{8,4},{9,13},{12,8},{13,15},{14,12},{15,11... | collective-permute-start | bytes 786440 | tf_op jit(solution)/shard_map/ppermute | solution.py:52
  152.0 8.0 %collective-permute-start.3 = (bf16[512,256]{1,0:T(8,128)(2,1)S(1)}, bf16[512,256]{1,0:T(8,128)(2,1)S(1)}, u32[]{:S(2)}, u32[]{:S(2)}) collective-permute-start(bf16[512,256]{1,0:T(8,128)(2,1)S(1)} %add_convert_fusion.3), channel_id=1, source_target_pairs={{0,4},{1,3},{4,8},{5,1},{8,12},{9,5},{12,14},{13,9},{14,10},{15,13... | collective-permute-start | bytes 786440 | tf_op jit(solution)/shard_map/ppermute | solution.py:52
  153.2 14.0 %copy-start.3 = (bf16[1,512,256]{2,1,0:T(8,128)(2,1)S(1)}, bf16[1,512,256]{2,1,0:T(8,128)(2,1)}, u32[]{:S(2)}) copy-start(bf16[1,512,256]{2,1,0:T(8,128)(2,1)} %param.7) | copy-start | bytes 786436
  153.3 7.6 %collective-permute-start.7 = (bf16[512,256]{1,0:T(8,128)(2,1)S(1)}, bf16[512,256]{1,0:T(8,128)(2,1)S(1)}, u32[]{:S(2)}, u32[]{:S(2)}) collective-permute-start(bf16[512,256]{1,0:T(8,128)(2,1)S(1)} %add_convert_fusion), channel_id=1, source_target_pairs={{0,2},{1,5},{4,0},{5,9},{8,4},{9,13},{12,8},{13,15},{14,12},{15,11... | collective-permute-start | bytes 786440 | tf_op jit(solution)/shard_map/ppermute | solution.py:52
  160.0 7.2 %collective-permute-start.4 = (bf16[512,256]{1,0:T(8,128)(2,1)S(1)}, bf16[512,256]{1,0:T(8,128)(2,1)S(1)}, u32[]{:S(2)}, u32[]{:S(2)}) collective-permute-start(bf16[512,256]{1,0:T(8,128)(2,1)S(1)} %add_convert_fusion.2), channel_id=1, source_target_pairs={{0,4},{1,3},{4,8},{5,1},{8,12},{9,5},{12,14},{13,9},{14,10},{15,13... | collective-permute-start | bytes 786440 | tf_op jit(solution)/shard_map/ppermute | solution.py:52
  167.4 8.6 %collective-permute-start.8 = (bf16[512,256]{1,0:T(8,128)(2,1)S(1)}, bf16[512,256]{1,0:T(8,128)(2,1)S(1)}, u32[]{:S(2)}, u32[]{:S(2)}) collective-permute-start(bf16[512,256]{1,0:T(8,128)(2,1)S(1)} %fusion.2.refs_0_), channel_id=1, source_target_pairs={{0,4},{1,3},{4,8},{5,1},{8,12},{9,5},{12,14},{13,9},{14,10},{15,13... | collective-permute-start | bytes 786440 | tf_op jit(solution)/shard_map/ppermute | solution.py:52
  168.9 8.5 %collective-permute-start.11 = (bf16[512,256]{1,0:T(8,128)(2,1)S(1)}, bf16[512,256]{1,0:T(8,128)(2,1)S(1)}, u32[]{:S(2)}, u32[]{:S(2)}) collective-permute-start(bf16[512,256]{1,0:T(8,128)(2,1)S(1)} %fusion.2.refs_0_), channel_id=1, source_target_pairs={{0,2},{1,5},{4,0},{5,9},{8,4},{9,13},{12,8},{13,15},{14,12},{15,11... | collective-permute-start | bytes 786440 | tf_op jit(solution)/shard_map/ppermute | solution.py:52
  176.0 8.7 %collective-permute-start.9 = (bf16[512,256]{1,0:T(8,128)(2,1)S(1)}, bf16[512,256]{1,0:T(8,128)(2,1)S(1)}, u32[]{:S(2)}, u32[]{:S(2)}) collective-permute-start(bf16[512,256]{1,0:T(8,128)(2,1)S(1)} %collective-permute-done.8.refs_0_), channel_id=1, source_target_pairs={{0,4},{1,3},{4,8},{5,1},{8,12},{9,5},{12,14},{13,9},{14,10},{15,13... | collective-permute-start | bytes 786440 | tf_op jit(solution)/shard_map/ppermute | solution.py:52
  177.4 9.0 %collective-permute-start.12 = (bf16[512,256]{1,0:T(8,128)(2,1)S(1)}, bf16[512,256]{1,0:T(8,128)(2,1)S(1)}, u32[]{:S(2)}, u32[]{:S(2)}) collective-permute-start(bf16[512,256]{1,0:T(8,128)(2,1)S(1)} %collective-permute-done.11.refs_1_), channel_id=1, source_target_pairs={{0,2},{1,5},{4,0},{5,9},{8,4},{9,13},{12,8},{13,15},{14,12},{15,11... | collective-permute-start | bytes 786440 | tf_op jit(solution)/shard_map/ppermute | solution.py:52
  184.6 6.9 %collective-permute-start.10 = (bf16[512,256]{1,0:T(8,128)(2,1)S(1)}, bf16[512,256]{1,0:T(8,128)(2,1)S(1)}, u32[]{:S(2)}, u32[]{:S(2)}) collective-permute-start(bf16[512,256]{1,0:T(8,128)(2,1)S(1)} %collective-permute-done.9.refs_2_), channel_id=1, source_target_pairs={{0,4},{1,3},{4,8},{5,1},{8,12},{9,5},{12,14},{13,9},{14,10},{15,13... | collective-permute-start | bytes 786440 | tf_op jit(solution)/shard_map/ppermute | solution.py:52
  186.4 6.4 %collective-permute-start.14 = (bf16[512,256]{1,0:T(8,128)(2,1)S(1)}, bf16[512,256]{1,0:T(8,128)(2,1)S(1)}, u32[]{:S(2)}, u32[]{:S(2)}) collective-permute-start(bf16[512,256]{1,0:T(8,128)(2,1)S(1)} %collective-permute-done.12.refs_3_), channel_id=1, source_target_pairs={{0,2},{1,5},{4,0},{5,9},{8,4},{9,13},{12,8},{13,15},{14,12},{15,11... | collective-permute-start | bytes 786440 | tf_op jit(solution)/shard_map/ppermute | solution.py:52
  191.6 6.4 %collective-permute-start.13 = (bf16[512,256]{1,0:T(8,128)(2,1)S(1)}, bf16[512,256]{1,0:T(8,128)(2,1)S(1)}, u32[]{:S(2)}, u32[]{:S(2)}) collective-permute-start(bf16[512,256]{1,0:T(8,128)(2,1)S(1)} %collective-permute-done.10.refs_0_), channel_id=1, source_target_pairs={{0,4},{1,3},{4,8},{5,1},{8,12},{9,5},{12,14},{13,9},{14,10},{15,13... | collective-permute-start | bytes 786440 | tf_op jit(solution)/shard_map/ppermute | solution.py:52
  199.5 4.8 %collective-permute-start.16 = (f32[128,1024]{1,0:T(8,128)S(1)}, f32[128,1024]{1,0:T(8,128)S(1)}, u32[]{:S(2)}, u32[]{:S(2)}) collective-permute-start(f32[128,1024]{1,0:T(8,128)S(1)} %get-tuple-element.76), channel_id=1, source_target_pairs={{1,0},{3,2},{5,4},{7,6},{9,8},{11,10},{13,12},{15,14},{17,16},{19,... | collective-permute-start | bytes 1572872 | tf_op jit(solution)/shard_map/ppermute | solution.py:24
  200.8 3.5 %collective-permute-start.15 = (f32[512,128]{1,0:T(8,128)S(1)}, f32[512,128]{1,0:T(8,128)S(1)}, u32[]{:S(2)}, u32[]{:S(2)}) collective-permute-start(f32[512,128]{1,0:T(8,128)S(1)} %get-tuple-element.75), channel_id=1, source_target_pairs={{1,0},{3,2},{5,4},{7,6},{9,8},{11,10},{13,12},{15,14},{17,16},{19,... | collective-permute-start | bytes 786440 | tf_op jit(solution)/shard_map/ppermute | solution.py:24

commit v5 on v0

v5 whole, which is shorter than its diff:
```python
import functools
import math

import jax
import jax.numpy as jnp
from jax import lax
from jax.experimental import pallas as pl
from jax.experimental.pallas import tpu as pltpu
from jax.sharding import PartitionSpec as P

F32 = jnp.float32
BF16 = jnp.bfloat16
OVER_ROWS = (((0,), (0,)), ((), ()))
OVER_COLS = (((1,), (1,)), ((), ()))
RING_LIMIT = 16
VMEM_BYTES = 24 * 1024 * 1024
PIECES = 8


def passed_along(shard, axis, by):
    size = lax.axis_size(axis)
    pairs = [(i, i + by) for i in range(size) if 0 <= i + by < size]
    return lax.ppermute(shard, axis, pairs)


def matmul(a, b, dims=(((1,), (0,)), ((), ()))):
    return lax.dot_general(a, b, dims, preferred_element_type=F32)


def ring_order(size):
    return [2 * p if p < size // 2 else 2 * (size - 1 - p) + 1 for p in range(size)]


def ring_member(place, size):
    place = lax.rem(place + 2 * size, size)
    return jnp.where(place < size // 2, 2 * place, 2 * (size - 1 - place) + 1)


def ring_place(member, size):
    return jnp.where(member % 2 == 0, member // 2, size - 1 - member // 2)


def hop(shard, way):
    size, layers = lax.axis_size("latent"), lax.axis_size("layer")
    order = ring_order(size)
    pairs = []
    for p in range(size):
        for layer in range(layers):
            by = way if layer % 2 == 0 else -way
            pairs.append((order[p] * layers + layer, order[(p + by) % size] * layers + layer))
    return lax.ppermute(shard, ("latent", "layer"), pairs)


def after(value, *others):
    return lax.optimization_barrier((value,) + others)[0]


def call(kernel, outs, flops, operands, spaces=None, out_spaces=None, scratch=(), aliases=None):
    def spec(space):
        return pl.BlockSpec(memory_space=space)

    spaces = spaces or [pltpu.VMEM] * (len(operands) - 1)
    out_spaces = out_spaces or [pltpu.VMEM] * len(outs)
    size = sum(math.prod(x.shape) * x.dtype.itemsize for x in list(operands) + list(outs))
    return pl.pallas_call(
        kernel,
        out_shape=outs,
        in_specs=[spec(pltpu.SMEM)] + [spec(space) for space in spaces],
        out_specs=[spec(space) for space in out_spaces],
        scratch_shapes=list(scratch),
        input_output_aliases=aliases or {},
        compiler_params=pltpu.CompilerParams(vmem_limit_bytes=VMEM_BYTES),
        cost_estimate=pl.CostEstimate(flops=flops, bytes_accessed=size, transcendentals=0),
    )(*operands)


def block_of(starts, slot, wide):
    return pl.ds(pl.multiple_of(starts[slot], wide), wide)


def prepare_kernel(starts, own_dec, low_cross, high_cross, weight, stacked, weight_here):
    lat, half_width = high_cross.shape
    stacked[:lat, :] = own_dec[0]
    stacked[lat:, :half_width] = low_cross[...]
    stacked[lat:, half_width:] = high_cross[...]
    weight_here[...] = weight[0]


def encode_kernel(slots, last, starts, *refs):
    shards, (weight, before, *outs) = refs[:len(slots)], refs[len(slots):]
    total = jnp.broadcast_to(before[...], outs[0].shape)
    for slot, shard in zip(slots, shards):
        block = weight[block_of(starts, slot, shard.shape[1]), :]
        total = total + jnp.dot(shard[...], block, preferred_element_type=F32)
    outs[0][...] = total
    if last:
        outs[1][...] = jnp.maximum(total, 0.0).astype(BF16)


def turn_kernel(starts, *refs):
    *shards, turned = refs
    rows, wide = shards[0].shape
    for k in range(len(shards) // 2):
        at = block_of(starts, k, wide)
        for chain in range(2):
            turned[at, chain * rows:(chain + 1) * rows] = shards[2 * k + chain][...].T


def spread_kernel(slots, starts, codes, earlier, stacked, *outs):
    *partials, both_t = outs
    both = jnp.concatenate([codes[...], earlier[...]], axis=1)
    for slot, partial in zip(slots, partials):
        block = stacked[:, block_of(starts, slot, partial.shape[1])]
        partial[...] = jnp.dot(both, block, preferred_element_type=F32).astype(partial.dtype)
    both_t[...] = both.T


def back_products(slots, starts, shards, stacked, both_t, before):
    wide = shards[0].shape[1]
    blocks, totals = [], [None, None] if before is None else [before[0], before[1]]
    for i, slot in enumerate(slots):
        decoder = stacked[:, block_of(starts, slot, wide)]
        block = 0.0
        for chain in range(2):
            error = shards[2 * i + chain][...]
            block = block + jnp.dot(both_t[chain][...], error, preferred_element_type=F32)
            term = lax.dot_general(error, decoder, OVER_COLS, preferred_element_type=F32)
            totals[chain] = term if totals[chain] is None else totals[chain] + term
        blocks.append(block)
    return blocks, totals


def back_kernel(slots, first, starts, *refs):
    count = 2 * len(slots)
    shards, (stacked, *both_t), (*before, outer, back) = refs[:count], refs[count:count + 3], refs[count + 3:]
    blocks, totals = back_products(slots, starts, shards, stacked, both_t, None if first else before[0])
    for i, block in enumerate(blocks):
        outer[i] = block
    for chain in range(2):
        back[chain] = totals[chain]


def last_back_kernel(slots, far, starts, *refs):
    near_refs, (before, same, back_own, sent, high) = refs[:-5], refs[-5:]
    shards, (stacked, *both_t), outers = near_refs[:2], near_refs[2:5], near_refs[5:]
    (block,), totals = back_products((far,), starts, shards, stacked, both_t, before)
    rows, wide = shards[0].shape
    lat = high.shape[1]
    half_width = high.shape[0]
    for chain in range(2):
        back_own[chain * rows:(chain + 1) * rows, :] = totals[chain][:, :lat]
        sent[chain * rows:(chain + 1) * rows, :] = totals[chain][:, lat:]
    same[...] = block[:lat]
    pieces = [(far, block[lat:])]
    for group, outer in zip(slots, outers):
        pieces += [(slot, outer[i, lat:]) for i, slot in enumerate(group)]
    for slot, piece in pieces:
        start = pl.multiple_of(starts[slot], wide)

        @pl.when(start < half_width)
        def _():
            for c in range(0, wide, lat):
                sent[pl.ds(2 * rows + start + c, lat), :] = piece[:, c:c + lat]

        @pl.when(start >= half_width)
        def _():
            for c in range(0, wide, lat):
                high[pl.ds(start - half_width + c, lat), :] = piece[:, c:c + lat]


def finish_kernel(slots, far, starts, *refs):
    turned, pre_0, pre_1, back_own, arrived, high, last_same, *outers = refs[:7 + len(slots)]
    grad, bias, same, cross, stage, value, grad_sems, same_sems, cross_sems = refs[7 + len(slots):]
    pieces, height, lat = stage.shape
    rows = pre_0.shape[0]
    half_width = high.shape[0]
    wide = last_same.shape[1]
    copies = []
    blocks = [(far, last_same)]
    for group, outer in zip(slots, outers):
        blocks += [(slot, outer.at[i, :lat, :]) for i, slot in enumerate(group)]
    for i, (slot, block) in enumerate(blocks):
        copies.append(pltpu.make_async_copy(block, same.at[0, :, block_of(starts, slot, wide)], same_sems.at[i]))
        copies[-1].start()
    first = starts[starts.shape[0] - 1] == 0
    steps = range(half_width // lat)
    for c in steps:
        at = pl.ds(c * lat, lat)

        @pl.when(first)
        def _():
            source = arrived.at[pl.ds(2 * rows + c * lat, lat), :]
            pltpu.make_async_copy(source, cross.at[:, at], cross_sems.at[c]).start()

        @pl.when(jnp.logical_not(first))
        def _():
            pltpu.make_async_copy(high.at[at, :], cross.at[:, at], cross_sems.at[c]).start()

        copies.append(pltpu.make_async_copy(high.at[at, :], cross.at[:, at], cross_sems.at[c]))
    total = 0.0
    for chain, preact in enumerate((pre_0, pre_1)):
        at = slice(chain * rows, (chain + 1) * rows)
        masked = jnp.where(preact[...] > 0, back_own[at, :] + arrived[at, :], 0.0).astype(BF16)
        value[at, :] = masked
        total = total + jnp.sum(masked.astype(F32), axis=0, keepdims=True)
    bias[...] = total
    for i in range(pieces):
        at = pl.ds(i * height, height)
        stage[i] = jnp.dot(turned[at, :], value[...], preferred_element_type=F32)
        copies.append(pltpu.make_async_copy(stage.at[i], grad.at[0, at, :], grad_sems.at[i]))
        copies[-1].start()
    for copy in copies:
        copy.wait()


def ring_shards(residual_in, targets, enc_weight, enc_bias, dec_same, dec_cross):
    size = lax.axis_size("latent")
    reach = size // 2
    place = ring_place(lax.axis_index("latent"), size)
    layer = lax.axis_index("layer")
    sign = jnp.where(layer % 2 == 0, 1, -1)
    rows, wide = residual_in.shape[1:]
    half = rows // 2
    deep, lat = enc_weight.shape[1:]
    half_width = deep // 2
    err_scale = 1.0 / math.sqrt(rows)
    shape = jax.ShapeDtypeStruct
    unit = rows * wide * lat
    chains = (0, 1)

    def halves(array):
        return [array[:half], array[half:]]

    slot_p = {s: 2 * s - 1 for s in range(1, reach)}
    slot_q = {s: 2 * s for s in range(1, reach)}
    far = size - 1
    offsets = [0] * size
    offsets[far] = reach
    for s in range(1, reach):
        offsets[slot_p[s]] = -s
        offsets[slot_q[s]] = s
    starts = jnp.stack([ring_member(place + sign * offset, size) * wide for offset in offsets] + [layer])
    starts = starts.astype(jnp.int32)

    def gather_step(found, s):
        for chain in chains:
            at_p, at_q = (0, 0) if s == 1 else (slot_p[s - 1], slot_q[s - 1])
            if s < reach:
                pair = hop(found[chain][at_p], 1), hop(found[chain][at_q], -1)
                found[chain][slot_p[s]], found[chain][slot_q[s]] = lax.optimization_barrier(pair)
            else:
                found[chain][far] = hop(found[chain][at_q if chain else at_p], -1 if chain else 1)

    inputs = [[part] + [None] * (size - 1) for part in halves(residual_in[0])]
    for s in range(1, reach + 1):
        gather_step(inputs, s)
    low_cross = passed_along(dec_cross, "layer", 1)
    stacked, weight = call(
        prepare_kernel,
        [shape((2 * lat, deep), BF16), shape((deep, lat), BF16)],
        0,
        [starts, dec_same, low_cross, dec_cross, enc_weight],
    )
    early = tuple(range(size - 1))
    preacts, codes, earlier = [], [], []
    for chain in chains:
        part = call(
            functools.partial(encode_kernel, early, False),
            [shape((half, lat), F32)],
            unit * len(early),
            [starts] + inputs[chain][:-1] + [weight, enc_bias],
        )[0]
        preact, now = call(
            functools.partial(encode_kernel, (far,), True),
            [shape((half, lat), F32), shape((half, lat), BF16)],
            unit,
            [starts, inputs[chain][far], weight, part],
        )
        preacts.append(preact)
        codes.append(now)
        earlier.append(passed_along(now, "layer", 1))

    spread = (far,) + tuple(slot for s in range(reach - 1, 0, -1) for slot in (slot_q[s], slot_p[s])) + (0,)
    partial, both_t, ahead, behind = [], [], [], []
    for chain in chains:
        instant = {far, slot_q.get(reach - 1) if chain else slot_p.get(reach - 1)}
        *pieces, turned_codes = call(
            functools.partial(spread_kernel, spread),
            [shape((half, wide), BF16 if slot in instant else F32) for slot in spread]
            + [shape((2 * lat, half), BF16)],
            2 * unit * len(spread),
            [starts, codes[chain], earlier[chain], stacked],
        )
        partial.append(dict(zip(spread, pieces)))
        both_t.append(turned_codes)
    both = [shard for pair in zip(*inputs) for shard in pair]
    turned = call(turn_kernel, [shape((deep, rows), BF16)], unit, [starts] + both)[0]
    ahead = [hop(partial[0][far], 1), None]
    behind = [None, hop(partial[1][far], -1)]
    for s in range(reach - 1, 0, -1):
        for chain in chains:
            plus, minus = partial[chain][slot_q[s]], partial[chain][slot_p[s]]
            if ahead[chain] is not None:
                plus = (plus + ahead[chain].astype(F32)).astype(BF16)
            if behind[chain] is not None:
                minus = (minus + behind[chain].astype(F32)).astype(BF16)
            ahead[chain] = hop(plus, 1)
            behind[chain] = hop(minus, -1)
    errors = []
    for chain, wanted in zip(chains, halves(targets[0])):
        total = partial[chain][0]
        for arrived in (ahead[chain], behind[chain]):
            if arrived is not None:
                total = total + arrived.astype(F32)
        if chain == 1:
            wanted = after(wanted, errors[0][0])
        errors.append([((total - wanted.astype(F32)) * err_scale).astype(BF16)] + [None] * (size - 1))

    def near(slots):
        return [errors[chain][slot] for slot in slots for chain in chains]

    def back(slots, before):
        return call(
            functools.partial(back_kernel, slots, before is None),
            [shape((len(slots), 2 * lat, wide), F32), shape((2, half, 2 * lat), F32)],
            4 * unit * len(slots),
            [starts] + near(slots) + [stacked] + both_t + ([] if before is None else [before]),
        )

    groups, outers, acc, pending = [], [], None, [0]
    for s in range(1, reach + 1):
        gather_step(errors, s)
        if s < reach:
            pending += [slot_p[s], slot_q[s]]
        if s == 1 or s == reach - 1:
            groups.append(tuple(pending))
            outer, acc = back(groups[-1], acc)
            outers.append(outer)
            pending = []
    if not groups:
        groups.append((0,))
        outer, acc = back(groups[-1], acc)
        outers.append(outer)
    last_same, back_own, sent, high = call(
        functools.partial(last_back_kernel, groups, far),
        [
            shape((lat, wide), F32),
            shape((rows, lat), F32),
            shape((rows + half_width, lat), F32),
            shape((half_width, lat), F32),
        ],
        4 * unit,
        [starts] + near((far,)) + [stacked] + both_t + outers + [acc],
    )
    arrived = passed_along(sent, "layer", -1)
    height = deep // PIECES
    grad_enc, grad_bias, grad_same, grad_cross = call(
        functools.partial(finish_kernel, groups, far),
        [
            shape((1, deep, lat), F32),
            shape((1, lat), F32),
            shape((1, lat, deep), F32),
            shape((lat, half_width), F32),
        ],
        2 * unit * size,
        [starts, turned] + preacts + [back_own, arrived, high, last_same] + outers,
        out_spaces=[pl.ANY, pltpu.VMEM, pl.ANY, pl.ANY],
        scratch=[
            pltpu.VMEM((PIECES, height, lat), F32),
            pltpu.VMEM((rows, lat), BF16),
            pltpu.SemaphoreType.DMA((PIECES,)),
            pltpu.SemaphoreType.DMA((size,)),
            pltpu.SemaphoreType.DMA((half_width // lat,)),
        ],
    )
    return (grad_enc, grad_bias, grad_same, grad_cross)


def wide_shards(residual_in, targets, enc_weight, enc_bias, dec_same, dec_cross):
    is_first = lax.axis_index("layer") == 0
    err_scale = 1.0 / math.sqrt(residual_in.shape[1])
    inputs = lax.all_gather(residual_in[0], "latent", axis=1, tiled=True)
    preact = matmul(inputs, enc_weight[0]) + enc_bias[0]
    codes_now = jnp.maximum(preact, 0.0).astype(BF16)
    earlier = passed_along(codes_now, "layer", 1)
    cross_full = lax.all_gather(dec_cross, "layer", axis=1, tiled=True)
    own_dec = dec_same[0]
    half_width = own_dec.shape[1] // 2
    recon_full = lax.psum(matmul(codes_now, own_dec) + matmul(earlier, cross_full), "latent")
    wanted = lax.all_gather(targets[0], "latent", axis=1, tiled=True)
    errors = ((recon_full - wanted.astype(F32)) * err_scale).astype(BF16)
    grad_same = matmul(codes_now, errors, OVER_ROWS)
    grad_full = matmul(earlier, errors, OVER_ROWS)
    returned = passed_along(grad_full[:, :half_width], "layer", -1)
    grad_cross = jnp.where(is_first, returned, grad_full[:, half_width:])
    from_next = passed_along(matmul(errors, cross_full, OVER_COLS), "layer", -1)
    grad_codes = matmul(errors, own_dec, OVER_COLS) + from_next
    grad_pre = jnp.where(preact > 0, grad_codes, 0.0).astype(BF16)
    grad_enc = matmul(inputs, grad_pre, OVER_ROWS)
    grad_bias = jnp.sum(grad_pre.astype(F32), axis=0)
    return (grad_enc[None], grad_bias[None], grad_same[None], grad_cross)


def solution(mesh):
    size = mesh.shape["latent"]
    placed = (
        P("layer", "groups", "latent"),
        P("layer", "groups", "latent"),
        P("layer", None, "latent"),
        P("layer", "latent"),
        P("layer", "latent", None),
        P("latent", "layer"),
    )
    return jax.shard_map(
        ring_shards if size % 2 == 0 and size <= RING_LIMIT else wide_shards,
        mesh=mesh,
        in_specs=placed,
        out_specs=(
            P(("groups", "layer"), None, "latent"),
            P(("groups", "layer"), "latent"),
            P(("groups", "layer"), "latent", None),
            P(("groups", "latent"), "layer"),
        ),
        check_vma=False,
    )
```

time: 295 us -> 101 us (0.34)
  waiting for transfers between devices: 256 us -> 29.6 us
  starting transfers between devices: 3.98 us -> 52.2 us
  Pallas kernels: 0 us -> 13.6 us
  between operations: 13.8 us -> 0.9 us
  matrix products: 10.2 us -> 0 us
  other arithmetic: 4.43 us -> 0.42 us
    psum x1 -> x0, waiting for transfers between devices: 158 us -> none  [shards(): recon_full = lax.psum(partial_value, 'latent')]
    all_gather x2 -> x0, waiting for transfers between devices: 96.6 us -> none  [the longest x1 52.7 us: shards(): inputs = lax.all_gather(residual_in[0], 'latent', axis=1, tiled=True)]
    ppermute x0 -> x42, starting transfers between devices: none -> 46.5 us  [hop(): return lax.ppermute(shard, ('latent', 'layer'), pairs)]
    ppermute x0 -> x42, waiting for transfers between devices: none -> 27.9 us  [hop(): return lax.ppermute(shard, ('latent', 'layer'), pairs)]
    pallas_call x0 -> x12, Pallas kernels: none -> 13.6 us  [call(): pl.pallas_call(kernel, out_shape=outs, in_specs=[spec(pltpu.SMEM)] + [spe...]
    dot_general x8 -> x0, matrix products: 10.2 us -> none  [the longest x1 2.68 us: shards(): jnp.dot(earlier, cross_full, preferred_element_type=jnp.float32)]
    convert_element_type x1 -> x12, other arithmetic: 3.58 us -> 0.42 us  [the longest x5 0.14 us: ring_shards(): minus = (minus + behind[chain].astype(F32)).astype(BF16)]
  transfers between devices with their start and end apart: 6 -> 46, of which waited for: 4 -> 27; matrix products, arithmetic and copies ran while one was open for 4% -> 1% of each run, Pallas kernels for 0% -> 9%
where the time goes in v5:
time: 101 us
  starting transfers between devices  52.2 us (52%)
  waiting for transfers between devices  29.6 us (29%)
  Pallas kernels  13.6 us (13%)
  local copies, waits for them, and re-layouts  4.12 us (4%)
    ppermute x42, starting transfers between devices, hop(): return lax.ppermute(shard, ('latent', 'layer'), pairs)  46.5 us
    ppermute x42, waiting for transfers between devices, hop(): return lax.ppermute(shard, ('latent', 'layer'), pairs)  27.9 us
    pallas_call x12, Pallas kernels, call(): pl.pallas_call(kernel, out_shape=outs, in_specs=[spec(pltpu.SMEM)] + [spe...  13.6 us
    ppermute x4, starting transfers between devices, passed_along(): return lax.ppermute(shard, axis, pairs)  5.62 us
    unnamed x10, local copies, waits for them, and re-layouts  3.04 us
  transfers between devices with their start and end apart: 46, of which 27 were waited for; matrix products, arithmetic and copies ran while one was open for 1% of the time, Pallas kernels for 9%

profile of v5, /device:TPU:0, one launch (start us, length us, event | category | flops | bytes accessed | tf_op | source)
XLA Modules:
  0.0 100.9 jit_solution(8588325730873088233)
XLA Ops:
  1.6 3.0 %collective-permute-start.1 = (bf16[256,256]{1,0:T(8,128)(2,1)S(1)}, bf16[256,256]{1,0:T(8,128)(2,1)S(1)}, u32[]{:S(2)}, u32[]{:S(2)}) collective-permute-start(bf16[256,256]{1,0:T(8,128)(2,1)S(1)} %get-tuple-element.119.refs_0_), channel_id=1, source_target_pairs={{0,2},{1,5},{4,0},{5,9},{8,4},{9,13},{12,8},{13,15},{14,12},{15,11... | collective-permute-start | bytes 393224 | tf_op jit(solution)/shard_map/ppermute | solution.py:51
  4.8 1.9 %collective-permute-start.3 = (bf16[256,256]{1,0:T(8,128)(2,1)S(1)}, bf16[256,256]{1,0:T(8,128)(2,1)S(1)}, u32[]{:S(2)}, u32[]{:S(2)}) collective-permute-start(bf16[256,256]{1,0:T(8,128)(2,1)S(1)} %get-tuple-element.118.refs_1_.refs_0_), channel_id=1, source_target_pairs={{0,2},{1,5},{4,0},{5,9},{8,4},{9,13},{12,8},{13,15},{14,12},{15,11... | collective-permute-start | bytes 393224 | tf_op jit(solution)/shard_map/ppermute | solution.py:51
  6.8 1.7 %collective-permute-done.1.refs_4_.refs_2_ = bf16[256,256]{1,0:T(8,128)(2,1)S(1)} collective-permute-done((bf16[256,256]{1,0:T(8,128)(2,1)S(1)}, bf16[256,256]{1,0:T(8,128)(2,1)S(1)}, u32[]{:S(2)}, u32[]{:S(2)}) %collective-permute-start.1) | collective-permute-done | bytes 131104 | tf_op jit(solution)/shard_map/ppermute | solution.py:51
  9.7 1.5 %collective-permute-start.4 = (bf16[256,256]{1,0:T(8,128)(2,1)S(1)}, bf16[256,256]{1,0:T(8,128)(2,1)S(1)}, u32[]{:S(2)}, u32[]{:S(2)}) collective-permute-start(bf16[256,256]{1,0:T(8,128)(2,1)S(1)} %collective-permute-done.refs_2_.refs_1_), channel_id=1, source_target_pairs={{0,4},{1,3},{4,8},{5,1},{8,12},{9,5},{12,14},{13,9},{14,10},{15,13... | collective-permute-start | bytes 393224 | tf_op jit(solution)/shard_map/ppermute | solution.py:51
  11.7 2.0 %collective-permute-start.6 = (bf16[256,256]{1,0:T(8,128)(2,1)S(1)}, bf16[256,256]{1,0:T(8,128)(2,1)S(1)}, u32[]{:S(2)}, u32[]{:S(2)}) collective-permute-start(bf16[256,256]{1,0:T(8,128)(2,1)S(1)} %collective-permute-done.2.refs_3_.refs_1_), channel_id=1, source_target_pairs={{0,4},{1,3},{4,8},{5,1},{8,12},{9,5},{12,14},{13,9},{14,10},{15,13... | collective-permute-start | bytes 393224 | tf_op jit(solution)/shard_map/ppermute | solution.py:51
  13.7 1.7 %collective-permute-start.14 = (bf16[128,1024]{1,0:T(8,128)(2,1)}, bf16[128,1024]{1,0:T(8,128)(2,1)S(1)}, u32[]{:S(2)}, u32[]{:S(2)}) collective-permute-start(bf16[128,1024]{1,0:T(8,128)(2,1)} %high_cross.1), channel_id=1, source_target_pairs={{0,1},{2,3},{4,5},{6,7},{8,9},{10,11},{12,13},{14,15},{16,17},{18,... | collective-permute-start | bytes 786440 | tf_op jit(solution)/shard_map/ppermute | solution.py:23
  15.9 1.6 %collective-permute-done.5.refs_8_.refs_4_ = bf16[256,256]{1,0:T(8,128)(2,1)S(1)} collective-permute-done((bf16[256,256]{1,0:T(8,128)(2,1)S(1)}, bf16[256,256]{1,0:T(8,128)(2,1)S(1)}, u32[]{:S(2)}, u32[]{:S(2)}) %collective-permute-start.5) | collective-permute-done | bytes 131104 | tf_op jit(solution)/shard_map/ppermute | solution.py:51
  17.5 1.7 %collective-permute-start.8 = (bf16[256,256]{1,0:T(8,128)(2,1)S(1)}, bf16[256,256]{1,0:T(8,128)(2,1)S(1)}, u32[]{:S(2)}, u32[]{:S(2)}) collective-permute-start(bf16[256,256]{1,0:T(8,128)(2,1)S(1)} %collective-permute-done.4.refs_6_.refs_3_), channel_id=1, source_target_pairs={{0,4},{1,3},{4,8},{5,1},{8,12},{9,5},{12,14},{13,9},{14,10},{15,13... | collective-permute-start | bytes 393224 | tf_op jit(solution)/shard_map/ppermute | solution.py:51
  20.2 1.7 %collective-permute-start.10 = (bf16[256,256]{1,0:T(8,128)(2,1)S(1)}, bf16[256,256]{1,0:T(8,128)(2,1)S(1)}, u32[]{:S(2)}, u32[]{:S(2)}) collective-permute-start(bf16[256,256]{1,0:T(8,128)(2,1)S(1)} %collective-permute-done.6.refs_7_.refs_3_), channel_id=1, source_target_pairs={{0,4},{1,3},{4,8},{5,1},{8,12},{9,5},{12,14},{13,9},{14,10},{15,13... | collective-permute-start | bytes 393224 | tf_op jit(solution)/shard_map/ppermute | solution.py:51
  22.2 1.5 %collective-permute-done.8.refs_10_.refs_5_ = bf16[256,256]{1,0:T(8,128)(2,1)S(1)} collective-permute-done((bf16[256,256]{1,0:T(8,128)(2,1)S(1)}, bf16[256,256]{1,0:T(8,128)(2,1)S(1)}, u32[]{:S(2)}, u32[]{:S(2)}) %collective-permute-start.8) | collective-permute-done | bytes 131104 | tf_op jit(solution)/shard_map/ppermute | solution.py:51
  23.7 1.8 %collective-permute-done.9.refs_12_.refs_6_ = bf16[256,256]{1,0:T(8,128)(2,1)S(1)} collective-permute-done((bf16[256,256]{1,0:T(8,128)(2,1)S(1)}, bf16[256,256]{1,0:T(8,128)(2,1)S(1)}, u32[]{:S(2)}, u32[]{:S(2)}) %collective-permute-start.9) | collective-permute-done | bytes 131104 | tf_op jit(solution)/shard_map/ppermute | solution.py:51
  25.5 1.4 %collective-permute-start.12 = (bf16[256,256]{1,0:T(8,128)(2,1)S(1)}, bf16[256,256]{1,0:T(8,128)(2,1)S(1)}, u32[]{:S(2)}, u32[]{:S(2)}) collective-permute-start(bf16[256,256]{1,0:T(8,128)(2,1)S(1)} %collective-permute-done.8.refs_10_.refs_5_), channel_id=1, source_target_pairs={{0,4},{1,3},{4,8},{5,1},{8,12},{9,5},{12,14},{13,9},{14,10},{15,13... | collective-permute-start | bytes 393224 | tf_op jit(solution)/shard_map/ppermute | solution.py:51
  38.3 1.6 %collective-permute-start.16 = (bf16[256,256]{1,0:T(8,128)(2,1)S(1)}, bf16[256,256]{1,0:T(8,128)(2,1)S(1)}, u32[]{:S(2)}, u32[]{:S(2)}) collective-permute-start(bf16[256,256]{1,0:T(8,128)(2,1)S(1)} %get-tuple-element.82), channel_id=1, source_target_pairs={{0,4},{1,3},{4,8},{5,1},{8,12},{9,5},{12,14},{13,9},{14,10},{15,13... | collective-permute-start | bytes 393224 | tf_op jit(solution)/shard_map/ppermute | solution.py:51
  41.4 1.6 %collective-permute-start.31 = (bf16[256,256]{1,0:T(8,128)(2,1)S(1)}, bf16[256,256]{1,0:T(8,128)(2,1)S(1)}, u32[]{:S(2)}, u32[]{:S(2)}) collective-permute-start(bf16[256,256]{1,0:T(8,128)(2,1)S(1)} %get-tuple-element.95), channel_id=1, source_target_pairs={{0,4},{1,3},{4,8},{5,1},{8,12},{9,5},{12,14},{13,9},{14,10},{15,13... | collective-permute-start | bytes 393224 | tf_op jit(solution)/shard_map/ppermute | solution.py:51
  43.7 2.2 %collective-permute-start.17 = (bf16[256,256]{1,0:T(8,128)(2,1)S(1)}, bf16[256,256]{1,0:T(8,128)(2,1)S(1)}, u32[]{:S(2)}, u32[]{:S(2)}) collective-permute-start(bf16[256,256]{1,0:T(8,128)(2,1)S(1)} %add_convert_fusion.9), channel_id=1, source_target_pairs={{0,4},{1,3},{4,8},{5,1},{8,12},{9,5},{12,14},{13,9},{14,10},{15,13... | collective-permute-start | bytes 393224 | tf_op jit(solution)/shard_map/ppermute | solution.py:51
  47.6 1.6 %collective-permute-start.32 = (bf16[256,256]{1,0:T(8,128)(2,1)S(1)}, bf16[256,256]{1,0:T(8,128)(2,1)S(1)}, u32[]{:S(2)}, u32[]{:S(2)}) collective-permute-start(bf16[256,256]{1,0:T(8,128)(2,1)S(1)} %add_convert_fusion.4), channel_id=1, source_target_pairs={{0,4},{1,3},{4,8},{5,1},{8,12},{9,5},{12,14},{13,9},{14,10},{15,13... | collective-permute-start | bytes 393224 | tf_op jit(solution)/shard_map/ppermute | solution.py:51
  49.9 2.4 %collective-permute-start.18 = (bf16[256,256]{1,0:T(8,128)(2,1)S(1)}, bf16[256,256]{1,0:T(8,128)(2,1)S(1)}, u32[]{:S(2)}, u32[]{:S(2)}) collective-permute-start(bf16[256,256]{1,0:T(8,128)(2,1)S(1)} %add_convert_fusion.8), channel_id=1, source_target_pairs={{0,4},{1,3},{4,8},{5,1},{8,12},{9,5},{12,14},{13,9},{14,10},{15,13... | collective-permute-start | bytes 393224 | tf_op jit(solution)/shard_map/ppermute | solution.py:51
  53.2 1.8 %collective-permute-start.33 = (bf16[256,256]{1,0:T(8,128)(2,1)S(1)}, bf16[256,256]{1,0:T(8,128)(2,1)S(1)}, u32[]{:S(2)}, u32[]{:S(2)}) collective-permute-start(bf16[256,256]{1,0:T(8,128)(2,1)S(1)} %add_convert_fusion.3), channel_id=1, source_target_pairs={{0,4},{1,3},{4,8},{5,1},{8,12},{9,5},{12,14},{13,9},{14,10},{15,13... | collective-permute-start | bytes 393224 | tf_op jit(solution)/shard_map/ppermute | solution.py:51
  56.2 1.5 %collective-permute-start.19 = (bf16[256,256]{1,0:T(8,128)(2,1)S(1)}, bf16[256,256]{1,0:T(8,128)(2,1)S(1)}, u32[]{:S(2)}, u32[]{:S(2)}) collective-permute-start(bf16[256,256]{1,0:T(8,128)(2,1)S(1)} %add_convert_fusion.7), channel_id=1, source_target_pairs={{0,4},{1,3},{4,8},{5,1},{8,12},{9,5},{12,14},{13,9},{14,10},{15,13... | collective-permute-start | bytes 393224 | tf_op jit(solution)/shard_map/ppermute | solution.py:51
  57.6 2.9 %collective-permute-done.36 = bf16[256,256]{1,0:T(8,128)(2,1)S(1)} collective-permute-done((bf16[256,256]{1,0:T(8,128)(2,1)S(1)}, bf16[256,256]{1,0:T(8,128)(2,1)S(1)}, u32[]{:S(2)}, u32[]{:S(2)}) %collective-permute-start.36) | collective-permute-done | bytes 131104 | tf_op jit(solution)/shard_map/ppermute | solution.py:51
  61.2 1.4 %collective-permute-done.19 = bf16[256,256]{1,0:T(8,128)(2,1)S(1)} collective-permute-done((bf16[256,256]{1,0:T(8,128)(2,1)S(1)}, bf16[256,256]{1,0:T(8,128)(2,1)S(1)}, u32[]{:S(2)}, u32[]{:S(2)}) %collective-permute-start.19) | collective-permute-done | bytes 131104 | tf_op jit(solution)/shard_map/ppermute | solution.py:51
  62.6 2.0 %collective-permute-start.24 = (bf16[256,256]{1,0:T(8,128)(2,1)S(1)}, bf16[256,256]{1,0:T(8,128)(2,1)S(1)}, u32[]{:S(2)}, u32[]{:S(2)}) collective-permute-start(bf16[256,256]{1,0:T(8,128)(2,1)S(1)} %fusion.1.refs_0_), channel_id=1, source_target_pairs={{0,2},{1,5},{4,0},{5,9},{8,4},{9,13},{12,8},{13,15},{14,12},{15,11... | collective-permute-start | bytes 393224 | tf_op jit(solution)/shard_map/ppermute | solution.py:51
  64.7 2.0 %collective-permute-done.37 = bf16[256,256]{1,0:T(8,128)(2,1)S(1)} collective-permute-done((bf16[256,256]{1,0:T(8,128)(2,1)S(1)}, bf16[256,256]{1,0:T(8,128)(2,1)S(1)}, u32[]{:S(2)}, u32[]{:S(2)}) %collective-permute-start.37) | collective-permute-done | bytes 131104 | tf_op jit(solution)/shard_map/ppermute | solution.py:51
  66.9 2.0 %collective-permute-start.38 = (bf16[256,256]{1,0:T(8,128)(2,1)S(1)}, bf16[256,256]{1,0:T(8,128)(2,1)S(1)}, u32[]{:S(2)}, u32[]{:S(2)}) collective-permute-start(bf16[256,256]{1,0:T(8,128)(2,1)S(1)} %multiply_convert_fusion.refs_1_), channel_id=1, source_target_pairs={{0,4},{1,3},{4,8},{5,1},{8,12},{9,5},{12,14},{13,9},{14,10},{15,13... | collective-permute-start | bytes 393224 | tf_op jit(solution)/shard_map/ppermute | solution.py:51
  70.9 2.0 %collective-permute-start.26 = (bf16[256,256]{1,0:T(8,128)(2,1)S(1)}, bf16[256,256]{1,0:T(8,128)(2,1)S(1)}, u32[]{:S(2)}, u32[]{:S(2)}) collective-permute-start(bf16[256,256]{1,0:T(8,128)(2,1)S(1)} %collective-permute-done.24.refs_4_), channel_id=1, source_target_pairs={{0,2},{1,5},{4,0},{5,9},{8,4},{9,13},{12,8},{13,15},{14,12},{15,11... | collective-permute-start | bytes 393224 | tf_op jit(solution)/shard_map/ppermute | solution.py:51
  75.2 1.5 %collective-permute-done.25.refs_0_ = bf16[256,256]{1,0:T(8,128)(2,1)S(1)} collective-permute-done((bf16[256,256]{1,0:T(8,128)(2,1)S(1)}, bf16[256,256]{1,0:T(8,128)(2,1)S(1)}, u32[]{:S(2)}, u32[]{:S(2)}) %collective-permute-start.25) | collective-permute-done | bytes 131104 | tf_op jit(solution)/shard_map/ppermute | solution.py:51
  76.7 1.7 %collective-permute-start.27 = (bf16[256,256]{1,0:T(8,128)(2,1)S(1)}, bf16[256,256]{1,0:T(8,128)(2,1)S(1)}, u32[]{:S(2)}, u32[]{:S(2)}) collective-permute-start(bf16[256,256]{1,0:T(8,128)(2,1)S(1)} %collective-permute-done.25.refs_0_), channel_id=1, source_target_pairs={{0,4},{1,3},{4,8},{5,1},{8,12},{9,5},{12,14},{13,9},{14,10},{15,13... | collective-permute-start | bytes 393224 | tf_op jit(solution)/shard_map/ppermute | solution.py:51
  79.9 2.7 %collective-permute-start.42 = (bf16[256,256]{1,0:T(8,128)(2,1)S(1)}, bf16[256,256]{1,0:T(8,128)(2,1)S(1)}, u32[]{:S(2)}, u32[]{:S(2)}) collective-permute-start(bf16[256,256]{1,0:T(8,128)(2,1)S(1)} %collective-permute-done.40.refs_1_), channel_id=1, source_target_pairs={{0,4},{1,3},{4,8},{5,1},{8,12},{9,5},{12,14},{13,9},{14,10},{15,13... | collective-permute-start | bytes 393224 | tf_op jit(solution)/shard_map/ppermute | solution.py:51
  85.1 2.4 %collective-permute-done.43.refs_7_ = bf16[256,256]{1,0:T(8,128)(2,1)S(1)} collective-permute-done((bf16[256,256]{1,0:T(8,128)(2,1)S(1)}, bf16[256,256]{1,0:T(8,128)(2,1)S(1)}, u32[]{:S(2)}, u32[]{:S(2)}) %collective-permute-start.43) | collective-permute-done | bytes 131104 | tf_op jit(solution)/shard_map/ppermute | solution.py:51
  90.0 2.5 %collective-permute-done.44.refs_1_ = bf16[256,256]{1,0:T(8,128)(2,1)S(1)} collective-permute-done((bf16[256,256]{1,0:T(8,128)(2,1)S(1)}, bf16[256,256]{1,0:T(8,128)(2,1)S(1)}, u32[]{:S(2)}, u32[]{:S(2)}) %collective-permute-start.44) | collective-permute-done | bytes 131104 | tf_op jit(solution)/shard_map/ppermute | solution.py:51
  96.0 1.7 %collective-permute-done.45.refs_4_ = f32[1536,128]{1,0:T(8,128)S(1)} collective-permute-done((f32[1536,128]{1,0:T(8,128)S(1)}, f32[1536,128]{1,0:T(8,128)S(1)}, u32[]{:S(2)}, u32[]{:S(2)}) %collective-permute-start.45) | collective-permute-done | bytes 786464 | tf_op jit(solution)/shard_map/ppermute | solution.py:23
  97.7 3.1 %shard_map.104 = (f32[1,2048,128]{2,1,0:T(8,128)}, f32[1,128]{1,0:T(1,128)}, f32[1,128,2048]{2,1,0:T(8,128)}, f32[128,1024]{1,0:T(8,128)}) custom-call(s32[9]{0:T(128)S(1)} %stack.39.starts, bf16[2048,512]{1,0:T(8,128)(2,1)S(1)} %shard_map.93.refs_0_, f32[256,128]{1,0:T(8,128)S(1)} %get-tuple-element.74.refs_1_, f32[256,128]{1,0:T(8,128)S(1)} %get-tuple-element.75.refs_2_, ...), custom_call_target="tpu_custom_call" | custom-call | flops 268435456 | bytes 8520228 | tf_op jit(solution)/shard_map/pallas_call | solution.py:65
  (97 shorter events, 37.6 us)
Async XLA Ops:
  1.6 6.9 %collective-permute-start.1 = (bf16[256,256]{1,0:T(8,128)(2,1)S(1)}, bf16[256,256]{1,0:T(8,128)(2,1)S(1)}, u32[]{:S(2)}, u32[]{:S(2)}) collective-permute-start(bf16[256,256]{1,0:T(8,128)(2,1)S(1)} %get-tuple-element.119.refs_0_), channel_id=1, source_target_pairs={{0,2},{1,5},{4,0},{5,9},{8,4},{9,13},{12,8},{13,15},{14,12},{15,11... | collective-permute-start | bytes 393224 | tf_op jit(solution)/shard_map/ppermute | solution.py:51
  4.8 6.9 %collective-permute-start.3 = (bf16[256,256]{1,0:T(8,128)(2,1)S(1)}, bf16[256,256]{1,0:T(8,128)(2,1)S(1)}, u32[]{:S(2)}, u32[]{:S(2)}) collective-permute-start(bf16[256,256]{1,0:T(8,128)(2,1)S(1)} %get-tuple-element.118.refs_1_.refs_0_), channel_id=1, source_target_pairs={{0,2},{1,5},{4,0},{5,9},{8,4},{9,13},{12,8},{13,15},{14,12},{15,11... | collective-permute-start | bytes 393224 | tf_op jit(solution)/shard_map/ppermute | solution.py:51
  9.7 6.2 %collective-permute-start.4 = (bf16[256,256]{1,0:T(8,128)(2,1)S(1)}, bf16[256,256]{1,0:T(8,128)(2,1)S(1)}, u32[]{:S(2)}, u32[]{:S(2)}) collective-permute-start(bf16[256,256]{1,0:T(8,128)(2,1)S(1)} %collective-permute-done.refs_2_.refs_1_), channel_id=1, source_target_pairs={{0,4},{1,3},{4,8},{5,1},{8,12},{9,5},{12,14},{13,9},{14,10},{15,13... | collective-permute-start | bytes 393224 | tf_op jit(solution)/shard_map/ppermute | solution.py:51
  11.2 6.3 %collective-permute-start.5 = (bf16[256,256]{1,0:T(8,128)(2,1)S(1)}, bf16[256,256]{1,0:T(8,128)(2,1)S(1)}, u32[]{:S(2)}, u32[]{:S(2)}) collective-permute-start(bf16[256,256]{1,0:T(8,128)(2,1)S(1)} %collective-permute-done.1.refs_4_.refs_2_), channel_id=1, source_target_pairs={{0,2},{1,5},{4,0},{5,9},{8,4},{9,13},{12,8},{13,15},{14,12},{15,11... | collective-permute-start | bytes 393224 | tf_op jit(solution)/shard_map/ppermute | solution.py:51
  11.7 7.8 %collective-permute-start.6 = (bf16[256,256]{1,0:T(8,128)(2,1)S(1)}, bf16[256,256]{1,0:T(8,128)(2,1)S(1)}, u32[]{:S(2)}, u32[]{:S(2)}) collective-permute-start(bf16[256,256]{1,0:T(8,128)(2,1)S(1)} %collective-permute-done.2.refs_3_.refs_1_), channel_id=1, source_target_pairs={{0,4},{1,3},{4,8},{5,1},{8,12},{9,5},{12,14},{13,9},{14,10},{15,13... | collective-permute-start | bytes 393224 | tf_op jit(solution)/shard_map/ppermute | solution.py:51
  13.7 6.5 %collective-permute-start.7 = (bf16[256,256]{1,0:T(8,128)(2,1)S(1)}, bf16[256,256]{1,0:T(8,128)(2,1)S(1)}, u32[]{:S(2)}, u32[]{:S(2)}) collective-permute-start(bf16[256,256]{1,0:T(8,128)(2,1)S(1)} %collective-permute-done.3.refs_5_.refs_2_), channel_id=1, source_target_pairs={{0,2},{1,5},{4,0},{5,9},{8,4},{9,13},{12,8},{13,15},{14,12},{15,11... | collective-permute-start | bytes 393224 | tf_op jit(solution)/shard_map/ppermute | solution.py:51
  13.7 13.9 %collective-permute-start.14 = (bf16[128,1024]{1,0:T(8,128)(2,1)}, bf16[128,1024]{1,0:T(8,128)(2,1)S(1)}, u32[]{:S(2)}, u32[]{:S(2)}) collective-permute-start(bf16[128,1024]{1,0:T(8,128)(2,1)} %high_cross.1), channel_id=1, source_target_pairs={{0,1},{2,3},{4,5},{6,7},{8,9},{10,11},{12,13},{14,15},{16,17},{18,... | collective-permute-start | bytes 786440 | tf_op jit(solution)/shard_map/ppermute | solution.py:23
  17.5 6.2 %collective-permute-start.8 = (bf16[256,256]{1,0:T(8,128)(2,1)S(1)}, bf16[256,256]{1,0:T(8,128)(2,1)S(1)}, u32[]{:S(2)}, u32[]{:S(2)}) collective-permute-start(bf16[256,256]{1,0:T(8,128)(2,1)S(1)} %collective-permute-done.4.refs_6_.refs_3_), channel_id=1, source_target_pairs={{0,4},{1,3},{4,8},{5,1},{8,12},{9,5},{12,14},{13,9},{14,10},{15,13... | collective-permute-start | bytes 393224 | tf_op jit(solution)/shard_map/ppermute | solution.py:51
  19.2 6.2 %collective-permute-start.9 = (bf16[256,256]{1,0:T(8,128)(2,1)S(1)}, bf16[256,256]{1,0:T(8,128)(2,1)S(1)}, u32[]{:S(2)}, u32[]{:S(2)}) collective-permute-start(bf16[256,256]{1,0:T(8,128)(2,1)S(1)} %collective-permute-done.5.refs_8_.refs_4_), channel_id=1, source_target_pairs={{0,2},{1,5},{4,0},{5,9},{8,4},{9,13},{12,8},{13,15},{14,12},{15,11... | collective-permute-start | bytes 393224 | tf_op jit(solution)/shard_map/ppermute | solution.py:51
  20.2 6.7 %collective-permute-start.10 = (bf16[256,256]{1,0:T(8,128)(2,1)S(1)}, bf16[256,256]{1,0:T(8,128)(2,1)S(1)}, u32[]{:S(2)}, u32[]{:S(2)}) collective-permute-start(bf16[256,256]{1,0:T(8,128)(2,1)S(1)} %collective-permute-done.6.refs_7_.refs_3_), channel_id=1, source_target_pairs={{0,4},{1,3},{4,8},{5,1},{8,12},{9,5},{12,14},{13,9},{14,10},{15,13... | collective-permute-start | bytes 393224 | tf_op jit(solution)/shard_map/ppermute | solution.py:51
  25.5 6.8 %collective-permute-start.12 = (bf16[256,256]{1,0:T(8,128)(2,1)S(1)}, bf16[256,256]{1,0:T(8,128)(2,1)S(1)}, u32[]{:S(2)}, u32[]{:S(2)}) collective-permute-start(bf16[256,256]{1,0:T(8,128)(2,1)S(1)} %collective-permute-done.8.refs_10_.refs_5_), channel_id=1, source_target_pairs={{0,4},{1,3},{4,8},{5,1},{8,12},{9,5},{12,14},{13,9},{14,10},{15,13... | collective-permute-start | bytes 393224 | tf_op jit(solution)/shard_map/ppermute | solution.py:51
  27.0 8.2 %collective-permute-start.13 = (bf16[256,256]{1,0:T(8,128)(2,1)S(1)}, bf16[256,256]{1,0:T(8,128)(2,1)S(1)}, u32[]{:S(2)}, u32[]{:S(2)}) collective-permute-start(bf16[256,256]{1,0:T(8,128)(2,1)S(1)} %collective-permute-done.11.refs_13_.refs_6_), channel_id=1, source_target_pairs={{0,2},{1,5},{4,0},{5,9},{8,4},{9,13},{12,8},{13,15},{14,12},{15,11... | collective-permute-start | bytes 393224 | tf_op jit(solution)/shard_map/ppermute | solution.py:51
  39.9 6.3 %collective-permute-start.20 = (bf16[256,256]{1,0:T(8,128)(2,1)S(1)}, bf16[256,256]{1,0:T(8,128)(2,1)S(1)}, u32[]{:S(2)}, u32[]{:S(2)}) collective-permute-start(bf16[256,256]{1,0:T(8,128)(2,1)S(1)} %get-tuple-element.85), channel_id=1, source_target_pairs={{0,2},{1,5},{4,0},{5,9},{8,4},{9,13},{12,8},{13,15},{14,12},{15,11... | collective-permute-start | bytes 393224 | tf_op jit(solution)/shard_map/ppermute | solution.py:51
  41.4 6.1 %collective-permute-start.31 = (bf16[256,256]{1,0:T(8,128)(2,1)S(1)}, bf16[256,256]{1,0:T(8,128)(2,1)S(1)}, u32[]{:S(2)}, u32[]{:S(2)}) collective-permute-start(bf16[256,256]{1,0:T(8,128)(2,1)S(1)} %get-tuple-element.95), channel_id=1, source_target_pairs={{0,4},{1,3},{4,8},{5,1},{8,12},{9,5},{12,14},{13,9},{14,10},{15,13... | collective-permute-start | bytes 393224 | tf_op jit(solution)/shard_map/ppermute | solution.py:51
  43.0 6.2 %collective-permute-start.34 = (bf16[256,256]{1,0:T(8,128)(2,1)S(1)}, bf16[256,256]{1,0:T(8,128)(2,1)S(1)}, u32[]{:S(2)}, u32[]{:S(2)}) collective-permute-start(bf16[256,256]{1,0:T(8,128)(2,1)S(1)} %get-tuple-element.99), channel_id=1, source_target_pairs={{0,2},{1,5},{4,0},{5,9},{8,4},{9,13},{12,8},{13,15},{14,12},{15,11... | collective-permute-start | bytes 393224 | tf_op jit(solution)/shard_map/ppermute | solution.py:51
  43.7 6.2 %collective-permute-start.17 = (bf16[256,256]{1,0:T(8,128)(2,1)S(1)}, bf16[256,256]{1,0:T(8,128)(2,1)S(1)}, u32[]{:S(2)}, u32[]{:S(2)}) collective-permute-start(bf16[256,256]{1,0:T(8,128)(2,1)S(1)} %add_convert_fusion.9), channel_id=1, source_target_pairs={{0,4},{1,3},{4,8},{5,1},{8,12},{9,5},{12,14},{13,9},{14,10},{15,13... | collective-permute-start | bytes 393224 | tf_op jit(solution)/shard_map/ppermute | solution.py:51
  46.3 6.1 %collective-permute-start.21 = (bf16[256,256]{1,0:T(8,128)(2,1)S(1)}, bf16[256,256]{1,0:T(8,128)(2,1)S(1)}, u32[]{:S(2)}, u32[]{:S(2)}) collective-permute-start(bf16[256,256]{1,0:T(8,128)(2,1)S(1)} %add_convert_fusion.6), channel_id=1, source_target_pairs={{0,2},{1,5},{4,0},{5,9},{8,4},{9,13},{12,8},{13,15},{14,12},{15,11... | collective-permute-start | bytes 393224 | tf_op jit(solution)/shard_map/ppermute | solution.py:51
  49.2 6.2 %collective-permute-start.35 = (bf16[256,256]{1,0:T(8,128)(2,1)S(1)}, bf16[256,256]{1,0:T(8,128)(2,1)S(1)}, u32[]{:S(2)}, u32[]{:S(2)}) collective-permute-start(bf16[256,256]{1,0:T(8,128)(2,1)S(1)} %add_convert_fusion.2), channel_id=1, source_target_pairs={{0,2},{1,5},{4,0},{5,9},{8,4},{9,13},{12,8},{13,15},{14,12},{15,11... | collective-permute-start | bytes 393224 | tf_op jit(solution)/shard_map/ppermute | solution.py:51
  49.9 6.2 %collective-permute-start.18 = (bf16[256,256]{1,0:T(8,128)(2,1)S(1)}, bf16[256,256]{1,0:T(8,128)(2,1)S(1)}, u32[]{:S(2)}, u32[]{:S(2)}) collective-permute-start(bf16[256,256]{1,0:T(8,128)(2,1)S(1)} %add_convert_fusion.8), channel_id=1, source_target_pairs={{0,4},{1,3},{4,8},{5,1},{8,12},{9,5},{12,14},{13,9},{14,10},{15,13... | collective-permute-start | bytes 393224 | tf_op jit(solution)/shard_map/ppermute | solution.py:51
  52.3 8.8 %collective-permute-start.22 = (bf16[256,256]{1,0:T(8,128)(2,1)S(1)}, bf16[256,256]{1,0:T(8,128)(2,1)S(1)}, u32[]{:S(2)}, u32[]{:S(2)}) collective-permute-start(bf16[256,256]{1,0:T(8,128)(2,1)S(1)} %add_convert_fusion.5), channel_id=1, source_target_pairs={{0,2},{1,5},{4,0},{5,9},{8,4},{9,13},{12,8},{13,15},{14,12},{15,11... | collective-permute-start | bytes 393224 | tf_op jit(solution)/shard_map/ppermute | solution.py:51
  53.2 11.5 %collective-permute-start.33 = (bf16[256,256]{1,0:T(8,128)(2,1)S(1)}, bf16[256,256]{1,0:T(8,128)(2,1)S(1)}, u32[]{:S(2)}, u32[]{:S(2)}) collective-permute-start(bf16[256,256]{1,0:T(8,128)(2,1)S(1)} %add_convert_fusion.3), channel_id=1, source_target_pairs={{0,4},{1,3},{4,8},{5,1},{8,12},{9,5},{12,14},{13,9},{14,10},{15,13... | collective-permute-start | bytes 393224 | tf_op jit(solution)/shard_map/ppermute | solution.py:51
  56.2 6.4 %collective-permute-start.19 = (bf16[256,256]{1,0:T(8,128)(2,1)S(1)}, bf16[256,256]{1,0:T(8,128)(2,1)S(1)}, u32[]{:S(2)}, u32[]{:S(2)}) collective-permute-start(bf16[256,256]{1,0:T(8,128)(2,1)S(1)} %add_convert_fusion.7), channel_id=1, source_target_pairs={{0,4},{1,3},{4,8},{5,1},{8,12},{9,5},{12,14},{13,9},{14,10},{15,13... | collective-permute-start | bytes 393224 | tf_op jit(solution)/shard_map/ppermute | solution.py:51
  60.5 6.3 %collective-permute-start.37 = (bf16[256,256]{1,0:T(8,128)(2,1)S(1)}, bf16[256,256]{1,0:T(8,128)(2,1)S(1)}, u32[]{:S(2)}, u32[]{:S(2)}) collective-permute-start(bf16[256,256]{1,0:T(8,128)(2,1)S(1)} %add_convert_fusion), channel_id=1, source_target_pairs={{0,2},{1,5},{4,0},{5,9},{8,4},{9,13},{12,8},{13,15},{14,12},{15,11... | collective-permute-start | bytes 393224 | tf_op jit(solution)/shard_map/ppermute | solution.py:51
  62.6 6.9 %collective-permute-start.24 = (bf16[256,256]{1,0:T(8,128)(2,1)S(1)}, bf16[256,256]{1,0:T(8,128)(2,1)S(1)}, u32[]{:S(2)}, u32[]{:S(2)}) collective-permute-start(bf16[256,256]{1,0:T(8,128)(2,1)S(1)} %fusion.1.refs_0_), channel_id=1, source_target_pairs={{0,2},{1,5},{4,0},{5,9},{8,4},{9,13},{12,8},{13,15},{14,12},{15,11... | collective-permute-start | bytes 393224 | tf_op jit(solution)/shard_map/ppermute | solution.py:51
  64.7 6.2 %collective-permute-start.23 = (bf16[256,256]{1,0:T(8,128)(2,1)S(1)}, bf16[256,256]{1,0:T(8,128)(2,1)S(1)}, u32[]{:S(2)}, u32[]{:S(2)}) collective-permute-start(bf16[256,256]{1,0:T(8,128)(2,1)S(1)} %fusion.1.refs_0_), channel_id=1, source_target_pairs={{0,4},{1,3},{4,8},{5,1},{8,12},{9,5},{12,14},{13,9},{14,10},{15,13... | collective-permute-start | bytes 393224 | tf_op jit(solution)/shard_map/ppermute | solution.py:51
  66.8 6.1 %collective-permute-start.39 = (bf16[256,256]{1,0:T(8,128)(2,1)S(1)}, bf16[256,256]{1,0:T(8,128)(2,1)S(1)}, u32[]{:S(2)}, u32[]{:S(2)}) collective-permute-start(bf16[256,256]{1,0:T(8,128)(2,1)S(1)} %multiply_convert_fusion.refs_1_), channel_id=1, source_target_pairs={{0,2},{1,5},{4,0},{5,9},{8,4},{9,13},{12,8},{13,15},{14,12},{15,11... | collective-permute-start | bytes 393224 | tf_op jit(solution)/shard_map/ppermute | solution.py:51
  66.9 6.3 %collective-permute-start.38 = (bf16[256,256]{1,0:T(8,128)(2,1)S(1)}, bf16[256,256]{1,0:T(8,128)(2,1)S(1)}, u32[]{:S(2)}, u32[]{:S(2)}) collective-permute-start(bf16[256,256]{1,0:T(8,128)(2,1)S(1)} %multiply_convert_fusion.refs_1_), channel_id=1, source_target_pairs={{0,4},{1,3},{4,8},{5,1},{8,12},{9,5},{12,14},{13,9},{14,10},{15,13... | collective-permute-start | bytes 393224 | tf_op jit(solution)/shard_map/ppermute | solution.py:51
  70.9 5.8 %collective-permute-start.25 = (bf16[256,256]{1,0:T(8,128)(2,1)S(1)}, bf16[256,256]{1,0:T(8,128)(2,1)S(1)}, u32[]{:S(2)}, u32[]{:S(2)}) collective-permute-start(bf16[256,256]{1,0:T(8,128)(2,1)S(1)} %collective-permute-done.23.refs_2_), channel_id=1, source_target_pairs={{0,4},{1,3},{4,8},{5,1},{8,12},{9,5},{12,14},{13,9},{14,10},{15,13... | collective-permute-start | bytes 393224 | tf_op jit(solution)/shard_map/ppermute | solution.py:51
  70.9 5.8 %collective-permute-start.26 = (bf16[256,256]{1,0:T(8,128)(2,1)S(1)}, bf16[256,256]{1,0:T(8,128)(2,1)S(1)}, u32[]{:S(2)}, u32[]{:S(2)}) collective-permute-start(bf16[256,256]{1,0:T(8,128)(2,1)S(1)} %collective-permute-done.24.refs_4_), channel_id=1, source_target_pairs={{0,2},{1,5},{4,0},{5,9},{8,4},{9,13},{12,8},{13,15},{14,12},{15,11... | collective-permute-start | bytes 393224 | tf_op jit(solution)/shard_map/ppermute | solution.py:51
  73.2 6.3 %collective-permute-start.40 = (bf16[256,256]{1,0:T(8,128)(2,1)S(1)}, bf16[256,256]{1,0:T(8,128)(2,1)S(1)}, u32[]{:S(2)}, u32[]{:S(2)}) collective-permute-start(bf16[256,256]{1,0:T(8,128)(2,1)S(1)} %collective-permute-done.38.refs_3_), channel_id=1, source_target_pairs={{0,4},{1,3},{4,8},{5,1},{8,12},{9,5},{12,14},{13,9},{14,10},{15,13... | collective-permute-start | bytes 393224 | tf_op jit(solution)/shard_map/ppermute | solution.py:51
  76.7 5.9 %collective-permute-start.27 = (bf16[256,256]{1,0:T(8,128)(2,1)S(1)}, bf16[256,256]{1,0:T(8,128)(2,1)S(1)}, u32[]{:S(2)}, u32[]{:S(2)}) collective-permute-start(bf16[256,256]{1,0:T(8,128)(2,1)S(1)} %collective-permute-done.25.refs_0_), channel_id=1, source_target_pairs={{0,4},{1,3},{4,8},{5,1},{8,12},{9,5},{12,14},{13,9},{14,10},{15,13... | collective-permute-start | bytes 393224 | tf_op jit(solution)/shard_map/ppermute | solution.py:51
  83.4 6.6 %collective-permute-start.29 = (bf16[256,256]{1,0:T(8,128)(2,1)S(1)}, bf16[256,256]{1,0:T(8,128)(2,1)S(1)}, u32[]{:S(2)}, u32[]{:S(2)}) collective-permute-start(bf16[256,256]{1,0:T(8,128)(2,1)S(1)} %collective-permute-done.27.refs_4_), channel_id=1, source_target_pairs={{0,4},{1,3},{4,8},{5,1},{8,12},{9,5},{12,14},{13,9},{14,10},{15,13... | collective-permute-start | bytes 393224 | tf_op jit(solution)/shard_map/ppermute | solution.py:51
  (19 other events, 111.0 us)

commit v6 on v5

v6 whole, which is shorter than its diff:
```python
import functools
import math

import jax
import jax.numpy as jnp
from jax import lax
from jax.experimental import pallas as pl
from jax.experimental.pallas import tpu as pltpu
from jax.sharding import PartitionSpec as P

F32 = jnp.float32
BF16 = jnp.bfloat16
OVER_ROWS = (((0,), (0,)), ((), ()))
OVER_COLS = (((1,), (1,)), ((), ()))
GRID_SIZES = (2, 4, 8, 16)
VMEM_BYTES = 24 * 1024 * 1024
PIECES = 8


def passed_along(shard, axis, by):
    size = lax.axis_size(axis)
    pairs = [(i, i + by) for i in range(size) if 0 <= i + by < size]
    return lax.ppermute(shard, axis, pairs)


def matmul(a, b, dims=(((1,), (0,)), ((), ()))):
    return lax.dot_general(a, b, dims, preferred_element_type=F32)


def hop(shard, mask):
    return lax.ppermute(shard, "latent", [(i, i ^ mask) for i in range(lax.axis_size("latent"))])


def after(value, *others):
    return lax.optimization_barrier((value,) + others)[0]


def call(kernel, outs, flops, operands, spaces=None, out_spaces=None, scratch=(), aliases=None):
    def spec(space):
        return pl.BlockSpec(memory_space=space)

    spaces = spaces or [pltpu.VMEM] * (len(operands) - 1)
    out_spaces = out_spaces or [pltpu.VMEM] * len(outs)
    size = sum(math.prod(x.shape) * x.dtype.itemsize for x in list(operands) + list(outs))
    return pl.pallas_call(
        kernel,
        out_shape=outs,
        in_specs=[spec(pltpu.SMEM)] + [spec(space) for space in spaces],
        out_specs=[spec(space) for space in out_spaces],
        scratch_shapes=list(scratch),
        input_output_aliases=aliases or {},
        compiler_params=pltpu.CompilerParams(vmem_limit_bytes=VMEM_BYTES),
        cost_estimate=pl.CostEstimate(flops=flops, bytes_accessed=size, transcendentals=0),
    )(*operands)


def block_of(starts, slot, wide):
    return pl.ds(pl.multiple_of(starts[slot], wide), wide)


def prepare_kernel(starts, own_dec, low_cross, high_cross, weight, stacked, weight_here):
    lat, half_width = high_cross.shape
    stacked[:lat, :] = own_dec[0]
    stacked[lat:, :half_width] = low_cross[...]
    stacked[lat:, half_width:] = high_cross[...]
    weight_here[...] = weight[0]


def encode_kernel(slots, last, starts, *refs):
    shards, (weight, before, *outs) = refs[:len(slots)], refs[len(slots):]
    total = jnp.broadcast_to(before[...], outs[0].shape)
    for slot, shard in zip(slots, shards):
        block = weight[block_of(starts, slot, shard.shape[1]), :]
        total = total + jnp.dot(shard[...], block, preferred_element_type=F32)
    outs[0][...] = total
    if last:
        outs[1][...] = jnp.maximum(total, 0.0).astype(BF16)


def turn_kernel(starts, *refs):
    *shards, turned = refs
    for slot, shard in enumerate(shards):
        turned[block_of(starts, slot, shard.shape[1]), :] = shard[...].T


def spread_kernel(slots, starts, codes, earlier, stacked, *partials):
    both = jnp.concatenate([codes[...], earlier[...]], axis=1)
    for slot, partial in zip(slots, partials):
        block = stacked[:, block_of(starts, slot, partial.shape[1])]
        partial[...] = jnp.dot(both, block, preferred_element_type=F32).astype(partial.dtype)
    if len(partials) > len(slots):
        partials[-1][...] = both.T


def back_products(slots, starts, shards, stacked, both_t, before):
    blocks, total = [], before
    for slot, shard in zip(slots, shards):
        error = shard[...]
        decoder = stacked[:, block_of(starts, slot, error.shape[1])]
        blocks.append(jnp.dot(both_t[...], error, preferred_element_type=F32))
        term = lax.dot_general(error, decoder, OVER_COLS, preferred_element_type=F32)
        total = term if total is None else total + term
    return blocks, total


def back_kernel(slots, first, starts, *refs):
    count = len(slots)
    shards, (stacked, both_t), (*before, outer, back) = refs[:count], refs[count:count + 2], refs[count + 2:]
    blocks, total = back_products(slots, starts, shards, stacked, both_t, None if first else before[0][...])
    for i, block in enumerate(blocks):
        outer[i] = block
    back[...] = total


def last_back_kernel(slots, far, starts, *refs):
    shard, stacked, both_t, *outers, before, same, back_own, sent, high = refs
    (block,), total = back_products((far,), starts, (shard,), stacked, both_t, before[...])
    rows, wide = shard.shape
    half_width, lat = high.shape
    back_own[...] = total[:, :lat]
    sent[:rows, :] = total[:, lat:]
    same[...] = block[:lat]
    pieces = [(far, block[lat:])]
    for group, outer in zip(slots, outers):
        pieces += [(slot, outer[i, lat:]) for i, slot in enumerate(group)]
    for slot, piece in pieces:
        start = pl.multiple_of(starts[slot], wide)

        @pl.when(start < half_width)
        def _():
            for c in range(0, wide, lat):
                sent[pl.ds(rows + start + c, lat), :] = piece[:, c:c + lat]

        @pl.when(start >= half_width)
        def _():
            for c in range(0, wide, lat):
                high[pl.ds(start - half_width + c, lat), :] = piece[:, c:c + lat]


def finish_kernel(slots, far, starts, *refs):
    turned, preact, back_own, arrived, high, last_same, *outers = refs[:6 + len(slots)]
    grad, bias, same, cross, stage, grad_sems, same_sems, cross_sems = refs[6 + len(slots):]
    pieces, height, lat = stage.shape
    rows = preact.shape[0]
    half_width = high.shape[0]
    wide = last_same.shape[1]
    copies = []
    blocks = [(far, last_same)]
    for group, outer in zip(slots, outers):
        blocks += [(slot, outer.at[i, :lat, :]) for i, slot in enumerate(group)]
    for i, (slot, block) in enumerate(blocks):
        copies.append(pltpu.make_async_copy(block, same.at[0, :, block_of(starts, slot, wide)], same_sems.at[i]))
        copies[-1].start()
    first = starts[starts.shape[0] - 1] == 0
    for c in range(half_width // lat):
        at = pl.ds(c * lat, lat)

        @pl.when(first)
        def _():
            source = arrived.at[pl.ds(rows + c * lat, lat), :]
            pltpu.make_async_copy(source, cross.at[:, at], cross_sems.at[c]).start()

        @pl.when(jnp.logical_not(first))
        def _():
            pltpu.make_async_copy(high.at[at, :], cross.at[:, at], cross_sems.at[c]).start()

        copies.append(pltpu.make_async_copy(high.at[at, :], cross.at[:, at], cross_sems.at[c]))
    value = jnp.where(preact[...] > 0, back_own[...] + arrived[:rows, :], 0.0).astype(BF16)
    for i in range(pieces):
        at = pl.ds(i * height, height)
        stage[i] = jnp.dot(turned[at, :], value, preferred_element_type=F32)
        copies.append(pltpu.make_async_copy(stage.at[i], grad.at[0, at, :], grad_sems.at[i]))
        copies[-1].start()
    bias[...] = jnp.sum(value.astype(F32), axis=0, keepdims=True)
    for copy in copies:
        copy.wait()


def grid_shards(residual_in, targets, enc_weight, enc_bias, dec_same, dec_cross):
    size = lax.axis_size("latent")
    tall = size // 2
    member = lax.axis_index("latent")
    layer = lax.axis_index("layer")
    rows, wide = residual_in.shape[1:]
    deep, lat = enc_weight.shape[1:]
    half_width = deep // 2
    err_scale = 1.0 / math.sqrt(rows)
    shape = jax.ShapeDtypeStruct
    unit = 2 * rows * wide * lat

    starts = jnp.stack([(member ^ (2 * (j % tall) + j // tall)) * wide for j in range(size)] + [layer])
    starts = starts.astype(jnp.int32)
    along = [1] + list(range(tall - 1, 1, -1)) if tall > 1 else []
    last = tall + (along[-1] if along else 0)

    def gather(own, ready=None):
        found = [own] + [None] * (size - 1)
        for k in along:
            found[k] = hop(own, 2 * k)
        found[tall] = hop(own, 1)
        for k in along:
            passing = found[k]
            if ready is not None and k == along[-1]:
                passing = after(passing, ready)
            found[tall + k] = hop(passing, 1)
        return found

    low_cross = passed_along(dec_cross, "layer", 1)
    stacked, weight = call(
        prepare_kernel,
        [shape((2 * lat, deep), BF16), shape((deep, lat), BF16)],
        0,
        [starts, dec_same, low_cross, dec_cross, enc_weight],
    )
    inputs = gather(residual_in[0], stacked)
    early = tuple(slot for slot in range(size) if slot != last)
    part = call(
        functools.partial(encode_kernel, early, False),
        [shape((rows, lat), F32)],
        unit * len(early),
        [starts] + [inputs[slot] for slot in early] + [weight, enc_bias],
    )[0]
    preact, codes = call(
        functools.partial(encode_kernel, (last,), True),
        [shape((rows, lat), F32), shape((rows, lat), BF16)],
        unit,
        [starts, inputs[last], weight, part],
    )
    earlier = passed_along(codes, "layer", 1)

    across = tuple(tall + k for k in reversed([0] + along)) if along else (tall,)
    messages = call(
        functools.partial(spread_kernel, across),
        [shape((rows, wide), BF16)] * len(across),
        2 * unit * len(across),
        [starts, codes, earlier, stacked],
    )
    arrived = {slot - tall: hop(message, 1) for slot, message in zip(across, messages)}
    column = tuple(range(tall))
    *partials, both_t = call(
        functools.partial(spread_kernel, column),
        [shape((rows, wide), F32)] * tall + [shape((2 * lat, rows), BF16)],
        2 * unit * tall,
        [starts, codes, earlier, stacked],
    )
    summed = {}
    for k in reversed(along):
        summed[k] = hop((partials[k] + arrived[k].astype(F32)).astype(BF16), 2 * k)
    total = partials[0] + arrived[0].astype(F32)
    for k in along:
        total = total + summed[k].astype(F32)
    own_errors = ((total - targets[0].astype(F32)) * err_scale).astype(BF16)

    errors = gather(own_errors)
    turned = call(turn_kernel, [shape((deep, rows), BF16)], unit, [starts] + inputs)[0]

    def back(slots, before):
        return call(
            functools.partial(back_kernel, slots, before is None),
            [shape((len(slots), 2 * lat, wide), F32), shape((rows, 2 * lat), F32)],
            4 * unit * len(slots),
            [starts] + [errors[slot] for slot in slots] + [stacked, both_t] + ([] if before is None else [before]),
        )

    first_group = (0,) + tuple(along[:1])
    if last != tall:
        first_group += (tall,)
    groups = [first_group, tuple(slot for slot in range(size) if slot not in first_group and slot != last)]
    groups = [group for group in groups if group]
    outers, acc = [], None
    for group in groups:
        outer, acc = back(group, acc)
        outers.append(outer)
    last_same, back_own, sent, high = call(
        functools.partial(last_back_kernel, groups, last),
        [
            shape((lat, wide), F32),
            shape((rows, lat), F32),
            shape((rows + half_width, lat), F32),
            shape((half_width, lat), F32),
        ],
        4 * unit,
        [starts, errors[last], stacked, both_t] + outers + [acc],
    )
    returned = passed_along(sent, "layer", -1)
    height = deep // PIECES
    grad_enc, grad_bias, grad_same, grad_cross = call(
        functools.partial(finish_kernel, groups, last),
        [
            shape((1, deep, lat), F32),
            shape((1, lat), F32),
            shape((1, lat, deep), F32),
            shape((lat, half_width), F32),
        ],
        unit * size,
        [starts, turned, preact, back_own, returned, high, last_same] + outers,
        out_spaces=[pl.ANY, pltpu.VMEM, pl.ANY, pl.ANY],
        scratch=[
            pltpu.VMEM((PIECES, height, lat), F32),
            pltpu.SemaphoreType.DMA((PIECES,)),
            pltpu.SemaphoreType.DMA((size,)),
            pltpu.SemaphoreType.DMA((half_width // lat,)),
        ],
    )
    return (grad_enc, grad_bias, grad_same, grad_cross)


def wide_shards(residual_in, targets, enc_weight, enc_bias, dec_same, dec_cross):
    is_first = lax.axis_index("layer") == 0
    err_scale = 1.0 / math.sqrt(residual_in.shape[1])
    inputs = lax.all_gather(residual_in[0], "latent", axis=1, tiled=True)
    preact = matmul(inputs, enc_weight[0]) + enc_bias[0]
    codes_now = jnp.maximum(preact, 0.0).astype(BF16)
    earlier = passed_along(codes_now, "layer", 1)
    cross_full = lax.all_gather(dec_cross, "layer", axis=1, tiled=True)
    own_dec = dec_same[0]
    half_width = own_dec.shape[1] // 2
    recon_full = lax.psum(matmul(codes_now, own_dec) + matmul(earlier, cross_full), "latent")
    wanted = lax.all_gather(targets[0], "latent", axis=1, tiled=True)
    errors = ((recon_full - wanted.astype(F32)) * err_scale).astype(BF16)
    grad_same = matmul(codes_now, errors, OVER_ROWS)
    grad_full = matmul(earlier, errors, OVER_ROWS)
    returned = passed_along(grad_full[:, :half_width], "layer", -1)
    grad_cross = jnp.where(is_first, returned, grad_full[:, half_width:])
    from_next = passed_along(matmul(errors, cross_full, OVER_COLS), "layer", -1)
    grad_codes = matmul(errors, own_dec, OVER_COLS) + from_next
    grad_pre = jnp.where(preact > 0, grad_codes, 0.0).astype(BF16)
    grad_enc = matmul(inputs, grad_pre, OVER_ROWS)
    grad_bias = jnp.sum(grad_pre.astype(F32), axis=0)
    return (grad_enc[None], grad_bias[None], grad_same[None], grad_cross)


def solution(mesh):
    size = mesh.shape["latent"]
    placed = (
        P("layer", "groups", "latent"),
        P("layer", "groups", "latent"),
        P("layer", None, "latent"),
        P("layer", "latent"),
        P("layer", "latent", None),
        P("latent", "layer"),
    )
    return jax.shard_map(
        grid_shards if size in GRID_SIZES else wide_shards,
        mesh=mesh,
        in_specs=placed,
        out_specs=(
            P(("groups", "layer"), None, "latent"),
            P(("groups", "layer"), "latent"),
            P(("groups", "layer"), "latent", None),
            P(("groups", "latent"), "layer"),
        ),
        check_vma=False,
    )
```

time: 101 us -> 123 us (1.22)
  waiting for transfers between devices: 29.6 us -> 69.8 us
  starting transfers between devices: 52.2 us -> 34.9 us
  Pallas kernels: 13.6 us -> 12.2 us
    ppermute x42 -> x21, waiting for transfers between devices: 27.9 us -> 67.1 us  [hop(): lax.ppermute(shard, 'latent', [(i, i ^ mask) for i in range(lax.axis_size...]
    ppermute x42 -> x21, starting transfers between devices: 46.5 us -> 30.8 us  [hop(): lax.ppermute(shard, 'latent', [(i, i ^ mask) for i in range(lax.axis_size...]
    unnamed x10 -> x14, local copies, waits for them, and re-layouts: 3.04 us -> 4.64 us
    ppermute x4 -> x3, starting transfers between devices: 5.62 us -> 4.05 us  [passed_along(): return lax.ppermute(shard, axis, pairs)]
    pallas_call x12 -> x10, Pallas kernels: 13.6 us -> 12.2 us  [call(): pl.pallas_call(kernel, out_shape=outs, in_specs=[spec(pltpu.SMEM)] + [spe...]
    ppermute x4 -> x3, waiting for transfers between devices: 1.74 us -> 2.7 us  [passed_along(): return lax.ppermute(shard, axis, pairs)]
  transfers between devices with their start and end apart: 46 -> 24, of which waited for: 27 -> 16; matrix products, arithmetic and copies ran while one was open for 1% -> 0% of each run, Pallas kernels for 9% -> 5%
where the time goes in v6:
time: 123 us
  waiting for transfers between devices  69.8 us (57%)
  starting transfers between devices  34.9 us (28%)
  Pallas kernels  12.2 us (10%)
  local copies, waits for them, and re-layouts  4.72 us (4%)
    ppermute x21, waiting for transfers between devices, hop(): lax.ppermute(shard, 'latent', [(i, i ^ mask) for i in range(lax.axis_size...  67.1 us
    ppermute x21, starting transfers between devices, hop(): lax.ppermute(shard, 'latent', [(i, i ^ mask) for i in range(lax.axis_size...  30.8 us
    pallas_call x10, Pallas kernels, call(): pl.pallas_call(kernel, out_shape=outs, in_specs=[spec(pltpu.SMEM)] + [spe...  12.2 us
    unnamed x14, local copies, waits for them, and re-layouts  4.64 us
    ppermute x3, starting transfers between devices, passed_along(): return lax.ppermute(shard, axis, pairs)  4.05 us
    ppermute x3, waiting for transfers between devices, passed_along(): return lax.ppermute(shard, axis, pairs)  2.7 us
  transfers between devices with their start and end apart: 24, of which 16 were waited for; matrix products, arithmetic and copies ran while one was open for 0% of the time, Pallas kernels for 5%

profile of v6, /device:TPU:0, one launch (start us, length us, event | category | flops | bytes accessed | tf_op | source)
XLA Modules:
  0.0 122.8 jit_solution(9102632576216690212)
XLA Ops:
  0.6 5.1 %collective-permute-start.2 = (bf16[512,256]{1,0:T(8,128)(2,1)}, bf16[512,256]{1,0:T(8,128)(2,1)S(1)}, u32[]{:S(2)}, u32[]{:S(2)}) collective-permute-start(bf16[512,256]{1,0:T(8,128)(2,1)} %bitcast.13), channel_id=1, source_target_pairs={{0,12},{2,14},{4,8},{6,10},{8,4},{10,6},{12,0},{14,2},{1,13},{3,15... | collective-permute-start | bytes 786440 | tf_op jit(solution)/shard_map/ppermute | solution.py:31
  5.7 1.5 %collective-permute-start.5 = (bf16[128,1024]{1,0:T(8,128)(2,1)}, bf16[128,1024]{1,0:T(8,128)(2,1)S(1)}, u32[]{:S(2)}, u32[]{:S(2)}) collective-permute-start(bf16[128,1024]{1,0:T(8,128)(2,1)} %high_cross.1), channel_id=1, source_target_pairs={{0,1},{2,3},{4,5},{6,7},{8,9},{10,11},{12,13},{14,15},{16,17},{18,... | collective-permute-start | bytes 786440 | tf_op jit(solution)/shard_map/ppermute | solution.py:23
  7.9 1.5 %collective-permute-start.3 = (bf16[512,256]{1,0:T(8,128)(2,1)}, bf16[512,256]{1,0:T(8,128)(2,1)S(1)}, u32[]{:S(2)}, u32[]{:S(2)}) collective-permute-start(bf16[512,256]{1,0:T(8,128)(2,1)} %bitcast.16), channel_id=1, source_target_pairs={{0,2},{2,0},{4,6},{6,4},{8,10},{10,8},{12,14},{14,12},{1,3},{3,1},... | collective-permute-start | bytes 786440 | tf_op jit(solution)/shard_map/ppermute | solution.py:31
  9.4 3.8 %collective-permute-done.2.refs_3_ = bf16[512,256]{1,0:T(8,128)(2,1)S(1)} collective-permute-done((bf16[512,256]{1,0:T(8,128)(2,1)}, bf16[512,256]{1,0:T(8,128)(2,1)S(1)}, u32[]{:S(2)}, u32[]{:S(2)}) %collective-permute-start.2) | collective-permute-done | bytes 262176 | tf_op jit(solution)/shard_map/ppermute | solution.py:31
  13.2 1.7 %collective-permute-start.7 = (bf16[512,256]{1,0:T(8,128)(2,1)S(1)}, bf16[512,256]{1,0:T(8,128)(2,1)S(1)}, u32[]{:S(2)}, u32[]{:S(2)}) collective-permute-start(bf16[512,256]{1,0:T(8,128)(2,1)S(1)} %collective-permute-done.2.refs_3_), channel_id=1, source_target_pairs={{0,2},{2,0},{4,6},{6,4},{8,10},{10,8},{12,14},{14,12},{1,3},{3,1},... | collective-permute-start | bytes 786440 | tf_op jit(solution)/shard_map/ppermute | solution.py:31
  14.9 4.2 %collective-permute-done.refs_1_ = bf16[512,256]{1,0:T(8,128)(2,1)S(1)} collective-permute-done((bf16[512,256]{1,0:T(8,128)(2,1)}, bf16[512,256]{1,0:T(8,128)(2,1)S(1)}, u32[]{:S(2)}, u32[]{:S(2)}) %collective-permute-start) | collective-permute-done | bytes 262176 | tf_op jit(solution)/shard_map/ppermute | solution.py:31
  19.0 1.4 %collective-permute-start.4 = (bf16[512,256]{1,0:T(8,128)(2,1)S(1)}, bf16[512,256]{1,0:T(8,128)(2,1)S(1)}, u32[]{:S(2)}, u32[]{:S(2)}) collective-permute-start(bf16[512,256]{1,0:T(8,128)(2,1)S(1)} %collective-permute-done.refs_1_), channel_id=1, source_target_pairs={{0,2},{2,0},{4,6},{6,4},{8,10},{10,8},{12,14},{14,12},{1,3},{3,1},... | collective-permute-start | bytes 786440 | tf_op jit(solution)/shard_map/ppermute | solution.py:31
  24.2 4.1 %collective-permute-done.1.refs_2_ = bf16[512,256]{1,0:T(8,128)(2,1)S(1)} collective-permute-done((bf16[512,256]{1,0:T(8,128)(2,1)}, bf16[512,256]{1,0:T(8,128)(2,1)S(1)}, u32[]{:S(2)}, u32[]{:S(2)}) %collective-permute-start.1) | collective-permute-done | bytes 262176 | tf_op jit(solution)/shard_map/ppermute | solution.py:31
  28.3 1.5 %collective-permute-start.6 = (bf16[512,256]{1,0:T(8,128)(2,1)S(1)}, bf16[512,256]{1,0:T(8,128)(2,1)S(1)}, u32[]{:S(2)}, u32[]{:S(2)}) collective-permute-start(bf16[512,256]{1,0:T(8,128)(2,1)S(1)} %collective-permute-done.1.refs_2_), channel_id=1, source_target_pairs={{0,2},{2,0},{4,6},{6,4},{8,10},{10,8},{12,14},{14,12},{1,3},{3,1},... | collective-permute-start | bytes 786440 | tf_op jit(solution)/shard_map/ppermute | solution.py:31
  32.6 3.1 %collective-permute-done.6.refs_6_.refs_0_ = bf16[512,256]{1,0:T(8,128)(2,1)S(1)} collective-permute-done((bf16[512,256]{1,0:T(8,128)(2,1)S(1)}, bf16[512,256]{1,0:T(8,128)(2,1)S(1)}, u32[]{:S(2)}, u32[]{:S(2)}) %collective-permute-start.6) | collective-permute-done | bytes 262176 | tf_op jit(solution)/shard_map/ppermute | solution.py:31
  36.4 1.3 %collective-permute-start.8 = (bf16[512,128]{1,0:T(8,128)(2,1)S(1)}, bf16[512,128]{1,0:T(8,128)(2,1)S(1)}, u32[]{:S(2)}, u32[]{:S(2)}) collective-permute-start(bf16[512,128]{1,0:T(8,128)(2,1)S(1)} %get-tuple-element.30.codes), channel_id=1, source_target_pairs={{0,1},{2,3},{4,5},{6,7},{8,9},{10,11},{12,13},{14,15},{16,17},{18,... | collective-permute-start | bytes 393224 | tf_op jit(solution)/shard_map/ppermute | solution.py:23
  39.7 1.6 %collective-permute-start.10 = (bf16[512,256]{1,0:T(8,128)(2,1)S(1)}, bf16[512,256]{1,0:T(8,128)(2,1)S(1)}, u32[]{:S(2)}, u32[]{:S(2)}) collective-permute-start(bf16[512,256]{1,0:T(8,128)(2,1)S(1)} %get-tuple-element.34), channel_id=1, source_target_pairs={{0,2},{2,0},{4,6},{6,4},{8,10},{10,8},{12,14},{14,12},{1,3},{3,1},... | collective-permute-start | bytes 786440 | tf_op jit(solution)/shard_map/ppermute | solution.py:31
  41.8 1.5 %collective-permute-start.12 = (bf16[512,256]{1,0:T(8,128)(2,1)S(1)}, bf16[512,256]{1,0:T(8,128)(2,1)S(1)}, u32[]{:S(2)}, u32[]{:S(2)}) collective-permute-start(bf16[512,256]{1,0:T(8,128)(2,1)S(1)} %get-tuple-element.36), channel_id=1, source_target_pairs={{0,2},{2,0},{4,6},{6,4},{8,10},{10,8},{12,14},{14,12},{1,3},{3,1},... | collective-permute-start | bytes 786440 | tf_op jit(solution)/shard_map/ppermute | solution.py:31
  44.8 4.1 %collective-permute-done.10 = bf16[512,256]{1,0:T(8,128)(2,1)S(1)} collective-permute-done((bf16[512,256]{1,0:T(8,128)(2,1)S(1)}, bf16[512,256]{1,0:T(8,128)(2,1)S(1)}, u32[]{:S(2)}, u32[]{:S(2)}) %collective-permute-start.10) | collective-permute-done | bytes 262176 | tf_op jit(solution)/shard_map/ppermute | solution.py:31
  49.5 10.6 %collective-permute-done.12 = bf16[512,256]{1,0:T(8,128)(2,1)S(1)} collective-permute-done((bf16[512,256]{1,0:T(8,128)(2,1)S(1)}, bf16[512,256]{1,0:T(8,128)(2,1)S(1)}, u32[]{:S(2)}, u32[]{:S(2)}) %collective-permute-start.12) | collective-permute-done | bytes 262176 | tf_op jit(solution)/shard_map/ppermute | solution.py:31
  60.2 2.4 %collective-permute-start.13 = (bf16[512,256]{1,0:T(8,128)(2,1)S(1)}, bf16[512,256]{1,0:T(8,128)(2,1)S(1)}, u32[]{:S(2)}, u32[]{:S(2)}) collective-permute-start(bf16[512,256]{1,0:T(8,128)(2,1)S(1)} %add_convert_fusion.1), channel_id=1, source_target_pairs={{0,12},{2,14},{4,8},{6,10},{8,4},{10,6},{12,0},{14,2},{1,13},{3,15... | collective-permute-start | bytes 786440 | tf_op jit(solution)/shard_map/ppermute | solution.py:31
  62.5 2.6 %collective-permute-done.14 = bf16[512,256]{1,0:T(8,128)(2,1)S(1)} collective-permute-done((bf16[512,256]{1,0:T(8,128)(2,1)S(1)}, bf16[512,256]{1,0:T(8,128)(2,1)S(1)}, u32[]{:S(2)}, u32[]{:S(2)}) %collective-permute-start.14) | collective-permute-done | bytes 262176 | tf_op jit(solution)/shard_map/ppermute | solution.py:31
  65.2 1.5 %collective-permute-start.15 = (bf16[512,256]{1,0:T(8,128)(2,1)S(1)}, bf16[512,256]{1,0:T(8,128)(2,1)S(1)}, u32[]{:S(2)}, u32[]{:S(2)}) collective-permute-start(bf16[512,256]{1,0:T(8,128)(2,1)S(1)} %add_convert_fusion), channel_id=1, source_target_pairs={{0,8},{2,10},{4,12},{6,14},{8,0},{10,2},{12,4},{14,6},{1,9},{3,11}... | collective-permute-start | bytes 786440 | tf_op jit(solution)/shard_map/ppermute | solution.py:31
  66.7 3.5 %collective-permute-done.13 = bf16[512,256]{1,0:T(8,128)(2,1)S(1)} collective-permute-done((bf16[512,256]{1,0:T(8,128)(2,1)S(1)}, bf16[512,256]{1,0:T(8,128)(2,1)S(1)}, u32[]{:S(2)}, u32[]{:S(2)}) %collective-permute-start.13) | collective-permute-done | bytes 262176 | tf_op jit(solution)/shard_map/ppermute | solution.py:31
  70.2 14.1 %collective-permute-done.15 = bf16[512,256]{1,0:T(8,128)(2,1)S(1)} collective-permute-done((bf16[512,256]{1,0:T(8,128)(2,1)S(1)}, bf16[512,256]{1,0:T(8,128)(2,1)S(1)}, u32[]{:S(2)}, u32[]{:S(2)}) %collective-permute-start.15) | collective-permute-done | bytes 262176 | tf_op jit(solution)/shard_map/ppermute | solution.py:31
  84.5 3.1 %collective-permute-start.20 = (bf16[512,256]{1,0:T(8,128)(2,1)S(1)}, bf16[512,256]{1,0:T(8,128)(2,1)S(1)}, u32[]{:S(2)}, u32[]{:S(2)}) collective-permute-start(bf16[512,256]{1,0:T(8,128)(2,1)S(1)} %fusion.1.refs_0_), channel_id=1, source_target_pairs={{0,12},{2,14},{4,8},{6,10},{8,4},{10,6},{12,0},{14,2},{1,13},{3,15... | collective-permute-start | bytes 786440 | tf_op jit(solution)/shard_map/ppermute | solution.py:31
  87.6 1.3 %collective-permute-start.16 = (bf16[512,256]{1,0:T(8,128)(2,1)S(1)}, bf16[512,256]{1,0:T(8,128)(2,1)S(1)}, u32[]{:S(2)}, u32[]{:S(2)}) collective-permute-start(bf16[512,256]{1,0:T(8,128)(2,1)S(1)} %fusion.1.refs_0_), channel_id=1, source_target_pairs={{0,8},{2,10},{4,12},{6,14},{8,0},{10,2},{12,4},{14,6},{1,9},{3,11}... | collective-permute-start | bytes 786440 | tf_op jit(solution)/shard_map/ppermute | solution.py:31
  88.9 1.5 %collective-permute-start.19 = (bf16[512,256]{1,0:T(8,128)(2,1)S(1)}, bf16[512,256]{1,0:T(8,128)(2,1)S(1)}, u32[]{:S(2)}, u32[]{:S(2)}) collective-permute-start(bf16[512,256]{1,0:T(8,128)(2,1)S(1)} %fusion.1.refs_0_), channel_id=1, source_target_pairs={{0,2},{2,0},{4,6},{6,4},{8,10},{10,8},{12,14},{14,12},{1,3},{3,1},... | collective-permute-start | bytes 786440 | tf_op jit(solution)/shard_map/ppermute | solution.py:31
  90.4 5.2 %collective-permute-done.20.refs_1_ = bf16[512,256]{1,0:T(8,128)(2,1)S(1)} collective-permute-done((bf16[512,256]{1,0:T(8,128)(2,1)S(1)}, bf16[512,256]{1,0:T(8,128)(2,1)S(1)}, u32[]{:S(2)}, u32[]{:S(2)}) %collective-permute-start.20) | collective-permute-done | bytes 262176 | tf_op jit(solution)/shard_map/ppermute | solution.py:31
  95.6 1.5 %collective-permute-start.22 = (bf16[512,256]{1,0:T(8,128)(2,1)S(1)}, bf16[512,256]{1,0:T(8,128)(2,1)S(1)}, u32[]{:S(2)}, u32[]{:S(2)}) collective-permute-start(bf16[512,256]{1,0:T(8,128)(2,1)S(1)} %collective-permute-done.20.refs_1_), channel_id=1, source_target_pairs={{0,2},{2,0},{4,6},{6,4},{8,10},{10,8},{12,14},{14,12},{1,3},{3,1},... | collective-permute-start | bytes 786440 | tf_op jit(solution)/shard_map/ppermute | solution.py:31
  97.1 4.1 %collective-permute-done.18.refs_1_ = bf16[512,256]{1,0:T(8,128)(2,1)S(1)} collective-permute-done((bf16[512,256]{1,0:T(8,128)(2,1)S(1)}, bf16[512,256]{1,0:T(8,128)(2,1)S(1)}, u32[]{:S(2)}, u32[]{:S(2)}) %collective-permute-start.18) | collective-permute-done | bytes 262176 | tf_op jit(solution)/shard_map/ppermute | solution.py:31
  101.1 1.5 %collective-permute-start.21 = (bf16[512,256]{1,0:T(8,128)(2,1)S(1)}, bf16[512,256]{1,0:T(8,128)(2,1)S(1)}, u32[]{:S(2)}, u32[]{:S(2)}) collective-permute-start(bf16[512,256]{1,0:T(8,128)(2,1)S(1)} %collective-permute-done.18.refs_1_), channel_id=1, source_target_pairs={{0,2},{2,0},{4,6},{6,4},{8,10},{10,8},{12,14},{14,12},{1,3},{3,1},... | collective-permute-start | bytes 786440 | tf_op jit(solution)/shard_map/ppermute | solution.py:31
  102.6 4.1 %collective-permute-done.16.refs_0_ = bf16[512,256]{1,0:T(8,128)(2,1)S(1)} collective-permute-done((bf16[512,256]{1,0:T(8,128)(2,1)S(1)}, bf16[512,256]{1,0:T(8,128)(2,1)S(1)}, u32[]{:S(2)}, u32[]{:S(2)}) %collective-permute-start.16) | collective-permute-done | bytes 262176 | tf_op jit(solution)/shard_map/ppermute | solution.py:31
  106.7 1.5 %collective-permute-start.17 = (bf16[512,256]{1,0:T(8,128)(2,1)S(1)}, bf16[512,256]{1,0:T(8,128)(2,1)S(1)}, u32[]{:S(2)}, u32[]{:S(2)}) collective-permute-start(bf16[512,256]{1,0:T(8,128)(2,1)S(1)} %collective-permute-done.16.refs_0_), channel_id=1, source_target_pairs={{0,2},{2,0},{4,6},{6,4},{8,10},{10,8},{12,14},{14,12},{1,3},{3,1},... | collective-permute-start | bytes 786440 | tf_op jit(solution)/shard_map/ppermute | solution.py:31
  111.7 2.8 %collective-permute-done.17.refs_0_ = bf16[512,256]{1,0:T(8,128)(2,1)S(1)} collective-permute-done((bf16[512,256]{1,0:T(8,128)(2,1)S(1)}, bf16[512,256]{1,0:T(8,128)(2,1)S(1)}, u32[]{:S(2)}, u32[]{:S(2)}) %collective-permute-start.17) | collective-permute-done | bytes 262176 | tf_op jit(solution)/shard_map/ppermute | solution.py:31
  117.9 1.7 %collective-permute-done.23.refs_3_ = f32[1536,128]{1,0:T(8,128)S(1)} collective-permute-done((f32[1536,128]{1,0:T(8,128)S(1)}, f32[1536,128]{1,0:T(8,128)S(1)}, u32[]{:S(2)}, u32[]{:S(2)}) %collective-permute-start.23) | collective-permute-done | bytes 786464 | tf_op jit(solution)/shard_map/ppermute | solution.py:23
  119.7 3.1 %shard_map.102 = (f32[1,2048,128]{2,1,0:T(8,128)}, f32[1,128]{1,0:T(1,128)}, f32[1,128,2048]{2,1,0:T(8,128)}, f32[128,1024]{1,0:T(8,128)}) custom-call(s32[9]{0:T(128)S(1)} %stack.39.starts, bf16[2048,512]{1,0:T(8,128)(2,1)S(1)} %shard_map.94.refs_0_, f32[512,128]{1,0:T(8,128)S(1)} %get-tuple-element.29.refs_1_, f32[512,128]{1,0:T(8,128)S(1)} %get-tuple-element.44.refs_2_, ...), custom_call_target="tpu_custom_call" | custom-call | flops 268435456 | bytes 8520228 | tf_op jit(solution)/shard_map/pallas_call | solution.py:45
  (45 shorter events, 19.9 us)
Async XLA Ops:
  0.6 12.6 %collective-permute-start.2 = (bf16[512,256]{1,0:T(8,128)(2,1)}, bf16[512,256]{1,0:T(8,128)(2,1)S(1)}, u32[]{:S(2)}, u32[]{:S(2)}) collective-permute-start(bf16[512,256]{1,0:T(8,128)(2,1)} %bitcast.13), channel_id=1, source_target_pairs={{0,12},{2,14},{4,8},{6,10},{8,4},{10,6},{12,0},{14,2},{1,13},{3,15... | collective-permute-start | bytes 786440 | tf_op jit(solution)/shard_map/ppermute | solution.py:31
  5.7 13.3 %collective-permute-start = (bf16[512,256]{1,0:T(8,128)(2,1)}, bf16[512,256]{1,0:T(8,128)(2,1)S(1)}, u32[]{:S(2)}, u32[]{:S(2)}) collective-permute-start(bf16[512,256]{1,0:T(8,128)(2,1)} %bitcast.14), channel_id=1, source_target_pairs={{0,4},{2,6},{4,0},{6,2},{8,12},{10,14},{12,8},{14,10},{1,5},{3,7},... | collective-permute-start | bytes 786440 | tf_op jit(solution)/shard_map/ppermute | solution.py:31
  5.7 14.7 %collective-permute-start.5 = (bf16[128,1024]{1,0:T(8,128)(2,1)}, bf16[128,1024]{1,0:T(8,128)(2,1)S(1)}, u32[]{:S(2)}, u32[]{:S(2)}) collective-permute-start(bf16[128,1024]{1,0:T(8,128)(2,1)} %high_cross.1), channel_id=1, source_target_pairs={{0,1},{2,3},{4,5},{6,7},{8,9},{10,11},{12,13},{14,15},{16,17},{18,... | collective-permute-start | bytes 786440 | tf_op jit(solution)/shard_map/ppermute | solution.py:23
  7.2 21.0 %collective-permute-start.1 = (bf16[512,256]{1,0:T(8,128)(2,1)}, bf16[512,256]{1,0:T(8,128)(2,1)S(1)}, u32[]{:S(2)}, u32[]{:S(2)}) collective-permute-start(bf16[512,256]{1,0:T(8,128)(2,1)} %bitcast.15), channel_id=1, source_target_pairs={{0,8},{2,10},{4,12},{6,14},{8,0},{10,2},{12,4},{14,6},{1,9},{3,11}... | collective-permute-start | bytes 786440 | tf_op jit(solution)/shard_map/ppermute | solution.py:31
  7.9 21.8 %collective-permute-start.3 = (bf16[512,256]{1,0:T(8,128)(2,1)}, bf16[512,256]{1,0:T(8,128)(2,1)S(1)}, u32[]{:S(2)}, u32[]{:S(2)}) collective-permute-start(bf16[512,256]{1,0:T(8,128)(2,1)} %bitcast.16), channel_id=1, source_target_pairs={{0,2},{2,0},{4,6},{6,4},{8,10},{10,8},{12,14},{14,12},{1,3},{3,1},... | collective-permute-start | bytes 786440 | tf_op jit(solution)/shard_map/ppermute | solution.py:31
  13.2 16.6 %collective-permute-start.7 = (bf16[512,256]{1,0:T(8,128)(2,1)S(1)}, bf16[512,256]{1,0:T(8,128)(2,1)S(1)}, u32[]{:S(2)}, u32[]{:S(2)}) collective-permute-start(bf16[512,256]{1,0:T(8,128)(2,1)S(1)} %collective-permute-done.2.refs_3_), channel_id=1, source_target_pairs={{0,2},{2,0},{4,6},{6,4},{8,10},{10,8},{12,14},{14,12},{1,3},{3,1},... | collective-permute-start | bytes 786440 | tf_op jit(solution)/shard_map/ppermute | solution.py:31
  19.0 10.7 %collective-permute-start.4 = (bf16[512,256]{1,0:T(8,128)(2,1)S(1)}, bf16[512,256]{1,0:T(8,128)(2,1)S(1)}, u32[]{:S(2)}, u32[]{:S(2)}) collective-permute-start(bf16[512,256]{1,0:T(8,128)(2,1)S(1)} %collective-permute-done.refs_1_), channel_id=1, source_target_pairs={{0,2},{2,0},{4,6},{6,4},{8,10},{10,8},{12,14},{14,12},{1,3},{3,1},... | collective-permute-start | bytes 786440 | tf_op jit(solution)/shard_map/ppermute | solution.py:31
  20.5 1.0 copy-start.2
  21.5 1.0 copy-start.3
  22.6 0.9 copy-start.4
  28.3 7.4 %collective-permute-start.6 = (bf16[512,256]{1,0:T(8,128)(2,1)S(1)}, bf16[512,256]{1,0:T(8,128)(2,1)S(1)}, u32[]{:S(2)}, u32[]{:S(2)}) collective-permute-start(bf16[512,256]{1,0:T(8,128)(2,1)S(1)} %collective-permute-done.1.refs_2_), channel_id=1, source_target_pairs={{0,2},{2,0},{4,6},{6,4},{8,10},{10,8},{12,14},{14,12},{1,3},{3,1},... | collective-permute-start | bytes 786440 | tf_op jit(solution)/shard_map/ppermute | solution.py:31
  29.8 1.0 copy-start
  30.7 0.7 copy-start.5
  36.4 2.3 %collective-permute-start.8 = (bf16[512,128]{1,0:T(8,128)(2,1)S(1)}, bf16[512,128]{1,0:T(8,128)(2,1)S(1)}, u32[]{:S(2)}, u32[]{:S(2)}) collective-permute-start(bf16[512,128]{1,0:T(8,128)(2,1)S(1)} %get-tuple-element.30.codes), channel_id=1, source_target_pairs={{0,1},{2,3},{4,5},{6,7},{8,9},{10,11},{12,13},{14,15},{16,17},{18,... | collective-permute-start | bytes 393224 | tf_op jit(solution)/shard_map/ppermute | solution.py:23
  39.7 9.2 %collective-permute-start.10 = (bf16[512,256]{1,0:T(8,128)(2,1)S(1)}, bf16[512,256]{1,0:T(8,128)(2,1)S(1)}, u32[]{:S(2)}, u32[]{:S(2)}) collective-permute-start(bf16[512,256]{1,0:T(8,128)(2,1)S(1)} %get-tuple-element.34), channel_id=1, source_target_pairs={{0,2},{2,0},{4,6},{6,4},{8,10},{10,8},{12,14},{14,12},{1,3},{3,1},... | collective-permute-start | bytes 786440 | tf_op jit(solution)/shard_map/ppermute | solution.py:31
  41.2 25.5 %collective-permute-start.9 = (bf16[512,256]{1,0:T(8,128)(2,1)S(1)}, bf16[512,256]{1,0:T(8,128)(2,1)S(1)}, u32[]{:S(2)}, u32[]{:S(2)}) collective-permute-start(bf16[512,256]{1,0:T(8,128)(2,1)S(1)} %get-tuple-element.32), channel_id=1, source_target_pairs={{0,2},{2,0},{4,6},{6,4},{8,10},{10,8},{12,14},{14,12},{1,3},{3,1},... | collective-permute-start | bytes 786440 | tf_op jit(solution)/shard_map/ppermute | solution.py:31
  41.8 18.3 %collective-permute-start.12 = (bf16[512,256]{1,0:T(8,128)(2,1)S(1)}, bf16[512,256]{1,0:T(8,128)(2,1)S(1)}, u32[]{:S(2)}, u32[]{:S(2)}) collective-permute-start(bf16[512,256]{1,0:T(8,128)(2,1)S(1)} %get-tuple-element.36), channel_id=1, source_target_pairs={{0,2},{2,0},{4,6},{6,4},{8,10},{10,8},{12,14},{14,12},{1,3},{3,1},... | collective-permute-start | bytes 786440 | tf_op jit(solution)/shard_map/ppermute | solution.py:31
  43.2 41.0 %copy-start.6 = (bf16[1,512,256]{2,1,0:T(8,128)(2,1)S(1)}, bf16[1,512,256]{2,1,0:T(8,128)(2,1)}, u32[]{:S(2)}) copy-start(bf16[1,512,256]{2,1,0:T(8,128)(2,1)} %param.7) | copy-start | bytes 786436
  43.3 21.9 %collective-permute-start.14 = (bf16[512,256]{1,0:T(8,128)(2,1)S(1)}, bf16[512,256]{1,0:T(8,128)(2,1)S(1)}, u32[]{:S(2)}, u32[]{:S(2)}) collective-permute-start(bf16[512,256]{1,0:T(8,128)(2,1)S(1)} %get-tuple-element.38), channel_id=1, source_target_pairs={{0,2},{2,0},{4,6},{6,4},{8,10},{10,8},{12,14},{14,12},{1,3},{3,1},... | collective-permute-start | bytes 786440 | tf_op jit(solution)/shard_map/ppermute | solution.py:31
  48.9 17.8 %collective-permute-start.11 = (bf16[512,256]{1,0:T(8,128)(2,1)S(1)}, bf16[512,256]{1,0:T(8,128)(2,1)S(1)}, u32[]{:S(2)}, u32[]{:S(2)}) collective-permute-start(bf16[512,256]{1,0:T(8,128)(2,1)S(1)} %add_convert_fusion.2), channel_id=1, source_target_pairs={{0,4},{2,6},{4,0},{6,2},{8,12},{10,14},{12,8},{14,10},{1,5},{3,7},... | collective-permute-start | bytes 786440 | tf_op jit(solution)/shard_map/ppermute | solution.py:31
  60.2 10.1 %collective-permute-start.13 = (bf16[512,256]{1,0:T(8,128)(2,1)S(1)}, bf16[512,256]{1,0:T(8,128)(2,1)S(1)}, u32[]{:S(2)}, u32[]{:S(2)}) collective-permute-start(bf16[512,256]{1,0:T(8,128)(2,1)S(1)} %add_convert_fusion.1), channel_id=1, source_target_pairs={{0,12},{2,14},{4,8},{6,10},{8,4},{10,6},{12,0},{14,2},{1,13},{3,15... | collective-permute-start | bytes 786440 | tf_op jit(solution)/shard_map/ppermute | solution.py:31
  65.2 19.1 %collective-permute-start.15 = (bf16[512,256]{1,0:T(8,128)(2,1)S(1)}, bf16[512,256]{1,0:T(8,128)(2,1)S(1)}, u32[]{:S(2)}, u32[]{:S(2)}) collective-permute-start(bf16[512,256]{1,0:T(8,128)(2,1)S(1)} %add_convert_fusion), channel_id=1, source_target_pairs={{0,8},{2,10},{4,12},{6,14},{8,0},{10,2},{12,4},{14,6},{1,9},{3,11}... | collective-permute-start | bytes 786440 | tf_op jit(solution)/shard_map/ppermute | solution.py:31
  84.5 11.1 %collective-permute-start.20 = (bf16[512,256]{1,0:T(8,128)(2,1)S(1)}, bf16[512,256]{1,0:T(8,128)(2,1)S(1)}, u32[]{:S(2)}, u32[]{:S(2)}) collective-permute-start(bf16[512,256]{1,0:T(8,128)(2,1)S(1)} %fusion.1.refs_0_), channel_id=1, source_target_pairs={{0,12},{2,14},{4,8},{6,10},{8,4},{10,6},{12,0},{14,2},{1,13},{3,15... | collective-permute-start | bytes 786440 | tf_op jit(solution)/shard_map/ppermute | solution.py:31
  87.6 13.5 %collective-permute-start.18 = (bf16[512,256]{1,0:T(8,128)(2,1)S(1)}, bf16[512,256]{1,0:T(8,128)(2,1)S(1)}, u32[]{:S(2)}, u32[]{:S(2)}) collective-permute-start(bf16[512,256]{1,0:T(8,128)(2,1)S(1)} %fusion.1.refs_0_), channel_id=1, source_target_pairs={{0,4},{2,6},{4,0},{6,2},{8,12},{10,14},{12,8},{14,10},{1,5},{3,7},... | collective-permute-start | bytes 786440 | tf_op jit(solution)/shard_map/ppermute | solution.py:31
  87.6 19.1 %collective-permute-start.16 = (bf16[512,256]{1,0:T(8,128)(2,1)S(1)}, bf16[512,256]{1,0:T(8,128)(2,1)S(1)}, u32[]{:S(2)}, u32[]{:S(2)}) collective-permute-start(bf16[512,256]{1,0:T(8,128)(2,1)S(1)} %fusion.1.refs_0_), channel_id=1, source_target_pairs={{0,8},{2,10},{4,12},{6,14},{8,0},{10,2},{12,4},{14,6},{1,9},{3,11}... | collective-permute-start | bytes 786440 | tf_op jit(solution)/shard_map/ppermute | solution.py:31
  88.9 19.3 %collective-permute-start.19 = (bf16[512,256]{1,0:T(8,128)(2,1)S(1)}, bf16[512,256]{1,0:T(8,128)(2,1)S(1)}, u32[]{:S(2)}, u32[]{:S(2)}) collective-permute-start(bf16[512,256]{1,0:T(8,128)(2,1)S(1)} %fusion.1.refs_0_), channel_id=1, source_target_pairs={{0,2},{2,0},{4,6},{6,4},{8,10},{10,8},{12,14},{14,12},{1,3},{3,1},... | collective-permute-start | bytes 786440 | tf_op jit(solution)/shard_map/ppermute | solution.py:31
  95.6 13.8 %collective-permute-start.22 = (bf16[512,256]{1,0:T(8,128)(2,1)S(1)}, bf16[512,256]{1,0:T(8,128)(2,1)S(1)}, u32[]{:S(2)}, u32[]{:S(2)}) collective-permute-start(bf16[512,256]{1,0:T(8,128)(2,1)S(1)} %collective-permute-done.20.refs_1_), channel_id=1, source_target_pairs={{0,2},{2,0},{4,6},{6,4},{8,10},{10,8},{12,14},{14,12},{1,3},{3,1},... | collective-permute-start | bytes 786440 | tf_op jit(solution)/shard_map/ppermute | solution.py:31
  101.1 9.2 %collective-permute-start.21 = (bf16[512,256]{1,0:T(8,128)(2,1)S(1)}, bf16[512,256]{1,0:T(8,128)(2,1)S(1)}, u32[]{:S(2)}, u32[]{:S(2)}) collective-permute-start(bf16[512,256]{1,0:T(8,128)(2,1)S(1)} %collective-permute-done.18.refs_1_), channel_id=1, source_target_pairs={{0,2},{2,0},{4,6},{6,4},{8,10},{10,8},{12,14},{14,12},{1,3},{3,1},... | collective-permute-start | bytes 786440 | tf_op jit(solution)/shard_map/ppermute | solution.py:31
  106.7 7.7 %collective-permute-start.17 = (bf16[512,256]{1,0:T(8,128)(2,1)S(1)}, bf16[512,256]{1,0:T(8,128)(2,1)S(1)}, u32[]{:S(2)}, u32[]{:S(2)}) collective-permute-start(bf16[512,256]{1,0:T(8,128)(2,1)S(1)} %collective-permute-done.16.refs_0_), channel_id=1, source_target_pairs={{0,2},{2,0},{4,6},{6,4},{8,10},{10,8},{12,14},{14,12},{1,3},{3,1},... | collective-permute-start | bytes 786440 | tf_op jit(solution)/shard_map/ppermute | solution.py:31
  111.6 5.1 %copy-start.1 = (bf16[1,512,256]{2,1,0:T(8,128)(2,1)S(1)}, bf16[1,512,256]{2,1,0:T(8,128)(2,1)}, u32[]{:S(2)}) copy-start(bf16[1,512,256]{2,1,0:T(8,128)(2,1)} %param.6) | copy-start | bytes 786436
  115.5 4.2 %collective-permute-start.23 = (f32[1536,128]{1,0:T(8,128)S(1)}, f32[1536,128]{1,0:T(8,128)S(1)}, u32[]{:S(2)}, u32[]{:S(2)}) collective-permute-start(f32[1536,128]{1,0:T(8,128)S(1)} %get-tuple-element.45), channel_id=1, source_target_pairs={{1,0},{3,2},{5,4},{7,6},{9,8},{11,10},{13,12},{15,14},{17,16},{19,... | collective-permute-start | bytes 2359304 | tf_op jit(solution)/shard_map/ppermute | solution.py:23

commit v7 on v5

--- a/solution.py
+++ b/solution.py
@@ -78,23 +78,33 @@
     return pl.ds(pl.multiple_of(starts[slot], wide), wide)
 
 
-def prepare_kernel(starts, own_dec, low_cross, high_cross, weight, stacked, weight_here):
+def prepare_kernel(starts, own_dec, low_cross, high_cross, weight, stacked, weight_here, sems):
     lat, half_width = high_cross.shape
-    stacked[:lat, :] = own_dec[0]
-    stacked[lat:, :half_width] = low_cross[...]
-    stacked[lat:, half_width:] = high_cross[...]
-    weight_here[...] = weight[0]
+    copies = [
+        pltpu.make_async_copy(own_dec.at[0], stacked.at[:lat, :], sems.at[0]),
+        pltpu.make_async_copy(low_cross, stacked.at[lat:, :half_width], sems.at[1]),
+        pltpu.make_async_copy(high_cross, stacked.at[lat:, half_width:], sems.at[2]),
+        pltpu.make_async_copy(weight.at[0], weight_here, sems.at[3]),
+    ]
+    for copy in copies:
+        copy.start()
+    for copy in copies:
+        copy.wait()
 
 
 def encode_kernel(slots, last, starts, *refs):
-    shards, (weight, before, *outs) = refs[:len(slots)], refs[len(slots):]
-    total = jnp.broadcast_to(before[...], outs[0].shape)
-    for slot, shard in zip(slots, shards):
-        block = weight[block_of(starts, slot, shard.shape[1]), :]
-        total = total + jnp.dot(shard[...], block, preferred_element_type=F32)
-    outs[0][...] = total
-    if last:
-        outs[1][...] = jnp.maximum(total, 0.0).astype(BF16)
+    count = 2 * len(slots)
+    shards, (weight, before, *outs) = refs[:count], refs[count:]
+    rows, wide = shards[0].shape
+    for chain in range(2):
+        at = slice(chain * rows, (chain + 1) * rows)
+        total = before[at, :] if last else jnp.broadcast_to(before[...], (rows, before.shape[1]))
+        for i, slot in enumerate(slots):
+            block = weight[block_of(starts, slot, wide), :]
+            total = total + jnp.dot(shards[2 * i + chain][...], block, preferred_element_type=F32)
+        outs[0][at, :] = total
+        if last:
+            outs[1][at, :] = jnp.maximum(total, 0.0).astype(BF16)
 
 
 def turn_kernel(starts, *refs):
@@ -106,13 +116,15 @@
             turned[at, chain * rows:(chain + 1) * rows] = shards[2 * k + chain][...].T
 
 
-def spread_kernel(slots, starts, codes, earlier, stacked, *outs):
-    *partials, both_t = outs
-    both = jnp.concatenate([codes[...], earlier[...]], axis=1)
+def spread_kernel(chain, slots, starts, codes, earlier, stacked, *partials):
+    rows = codes.shape[0] // 2
+    at = slice(chain * rows, (chain + 1) * rows)
+    both = jnp.concatenate([codes[at, :], earlier[at, :]], axis=1)
     for slot, partial in zip(slots, partials):
         block = stacked[:, block_of(starts, slot, partial.shape[1])]
         partial[...] = jnp.dot(both, block, preferred_element_type=F32).astype(partial.dtype)
-    both_t[...] = both.T
+    if len(partials) > len(slots):
+        partials[-1][...] = both.T
 
 
 def back_products(slots, starts, shards, stacked, both_t, before):
@@ -169,10 +181,10 @@
 
 
 def finish_kernel(slots, far, starts, *refs):
-    turned, pre_0, pre_1, back_own, arrived, high, last_same, *outers = refs[:7 + len(slots)]
-    grad, bias, same, cross, stage, value, grad_sems, same_sems, cross_sems = refs[7 + len(slots):]
+    turned, preact, back_own, arrived, high, last_same, *outers = refs[:6 + len(slots)]
+    grad, bias, same, cross, stage, grad_sems, same_sems, cross_sems = refs[6 + len(slots):]
     pieces, height, lat = stage.shape
-    rows = pre_0.shape[0]
+    rows = preact.shape[0]
     half_width = high.shape[0]
     wide = last_same.shape[1]
     copies = []
@@ -183,13 +195,12 @@
         copies.append(pltpu.make_async_copy(block, same.at[0, :, block_of(starts, slot, wide)], same_sems.at[i]))
         copies[-1].start()
     first = starts[starts.shape[0] - 1] == 0
-    steps = range(half_width // lat)
-    for c in steps:
+    for c in range(half_width // lat):
         at = pl.ds(c * lat, lat)
 
         @pl.when(first)
         def _():
-            source = arrived.at[pl.ds(2 * rows + c * lat, lat), :]
+            source = arrived.at[pl.ds(rows + c * lat, lat), :]
             pltpu.make_async_copy(source, cross.at[:, at], cross_sems.at[c]).start()
 
         @pl.when(jnp.logical_not(first))
@@ -197,18 +208,13 @@
             pltpu.make_async_copy(high.at[at, :], cross.at[:, at], cross_sems.at[c]).start()
 
         copies.append(pltpu.make_async_copy(high.at[at, :], cross.at[:, at], cross_sems.at[c]))
-    total = 0.0
-    for chain, preact in enumerate((pre_0, pre_1)):
-        at = slice(chain * rows, (chain + 1) * rows)
-        masked = jnp.where(preact[...] > 0, back_own[at, :] + arrived[at, :], 0.0).astype(BF16)
-        value[at, :] = masked
-        total = total + jnp.sum(masked.astype(F32), axis=0, keepdims=True)
-    bias[...] = total
+    value = jnp.where(preact[...] > 0, back_own[...] + arrived[:rows, :], 0.0).astype(BF16)
     for i in range(pieces):
         at = pl.ds(i * height, height)
-        stage[i] = jnp.dot(turned[at, :], value[...], preferred_element_type=F32)
+        stage[i] = jnp.dot(turned[at, :], value, preferred_element_type=F32)
         copies.append(pltpu.make_async_copy(stage.at[i], grad.at[0, at, :], grad_sems.at[i]))
         copies[-1].start()
+    bias[...] = jnp.sum(value.astype(F32), axis=0, keepdims=True)
     for copy in copies:
         copy.wait()
 
@@ -247,56 +253,63 @@
             at_p, at_q = (0, 0) if s == 1 else (slot_p[s - 1], slot_q[s - 1])
             if s < reach:
                 pair = hop(found[chain][at_p], 1), hop(found[chain][at_q], -1)
-                found[chain][slot_p[s]], found[chain][slot_q[s]] = lax.optimization_barrier(pair)
+                if s == 1:
+                    pair = lax.optimization_barrier(pair)
+                found[chain][slot_p[s]], found[chain][slot_q[s]] = pair
             else:
                 found[chain][far] = hop(found[chain][at_q if chain else at_p], -1 if chain else 1)
 
     inputs = [[part] + [None] * (size - 1) for part in halves(residual_in[0])]
-    for s in range(1, reach + 1):
-        gather_step(inputs, s)
     low_cross = passed_along(dec_cross, "layer", 1)
     stacked, weight = call(
         prepare_kernel,
         [shape((2 * lat, deep), BF16), shape((deep, lat), BF16)],
         0,
         [starts, dec_same, low_cross, dec_cross, enc_weight],
-    )
+        spaces=[pl.ANY] * 4,
+        scratch=[pltpu.SemaphoreType.DMA((4,))],
+    )
+    for s in range(1, reach + 1):
+        if s == reach and reach > 1:
+            inputs[0][slot_p[s - 1]] = after(inputs[0][slot_p[s - 1]], stacked)
+        gather_step(inputs, s)
+
+    def both_chains(found, slots):
+        return [found[chain][slot] for slot in slots for chain in chains]
+
     early = tuple(range(size - 1))
-    preacts, codes, earlier = [], [], []
+    part = call(
+        functools.partial(encode_kernel, early, False),
+        [shape((rows, lat), F32)],
+        2 * unit * len(early),
+        [starts] + both_chains(inputs, early) + [weight, enc_bias],
+    )[0]
+    preact, codes = call(
+        functools.partial(encode_kernel, (far,), True),
+        [shape((rows, lat), F32), shape((rows, lat), BF16)],
+        2 * unit,
+        [starts] + both_chains(inputs, (far,)) + [weight, part],
+    )
+    earlier = passed_along(codes, "layer", 1)
+
+    def spread(chain, slots, dtype, turned):
+        return call(
+            functools.partial(spread_kernel, chain, slots),
+            [shape((half, wide), dtype) for _ in slots] + ([shape((2 * lat, half), BF16)] if turned else []),
+            2 * unit * len(slots),
+            [starts, codes, earlier, stacked],
+        )
+
+    first = [(far, slot_p[reach - 1]), (far, slot_q[reach - 1])] if reach > 1 else [(far,), (far,)]
+    partial, both_t = [], []
+    ahead, behind = [None, None], [None, None]
     for chain in chains:
-        part = call(
-            functools.partial(encode_kernel, early, False),
-            [shape((half, lat), F32)],
-            unit * len(early),
-            [starts] + inputs[chain][:-1] + [weight, enc_bias],
-        )[0]
-        preact, now = call(
-            functools.partial(encode_kernel, (far,), True),
-            [shape((half, lat), F32), shape((half, lat), BF16)],
-            unit,
-            [starts, inputs[chain][far], weight, part],
-        )
-        preacts.append(preact)
-        codes.append(now)
-        earlier.append(passed_along(now, "layer", 1))
-
-    spread = (far,) + tuple(slot for s in range(reach - 1, 0, -1) for slot in (slot_q[s], slot_p[s])) + (0,)
-    partial, both_t, ahead, behind = [], [], [], []
-    for chain in chains:
-        instant = {far, slot_q.get(reach - 1) if chain else slot_p.get(reach - 1)}
-        *pieces, turned_codes = call(
-            functools.partial(spread_kernel, spread),
-            [shape((half, wide), BF16 if slot in instant else F32) for slot in spread]
-            + [shape((2 * lat, half), BF16)],
-            2 * unit * len(spread),
-            [starts, codes[chain], earlier[chain], stacked],
-        )
-        partial.append(dict(zip(spread, pieces)))
+        rest = tuple(slot for slot in range(size) if slot not in first[chain])
+        instant = dict(zip(first[chain], spread(chain, first[chain], BF16, False)))
+        *pieces, turned_codes = spread(chain, rest, F32, True)
+        partial.append({**dict(zip(rest, pieces)), **instant})
         both_t.append(turned_codes)
-    both = [shard for pair in zip(*inputs) for shard in pair]
-    turned = call(turn_kernel, [shape((deep, rows), BF16)], unit, [starts] + both)[0]
-    ahead = [hop(partial[0][far], 1), None]
-    behind = [None, hop(partial[1][far], -1)]
+    ahead[0], behind[1] = hop(partial[0][far], 1), hop(partial[1][far], -1)
     for s in range(reach - 1, 0, -1):
         for chain in chains:
             plus, minus = partial[chain][slot_q[s]], partial[chain][slot_p[s]]
@@ -316,15 +329,12 @@
             wanted = after(wanted, errors[0][0])
         errors.append([((total - wanted.astype(F32)) * err_scale).astype(BF16)] + [None] * (size - 1))
 
-    def near(slots):
-        return [errors[chain][slot] for slot in slots for chain in chains]
-
     def back(slots, before):
         return call(
             functools.partial(back_kernel, slots, before is None),
             [shape((len(slots), 2 * lat, wide), F32), shape((2, half, 2 * lat), F32)],
             4 * unit * len(slots),
-            [starts] + near(slots) + [stacked] + both_t + ([] if before is None else [before]),
+            [starts] + both_chains(errors, slots) + [stacked] + both_t + ([] if before is None else [before]),
         )
 
     groups, outers, acc, pending = [], [], None, [0]
@@ -337,10 +347,6 @@
             outer, acc = back(groups[-1], acc)
             outers.append(outer)
             pending = []
-    if not groups:
-        groups.append((0,))
-        outer, acc = back(groups[-1], acc)
-        outers.append(outer)
     last_same, back_own, sent, high = call(
         functools.partial(last_back_kernel, groups, far),
         [
@@ -350,9 +356,10 @@
             shape((half_width, lat), F32),
         ],
         4 * unit,
-        [starts] + near((far,)) + [stacked] + both_t + outers + [acc],
-    )
-    arrived = passed_along(sent, "layer", -1)
+        [starts] + both_chains(errors, (far,)) + [stacked] + both_t + outers + [acc],
+    )
+    returned = passed_along(sent, "layer", -1)
+    turned = call(turn_kernel, [shape((deep, rows), BF16)], unit, [starts] + both_chains(inputs, range(size)))[0]
     height = deep // PIECES
     grad_enc, grad_bias, grad_same, grad_cross = call(
         functools.partial(finish_kernel, groups, far),
@@ -363,11 +370,10 @@
             shape((lat, half_width), F32),
         ],
         2 * unit * size,
-        [starts, turned] + preacts + [back_own, arrived, high, last_same] + outers,
+        [starts, turned, preact, back_own, returned, high, last_same] + outers,
         out_spaces=[pl.ANY, pltpu.VMEM, pl.ANY, pl.ANY],
         scratch=[
             pltpu.VMEM((PIECES, height, lat), F32),
-            pltpu.VMEM((rows, lat), BF16),
             pltpu.SemaphoreType.DMA((PIECES,)),
             pltpu.SemaphoreType.DMA((size,)),
             pltpu.SemaphoreType.DMA((half_width // lat,)),

time: 101 us -> 99.9 us (0.989)
  starting transfers between devices: 52.2 us -> 50.4 us
    ppermute x4 -> x3, starting transfers between devices: 5.62 us -> 3.89 us  [passed_along(): return lax.ppermute(shard, axis, pairs)]
    ppermute x4 -> x3, waiting for transfers between devices: 1.74 us -> 2.7 us  [passed_along(): return lax.ppermute(shard, axis, pairs)]
  transfers between devices with their start and end apart: 46 -> 45, of which waited for: 27 -> 23; matrix products, arithmetic and copies ran while one was open for 1% -> 0% of each run, Pallas kernels for 9% -> 8%
where the time goes in v7:
time: 99.9 us; the launch traced here: 99.6 us
  starting transfers between devices  50.4 us (50%)
  waiting for transfers between devices  30.1 us (30%)
  Pallas kernels  13.7 us (14%)
  local copies, waits for them, and re-layouts  4.12 us (4%)
    ppermute x42, starting transfers between devices, hop(): return lax.ppermute(shard, ('latent', 'layer'), pairs)  46.5 us
    ppermute x42, waiting for transfers between devices, hop(): return lax.ppermute(shard, ('latent', 'layer'), pairs)  27.4 us
    pallas_call x12, Pallas kernels, call(): pl.pallas_call(kernel, out_shape=outs, in_specs=[spec(pltpu.SMEM)] + [spe...  13.7 us
    ppermute x3, starting transfers between devices, passed_along(): return lax.ppermute(shard, axis, pairs)  3.89 us
    unnamed x10, local copies, waits for them, and re-layouts  3.04 us
    ppermute x3, waiting for transfers between devices, passed_along(): return lax.ppermute(shard, axis, pairs)  2.7 us
  transfers between devices with their start and end apart: 45, of which 23 were waited for; matrix products, arithmetic and copies ran while one was open for 0% of the time, Pallas kernels for 8%

profile of v7, /device:TPU:0, one launch (start us, length us, event | category | flops | bytes accessed | tf_op | source)
XLA Modules:
  0.0 99.6 jit_solution(18028459210429586132)
XLA Ops:
  1.6 3.0 %collective-permute-start.1 = (bf16[256,256]{1,0:T(8,128)(2,1)S(1)}, bf16[256,256]{1,0:T(8,128)(2,1)S(1)}, u32[]{:S(2)}, u32[]{:S(2)}) collective-permute-start(bf16[256,256]{1,0:T(8,128)(2,1)S(1)} %get-tuple-element.85.refs_0_), channel_id=1, source_target_pairs={{0,2},{1,5},{4,0},{5,9},{8,4},{9,13},{12,8},{13,15},{14,12},{15,11... | collective-permute-start | bytes 393224 | tf_op jit(solution)/shard_map/ppermute | solution.py:51
  4.8 1.9 %collective-permute-start.3 = (bf16[256,256]{1,0:T(8,128)(2,1)S(1)}, bf16[256,256]{1,0:T(8,128)(2,1)S(1)}, u32[]{:S(2)}, u32[]{:S(2)}) collective-permute-start(bf16[256,256]{1,0:T(8,128)(2,1)S(1)} %get-tuple-element.84.refs_1_), channel_id=1, source_target_pairs={{0,2},{1,5},{4,0},{5,9},{8,4},{9,13},{12,8},{13,15},{14,12},{15,11... | collective-permute-start | bytes 393224 | tf_op jit(solution)/shard_map/ppermute | solution.py:51
  6.8 1.3 %collective-permute-start.9 = (bf16[128,1024]{1,0:T(8,128)(2,1)}, bf16[128,1024]{1,0:T(8,128)(2,1)S(1)}, u32[]{:S(2)}, u32[]{:S(2)}) collective-permute-start(bf16[128,1024]{1,0:T(8,128)(2,1)} %high_cross.1), channel_id=1, source_target_pairs={{0,1},{2,3},{4,5},{6,7},{8,9},{10,11},{12,13},{14,15},{16,17},{18,... | collective-permute-start | bytes 786440 | tf_op jit(solution)/shard_map/ppermute | solution.py:23
  9.7 1.5 %collective-permute-start.4 = (bf16[256,256]{1,0:T(8,128)(2,1)S(1)}, bf16[256,256]{1,0:T(8,128)(2,1)S(1)}, u32[]{:S(2)}, u32[]{:S(2)}) collective-permute-start(bf16[256,256]{1,0:T(8,128)(2,1)S(1)} %collective-permute-done.refs_2_), channel_id=1, source_target_pairs={{0,4},{1,3},{4,8},{5,1},{8,12},{9,5},{12,14},{13,9},{14,10},{15,13... | collective-permute-start | bytes 393224 | tf_op jit(solution)/shard_map/ppermute | solution.py:51
  11.6 1.6 %collective-permute-start.7 = (bf16[256,256]{1,0:T(8,128)(2,1)S(1)}, bf16[256,256]{1,0:T(8,128)(2,1)S(1)}, u32[]{:S(2)}, u32[]{:S(2)}) collective-permute-start(bf16[256,256]{1,0:T(8,128)(2,1)S(1)} %collective-permute-done.3.refs_5_), channel_id=1, source_target_pairs={{0,2},{1,5},{4,0},{5,9},{8,4},{9,13},{12,8},{13,15},{14,12},{15,11... | collective-permute-start | bytes 393224 | tf_op jit(solution)/shard_map/ppermute | solution.py:51
  13.7 1.6 %collective-permute-start.6 = (bf16[256,256]{1,0:T(8,128)(2,1)S(1)}, bf16[256,256]{1,0:T(8,128)(2,1)S(1)}, u32[]{:S(2)}, u32[]{:S(2)}) collective-permute-start(bf16[256,256]{1,0:T(8,128)(2,1)S(1)} %collective-permute-done.1.refs_4_), channel_id=1, source_target_pairs={{0,2},{1,5},{4,0},{5,9},{8,4},{9,13},{12,8},{13,15},{14,12},{15,11... | collective-permute-start | bytes 393224 | tf_op jit(solution)/shard_map/ppermute | solution.py:51
  17.2 2.4 %collective-permute-start.12 = (bf16[256,256]{1,0:T(8,128)(2,1)S(1)}, bf16[256,256]{1,0:T(8,128)(2,1)S(1)}, u32[]{:S(2)}, u32[]{:S(2)}) collective-permute-start(bf16[256,256]{1,0:T(8,128)(2,1)S(1)} %collective-permute-done.7.refs_9_), channel_id=1, source_target_pairs={{0,2},{1,5},{4,0},{5,9},{8,4},{9,13},{12,8},{13,15},{14,12},{15,11... | collective-permute-start | bytes 393224 | tf_op jit(solution)/shard_map/ppermute | solution.py:51
  20.1 2.1 %collective-permute-start.11 = (bf16[256,256]{1,0:T(8,128)(2,1)S(1)}, bf16[256,256]{1,0:T(8,128)(2,1)S(1)}, u32[]{:S(2)}, u32[]{:S(2)}) collective-permute-start(bf16[256,256]{1,0:T(8,128)(2,1)S(1)} %collective-permute-done.6.refs_8_), channel_id=1, source_target_pairs={{0,2},{1,5},{4,0},{5,9},{8,4},{9,13},{12,8},{13,15},{14,12},{15,11... | collective-permute-start | bytes 393224 | tf_op jit(solution)/shard_map/ppermute | solution.py:51
  29.4 1.8 %collective-permute-done.14.refs_15_.refs_1_ = bf16[256,256]{1,0:T(8,128)(2,1)S(1)} collective-permute-done((bf16[256,256]{1,0:T(8,128)(2,1)S(1)}, bf16[256,256]{1,0:T(8,128)(2,1)S(1)}, u32[]{:S(2)}, u32[]{:S(2)}) %collective-permute-start.14) | collective-permute-done | bytes 131104 | tf_op jit(solution)/shard_map/ppermute | solution.py:51
  32.8 1.3 %collective-permute-start.15 = (bf16[512,128]{1,0:T(8,128)(2,1)S(1)}, bf16[512,128]{1,0:T(8,128)(2,1)S(1)}, u32[]{:S(2)}, u32[]{:S(2)}) collective-permute-start(bf16[512,128]{1,0:T(8,128)(2,1)S(1)} %get-tuple-element.52.codes), channel_id=1, source_target_pairs={{0,1},{2,3},{4,5},{6,7},{8,9},{10,11},{12,13},{14,15},{16,17},{18,... | collective-permute-start | bytes 393224 | tf_op jit(solution)/shard_map/ppermute | solution.py:23
  35.8 1.6 %collective-permute-start.28 = (bf16[256,256]{1,0:T(8,128)(2,1)S(1)}, bf16[256,256]{1,0:T(8,128)(2,1)S(1)}, u32[]{:S(2)}, u32[]{:S(2)}) collective-permute-start(bf16[256,256]{1,0:T(8,128)(2,1)S(1)} %get-tuple-element.65), channel_id=1, source_target_pairs={{0,4},{1,3},{4,8},{5,1},{8,12},{9,5},{12,14},{13,9},{14,10},{15,13... | collective-permute-start | bytes 393224 | tf_op jit(solution)/shard_map/ppermute | solution.py:51
  38.7 1.6 %collective-permute-start.16 = (bf16[256,256]{1,0:T(8,128)(2,1)S(1)}, bf16[256,256]{1,0:T(8,128)(2,1)S(1)}, u32[]{:S(2)}, u32[]{:S(2)}) collective-permute-start(bf16[256,256]{1,0:T(8,128)(2,1)S(1)} %get-tuple-element.57), channel_id=1, source_target_pairs={{0,4},{1,3},{4,8},{5,1},{8,12},{9,5},{12,14},{13,9},{14,10},{15,13... | collective-permute-start | bytes 393224 | tf_op jit(solution)/shard_map/ppermute | solution.py:51
  42.7 1.6 %collective-permute-start.29 = (bf16[256,256]{1,0:T(8,128)(2,1)S(1)}, bf16[256,256]{1,0:T(8,128)(2,1)S(1)}, u32[]{:S(2)}, u32[]{:S(2)}) collective-permute-start(bf16[256,256]{1,0:T(8,128)(2,1)S(1)} %add_convert_fusion.4), channel_id=1, source_target_pairs={{0,4},{1,3},{4,8},{5,1},{8,12},{9,5},{12,14},{13,9},{14,10},{15,13... | collective-permute-start | bytes 393224 | tf_op jit(solution)/shard_map/ppermute | solution.py:51
  44.9 1.6 %collective-permute-start.17 = (bf16[256,256]{1,0:T(8,128)(2,1)S(1)}, bf16[256,256]{1,0:T(8,128)(2,1)S(1)}, u32[]{:S(2)}, u32[]{:S(2)}) collective-permute-start(bf16[256,256]{1,0:T(8,128)(2,1)S(1)} %add_convert_fusion.9), channel_id=1, source_target_pairs={{0,4},{1,3},{4,8},{5,1},{8,12},{9,5},{12,14},{13,9},{14,10},{15,13... | collective-permute-start | bytes 393224 | tf_op jit(solution)/shard_map/ppermute | solution.py:51
  47.1 2.0 %collective-permute-done.29 = bf16[256,256]{1,0:T(8,128)(2,1)S(1)} collective-permute-done((bf16[256,256]{1,0:T(8,128)(2,1)S(1)}, bf16[256,256]{1,0:T(8,128)(2,1)S(1)}, u32[]{:S(2)}, u32[]{:S(2)}) %collective-permute-start.29) | collective-permute-done | bytes 131104 | tf_op jit(solution)/shard_map/ppermute | solution.py:51
  54.1 3.2 %collective-permute-done.18 = bf16[256,256]{1,0:T(8,128)(2,1)S(1)} collective-permute-done((bf16[256,256]{1,0:T(8,128)(2,1)S(1)}, bf16[256,256]{1,0:T(8,128)(2,1)S(1)}, u32[]{:S(2)}, u32[]{:S(2)}) %collective-permute-start.18) | collective-permute-done | bytes 131104 | tf_op jit(solution)/shard_map/ppermute | solution.py:51
  58.1 1.4 %collective-permute-start.34 = (bf16[256,256]{1,0:T(8,128)(2,1)S(1)}, bf16[256,256]{1,0:T(8,128)(2,1)S(1)}, u32[]{:S(2)}, u32[]{:S(2)}) collective-permute-start(bf16[256,256]{1,0:T(8,128)(2,1)S(1)} %add_convert_fusion), channel_id=1, source_target_pairs={{0,2},{1,5},{4,0},{5,9},{8,4},{9,13},{12,8},{13,15},{14,12},{15,11... | collective-permute-start | bytes 393224 | tf_op jit(solution)/shard_map/ppermute | solution.py:51
  59.6 3.0 %collective-permute-done.19 = bf16[256,256]{1,0:T(8,128)(2,1)S(1)} collective-permute-done((bf16[256,256]{1,0:T(8,128)(2,1)S(1)}, bf16[256,256]{1,0:T(8,128)(2,1)S(1)}, u32[]{:S(2)}, u32[]{:S(2)}) %collective-permute-start.19) | collective-permute-done | bytes 131104 | tf_op jit(solution)/shard_map/ppermute | solution.py:51
  63.3 1.9 %collective-permute-start.36 = (bf16[256,256]{1,0:T(8,128)(2,1)S(1)}, bf16[256,256]{1,0:T(8,128)(2,1)S(1)}, u32[]{:S(2)}, u32[]{:S(2)}) collective-permute-start(bf16[256,256]{1,0:T(8,128)(2,1)S(1)} %multiply_convert_fusion.refs_1_), channel_id=1, source_target_pairs={{0,2},{1,5},{4,0},{5,9},{8,4},{9,13},{12,8},{13,15},{14,12},{15,11... | collective-permute-start | bytes 393224 | tf_op jit(solution)/shard_map/ppermute | solution.py:51
  65.4 1.8 %collective-permute-start.24 = (bf16[256,256]{1,0:T(8,128)(2,1)S(1)}, bf16[256,256]{1,0:T(8,128)(2,1)S(1)}, u32[]{:S(2)}, u32[]{:S(2)}) collective-permute-start(bf16[256,256]{1,0:T(8,128)(2,1)S(1)} %fusion.1.refs_0_), channel_id=1, source_target_pairs={{0,2},{1,5},{4,0},{5,9},{8,4},{9,13},{12,8},{13,15},{14,12},{15,11... | collective-permute-start | bytes 393224 | tf_op jit(solution)/shard_map/ppermute | solution.py:51
  68.4 1.8 %collective-permute-done.35.refs_3_ = bf16[256,256]{1,0:T(8,128)(2,1)S(1)} collective-permute-done((bf16[256,256]{1,0:T(8,128)(2,1)S(1)}, bf16[256,256]{1,0:T(8,128)(2,1)S(1)}, u32[]{:S(2)}, u32[]{:S(2)}) %collective-permute-start.35) | collective-permute-done | bytes 131104 | tf_op jit(solution)/shard_map/ppermute | solution.py:51
  70.2 1.8 %collective-permute-start.37 = (bf16[256,256]{1,0:T(8,128)(2,1)S(1)}, bf16[256,256]{1,0:T(8,128)(2,1)S(1)}, u32[]{:S(2)}, u32[]{:S(2)}) collective-permute-start(bf16[256,256]{1,0:T(8,128)(2,1)S(1)} %collective-permute-done.36.refs_5_), channel_id=1, source_target_pairs={{0,2},{1,5},{4,0},{5,9},{8,4},{9,13},{12,8},{13,15},{14,12},{15,11... | collective-permute-start | bytes 393224 | tf_op jit(solution)/shard_map/ppermute | solution.py:51
  72.0 1.6 %collective-permute-done.23.refs_2_ = bf16[256,256]{1,0:T(8,128)(2,1)S(1)} collective-permute-done((bf16[256,256]{1,0:T(8,128)(2,1)S(1)}, bf16[256,256]{1,0:T(8,128)(2,1)S(1)}, u32[]{:S(2)}, u32[]{:S(2)}) %collective-permute-start.23) | collective-permute-done | bytes 131104 | tf_op jit(solution)/shard_map/ppermute | solution.py:51
  73.6 1.8 %collective-permute-start.40 = (bf16[256,256]{1,0:T(8,128)(2,1)S(1)}, bf16[256,256]{1,0:T(8,128)(2,1)S(1)}, u32[]{:S(2)}, u32[]{:S(2)}) collective-permute-start(bf16[256,256]{1,0:T(8,128)(2,1)S(1)} %collective-permute-done.35.refs_3_), channel_id=1, source_target_pairs={{0,4},{1,3},{4,8},{5,1},{8,12},{9,5},{12,14},{13,9},{14,10},{15,13... | collective-permute-start | bytes 393224 | tf_op jit(solution)/shard_map/ppermute | solution.py:51
  76.5 1.8 %collective-permute-start.38 = (bf16[256,256]{1,0:T(8,128)(2,1)S(1)}, bf16[256,256]{1,0:T(8,128)(2,1)S(1)}, u32[]{:S(2)}, u32[]{:S(2)}) collective-permute-start(bf16[256,256]{1,0:T(8,128)(2,1)S(1)} %collective-permute-done.37.refs_3_), channel_id=1, source_target_pairs={{0,2},{1,5},{4,0},{5,9},{8,4},{9,13},{12,8},{13,15},{14,12},{15,11... | collective-permute-start | bytes 393224 | tf_op jit(solution)/shard_map/ppermute | solution.py:51
  78.3 1.7 %collective-permute-done.25.refs_0_ = bf16[256,256]{1,0:T(8,128)(2,1)S(1)} collective-permute-done((bf16[256,256]{1,0:T(8,128)(2,1)S(1)}, bf16[256,256]{1,0:T(8,128)(2,1)S(1)}, u32[]{:S(2)}, u32[]{:S(2)}) %collective-permute-start.25) | collective-permute-done | bytes 131104 | tf_op jit(solution)/shard_map/ppermute | solution.py:51
  80.0 2.5 %collective-permute-done.40.refs_1_ = bf16[256,256]{1,0:T(8,128)(2,1)S(1)} collective-permute-done((bf16[256,256]{1,0:T(8,128)(2,1)S(1)}, bf16[256,256]{1,0:T(8,128)(2,1)S(1)}, u32[]{:S(2)}, u32[]{:S(2)}) %collective-permute-start.40) | collective-permute-done | bytes 131104 | tf_op jit(solution)/shard_map/ppermute | solution.py:51
  82.7 1.8 %collective-permute-start.43 = (bf16[256,256]{1,0:T(8,128)(2,1)S(1)}, bf16[256,256]{1,0:T(8,128)(2,1)S(1)}, u32[]{:S(2)}, u32[]{:S(2)}) collective-permute-start(bf16[256,256]{1,0:T(8,128)(2,1)S(1)} %collective-permute-done.41.refs_2_), channel_id=1, source_target_pairs={{0,2},{1,5},{4,0},{5,9},{8,4},{9,13},{12,8},{13,15},{14,12},{15,11... | collective-permute-start | bytes 393224 | tf_op jit(solution)/shard_map/ppermute | solution.py:51
  84.6 1.8 %collective-permute-start.39 = (bf16[256,256]{1,0:T(8,128)(2,1)S(1)}, bf16[256,256]{1,0:T(8,128)(2,1)S(1)}, u32[]{:S(2)}, u32[]{:S(2)}) collective-permute-start(bf16[256,256]{1,0:T(8,128)(2,1)S(1)} %collective-permute-done.38.refs_7_), channel_id=1, source_target_pairs={{0,2},{1,5},{4,0},{5,9},{8,4},{9,13},{12,8},{13,15},{14,12},{15,11... | collective-permute-start | bytes 393224 | tf_op jit(solution)/shard_map/ppermute | solution.py:51
  89.5 1.8 %collective-permute-done.27.refs_0_ = bf16[256,256]{1,0:T(8,128)(2,1)S(1)} collective-permute-done((bf16[256,256]{1,0:T(8,128)(2,1)S(1)}, bf16[256,256]{1,0:T(8,128)(2,1)S(1)}, u32[]{:S(2)}, u32[]{:S(2)}) %collective-permute-start.27) | collective-permute-done | bytes 131104 | tf_op jit(solution)/shard_map/ppermute | solution.py:51
  94.8 1.7 %collective-permute-done.44.refs_3_ = f32[1536,128]{1,0:T(8,128)S(1)} collective-permute-done((f32[1536,128]{1,0:T(8,128)S(1)}, f32[1536,128]{1,0:T(8,128)S(1)}, u32[]{:S(2)}, u32[]{:S(2)}) %collective-permute-start.44) | collective-permute-done | bytes 786464 | tf_op jit(solution)/shard_map/ppermute | solution.py:23
  96.5 3.1 %shard_map.104 = (f32[1,2048,128]{2,1,0:T(8,128)}, f32[1,128]{1,0:T(1,128)}, f32[1,128,2048]{2,1,0:T(8,128)}, f32[128,1024]{1,0:T(8,128)}) custom-call(s32[9]{0:T(128)S(1)} %stack.39.starts, bf16[2048,512]{1,0:T(8,128)(2,1)S(1)} %shard_map.94.refs_0_, f32[512,128]{1,0:T(8,128)S(1)} %get-tuple-element.51.refs_1_, f32[512,128]{1,0:T(8,128)S(1)} %get-tuple-element.80.refs_2_, ...), custom_call_target="tpu_custom_call" | custom-call | flops 268435456 | bytes 8520228 | tf_op jit(solution)/shard_map/pallas_call | solution.py:65
  (95 shorter events, 37.2 us)
Async XLA Ops:
  1.6 6.9 %collective-permute-start.1 = (bf16[256,256]{1,0:T(8,128)(2,1)S(1)}, bf16[256,256]{1,0:T(8,128)(2,1)S(1)}, u32[]{:S(2)}, u32[]{:S(2)}) collective-permute-start(bf16[256,256]{1,0:T(8,128)(2,1)S(1)} %get-tuple-element.85.refs_0_), channel_id=1, source_target_pairs={{0,2},{1,5},{4,0},{5,9},{8,4},{9,13},{12,8},{13,15},{14,12},{15,11... | collective-permute-start | bytes 393224 | tf_op jit(solution)/shard_map/ppermute | solution.py:51
  4.8 6.5 %collective-permute-start.3 = (bf16[256,256]{1,0:T(8,128)(2,1)S(1)}, bf16[256,256]{1,0:T(8,128)(2,1)S(1)}, u32[]{:S(2)}, u32[]{:S(2)}) collective-permute-start(bf16[256,256]{1,0:T(8,128)(2,1)S(1)} %get-tuple-element.84.refs_1_), channel_id=1, source_target_pairs={{0,2},{1,5},{4,0},{5,9},{8,4},{9,13},{12,8},{13,15},{14,12},{15,11... | collective-permute-start | bytes 393224 | tf_op jit(solution)/shard_map/ppermute | solution.py:51
  6.8 15.5 %collective-permute-start.9 = (bf16[128,1024]{1,0:T(8,128)(2,1)}, bf16[128,1024]{1,0:T(8,128)(2,1)S(1)}, u32[]{:S(2)}, u32[]{:S(2)}) collective-permute-start(bf16[128,1024]{1,0:T(8,128)(2,1)} %high_cross.1), channel_id=1, source_target_pairs={{0,1},{2,3},{4,5},{6,7},{8,9},{10,11},{12,13},{14,15},{16,17},{18,... | collective-permute-start | bytes 786440 | tf_op jit(solution)/shard_map/ppermute | solution.py:23
  9.7 5.7 %collective-permute-start.4 = (bf16[256,256]{1,0:T(8,128)(2,1)S(1)}, bf16[256,256]{1,0:T(8,128)(2,1)S(1)}, u32[]{:S(2)}, u32[]{:S(2)}) collective-permute-start(bf16[256,256]{1,0:T(8,128)(2,1)S(1)} %collective-permute-done.refs_2_), channel_id=1, source_target_pairs={{0,4},{1,3},{4,8},{5,1},{8,12},{9,5},{12,14},{13,9},{14,10},{15,13... | collective-permute-start | bytes 393224 | tf_op jit(solution)/shard_map/ppermute | solution.py:51
  11.6 5.6 %collective-permute-start.7 = (bf16[256,256]{1,0:T(8,128)(2,1)S(1)}, bf16[256,256]{1,0:T(8,128)(2,1)S(1)}, u32[]{:S(2)}, u32[]{:S(2)}) collective-permute-start(bf16[256,256]{1,0:T(8,128)(2,1)S(1)} %collective-permute-done.3.refs_5_), channel_id=1, source_target_pairs={{0,2},{1,5},{4,0},{5,9},{8,4},{9,13},{12,8},{13,15},{14,12},{15,11... | collective-permute-start | bytes 393224 | tf_op jit(solution)/shard_map/ppermute | solution.py:51
  13.2 6.4 %collective-permute-start.5 = (bf16[256,256]{1,0:T(8,128)(2,1)S(1)}, bf16[256,256]{1,0:T(8,128)(2,1)S(1)}, u32[]{:S(2)}, u32[]{:S(2)}) collective-permute-start(bf16[256,256]{1,0:T(8,128)(2,1)S(1)} %collective-permute-done.2.refs_3_), channel_id=1, source_target_pairs={{0,4},{1,3},{4,8},{5,1},{8,12},{9,5},{12,14},{13,9},{14,10},{15,13... | collective-permute-start | bytes 393224 | tf_op jit(solution)/shard_map/ppermute | solution.py:51
  13.7 6.4 %collective-permute-start.6 = (bf16[256,256]{1,0:T(8,128)(2,1)S(1)}, bf16[256,256]{1,0:T(8,128)(2,1)S(1)}, u32[]{:S(2)}, u32[]{:S(2)}) collective-permute-start(bf16[256,256]{1,0:T(8,128)(2,1)S(1)} %collective-permute-done.1.refs_4_), channel_id=1, source_target_pairs={{0,2},{1,5},{4,0},{5,9},{8,4},{9,13},{12,8},{13,15},{14,12},{15,11... | collective-permute-start | bytes 393224 | tf_op jit(solution)/shard_map/ppermute | solution.py:51
  15.4 10.7 %collective-permute-start.8 = (bf16[256,256]{1,0:T(8,128)(2,1)S(1)}, bf16[256,256]{1,0:T(8,128)(2,1)S(1)}, u32[]{:S(2)}, u32[]{:S(2)}) collective-permute-start(bf16[256,256]{1,0:T(8,128)(2,1)S(1)} %collective-permute-done.4.refs_6_), channel_id=1, source_target_pairs={{0,4},{1,3},{4,8},{5,1},{8,12},{9,5},{12,14},{13,9},{14,10},{15,13... | collective-permute-start | bytes 393224 | tf_op jit(solution)/shard_map/ppermute | solution.py:51
  17.2 8.8 %collective-permute-start.12 = (bf16[256,256]{1,0:T(8,128)(2,1)S(1)}, bf16[256,256]{1,0:T(8,128)(2,1)S(1)}, u32[]{:S(2)}, u32[]{:S(2)}) collective-permute-start(bf16[256,256]{1,0:T(8,128)(2,1)S(1)} %collective-permute-done.7.refs_9_), channel_id=1, source_target_pairs={{0,2},{1,5},{4,0},{5,9},{8,4},{9,13},{12,8},{13,15},{14,12},{15,11... | collective-permute-start | bytes 393224 | tf_op jit(solution)/shard_map/ppermute | solution.py:51
  19.6 8.6 %collective-permute-start.10 = (bf16[256,256]{1,0:T(8,128)(2,1)S(1)}, bf16[256,256]{1,0:T(8,128)(2,1)S(1)}, u32[]{:S(2)}, u32[]{:S(2)}) collective-permute-start(bf16[256,256]{1,0:T(8,128)(2,1)S(1)} %collective-permute-done.5.refs_7_), channel_id=1, source_target_pairs={{0,4},{1,3},{4,8},{5,1},{8,12},{9,5},{12,14},{13,9},{14,10},{15,13... | collective-permute-start | bytes 393224 | tf_op jit(solution)/shard_map/ppermute | solution.py:51
  20.1 8.0 %collective-permute-start.11 = (bf16[256,256]{1,0:T(8,128)(2,1)S(1)}, bf16[256,256]{1,0:T(8,128)(2,1)S(1)}, u32[]{:S(2)}, u32[]{:S(2)}) collective-permute-start(bf16[256,256]{1,0:T(8,128)(2,1)S(1)} %collective-permute-done.6.refs_8_), channel_id=1, source_target_pairs={{0,2},{1,5},{4,0},{5,9},{8,4},{9,13},{12,8},{13,15},{14,12},{15,11... | collective-permute-start | bytes 393224 | tf_op jit(solution)/shard_map/ppermute | solution.py:51
  35.8 6.9 %collective-permute-start.28 = (bf16[256,256]{1,0:T(8,128)(2,1)S(1)}, bf16[256,256]{1,0:T(8,128)(2,1)S(1)}, u32[]{:S(2)}, u32[]{:S(2)}) collective-permute-start(bf16[256,256]{1,0:T(8,128)(2,1)S(1)} %get-tuple-element.65), channel_id=1, source_target_pairs={{0,4},{1,3},{4,8},{5,1},{8,12},{9,5},{12,14},{13,9},{14,10},{15,13... | collective-permute-start | bytes 393224 | tf_op jit(solution)/shard_map/ppermute | solution.py:51
  37.4 6.9 %collective-permute-start.31 = (bf16[256,256]{1,0:T(8,128)(2,1)S(1)}, bf16[256,256]{1,0:T(8,128)(2,1)S(1)}, u32[]{:S(2)}, u32[]{:S(2)}) collective-permute-start(bf16[256,256]{1,0:T(8,128)(2,1)S(1)} %get-tuple-element.69), channel_id=1, source_target_pairs={{0,2},{1,5},{4,0},{5,9},{8,4},{9,13},{12,8},{13,15},{14,12},{15,11... | collective-permute-start | bytes 393224 | tf_op jit(solution)/shard_map/ppermute | solution.py:51
  38.7 6.2 %collective-permute-start.16 = (bf16[256,256]{1,0:T(8,128)(2,1)S(1)}, bf16[256,256]{1,0:T(8,128)(2,1)S(1)}, u32[]{:S(2)}, u32[]{:S(2)}) collective-permute-start(bf16[256,256]{1,0:T(8,128)(2,1)S(1)} %get-tuple-element.57), channel_id=1, source_target_pairs={{0,4},{1,3},{4,8},{5,1},{8,12},{9,5},{12,14},{13,9},{14,10},{15,13... | collective-permute-start | bytes 393224 | tf_op jit(solution)/shard_map/ppermute | solution.py:51
  40.4 6.2 %collective-permute-start.20 = (bf16[256,256]{1,0:T(8,128)(2,1)S(1)}, bf16[256,256]{1,0:T(8,128)(2,1)S(1)}, u32[]{:S(2)}, u32[]{:S(2)}) collective-permute-start(bf16[256,256]{1,0:T(8,128)(2,1)S(1)} %get-tuple-element.60), channel_id=1, source_target_pairs={{0,2},{1,5},{4,0},{5,9},{8,4},{9,13},{12,8},{13,15},{14,12},{15,11... | collective-permute-start | bytes 393224 | tf_op jit(solution)/shard_map/ppermute | solution.py:51
  42.7 6.4 %collective-permute-start.29 = (bf16[256,256]{1,0:T(8,128)(2,1)S(1)}, bf16[256,256]{1,0:T(8,128)(2,1)S(1)}, u32[]{:S(2)}, u32[]{:S(2)}) collective-permute-start(bf16[256,256]{1,0:T(8,128)(2,1)S(1)} %add_convert_fusion.4), channel_id=1, source_target_pairs={{0,4},{1,3},{4,8},{5,1},{8,12},{9,5},{12,14},{13,9},{14,10},{15,13... | collective-permute-start | bytes 393224 | tf_op jit(solution)/shard_map/ppermute | solution.py:51
  44.4 5.9 %collective-permute-start.32 = (bf16[256,256]{1,0:T(8,128)(2,1)S(1)}, bf16[256,256]{1,0:T(8,128)(2,1)S(1)}, u32[]{:S(2)}, u32[]{:S(2)}) collective-permute-start(bf16[256,256]{1,0:T(8,128)(2,1)S(1)} %add_convert_fusion.2), channel_id=1, source_target_pairs={{0,2},{1,5},{4,0},{5,9},{8,4},{9,13},{12,8},{13,15},{14,12},{15,11... | collective-permute-start | bytes 393224 | tf_op jit(solution)/shard_map/ppermute | solution.py:51
  44.9 7.0 %collective-permute-start.17 = (bf16[256,256]{1,0:T(8,128)(2,1)S(1)}, bf16[256,256]{1,0:T(8,128)(2,1)S(1)}, u32[]{:S(2)}, u32[]{:S(2)}) collective-permute-start(bf16[256,256]{1,0:T(8,128)(2,1)S(1)} %add_convert_fusion.9), channel_id=1, source_target_pairs={{0,4},{1,3},{4,8},{5,1},{8,12},{9,5},{12,14},{13,9},{14,10},{15,13... | collective-permute-start | bytes 393224 | tf_op jit(solution)/shard_map/ppermute | solution.py:51
  46.6 6.4 %collective-permute-start.21 = (bf16[256,256]{1,0:T(8,128)(2,1)S(1)}, bf16[256,256]{1,0:T(8,128)(2,1)S(1)}, u32[]{:S(2)}, u32[]{:S(2)}) collective-permute-start(bf16[256,256]{1,0:T(8,128)(2,1)S(1)} %add_convert_fusion.6), channel_id=1, source_target_pairs={{0,2},{1,5},{4,0},{5,9},{8,4},{9,13},{12,8},{13,15},{14,12},{15,11... | collective-permute-start | bytes 393224 | tf_op jit(solution)/shard_map/ppermute | solution.py:51
  49.2 13.5 %collective-permute-start.30 = (bf16[256,256]{1,0:T(8,128)(2,1)S(1)}, bf16[256,256]{1,0:T(8,128)(2,1)S(1)}, u32[]{:S(2)}, u32[]{:S(2)}) collective-permute-start(bf16[256,256]{1,0:T(8,128)(2,1)S(1)} %add_convert_fusion.3), channel_id=1, source_target_pairs={{0,4},{1,3},{4,8},{5,1},{8,12},{9,5},{12,14},{13,9},{14,10},{15,13... | collective-permute-start | bytes 393224 | tf_op jit(solution)/shard_map/ppermute | solution.py:51
  50.3 7.8 %collective-permute-start.33 = (bf16[256,256]{1,0:T(8,128)(2,1)S(1)}, bf16[256,256]{1,0:T(8,128)(2,1)S(1)}, u32[]{:S(2)}, u32[]{:S(2)}) collective-permute-start(bf16[256,256]{1,0:T(8,128)(2,1)S(1)} %add_convert_fusion.1), channel_id=1, source_target_pairs={{0,2},{1,5},{4,0},{5,9},{8,4},{9,13},{12,8},{13,15},{14,12},{15,11... | collective-permute-start | bytes 393224 | tf_op jit(solution)/shard_map/ppermute | solution.py:51
  52.0 5.4 %collective-permute-start.18 = (bf16[256,256]{1,0:T(8,128)(2,1)S(1)}, bf16[256,256]{1,0:T(8,128)(2,1)S(1)}, u32[]{:S(2)}, u32[]{:S(2)}) collective-permute-start(bf16[256,256]{1,0:T(8,128)(2,1)S(1)} %add_convert_fusion.8), channel_id=1, source_target_pairs={{0,4},{1,3},{4,8},{5,1},{8,12},{9,5},{12,14},{13,9},{14,10},{15,13... | collective-permute-start | bytes 393224 | tf_op jit(solution)/shard_map/ppermute | solution.py:51
  53.0 6.6 %collective-permute-start.22 = (bf16[256,256]{1,0:T(8,128)(2,1)S(1)}, bf16[256,256]{1,0:T(8,128)(2,1)S(1)}, u32[]{:S(2)}, u32[]{:S(2)}) collective-permute-start(bf16[256,256]{1,0:T(8,128)(2,1)S(1)} %add_convert_fusion.5), channel_id=1, source_target_pairs={{0,2},{1,5},{4,0},{5,9},{8,4},{9,13},{12,8},{13,15},{14,12},{15,11... | collective-permute-start | bytes 393224 | tf_op jit(solution)/shard_map/ppermute | solution.py:51
  65.4 6.6 %collective-permute-start.24 = (bf16[256,256]{1,0:T(8,128)(2,1)S(1)}, bf16[256,256]{1,0:T(8,128)(2,1)S(1)}, u32[]{:S(2)}, u32[]{:S(2)}) collective-permute-start(bf16[256,256]{1,0:T(8,128)(2,1)S(1)} %fusion.1.refs_0_), channel_id=1, source_target_pairs={{0,2},{1,5},{4,0},{5,9},{8,4},{9,13},{12,8},{13,15},{14,12},{15,11... | collective-permute-start | bytes 393224 | tf_op jit(solution)/shard_map/ppermute | solution.py:51
  67.3 6.4 %collective-permute-start.23 = (bf16[256,256]{1,0:T(8,128)(2,1)S(1)}, bf16[256,256]{1,0:T(8,128)(2,1)S(1)}, u32[]{:S(2)}, u32[]{:S(2)}) collective-permute-start(bf16[256,256]{1,0:T(8,128)(2,1)S(1)} %fusion.1.refs_0_), channel_id=1, source_target_pairs={{0,4},{1,3},{4,8},{5,1},{8,12},{9,5},{12,14},{13,9},{14,10},{15,13... | collective-permute-start | bytes 393224 | tf_op jit(solution)/shard_map/ppermute | solution.py:51
  70.2 6.3 %collective-permute-start.37 = (bf16[256,256]{1,0:T(8,128)(2,1)S(1)}, bf16[256,256]{1,0:T(8,128)(2,1)S(1)}, u32[]{:S(2)}, u32[]{:S(2)}) collective-permute-start(bf16[256,256]{1,0:T(8,128)(2,1)S(1)} %collective-permute-done.36.refs_5_), channel_id=1, source_target_pairs={{0,2},{1,5},{4,0},{5,9},{8,4},{9,13},{12,8},{13,15},{14,12},{15,11... | collective-permute-start | bytes 393224 | tf_op jit(solution)/shard_map/ppermute | solution.py:51
  73.6 6.4 %collective-permute-start.25 = (bf16[256,256]{1,0:T(8,128)(2,1)S(1)}, bf16[256,256]{1,0:T(8,128)(2,1)S(1)}, u32[]{:S(2)}, u32[]{:S(2)}) collective-permute-start(bf16[256,256]{1,0:T(8,128)(2,1)S(1)} %collective-permute-done.23.refs_2_), channel_id=1, source_target_pairs={{0,4},{1,3},{4,8},{5,1},{8,12},{9,5},{12,14},{13,9},{14,10},{15,13... | collective-permute-start | bytes 393224 | tf_op jit(solution)/shard_map/ppermute | solution.py:51
  73.6 8.9 %collective-permute-start.40 = (bf16[256,256]{1,0:T(8,128)(2,1)S(1)}, bf16[256,256]{1,0:T(8,128)(2,1)S(1)}, u32[]{:S(2)}, u32[]{:S(2)}) collective-permute-start(bf16[256,256]{1,0:T(8,128)(2,1)S(1)} %collective-permute-done.35.refs_3_), channel_id=1, source_target_pairs={{0,4},{1,3},{4,8},{5,1},{8,12},{9,5},{12,14},{13,9},{14,10},{15,13... | collective-permute-start | bytes 393224 | tf_op jit(solution)/shard_map/ppermute | solution.py:51
  75.4 7.3 %collective-permute-start.41 = (bf16[256,256]{1,0:T(8,128)(2,1)S(1)}, bf16[256,256]{1,0:T(8,128)(2,1)S(1)}, u32[]{:S(2)}, u32[]{:S(2)}) collective-permute-start(bf16[256,256]{1,0:T(8,128)(2,1)S(1)} %collective-permute-done.24.refs_4_), channel_id=1, source_target_pairs={{0,2},{1,5},{4,0},{5,9},{8,4},{9,13},{12,8},{13,15},{14,12},{15,11... | collective-permute-start | bytes 393224 | tf_op jit(solution)/shard_map/ppermute | solution.py:51
  76.5 8.1 %collective-permute-start.38 = (bf16[256,256]{1,0:T(8,128)(2,1)S(1)}, bf16[256,256]{1,0:T(8,128)(2,1)S(1)}, u32[]{:S(2)}, u32[]{:S(2)}) collective-permute-start(bf16[256,256]{1,0:T(8,128)(2,1)S(1)} %collective-permute-done.37.refs_3_), channel_id=1, source_target_pairs={{0,2},{1,5},{4,0},{5,9},{8,4},{9,13},{12,8},{13,15},{14,12},{15,11... | collective-permute-start | bytes 393224 | tf_op jit(solution)/shard_map/ppermute | solution.py:51
  80.0 6.3 %collective-permute-start.26 = (bf16[256,256]{1,0:T(8,128)(2,1)S(1)}, bf16[256,256]{1,0:T(8,128)(2,1)S(1)}, u32[]{:S(2)}, u32[]{:S(2)}) collective-permute-start(bf16[256,256]{1,0:T(8,128)(2,1)S(1)} %collective-permute-done.25.refs_0_), channel_id=1, source_target_pairs={{0,4},{1,3},{4,8},{5,1},{8,12},{9,5},{12,14},{13,9},{14,10},{15,13... | collective-permute-start | bytes 393224 | tf_op jit(solution)/shard_map/ppermute | solution.py:51
  82.5 5.2 %collective-permute-start.42 = (bf16[256,256]{1,0:T(8,128)(2,1)S(1)}, bf16[256,256]{1,0:T(8,128)(2,1)S(1)}, u32[]{:S(2)}, u32[]{:S(2)}) collective-permute-start(bf16[256,256]{1,0:T(8,128)(2,1)S(1)} %collective-permute-done.40.refs_1_), channel_id=1, source_target_pairs={{0,4},{1,3},{4,8},{5,1},{8,12},{9,5},{12,14},{13,9},{14,10},{15,13... | collective-permute-start | bytes 393224 | tf_op jit(solution)/shard_map/ppermute | solution.py:51
  (18 other events, 101.6 us)

commit v8 on v7

--- a/solution.py
+++ b/solution.py
@@ -41,14 +41,9 @@
 
 
 def hop(shard, way):
-    size, layers = lax.axis_size("latent"), lax.axis_size("layer")
+    size = lax.axis_size("latent")
     order = ring_order(size)
-    pairs = []
-    for p in range(size):
-        for layer in range(layers):
-            by = way if layer % 2 == 0 else -way
-            pairs.append((order[p] * layers + layer, order[(p + by) % size] * layers + layer))
-    return lax.ppermute(shard, ("latent", "layer"), pairs)
+    return lax.ppermute(shard, "latent", [(order[p], order[(p + way) % size]) for p in range(size)])
 
 
 def after(value, *others):
@@ -61,7 +56,6 @@
 
     spaces = spaces or [pltpu.VMEM] * (len(operands) - 1)
     out_spaces = out_spaces or [pltpu.VMEM] * len(outs)
-    size = sum(math.prod(x.shape) * x.dtype.itemsize for x in list(operands) + list(outs))
     return pl.pallas_call(
         kernel,
         out_shape=outs,
@@ -70,26 +64,12 @@
         scratch_shapes=list(scratch),
         input_output_aliases=aliases or {},
         compiler_params=pltpu.CompilerParams(vmem_limit_bytes=VMEM_BYTES),
-        cost_estimate=pl.CostEstimate(flops=flops, bytes_accessed=size, transcendentals=0),
+        cost_estimate=pl.CostEstimate(flops=flops, bytes_accessed=1024, transcendentals=0),
     )(*operands)
 
 
 def block_of(starts, slot, wide):
     return pl.ds(pl.multiple_of(starts[slot], wide), wide)
-
-
-def prepare_kernel(starts, own_dec, low_cross, high_cross, weight, stacked, weight_here, sems):
-    lat, half_width = high_cross.shape
-    copies = [
-        pltpu.make_async_copy(own_dec.at[0], stacked.at[:lat, :], sems.at[0]),
-        pltpu.make_async_copy(low_cross, stacked.at[lat:, :half_width], sems.at[1]),
-        pltpu.make_async_copy(high_cross, stacked.at[lat:, half_width:], sems.at[2]),
-        pltpu.make_async_copy(weight.at[0], weight_here, sems.at[3]),
-    ]
-    for copy in copies:
-        copy.start()
-    for copy in copies:
-        copy.wait()
 
 
 def encode_kernel(slots, last, starts, *refs):
@@ -100,7 +80,7 @@
         at = slice(chain * rows, (chain + 1) * rows)
         total = before[at, :] if last else jnp.broadcast_to(before[...], (rows, before.shape[1]))
         for i, slot in enumerate(slots):
-            block = weight[block_of(starts, slot, wide), :]
+            block = weight[0, block_of(starts, slot, wide), :]
             total = total + jnp.dot(shards[2 * i + chain][...], block, preferred_element_type=F32)
         outs[0][at, :] = total
         if last:
@@ -116,15 +96,18 @@
             turned[at, chain * rows:(chain + 1) * rows] = shards[2 * k + chain][...].T
 
 
-def spread_kernel(chain, slots, starts, codes, earlier, stacked, *partials):
+def spread_kernel(slots, starts, codes, earlier, stacked, *outs):
     rows = codes.shape[0] // 2
-    at = slice(chain * rows, (chain + 1) * rows)
-    both = jnp.concatenate([codes[at, :], earlier[at, :]], axis=1)
-    for slot, partial in zip(slots, partials):
-        block = stacked[:, block_of(starts, slot, partial.shape[1])]
-        partial[...] = jnp.dot(both, block, preferred_element_type=F32).astype(partial.dtype)
-    if len(partials) > len(slots):
-        partials[-1][...] = both.T
+    outs = list(outs)
+    for chain in range(2):
+        at = slice(chain * rows, (chain + 1) * rows)
+        both = jnp.concatenate([codes[at, :], earlier[at, :]], axis=1)
+        for slot in slots:
+            partial = outs.pop(0)
+            block = stacked[:, block_of(starts, slot, partial.shape[1])]
+            partial[...] = jnp.dot(both, block, preferred_element_type=F32).astype(partial.dtype)
+        if len(outs) > (1 - chain) * len(slots):
+            outs.pop(0)[...] = both.T
 
 
 def back_products(slots, starts, shards, stacked, both_t, before):
@@ -224,7 +207,6 @@
     reach = size // 2
     place = ring_place(lax.axis_index("latent"), size)
     layer = lax.axis_index("layer")
-    sign = jnp.where(layer % 2 == 0, 1, -1)
     rows, wide = residual_in.shape[1:]
     half = rows // 2
     deep, lat = enc_weight.shape[1:]
@@ -245,34 +227,27 @@
     for s in range(1, reach):
         offsets[slot_p[s]] = -s
         offsets[slot_q[s]] = s
-    starts = jnp.stack([ring_member(place + sign * offset, size) * wide for offset in offsets] + [layer])
+    starts = jnp.stack([ring_member(place + offset, size) * wide for offset in offsets] + [layer])
     starts = starts.astype(jnp.int32)
 
-    def gather_step(found, s):
+    def gather_step(found, s, ready=None):
         for chain in chains:
             at_p, at_q = (0, 0) if s == 1 else (slot_p[s - 1], slot_q[s - 1])
             if s < reach:
-                pair = hop(found[chain][at_p], 1), hop(found[chain][at_q], -1)
-                if s == 1:
-                    pair = lax.optimization_barrier(pair)
-                found[chain][slot_p[s]], found[chain][slot_q[s]] = pair
+                ahead, behind = found[chain][at_p], found[chain][at_q]
+                if ready is not None:
+                    ahead, behind = (after(ahead, ready), behind) if chain else (ahead, after(behind, ready))
+                found[chain][slot_p[s]], found[chain][slot_q[s]] = hop(ahead, 1), hop(behind, -1)
             else:
                 found[chain][far] = hop(found[chain][at_q if chain else at_p], -1 if chain else 1)
 
     inputs = [[part] + [None] * (size - 1) for part in halves(residual_in[0])]
-    low_cross = passed_along(dec_cross, "layer", 1)
-    stacked, weight = call(
-        prepare_kernel,
-        [shape((2 * lat, deep), BF16), shape((deep, lat), BF16)],
-        0,
-        [starts, dec_same, low_cross, dec_cross, enc_weight],
-        spaces=[pl.ANY] * 4,
-        scratch=[pltpu.SemaphoreType.DMA((4,))],
-    )
+    low_cross = passed_along(after(dec_cross, inputs[0][0]), "layer", 1)
+    stacked = jnp.concatenate([dec_same[0], jnp.concatenate([low_cross, dec_cross], axis=1)], axis=0)
     for s in range(1, reach + 1):
         if s == reach and reach > 1:
             inputs[0][slot_p[s - 1]] = after(inputs[0][slot_p[s - 1]], stacked)
-        gather_step(inputs, s)
+        gather_step(inputs, s, low_cross if s == 1 else None)
 
     def both_chains(found, slots):
         return [found[chain][slot] for slot in slots for chain in chains]
@@ -282,34 +257,34 @@
         functools.partial(encode_kernel, early, False),
         [shape((rows, lat), F32)],
         2 * unit * len(early),
-        [starts] + both_chains(inputs, early) + [weight, enc_bias],
+        [starts] + both_chains(inputs, early) + [enc_weight, enc_bias],
     )[0]
     preact, codes = call(
         functools.partial(encode_kernel, (far,), True),
         [shape((rows, lat), F32), shape((rows, lat), BF16)],
         2 * unit,
-        [starts] + both_chains(inputs, (far,)) + [weight, part],
+        [starts] + both_chains(inputs, (far,)) + [enc_weight, part],
     )
     earlier = passed_along(codes, "layer", 1)
 
-    def spread(chain, slots, dtype, turned):
-        return call(
-            functools.partial(spread_kernel, chain, slots),
-            [shape((half, wide), dtype) for _ in slots] + ([shape((2 * lat, half), BF16)] if turned else []),
-            2 * unit * len(slots),
-            [starts, codes, earlier, stacked],
+    def spread(slots, dtypes, turned):
+        outs = []
+        for chain in chains:
+            outs += [shape((half, wide), dtypes[chain].get(slot, F32)) for slot in slots]
+            outs += [shape((2 * lat, half), BF16)] if turned else []
+        found = call(
+            functools.partial(spread_kernel, slots), outs, 4 * unit * len(slots), [starts, codes, earlier, stacked]
         )
-
-    first = [(far, slot_p[reach - 1]), (far, slot_q[reach - 1])] if reach > 1 else [(far,), (far,)]
+        return found[:len(outs) // 2], found[len(outs) // 2:]
+
+    rest = tuple(slot for slot in range(size) if slot != far)
+    instant = ({far: BF16, slot_p.get(reach - 1): BF16}, {far: BF16, slot_q.get(reach - 1): BF16})
+    far_0, far_1 = spread((far,), instant, False)
+    ahead, behind = [hop(far_0[0], 1), None], [None, hop(far_1[0], -1)]
     partial, both_t = [], []
-    ahead, behind = [None, None], [None, None]
-    for chain in chains:
-        rest = tuple(slot for slot in range(size) if slot not in first[chain])
-        instant = dict(zip(first[chain], spread(chain, first[chain], BF16, False)))
-        *pieces, turned_codes = spread(chain, rest, F32, True)
-        partial.append({**dict(zip(rest, pieces)), **instant})
-        both_t.append(turned_codes)
-    ahead[0], behind[1] = hop(partial[0][far], 1), hop(partial[1][far], -1)
+    for pieces in spread(rest, instant, True):
+        partial.append(dict(zip(rest, pieces)))
+        both_t.append(pieces[-1])
     for s in range(reach - 1, 0, -1):
         for chain in chains:
             plus, minus = partial[chain][slot_q[s]], partial[chain][slot_p[s]]

time: 99.9 us -> 98.8 us (0.989)
  waiting for transfers between devices: 30.1 us -> 34.8 us
  local copies, waits for them, and re-layouts: 4.12 us -> 1.15 us
  starting transfers between devices: 50.4 us -> 47.8 us
  Pallas kernels: 13.7 us -> 12.3 us
  other arithmetic: 0.42 us -> 1.62 us
    ppermute x42, waiting for transfers between devices: 27.4 us -> 32.5 us  [hop(): lax.ppermute(shard, 'latent', [(order[p], order[(p + way) % size]) for p...]
    ppermute x42, starting transfers between devices: 46.5 us -> 42.9 us  [hop(): lax.ppermute(shard, 'latent', [(order[p], order[(p + way) % size]) for p...]
    unnamed x10 -> x6, local copies, waits for them, and re-layouts: 3.04 us -> 0.01 us
    pallas_call x12 -> x9, Pallas kernels: 13.7 us -> 12.3 us  [call(): pl.pallas_call(kernel, out_shape=outs, in_specs=[spec(pltpu.SMEM)] + [spe...]
    concatenate x0 -> x1, other arithmetic: none -> 1.19 us  [ring_shards(): jnp.concatenate([dec_same[0], jnp.concatenate([low_cross, dec_cross], axi...]
    ppermute x3, starting transfers between devices: 3.89 us -> 4.96 us  [passed_along(): return lax.ppermute(shard, axis, pairs)]
  transfers between devices with their start and end apart: 45 -> 45, of which waited for: 23 -> 23; matrix products, arithmetic and copies ran while one was open for 0% -> 2% of each run, Pallas kernels for 8% -> 6%
where the time goes in v8:
time: 98.8 us; the launch traced here: 98.6 us
  starting transfers between devices  47.8 us (48%)
  waiting for transfers between devices  34.8 us (35%)
  Pallas kernels  12.3 us (12%)
  other arithmetic  1.62 us (2%)
  local copies, waits for them, and re-layouts  1.15 us (1%)
    ppermute x42, starting transfers between devices, hop(): lax.ppermute(shard, 'latent', [(order[p], order[(p + way) % size]) for p...  42.9 us
    ppermute x42, waiting for transfers between devices, hop(): lax.ppermute(shard, 'latent', [(order[p], order[(p + way) % size]) for p...  32.5 us
    pallas_call x9, Pallas kernels, call(): pl.pallas_call(kernel, out_shape=outs, in_specs=[spec(pltpu.SMEM)] + [spe...  12.3 us
    ppermute x3, starting transfers between devices, passed_along(): return lax.ppermute(shard, axis, pairs)  4.96 us
    ppermute x3, waiting for transfers between devices, passed_along(): return lax.ppermute(shard, axis, pairs)  2.32 us
  transfers between devices with their start and end apart: 45, of which 23 were waited for; matrix products, arithmetic and copies ran while one was open for 2% of the time, Pallas kernels for 6%

profile of v8, /device:TPU:0, one launch (start us, length us, event | category | flops | bytes accessed | tf_op | source)
XLA Modules:
  0.0 98.6 jit_solution(10412247434203047928)
XLA Ops:
  1.7 2.4 %collective-permute-start.1 = (bf16[128,1024]{1,0:T(8,128)(2,1)}, bf16[128,1024]{1,0:T(8,128)(2,1)S(1)}, u32[]{:S(2)}, u32[]{:S(2)}) collective-permute-start(bf16[128,1024]{1,0:T(8,128)(2,1)} %param.11), channel_id=1, source_target_pairs={{0,1},{2,3},{4,5},{6,7},{8,9},{10,11},{12,13},{14,15},{16,17},{18,... | collective-permute-start | bytes 786440 | tf_op jit(solution)/shard_map/ppermute | solution.py:23
  4.1 2.5 %collective-permute-start = (bf16[256,256]{1,0:T(8,128)(2,1)S(1)}, bf16[256,256]{1,0:T(8,128)(2,1)S(1)}, u32[]{:S(2)}, u32[]{:S(2)}) collective-permute-start(bf16[256,256]{1,0:T(8,128)(2,1)S(1)} %get-tuple-element.39.refs_0_), channel_id=1, source_target_pairs={{0,4},{4,8},{8,12},{12,14},{14,10},{10,6},{6,2},{2,0},{1,5},{5,9},... | collective-permute-start | bytes 393224 | tf_op jit(solution)/shard_map/ppermute | solution.py:46
  6.5 2.0 %collective-permute-start.2 = (bf16[256,256]{1,0:T(8,128)(2,1)S(1)}, bf16[256,256]{1,0:T(8,128)(2,1)S(1)}, u32[]{:S(2)}, u32[]{:S(2)}) collective-permute-start(bf16[256,256]{1,0:T(8,128)(2,1)S(1)} %get-tuple-element.38.refs_1_), channel_id=1, source_target_pairs={{0,4},{4,8},{8,12},{12,14},{14,10},{10,6},{6,2},{2,0},{1,5},{5,9},... | collective-permute-start | bytes 393224 | tf_op jit(solution)/shard_map/ppermute | solution.py:46
  8.6 4.0 %collective-permute-done.4.refs_5_ = bf16[256,256]{1,0:T(8,128)(2,1)S(1)} collective-permute-done((bf16[256,256]{1,0:T(8,128)(2,1)S(1)}, bf16[256,256]{1,0:T(8,128)(2,1)S(1)}, u32[]{:S(2)}, u32[]{:S(2)}) %collective-permute-start.4) | collective-permute-done | bytes 131104 | tf_op jit(solution)/shard_map/ppermute | solution.py:46
  12.6 2.0 %collective-permute-start.5 = (bf16[256,256]{1,0:T(8,128)(2,1)S(1)}, bf16[256,256]{1,0:T(8,128)(2,1)S(1)}, u32[]{:S(2)}, u32[]{:S(2)}) collective-permute-start(bf16[256,256]{1,0:T(8,128)(2,1)S(1)} %collective-permute-done.refs_2_), channel_id=1, source_target_pairs={{0,4},{4,8},{8,12},{12,14},{14,10},{10,6},{6,2},{2,0},{1,5},{5,9},... | collective-permute-start | bytes 393224 | tf_op jit(solution)/shard_map/ppermute | solution.py:46
  14.6 1.6 %collective-permute-start.6 = (bf16[256,256]{1,0:T(8,128)(2,1)S(1)}, bf16[256,256]{1,0:T(8,128)(2,1)S(1)}, u32[]{:S(2)}, u32[]{:S(2)}) collective-permute-start(bf16[256,256]{1,0:T(8,128)(2,1)S(1)} %collective-permute-done.2.refs_3_), channel_id=1, source_target_pairs={{0,4},{4,8},{8,12},{12,14},{14,10},{10,6},{6,2},{2,0},{1,5},{5,9},... | collective-permute-start | bytes 393224 | tf_op jit(solution)/shard_map/ppermute | solution.py:46
  16.6 2.3 %collective-permute-done.8.refs_9_ = bf16[256,256]{1,0:T(8,128)(2,1)S(1)} collective-permute-done((bf16[256,256]{1,0:T(8,128)(2,1)S(1)}, bf16[256,256]{1,0:T(8,128)(2,1)S(1)}, u32[]{:S(2)}, u32[]{:S(2)}) %collective-permute-start.8) | collective-permute-done | bytes 131104 | tf_op jit(solution)/shard_map/ppermute | solution.py:46
  19.0 2.0 %collective-permute-start.9 = (bf16[256,256]{1,0:T(8,128)(2,1)S(1)}, bf16[256,256]{1,0:T(8,128)(2,1)S(1)}, u32[]{:S(2)}, u32[]{:S(2)}) collective-permute-start(bf16[256,256]{1,0:T(8,128)(2,1)S(1)} %collective-permute-done.5.refs_6_), channel_id=1, source_target_pairs={{0,4},{4,8},{8,12},{12,14},{14,10},{10,6},{6,2},{2,0},{1,5},{5,9},... | collective-permute-start | bytes 393224 | tf_op jit(solution)/shard_map/ppermute | solution.py:46
  21.0 1.6 %collective-permute-start.10 = (bf16[256,256]{1,0:T(8,128)(2,1)S(1)}, bf16[256,256]{1,0:T(8,128)(2,1)S(1)}, u32[]{:S(2)}, u32[]{:S(2)}) collective-permute-start(bf16[256,256]{1,0:T(8,128)(2,1)S(1)} %collective-permute-done.6.refs_7_), channel_id=1, source_target_pairs={{0,4},{4,8},{8,12},{12,14},{14,10},{10,6},{6,2},{2,0},{1,5},{5,9},... | collective-permute-start | bytes 393224 | tf_op jit(solution)/shard_map/ppermute | solution.py:46
  25.9 1.3 %collective-permute-start.13 = (bf16[256,256]{1,0:T(8,128)(2,1)S(1)}, bf16[256,256]{1,0:T(8,128)(2,1)}, u32[]{:S(2)}, u32[]{:S(2)}) collective-permute-start(bf16[256,256]{1,0:T(8,128)(2,1)S(1)} %collective-permute-done.9.refs_10_), channel_id=1, source_target_pairs={{0,4},{4,8},{8,12},{12,14},{14,10},{10,6},{6,2},{2,0},{1,5},{5,9},... | collective-permute-start | bytes 393224 | tf_op jit(solution)/shard_map/ppermute | solution.py:46
  28.7 1.4 %collective-permute-done.14.refs_15_.refs_1_ = bf16[256,256]{1,0:T(8,128)(2,1)S(1)} collective-permute-done((bf16[256,256]{1,0:T(8,128)(2,1)S(1)}, bf16[256,256]{1,0:T(8,128)(2,1)S(1)}, u32[]{:S(2)}, u32[]{:S(2)}) %collective-permute-start.14) | collective-permute-done | bytes 131104 | tf_op jit(solution)/shard_map/ppermute | solution.py:46
  35.1 1.4 %collective-permute-start.16 = (bf16[256,256]{1,0:T(8,128)(2,1)S(1)}, bf16[256,256]{1,0:T(8,128)(2,1)S(1)}, u32[]{:S(2)}, u32[]{:S(2)}) collective-permute-start(bf16[256,256]{1,0:T(8,128)(2,1)S(1)} %get-tuple-element.47), channel_id=1, source_target_pairs={{0,4},{4,8},{8,12},{12,14},{14,10},{10,6},{6,2},{2,0},{1,5},{5,9},... | collective-permute-start | bytes 393224 | tf_op jit(solution)/shard_map/ppermute | solution.py:46
  38.5 1.6 %collective-permute-start.20 = (bf16[256,256]{1,0:T(8,128)(2,1)S(1)}, bf16[256,256]{1,0:T(8,128)(2,1)S(1)}, u32[]{:S(2)}, u32[]{:S(2)}) collective-permute-start(bf16[256,256]{1,0:T(8,128)(2,1)S(1)} %get-tuple-element.50), channel_id=1, source_target_pairs={{0,2},{4,0},{8,4},{12,8},{14,12},{10,14},{6,10},{2,6},{1,3},{5,1},... | collective-permute-start | bytes 393224 | tf_op jit(solution)/shard_map/ppermute | solution.py:46
  41.0 1.4 %collective-permute-start.17 = (bf16[256,256]{1,0:T(8,128)(2,1)S(1)}, bf16[256,256]{1,0:T(8,128)(2,1)S(1)}, u32[]{:S(2)}, u32[]{:S(2)}) collective-permute-start(bf16[256,256]{1,0:T(8,128)(2,1)S(1)} %add_convert_fusion.9), channel_id=1, source_target_pairs={{0,4},{4,8},{8,12},{12,14},{14,10},{10,6},{6,2},{2,0},{1,5},{5,9},... | collective-permute-start | bytes 393224 | tf_op jit(solution)/shard_map/ppermute | solution.py:46
  42.4 2.5 %collective-permute-done.20 = bf16[256,256]{1,0:T(8,128)(2,1)S(1)} collective-permute-done((bf16[256,256]{1,0:T(8,128)(2,1)S(1)}, bf16[256,256]{1,0:T(8,128)(2,1)S(1)}, u32[]{:S(2)}, u32[]{:S(2)}) %collective-permute-start.20) | collective-permute-done | bytes 131104 | tf_op jit(solution)/shard_map/ppermute | solution.py:46
  47.1 1.6 %collective-permute-start.31 = (bf16[256,256]{1,0:T(8,128)(2,1)S(1)}, bf16[256,256]{1,0:T(8,128)(2,1)S(1)}, u32[]{:S(2)}, u32[]{:S(2)}) collective-permute-start(bf16[256,256]{1,0:T(8,128)(2,1)S(1)} %add_convert_fusion.2), channel_id=1, source_target_pairs={{0,2},{4,0},{8,4},{12,8},{14,12},{10,14},{6,10},{2,6},{1,3},{5,1},... | collective-permute-start | bytes 393224 | tf_op jit(solution)/shard_map/ppermute | solution.py:46
  49.3 2.1 %collective-permute-done.21 = bf16[256,256]{1,0:T(8,128)(2,1)S(1)} collective-permute-done((bf16[256,256]{1,0:T(8,128)(2,1)S(1)}, bf16[256,256]{1,0:T(8,128)(2,1)S(1)}, u32[]{:S(2)}, u32[]{:S(2)}) %collective-permute-start.21) | collective-permute-done | bytes 131104 | tf_op jit(solution)/shard_map/ppermute | solution.py:46
  52.2 1.4 %collective-permute-start.29 = (bf16[256,256]{1,0:T(8,128)(2,1)S(1)}, bf16[256,256]{1,0:T(8,128)(2,1)S(1)}, u32[]{:S(2)}, u32[]{:S(2)}) collective-permute-start(bf16[256,256]{1,0:T(8,128)(2,1)S(1)} %add_convert_fusion.3), channel_id=1, source_target_pairs={{0,4},{4,8},{8,12},{12,14},{14,10},{10,6},{6,2},{2,0},{1,5},{5,9},... | collective-permute-start | bytes 393224 | tf_op jit(solution)/shard_map/ppermute | solution.py:46
  56.3 3.4 %collective-permute-done.32 = bf16[256,256]{1,0:T(8,128)(2,1)S(1)} collective-permute-done((bf16[256,256]{1,0:T(8,128)(2,1)S(1)}, bf16[256,256]{1,0:T(8,128)(2,1)S(1)}, u32[]{:S(2)}, u32[]{:S(2)}) %collective-permute-start.32) | collective-permute-done | bytes 131104 | tf_op jit(solution)/shard_map/ppermute | solution.py:46
  60.9 1.4 %collective-permute-start.23 = (bf16[256,256]{1,0:T(8,128)(2,1)S(1)}, bf16[256,256]{1,0:T(8,128)(2,1)S(1)}, u32[]{:S(2)}, u32[]{:S(2)}) collective-permute-start(bf16[256,256]{1,0:T(8,128)(2,1)S(1)} %fusion.1.refs_0_), channel_id=1, source_target_pairs={{0,4},{4,8},{8,12},{12,14},{14,10},{10,6},{6,2},{2,0},{1,5},{5,9},... | collective-permute-start | bytes 393224 | tf_op jit(solution)/shard_map/ppermute | solution.py:46
  62.3 3.9 %collective-permute-done.33 = bf16[256,256]{1,0:T(8,128)(2,1)S(1)} collective-permute-done((bf16[256,256]{1,0:T(8,128)(2,1)S(1)}, bf16[256,256]{1,0:T(8,128)(2,1)S(1)}, u32[]{:S(2)}, u32[]{:S(2)}) %collective-permute-start.33) | collective-permute-done | bytes 131104 | tf_op jit(solution)/shard_map/ppermute | solution.py:46
  67.1 1.6 %collective-permute-start.39 = (bf16[256,256]{1,0:T(8,128)(2,1)S(1)}, bf16[256,256]{1,0:T(8,128)(2,1)S(1)}, u32[]{:S(2)}, u32[]{:S(2)}) collective-permute-start(bf16[256,256]{1,0:T(8,128)(2,1)S(1)} %fusion.1.refs_0_), channel_id=1, source_target_pairs={{0,2},{4,0},{8,4},{12,8},{14,12},{10,14},{6,10},{2,6},{1,3},{5,1},... | collective-permute-start | bytes 393224 | tf_op jit(solution)/shard_map/ppermute | solution.py:46
  70.4 2.3 %collective-permute-done.34.refs_5_ = bf16[256,256]{1,0:T(8,128)(2,1)S(1)} collective-permute-done((bf16[256,256]{1,0:T(8,128)(2,1)S(1)}, bf16[256,256]{1,0:T(8,128)(2,1)S(1)}, u32[]{:S(2)}, u32[]{:S(2)}) %collective-permute-start.34) | collective-permute-done | bytes 131104 | tf_op jit(solution)/shard_map/ppermute | solution.py:46
  73.4 2.1 %collective-permute-done.39.refs_4_ = bf16[256,256]{1,0:T(8,128)(2,1)S(1)} collective-permute-done((bf16[256,256]{1,0:T(8,128)(2,1)S(1)}, bf16[256,256]{1,0:T(8,128)(2,1)S(1)}, u32[]{:S(2)}, u32[]{:S(2)}) %collective-permute-start.39) | collective-permute-done | bytes 131104 | tf_op jit(solution)/shard_map/ppermute | solution.py:46
  77.5 1.5 %collective-permute-start.25 = (bf16[256,256]{1,0:T(8,128)(2,1)S(1)}, bf16[256,256]{1,0:T(8,128)(2,1)S(1)}, u32[]{:S(2)}, u32[]{:S(2)}) collective-permute-start(bf16[256,256]{1,0:T(8,128)(2,1)S(1)} %collective-permute-done.24.refs_0_), channel_id=1, source_target_pairs={{0,4},{4,8},{8,12},{12,14},{14,10},{10,6},{6,2},{2,0},{1,5},{5,9},... | collective-permute-start | bytes 393224 | tf_op jit(solution)/shard_map/ppermute | solution.py:46
  79.6 2.2 %collective-permute-done.41.refs_2_ = bf16[256,256]{1,0:T(8,128)(2,1)S(1)} collective-permute-done((bf16[256,256]{1,0:T(8,128)(2,1)S(1)}, bf16[256,256]{1,0:T(8,128)(2,1)S(1)}, u32[]{:S(2)}, u32[]{:S(2)}) %collective-permute-start.41) | collective-permute-done | bytes 131104 | tf_op jit(solution)/shard_map/ppermute | solution.py:46
  82.4 1.5 %collective-permute-start.42 = (bf16[256,256]{1,0:T(8,128)(2,1)S(1)}, bf16[256,256]{1,0:T(8,128)(2,1)S(1)}, u32[]{:S(2)}, u32[]{:S(2)}) collective-permute-start(bf16[256,256]{1,0:T(8,128)(2,1)S(1)} %collective-permute-done.40.refs_1_), channel_id=1, source_target_pairs={{0,4},{4,8},{8,12},{12,14},{14,10},{10,6},{6,2},{2,0},{1,5},{5,9},... | collective-permute-start | bytes 393224 | tf_op jit(solution)/shard_map/ppermute | solution.py:46
  83.9 1.4 %collective-permute-start.26 = (bf16[256,256]{1,0:T(8,128)(2,1)S(1)}, bf16[256,256]{1,0:T(8,128)(2,1)S(1)}, u32[]{:S(2)}, u32[]{:S(2)}) collective-permute-start(bf16[256,256]{1,0:T(8,128)(2,1)S(1)} %collective-permute-done.25.refs_4_), channel_id=1, source_target_pairs={{0,4},{4,8},{8,12},{12,14},{14,10},{10,6},{6,2},{2,0},{1,5},{5,9},... | collective-permute-start | bytes 393224 | tf_op jit(solution)/shard_map/ppermute | solution.py:46
  88.9 1.4 %collective-permute-done.37.refs_1_ = bf16[256,256]{1,0:T(8,128)(2,1)S(1)} collective-permute-done((bf16[256,256]{1,0:T(8,128)(2,1)S(1)}, bf16[256,256]{1,0:T(8,128)(2,1)S(1)}, u32[]{:S(2)}, u32[]{:S(2)}) %collective-permute-start.37) | collective-permute-done | bytes 131104 | tf_op jit(solution)/shard_map/ppermute | solution.py:46
  92.6 1.5 %shard_map.93.refs_0_ = bf16[2048,512]{1,0:T(8,128)(2,1)S(1)} custom-call(s32[9]{0:T(128)S(1)} %stack.39.starts, bf16[256,256]{1,0:T(8,128)(2,1)S(1)} %get-tuple-element.39.refs_0_, bf16[256,256]{1,0:T(8,128)(2,1)S(1)} %get-tuple-element.38.refs_1_, bf16[256,256]{1,0:T(8,128)(2,1)S(1)} %collective-permute-done.refs_2_, ...), custom_call_target="tpu_custom_call" | custom-call | flops 16777216 | bytes 1024 | tf_op jit(solution)/shard_map/pallas_call | solution.py:59
  94.1 1.4 %collective-permute-done.44.refs_3_ = f32[1536,128]{1,0:T(8,128)S(1)} collective-permute-done((f32[1536,128]{1,0:T(8,128)S(1)}, f32[1536,128]{1,0:T(8,128)S(1)}, u32[]{:S(2)}, u32[]{:S(2)}) %collective-permute-start.44) | collective-permute-done | bytes 786464 | tf_op jit(solution)/shard_map/ppermute | solution.py:23
  95.5 3.1 %shard_map.101 = (f32[1,2048,128]{2,1,0:T(8,128)}, f32[1,128]{1,0:T(1,128)}, f32[1,128,2048]{2,1,0:T(8,128)}, f32[128,1024]{1,0:T(8,128)}) custom-call(s32[9]{0:T(128)S(1)} %stack.39.starts, bf16[2048,512]{1,0:T(8,128)(2,1)S(1)} %shard_map.93.refs_0_, f32[512,128]{1,0:T(8,128)S(1)} %get-tuple-element.41.refs_1_, f32[512,128]{1,0:T(8,128)S(1)} %get-tuple-element.66.refs_2_, ...), custom_call_target="tpu_custom_call" | custom-call | flops 268435456 | bytes 1024 | tf_op jit(solution)/shard_map/pallas_call | solution.py:59
  (89 shorter events, 34.0 us)
Async XLA Ops:
  4.1 8.5 %collective-permute-start = (bf16[256,256]{1,0:T(8,128)(2,1)S(1)}, bf16[256,256]{1,0:T(8,128)(2,1)S(1)}, u32[]{:S(2)}, u32[]{:S(2)}) collective-permute-start(bf16[256,256]{1,0:T(8,128)(2,1)S(1)} %get-tuple-element.39.refs_0_), channel_id=1, source_target_pairs={{0,4},{4,8},{8,12},{12,14},{14,10},{10,6},{6,2},{2,0},{1,5},{5,9},... | collective-permute-start | bytes 393224 | tf_op jit(solution)/shard_map/ppermute | solution.py:46
  6.5 6.0 %collective-permute-start.4 = (bf16[256,256]{1,0:T(8,128)(2,1)S(1)}, bf16[256,256]{1,0:T(8,128)(2,1)S(1)}, u32[]{:S(2)}, u32[]{:S(2)}) collective-permute-start(bf16[256,256]{1,0:T(8,128)(2,1)S(1)} %get-tuple-element.38.refs_1_), channel_id=1, source_target_pairs={{0,2},{4,0},{8,4},{12,8},{14,12},{10,14},{6,10},{2,6},{1,3},{5,1},... | collective-permute-start | bytes 393224 | tf_op jit(solution)/shard_map/ppermute | solution.py:46
  6.5 8.1 %collective-permute-start.2 = (bf16[256,256]{1,0:T(8,128)(2,1)S(1)}, bf16[256,256]{1,0:T(8,128)(2,1)S(1)}, u32[]{:S(2)}, u32[]{:S(2)}) collective-permute-start(bf16[256,256]{1,0:T(8,128)(2,1)S(1)} %get-tuple-element.38.refs_1_), channel_id=1, source_target_pairs={{0,4},{4,8},{8,12},{12,14},{14,10},{10,6},{6,2},{2,0},{1,5},{5,9},... | collective-permute-start | bytes 393224 | tf_op jit(solution)/shard_map/ppermute | solution.py:46
  8.6 7.6 %collective-permute-start.3 = (bf16[256,256]{1,0:T(8,128)(2,1)S(1)}, bf16[256,256]{1,0:T(8,128)(2,1)S(1)}, u32[]{:S(2)}, u32[]{:S(2)}) collective-permute-start(bf16[256,256]{1,0:T(8,128)(2,1)S(1)} %get-tuple-element.39.refs_0_), channel_id=1, source_target_pairs={{0,2},{4,0},{8,4},{12,8},{14,12},{10,14},{6,10},{2,6},{1,3},{5,1},... | collective-permute-start | bytes 393224 | tf_op jit(solution)/shard_map/ppermute | solution.py:46
  12.6 6.4 %collective-permute-start.8 = (bf16[256,256]{1,0:T(8,128)(2,1)S(1)}, bf16[256,256]{1,0:T(8,128)(2,1)S(1)}, u32[]{:S(2)}, u32[]{:S(2)}) collective-permute-start(bf16[256,256]{1,0:T(8,128)(2,1)S(1)} %collective-permute-done.4.refs_5_), channel_id=1, source_target_pairs={{0,2},{4,0},{8,4},{12,8},{14,12},{10,14},{6,10},{2,6},{1,3},{5,1},... | collective-permute-start | bytes 393224 | tf_op jit(solution)/shard_map/ppermute | solution.py:46
  12.6 6.4 %collective-permute-start.5 = (bf16[256,256]{1,0:T(8,128)(2,1)S(1)}, bf16[256,256]{1,0:T(8,128)(2,1)S(1)}, u32[]{:S(2)}, u32[]{:S(2)}) collective-permute-start(bf16[256,256]{1,0:T(8,128)(2,1)S(1)} %collective-permute-done.refs_2_), channel_id=1, source_target_pairs={{0,4},{4,8},{8,12},{12,14},{14,10},{10,6},{6,2},{2,0},{1,5},{5,9},... | collective-permute-start | bytes 393224 | tf_op jit(solution)/shard_map/ppermute | solution.py:46
  14.6 6.4 %collective-permute-start.6 = (bf16[256,256]{1,0:T(8,128)(2,1)S(1)}, bf16[256,256]{1,0:T(8,128)(2,1)S(1)}, u32[]{:S(2)}, u32[]{:S(2)}) collective-permute-start(bf16[256,256]{1,0:T(8,128)(2,1)S(1)} %collective-permute-done.2.refs_3_), channel_id=1, source_target_pairs={{0,4},{4,8},{8,12},{12,14},{14,10},{10,6},{6,2},{2,0},{1,5},{5,9},... | collective-permute-start | bytes 393224 | tf_op jit(solution)/shard_map/ppermute | solution.py:46
  16.2 6.4 %collective-permute-start.7 = (bf16[256,256]{1,0:T(8,128)(2,1)S(1)}, bf16[256,256]{1,0:T(8,128)(2,1)S(1)}, u32[]{:S(2)}, u32[]{:S(2)}) collective-permute-start(bf16[256,256]{1,0:T(8,128)(2,1)S(1)} %collective-permute-done.3.refs_4_), channel_id=1, source_target_pairs={{0,2},{4,0},{8,4},{12,8},{14,12},{10,14},{6,10},{2,6},{1,3},{5,1},... | collective-permute-start | bytes 393224 | tf_op jit(solution)/shard_map/ppermute | solution.py:46
  19.0 6.2 %collective-permute-start.12 = (bf16[256,256]{1,0:T(8,128)(2,1)S(1)}, bf16[256,256]{1,0:T(8,128)(2,1)S(1)}, u32[]{:S(2)}, u32[]{:S(2)}) collective-permute-start(bf16[256,256]{1,0:T(8,128)(2,1)S(1)} %collective-permute-done.8.refs_9_), channel_id=1, source_target_pairs={{0,2},{4,0},{8,4},{12,8},{14,12},{10,14},{6,10},{2,6},{1,3},{5,1},... | collective-permute-start | bytes 393224 | tf_op jit(solution)/shard_map/ppermute | solution.py:46
  21.0 6.3 %collective-permute-start.10 = (bf16[256,256]{1,0:T(8,128)(2,1)S(1)}, bf16[256,256]{1,0:T(8,128)(2,1)S(1)}, u32[]{:S(2)}, u32[]{:S(2)}) collective-permute-start(bf16[256,256]{1,0:T(8,128)(2,1)S(1)} %collective-permute-done.6.refs_7_), channel_id=1, source_target_pairs={{0,4},{4,8},{8,12},{12,14},{14,10},{10,6},{6,2},{2,0},{1,5},{5,9},... | collective-permute-start | bytes 393224 | tf_op jit(solution)/shard_map/ppermute | solution.py:46
  35.1 5.8 %collective-permute-start.16 = (bf16[256,256]{1,0:T(8,128)(2,1)S(1)}, bf16[256,256]{1,0:T(8,128)(2,1)S(1)}, u32[]{:S(2)}, u32[]{:S(2)}) collective-permute-start(bf16[256,256]{1,0:T(8,128)(2,1)S(1)} %get-tuple-element.47), channel_id=1, source_target_pairs={{0,4},{4,8},{8,12},{12,14},{14,10},{10,6},{6,2},{2,0},{1,5},{5,9},... | collective-permute-start | bytes 393224 | tf_op jit(solution)/shard_map/ppermute | solution.py:46
  36.5 10.5 %collective-permute-start.30 = (bf16[256,256]{1,0:T(8,128)(2,1)S(1)}, bf16[256,256]{1,0:T(8,128)(2,1)S(1)}, u32[]{:S(2)}, u32[]{:S(2)}) collective-permute-start(bf16[256,256]{1,0:T(8,128)(2,1)S(1)} %get-tuple-element.58), channel_id=1, source_target_pairs={{0,2},{4,0},{8,4},{12,8},{14,12},{10,14},{6,10},{2,6},{1,3},{5,1},... | collective-permute-start | bytes 393224 | tf_op jit(solution)/shard_map/ppermute | solution.py:46
  38.5 6.4 %collective-permute-start.20 = (bf16[256,256]{1,0:T(8,128)(2,1)S(1)}, bf16[256,256]{1,0:T(8,128)(2,1)S(1)}, u32[]{:S(2)}, u32[]{:S(2)}) collective-permute-start(bf16[256,256]{1,0:T(8,128)(2,1)S(1)} %get-tuple-element.50), channel_id=1, source_target_pairs={{0,2},{4,0},{8,4},{12,8},{14,12},{10,14},{6,10},{2,6},{1,3},{5,1},... | collective-permute-start | bytes 393224 | tf_op jit(solution)/shard_map/ppermute | solution.py:46
  40.1 6.3 %collective-permute-start.27 = (bf16[256,256]{1,0:T(8,128)(2,1)S(1)}, bf16[256,256]{1,0:T(8,128)(2,1)S(1)}, u32[]{:S(2)}, u32[]{:S(2)}) collective-permute-start(bf16[256,256]{1,0:T(8,128)(2,1)S(1)} %get-tuple-element.54), channel_id=1, source_target_pairs={{0,4},{4,8},{8,12},{12,14},{14,10},{10,6},{6,2},{2,0},{1,5},{5,9},... | collective-permute-start | bytes 393224 | tf_op jit(solution)/shard_map/ppermute | solution.py:46
  41.0 7.7 %collective-permute-start.17 = (bf16[256,256]{1,0:T(8,128)(2,1)S(1)}, bf16[256,256]{1,0:T(8,128)(2,1)S(1)}, u32[]{:S(2)}, u32[]{:S(2)}) collective-permute-start(bf16[256,256]{1,0:T(8,128)(2,1)S(1)} %add_convert_fusion.9), channel_id=1, source_target_pairs={{0,4},{4,8},{8,12},{12,14},{14,10},{10,6},{6,2},{2,0},{1,5},{5,9},... | collective-permute-start | bytes 393224 | tf_op jit(solution)/shard_map/ppermute | solution.py:46
  44.9 6.4 %collective-permute-start.21 = (bf16[256,256]{1,0:T(8,128)(2,1)S(1)}, bf16[256,256]{1,0:T(8,128)(2,1)S(1)}, u32[]{:S(2)}, u32[]{:S(2)}) collective-permute-start(bf16[256,256]{1,0:T(8,128)(2,1)S(1)} %add_convert_fusion.6), channel_id=1, source_target_pairs={{0,2},{4,0},{8,4},{12,8},{14,12},{10,14},{6,10},{2,6},{1,3},{5,1},... | collective-permute-start | bytes 393224 | tf_op jit(solution)/shard_map/ppermute | solution.py:46
  47.1 7.0 %collective-permute-start.31 = (bf16[256,256]{1,0:T(8,128)(2,1)S(1)}, bf16[256,256]{1,0:T(8,128)(2,1)S(1)}, u32[]{:S(2)}, u32[]{:S(2)}) collective-permute-start(bf16[256,256]{1,0:T(8,128)(2,1)S(1)} %add_convert_fusion.2), channel_id=1, source_target_pairs={{0,2},{4,0},{8,4},{12,8},{14,12},{10,14},{6,10},{2,6},{1,3},{5,1},... | collective-permute-start | bytes 393224 | tf_op jit(solution)/shard_map/ppermute | solution.py:46
  48.7 6.4 %collective-permute-start.18 = (bf16[256,256]{1,0:T(8,128)(2,1)S(1)}, bf16[256,256]{1,0:T(8,128)(2,1)S(1)}, u32[]{:S(2)}, u32[]{:S(2)}) collective-permute-start(bf16[256,256]{1,0:T(8,128)(2,1)S(1)} %add_convert_fusion.8), channel_id=1, source_target_pairs={{0,4},{4,8},{8,12},{12,14},{14,10},{10,6},{6,2},{2,0},{1,5},{5,9},... | collective-permute-start | bytes 393224 | tf_op jit(solution)/shard_map/ppermute | solution.py:46
  51.4 9.2 %collective-permute-start.22 = (bf16[256,256]{1,0:T(8,128)(2,1)S(1)}, bf16[256,256]{1,0:T(8,128)(2,1)S(1)}, u32[]{:S(2)}, u32[]{:S(2)}) collective-permute-start(bf16[256,256]{1,0:T(8,128)(2,1)S(1)} %add_convert_fusion.5), channel_id=1, source_target_pairs={{0,2},{4,0},{8,4},{12,8},{14,12},{10,14},{6,10},{2,6},{1,3},{5,1},... | collective-permute-start | bytes 393224 | tf_op jit(solution)/shard_map/ppermute | solution.py:46
  52.2 10.1 %collective-permute-start.29 = (bf16[256,256]{1,0:T(8,128)(2,1)S(1)}, bf16[256,256]{1,0:T(8,128)(2,1)S(1)}, u32[]{:S(2)}, u32[]{:S(2)}) collective-permute-start(bf16[256,256]{1,0:T(8,128)(2,1)S(1)} %add_convert_fusion.3), channel_id=1, source_target_pairs={{0,4},{4,8},{8,12},{12,14},{14,10},{10,6},{6,2},{2,0},{1,5},{5,9},... | collective-permute-start | bytes 393224 | tf_op jit(solution)/shard_map/ppermute | solution.py:46
  55.2 5.7 %collective-permute-start.19 = (bf16[256,256]{1,0:T(8,128)(2,1)S(1)}, bf16[256,256]{1,0:T(8,128)(2,1)S(1)}, u32[]{:S(2)}, u32[]{:S(2)}) collective-permute-start(bf16[256,256]{1,0:T(8,128)(2,1)S(1)} %add_convert_fusion.7), channel_id=1, source_target_pairs={{0,4},{4,8},{8,12},{12,14},{14,10},{10,6},{6,2},{2,0},{1,5},{5,9},... | collective-permute-start | bytes 393224 | tf_op jit(solution)/shard_map/ppermute | solution.py:46
  59.8 6.4 %collective-permute-start.33 = (bf16[256,256]{1,0:T(8,128)(2,1)S(1)}, bf16[256,256]{1,0:T(8,128)(2,1)S(1)}, u32[]{:S(2)}, u32[]{:S(2)}) collective-permute-start(bf16[256,256]{1,0:T(8,128)(2,1)S(1)} %add_convert_fusion), channel_id=1, source_target_pairs={{0,2},{4,0},{8,4},{12,8},{14,12},{10,14},{6,10},{2,6},{1,3},{5,1},... | collective-permute-start | bytes 393224 | tf_op jit(solution)/shard_map/ppermute | solution.py:46
  60.9 8.2 %collective-permute-start.23 = (bf16[256,256]{1,0:T(8,128)(2,1)S(1)}, bf16[256,256]{1,0:T(8,128)(2,1)S(1)}, u32[]{:S(2)}, u32[]{:S(2)}) collective-permute-start(bf16[256,256]{1,0:T(8,128)(2,1)S(1)} %fusion.1.refs_0_), channel_id=1, source_target_pairs={{0,4},{4,8},{8,12},{12,14},{14,10},{10,6},{6,2},{2,0},{1,5},{5,9},... | collective-permute-start | bytes 393224 | tf_op jit(solution)/shard_map/ppermute | solution.py:46
  66.3 6.4 %collective-permute-start.34 = (bf16[256,256]{1,0:T(8,128)(2,1)S(1)}, bf16[256,256]{1,0:T(8,128)(2,1)S(1)}, u32[]{:S(2)}, u32[]{:S(2)}) collective-permute-start(bf16[256,256]{1,0:T(8,128)(2,1)S(1)} %multiply_convert_fusion.refs_1_), channel_id=1, source_target_pairs={{0,2},{4,0},{8,4},{12,8},{14,12},{10,14},{6,10},{2,6},{1,3},{5,1},... | collective-permute-start | bytes 393224 | tf_op jit(solution)/shard_map/ppermute | solution.py:46
  67.1 8.4 %collective-permute-start.39 = (bf16[256,256]{1,0:T(8,128)(2,1)S(1)}, bf16[256,256]{1,0:T(8,128)(2,1)S(1)}, u32[]{:S(2)}, u32[]{:S(2)}) collective-permute-start(bf16[256,256]{1,0:T(8,128)(2,1)S(1)} %fusion.1.refs_0_), channel_id=1, source_target_pairs={{0,2},{4,0},{8,4},{12,8},{14,12},{10,14},{6,10},{2,6},{1,3},{5,1},... | collective-permute-start | bytes 393224 | tf_op jit(solution)/shard_map/ppermute | solution.py:46
  68.6 7.6 %collective-permute-start.38 = (bf16[256,256]{1,0:T(8,128)(2,1)S(1)}, bf16[256,256]{1,0:T(8,128)(2,1)S(1)}, u32[]{:S(2)}, u32[]{:S(2)}) collective-permute-start(bf16[256,256]{1,0:T(8,128)(2,1)S(1)} %multiply_convert_fusion.refs_1_), channel_id=1, source_target_pairs={{0,4},{4,8},{8,12},{12,14},{14,10},{10,6},{6,2},{2,0},{1,5},{5,9},... | collective-permute-start | bytes 393224 | tf_op jit(solution)/shard_map/ppermute | solution.py:46
  69.1 8.4 %collective-permute-start.24 = (bf16[256,256]{1,0:T(8,128)(2,1)S(1)}, bf16[256,256]{1,0:T(8,128)(2,1)S(1)}, u32[]{:S(2)}, u32[]{:S(2)}) collective-permute-start(bf16[256,256]{1,0:T(8,128)(2,1)S(1)} %collective-permute-done.23.refs_2_), channel_id=1, source_target_pairs={{0,4},{4,8},{8,12},{12,14},{14,10},{10,6},{6,2},{2,0},{1,5},{5,9},... | collective-permute-start | bytes 393224 | tf_op jit(solution)/shard_map/ppermute | solution.py:46
  72.7 6.4 %collective-permute-start.35 = (bf16[256,256]{1,0:T(8,128)(2,1)S(1)}, bf16[256,256]{1,0:T(8,128)(2,1)S(1)}, u32[]{:S(2)}, u32[]{:S(2)}) collective-permute-start(bf16[256,256]{1,0:T(8,128)(2,1)S(1)} %collective-permute-done.34.refs_5_), channel_id=1, source_target_pairs={{0,2},{4,0},{8,4},{12,8},{14,12},{10,14},{6,10},{2,6},{1,3},{5,1},... | collective-permute-start | bytes 393224 | tf_op jit(solution)/shard_map/ppermute | solution.py:46
  75.5 6.4 %collective-permute-start.41 = (bf16[256,256]{1,0:T(8,128)(2,1)S(1)}, bf16[256,256]{1,0:T(8,128)(2,1)S(1)}, u32[]{:S(2)}, u32[]{:S(2)}) collective-permute-start(bf16[256,256]{1,0:T(8,128)(2,1)S(1)} %collective-permute-done.39.refs_4_), channel_id=1, source_target_pairs={{0,2},{4,0},{8,4},{12,8},{14,12},{10,14},{6,10},{2,6},{1,3},{5,1},... | collective-permute-start | bytes 393224 | tf_op jit(solution)/shard_map/ppermute | solution.py:46
  76.3 6.2 %collective-permute-start.40 = (bf16[256,256]{1,0:T(8,128)(2,1)S(1)}, bf16[256,256]{1,0:T(8,128)(2,1)S(1)}, u32[]{:S(2)}, u32[]{:S(2)}) collective-permute-start(bf16[256,256]{1,0:T(8,128)(2,1)S(1)} %collective-permute-done.38.refs_3_), channel_id=1, source_target_pairs={{0,4},{4,8},{8,12},{12,14},{14,10},{10,6},{6,2},{2,0},{1,5},{5,9},... | collective-permute-start | bytes 393224 | tf_op jit(solution)/shard_map/ppermute | solution.py:46
  77.5 6.4 %collective-permute-start.25 = (bf16[256,256]{1,0:T(8,128)(2,1)S(1)}, bf16[256,256]{1,0:T(8,128)(2,1)S(1)}, u32[]{:S(2)}, u32[]{:S(2)}) collective-permute-start(bf16[256,256]{1,0:T(8,128)(2,1)S(1)} %collective-permute-done.24.refs_0_), channel_id=1, source_target_pairs={{0,4},{4,8},{8,12},{12,14},{14,10},{10,6},{6,2},{2,0},{1,5},{5,9},... | collective-permute-start | bytes 393224 | tf_op jit(solution)/shard_map/ppermute | solution.py:46
  79.1 6.2 %collective-permute-start.36 = (bf16[256,256]{1,0:T(8,128)(2,1)S(1)}, bf16[256,256]{1,0:T(8,128)(2,1)S(1)}, u32[]{:S(2)}, u32[]{:S(2)}) collective-permute-start(bf16[256,256]{1,0:T(8,128)(2,1)S(1)} %collective-permute-done.35.refs_3_), channel_id=1, source_target_pairs={{0,2},{4,0},{8,4},{12,8},{14,12},{10,14},{6,10},{2,6},{1,3},{5,1},... | collective-permute-start | bytes 393224 | tf_op jit(solution)/shard_map/ppermute | solution.py:46
  (16 other events, 126.0 us)

commit v9 on v8

--- a/solution.py
+++ b/solution.py
@@ -72,13 +72,13 @@
     return pl.ds(pl.multiple_of(starts[slot], wide), wide)
 
 
-def encode_kernel(slots, last, starts, *refs):
+def encode_kernel(slots, first, last, starts, *refs):
     count = 2 * len(slots)
     shards, (weight, before, *outs) = refs[:count], refs[count:]
     rows, wide = shards[0].shape
     for chain in range(2):
         at = slice(chain * rows, (chain + 1) * rows)
-        total = before[at, :] if last else jnp.broadcast_to(before[...], (rows, before.shape[1]))
+        total = jnp.broadcast_to(before[...], (rows, before.shape[1])) if first else before[at, :]
         for i, slot in enumerate(slots):
             block = weight[0, block_of(starts, slot, wide), :]
             total = total + jnp.dot(shards[2 * i + chain][...], block, preferred_element_type=F32)
@@ -230,41 +230,38 @@
     starts = jnp.stack([ring_member(place + offset, size) * wide for offset in offsets] + [layer])
     starts = starts.astype(jnp.int32)
 
+    urgent, later = ((0, 1), (1, -1)), ((0, -1), (1, 1))
+
     def gather_step(found, s, ready=None):
-        for chain in chains:
-            at_p, at_q = (0, 0) if s == 1 else (slot_p[s - 1], slot_q[s - 1])
-            if s < reach:
-                ahead, behind = found[chain][at_p], found[chain][at_q]
-                if ready is not None:
-                    ahead, behind = (after(ahead, ready), behind) if chain else (ahead, after(behind, ready))
-                found[chain][slot_p[s]], found[chain][slot_q[s]] = hop(ahead, 1), hop(behind, -1)
-            else:
-                found[chain][far] = hop(found[chain][at_q if chain else at_p], -1 if chain else 1)
-
-    inputs = [[part] + [None] * (size - 1) for part in halves(residual_in[0])]
-    low_cross = passed_along(after(dec_cross, inputs[0][0]), "layer", 1)
-    stacked = jnp.concatenate([dec_same[0], jnp.concatenate([low_cross, dec_cross], axis=1)], axis=0)
-    for s in range(1, reach + 1):
-        if s == reach and reach > 1:
-            inputs[0][slot_p[s - 1]] = after(inputs[0][slot_p[s - 1]], stacked)
-        gather_step(inputs, s, low_cross if s == 1 else None)
+        for chain, way in urgent + later if s < reach else urgent:
+            slots = slot_p if way == 1 else slot_q
+            shard = found[chain][slots[s - 1] if s > 1 else 0]
+            if ready is not None and (chain, way) in later:
+                shard = after(shard, ready)
+            found[chain][slots[s] if s < reach else far] = hop(shard, way)
 
     def both_chains(found, slots):
         return [found[chain][slot] for slot in slots for chain in chains]
 
-    early = tuple(range(size - 1))
-    part = call(
-        functools.partial(encode_kernel, early, False),
-        [shape((rows, lat), F32)],
-        2 * unit * len(early),
-        [starts] + both_chains(inputs, early) + [enc_weight, enc_bias],
-    )[0]
-    preact, codes = call(
-        functools.partial(encode_kernel, (far,), True),
-        [shape((rows, lat), F32), shape((rows, lat), BF16)],
-        2 * unit,
-        [starts] + both_chains(inputs, (far,)) + [enc_weight, part],
-    )
+    def encode(slots, before):
+        first, last = slots[0] == 0, slots[-1] == far
+        return call(
+            functools.partial(encode_kernel, slots, first, last),
+            [shape((rows, lat), F32)] + ([shape((rows, lat), BF16)] if last else []),
+            2 * unit * len(slots),
+            [starts] + both_chains(inputs, slots) + [enc_weight, before],
+        )
+
+    front = residual_in[0, :half]
+    inputs = [[front] + [None] * (size - 1), [after(residual_in, front)[0, half:]] + [None] * (size - 1)]
+    part = encode((0,), enc_bias)[0]
+    for s in range(1, reach + 1):
+        gather_step(inputs, s, part if s == 1 else None)
+    low_cross = passed_along(after(dec_cross, inputs[0][slot_p.get(1, far)]), "layer", 1)
+    stacked = jnp.concatenate([dec_same[0], jnp.concatenate([low_cross, dec_cross], axis=1)], axis=0)
+    if size > 2:
+        part = encode(tuple(range(1, far)), after(part, stacked))[0]
+    preact, codes = encode((far,), part)
     earlier = passed_along(codes, "layer", 1)
 
     def spread(slots, dtypes, turned):
@@ -280,26 +277,28 @@
     rest = tuple(slot for slot in range(size) if slot != far)
     instant = ({far: BF16, slot_p.get(reach - 1): BF16}, {far: BF16, slot_q.get(reach - 1): BF16})
     far_0, far_1 = spread((far,), instant, False)
-    ahead, behind = [hop(far_0[0], 1), None], [None, hop(far_1[0], -1)]
+    moving = {(0, 1): hop(far_0[0], 1), (1, -1): hop(far_1[0], -1)}
     partial, both_t = [], []
     for pieces in spread(rest, instant, True):
         partial.append(dict(zip(rest, pieces)))
         both_t.append(pieces[-1])
+    before = []
     for s in range(reach - 1, 0, -1):
-        for chain in chains:
-            plus, minus = partial[chain][slot_q[s]], partial[chain][slot_p[s]]
-            if ahead[chain] is not None:
-                plus = (plus + ahead[chain].astype(F32)).astype(BF16)
-            if behind[chain] is not None:
-                minus = (minus + behind[chain].astype(F32)).astype(BF16)
-            ahead[chain] = hop(plus, 1)
-            behind[chain] = hop(minus, -1)
+        landed = [moving[loop] for loop in urgent]
+        for chain, way in urgent + later:
+            message = partial[chain][slot_q[s] if way == 1 else slot_p[s]]
+            if (chain, way) in moving:
+                message = (message + moving[chain, way].astype(F32)).astype(BF16)
+            if (chain, way) in later and before:
+                message = after(message, *before)
+            moving[chain, way] = hop(message, way)
+        before = landed
     errors = []
     for chain, wanted in zip(chains, halves(targets[0])):
         total = partial[chain][0]
-        for arrived in (ahead[chain], behind[chain]):
-            if arrived is not None:
-                total = total + arrived.astype(F32)
+        for way in (1, -1):
+            if (chain, way) in moving:
+                total = total + moving[chain, way].astype(F32)
         if chain == 1:
             wanted = after(wanted, errors[0][0])
         errors.append([((total - wanted.astype(F32)) * err_scale).astype(BF16)] + [None] * (size - 1))

time: 98.8 us -> 93.1 us (0.942)
  waiting for transfers between devices: 34.8 us -> 25.5 us
  local copies, waits for them, and re-layouts: 1.15 us -> 3.7 us
  starting transfers between devices: 47.8 us -> 48.8 us
    ppermute x42, waiting for transfers between devices: 32.5 us -> 22.8 us  [hop(): lax.ppermute(shard, 'latent', [(order[p], order[(p + way) % size]) for p...]
    ppermute x42, starting transfers between devices: 42.9 us -> 44.9 us  [hop(): lax.ppermute(shard, 'latent', [(order[p], order[(p + way) % size]) for p...]
    squeeze x0 -> x2, local copies, waits for them, and re-layouts: none -> 1.89 us  [the longest x1 0.97 us: ring_shards(): front = residual_in[0, :half]]
    unnamed x6 -> x8, local copies, waits for them, and re-layouts: 0.01 us -> 1.71 us
    ppermute x3, starting transfers between devices: 4.96 us -> 3.89 us  [passed_along(): return lax.ppermute(shard, axis, pairs)]
    slice x2 -> x1, local copies, waits for them, and re-layouts: 1.05 us -> 0.01 us  [halves(): return [array[:half], array[half:]]]
    pallas_call x9 -> x10, Pallas kernels: 12.3 us -> 12.3 us  [call(): pl.pallas_call(kernel, out_shape=outs, in_specs=[spec(pltpu.SMEM)] + [spe...]
  transfers between devices with their start and end apart: 45 -> 45, of which waited for: 23 -> 24; matrix products, arithmetic and copies ran while one was open for 2% -> 2% of each run, Pallas kernels for 6% -> 7%
where the time goes in v9:
time: 93.1 us; the launch traced here: 92.8 us
  starting transfers between devices  48.8 us (52%)
  waiting for transfers between devices  25.5 us (27%)
  Pallas kernels  12.3 us (13%)
  local copies, waits for them, and re-layouts  3.7 us (4%)
  other arithmetic  1.63 us (2%)
    ppermute x42, starting transfers between devices, hop(): lax.ppermute(shard, 'latent', [(order[p], order[(p + way) % size]) for p...  44.9 us
    ppermute x42, waiting for transfers between devices, hop(): lax.ppermute(shard, 'latent', [(order[p], order[(p + way) % size]) for p...  22.8 us
    pallas_call x10, Pallas kernels, call(): pl.pallas_call(kernel, out_shape=outs, in_specs=[spec(pltpu.SMEM)] + [spe...  12.3 us
    ppermute x3, starting transfers between devices, passed_along(): return lax.ppermute(shard, axis, pairs)  3.89 us
    ppermute x3, waiting for transfers between devices, passed_along(): return lax.ppermute(shard, axis, pairs)  2.7 us
  transfers between devices with their start and end apart: 45, of which 24 were waited for; matrix products, arithmetic and copies ran while one was open for 2% of the time, Pallas kernels for 7%

profile of v9, /device:TPU:0, one launch (start us, length us, event | category | flops | bytes accessed | tf_op | source)
XLA Modules:
  0.0 92.8 jit_solution(12660508084873739865)
XLA Ops:
  2.5 3.0 %collective-permute-start.3 = (bf16[256,256]{1,0:T(8,128)(2,1)S(1)}, bf16[256,256]{1,0:T(8,128)(2,1)S(1)}, u32[]{:S(2)}, u32[]{:S(2)}) collective-permute-start(bf16[256,256]{1,0:T(8,128)(2,1)S(1)} %slice_bitcast_fusion.1.refs_1_), channel_id=1, source_target_pairs={{0,2},{4,0},{8,4},{12,8},{14,12},{10,14},{6,10},{2,6},{1,3},{5,1},... | collective-permute-start | bytes 393224 | tf_op jit(solution)/shard_map/ppermute | solution.py:46
  8.2 2.0 %collective-permute-start.1 = (bf16[256,256]{1,0:T(8,128)(2,1)S(1)}, bf16[256,256]{1,0:T(8,128)(2,1)S(1)}, u32[]{:S(2)}, u32[]{:S(2)}) collective-permute-start(bf16[256,256]{1,0:T(8,128)(2,1)S(1)} %slice_bitcast_fusion.1.refs_1_), channel_id=1, source_target_pairs={{0,4},{4,8},{8,12},{12,14},{14,10},{10,6},{6,2},{2,0},{1,5},{5,9},... | collective-permute-start | bytes 393224 | tf_op jit(solution)/shard_map/ppermute | solution.py:46
  10.3 1.9 %collective-permute-start.7 = (bf16[256,256]{1,0:T(8,128)(2,1)S(1)}, bf16[256,256]{1,0:T(8,128)(2,1)S(1)}, u32[]{:S(2)}, u32[]{:S(2)}) collective-permute-start(bf16[256,256]{1,0:T(8,128)(2,1)S(1)} %collective-permute-done.3.refs_5_.refs_3_), channel_id=1, source_target_pairs={{0,2},{4,0},{8,4},{12,8},{14,12},{10,14},{6,10},{2,6},{1,3},{5,1},... | collective-permute-start | bytes 393224 | tf_op jit(solution)/shard_map/ppermute | solution.py:46
  12.3 1.3 %collective-permute-start.14 = (bf16[128,1024]{1,0:T(8,128)(2,1)}, bf16[128,1024]{1,0:T(8,128)(2,1)S(1)}, u32[]{:S(2)}, u32[]{:S(2)}) collective-permute-start(bf16[128,1024]{1,0:T(8,128)(2,1)} %param.11), channel_id=1, source_target_pairs={{0,1},{2,3},{4,5},{6,7},{8,9},{10,11},{12,13},{14,15},{16,17},{18,... | collective-permute-start | bytes 786440 | tf_op jit(solution)/shard_map/ppermute | solution.py:23
  14.0 2.5 %collective-permute-start.5 = (bf16[256,256]{1,0:T(8,128)(2,1)S(1)}, bf16[256,256]{1,0:T(8,128)(2,1)S(1)}, u32[]{:S(2)}, u32[]{:S(2)}) collective-permute-start(bf16[256,256]{1,0:T(8,128)(2,1)S(1)} %collective-permute-done.1.refs_3_.refs_1_), channel_id=1, source_target_pairs={{0,4},{4,8},{8,12},{12,14},{14,10},{10,6},{6,2},{2,0},{1,5},{5,9},... | collective-permute-start | bytes 393224 | tf_op jit(solution)/shard_map/ppermute | solution.py:46
  16.5 2.2 %collective-permute-done.7.refs_9_.refs_7_ = bf16[256,256]{1,0:T(8,128)(2,1)S(1)} collective-permute-done((bf16[256,256]{1,0:T(8,128)(2,1)S(1)}, bf16[256,256]{1,0:T(8,128)(2,1)S(1)}, u32[]{:S(2)}, u32[]{:S(2)}) %collective-permute-start.7) | collective-permute-done | bytes 131104 | tf_op jit(solution)/shard_map/ppermute | solution.py:46
  19.1 1.7 %collective-permute-start.8 = (bf16[256,256]{1,0:T(8,128)(2,1)S(1)}, bf16[256,256]{1,0:T(8,128)(2,1)S(1)}, u32[]{:S(2)}, u32[]{:S(2)}) collective-permute-start(bf16[256,256]{1,0:T(8,128)(2,1)S(1)} %collective-permute-done.4.refs_6_.refs_4_), channel_id=1, source_target_pairs={{0,4},{4,8},{8,12},{12,14},{14,10},{10,6},{6,2},{2,0},{1,5},{5,9},... | collective-permute-start | bytes 393224 | tf_op jit(solution)/shard_map/ppermute | solution.py:46
  20.7 2.1 %collective-permute-start.9 = (bf16[256,256]{1,0:T(8,128)(2,1)S(1)}, bf16[256,256]{1,0:T(8,128)(2,1)S(1)}, u32[]{:S(2)}, u32[]{:S(2)}) collective-permute-start(bf16[256,256]{1,0:T(8,128)(2,1)S(1)} %collective-permute-done.5.refs_7_.refs_5_), channel_id=1, source_target_pairs={{0,4},{4,8},{8,12},{12,14},{14,10},{10,6},{6,2},{2,0},{1,5},{5,9},... | collective-permute-start | bytes 393224 | tf_op jit(solution)/shard_map/ppermute | solution.py:46
  22.8 2.2 %collective-permute-done.11.refs_13_.refs_11_ = bf16[256,256]{1,0:T(8,128)(2,1)S(1)} collective-permute-done((bf16[256,256]{1,0:T(8,128)(2,1)S(1)}, bf16[256,256]{1,0:T(8,128)(2,1)S(1)}, u32[]{:S(2)}, u32[]{:S(2)}) %collective-permute-start.11) | collective-permute-done | bytes 131104 | tf_op jit(solution)/shard_map/ppermute | solution.py:46
  25.4 1.7 %collective-permute-start.12 = (bf16[256,256]{1,0:T(8,128)(2,1)S(1)}, bf16[256,256]{1,0:T(8,128)(2,1)S(1)}, u32[]{:S(2)}, u32[]{:S(2)}) collective-permute-start(bf16[256,256]{1,0:T(8,128)(2,1)S(1)} %collective-permute-done.8.refs_10_.refs_8_), channel_id=1, source_target_pairs={{0,4},{4,8},{8,12},{12,14},{14,10},{10,6},{6,2},{2,0},{1,5},{5,9},... | collective-permute-start | bytes 393224 | tf_op jit(solution)/shard_map/ppermute | solution.py:46
  31.1 1.3 %collective-permute-start.15 = (bf16[512,128]{1,0:T(8,128)(2,1)S(1)}, bf16[512,128]{1,0:T(8,128)(2,1)S(1)}, u32[]{:S(2)}, u32[]{:S(2)}) collective-permute-start(bf16[512,128]{1,0:T(8,128)(2,1)S(1)} %get-tuple-element.48.codes), channel_id=1, source_target_pairs={{0,1},{2,3},{4,5},{6,7},{8,9},{10,11},{12,13},{14,15},{16,17},{18,... | collective-permute-start | bytes 393224 | tf_op jit(solution)/shard_map/ppermute | solution.py:23
  34.2 1.7 %collective-permute-start.21 = (bf16[256,256]{1,0:T(8,128)(2,1)S(1)}, bf16[256,256]{1,0:T(8,128)(2,1)S(1)}, u32[]{:S(2)}, u32[]{:S(2)}) collective-permute-start(bf16[256,256]{1,0:T(8,128)(2,1)S(1)} %get-tuple-element.57), channel_id=1, source_target_pairs={{0,2},{4,0},{8,4},{12,8},{14,12},{10,14},{6,10},{2,6},{1,3},{5,1},... | collective-permute-start | bytes 393224 | tf_op jit(solution)/shard_map/ppermute | solution.py:46
  37.5 1.6 %collective-permute-start.20 = (bf16[256,256]{1,0:T(8,128)(2,1)S(1)}, bf16[256,256]{1,0:T(8,128)(2,1)S(1)}, u32[]{:S(2)}, u32[]{:S(2)}) collective-permute-start(bf16[256,256]{1,0:T(8,128)(2,1)S(1)} %get-tuple-element.56), channel_id=1, source_target_pairs={{0,2},{4,0},{8,4},{12,8},{14,12},{10,14},{6,10},{2,6},{1,3},{5,1},... | collective-permute-start | bytes 393224 | tf_op jit(solution)/shard_map/ppermute | solution.py:46
  40.0 1.7 %collective-permute-start.23 = (bf16[256,256]{1,0:T(8,128)(2,1)S(1)}, bf16[256,256]{1,0:T(8,128)(2,1)S(1)}, u32[]{:S(2)}, u32[]{:S(2)}) collective-permute-start(bf16[256,256]{1,0:T(8,128)(2,1)S(1)} %add_convert_fusion.4), channel_id=1, source_target_pairs={{0,2},{4,0},{8,4},{12,8},{14,12},{10,14},{6,10},{2,6},{1,3},{5,1},... | collective-permute-start | bytes 393224 | tf_op jit(solution)/shard_map/ppermute | solution.py:46
  43.4 1.7 %collective-permute-start.22 = (bf16[256,256]{1,0:T(8,128)(2,1)S(1)}, bf16[256,256]{1,0:T(8,128)(2,1)S(1)}, u32[]{:S(2)}, u32[]{:S(2)}) collective-permute-start(bf16[256,256]{1,0:T(8,128)(2,1)S(1)} %add_convert_fusion.6), channel_id=1, source_target_pairs={{0,2},{4,0},{8,4},{12,8},{14,12},{10,14},{6,10},{2,6},{1,3},{5,1},... | collective-permute-start | bytes 393224 | tf_op jit(solution)/shard_map/ppermute | solution.py:46
  46.5 1.7 %collective-permute-start.32 = (bf16[256,256]{1,0:T(8,128)(2,1)S(1)}, bf16[256,256]{1,0:T(8,128)(2,1)S(1)}, u32[]{:S(2)}, u32[]{:S(2)}) collective-permute-start(bf16[256,256]{1,0:T(8,128)(2,1)S(1)} %add_convert_fusion.1), channel_id=1, source_target_pairs={{0,2},{4,0},{8,4},{12,8},{14,12},{10,14},{6,10},{2,6},{1,3},{5,1},... | collective-permute-start | bytes 393224 | tf_op jit(solution)/shard_map/ppermute | solution.py:46
  49.4 1.7 %collective-permute-start.24 = (bf16[256,256]{1,0:T(8,128)(2,1)S(1)}, bf16[256,256]{1,0:T(8,128)(2,1)S(1)}, u32[]{:S(2)}, u32[]{:S(2)}) collective-permute-start(bf16[256,256]{1,0:T(8,128)(2,1)S(1)} %add_convert_fusion.5), channel_id=1, source_target_pairs={{0,2},{4,0},{8,4},{12,8},{14,12},{10,14},{6,10},{2,6},{1,3},{5,1},... | collective-permute-start | bytes 393224 | tf_op jit(solution)/shard_map/ppermute | solution.py:46
  51.8 2.5 %collective-permute-done.18 = bf16[256,256]{1,0:T(8,128)(2,1)S(1)} collective-permute-done((bf16[256,256]{1,0:T(8,128)(2,1)S(1)}, bf16[256,256]{1,0:T(8,128)(2,1)S(1)}, u32[]{:S(2)}, u32[]{:S(2)}) %collective-permute-start.18) | collective-permute-done | bytes 131104 | tf_op jit(solution)/shard_map/ppermute | solution.py:46
  54.9 1.7 %collective-permute-start.33 = (bf16[256,256]{1,0:T(8,128)(2,1)S(1)}, bf16[256,256]{1,0:T(8,128)(2,1)S(1)}, u32[]{:S(2)}, u32[]{:S(2)}) collective-permute-start(bf16[256,256]{1,0:T(8,128)(2,1)S(1)} %add_convert_fusion), channel_id=1, source_target_pairs={{0,2},{4,0},{8,4},{12,8},{14,12},{10,14},{6,10},{2,6},{1,3},{5,1},... | collective-permute-start | bytes 393224 | tf_op jit(solution)/shard_map/ppermute | solution.py:46
  56.5 2.9 %collective-permute-done.19 = bf16[256,256]{1,0:T(8,128)(2,1)S(1)} collective-permute-done((bf16[256,256]{1,0:T(8,128)(2,1)S(1)}, bf16[256,256]{1,0:T(8,128)(2,1)S(1)}, u32[]{:S(2)}, u32[]{:S(2)}) %collective-permute-start.19) | collective-permute-done | bytes 131104 | tf_op jit(solution)/shard_map/ppermute | solution.py:46
  60.2 1.7 %collective-permute-start.34 = (bf16[256,256]{1,0:T(8,128)(2,1)S(1)}, bf16[256,256]{1,0:T(8,128)(2,1)S(1)}, u32[]{:S(2)}, u32[]{:S(2)}) collective-permute-start(bf16[256,256]{1,0:T(8,128)(2,1)S(1)} %multiply_convert_fusion.refs_1_), channel_id=1, source_target_pairs={{0,2},{4,0},{8,4},{12,8},{14,12},{10,14},{6,10},{2,6},{1,3},{5,1},... | collective-permute-start | bytes 393224 | tf_op jit(solution)/shard_map/ppermute | solution.py:46
  61.8 1.6 %collective-permute-start.39 = (bf16[256,256]{1,0:T(8,128)(2,1)S(1)}, bf16[256,256]{1,0:T(8,128)(2,1)S(1)}, u32[]{:S(2)}, u32[]{:S(2)}) collective-permute-start(bf16[256,256]{1,0:T(8,128)(2,1)S(1)} %fusion.1.refs_0_), channel_id=1, source_target_pairs={{0,2},{4,0},{8,4},{12,8},{14,12},{10,14},{6,10},{2,6},{1,3},{5,1},... | collective-permute-start | bytes 393224 | tf_op jit(solution)/shard_map/ppermute | solution.py:46
  63.8 2.0 %collective-permute-done.25.refs_2_ = bf16[256,256]{1,0:T(8,128)(2,1)S(1)} collective-permute-done((bf16[256,256]{1,0:T(8,128)(2,1)S(1)}, bf16[256,256]{1,0:T(8,128)(2,1)S(1)}, u32[]{:S(2)}, u32[]{:S(2)}) %collective-permute-start.25) | collective-permute-done | bytes 131104 | tf_op jit(solution)/shard_map/ppermute | solution.py:46
  66.6 1.6 %collective-permute-start.35 = (bf16[256,256]{1,0:T(8,128)(2,1)S(1)}, bf16[256,256]{1,0:T(8,128)(2,1)S(1)}, u32[]{:S(2)}, u32[]{:S(2)}) collective-permute-start(bf16[256,256]{1,0:T(8,128)(2,1)S(1)} %collective-permute-done.34.refs_5_), channel_id=1, source_target_pairs={{0,2},{4,0},{8,4},{12,8},{14,12},{10,14},{6,10},{2,6},{1,3},{5,1},... | collective-permute-start | bytes 393224 | tf_op jit(solution)/shard_map/ppermute | solution.py:46
  69.3 1.6 %collective-permute-start.41 = (bf16[256,256]{1,0:T(8,128)(2,1)S(1)}, bf16[256,256]{1,0:T(8,128)(2,1)S(1)}, u32[]{:S(2)}, u32[]{:S(2)}) collective-permute-start(bf16[256,256]{1,0:T(8,128)(2,1)S(1)} %collective-permute-done.39.refs_4_), channel_id=1, source_target_pairs={{0,2},{4,0},{8,4},{12,8},{14,12},{10,14},{6,10},{2,6},{1,3},{5,1},... | collective-permute-start | bytes 393224 | tf_op jit(solution)/shard_map/ppermute | solution.py:46
  73.1 1.4 %collective-permute-start.36 = (bf16[256,256]{1,0:T(8,128)(2,1)S(1)}, bf16[256,256]{1,0:T(8,128)(2,1)S(1)}, u32[]{:S(2)}, u32[]{:S(2)}) collective-permute-start(bf16[256,256]{1,0:T(8,128)(2,1)S(1)} %collective-permute-done.35.refs_3_), channel_id=1, source_target_pairs={{0,2},{4,0},{8,4},{12,8},{14,12},{10,14},{6,10},{2,6},{1,3},{5,1},... | collective-permute-start | bytes 393224 | tf_op jit(solution)/shard_map/ppermute | solution.py:46
  75.0 1.6 %collective-permute-start.43 = (bf16[256,256]{1,0:T(8,128)(2,1)S(1)}, bf16[256,256]{1,0:T(8,128)(2,1)S(1)}, u32[]{:S(2)}, u32[]{:S(2)}) collective-permute-start(bf16[256,256]{1,0:T(8,128)(2,1)S(1)} %collective-permute-done.41.refs_2_), channel_id=1, source_target_pairs={{0,2},{4,0},{8,4},{12,8},{14,12},{10,14},{6,10},{2,6},{1,3},{5,1},... | collective-permute-start | bytes 393224 | tf_op jit(solution)/shard_map/ppermute | solution.py:46
  77.3 1.6 %collective-permute-done.27.refs_4_ = bf16[256,256]{1,0:T(8,128)(2,1)S(1)} collective-permute-done((bf16[256,256]{1,0:T(8,128)(2,1)S(1)}, bf16[256,256]{1,0:T(8,128)(2,1)S(1)}, u32[]{:S(2)}, u32[]{:S(2)}) %collective-permute-start.27) | collective-permute-done | bytes 131104 | tf_op jit(solution)/shard_map/ppermute | solution.py:46
  79.5 1.4 %collective-permute-start.37 = (bf16[256,256]{1,0:T(8,128)(2,1)S(1)}, bf16[256,256]{1,0:T(8,128)(2,1)S(1)}, u32[]{:S(2)}, u32[]{:S(2)}) collective-permute-start(bf16[256,256]{1,0:T(8,128)(2,1)S(1)} %collective-permute-done.36.refs_7_), channel_id=1, source_target_pairs={{0,2},{4,0},{8,4},{12,8},{14,12},{10,14},{6,10},{2,6},{1,3},{5,1},... | collective-permute-start | bytes 393224 | tf_op jit(solution)/shard_map/ppermute | solution.py:46
  85.5 1.3 %collective-permute-start.44 = (f32[1536,128]{1,0:T(8,128)S(1)}, f32[1536,128]{1,0:T(8,128)S(1)}, u32[]{:S(2)}, u32[]{:S(2)}) collective-permute-start(f32[1536,128]{1,0:T(8,128)S(1)} %get-tuple-element.77), channel_id=1, source_target_pairs={{1,0},{3,2},{5,4},{7,6},{9,8},{11,10},{13,12},{15,14},{17,16},{19,... | collective-permute-start | bytes 2359304 | tf_op jit(solution)/shard_map/ppermute | solution.py:23
  87.9 1.7 %collective-permute-done.44.refs_3_ = f32[1536,128]{1,0:T(8,128)S(1)} collective-permute-done((f32[1536,128]{1,0:T(8,128)S(1)}, f32[1536,128]{1,0:T(8,128)S(1)}, u32[]{:S(2)}, u32[]{:S(2)}) %collective-permute-start.44) | collective-permute-done | bytes 786464 | tf_op jit(solution)/shard_map/ppermute | solution.py:23
  89.7 3.1 %shard_map.102 = (f32[1,2048,128]{2,1,0:T(8,128)}, f32[1,128]{1,0:T(1,128)}, f32[1,128,2048]{2,1,0:T(8,128)}, f32[128,1024]{1,0:T(8,128)}) custom-call(s32[9]{0:T(128)S(1)} %stack.39.starts, bf16[2048,512]{1,0:T(8,128)(2,1)S(1)} %shard_map.94.refs_0_, f32[512,128]{1,0:T(8,128)S(1)} %get-tuple-element.47.refs_1_, f32[512,128]{1,0:T(8,128)S(1)} %get-tuple-element.76.refs_2_, ...), custom_call_target="tpu_custom_call" | custom-call | flops 268435456 | bytes 1024 | tf_op jit(solution)/shard_map/pallas_call | solution.py:59
  (93 shorter events, 32.6 us)
Async XLA Ops:
  2.5 7.8 %collective-permute-start.3 = (bf16[256,256]{1,0:T(8,128)(2,1)S(1)}, bf16[256,256]{1,0:T(8,128)(2,1)S(1)}, u32[]{:S(2)}, u32[]{:S(2)}) collective-permute-start(bf16[256,256]{1,0:T(8,128)(2,1)S(1)} %slice_bitcast_fusion.1.refs_1_), channel_id=1, source_target_pairs={{0,2},{4,0},{8,4},{12,8},{14,12},{10,14},{6,10},{2,6},{1,3},{5,1},... | collective-permute-start | bytes 393224 | tf_op jit(solution)/shard_map/ppermute | solution.py:46
  5.5 6.7 %collective-permute-start = (bf16[256,256]{1,0:T(8,128)(2,1)S(1)}, bf16[256,256]{1,0:T(8,128)(2,1)S(1)}, u32[]{:S(2)}, u32[]{:S(2)}) collective-permute-start(bf16[256,256]{1,0:T(8,128)(2,1)S(1)} %slice_bitcast_fusion.2.refs_0_), channel_id=1, source_target_pairs={{0,4},{4,8},{8,12},{12,14},{14,10},{10,6},{6,2},{2,0},{1,5},{5,9},... | collective-permute-start | bytes 393224 | tf_op jit(solution)/shard_map/ppermute | solution.py:46
  10.2 6.2 %collective-permute-start.2 = (bf16[256,256]{1,0:T(8,128)(2,1)S(1)}, bf16[256,256]{1,0:T(8,128)(2,1)S(1)}, u32[]{:S(2)}, u32[]{:S(2)}) collective-permute-start(bf16[256,256]{1,0:T(8,128)(2,1)S(1)} %slice_bitcast_fusion.2.refs_0_), channel_id=1, source_target_pairs={{0,2},{4,0},{8,4},{12,8},{14,12},{10,14},{6,10},{2,6},{1,3},{5,1},... | collective-permute-start | bytes 393224 | tf_op jit(solution)/shard_map/ppermute | solution.py:46
  10.3 8.4 %collective-permute-start.7 = (bf16[256,256]{1,0:T(8,128)(2,1)S(1)}, bf16[256,256]{1,0:T(8,128)(2,1)S(1)}, u32[]{:S(2)}, u32[]{:S(2)}) collective-permute-start(bf16[256,256]{1,0:T(8,128)(2,1)S(1)} %collective-permute-done.3.refs_5_.refs_3_), channel_id=1, source_target_pairs={{0,2},{4,0},{8,4},{12,8},{14,12},{10,14},{6,10},{2,6},{1,3},{5,1},... | collective-permute-start | bytes 393224 | tf_op jit(solution)/shard_map/ppermute | solution.py:46
  12.2 6.9 %collective-permute-start.4 = (bf16[256,256]{1,0:T(8,128)(2,1)S(1)}, bf16[256,256]{1,0:T(8,128)(2,1)S(1)}, u32[]{:S(2)}, u32[]{:S(2)}) collective-permute-start(bf16[256,256]{1,0:T(8,128)(2,1)S(1)} %collective-permute-done.refs_2_.refs_0_), channel_id=1, source_target_pairs={{0,4},{4,8},{8,12},{12,14},{14,10},{10,6},{6,2},{2,0},{1,5},{5,9},... | collective-permute-start | bytes 393224 | tf_op jit(solution)/shard_map/ppermute | solution.py:46
  12.3 14.7 %collective-permute-start.14 = (bf16[128,1024]{1,0:T(8,128)(2,1)}, bf16[128,1024]{1,0:T(8,128)(2,1)S(1)}, u32[]{:S(2)}, u32[]{:S(2)}) collective-permute-start(bf16[128,1024]{1,0:T(8,128)(2,1)} %param.11), channel_id=1, source_target_pairs={{0,1},{2,3},{4,5},{6,7},{8,9},{10,11},{12,13},{14,15},{16,17},{18,... | collective-permute-start | bytes 786440 | tf_op jit(solution)/shard_map/ppermute | solution.py:23
  14.0 6.8 %collective-permute-start.5 = (bf16[256,256]{1,0:T(8,128)(2,1)S(1)}, bf16[256,256]{1,0:T(8,128)(2,1)S(1)}, u32[]{:S(2)}, u32[]{:S(2)}) collective-permute-start(bf16[256,256]{1,0:T(8,128)(2,1)S(1)} %collective-permute-done.1.refs_3_.refs_1_), channel_id=1, source_target_pairs={{0,4},{4,8},{8,12},{12,14},{14,10},{10,6},{6,2},{2,0},{1,5},{5,9},... | collective-permute-start | bytes 393224 | tf_op jit(solution)/shard_map/ppermute | solution.py:46
  16.5 6.4 %collective-permute-start.6 = (bf16[256,256]{1,0:T(8,128)(2,1)S(1)}, bf16[256,256]{1,0:T(8,128)(2,1)S(1)}, u32[]{:S(2)}, u32[]{:S(2)}) collective-permute-start(bf16[256,256]{1,0:T(8,128)(2,1)S(1)} %collective-permute-done.2.refs_4_.refs_2_), channel_id=1, source_target_pairs={{0,2},{4,0},{8,4},{12,8},{14,12},{10,14},{6,10},{2,6},{1,3},{5,1},... | collective-permute-start | bytes 393224 | tf_op jit(solution)/shard_map/ppermute | solution.py:46
  18.7 6.3 %collective-permute-start.11 = (bf16[256,256]{1,0:T(8,128)(2,1)S(1)}, bf16[256,256]{1,0:T(8,128)(2,1)S(1)}, u32[]{:S(2)}, u32[]{:S(2)}) collective-permute-start(bf16[256,256]{1,0:T(8,128)(2,1)S(1)} %collective-permute-done.7.refs_9_.refs_7_), channel_id=1, source_target_pairs={{0,2},{4,0},{8,4},{12,8},{14,12},{10,14},{6,10},{2,6},{1,3},{5,1},... | collective-permute-start | bytes 393224 | tf_op jit(solution)/shard_map/ppermute | solution.py:46
  19.1 6.3 %collective-permute-start.8 = (bf16[256,256]{1,0:T(8,128)(2,1)S(1)}, bf16[256,256]{1,0:T(8,128)(2,1)S(1)}, u32[]{:S(2)}, u32[]{:S(2)}) collective-permute-start(bf16[256,256]{1,0:T(8,128)(2,1)S(1)} %collective-permute-done.4.refs_6_.refs_4_), channel_id=1, source_target_pairs={{0,4},{4,8},{8,12},{12,14},{14,10},{10,6},{6,2},{2,0},{1,5},{5,9},... | collective-permute-start | bytes 393224 | tf_op jit(solution)/shard_map/ppermute | solution.py:46
  20.7 7.5 %collective-permute-start.9 = (bf16[256,256]{1,0:T(8,128)(2,1)S(1)}, bf16[256,256]{1,0:T(8,128)(2,1)S(1)}, u32[]{:S(2)}, u32[]{:S(2)}) collective-permute-start(bf16[256,256]{1,0:T(8,128)(2,1)S(1)} %collective-permute-done.5.refs_7_.refs_5_), channel_id=1, source_target_pairs={{0,4},{4,8},{8,12},{12,14},{14,10},{10,6},{6,2},{2,0},{1,5},{5,9},... | collective-permute-start | bytes 393224 | tf_op jit(solution)/shard_map/ppermute | solution.py:46
  35.8 5.8 %collective-permute-start.16 = (bf16[256,256]{1,0:T(8,128)(2,1)S(1)}, bf16[256,256]{1,0:T(8,128)(2,1)S(1)}, u32[]{:S(2)}, u32[]{:S(2)}) collective-permute-start(bf16[256,256]{1,0:T(8,128)(2,1)S(1)} %get-tuple-element.53), channel_id=1, source_target_pairs={{0,4},{4,8},{8,12},{12,14},{14,10},{10,6},{6,2},{2,0},{1,5},{5,9},... | collective-permute-start | bytes 393224 | tf_op jit(solution)/shard_map/ppermute | solution.py:46
  37.5 5.8 %collective-permute-start.20 = (bf16[256,256]{1,0:T(8,128)(2,1)S(1)}, bf16[256,256]{1,0:T(8,128)(2,1)S(1)}, u32[]{:S(2)}, u32[]{:S(2)}) collective-permute-start(bf16[256,256]{1,0:T(8,128)(2,1)S(1)} %get-tuple-element.56), channel_id=1, source_target_pairs={{0,2},{4,0},{8,4},{12,8},{14,12},{10,14},{6,10},{2,6},{1,3},{5,1},... | collective-permute-start | bytes 393224 | tf_op jit(solution)/shard_map/ppermute | solution.py:46
  39.2 5.9 %collective-permute-start.29 = (bf16[256,256]{1,0:T(8,128)(2,1)S(1)}, bf16[256,256]{1,0:T(8,128)(2,1)S(1)}, u32[]{:S(2)}, u32[]{:S(2)}) collective-permute-start(bf16[256,256]{1,0:T(8,128)(2,1)S(1)} %get-tuple-element.64), channel_id=1, source_target_pairs={{0,4},{4,8},{8,12},{12,14},{14,10},{10,6},{6,2},{2,0},{1,5},{5,9},... | collective-permute-start | bytes 393224 | tf_op jit(solution)/shard_map/ppermute | solution.py:46
  40.0 6.5 %collective-permute-start.23 = (bf16[256,256]{1,0:T(8,128)(2,1)S(1)}, bf16[256,256]{1,0:T(8,128)(2,1)S(1)}, u32[]{:S(2)}, u32[]{:S(2)}) collective-permute-start(bf16[256,256]{1,0:T(8,128)(2,1)S(1)} %add_convert_fusion.4), channel_id=1, source_target_pairs={{0,2},{4,0},{8,4},{12,8},{14,12},{10,14},{6,10},{2,6},{1,3},{5,1},... | collective-permute-start | bytes 393224 | tf_op jit(solution)/shard_map/ppermute | solution.py:46
  41.7 6.5 %collective-permute-start.17 = (bf16[256,256]{1,0:T(8,128)(2,1)S(1)}, bf16[256,256]{1,0:T(8,128)(2,1)S(1)}, u32[]{:S(2)}, u32[]{:S(2)}) collective-permute-start(bf16[256,256]{1,0:T(8,128)(2,1)S(1)} %add_convert_fusion.9), channel_id=1, source_target_pairs={{0,4},{4,8},{8,12},{12,14},{14,10},{10,6},{6,2},{2,0},{1,5},{5,9},... | collective-permute-start | bytes 393224 | tf_op jit(solution)/shard_map/ppermute | solution.py:46
  43.4 6.0 %collective-permute-start.22 = (bf16[256,256]{1,0:T(8,128)(2,1)S(1)}, bf16[256,256]{1,0:T(8,128)(2,1)S(1)}, u32[]{:S(2)}, u32[]{:S(2)}) collective-permute-start(bf16[256,256]{1,0:T(8,128)(2,1)S(1)} %add_convert_fusion.6), channel_id=1, source_target_pairs={{0,2},{4,0},{8,4},{12,8},{14,12},{10,14},{6,10},{2,6},{1,3},{5,1},... | collective-permute-start | bytes 393224 | tf_op jit(solution)/shard_map/ppermute | solution.py:46
  45.1 6.2 %collective-permute-start.30 = (bf16[256,256]{1,0:T(8,128)(2,1)S(1)}, bf16[256,256]{1,0:T(8,128)(2,1)S(1)}, u32[]{:S(2)}, u32[]{:S(2)}) collective-permute-start(bf16[256,256]{1,0:T(8,128)(2,1)S(1)} %add_convert_fusion.3), channel_id=1, source_target_pairs={{0,4},{4,8},{8,12},{12,14},{14,10},{10,6},{6,2},{2,0},{1,5},{5,9},... | collective-permute-start | bytes 393224 | tf_op jit(solution)/shard_map/ppermute | solution.py:46
  46.5 8.3 %collective-permute-start.32 = (bf16[256,256]{1,0:T(8,128)(2,1)S(1)}, bf16[256,256]{1,0:T(8,128)(2,1)S(1)}, u32[]{:S(2)}, u32[]{:S(2)}) collective-permute-start(bf16[256,256]{1,0:T(8,128)(2,1)S(1)} %add_convert_fusion.1), channel_id=1, source_target_pairs={{0,2},{4,0},{8,4},{12,8},{14,12},{10,14},{6,10},{2,6},{1,3},{5,1},... | collective-permute-start | bytes 393224 | tf_op jit(solution)/shard_map/ppermute | solution.py:46
  48.2 6.1 %collective-permute-start.18 = (bf16[256,256]{1,0:T(8,128)(2,1)S(1)}, bf16[256,256]{1,0:T(8,128)(2,1)S(1)}, u32[]{:S(2)}, u32[]{:S(2)}) collective-permute-start(bf16[256,256]{1,0:T(8,128)(2,1)S(1)} %add_convert_fusion.8), channel_id=1, source_target_pairs={{0,4},{4,8},{8,12},{12,14},{14,10},{10,6},{6,2},{2,0},{1,5},{5,9},... | collective-permute-start | bytes 393224 | tf_op jit(solution)/shard_map/ppermute | solution.py:46
  49.4 7.1 %collective-permute-start.24 = (bf16[256,256]{1,0:T(8,128)(2,1)S(1)}, bf16[256,256]{1,0:T(8,128)(2,1)S(1)}, u32[]{:S(2)}, u32[]{:S(2)}) collective-permute-start(bf16[256,256]{1,0:T(8,128)(2,1)S(1)} %add_convert_fusion.5), channel_id=1, source_target_pairs={{0,2},{4,0},{8,4},{12,8},{14,12},{10,14},{6,10},{2,6},{1,3},{5,1},... | collective-permute-start | bytes 393224 | tf_op jit(solution)/shard_map/ppermute | solution.py:46
  51.3 8.6 %collective-permute-start.31 = (bf16[256,256]{1,0:T(8,128)(2,1)S(1)}, bf16[256,256]{1,0:T(8,128)(2,1)S(1)}, u32[]{:S(2)}, u32[]{:S(2)}) collective-permute-start(bf16[256,256]{1,0:T(8,128)(2,1)S(1)} %add_convert_fusion.2), channel_id=1, source_target_pairs={{0,4},{4,8},{8,12},{12,14},{14,10},{10,6},{6,2},{2,0},{1,5},{5,9},... | collective-permute-start | bytes 393224 | tf_op jit(solution)/shard_map/ppermute | solution.py:46
  59.4 6.4 %collective-permute-start.25 = (bf16[256,256]{1,0:T(8,128)(2,1)S(1)}, bf16[256,256]{1,0:T(8,128)(2,1)S(1)}, u32[]{:S(2)}, u32[]{:S(2)}) collective-permute-start(bf16[256,256]{1,0:T(8,128)(2,1)S(1)} %fusion.1.refs_0_), channel_id=1, source_target_pairs={{0,4},{4,8},{8,12},{12,14},{14,10},{10,6},{6,2},{2,0},{1,5},{5,9},... | collective-permute-start | bytes 393224 | tf_op jit(solution)/shard_map/ppermute | solution.py:46
  60.2 6.4 %collective-permute-start.34 = (bf16[256,256]{1,0:T(8,128)(2,1)S(1)}, bf16[256,256]{1,0:T(8,128)(2,1)S(1)}, u32[]{:S(2)}, u32[]{:S(2)}) collective-permute-start(bf16[256,256]{1,0:T(8,128)(2,1)S(1)} %multiply_convert_fusion.refs_1_), channel_id=1, source_target_pairs={{0,2},{4,0},{8,4},{12,8},{14,12},{10,14},{6,10},{2,6},{1,3},{5,1},... | collective-permute-start | bytes 393224 | tf_op jit(solution)/shard_map/ppermute | solution.py:46
  61.8 7.5 %collective-permute-start.39 = (bf16[256,256]{1,0:T(8,128)(2,1)S(1)}, bf16[256,256]{1,0:T(8,128)(2,1)S(1)}, u32[]{:S(2)}, u32[]{:S(2)}) collective-permute-start(bf16[256,256]{1,0:T(8,128)(2,1)S(1)} %fusion.1.refs_0_), channel_id=1, source_target_pairs={{0,2},{4,0},{8,4},{12,8},{14,12},{10,14},{6,10},{2,6},{1,3},{5,1},... | collective-permute-start | bytes 393224 | tf_op jit(solution)/shard_map/ppermute | solution.py:46
  63.4 7.5 %collective-permute-start.38 = (bf16[256,256]{1,0:T(8,128)(2,1)S(1)}, bf16[256,256]{1,0:T(8,128)(2,1)S(1)}, u32[]{:S(2)}, u32[]{:S(2)}) collective-permute-start(bf16[256,256]{1,0:T(8,128)(2,1)S(1)} %multiply_convert_fusion.refs_1_), channel_id=1, source_target_pairs={{0,4},{4,8},{8,12},{12,14},{14,10},{10,6},{6,2},{2,0},{1,5},{5,9},... | collective-permute-start | bytes 393224 | tf_op jit(solution)/shard_map/ppermute | solution.py:46
  65.8 6.7 %collective-permute-start.26 = (bf16[256,256]{1,0:T(8,128)(2,1)S(1)}, bf16[256,256]{1,0:T(8,128)(2,1)S(1)}, u32[]{:S(2)}, u32[]{:S(2)}) collective-permute-start(bf16[256,256]{1,0:T(8,128)(2,1)S(1)} %collective-permute-done.25.refs_2_), channel_id=1, source_target_pairs={{0,4},{4,8},{8,12},{12,14},{14,10},{10,6},{6,2},{2,0},{1,5},{5,9},... | collective-permute-start | bytes 393224 | tf_op jit(solution)/shard_map/ppermute | solution.py:46
  66.6 6.5 %collective-permute-start.35 = (bf16[256,256]{1,0:T(8,128)(2,1)S(1)}, bf16[256,256]{1,0:T(8,128)(2,1)S(1)}, u32[]{:S(2)}, u32[]{:S(2)}) collective-permute-start(bf16[256,256]{1,0:T(8,128)(2,1)S(1)} %collective-permute-done.34.refs_5_), channel_id=1, source_target_pairs={{0,2},{4,0},{8,4},{12,8},{14,12},{10,14},{6,10},{2,6},{1,3},{5,1},... | collective-permute-start | bytes 393224 | tf_op jit(solution)/shard_map/ppermute | solution.py:46
  70.9 6.1 %collective-permute-start.40 = (bf16[256,256]{1,0:T(8,128)(2,1)S(1)}, bf16[256,256]{1,0:T(8,128)(2,1)S(1)}, u32[]{:S(2)}, u32[]{:S(2)}) collective-permute-start(bf16[256,256]{1,0:T(8,128)(2,1)S(1)} %collective-permute-done.38.refs_3_), channel_id=1, source_target_pairs={{0,4},{4,8},{8,12},{12,14},{14,10},{10,6},{6,2},{2,0},{1,5},{5,9},... | collective-permute-start | bytes 393224 | tf_op jit(solution)/shard_map/ppermute | solution.py:46
  72.5 6.4 %collective-permute-start.27 = (bf16[256,256]{1,0:T(8,128)(2,1)S(1)}, bf16[256,256]{1,0:T(8,128)(2,1)S(1)}, u32[]{:S(2)}, u32[]{:S(2)}) collective-permute-start(bf16[256,256]{1,0:T(8,128)(2,1)S(1)} %collective-permute-done.26.refs_0_), channel_id=1, source_target_pairs={{0,4},{4,8},{8,12},{12,14},{14,10},{10,6},{6,2},{2,0},{1,5},{5,9},... | collective-permute-start | bytes 393224 | tf_op jit(solution)/shard_map/ppermute | solution.py:46
  73.1 6.4 %collective-permute-start.36 = (bf16[256,256]{1,0:T(8,128)(2,1)S(1)}, bf16[256,256]{1,0:T(8,128)(2,1)S(1)}, u32[]{:S(2)}, u32[]{:S(2)}) collective-permute-start(bf16[256,256]{1,0:T(8,128)(2,1)S(1)} %collective-permute-done.35.refs_3_), channel_id=1, source_target_pairs={{0,2},{4,0},{8,4},{12,8},{14,12},{10,14},{6,10},{2,6},{1,3},{5,1},... | collective-permute-start | bytes 393224 | tf_op jit(solution)/shard_map/ppermute | solution.py:46
  75.0 7.1 %collective-permute-start.43 = (bf16[256,256]{1,0:T(8,128)(2,1)S(1)}, bf16[256,256]{1,0:T(8,128)(2,1)S(1)}, u32[]{:S(2)}, u32[]{:S(2)}) collective-permute-start(bf16[256,256]{1,0:T(8,128)(2,1)S(1)} %collective-permute-done.41.refs_2_), channel_id=1, source_target_pairs={{0,2},{4,0},{8,4},{12,8},{14,12},{10,14},{6,10},{2,6},{1,3},{5,1},... | collective-permute-start | bytes 393224 | tf_op jit(solution)/shard_map/ppermute | solution.py:46
  (17 other events, 101.2 us)

commit v10 on v9

--- a/solution.py
+++ b/solution.py
@@ -87,11 +87,19 @@
             outs[1][at, :] = jnp.maximum(total, 0.0).astype(BF16)
 
 
-def turn_kernel(starts, *refs):
+def turn_own_kernel(starts, *refs):
+    *shards, turned = refs
+    rows = shards[0].shape[0]
+    for chain, shard in enumerate(shards):
+        turned[:, chain * rows:(chain + 1) * rows] = shard[...].T
+
+
+def turn_kernel(starts, own, *refs):
     *shards, turned = refs
     rows, wide = shards[0].shape
+    turned[block_of(starts, 0, wide), :] = own[...]
     for k in range(len(shards) // 2):
-        at = block_of(starts, k, wide)
+        at = block_of(starts, k + 1, wide)
         for chain in range(2):
             turned[at, chain * rows:(chain + 1) * rows] = shards[2 * k + chain][...].T
 
@@ -163,20 +171,25 @@
                 high[pl.ds(start - half_width + c, lat), :] = piece[:, c:c + lat]
 
 
-def finish_kernel(slots, far, starts, *refs):
-    turned, preact, back_own, arrived, high, last_same, *outers = refs[:6 + len(slots)]
-    grad, bias, same, cross, stage, grad_sems, same_sems, cross_sems = refs[6 + len(slots):]
+def place_kernel(slots, far, starts, *refs):
+    last, *outers, same, sems = refs
+    lat, wide = last.shape
+    blocks = [(far, last)]
+    for group, outer in zip(slots, outers):
+        blocks += [(slot, outer.at[i, :lat, :]) for i, slot in enumerate(group)]
+    copies = []
+    for i, (slot, block) in enumerate(blocks):
+        copies.append(pltpu.make_async_copy(block, same.at[0, :, block_of(starts, slot, wide)], sems.at[i]))
+        copies[-1].start()
+    for copy in copies:
+        copy.wait()
+
+
+def finish_kernel(starts, turned, preact, back_own, arrived, high, grad, bias, cross, stage, grad_sems, cross_sems):
     pieces, height, lat = stage.shape
     rows = preact.shape[0]
     half_width = high.shape[0]
-    wide = last_same.shape[1]
     copies = []
-    blocks = [(far, last_same)]
-    for group, outer in zip(slots, outers):
-        blocks += [(slot, outer.at[i, :lat, :]) for i, slot in enumerate(group)]
-    for i, (slot, block) in enumerate(blocks):
-        copies.append(pltpu.make_async_copy(block, same.at[0, :, block_of(starts, slot, wide)], same_sems.at[i]))
-        copies[-1].start()
     first = starts[starts.shape[0] - 1] == 0
     for c in range(half_width // lat):
         at = pl.ds(c * lat, lat)
@@ -252,15 +265,15 @@
             [starts] + both_chains(inputs, slots) + [enc_weight, before],
         )
 
-    front = residual_in[0, :half]
-    inputs = [[front] + [None] * (size - 1), [after(residual_in, front)[0, half:]] + [None] * (size - 1)]
-    part = encode((0,), enc_bias)[0]
+    inputs = [[part] + [None] * (size - 1) for part in halves(residual_in[0])]
+    turned_own = call(
+        turn_own_kernel, [shape((wide, rows), BF16)], 0, [starts] + both_chains(inputs, (0,))
+    )[0]
     for s in range(1, reach + 1):
-        gather_step(inputs, s, part if s == 1 else None)
+        gather_step(inputs, s, turned_own if s == 1 else None)
     low_cross = passed_along(after(dec_cross, inputs[0][slot_p.get(1, far)]), "layer", 1)
     stacked = jnp.concatenate([dec_same[0], jnp.concatenate([low_cross, dec_cross], axis=1)], axis=0)
-    if size > 2:
-        part = encode(tuple(range(1, far)), after(part, stacked))[0]
+    part = encode(tuple(range(far)), after(enc_bias, stacked))[0]
     preact, codes = encode((far,), part)
     earlier = passed_along(codes, "layer", 1)
 
@@ -312,8 +325,15 @@
         )
 
     groups, outers, acc, pending = [], [], None, [0]
+    arrived = [inputs[0][1]] if size == 2 else [after(inputs[0][1], errors[1][0])]
+    turned = call(
+        turn_kernel,
+        [shape((deep, rows), BF16)],
+        0,
+        [starts, turned_own] + arrived + both_chains(inputs, range(1, size))[1:],
+    )[0]
     for s in range(1, reach + 1):
-        gather_step(errors, s)
+        gather_step(errors, s, turned if s == 2 else None)
         if s < reach:
             pending += [slot_p[s], slot_q[s]]
         if s == 1 or s == reach - 1:
@@ -333,23 +353,24 @@
         [starts] + both_chains(errors, (far,)) + [stacked] + both_t + outers + [acc],
     )
     returned = passed_along(sent, "layer", -1)
-    turned = call(turn_kernel, [shape((deep, rows), BF16)], unit, [starts] + both_chains(inputs, range(size)))[0]
+    grad_same = call(
+        functools.partial(place_kernel, groups, far),
+        [shape((1, lat, deep), F32)],
+        0,
+        [starts, last_same] + outers,
+        out_spaces=[pl.ANY],
+        scratch=[pltpu.SemaphoreType.DMA((size,))],
+    )[0]
     height = deep // PIECES
-    grad_enc, grad_bias, grad_same, grad_cross = call(
-        functools.partial(finish_kernel, groups, far),
-        [
-            shape((1, deep, lat), F32),
-            shape((1, lat), F32),
-            shape((1, lat, deep), F32),
-            shape((lat, half_width), F32),
-        ],
+    grad_enc, grad_bias, grad_cross = call(
+        finish_kernel,
+        [shape((1, deep, lat), F32), shape((1, lat), F32), shape((lat, half_width), F32)],
         2 * unit * size,
-        [starts, turned, preact, back_own, returned, high, last_same] + outers,
-        out_spaces=[pl.ANY, pltpu.VMEM, pl.ANY, pl.ANY],
+        [starts, turned, preact, back_own, returned, high],
+        out_spaces=[pl.ANY, pltpu.VMEM, pl.ANY],
         scratch=[
             pltpu.VMEM((PIECES, height, lat), F32),
             pltpu.SemaphoreType.DMA((PIECES,)),
-            pltpu.SemaphoreType.DMA((size,)),
             pltpu.SemaphoreType.DMA((half_width // lat,)),
         ],
     )

time: 93.1 us -> 92.3 us (level)
  local copies, waits for them, and re-layouts: 3.7 us -> 1.15 us
  waiting for transfers between devices: 25.5 us -> 26.9 us
  Pallas kernels: 12.3 us -> 13.3 us
    squeeze x2 -> x0, local copies, waits for them, and re-layouts: 1.89 us -> none  [the longest x1 0.97 us: ring_shards(): front = residual_in[0, :half]]
    ppermute x42, waiting for transfers between devices: 22.8 us -> 24.6 us  [hop(): lax.ppermute(shard, 'latent', [(order[p], order[(p + way) % size]) for p...]
    unnamed x8 -> x6, local copies, waits for them, and re-layouts: 1.71 us -> 0.01 us
    slice x1 -> x2, local copies, waits for them, and re-layouts: 0.01 us -> 1.05 us  [halves(): return [array[:half], array[half:]]]
    pallas_call x10 -> x11, Pallas kernels: 12.3 us -> 13.3 us  [call(): pl.pallas_call(kernel, out_shape=outs, in_specs=[spec(pltpu.SMEM)] + [spe...]
  transfers between devices with their start and end apart: 45 -> 45, of which waited for: 24 -> 23; matrix products, arithmetic and copies ran while one was open for 2% -> 2% of each run, Pallas kernels for 7% -> 9%
where the time goes in v10:
time: 92.3 us; the launch traced here: 92.1 us
  starting transfers between devices  48.3 us (52%)
  waiting for transfers between devices  26.9 us (29%)
  Pallas kernels  13.3 us (14%)
  other arithmetic  1.63 us (2%)
  local copies, waits for them, and re-layouts  1.15 us (1%)
    ppermute x42, starting transfers between devices, hop(): lax.ppermute(shard, 'latent', [(order[p], order[(p + way) % size]) for p...  44.4 us
    ppermute x42, waiting for transfers between devices, hop(): lax.ppermute(shard, 'latent', [(order[p], order[(p + way) % size]) for p...  24.6 us
    pallas_call x11, Pallas kernels, call(): pl.pallas_call(kernel, out_shape=outs, in_specs=[spec(pltpu.SMEM)] + [spe...  13.3 us
    ppermute x3, starting transfers between devices, passed_along(): return lax.ppermute(shard, axis, pairs)  3.89 us
    ppermute x3, waiting for transfers between devices, passed_along(): return lax.ppermute(shard, axis, pairs)  2.27 us
  transfers between devices with their start and end apart: 45, of which 23 were waited for; matrix products, arithmetic and copies ran while one was open for 2% of the time, Pallas kernels for 9%

profile of v10, /device:TPU:0, one launch (start us, length us, event | category | flops | bytes accessed | tf_op | source)
XLA Modules:
  0.0 92.1 jit_solution(9574385169644106573)
XLA Ops:
  1.7 3.0 %collective-permute-start.4 = (bf16[256,256]{1,0:T(8,128)(2,1)S(1)}, bf16[256,256]{1,0:T(8,128)(2,1)S(1)}, u32[]{:S(2)}, u32[]{:S(2)}) collective-permute-start(bf16[256,256]{1,0:T(8,128)(2,1)S(1)} %get-tuple-element.47.refs_1_), channel_id=1, source_target_pairs={{0,2},{4,0},{8,4},{12,8},{14,12},{10,14},{6,10},{2,6},{1,3},{5,1},... | collective-permute-start | bytes 393224 | tf_op jit(solution)/shard_map/ppermute | solution.py:46
  5.6 2.0 %collective-permute-start.8 = (bf16[256,256]{1,0:T(8,128)(2,1)S(1)}, bf16[256,256]{1,0:T(8,128)(2,1)S(1)}, u32[]{:S(2)}, u32[]{:S(2)}) collective-permute-start(bf16[256,256]{1,0:T(8,128)(2,1)S(1)} %get-tuple-element.47.refs_1_), channel_id=1, source_target_pairs={{0,4},{4,8},{8,12},{12,14},{14,10},{10,6},{6,2},{2,0},{1,5},{5,9},... | collective-permute-start | bytes 393224 | tf_op jit(solution)/shard_map/ppermute | solution.py:46
  8.3 2.0 %collective-permute-start.5 = (bf16[256,256]{1,0:T(8,128)(2,1)S(1)}, bf16[256,256]{1,0:T(8,128)(2,1)S(1)}, u32[]{:S(2)}, u32[]{:S(2)}) collective-permute-start(bf16[256,256]{1,0:T(8,128)(2,1)S(1)} %collective-permute-done.4.refs_5_.refs_3_), channel_id=1, source_target_pairs={{0,2},{4,0},{8,4},{12,8},{14,12},{10,14},{6,10},{2,6},{1,3},{5,1},... | collective-permute-start | bytes 393224 | tf_op jit(solution)/shard_map/ppermute | solution.py:46
  13.9 1.7 %collective-permute-start.11 = (bf16[256,256]{1,0:T(8,128)(2,1)S(1)}, bf16[256,256]{1,0:T(8,128)(2,1)S(1)}, u32[]{:S(2)}, u32[]{:S(2)}) collective-permute-start(bf16[256,256]{1,0:T(8,128)(2,1)S(1)} %collective-permute-done.9.refs_4_.refs_2_), channel_id=1, source_target_pairs={{0,2},{4,0},{8,4},{12,8},{14,12},{10,14},{6,10},{2,6},{1,3},{5,1},... | collective-permute-start | bytes 393224 | tf_op jit(solution)/shard_map/ppermute | solution.py:46
  15.7 1.6 %collective-permute-start.6 = (bf16[256,256]{1,0:T(8,128)(2,1)S(1)}, bf16[256,256]{1,0:T(8,128)(2,1)S(1)}, u32[]{:S(2)}, u32[]{:S(2)}) collective-permute-start(bf16[256,256]{1,0:T(8,128)(2,1)S(1)} %collective-permute-done.5.refs_9_.refs_7_), channel_id=1, source_target_pairs={{0,2},{4,0},{8,4},{12,8},{14,12},{10,14},{6,10},{2,6},{1,3},{5,1},... | collective-permute-start | bytes 393224 | tf_op jit(solution)/shard_map/ppermute | solution.py:46
  17.7 2.2 %collective-permute-done.10.refs_7_.refs_5_ = bf16[256,256]{1,0:T(8,128)(2,1)S(1)} collective-permute-done((bf16[256,256]{1,0:T(8,128)(2,1)S(1)}, bf16[256,256]{1,0:T(8,128)(2,1)S(1)}, u32[]{:S(2)}, u32[]{:S(2)}) %collective-permute-start.10) | collective-permute-done | bytes 131104 | tf_op jit(solution)/shard_map/ppermute | solution.py:46
  20.3 1.7 %collective-permute-start.13 = (bf16[256,256]{1,0:T(8,128)(2,1)S(1)}, bf16[256,256]{1,0:T(8,128)(2,1)S(1)}, u32[]{:S(2)}, u32[]{:S(2)}) collective-permute-start(bf16[256,256]{1,0:T(8,128)(2,1)S(1)} %collective-permute-done.11.refs_8_.refs_6_), channel_id=1, source_target_pairs={{0,2},{4,0},{8,4},{12,8},{14,12},{10,14},{6,10},{2,6},{1,3},{5,1},... | collective-permute-start | bytes 393224 | tf_op jit(solution)/shard_map/ppermute | solution.py:46
  22.0 1.8 %collective-permute-start.7 = (bf16[256,256]{1,0:T(8,128)(2,1)S(1)}, bf16[256,256]{1,0:T(8,128)(2,1)S(1)}, u32[]{:S(2)}, u32[]{:S(2)}) collective-permute-start(bf16[256,256]{1,0:T(8,128)(2,1)S(1)} %collective-permute-done.6.refs_13_.refs_11_), channel_id=1, source_target_pairs={{0,2},{4,0},{8,4},{12,8},{14,12},{10,14},{6,10},{2,6},{1,3},{5,1},... | collective-permute-start | bytes 393224 | tf_op jit(solution)/shard_map/ppermute | solution.py:46
  26.9 1.8 %collective-permute-done.3.refs_0_.refs_12_ = bf16[256,256]{1,0:T(8,128)(2,1)S(1)} collective-permute-done((bf16[256,256]{1,0:T(8,128)(2,1)S(1)}, bf16[256,256]{1,0:T(8,128)(2,1)S(1)}, u32[]{:S(2)}, u32[]{:S(2)}) %collective-permute-start.3) | collective-permute-done | bytes 131104 | tf_op jit(solution)/shard_map/ppermute | solution.py:46
  32.5 1.6 %collective-permute-start.18 = (bf16[256,256]{1,0:T(8,128)(2,1)S(1)}, bf16[256,256]{1,0:T(8,128)(2,1)S(1)}, u32[]{:S(2)}, u32[]{:S(2)}) collective-permute-start(bf16[256,256]{1,0:T(8,128)(2,1)S(1)} %get-tuple-element.57), channel_id=1, source_target_pairs={{0,2},{4,0},{8,4},{12,8},{14,12},{10,14},{6,10},{2,6},{1,3},{5,1},... | collective-permute-start | bytes 393224 | tf_op jit(solution)/shard_map/ppermute | solution.py:46
  36.2 1.8 %collective-permute-start.27 = (bf16[256,256]{1,0:T(8,128)(2,1)S(1)}, bf16[256,256]{1,0:T(8,128)(2,1)S(1)}, u32[]{:S(2)}, u32[]{:S(2)}) collective-permute-start(bf16[256,256]{1,0:T(8,128)(2,1)S(1)} %get-tuple-element.69), channel_id=1, source_target_pairs={{0,2},{4,0},{8,4},{12,8},{14,12},{10,14},{6,10},{2,6},{1,3},{5,1},... | collective-permute-start | bytes 393224 | tf_op jit(solution)/shard_map/ppermute | solution.py:46
  38.4 1.6 %collective-permute-start.21 = (bf16[256,256]{1,0:T(8,128)(2,1)S(1)}, bf16[256,256]{1,0:T(8,128)(2,1)S(1)}, u32[]{:S(2)}, u32[]{:S(2)}) collective-permute-start(bf16[256,256]{1,0:T(8,128)(2,1)S(1)} %add_convert_fusion.6), channel_id=1, source_target_pairs={{0,2},{4,0},{8,4},{12,8},{14,12},{10,14},{6,10},{2,6},{1,3},{5,1},... | collective-permute-start | bytes 393224 | tf_op jit(solution)/shard_map/ppermute | solution.py:46
  41.1 1.9 %collective-permute-done.16 = bf16[256,256]{1,0:T(8,128)(2,1)S(1)} collective-permute-done((bf16[256,256]{1,0:T(8,128)(2,1)S(1)}, bf16[256,256]{1,0:T(8,128)(2,1)S(1)}, u32[]{:S(2)}, u32[]{:S(2)}) %collective-permute-start.16) | collective-permute-done | bytes 131104 | tf_op jit(solution)/shard_map/ppermute | solution.py:46
  43.6 1.6 %collective-permute-start.28 = (bf16[256,256]{1,0:T(8,128)(2,1)S(1)}, bf16[256,256]{1,0:T(8,128)(2,1)S(1)}, u32[]{:S(2)}, u32[]{:S(2)}) collective-permute-start(bf16[256,256]{1,0:T(8,128)(2,1)S(1)} %add_convert_fusion.1), channel_id=1, source_target_pairs={{0,2},{4,0},{8,4},{12,8},{14,12},{10,14},{6,10},{2,6},{1,3},{5,1},... | collective-permute-start | bytes 393224 | tf_op jit(solution)/shard_map/ppermute | solution.py:46
  45.3 1.6 %collective-permute-start.23 = (bf16[256,256]{1,0:T(8,128)(2,1)S(1)}, bf16[256,256]{1,0:T(8,128)(2,1)S(1)}, u32[]{:S(2)}, u32[]{:S(2)}) collective-permute-start(bf16[256,256]{1,0:T(8,128)(2,1)S(1)} %add_convert_fusion.5), channel_id=1, source_target_pairs={{0,2},{4,0},{8,4},{12,8},{14,12},{10,14},{6,10},{2,6},{1,3},{5,1},... | collective-permute-start | bytes 393224 | tf_op jit(solution)/shard_map/ppermute | solution.py:46
  47.4 1.9 %collective-permute-done.19 = bf16[256,256]{1,0:T(8,128)(2,1)S(1)} collective-permute-done((bf16[256,256]{1,0:T(8,128)(2,1)S(1)}, bf16[256,256]{1,0:T(8,128)(2,1)S(1)}, u32[]{:S(2)}, u32[]{:S(2)}) %collective-permute-start.19) | collective-permute-done | bytes 131104 | tf_op jit(solution)/shard_map/ppermute | solution.py:46
  50.0 1.6 %collective-permute-start.29 = (bf16[256,256]{1,0:T(8,128)(2,1)S(1)}, bf16[256,256]{1,0:T(8,128)(2,1)S(1)}, u32[]{:S(2)}, u32[]{:S(2)}) collective-permute-start(bf16[256,256]{1,0:T(8,128)(2,1)S(1)} %add_convert_fusion), channel_id=1, source_target_pairs={{0,2},{4,0},{8,4},{12,8},{14,12},{10,14},{6,10},{2,6},{1,3},{5,1},... | collective-permute-start | bytes 393224 | tf_op jit(solution)/shard_map/ppermute | solution.py:46
  51.6 1.4 %collective-permute-done.25 = bf16[256,256]{1,0:T(8,128)(2,1)S(1)} collective-permute-done((bf16[256,256]{1,0:T(8,128)(2,1)S(1)}, bf16[256,256]{1,0:T(8,128)(2,1)S(1)}, u32[]{:S(2)}, u32[]{:S(2)}) %collective-permute-start.25) | collective-permute-done | bytes 131104 | tf_op jit(solution)/shard_map/ppermute | solution.py:46
  53.5 1.6 %collective-permute-start.24 = (bf16[256,256]{1,0:T(8,128)(2,1)S(1)}, bf16[256,256]{1,0:T(8,128)(2,1)S(1)}, u32[]{:S(2)}, u32[]{:S(2)}) collective-permute-start(bf16[256,256]{1,0:T(8,128)(2,1)S(1)} %add_convert_fusion.4), channel_id=1, source_target_pairs={{0,2},{4,0},{8,4},{12,8},{14,12},{10,14},{6,10},{2,6},{1,3},{5,1},... | collective-permute-start | bytes 393224 | tf_op jit(solution)/shard_map/ppermute | solution.py:46
  55.7 2.3 %collective-permute-done.26 = bf16[256,256]{1,0:T(8,128)(2,1)S(1)} collective-permute-done((bf16[256,256]{1,0:T(8,128)(2,1)S(1)}, bf16[256,256]{1,0:T(8,128)(2,1)S(1)}, u32[]{:S(2)}, u32[]{:S(2)}) %collective-permute-start.26) | collective-permute-done | bytes 131104 | tf_op jit(solution)/shard_map/ppermute | solution.py:46
  58.7 1.7 %collective-permute-start.34 = (bf16[256,256]{1,0:T(8,128)(2,1)S(1)}, bf16[256,256]{1,0:T(8,128)(2,1)S(1)}, u32[]{:S(2)}, u32[]{:S(2)}) collective-permute-start(bf16[256,256]{1,0:T(8,128)(2,1)S(1)} %multiply_convert_fusion.refs_1_), channel_id=1, source_target_pairs={{0,2},{4,0},{8,4},{12,8},{14,12},{10,14},{6,10},{2,6},{1,3},{5,1},... | collective-permute-start | bytes 393224 | tf_op jit(solution)/shard_map/ppermute | solution.py:46
  62.8 2.3 %collective-permute-done.34.refs_5_ = bf16[256,256]{1,0:T(8,128)(2,1)S(1)} collective-permute-done((bf16[256,256]{1,0:T(8,128)(2,1)S(1)}, bf16[256,256]{1,0:T(8,128)(2,1)S(1)}, u32[]{:S(2)}, u32[]{:S(2)}) %collective-permute-start.34) | collective-permute-done | bytes 131104 | tf_op jit(solution)/shard_map/ppermute | solution.py:46
  65.1 1.6 %collective-permute-start.35 = (bf16[256,256]{1,0:T(8,128)(2,1)S(1)}, bf16[256,256]{1,0:T(8,128)(2,1)S(1)}, u32[]{:S(2)}, u32[]{:S(2)}) collective-permute-start(bf16[256,256]{1,0:T(8,128)(2,1)S(1)} %collective-permute-done.34.refs_5_), channel_id=1, source_target_pairs={{0,2},{4,0},{8,4},{12,8},{14,12},{10,14},{6,10},{2,6},{1,3},{5,1},... | collective-permute-start | bytes 393224 | tf_op jit(solution)/shard_map/ppermute | solution.py:46
  69.8 1.5 %collective-permute-start.41 = (bf16[256,256]{1,0:T(8,128)(2,1)S(1)}, bf16[256,256]{1,0:T(8,128)(2,1)S(1)}, u32[]{:S(2)}, u32[]{:S(2)}) collective-permute-start(bf16[256,256]{1,0:T(8,128)(2,1)S(1)} %collective-permute-done.39.refs_4_), channel_id=1, source_target_pairs={{0,2},{4,0},{8,4},{12,8},{14,12},{10,14},{6,10},{2,6},{1,3},{5,1},... | collective-permute-start | bytes 393224 | tf_op jit(solution)/shard_map/ppermute | solution.py:46
  71.3 1.6 %collective-permute-start.36 = (bf16[256,256]{1,0:T(8,128)(2,1)S(1)}, bf16[256,256]{1,0:T(8,128)(2,1)S(1)}, u32[]{:S(2)}, u32[]{:S(2)}) collective-permute-start(bf16[256,256]{1,0:T(8,128)(2,1)S(1)} %collective-permute-done.35.refs_3_), channel_id=1, source_target_pairs={{0,2},{4,0},{8,4},{12,8},{14,12},{10,14},{6,10},{2,6},{1,3},{5,1},... | collective-permute-start | bytes 393224 | tf_op jit(solution)/shard_map/ppermute | solution.py:46
  73.4 1.9 %collective-permute-done.40.refs_1_ = bf16[256,256]{1,0:T(8,128)(2,1)S(1)} collective-permute-done((bf16[256,256]{1,0:T(8,128)(2,1)S(1)}, bf16[256,256]{1,0:T(8,128)(2,1)S(1)}, u32[]{:S(2)}, u32[]{:S(2)}) %collective-permute-start.40) | collective-permute-done | bytes 131104 | tf_op jit(solution)/shard_map/ppermute | solution.py:46
  76.2 1.6 %collective-permute-start.43 = (bf16[256,256]{1,0:T(8,128)(2,1)S(1)}, bf16[256,256]{1,0:T(8,128)(2,1)S(1)}, u32[]{:S(2)}, u32[]{:S(2)}) collective-permute-start(bf16[256,256]{1,0:T(8,128)(2,1)S(1)} %collective-permute-done.41.refs_2_), channel_id=1, source_target_pairs={{0,2},{4,0},{8,4},{12,8},{14,12},{10,14},{6,10},{2,6},{1,3},{5,1},... | collective-permute-start | bytes 393224 | tf_op jit(solution)/shard_map/ppermute | solution.py:46
  77.7 1.5 %collective-permute-start.37 = (bf16[256,256]{1,0:T(8,128)(2,1)S(1)}, bf16[256,256]{1,0:T(8,128)(2,1)S(1)}, u32[]{:S(2)}, u32[]{:S(2)}) collective-permute-start(bf16[256,256]{1,0:T(8,128)(2,1)S(1)} %collective-permute-done.36.refs_7_), channel_id=1, source_target_pairs={{0,2},{4,0},{8,4},{12,8},{14,12},{10,14},{6,10},{2,6},{1,3},{5,1},... | collective-permute-start | bytes 393224 | tf_op jit(solution)/shard_map/ppermute | solution.py:46
  82.7 1.6 %collective-permute-done.33.refs_0_ = bf16[256,256]{1,0:T(8,128)(2,1)S(1)} collective-permute-done((bf16[256,256]{1,0:T(8,128)(2,1)S(1)}, bf16[256,256]{1,0:T(8,128)(2,1)S(1)}, u32[]{:S(2)}, u32[]{:S(2)}) %collective-permute-start.33) | collective-permute-done | bytes 131104 | tf_op jit(solution)/shard_map/ppermute | solution.py:46
  86.5 1.6 %shard_map.103 = f32[1,128,2048]{2,1,0:T(8,128)} custom-call(s32[9]{0:T(128)S(1)} %stack.39.starts, f32[128,256]{1,0:T(8,128)S(1)} %get-tuple-element.88.refs_0_, f32[3,256,256]{2,1,0:T(8,128)S(1)} %get-tuple-element.77.refs_5_.refs_1_, f32[4,256,256]{2,1,0:T(8,128)S(1)} %get-tuple-element.81.refs_6_.refs_2_), custom_call_target="tpu_custom_call" | custom-call | bytes 1024 | tf_op jit(solution)/shard_map/pallas_call | solution.py:59
  88.1 1.3 %collective-permute-done.44.arrived = f32[1536,128]{1,0:T(8,128)S(1)} collective-permute-done((f32[1536,128]{1,0:T(8,128)S(1)}, f32[1536,128]{1,0:T(8,128)S(1)}, u32[]{:S(2)}, u32[]{:S(2)}) %collective-permute-start.44) | collective-permute-done | bytes 786464 | tf_op jit(solution)/shard_map/ppermute | solution.py:23
  89.4 2.7 %shard_map.102 = (f32[1,2048,128]{2,1,0:T(8,128)}, f32[1,128]{1,0:T(1,128)}, f32[128,1024]{1,0:T(8,128)}) custom-call(s32[9]{0:T(128)S(1)} %stack.39.starts, bf16[2048,512]{1,0:T(8,128)(2,1)S(1)} %shard_map.98.turned, f32[512,128]{1,0:T(8,128)S(1)} %get-tuple-element.74.preact, f32[512,128]{1,0:T(8,128)S(1)} %get-tuple-element.83.back_own, ...), custom_call_target="tpu_custom_call" | custom-call | flops 268435456 | bytes 1024 | tf_op jit(solution)/shard_map/pallas_call | solution.py:59
  (91 shorter events, 33.6 us)
Async XLA Ops:
  1.7 6.6 %collective-permute-start.4 = (bf16[256,256]{1,0:T(8,128)(2,1)S(1)}, bf16[256,256]{1,0:T(8,128)(2,1)S(1)}, u32[]{:S(2)}, u32[]{:S(2)}) collective-permute-start(bf16[256,256]{1,0:T(8,128)(2,1)S(1)} %get-tuple-element.47.refs_1_), channel_id=1, source_target_pairs={{0,2},{4,0},{8,4},{12,8},{14,12},{10,14},{6,10},{2,6},{1,3},{5,1},... | collective-permute-start | bytes 393224 | tf_op jit(solution)/shard_map/ppermute | solution.py:46
  4.7 6.4 %collective-permute-start = (bf16[256,256]{1,0:T(8,128)(2,1)S(1)}, bf16[256,256]{1,0:T(8,128)(2,1)S(1)}, u32[]{:S(2)}, u32[]{:S(2)}) collective-permute-start(bf16[256,256]{1,0:T(8,128)(2,1)S(1)} %get-tuple-element.48.refs_0_), channel_id=1, source_target_pairs={{0,4},{4,8},{8,12},{12,14},{14,10},{10,6},{6,2},{2,0},{1,5},{5,9},... | collective-permute-start | bytes 393224 | tf_op jit(solution)/shard_map/ppermute | solution.py:46
  5.6 8.0 %collective-permute-start.8 = (bf16[256,256]{1,0:T(8,128)(2,1)S(1)}, bf16[256,256]{1,0:T(8,128)(2,1)S(1)}, u32[]{:S(2)}, u32[]{:S(2)}) collective-permute-start(bf16[256,256]{1,0:T(8,128)(2,1)S(1)} %get-tuple-element.47.refs_1_), channel_id=1, source_target_pairs={{0,4},{4,8},{8,12},{12,14},{14,10},{10,6},{6,2},{2,0},{1,5},{5,9},... | collective-permute-start | bytes 393224 | tf_op jit(solution)/shard_map/ppermute | solution.py:46
  7.6 6.3 %collective-permute-start.9 = (bf16[256,256]{1,0:T(8,128)(2,1)S(1)}, bf16[256,256]{1,0:T(8,128)(2,1)S(1)}, u32[]{:S(2)}, u32[]{:S(2)}) collective-permute-start(bf16[256,256]{1,0:T(8,128)(2,1)S(1)} %get-tuple-element.48.refs_0_), channel_id=1, source_target_pairs={{0,2},{4,0},{8,4},{12,8},{14,12},{10,14},{6,10},{2,6},{1,3},{5,1},... | collective-permute-start | bytes 393224 | tf_op jit(solution)/shard_map/ppermute | solution.py:46
  8.3 7.4 %collective-permute-start.5 = (bf16[256,256]{1,0:T(8,128)(2,1)S(1)}, bf16[256,256]{1,0:T(8,128)(2,1)S(1)}, u32[]{:S(2)}, u32[]{:S(2)}) collective-permute-start(bf16[256,256]{1,0:T(8,128)(2,1)S(1)} %collective-permute-done.4.refs_5_.refs_3_), channel_id=1, source_target_pairs={{0,2},{4,0},{8,4},{12,8},{14,12},{10,14},{6,10},{2,6},{1,3},{5,1},... | collective-permute-start | bytes 393224 | tf_op jit(solution)/shard_map/ppermute | solution.py:46
  11.1 6.2 %collective-permute-start.1 = (bf16[256,256]{1,0:T(8,128)(2,1)S(1)}, bf16[256,256]{1,0:T(8,128)(2,1)S(1)}, u32[]{:S(2)}, u32[]{:S(2)}) collective-permute-start(bf16[256,256]{1,0:T(8,128)(2,1)S(1)} %collective-permute-done.refs_2_.refs_0_), channel_id=1, source_target_pairs={{0,4},{4,8},{8,12},{12,14},{14,10},{10,6},{6,2},{2,0},{1,5},{5,9},... | collective-permute-start | bytes 393224 | tf_op jit(solution)/shard_map/ppermute | solution.py:46
  11.1 12.9 %collective-permute-start.14 = (bf16[128,1024]{1,0:T(8,128)(2,1)}, bf16[128,1024]{1,0:T(8,128)(2,1)S(1)}, u32[]{:S(2)}, u32[]{:S(2)}) collective-permute-start(bf16[128,1024]{1,0:T(8,128)(2,1)} %param.11), channel_id=1, source_target_pairs={{0,1},{2,3},{4,5},{6,7},{8,9},{10,11},{12,13},{14,15},{16,17},{18,... | collective-permute-start | bytes 786440 | tf_op jit(solution)/shard_map/ppermute | solution.py:23
  13.6 6.3 %collective-permute-start.10 = (bf16[256,256]{1,0:T(8,128)(2,1)S(1)}, bf16[256,256]{1,0:T(8,128)(2,1)S(1)}, u32[]{:S(2)}, u32[]{:S(2)}) collective-permute-start(bf16[256,256]{1,0:T(8,128)(2,1)S(1)} %collective-permute-done.8.refs_3_.refs_1_), channel_id=1, source_target_pairs={{0,4},{4,8},{8,12},{12,14},{14,10},{10,6},{6,2},{2,0},{1,5},{5,9},... | collective-permute-start | bytes 393224 | tf_op jit(solution)/shard_map/ppermute | solution.py:46
  13.9 6.4 %collective-permute-start.11 = (bf16[256,256]{1,0:T(8,128)(2,1)S(1)}, bf16[256,256]{1,0:T(8,128)(2,1)S(1)}, u32[]{:S(2)}, u32[]{:S(2)}) collective-permute-start(bf16[256,256]{1,0:T(8,128)(2,1)S(1)} %collective-permute-done.9.refs_4_.refs_2_), channel_id=1, source_target_pairs={{0,2},{4,0},{8,4},{12,8},{14,12},{10,14},{6,10},{2,6},{1,3},{5,1},... | collective-permute-start | bytes 393224 | tf_op jit(solution)/shard_map/ppermute | solution.py:46
  15.7 6.3 %collective-permute-start.6 = (bf16[256,256]{1,0:T(8,128)(2,1)S(1)}, bf16[256,256]{1,0:T(8,128)(2,1)S(1)}, u32[]{:S(2)}, u32[]{:S(2)}) collective-permute-start(bf16[256,256]{1,0:T(8,128)(2,1)S(1)} %collective-permute-done.5.refs_9_.refs_7_), channel_id=1, source_target_pairs={{0,2},{4,0},{8,4},{12,8},{14,12},{10,14},{6,10},{2,6},{1,3},{5,1},... | collective-permute-start | bytes 393224 | tf_op jit(solution)/shard_map/ppermute | solution.py:46
  17.2 6.5 %collective-permute-start.2 = (bf16[256,256]{1,0:T(8,128)(2,1)S(1)}, bf16[256,256]{1,0:T(8,128)(2,1)S(1)}, u32[]{:S(2)}, u32[]{:S(2)}) collective-permute-start(bf16[256,256]{1,0:T(8,128)(2,1)S(1)} %collective-permute-done.1.refs_6_.refs_4_), channel_id=1, source_target_pairs={{0,4},{4,8},{8,12},{12,14},{14,10},{10,6},{6,2},{2,0},{1,5},{5,9},... | collective-permute-start | bytes 393224 | tf_op jit(solution)/shard_map/ppermute | solution.py:46
  32.5 5.8 %collective-permute-start.18 = (bf16[256,256]{1,0:T(8,128)(2,1)S(1)}, bf16[256,256]{1,0:T(8,128)(2,1)S(1)}, u32[]{:S(2)}, u32[]{:S(2)}) collective-permute-start(bf16[256,256]{1,0:T(8,128)(2,1)S(1)} %get-tuple-element.57), channel_id=1, source_target_pairs={{0,2},{4,0},{8,4},{12,8},{14,12},{10,14},{6,10},{2,6},{1,3},{5,1},... | collective-permute-start | bytes 393224 | tf_op jit(solution)/shard_map/ppermute | solution.py:46
  34.2 6.4 %collective-permute-start.17 = (bf16[256,256]{1,0:T(8,128)(2,1)S(1)}, bf16[256,256]{1,0:T(8,128)(2,1)S(1)}, u32[]{:S(2)}, u32[]{:S(2)}) collective-permute-start(bf16[256,256]{1,0:T(8,128)(2,1)S(1)} %get-tuple-element.56), channel_id=1, source_target_pairs={{0,4},{4,8},{8,12},{12,14},{14,10},{10,6},{6,2},{2,0},{1,5},{5,9},... | collective-permute-start | bytes 393224 | tf_op jit(solution)/shard_map/ppermute | solution.py:46
  35.9 7.1 %collective-permute-start.16 = (bf16[256,256]{1,0:T(8,128)(2,1)S(1)}, bf16[256,256]{1,0:T(8,128)(2,1)S(1)}, u32[]{:S(2)}, u32[]{:S(2)}) collective-permute-start(bf16[256,256]{1,0:T(8,128)(2,1)S(1)} %get-tuple-element.55), channel_id=1, source_target_pairs={{0,4},{4,8},{8,12},{12,14},{14,10},{10,6},{6,2},{2,0},{1,5},{5,9},... | collective-permute-start | bytes 393224 | tf_op jit(solution)/shard_map/ppermute | solution.py:46
  36.2 7.4 %collective-permute-start.27 = (bf16[256,256]{1,0:T(8,128)(2,1)S(1)}, bf16[256,256]{1,0:T(8,128)(2,1)S(1)}, u32[]{:S(2)}, u32[]{:S(2)}) collective-permute-start(bf16[256,256]{1,0:T(8,128)(2,1)S(1)} %get-tuple-element.69), channel_id=1, source_target_pairs={{0,2},{4,0},{8,4},{12,8},{14,12},{10,14},{6,10},{2,6},{1,3},{5,1},... | collective-permute-start | bytes 393224 | tf_op jit(solution)/shard_map/ppermute | solution.py:46
  38.4 6.8 %collective-permute-start.21 = (bf16[256,256]{1,0:T(8,128)(2,1)S(1)}, bf16[256,256]{1,0:T(8,128)(2,1)S(1)}, u32[]{:S(2)}, u32[]{:S(2)}) collective-permute-start(bf16[256,256]{1,0:T(8,128)(2,1)S(1)} %add_convert_fusion.6), channel_id=1, source_target_pairs={{0,2},{4,0},{8,4},{12,8},{14,12},{10,14},{6,10},{2,6},{1,3},{5,1},... | collective-permute-start | bytes 393224 | tf_op jit(solution)/shard_map/ppermute | solution.py:46
  40.6 6.2 %collective-permute-start.20 = (bf16[256,256]{1,0:T(8,128)(2,1)S(1)}, bf16[256,256]{1,0:T(8,128)(2,1)S(1)}, u32[]{:S(2)}, u32[]{:S(2)}) collective-permute-start(bf16[256,256]{1,0:T(8,128)(2,1)S(1)} %add_convert_fusion.7), channel_id=1, source_target_pairs={{0,4},{4,8},{8,12},{12,14},{14,10},{10,6},{6,2},{2,0},{1,5},{5,9},... | collective-permute-start | bytes 393224 | tf_op jit(solution)/shard_map/ppermute | solution.py:46
  43.1 6.3 %collective-permute-start.19 = (bf16[256,256]{1,0:T(8,128)(2,1)S(1)}, bf16[256,256]{1,0:T(8,128)(2,1)S(1)}, u32[]{:S(2)}, u32[]{:S(2)}) collective-permute-start(bf16[256,256]{1,0:T(8,128)(2,1)S(1)} %add_convert_fusion.9), channel_id=1, source_target_pairs={{0,4},{4,8},{8,12},{12,14},{14,10},{10,6},{6,2},{2,0},{1,5},{5,9},... | collective-permute-start | bytes 393224 | tf_op jit(solution)/shard_map/ppermute | solution.py:46
  43.6 6.3 %collective-permute-start.28 = (bf16[256,256]{1,0:T(8,128)(2,1)S(1)}, bf16[256,256]{1,0:T(8,128)(2,1)S(1)}, u32[]{:S(2)}, u32[]{:S(2)}) collective-permute-start(bf16[256,256]{1,0:T(8,128)(2,1)S(1)} %add_convert_fusion.1), channel_id=1, source_target_pairs={{0,2},{4,0},{8,4},{12,8},{14,12},{10,14},{6,10},{2,6},{1,3},{5,1},... | collective-permute-start | bytes 393224 | tf_op jit(solution)/shard_map/ppermute | solution.py:46
  45.3 8.2 %collective-permute-start.23 = (bf16[256,256]{1,0:T(8,128)(2,1)S(1)}, bf16[256,256]{1,0:T(8,128)(2,1)S(1)}, u32[]{:S(2)}, u32[]{:S(2)}) collective-permute-start(bf16[256,256]{1,0:T(8,128)(2,1)S(1)} %add_convert_fusion.5), channel_id=1, source_target_pairs={{0,2},{4,0},{8,4},{12,8},{14,12},{10,14},{6,10},{2,6},{1,3},{5,1},... | collective-permute-start | bytes 393224 | tf_op jit(solution)/shard_map/ppermute | solution.py:46
  46.9 6.0 %collective-permute-start.25 = (bf16[256,256]{1,0:T(8,128)(2,1)S(1)}, bf16[256,256]{1,0:T(8,128)(2,1)S(1)}, u32[]{:S(2)}, u32[]{:S(2)}) collective-permute-start(bf16[256,256]{1,0:T(8,128)(2,1)S(1)} %add_convert_fusion.3), channel_id=1, source_target_pairs={{0,4},{4,8},{8,12},{12,14},{14,10},{10,6},{6,2},{2,0},{1,5},{5,9},... | collective-permute-start | bytes 393224 | tf_op jit(solution)/shard_map/ppermute | solution.py:46
  49.4 8.7 %collective-permute-start.22 = (bf16[256,256]{1,0:T(8,128)(2,1)S(1)}, bf16[256,256]{1,0:T(8,128)(2,1)S(1)}, u32[]{:S(2)}, u32[]{:S(2)}) collective-permute-start(bf16[256,256]{1,0:T(8,128)(2,1)S(1)} %add_convert_fusion.8), channel_id=1, source_target_pairs={{0,4},{4,8},{8,12},{12,14},{14,10},{10,6},{6,2},{2,0},{1,5},{5,9},... | collective-permute-start | bytes 393224 | tf_op jit(solution)/shard_map/ppermute | solution.py:46
  58.7 6.4 %collective-permute-start.34 = (bf16[256,256]{1,0:T(8,128)(2,1)S(1)}, bf16[256,256]{1,0:T(8,128)(2,1)S(1)}, u32[]{:S(2)}, u32[]{:S(2)}) collective-permute-start(bf16[256,256]{1,0:T(8,128)(2,1)S(1)} %multiply_convert_fusion.refs_1_), channel_id=1, source_target_pairs={{0,2},{4,0},{8,4},{12,8},{14,12},{10,14},{6,10},{2,6},{1,3},{5,1},... | collective-permute-start | bytes 393224 | tf_op jit(solution)/shard_map/ppermute | solution.py:46
  60.3 6.4 %collective-permute-start.30 = (bf16[256,256]{1,0:T(8,128)(2,1)S(1)}, bf16[256,256]{1,0:T(8,128)(2,1)S(1)}, u32[]{:S(2)}, u32[]{:S(2)}) collective-permute-start(bf16[256,256]{1,0:T(8,128)(2,1)S(1)} %fusion.1.refs_0_), channel_id=1, source_target_pairs={{0,4},{4,8},{8,12},{12,14},{14,10},{10,6},{6,2},{2,0},{1,5},{5,9},... | collective-permute-start | bytes 393224 | tf_op jit(solution)/shard_map/ppermute | solution.py:46
  60.8 8.5 %collective-permute-start.38 = (bf16[256,256]{1,0:T(8,128)(2,1)S(1)}, bf16[256,256]{1,0:T(8,128)(2,1)S(1)}, u32[]{:S(2)}, u32[]{:S(2)}) collective-permute-start(bf16[256,256]{1,0:T(8,128)(2,1)S(1)} %multiply_convert_fusion.refs_1_), channel_id=1, source_target_pairs={{0,4},{4,8},{8,12},{12,14},{14,10},{10,6},{6,2},{2,0},{1,5},{5,9},... | collective-permute-start | bytes 393224 | tf_op jit(solution)/shard_map/ppermute | solution.py:46
  61.7 8.1 %collective-permute-start.39 = (bf16[256,256]{1,0:T(8,128)(2,1)S(1)}, bf16[256,256]{1,0:T(8,128)(2,1)S(1)}, u32[]{:S(2)}, u32[]{:S(2)}) collective-permute-start(bf16[256,256]{1,0:T(8,128)(2,1)S(1)} %fusion.1.refs_0_), channel_id=1, source_target_pairs={{0,2},{4,0},{8,4},{12,8},{14,12},{10,14},{6,10},{2,6},{1,3},{5,1},... | collective-permute-start | bytes 393224 | tf_op jit(solution)/shard_map/ppermute | solution.py:46
  65.1 6.3 %collective-permute-start.35 = (bf16[256,256]{1,0:T(8,128)(2,1)S(1)}, bf16[256,256]{1,0:T(8,128)(2,1)S(1)}, u32[]{:S(2)}, u32[]{:S(2)}) collective-permute-start(bf16[256,256]{1,0:T(8,128)(2,1)S(1)} %collective-permute-done.34.refs_5_), channel_id=1, source_target_pairs={{0,2},{4,0},{8,4},{12,8},{14,12},{10,14},{6,10},{2,6},{1,3},{5,1},... | collective-permute-start | bytes 393224 | tf_op jit(solution)/shard_map/ppermute | solution.py:46
  66.7 6.2 %collective-permute-start.31 = (bf16[256,256]{1,0:T(8,128)(2,1)S(1)}, bf16[256,256]{1,0:T(8,128)(2,1)S(1)}, u32[]{:S(2)}, u32[]{:S(2)}) collective-permute-start(bf16[256,256]{1,0:T(8,128)(2,1)S(1)} %collective-permute-done.30.refs_2_), channel_id=1, source_target_pairs={{0,4},{4,8},{8,12},{12,14},{14,10},{10,6},{6,2},{2,0},{1,5},{5,9},... | collective-permute-start | bytes 393224 | tf_op jit(solution)/shard_map/ppermute | solution.py:46
  69.3 5.9 %collective-permute-start.40 = (bf16[256,256]{1,0:T(8,128)(2,1)S(1)}, bf16[256,256]{1,0:T(8,128)(2,1)S(1)}, u32[]{:S(2)}, u32[]{:S(2)}) collective-permute-start(bf16[256,256]{1,0:T(8,128)(2,1)S(1)} %collective-permute-done.38.refs_3_), channel_id=1, source_target_pairs={{0,4},{4,8},{8,12},{12,14},{14,10},{10,6},{6,2},{2,0},{1,5},{5,9},... | collective-permute-start | bytes 393224 | tf_op jit(solution)/shard_map/ppermute | solution.py:46
  69.8 6.3 %collective-permute-start.41 = (bf16[256,256]{1,0:T(8,128)(2,1)S(1)}, bf16[256,256]{1,0:T(8,128)(2,1)S(1)}, u32[]{:S(2)}, u32[]{:S(2)}) collective-permute-start(bf16[256,256]{1,0:T(8,128)(2,1)S(1)} %collective-permute-done.39.refs_4_), channel_id=1, source_target_pairs={{0,2},{4,0},{8,4},{12,8},{14,12},{10,14},{6,10},{2,6},{1,3},{5,1},... | collective-permute-start | bytes 393224 | tf_op jit(solution)/shard_map/ppermute | solution.py:46
  71.3 6.4 %collective-permute-start.36 = (bf16[256,256]{1,0:T(8,128)(2,1)S(1)}, bf16[256,256]{1,0:T(8,128)(2,1)S(1)}, u32[]{:S(2)}, u32[]{:S(2)}) collective-permute-start(bf16[256,256]{1,0:T(8,128)(2,1)S(1)} %collective-permute-done.35.refs_3_), channel_id=1, source_target_pairs={{0,2},{4,0},{8,4},{12,8},{14,12},{10,14},{6,10},{2,6},{1,3},{5,1},... | collective-permute-start | bytes 393224 | tf_op jit(solution)/shard_map/ppermute | solution.py:46
  72.9 6.3 %collective-permute-start.32 = (bf16[256,256]{1,0:T(8,128)(2,1)S(1)}, bf16[256,256]{1,0:T(8,128)(2,1)S(1)}, u32[]{:S(2)}, u32[]{:S(2)}) collective-permute-start(bf16[256,256]{1,0:T(8,128)(2,1)S(1)} %collective-permute-done.31.refs_0_), channel_id=1, source_target_pairs={{0,4},{4,8},{8,12},{12,14},{14,10},{10,6},{6,2},{2,0},{1,5},{5,9},... | collective-permute-start | bytes 393224 | tf_op jit(solution)/shard_map/ppermute | solution.py:46
  (16 other events, 121.3 us)

commit v11 on v10

--- a/solution.py
+++ b/solution.py
@@ -41,9 +41,14 @@
 
 
 def hop(shard, way):
-    size = lax.axis_size("latent")
+    size, layers = lax.axis_size("latent"), lax.axis_size("layer")
     order = ring_order(size)
-    return lax.ppermute(shard, "latent", [(order[p], order[(p + way) % size]) for p in range(size)])
+    pairs = []
+    for p in range(size):
+        for layer in range(layers):
+            by = way if layer % 2 == 0 else -way
+            pairs.append((order[p] * layers + layer, order[(p + by) % size] * layers + layer))
+    return lax.ppermute(shard, ("latent", "layer"), pairs)
 
 
 def after(value, *others):
@@ -220,6 +225,7 @@
     reach = size // 2
     place = ring_place(lax.axis_index("latent"), size)
     layer = lax.axis_index("layer")
+    sign = jnp.where(layer % 2 == 0, 1, -1)
     rows, wide = residual_in.shape[1:]
     half = rows // 2
     deep, lat = enc_weight.shape[1:]
@@ -240,10 +246,10 @@
     for s in range(1, reach):
         offsets[slot_p[s]] = -s
         offsets[slot_q[s]] = s
-    starts = jnp.stack([ring_member(place + offset, size) * wide for offset in offsets] + [layer])
+    starts = jnp.stack([ring_member(place + sign * offset, size) * wide for offset in offsets] + [layer])
     starts = starts.astype(jnp.int32)
 
-    urgent, later = ((0, 1), (1, -1)), ((0, -1), (1, 1))
+    urgent, later = ((0, 1), (1, -1)), ((1, 1), (0, -1))
 
     def gather_step(found, s, ready=None):
         for chain, way in urgent + later if s < reach else urgent:

time: 92.3 us -> 91.6 us (level)
  transfers between devices with their start and end apart: 45 -> 45, of which waited for: 23 -> 26; matrix products, arithmetic and copies ran while one was open for 2% -> 2% of each run, Pallas kernels for 9% -> 9%
where the time goes in v11:
time: 91.6 us; the launch traced here: 91.4 us
  starting transfers between devices  48.2 us (53%)
  waiting for transfers between devices  26.1 us (28%)
  Pallas kernels  13.3 us (15%)
  other arithmetic  1.63 us (2%)
  local copies, waits for them, and re-layouts  1.15 us (1%)
    ppermute x42, starting transfers between devices, hop(): return lax.ppermute(shard, ('latent', 'layer'), pairs)  44.4 us
    ppermute x42, waiting for transfers between devices, hop(): return lax.ppermute(shard, ('latent', 'layer'), pairs)  23.8 us
    pallas_call x11, Pallas kernels, call(): pl.pallas_call(kernel, out_shape=outs, in_specs=[spec(pltpu.SMEM)] + [spe...  13.3 us
    ppermute x3, starting transfers between devices, passed_along(): return lax.ppermute(shard, axis, pairs)  3.89 us
    ppermute x3, waiting for transfers between devices, passed_along(): return lax.ppermute(shard, axis, pairs)  2.27 us
  transfers between devices with their start and end apart: 45, of which 26 were waited for; matrix products, arithmetic and copies ran while one was open for 2% of the time, Pallas kernels for 9%

profile of v11, /device:TPU:0, one launch (start us, length us, event | category | flops | bytes accessed | tf_op | source)
XLA Modules:
  0.0 91.4 jit_solution(12334494121395451928)
XLA Ops:
  1.7 3.0 %collective-permute-start.4 = (bf16[256,256]{1,0:T(8,128)(2,1)S(1)}, bf16[256,256]{1,0:T(8,128)(2,1)S(1)}, u32[]{:S(2)}, u32[]{:S(2)}) collective-permute-start(bf16[256,256]{1,0:T(8,128)(2,1)S(1)} %get-tuple-element.47.refs_1_), channel_id=1, source_target_pairs={{0,2},{1,5},{4,0},{5,9},{8,4},{9,13},{12,8},{13,15},{14,12},{15,11... | collective-permute-start | bytes 393224 | tf_op jit(solution)/shard_map/ppermute | solution.py:51
  5.6 2.0 %collective-permute-start.8 = (bf16[256,256]{1,0:T(8,128)(2,1)S(1)}, bf16[256,256]{1,0:T(8,128)(2,1)S(1)}, u32[]{:S(2)}, u32[]{:S(2)}) collective-permute-start(bf16[256,256]{1,0:T(8,128)(2,1)S(1)} %get-tuple-element.47.refs_1_), channel_id=1, source_target_pairs={{0,4},{1,3},{4,8},{5,1},{8,12},{9,5},{12,14},{13,9},{14,10},{15,13... | collective-permute-start | bytes 393224 | tf_op jit(solution)/shard_map/ppermute | solution.py:51
  8.6 2.1 %collective-permute-start.5 = (bf16[256,256]{1,0:T(8,128)(2,1)S(1)}, bf16[256,256]{1,0:T(8,128)(2,1)S(1)}, u32[]{:S(2)}, u32[]{:S(2)}) collective-permute-start(bf16[256,256]{1,0:T(8,128)(2,1)S(1)} %collective-permute-done.4.refs_5_.refs_3_), channel_id=1, source_target_pairs={{0,2},{1,5},{4,0},{5,9},{8,4},{9,13},{12,8},{13,15},{14,12},{15,11... | collective-permute-start | bytes 393224 | tf_op jit(solution)/shard_map/ppermute | solution.py:51
  11.0 1.3 %collective-permute-start.14 = (bf16[128,1024]{1,0:T(8,128)(2,1)}, bf16[128,1024]{1,0:T(8,128)(2,1)S(1)}, u32[]{:S(2)}, u32[]{:S(2)}) collective-permute-start(bf16[128,1024]{1,0:T(8,128)(2,1)} %param.11), channel_id=1, source_target_pairs={{0,1},{2,3},{4,5},{6,7},{8,9},{10,11},{12,13},{14,15},{16,17},{18,... | collective-permute-start | bytes 786440 | tf_op jit(solution)/shard_map/ppermute | solution.py:23
  13.0 1.3 %collective-permute-start.10 = (bf16[256,256]{1,0:T(8,128)(2,1)S(1)}, bf16[256,256]{1,0:T(8,128)(2,1)S(1)}, u32[]{:S(2)}, u32[]{:S(2)}) collective-permute-start(bf16[256,256]{1,0:T(8,128)(2,1)S(1)} %collective-permute-done.8.refs_3_.refs_1_), channel_id=1, source_target_pairs={{0,4},{1,3},{4,8},{5,1},{8,12},{9,5},{12,14},{13,9},{14,10},{15,13... | collective-permute-start | bytes 393224 | tf_op jit(solution)/shard_map/ppermute | solution.py:51
  16.8 1.3 %collective-permute-start.2 = (bf16[256,256]{1,0:T(8,128)(2,1)S(1)}, bf16[256,256]{1,0:T(8,128)(2,1)S(1)}, u32[]{:S(2)}, u32[]{:S(2)}) collective-permute-start(bf16[256,256]{1,0:T(8,128)(2,1)S(1)} %collective-permute-done.1.refs_6_.refs_4_), channel_id=1, source_target_pairs={{0,4},{1,3},{4,8},{5,1},{8,12},{9,5},{12,14},{13,9},{14,10},{15,13... | collective-permute-start | bytes 393224 | tf_op jit(solution)/shard_map/ppermute | solution.py:51
  18.1 1.4 %collective-permute-done.10.refs_7_.refs_5_ = bf16[256,256]{1,0:T(8,128)(2,1)S(1)} collective-permute-done((bf16[256,256]{1,0:T(8,128)(2,1)S(1)}, bf16[256,256]{1,0:T(8,128)(2,1)S(1)}, u32[]{:S(2)}, u32[]{:S(2)}) %collective-permute-start.10) | collective-permute-done | bytes 131104 | tf_op jit(solution)/shard_map/ppermute | solution.py:51
  21.5 1.9 %collective-permute-done.6.refs_13_.refs_11_ = bf16[256,256]{1,0:T(8,128)(2,1)S(1)} collective-permute-done((bf16[256,256]{1,0:T(8,128)(2,1)S(1)}, bf16[256,256]{1,0:T(8,128)(2,1)S(1)}, u32[]{:S(2)}, u32[]{:S(2)}) %collective-permute-start.6) | collective-permute-done | bytes 131104 | tf_op jit(solution)/shard_map/ppermute | solution.py:51
  24.0 1.5 %collective-permute-start.3 = (bf16[256,256]{1,0:T(8,128)(2,1)S(1)}, bf16[256,256]{1,0:T(8,128)(2,1)S(1)}, u32[]{:S(2)}, u32[]{:S(2)}) collective-permute-start(bf16[256,256]{1,0:T(8,128)(2,1)S(1)} %collective-permute-done.2.refs_10_.refs_8_), channel_id=1, source_target_pairs={{0,4},{1,3},{4,8},{5,1},{8,12},{9,5},{12,14},{13,9},{14,10},{15,13... | collective-permute-start | bytes 393224 | tf_op jit(solution)/shard_map/ppermute | solution.py:51
  29.7 1.3 %collective-permute-start.15 = (bf16[512,128]{1,0:T(8,128)(2,1)S(1)}, bf16[512,128]{1,0:T(8,128)(2,1)S(1)}, u32[]{:S(2)}, u32[]{:S(2)}) collective-permute-start(bf16[512,128]{1,0:T(8,128)(2,1)S(1)} %get-tuple-element.51.codes), channel_id=1, source_target_pairs={{0,1},{2,3},{4,5},{6,7},{8,9},{10,11},{12,13},{14,15},{16,17},{18,... | collective-permute-start | bytes 393224 | tf_op jit(solution)/shard_map/ppermute | solution.py:23
  32.7 1.6 %collective-permute-start.18 = (bf16[256,256]{1,0:T(8,128)(2,1)S(1)}, bf16[256,256]{1,0:T(8,128)(2,1)S(1)}, u32[]{:S(2)}, u32[]{:S(2)}) collective-permute-start(bf16[256,256]{1,0:T(8,128)(2,1)S(1)} %get-tuple-element.57), channel_id=1, source_target_pairs={{0,2},{1,5},{4,0},{5,9},{8,4},{9,13},{12,8},{13,15},{14,12},{15,11... | collective-permute-start | bytes 393224 | tf_op jit(solution)/shard_map/ppermute | solution.py:51
  36.1 1.5 %collective-permute-start.16 = (bf16[256,256]{1,0:T(8,128)(2,1)S(1)}, bf16[256,256]{1,0:T(8,128)(2,1)S(1)}, u32[]{:S(2)}, u32[]{:S(2)}) collective-permute-start(bf16[256,256]{1,0:T(8,128)(2,1)S(1)} %get-tuple-element.55), channel_id=1, source_target_pairs={{0,4},{1,3},{4,8},{5,1},{8,12},{9,5},{12,14},{13,9},{14,10},{15,13... | collective-permute-start | bytes 393224 | tf_op jit(solution)/shard_map/ppermute | solution.py:51
  38.6 2.1 %collective-permute-start.21 = (bf16[256,256]{1,0:T(8,128)(2,1)S(1)}, bf16[256,256]{1,0:T(8,128)(2,1)S(1)}, u32[]{:S(2)}, u32[]{:S(2)}) collective-permute-start(bf16[256,256]{1,0:T(8,128)(2,1)S(1)} %add_convert_fusion.6), channel_id=1, source_target_pairs={{0,2},{1,5},{4,0},{5,9},{8,4},{9,13},{12,8},{13,15},{14,12},{15,11... | collective-permute-start | bytes 393224 | tf_op jit(solution)/shard_map/ppermute | solution.py:51
  40.7 1.7 %collective-permute-done.16 = bf16[256,256]{1,0:T(8,128)(2,1)S(1)} collective-permute-done((bf16[256,256]{1,0:T(8,128)(2,1)S(1)}, bf16[256,256]{1,0:T(8,128)(2,1)S(1)}, u32[]{:S(2)}, u32[]{:S(2)}) %collective-permute-start.16) | collective-permute-done | bytes 131104 | tf_op jit(solution)/shard_map/ppermute | solution.py:51
  42.4 1.6 %collective-permute-start.19 = (bf16[256,256]{1,0:T(8,128)(2,1)S(1)}, bf16[256,256]{1,0:T(8,128)(2,1)S(1)}, u32[]{:S(2)}, u32[]{:S(2)}) collective-permute-start(bf16[256,256]{1,0:T(8,128)(2,1)S(1)} %add_convert_fusion.9), channel_id=1, source_target_pairs={{0,4},{1,3},{4,8},{5,1},{8,12},{9,5},{12,14},{13,9},{14,10},{15,13... | collective-permute-start | bytes 393224 | tf_op jit(solution)/shard_map/ppermute | solution.py:51
  44.6 1.4 %collective-permute-done.21 = bf16[256,256]{1,0:T(8,128)(2,1)S(1)} collective-permute-done((bf16[256,256]{1,0:T(8,128)(2,1)S(1)}, bf16[256,256]{1,0:T(8,128)(2,1)S(1)}, u32[]{:S(2)}, u32[]{:S(2)}) %collective-permute-start.21) | collective-permute-done | bytes 131104 | tf_op jit(solution)/shard_map/ppermute | solution.py:51
  48.9 1.5 %collective-permute-start.22 = (bf16[256,256]{1,0:T(8,128)(2,1)S(1)}, bf16[256,256]{1,0:T(8,128)(2,1)S(1)}, u32[]{:S(2)}, u32[]{:S(2)}) collective-permute-start(bf16[256,256]{1,0:T(8,128)(2,1)S(1)} %add_convert_fusion.8), channel_id=1, source_target_pairs={{0,4},{1,3},{4,8},{5,1},{8,12},{9,5},{12,14},{13,9},{14,10},{15,13... | collective-permute-start | bytes 393224 | tf_op jit(solution)/shard_map/ppermute | solution.py:51
  51.1 2.4 %collective-permute-done.25 = bf16[256,256]{1,0:T(8,128)(2,1)S(1)} collective-permute-done((bf16[256,256]{1,0:T(8,128)(2,1)S(1)}, bf16[256,256]{1,0:T(8,128)(2,1)S(1)}, u32[]{:S(2)}, u32[]{:S(2)}) %collective-permute-start.25) | collective-permute-done | bytes 131104 | tf_op jit(solution)/shard_map/ppermute | solution.py:51
  54.4 1.3 %collective-permute-start.24 = (bf16[256,256]{1,0:T(8,128)(2,1)S(1)}, bf16[256,256]{1,0:T(8,128)(2,1)S(1)}, u32[]{:S(2)}, u32[]{:S(2)}) collective-permute-start(bf16[256,256]{1,0:T(8,128)(2,1)S(1)} %add_convert_fusion.4), channel_id=1, source_target_pairs={{0,2},{1,5},{4,0},{5,9},{8,4},{9,13},{12,8},{13,15},{14,12},{15,11... | collective-permute-start | bytes 393224 | tf_op jit(solution)/shard_map/ppermute | solution.py:51
  56.0 2.6 %collective-permute-done.26 = bf16[256,256]{1,0:T(8,128)(2,1)S(1)} collective-permute-done((bf16[256,256]{1,0:T(8,128)(2,1)S(1)}, bf16[256,256]{1,0:T(8,128)(2,1)S(1)}, u32[]{:S(2)}, u32[]{:S(2)}) %collective-permute-start.26) | collective-permute-done | bytes 131104 | tf_op jit(solution)/shard_map/ppermute | solution.py:51
  59.5 1.3 %collective-permute-start.34 = (bf16[256,256]{1,0:T(8,128)(2,1)S(1)}, bf16[256,256]{1,0:T(8,128)(2,1)S(1)}, u32[]{:S(2)}, u32[]{:S(2)}) collective-permute-start(bf16[256,256]{1,0:T(8,128)(2,1)S(1)} %multiply_convert_fusion.refs_1_), channel_id=1, source_target_pairs={{0,2},{1,5},{4,0},{5,9},{8,4},{9,13},{12,8},{13,15},{14,12},{15,11... | collective-permute-start | bytes 393224 | tf_op jit(solution)/shard_map/ppermute | solution.py:51
  61.6 1.7 %collective-permute-start.38 = (bf16[256,256]{1,0:T(8,128)(2,1)S(1)}, bf16[256,256]{1,0:T(8,128)(2,1)S(1)}, u32[]{:S(2)}, u32[]{:S(2)}) collective-permute-start(bf16[256,256]{1,0:T(8,128)(2,1)S(1)} %multiply_convert_fusion.refs_1_), channel_id=1, source_target_pairs={{0,4},{1,3},{4,8},{5,1},{8,12},{9,5},{12,14},{13,9},{14,10},{15,13... | collective-permute-start | bytes 393224 | tf_op jit(solution)/shard_map/ppermute | solution.py:51
  63.6 1.9 %collective-permute-done.34.refs_5_ = bf16[256,256]{1,0:T(8,128)(2,1)S(1)} collective-permute-done((bf16[256,256]{1,0:T(8,128)(2,1)S(1)}, bf16[256,256]{1,0:T(8,128)(2,1)S(1)}, u32[]{:S(2)}, u32[]{:S(2)}) %collective-permute-start.34) | collective-permute-done | bytes 131104 | tf_op jit(solution)/shard_map/ppermute | solution.py:51
  65.5 1.4 %collective-permute-start.35 = (bf16[256,256]{1,0:T(8,128)(2,1)S(1)}, bf16[256,256]{1,0:T(8,128)(2,1)S(1)}, u32[]{:S(2)}, u32[]{:S(2)}) collective-permute-start(bf16[256,256]{1,0:T(8,128)(2,1)S(1)} %collective-permute-done.34.refs_5_), channel_id=1, source_target_pairs={{0,2},{1,5},{4,0},{5,9},{8,4},{9,13},{12,8},{13,15},{14,12},{15,11... | collective-permute-start | bytes 393224 | tf_op jit(solution)/shard_map/ppermute | solution.py:51
  68.6 1.9 %collective-permute-start.40 = (bf16[256,256]{1,0:T(8,128)(2,1)S(1)}, bf16[256,256]{1,0:T(8,128)(2,1)S(1)}, u32[]{:S(2)}, u32[]{:S(2)}) collective-permute-start(bf16[256,256]{1,0:T(8,128)(2,1)S(1)} %collective-permute-done.38.refs_3_), channel_id=1, source_target_pairs={{0,4},{1,3},{4,8},{5,1},{8,12},{9,5},{12,14},{13,9},{14,10},{15,13... | collective-permute-start | bytes 393224 | tf_op jit(solution)/shard_map/ppermute | solution.py:51
  75.0 1.8 %collective-permute-start.42 = (bf16[256,256]{1,0:T(8,128)(2,1)S(1)}, bf16[256,256]{1,0:T(8,128)(2,1)S(1)}, u32[]{:S(2)}, u32[]{:S(2)}) collective-permute-start(bf16[256,256]{1,0:T(8,128)(2,1)S(1)} %collective-permute-done.40.refs_1_), channel_id=1, source_target_pairs={{0,4},{1,3},{4,8},{5,1},{8,12},{9,5},{12,14},{13,9},{14,10},{15,13... | collective-permute-start | bytes 393224 | tf_op jit(solution)/shard_map/ppermute | solution.py:51
  78.5 1.7 %collective-permute-start.33 = (bf16[256,256]{1,0:T(8,128)(2,1)S(1)}, bf16[256,256]{1,0:T(8,128)(2,1)S(1)}, u32[]{:S(2)}, u32[]{:S(2)}) collective-permute-start(bf16[256,256]{1,0:T(8,128)(2,1)S(1)} %collective-permute-done.32.refs_4_), channel_id=1, source_target_pairs={{0,4},{1,3},{4,8},{5,1},{8,12},{9,5},{12,14},{13,9},{14,10},{15,13... | collective-permute-start | bytes 393224 | tf_op jit(solution)/shard_map/ppermute | solution.py:51
  81.8 1.3 %shard_map.100 = (f32[4,256,256]{2,1,0:T(8,128)S(1)}, f32[2,256,256]{2,1,0:T(8,128)S(1)}) custom-call(s32[9]{0:T(128)S(1)} %stack.39.starts, bf16[256,256]{1,0:T(8,128)(2,1)S(1)} %collective-permute-done.31.refs_0_, bf16[256,256]{1,0:T(8,128)(2,1)S(1)} %collective-permute-done.40.refs_1_, bf16[256,256]{1,0:T(8,128)(2,1)S(1)} %collective-permute-done.41.refs_2_, ...), custom_call_target="tpu_custom_call" | custom-call | flops 268435456 | bytes 1024 | tf_op jit(solution)/shard_map/pallas_call | solution.py:64
  84.5 1.3 %collective-permute-start.44 = (f32[1536,128]{1,0:T(8,128)S(1)}, f32[1536,128]{1,0:T(8,128)S(1)}, u32[]{:S(2)}, u32[]{:S(2)}) collective-permute-start(f32[1536,128]{1,0:T(8,128)S(1)} %get-tuple-element.84), channel_id=1, source_target_pairs={{1,0},{3,2},{5,4},{7,6},{9,8},{11,10},{13,12},{15,14},{17,16},{19,... | collective-permute-start | bytes 2359304 | tf_op jit(solution)/shard_map/ppermute | solution.py:23
  85.8 1.6 %shard_map.103 = f32[1,128,2048]{2,1,0:T(8,128)} custom-call(s32[9]{0:T(128)S(1)} %stack.39.starts, f32[128,256]{1,0:T(8,128)S(1)} %get-tuple-element.88.refs_0_, f32[3,256,256]{2,1,0:T(8,128)S(1)} %get-tuple-element.77.refs_5_.refs_1_, f32[4,256,256]{2,1,0:T(8,128)S(1)} %get-tuple-element.81.refs_6_.refs_2_), custom_call_target="tpu_custom_call" | custom-call | bytes 1024 | tf_op jit(solution)/shard_map/pallas_call | solution.py:64
  87.3 1.3 %collective-permute-done.44.arrived = f32[1536,128]{1,0:T(8,128)S(1)} collective-permute-done((f32[1536,128]{1,0:T(8,128)S(1)}, f32[1536,128]{1,0:T(8,128)S(1)}, u32[]{:S(2)}, u32[]{:S(2)}) %collective-permute-start.44) | collective-permute-done | bytes 786464 | tf_op jit(solution)/shard_map/ppermute | solution.py:23
  88.6 2.7 %shard_map.102 = (f32[1,2048,128]{2,1,0:T(8,128)}, f32[1,128]{1,0:T(1,128)}, f32[128,1024]{1,0:T(8,128)}) custom-call(s32[9]{0:T(128)S(1)} %stack.39.starts, bf16[2048,512]{1,0:T(8,128)(2,1)S(1)} %shard_map.98.turned, f32[512,128]{1,0:T(8,128)S(1)} %get-tuple-element.74.preact, f32[512,128]{1,0:T(8,128)S(1)} %get-tuple-element.83.back_own, ...), custom_call_target="tpu_custom_call" | custom-call | flops 268435456 | bytes 1024 | tf_op jit(solution)/shard_map/pallas_call | solution.py:64
  (91 shorter events, 35.9 us)
Async XLA Ops:
  1.7 6.9 %collective-permute-start.4 = (bf16[256,256]{1,0:T(8,128)(2,1)S(1)}, bf16[256,256]{1,0:T(8,128)(2,1)S(1)}, u32[]{:S(2)}, u32[]{:S(2)}) collective-permute-start(bf16[256,256]{1,0:T(8,128)(2,1)S(1)} %get-tuple-element.47.refs_1_), channel_id=1, source_target_pairs={{0,2},{1,5},{4,0},{5,9},{8,4},{9,13},{12,8},{13,15},{14,12},{15,11... | collective-permute-start | bytes 393224 | tf_op jit(solution)/shard_map/ppermute | solution.py:51
  5.6 7.4 %collective-permute-start.8 = (bf16[256,256]{1,0:T(8,128)(2,1)S(1)}, bf16[256,256]{1,0:T(8,128)(2,1)S(1)}, u32[]{:S(2)}, u32[]{:S(2)}) collective-permute-start(bf16[256,256]{1,0:T(8,128)(2,1)S(1)} %get-tuple-element.47.refs_1_), channel_id=1, source_target_pairs={{0,4},{1,3},{4,8},{5,1},{8,12},{9,5},{12,14},{13,9},{14,10},{15,13... | collective-permute-start | bytes 393224 | tf_op jit(solution)/shard_map/ppermute | solution.py:51
  7.6 6.8 %collective-permute-start.9 = (bf16[256,256]{1,0:T(8,128)(2,1)S(1)}, bf16[256,256]{1,0:T(8,128)(2,1)S(1)}, u32[]{:S(2)}, u32[]{:S(2)}) collective-permute-start(bf16[256,256]{1,0:T(8,128)(2,1)S(1)} %get-tuple-element.48.refs_0_), channel_id=1, source_target_pairs={{0,2},{1,5},{4,0},{5,9},{8,4},{9,13},{12,8},{13,15},{14,12},{15,11... | collective-permute-start | bytes 393224 | tf_op jit(solution)/shard_map/ppermute | solution.py:51
  8.6 7.5 %collective-permute-start.5 = (bf16[256,256]{1,0:T(8,128)(2,1)S(1)}, bf16[256,256]{1,0:T(8,128)(2,1)S(1)}, u32[]{:S(2)}, u32[]{:S(2)}) collective-permute-start(bf16[256,256]{1,0:T(8,128)(2,1)S(1)} %collective-permute-done.4.refs_5_.refs_3_), channel_id=1, source_target_pairs={{0,2},{1,5},{4,0},{5,9},{8,4},{9,13},{12,8},{13,15},{14,12},{15,11... | collective-permute-start | bytes 393224 | tf_op jit(solution)/shard_map/ppermute | solution.py:51
  10.6 6.2 %collective-permute-start.1 = (bf16[256,256]{1,0:T(8,128)(2,1)S(1)}, bf16[256,256]{1,0:T(8,128)(2,1)S(1)}, u32[]{:S(2)}, u32[]{:S(2)}) collective-permute-start(bf16[256,256]{1,0:T(8,128)(2,1)S(1)} %collective-permute-done.refs_2_.refs_0_), channel_id=1, source_target_pairs={{0,4},{1,3},{4,8},{5,1},{8,12},{9,5},{12,14},{13,9},{14,10},{15,13... | collective-permute-start | bytes 393224 | tf_op jit(solution)/shard_map/ppermute | solution.py:51
  11.0 14.4 %collective-permute-start.14 = (bf16[128,1024]{1,0:T(8,128)(2,1)}, bf16[128,1024]{1,0:T(8,128)(2,1)S(1)}, u32[]{:S(2)}, u32[]{:S(2)}) collective-permute-start(bf16[128,1024]{1,0:T(8,128)(2,1)} %param.11), channel_id=1, source_target_pairs={{0,1},{2,3},{4,5},{6,7},{8,9},{10,11},{12,13},{14,15},{16,17},{18,... | collective-permute-start | bytes 786440 | tf_op jit(solution)/shard_map/ppermute | solution.py:23
  13.0 6.4 %collective-permute-start.10 = (bf16[256,256]{1,0:T(8,128)(2,1)S(1)}, bf16[256,256]{1,0:T(8,128)(2,1)S(1)}, u32[]{:S(2)}, u32[]{:S(2)}) collective-permute-start(bf16[256,256]{1,0:T(8,128)(2,1)S(1)} %collective-permute-done.8.refs_3_.refs_1_), channel_id=1, source_target_pairs={{0,4},{1,3},{4,8},{5,1},{8,12},{9,5},{12,14},{13,9},{14,10},{15,13... | collective-permute-start | bytes 393224 | tf_op jit(solution)/shard_map/ppermute | solution.py:51
  14.4 6.3 %collective-permute-start.11 = (bf16[256,256]{1,0:T(8,128)(2,1)S(1)}, bf16[256,256]{1,0:T(8,128)(2,1)S(1)}, u32[]{:S(2)}, u32[]{:S(2)}) collective-permute-start(bf16[256,256]{1,0:T(8,128)(2,1)S(1)} %collective-permute-done.9.refs_4_.refs_2_), channel_id=1, source_target_pairs={{0,2},{1,5},{4,0},{5,9},{8,4},{9,13},{12,8},{13,15},{14,12},{15,11... | collective-permute-start | bytes 393224 | tf_op jit(solution)/shard_map/ppermute | solution.py:51
  16.0 7.4 %collective-permute-start.6 = (bf16[256,256]{1,0:T(8,128)(2,1)S(1)}, bf16[256,256]{1,0:T(8,128)(2,1)S(1)}, u32[]{:S(2)}, u32[]{:S(2)}) collective-permute-start(bf16[256,256]{1,0:T(8,128)(2,1)S(1)} %collective-permute-done.5.refs_9_.refs_7_), channel_id=1, source_target_pairs={{0,2},{1,5},{4,0},{5,9},{8,4},{9,13},{12,8},{13,15},{14,12},{15,11... | collective-permute-start | bytes 393224 | tf_op jit(solution)/shard_map/ppermute | solution.py:51
  16.8 7.2 %collective-permute-start.2 = (bf16[256,256]{1,0:T(8,128)(2,1)S(1)}, bf16[256,256]{1,0:T(8,128)(2,1)S(1)}, u32[]{:S(2)}, u32[]{:S(2)}) collective-permute-start(bf16[256,256]{1,0:T(8,128)(2,1)S(1)} %collective-permute-done.1.refs_6_.refs_4_), channel_id=1, source_target_pairs={{0,4},{1,3},{4,8},{5,1},{8,12},{9,5},{12,14},{13,9},{14,10},{15,13... | collective-permute-start | bytes 393224 | tf_op jit(solution)/shard_map/ppermute | solution.py:51
  19.5 7.2 %collective-permute-start.12 = (bf16[256,256]{1,0:T(8,128)(2,1)S(1)}, bf16[256,256]{1,0:T(8,128)(2,1)S(1)}, u32[]{:S(2)}, u32[]{:S(2)}) collective-permute-start(bf16[256,256]{1,0:T(8,128)(2,1)S(1)} %collective-permute-done.10.refs_7_.refs_5_), channel_id=1, source_target_pairs={{0,4},{1,3},{4,8},{5,1},{8,12},{9,5},{12,14},{13,9},{14,10},{15,13... | collective-permute-start | bytes 393224 | tf_op jit(solution)/shard_map/ppermute | solution.py:51
  20.7 6.0 %collective-permute-start.13 = (bf16[256,256]{1,0:T(8,128)(2,1)S(1)}, bf16[256,256]{1,0:T(8,128)(2,1)S(1)}, u32[]{:S(2)}, u32[]{:S(2)}) collective-permute-start(bf16[256,256]{1,0:T(8,128)(2,1)S(1)} %collective-permute-done.11.refs_8_.refs_6_), channel_id=1, source_target_pairs={{0,2},{1,5},{4,0},{5,9},{8,4},{9,13},{12,8},{13,15},{14,12},{15,11... | collective-permute-start | bytes 393224 | tf_op jit(solution)/shard_map/ppermute | solution.py:51
  34.4 6.3 %collective-permute-start.17 = (bf16[256,256]{1,0:T(8,128)(2,1)S(1)}, bf16[256,256]{1,0:T(8,128)(2,1)S(1)}, u32[]{:S(2)}, u32[]{:S(2)}) collective-permute-start(bf16[256,256]{1,0:T(8,128)(2,1)S(1)} %get-tuple-element.56), channel_id=1, source_target_pairs={{0,4},{1,3},{4,8},{5,1},{8,12},{9,5},{12,14},{13,9},{14,10},{15,13... | collective-permute-start | bytes 393224 | tf_op jit(solution)/shard_map/ppermute | solution.py:51
  36.1 6.3 %collective-permute-start.16 = (bf16[256,256]{1,0:T(8,128)(2,1)S(1)}, bf16[256,256]{1,0:T(8,128)(2,1)S(1)}, u32[]{:S(2)}, u32[]{:S(2)}) collective-permute-start(bf16[256,256]{1,0:T(8,128)(2,1)S(1)} %get-tuple-element.55), channel_id=1, source_target_pairs={{0,4},{1,3},{4,8},{5,1},{8,12},{9,5},{12,14},{13,9},{14,10},{15,13... | collective-permute-start | bytes 393224 | tf_op jit(solution)/shard_map/ppermute | solution.py:51
  37.6 6.4 %collective-permute-start.27 = (bf16[256,256]{1,0:T(8,128)(2,1)S(1)}, bf16[256,256]{1,0:T(8,128)(2,1)S(1)}, u32[]{:S(2)}, u32[]{:S(2)}) collective-permute-start(bf16[256,256]{1,0:T(8,128)(2,1)S(1)} %get-tuple-element.69), channel_id=1, source_target_pairs={{0,2},{1,5},{4,0},{5,9},{8,4},{9,13},{12,8},{13,15},{14,12},{15,11... | collective-permute-start | bytes 393224 | tf_op jit(solution)/shard_map/ppermute | solution.py:51
  38.6 7.5 %collective-permute-start.21 = (bf16[256,256]{1,0:T(8,128)(2,1)S(1)}, bf16[256,256]{1,0:T(8,128)(2,1)S(1)}, u32[]{:S(2)}, u32[]{:S(2)}) collective-permute-start(bf16[256,256]{1,0:T(8,128)(2,1)S(1)} %add_convert_fusion.6), channel_id=1, source_target_pairs={{0,2},{1,5},{4,0},{5,9},{8,4},{9,13},{12,8},{13,15},{14,12},{15,11... | collective-permute-start | bytes 393224 | tf_op jit(solution)/shard_map/ppermute | solution.py:51
  40.7 6.5 %collective-permute-start.20 = (bf16[256,256]{1,0:T(8,128)(2,1)S(1)}, bf16[256,256]{1,0:T(8,128)(2,1)S(1)}, u32[]{:S(2)}, u32[]{:S(2)}) collective-permute-start(bf16[256,256]{1,0:T(8,128)(2,1)S(1)} %add_convert_fusion.7), channel_id=1, source_target_pairs={{0,4},{1,3},{4,8},{5,1},{8,12},{9,5},{12,14},{13,9},{14,10},{15,13... | collective-permute-start | bytes 393224 | tf_op jit(solution)/shard_map/ppermute | solution.py:51
  42.4 6.4 %collective-permute-start.19 = (bf16[256,256]{1,0:T(8,128)(2,1)S(1)}, bf16[256,256]{1,0:T(8,128)(2,1)S(1)}, u32[]{:S(2)}, u32[]{:S(2)}) collective-permute-start(bf16[256,256]{1,0:T(8,128)(2,1)S(1)} %add_convert_fusion.9), channel_id=1, source_target_pairs={{0,4},{1,3},{4,8},{5,1},{8,12},{9,5},{12,14},{13,9},{14,10},{15,13... | collective-permute-start | bytes 393224 | tf_op jit(solution)/shard_map/ppermute | solution.py:51
  44.1 6.4 %collective-permute-start.28 = (bf16[256,256]{1,0:T(8,128)(2,1)S(1)}, bf16[256,256]{1,0:T(8,128)(2,1)S(1)}, u32[]{:S(2)}, u32[]{:S(2)}) collective-permute-start(bf16[256,256]{1,0:T(8,128)(2,1)S(1)} %add_convert_fusion.1), channel_id=1, source_target_pairs={{0,2},{1,5},{4,0},{5,9},{8,4},{9,13},{12,8},{13,15},{14,12},{15,11... | collective-permute-start | bytes 393224 | tf_op jit(solution)/shard_map/ppermute | solution.py:51
  46.1 8.3 %collective-permute-start.23 = (bf16[256,256]{1,0:T(8,128)(2,1)S(1)}, bf16[256,256]{1,0:T(8,128)(2,1)S(1)}, u32[]{:S(2)}, u32[]{:S(2)}) collective-permute-start(bf16[256,256]{1,0:T(8,128)(2,1)S(1)} %add_convert_fusion.5), channel_id=1, source_target_pairs={{0,2},{1,5},{4,0},{5,9},{8,4},{9,13},{12,8},{13,15},{14,12},{15,11... | collective-permute-start | bytes 393224 | tf_op jit(solution)/shard_map/ppermute | solution.py:51
  47.2 6.3 %collective-permute-start.25 = (bf16[256,256]{1,0:T(8,128)(2,1)S(1)}, bf16[256,256]{1,0:T(8,128)(2,1)S(1)}, u32[]{:S(2)}, u32[]{:S(2)}) collective-permute-start(bf16[256,256]{1,0:T(8,128)(2,1)S(1)} %add_convert_fusion.3), channel_id=1, source_target_pairs={{0,4},{1,3},{4,8},{5,1},{8,12},{9,5},{12,14},{13,9},{14,10},{15,13... | collective-permute-start | bytes 393224 | tf_op jit(solution)/shard_map/ppermute | solution.py:51
  48.9 9.7 %collective-permute-start.22 = (bf16[256,256]{1,0:T(8,128)(2,1)S(1)}, bf16[256,256]{1,0:T(8,128)(2,1)S(1)}, u32[]{:S(2)}, u32[]{:S(2)}) collective-permute-start(bf16[256,256]{1,0:T(8,128)(2,1)S(1)} %add_convert_fusion.8), channel_id=1, source_target_pairs={{0,4},{1,3},{4,8},{5,1},{8,12},{9,5},{12,14},{13,9},{14,10},{15,13... | collective-permute-start | bytes 393224 | tf_op jit(solution)/shard_map/ppermute | solution.py:51
  59.5 6.0 %collective-permute-start.34 = (bf16[256,256]{1,0:T(8,128)(2,1)S(1)}, bf16[256,256]{1,0:T(8,128)(2,1)S(1)}, u32[]{:S(2)}, u32[]{:S(2)}) collective-permute-start(bf16[256,256]{1,0:T(8,128)(2,1)S(1)} %multiply_convert_fusion.refs_1_), channel_id=1, source_target_pairs={{0,2},{1,5},{4,0},{5,9},{8,4},{9,13},{12,8},{13,15},{14,12},{15,11... | collective-permute-start | bytes 393224 | tf_op jit(solution)/shard_map/ppermute | solution.py:51
  60.8 6.1 %collective-permute-start.30 = (bf16[256,256]{1,0:T(8,128)(2,1)S(1)}, bf16[256,256]{1,0:T(8,128)(2,1)S(1)}, u32[]{:S(2)}, u32[]{:S(2)}) collective-permute-start(bf16[256,256]{1,0:T(8,128)(2,1)S(1)} %fusion.1.refs_0_), channel_id=1, source_target_pairs={{0,4},{1,3},{4,8},{5,1},{8,12},{9,5},{12,14},{13,9},{14,10},{15,13... | collective-permute-start | bytes 393224 | tf_op jit(solution)/shard_map/ppermute | solution.py:51
  61.6 7.1 %collective-permute-start.38 = (bf16[256,256]{1,0:T(8,128)(2,1)S(1)}, bf16[256,256]{1,0:T(8,128)(2,1)S(1)}, u32[]{:S(2)}, u32[]{:S(2)}) collective-permute-start(bf16[256,256]{1,0:T(8,128)(2,1)S(1)} %multiply_convert_fusion.refs_1_), channel_id=1, source_target_pairs={{0,4},{1,3},{4,8},{5,1},{8,12},{9,5},{12,14},{13,9},{14,10},{15,13... | collective-permute-start | bytes 393224 | tf_op jit(solution)/shard_map/ppermute | solution.py:51
  63.3 7.3 %collective-permute-start.39 = (bf16[256,256]{1,0:T(8,128)(2,1)S(1)}, bf16[256,256]{1,0:T(8,128)(2,1)S(1)}, u32[]{:S(2)}, u32[]{:S(2)}) collective-permute-start(bf16[256,256]{1,0:T(8,128)(2,1)S(1)} %fusion.1.refs_0_), channel_id=1, source_target_pairs={{0,2},{1,5},{4,0},{5,9},{8,4},{9,13},{12,8},{13,15},{14,12},{15,11... | collective-permute-start | bytes 393224 | tf_op jit(solution)/shard_map/ppermute | solution.py:51
  65.5 6.3 %collective-permute-start.35 = (bf16[256,256]{1,0:T(8,128)(2,1)S(1)}, bf16[256,256]{1,0:T(8,128)(2,1)S(1)}, u32[]{:S(2)}, u32[]{:S(2)}) collective-permute-start(bf16[256,256]{1,0:T(8,128)(2,1)S(1)} %collective-permute-done.34.refs_5_), channel_id=1, source_target_pairs={{0,2},{1,5},{4,0},{5,9},{8,4},{9,13},{12,8},{13,15},{14,12},{15,11... | collective-permute-start | bytes 393224 | tf_op jit(solution)/shard_map/ppermute | solution.py:51
  66.9 6.0 %collective-permute-start.31 = (bf16[256,256]{1,0:T(8,128)(2,1)S(1)}, bf16[256,256]{1,0:T(8,128)(2,1)S(1)}, u32[]{:S(2)}, u32[]{:S(2)}) collective-permute-start(bf16[256,256]{1,0:T(8,128)(2,1)S(1)} %collective-permute-done.30.refs_2_), channel_id=1, source_target_pairs={{0,4},{1,3},{4,8},{5,1},{8,12},{9,5},{12,14},{13,9},{14,10},{15,13... | collective-permute-start | bytes 393224 | tf_op jit(solution)/shard_map/ppermute | solution.py:51
  68.6 6.4 %collective-permute-start.40 = (bf16[256,256]{1,0:T(8,128)(2,1)S(1)}, bf16[256,256]{1,0:T(8,128)(2,1)S(1)}, u32[]{:S(2)}, u32[]{:S(2)}) collective-permute-start(bf16[256,256]{1,0:T(8,128)(2,1)S(1)} %collective-permute-done.38.refs_3_), channel_id=1, source_target_pairs={{0,4},{1,3},{4,8},{5,1},{8,12},{9,5},{12,14},{13,9},{14,10},{15,13... | collective-permute-start | bytes 393224 | tf_op jit(solution)/shard_map/ppermute | solution.py:51
  70.5 6.2 %collective-permute-start.41 = (bf16[256,256]{1,0:T(8,128)(2,1)S(1)}, bf16[256,256]{1,0:T(8,128)(2,1)S(1)}, u32[]{:S(2)}, u32[]{:S(2)}) collective-permute-start(bf16[256,256]{1,0:T(8,128)(2,1)S(1)} %collective-permute-done.39.refs_4_), channel_id=1, source_target_pairs={{0,2},{1,5},{4,0},{5,9},{8,4},{9,13},{12,8},{13,15},{14,12},{15,11... | collective-permute-start | bytes 393224 | tf_op jit(solution)/shard_map/ppermute | solution.py:51
  71.8 6.3 %collective-permute-start.36 = (bf16[256,256]{1,0:T(8,128)(2,1)S(1)}, bf16[256,256]{1,0:T(8,128)(2,1)S(1)}, u32[]{:S(2)}, u32[]{:S(2)}) collective-permute-start(bf16[256,256]{1,0:T(8,128)(2,1)S(1)} %collective-permute-done.35.refs_3_), channel_id=1, source_target_pairs={{0,2},{1,5},{4,0},{5,9},{8,4},{9,13},{12,8},{13,15},{14,12},{15,11... | collective-permute-start | bytes 393224 | tf_op jit(solution)/shard_map/ppermute | solution.py:51
  75.0 6.3 %collective-permute-start.42 = (bf16[256,256]{1,0:T(8,128)(2,1)S(1)}, bf16[256,256]{1,0:T(8,128)(2,1)S(1)}, u32[]{:S(2)}, u32[]{:S(2)}) collective-permute-start(bf16[256,256]{1,0:T(8,128)(2,1)S(1)} %collective-permute-done.40.refs_1_), channel_id=1, source_target_pairs={{0,4},{1,3},{4,8},{5,1},{8,12},{9,5},{12,14},{13,9},{14,10},{15,13... | collective-permute-start | bytes 393224 | tf_op jit(solution)/shard_map/ppermute | solution.py:51
  (16 other events, 124.0 us)

commit v12 on v11

--- a/solution.py
+++ b/solution.py
@@ -92,17 +92,15 @@
             outs[1][at, :] = jnp.maximum(total, 0.0).astype(BF16)
 
 
-def turn_own_kernel(starts, *refs):
-    *shards, turned = refs
-    rows = shards[0].shape[0]
-    for chain, shard in enumerate(shards):
-        turned[:, chain * rows:(chain + 1) * rows] = shard[...].T
-
-
-def turn_kernel(starts, own, *refs):
+def turn_own_kernel(starts, shard, *refs):
+    refs[-1][...] = shard[...].T
+
+
+def turn_kernel(starts, own_0, own_1, *refs):
     *shards, turned = refs
     rows, wide = shards[0].shape
-    turned[block_of(starts, 0, wide), :] = own[...]
+    for chain, own in enumerate((own_0, own_1)):
+        turned[block_of(starts, 0, wide), chain * rows:(chain + 1) * rows] = own[...]
     for k in range(len(shards) // 2):
         at = block_of(starts, k + 1, wide)
         for chain in range(2):
@@ -249,14 +247,14 @@
     starts = jnp.stack([ring_member(place + sign * offset, size) * wide for offset in offsets] + [layer])
     starts = starts.astype(jnp.int32)
 
-    urgent, later = ((0, 1), (1, -1)), ((1, 1), (0, -1))
+    urgent, later = ((0, 1), (1, -1)), ((0, -1), (1, 1))
 
     def gather_step(found, s, ready=None):
         for chain, way in urgent + later if s < reach else urgent:
             slots = slot_p if way == 1 else slot_q
             shard = found[chain][slots[s - 1] if s > 1 else 0]
             if ready is not None and (chain, way) in later:
-                shard = after(shard, ready)
+                shard = after(shard, ready[chain])
             found[chain][slots[s] if s < reach else far] = hop(shard, way)
 
     def both_chains(found, slots):
@@ -272,9 +270,10 @@
         )
 
     inputs = [[part] + [None] * (size - 1) for part in halves(residual_in[0])]
-    turned_own = call(
-        turn_own_kernel, [shape((wide, rows), BF16)], 0, [starts] + both_chains(inputs, (0,))
-    )[0]
+    turned_own = []
+    for chain in chains:
+        source = inputs[chain][0] if chain == 0 else after(inputs[chain][0], turned_own[0])
+        turned_own += call(turn_own_kernel, [shape((wide, half), BF16)], 0, [starts, source])
     for s in range(1, reach + 1):
         gather_step(inputs, s, turned_own if s == 1 else None)
     low_cross = passed_along(after(dec_cross, inputs[0][slot_p.get(1, far)]), "layer", 1)
@@ -322,31 +321,30 @@
             wanted = after(wanted, errors[0][0])
         errors.append([((total - wanted.astype(F32)) * err_scale).astype(BF16)] + [None] * (size - 1))
 
-    def back(slots, before):
+    def back(slots, before, decoders):
         return call(
             functools.partial(back_kernel, slots, before is None),
             [shape((len(slots), 2 * lat, wide), F32), shape((2, half, 2 * lat), F32)],
             4 * unit * len(slots),
-            [starts] + both_chains(errors, slots) + [stacked] + both_t + ([] if before is None else [before]),
+            [starts] + both_chains(errors, slots) + [decoders] + both_t + ([] if before is None else [before]),
         )
 
     groups, outers, acc, pending = [], [], None, [0]
-    arrived = [inputs[0][1]] if size == 2 else [after(inputs[0][1], errors[1][0])]
+    arrived = [after(inputs[0][1], errors[1][0])]
     turned = call(
         turn_kernel,
         [shape((deep, rows), BF16)],
         0,
-        [starts, turned_own] + arrived + both_chains(inputs, range(1, size))[1:],
+        [starts] + turned_own + arrived + both_chains(inputs, range(1, size))[1:],
     )[0]
+    groups = [(0,), tuple(range(1, far))] if reach > 1 else [(0,)]
+    outer, acc = back(groups[0], None, stacked)
+    outers = [outer]
     for s in range(1, reach + 1):
-        gather_step(errors, s, turned if s == 2 else None)
-        if s < reach:
-            pending += [slot_p[s], slot_q[s]]
-        if s == 1 or s == reach - 1:
-            groups.append(tuple(pending))
-            outer, acc = back(groups[-1], acc)
-            outers.append(outer)
-            pending = []
+        gather_step(errors, s, (turned, turned) if s == 2 else None)
+    if reach > 1:
+        outer, acc = back(groups[1], acc, stacked)
+        outers.append(outer)
     last_same, back_own, sent, high = call(
         functools.partial(last_back_kernel, groups, far),
         [

time: 91.6 us -> 97.5 us (1.064)
  waiting for transfers between devices: 26.1 us -> 31.6 us
    ppermute x42, waiting for transfers between devices: 23.8 us -> 29.3 us  [hop(): return lax.ppermute(shard, ('latent', 'layer'), pairs)]
    pallas_call x11 -> x12, Pallas kernels: 13.3 us -> 13.9 us  [call(): pl.pallas_call(kernel, out_shape=outs, in_specs=[spec(pltpu.SMEM)] + [spe...]
  transfers between devices with their start and end apart: 45 -> 45, of which waited for: 26 -> 26; matrix products, arithmetic and copies ran while one was open for 2% -> 2% of each run, Pallas kernels for 9% -> 8%
where the time goes in v12:
time: 97.5 us; the launch traced here: 97.3 us
  starting transfers between devices  48.1 us (49%)
  waiting for transfers between devices  31.6 us (32%)
  Pallas kernels  13.9 us (14%)
  other arithmetic  1.63 us (2%)
  local copies, waits for them, and re-layouts  1.15 us (1%)
    ppermute x42, starting transfers between devices, hop(): return lax.ppermute(shard, ('latent', 'layer'), pairs)  44.2 us
    ppermute x42, waiting for transfers between devices, hop(): return lax.ppermute(shard, ('latent', 'layer'), pairs)  29.3 us
    pallas_call x12, Pallas kernels, call(): pl.pallas_call(kernel, out_shape=outs, in_specs=[spec(pltpu.SMEM)] + [spe...  13.9 us
    ppermute x3, starting transfers between devices, passed_along(): return lax.ppermute(shard, axis, pairs)  3.89 us
    ppermute x3, waiting for transfers between devices, passed_along(): return lax.ppermute(shard, axis, pairs)  2.27 us
  transfers between devices with their start and end apart: 45, of which 26 were waited for; matrix products, arithmetic and copies ran while one was open for 2% of the time, Pallas kernels for 8%

profile of v12, /device:TPU:0, one launch (start us, length us, event | category | flops | bytes accessed | tf_op | source)
XLA Modules:
  0.0 97.3 jit_solution(10105852905004984907)
XLA Ops:
  1.7 3.1 %collective-permute-start = (bf16[256,256]{1,0:T(8,128)(2,1)S(1)}, bf16[256,256]{1,0:T(8,128)(2,1)S(1)}, u32[]{:S(2)}, u32[]{:S(2)}) collective-permute-start(bf16[256,256]{1,0:T(8,128)(2,1)S(1)} %get-tuple-element.50.shard.refs_0_), channel_id=1, source_target_pairs={{0,4},{1,3},{4,8},{5,1},{8,12},{9,5},{12,14},{13,9},{14,10},{15,13... | collective-permute-start | bytes 393224 | tf_op jit(solution)/shard_map/ppermute | solution.py:51
  6.1 2.1 %collective-permute-start.8 = (bf16[256,256]{1,0:T(8,128)(2,1)S(1)}, bf16[256,256]{1,0:T(8,128)(2,1)S(1)}, u32[]{:S(2)}, u32[]{:S(2)}) collective-permute-start(bf16[256,256]{1,0:T(8,128)(2,1)S(1)} %get-tuple-element.49.shard.refs_1_), channel_id=1, source_target_pairs={{0,4},{1,3},{4,8},{5,1},{8,12},{9,5},{12,14},{13,9},{14,10},{15,13... | collective-permute-start | bytes 393224 | tf_op jit(solution)/shard_map/ppermute | solution.py:51
  8.5 1.7 %collective-permute-start.1 = (bf16[256,256]{1,0:T(8,128)(2,1)S(1)}, bf16[256,256]{1,0:T(8,128)(2,1)S(1)}, u32[]{:S(2)}, u32[]{:S(2)}) collective-permute-start(bf16[256,256]{1,0:T(8,128)(2,1)S(1)} %collective-permute-done.refs_2_.refs_0_), channel_id=1, source_target_pairs={{0,4},{1,3},{4,8},{5,1},{8,12},{9,5},{12,14},{13,9},{14,10},{15,13... | collective-permute-start | bytes 393224 | tf_op jit(solution)/shard_map/ppermute | solution.py:51
  11.1 1.3 %collective-permute-start.14 = (bf16[128,1024]{1,0:T(8,128)(2,1)}, bf16[128,1024]{1,0:T(8,128)(2,1)S(1)}, u32[]{:S(2)}, u32[]{:S(2)}) collective-permute-start(bf16[128,1024]{1,0:T(8,128)(2,1)} %param.11), channel_id=1, source_target_pairs={{0,1},{2,3},{4,5},{6,7},{8,9},{10,11},{12,13},{14,15},{16,17},{18,... | collective-permute-start | bytes 786440 | tf_op jit(solution)/shard_map/ppermute | solution.py:23
  12.5 1.9 %collective-permute-start.10 = (bf16[256,256]{1,0:T(8,128)(2,1)S(1)}, bf16[256,256]{1,0:T(8,128)(2,1)S(1)}, u32[]{:S(2)}, u32[]{:S(2)}) collective-permute-start(bf16[256,256]{1,0:T(8,128)(2,1)S(1)} %collective-permute-done.8.refs_3_.refs_1_), channel_id=1, source_target_pairs={{0,4},{1,3},{4,8},{5,1},{8,12},{9,5},{12,14},{13,9},{14,10},{15,13... | collective-permute-start | bytes 393224 | tf_op jit(solution)/shard_map/ppermute | solution.py:51
  18.2 2.4 %collective-permute-start.12 = (bf16[256,256]{1,0:T(8,128)(2,1)S(1)}, bf16[256,256]{1,0:T(8,128)(2,1)S(1)}, u32[]{:S(2)}, u32[]{:S(2)}) collective-permute-start(bf16[256,256]{1,0:T(8,128)(2,1)S(1)} %collective-permute-done.10.refs_7_.refs_5_), channel_id=1, source_target_pairs={{0,4},{1,3},{4,8},{5,1},{8,12},{9,5},{12,14},{13,9},{14,10},{15,13... | collective-permute-start | bytes 393224 | tf_op jit(solution)/shard_map/ppermute | solution.py:51
  21.7 1.7 %collective-permute-start.3 = (bf16[256,256]{1,0:T(8,128)(2,1)S(1)}, bf16[256,256]{1,0:T(8,128)(2,1)S(1)}, u32[]{:S(2)}, u32[]{:S(2)}) collective-permute-start(bf16[256,256]{1,0:T(8,128)(2,1)S(1)} %collective-permute-done.2.refs_10_.refs_8_), channel_id=1, source_target_pairs={{0,4},{1,3},{4,8},{5,1},{8,12},{9,5},{12,14},{13,9},{14,10},{15,13... | collective-permute-start | bytes 393224 | tf_op jit(solution)/shard_map/ppermute | solution.py:51
  26.8 1.9 %collective-permute-done.7.refs_1_.refs_13_ = bf16[256,256]{1,0:T(8,128)(2,1)S(1)} collective-permute-done((bf16[256,256]{1,0:T(8,128)(2,1)S(1)}, bf16[256,256]{1,0:T(8,128)(2,1)S(1)}, u32[]{:S(2)}, u32[]{:S(2)}) %collective-permute-start.7) | collective-permute-done | bytes 131104 | tf_op jit(solution)/shard_map/ppermute | solution.py:51
  29.5 1.3 %collective-permute-start.15 = (bf16[512,128]{1,0:T(8,128)(2,1)S(1)}, bf16[512,128]{1,0:T(8,128)(2,1)S(1)}, u32[]{:S(2)}, u32[]{:S(2)}) collective-permute-start(bf16[512,128]{1,0:T(8,128)(2,1)S(1)} %get-tuple-element.53.codes), channel_id=1, source_target_pairs={{0,1},{2,3},{4,5},{6,7},{8,9},{10,11},{12,13},{14,15},{16,17},{18,... | collective-permute-start | bytes 393224 | tf_op jit(solution)/shard_map/ppermute | solution.py:23
  33.0 1.6 %collective-permute-start.16 = (bf16[256,256]{1,0:T(8,128)(2,1)S(1)}, bf16[256,256]{1,0:T(8,128)(2,1)S(1)}, u32[]{:S(2)}, u32[]{:S(2)}) collective-permute-start(bf16[256,256]{1,0:T(8,128)(2,1)S(1)} %get-tuple-element.57), channel_id=1, source_target_pairs={{0,4},{1,3},{4,8},{5,1},{8,12},{9,5},{12,14},{13,9},{14,10},{15,13... | collective-permute-start | bytes 393224 | tf_op jit(solution)/shard_map/ppermute | solution.py:51
  35.4 1.6 %collective-permute-start.17 = (bf16[256,256]{1,0:T(8,128)(2,1)S(1)}, bf16[256,256]{1,0:T(8,128)(2,1)S(1)}, u32[]{:S(2)}, u32[]{:S(2)}) collective-permute-start(bf16[256,256]{1,0:T(8,128)(2,1)S(1)} %get-tuple-element.58), channel_id=1, source_target_pairs={{0,4},{1,3},{4,8},{5,1},{8,12},{9,5},{12,14},{13,9},{14,10},{15,13... | collective-permute-start | bytes 393224 | tf_op jit(solution)/shard_map/ppermute | solution.py:51
  38.0 3.7 %collective-permute-done.17 = bf16[256,256]{1,0:T(8,128)(2,1)S(1)} collective-permute-done((bf16[256,256]{1,0:T(8,128)(2,1)S(1)}, bf16[256,256]{1,0:T(8,128)(2,1)S(1)}, u32[]{:S(2)}, u32[]{:S(2)}) %collective-permute-start.17) | collective-permute-done | bytes 131104 | tf_op jit(solution)/shard_map/ppermute | solution.py:51
  42.0 1.5 %collective-permute-start.19 = (bf16[256,256]{1,0:T(8,128)(2,1)S(1)}, bf16[256,256]{1,0:T(8,128)(2,1)S(1)}, u32[]{:S(2)}, u32[]{:S(2)}) collective-permute-start(bf16[256,256]{1,0:T(8,128)(2,1)S(1)} %add_convert_fusion.9), channel_id=1, source_target_pairs={{0,4},{1,3},{4,8},{5,1},{8,12},{9,5},{12,14},{13,9},{14,10},{15,13... | collective-permute-start | bytes 393224 | tf_op jit(solution)/shard_map/ppermute | solution.py:51
  44.1 1.5 %collective-permute-start.20 = (bf16[256,256]{1,0:T(8,128)(2,1)S(1)}, bf16[256,256]{1,0:T(8,128)(2,1)S(1)}, u32[]{:S(2)}, u32[]{:S(2)}) collective-permute-start(bf16[256,256]{1,0:T(8,128)(2,1)S(1)} %add_convert_fusion.7), channel_id=1, source_target_pairs={{0,4},{1,3},{4,8},{5,1},{8,12},{9,5},{12,14},{13,9},{14,10},{15,13... | collective-permute-start | bytes 393224 | tf_op jit(solution)/shard_map/ppermute | solution.py:51
  46.3 2.0 %collective-permute-done.19 = bf16[256,256]{1,0:T(8,128)(2,1)S(1)} collective-permute-done((bf16[256,256]{1,0:T(8,128)(2,1)S(1)}, bf16[256,256]{1,0:T(8,128)(2,1)S(1)}, u32[]{:S(2)}, u32[]{:S(2)}) %collective-permute-start.19) | collective-permute-done | bytes 131104 | tf_op jit(solution)/shard_map/ppermute | solution.py:51
  48.5 1.9 %collective-permute-done.20 = bf16[256,256]{1,0:T(8,128)(2,1)S(1)} collective-permute-done((bf16[256,256]{1,0:T(8,128)(2,1)S(1)}, bf16[256,256]{1,0:T(8,128)(2,1)S(1)}, u32[]{:S(2)}, u32[]{:S(2)}) %collective-permute-start.20) | collective-permute-done | bytes 131104 | tf_op jit(solution)/shard_map/ppermute | solution.py:51
  51.0 1.5 %collective-permute-start.23 = (bf16[256,256]{1,0:T(8,128)(2,1)S(1)}, bf16[256,256]{1,0:T(8,128)(2,1)S(1)}, u32[]{:S(2)}, u32[]{:S(2)}) collective-permute-start(bf16[256,256]{1,0:T(8,128)(2,1)S(1)} %add_convert_fusion.5), channel_id=1, source_target_pairs={{0,2},{1,5},{4,0},{5,9},{8,4},{9,13},{12,8},{13,15},{14,12},{15,11... | collective-permute-start | bytes 393224 | tf_op jit(solution)/shard_map/ppermute | solution.py:51
  53.2 1.5 %collective-permute-start.29 = (bf16[256,256]{1,0:T(8,128)(2,1)S(1)}, bf16[256,256]{1,0:T(8,128)(2,1)S(1)}, u32[]{:S(2)}, u32[]{:S(2)}) collective-permute-start(bf16[256,256]{1,0:T(8,128)(2,1)S(1)} %add_convert_fusion), channel_id=1, source_target_pairs={{0,2},{1,5},{4,0},{5,9},{8,4},{9,13},{12,8},{13,15},{14,12},{15,11... | collective-permute-start | bytes 393224 | tf_op jit(solution)/shard_map/ppermute | solution.py:51
  54.7 4.0 %collective-permute-done.25 = bf16[256,256]{1,0:T(8,128)(2,1)S(1)} collective-permute-done((bf16[256,256]{1,0:T(8,128)(2,1)S(1)}, bf16[256,256]{1,0:T(8,128)(2,1)S(1)}, u32[]{:S(2)}, u32[]{:S(2)}) %collective-permute-start.25) | collective-permute-done | bytes 131104 | tf_op jit(solution)/shard_map/ppermute | solution.py:51
  58.9 2.1 %collective-permute-start.24 = (bf16[256,256]{1,0:T(8,128)(2,1)S(1)}, bf16[256,256]{1,0:T(8,128)(2,1)S(1)}, u32[]{:S(2)}, u32[]{:S(2)}) collective-permute-start(bf16[256,256]{1,0:T(8,128)(2,1)S(1)} %add_convert_fusion.4), channel_id=1, source_target_pairs={{0,2},{1,5},{4,0},{5,9},{8,4},{9,13},{12,8},{13,15},{14,12},{15,11... | collective-permute-start | bytes 393224 | tf_op jit(solution)/shard_map/ppermute | solution.py:51
  60.9 4.2 %collective-permute-done.26 = bf16[256,256]{1,0:T(8,128)(2,1)S(1)} collective-permute-done((bf16[256,256]{1,0:T(8,128)(2,1)S(1)}, bf16[256,256]{1,0:T(8,128)(2,1)S(1)}, u32[]{:S(2)}, u32[]{:S(2)}) %collective-permute-start.26) | collective-permute-done | bytes 131104 | tf_op jit(solution)/shard_map/ppermute | solution.py:51
  65.3 2.1 %collective-permute-start.34 = (bf16[256,256]{1,0:T(8,128)(2,1)S(1)}, bf16[256,256]{1,0:T(8,128)(2,1)S(1)}, u32[]{:S(2)}, u32[]{:S(2)}) collective-permute-start(bf16[256,256]{1,0:T(8,128)(2,1)S(1)} %multiply_convert_fusion.refs_1_), channel_id=1, source_target_pairs={{0,2},{1,5},{4,0},{5,9},{8,4},{9,13},{12,8},{13,15},{14,12},{15,11... | collective-permute-start | bytes 393224 | tf_op jit(solution)/shard_map/ppermute | solution.py:51
  67.4 2.0 %collective-permute-start.39 = (bf16[256,256]{1,0:T(8,128)(2,1)S(1)}, bf16[256,256]{1,0:T(8,128)(2,1)S(1)}, u32[]{:S(2)}, u32[]{:S(2)}) collective-permute-start(bf16[256,256]{1,0:T(8,128)(2,1)S(1)} %fusion.1.refs_0_), channel_id=1, source_target_pairs={{0,2},{1,5},{4,0},{5,9},{8,4},{9,13},{12,8},{13,15},{14,12},{15,11... | collective-permute-start | bytes 393224 | tf_op jit(solution)/shard_map/ppermute | solution.py:51
  69.5 1.8 %collective-permute-done.34.refs_3_ = bf16[256,256]{1,0:T(8,128)(2,1)S(1)} collective-permute-done((bf16[256,256]{1,0:T(8,128)(2,1)S(1)}, bf16[256,256]{1,0:T(8,128)(2,1)S(1)}, u32[]{:S(2)}, u32[]{:S(2)}) %collective-permute-start.34) | collective-permute-done | bytes 131104 | tf_op jit(solution)/shard_map/ppermute | solution.py:51
  71.3 2.5 %collective-permute-start.35 = (bf16[256,256]{1,0:T(8,128)(2,1)S(1)}, bf16[256,256]{1,0:T(8,128)(2,1)S(1)}, u32[]{:S(2)}, u32[]{:S(2)}) collective-permute-start(bf16[256,256]{1,0:T(8,128)(2,1)S(1)} %collective-permute-done.34.refs_3_), channel_id=1, source_target_pairs={{0,2},{1,5},{4,0},{5,9},{8,4},{9,13},{12,8},{13,15},{14,12},{15,11... | collective-permute-start | bytes 393224 | tf_op jit(solution)/shard_map/ppermute | solution.py:51
  74.9 2.1 %collective-permute-start.41 = (bf16[256,256]{1,0:T(8,128)(2,1)S(1)}, bf16[256,256]{1,0:T(8,128)(2,1)S(1)}, u32[]{:S(2)}, u32[]{:S(2)}) collective-permute-start(bf16[256,256]{1,0:T(8,128)(2,1)S(1)} %collective-permute-done.39.refs_2_), channel_id=1, source_target_pairs={{0,2},{1,5},{4,0},{5,9},{8,4},{9,13},{12,8},{13,15},{14,12},{15,11... | collective-permute-start | bytes 393224 | tf_op jit(solution)/shard_map/ppermute | solution.py:51
  76.9 2.5 %collective-permute-start.36 = (bf16[256,256]{1,0:T(8,128)(2,1)S(1)}, bf16[256,256]{1,0:T(8,128)(2,1)S(1)}, u32[]{:S(2)}, u32[]{:S(2)}) collective-permute-start(bf16[256,256]{1,0:T(8,128)(2,1)S(1)} %collective-permute-done.35.refs_7_), channel_id=1, source_target_pairs={{0,2},{1,5},{4,0},{5,9},{8,4},{9,13},{12,8},{13,15},{14,12},{15,11... | collective-permute-start | bytes 393224 | tf_op jit(solution)/shard_map/ppermute | solution.py:51
  79.4 1.8 %collective-permute-done.41.refs_6_ = bf16[256,256]{1,0:T(8,128)(2,1)S(1)} collective-permute-done((bf16[256,256]{1,0:T(8,128)(2,1)S(1)}, bf16[256,256]{1,0:T(8,128)(2,1)S(1)}, u32[]{:S(2)}, u32[]{:S(2)}) %collective-permute-start.41) | collective-permute-done | bytes 131104 | tf_op jit(solution)/shard_map/ppermute | solution.py:51
  87.1 1.5 %shard_map.101 = (f32[6,256,256]{2,1,0:T(8,128)S(1)}, f32[2,256,256]{2,1,0:T(8,128)S(1)}) custom-call(s32[9]{0:T(128)S(1)} %stack.39.starts, bf16[256,256]{1,0:T(8,128)(2,1)S(1)} %collective-permute-done.30.refs_0_, bf16[256,256]{1,0:T(8,128)(2,1)S(1)} %collective-permute-done.38.refs_1_, bf16[256,256]{1,0:T(8,128)(2,1)S(1)} %collective-permute-done.39.refs_2_, ...), custom_call_target="tpu_custom_call" | custom-call | flops 402653184 | bytes 1024 | tf_op jit(solution)/shard_map/pallas_call | solution.py:64
  91.7 1.6 %shard_map.104 = f32[1,128,2048]{2,1,0:T(8,128)} custom-call(s32[9]{0:T(128)S(1)} %stack.39.starts, f32[128,256]{1,0:T(8,128)S(1)} %get-tuple-element.90.refs_0_, f32[1,256,256]{2,1,0:T(8,128)S(1)} %get-tuple-element.79.refs_5_.refs_1_, f32[6,256,256]{2,1,0:T(8,128)S(1)} %get-tuple-element.83.refs_6_.refs_2_), custom_call_target="tpu_custom_call" | custom-call | bytes 1024 | tf_op jit(solution)/shard_map/pallas_call | solution.py:64
  93.3 1.3 %collective-permute-done.44.arrived = f32[1536,128]{1,0:T(8,128)S(1)} collective-permute-done((f32[1536,128]{1,0:T(8,128)S(1)}, f32[1536,128]{1,0:T(8,128)S(1)}, u32[]{:S(2)}, u32[]{:S(2)}) %collective-permute-start.44) | collective-permute-done | bytes 786464 | tf_op jit(solution)/shard_map/ppermute | solution.py:23
  94.6 2.7 %shard_map.103 = (f32[1,2048,128]{2,1,0:T(8,128)}, f32[1,128]{1,0:T(1,128)}, f32[128,1024]{1,0:T(8,128)}) custom-call(s32[9]{0:T(128)S(1)} %stack.39.starts, bf16[2048,512]{1,0:T(8,128)(2,1)S(1)} %shard_map.99.turned, f32[512,128]{1,0:T(8,128)S(1)} %get-tuple-element.76.preact, f32[512,128]{1,0:T(8,128)S(1)} %get-tuple-element.85.back_own, ...), custom_call_target="tpu_custom_call" | custom-call | flops 268435456 | bytes 1024 | tf_op jit(solution)/shard_map/pallas_call | solution.py:64
  (92 shorter events, 29.7 us)
Async XLA Ops:
  1.7 6.8 %collective-permute-start = (bf16[256,256]{1,0:T(8,128)(2,1)S(1)}, bf16[256,256]{1,0:T(8,128)(2,1)S(1)}, u32[]{:S(2)}, u32[]{:S(2)}) collective-permute-start(bf16[256,256]{1,0:T(8,128)(2,1)S(1)} %get-tuple-element.50.shard.refs_0_), channel_id=1, source_target_pairs={{0,4},{1,3},{4,8},{5,1},{8,12},{9,5},{12,14},{13,9},{14,10},{15,13... | collective-permute-start | bytes 393224 | tf_op jit(solution)/shard_map/ppermute | solution.py:51
  4.8 6.3 %collective-permute-start.4 = (bf16[256,256]{1,0:T(8,128)(2,1)S(1)}, bf16[256,256]{1,0:T(8,128)(2,1)S(1)}, u32[]{:S(2)}, u32[]{:S(2)}) collective-permute-start(bf16[256,256]{1,0:T(8,128)(2,1)S(1)} %get-tuple-element.49.shard.refs_1_), channel_id=1, source_target_pairs={{0,2},{1,5},{4,0},{5,9},{8,4},{9,13},{12,8},{13,15},{14,12},{15,11... | collective-permute-start | bytes 393224 | tf_op jit(solution)/shard_map/ppermute | solution.py:51
  6.1 6.4 %collective-permute-start.8 = (bf16[256,256]{1,0:T(8,128)(2,1)S(1)}, bf16[256,256]{1,0:T(8,128)(2,1)S(1)}, u32[]{:S(2)}, u32[]{:S(2)}) collective-permute-start(bf16[256,256]{1,0:T(8,128)(2,1)S(1)} %get-tuple-element.49.shard.refs_1_), channel_id=1, source_target_pairs={{0,4},{1,3},{4,8},{5,1},{8,12},{9,5},{12,14},{13,9},{14,10},{15,13... | collective-permute-start | bytes 393224 | tf_op jit(solution)/shard_map/ppermute | solution.py:51
  8.2 6.3 %collective-permute-start.9 = (bf16[256,256]{1,0:T(8,128)(2,1)S(1)}, bf16[256,256]{1,0:T(8,128)(2,1)S(1)}, u32[]{:S(2)}, u32[]{:S(2)}) collective-permute-start(bf16[256,256]{1,0:T(8,128)(2,1)S(1)} %get-tuple-element.50.shard.refs_0_), channel_id=1, source_target_pairs={{0,2},{1,5},{4,0},{5,9},{8,4},{9,13},{12,8},{13,15},{14,12},{15,11... | collective-permute-start | bytes 393224 | tf_op jit(solution)/shard_map/ppermute | solution.py:51
  8.5 6.9 %collective-permute-start.1 = (bf16[256,256]{1,0:T(8,128)(2,1)S(1)}, bf16[256,256]{1,0:T(8,128)(2,1)S(1)}, u32[]{:S(2)}, u32[]{:S(2)}) collective-permute-start(bf16[256,256]{1,0:T(8,128)(2,1)S(1)} %collective-permute-done.refs_2_.refs_0_), channel_id=1, source_target_pairs={{0,4},{1,3},{4,8},{5,1},{8,12},{9,5},{12,14},{13,9},{14,10},{15,13... | collective-permute-start | bytes 393224 | tf_op jit(solution)/shard_map/ppermute | solution.py:51
  11.1 6.3 %collective-permute-start.5 = (bf16[256,256]{1,0:T(8,128)(2,1)S(1)}, bf16[256,256]{1,0:T(8,128)(2,1)S(1)}, u32[]{:S(2)}, u32[]{:S(2)}) collective-permute-start(bf16[256,256]{1,0:T(8,128)(2,1)S(1)} %collective-permute-done.4.refs_5_.refs_3_), channel_id=1, source_target_pairs={{0,2},{1,5},{4,0},{5,9},{8,4},{9,13},{12,8},{13,15},{14,12},{15,11... | collective-permute-start | bytes 393224 | tf_op jit(solution)/shard_map/ppermute | solution.py:51
  11.1 12.7 %collective-permute-start.14 = (bf16[128,1024]{1,0:T(8,128)(2,1)}, bf16[128,1024]{1,0:T(8,128)(2,1)S(1)}, u32[]{:S(2)}, u32[]{:S(2)}) collective-permute-start(bf16[128,1024]{1,0:T(8,128)(2,1)} %param.11), channel_id=1, source_target_pairs={{0,1},{2,3},{4,5},{6,7},{8,9},{10,11},{12,13},{14,15},{16,17},{18,... | collective-permute-start | bytes 786440 | tf_op jit(solution)/shard_map/ppermute | solution.py:23
  12.5 5.7 %collective-permute-start.10 = (bf16[256,256]{1,0:T(8,128)(2,1)S(1)}, bf16[256,256]{1,0:T(8,128)(2,1)S(1)}, u32[]{:S(2)}, u32[]{:S(2)}) collective-permute-start(bf16[256,256]{1,0:T(8,128)(2,1)S(1)} %collective-permute-done.8.refs_3_.refs_1_), channel_id=1, source_target_pairs={{0,4},{1,3},{4,8},{5,1},{8,12},{9,5},{12,14},{13,9},{14,10},{15,13... | collective-permute-start | bytes 393224 | tf_op jit(solution)/shard_map/ppermute | solution.py:51
  14.5 6.1 %collective-permute-start.11 = (bf16[256,256]{1,0:T(8,128)(2,1)S(1)}, bf16[256,256]{1,0:T(8,128)(2,1)S(1)}, u32[]{:S(2)}, u32[]{:S(2)}) collective-permute-start(bf16[256,256]{1,0:T(8,128)(2,1)S(1)} %collective-permute-done.9.refs_4_.refs_2_), channel_id=1, source_target_pairs={{0,2},{1,5},{4,0},{5,9},{8,4},{9,13},{12,8},{13,15},{14,12},{15,11... | collective-permute-start | bytes 393224 | tf_op jit(solution)/shard_map/ppermute | solution.py:51
  15.4 6.4 %collective-permute-start.2 = (bf16[256,256]{1,0:T(8,128)(2,1)S(1)}, bf16[256,256]{1,0:T(8,128)(2,1)S(1)}, u32[]{:S(2)}, u32[]{:S(2)}) collective-permute-start(bf16[256,256]{1,0:T(8,128)(2,1)S(1)} %collective-permute-done.1.refs_6_.refs_4_), channel_id=1, source_target_pairs={{0,4},{1,3},{4,8},{5,1},{8,12},{9,5},{12,14},{13,9},{14,10},{15,13... | collective-permute-start | bytes 393224 | tf_op jit(solution)/shard_map/ppermute | solution.py:51
  17.4 6.3 %collective-permute-start.6 = (bf16[256,256]{1,0:T(8,128)(2,1)S(1)}, bf16[256,256]{1,0:T(8,128)(2,1)S(1)}, u32[]{:S(2)}, u32[]{:S(2)}) collective-permute-start(bf16[256,256]{1,0:T(8,128)(2,1)S(1)} %collective-permute-done.5.refs_9_.refs_7_), channel_id=1, source_target_pairs={{0,2},{1,5},{4,0},{5,9},{8,4},{9,13},{12,8},{13,15},{14,12},{15,11... | collective-permute-start | bytes 393224 | tf_op jit(solution)/shard_map/ppermute | solution.py:51
  18.2 6.9 %collective-permute-start.12 = (bf16[256,256]{1,0:T(8,128)(2,1)S(1)}, bf16[256,256]{1,0:T(8,128)(2,1)S(1)}, u32[]{:S(2)}, u32[]{:S(2)}) collective-permute-start(bf16[256,256]{1,0:T(8,128)(2,1)S(1)} %collective-permute-done.10.refs_7_.refs_5_), channel_id=1, source_target_pairs={{0,4},{1,3},{4,8},{5,1},{8,12},{9,5},{12,14},{13,9},{14,10},{15,13... | collective-permute-start | bytes 393224 | tf_op jit(solution)/shard_map/ppermute | solution.py:51
  35.4 6.4 %collective-permute-start.17 = (bf16[256,256]{1,0:T(8,128)(2,1)S(1)}, bf16[256,256]{1,0:T(8,128)(2,1)S(1)}, u32[]{:S(2)}, u32[]{:S(2)}) collective-permute-start(bf16[256,256]{1,0:T(8,128)(2,1)S(1)} %get-tuple-element.58), channel_id=1, source_target_pairs={{0,4},{1,3},{4,8},{5,1},{8,12},{9,5},{12,14},{13,9},{14,10},{15,13... | collective-permute-start | bytes 393224 | tf_op jit(solution)/shard_map/ppermute | solution.py:51
  37.5 8.2 %collective-permute-start.27 = (bf16[256,256]{1,0:T(8,128)(2,1)S(1)}, bf16[256,256]{1,0:T(8,128)(2,1)S(1)}, u32[]{:S(2)}, u32[]{:S(2)}) collective-permute-start(bf16[256,256]{1,0:T(8,128)(2,1)S(1)} %get-tuple-element.71), channel_id=1, source_target_pairs={{0,2},{1,5},{4,0},{5,9},{8,4},{9,13},{12,8},{13,15},{14,12},{15,11... | collective-permute-start | bytes 393224 | tf_op jit(solution)/shard_map/ppermute | solution.py:51
  42.0 6.3 %collective-permute-start.19 = (bf16[256,256]{1,0:T(8,128)(2,1)S(1)}, bf16[256,256]{1,0:T(8,128)(2,1)S(1)}, u32[]{:S(2)}, u32[]{:S(2)}) collective-permute-start(bf16[256,256]{1,0:T(8,128)(2,1)S(1)} %add_convert_fusion.9), channel_id=1, source_target_pairs={{0,4},{1,3},{4,8},{5,1},{8,12},{9,5},{12,14},{13,9},{14,10},{15,13... | collective-permute-start | bytes 393224 | tf_op jit(solution)/shard_map/ppermute | solution.py:51
  44.1 6.3 %collective-permute-start.20 = (bf16[256,256]{1,0:T(8,128)(2,1)S(1)}, bf16[256,256]{1,0:T(8,128)(2,1)S(1)}, u32[]{:S(2)}, u32[]{:S(2)}) collective-permute-start(bf16[256,256]{1,0:T(8,128)(2,1)S(1)} %add_convert_fusion.7), channel_id=1, source_target_pairs={{0,4},{1,3},{4,8},{5,1},{8,12},{9,5},{12,14},{13,9},{14,10},{15,13... | collective-permute-start | bytes 393224 | tf_op jit(solution)/shard_map/ppermute | solution.py:51
  45.7 7.5 %collective-permute-start.28 = (bf16[256,256]{1,0:T(8,128)(2,1)S(1)}, bf16[256,256]{1,0:T(8,128)(2,1)S(1)}, u32[]{:S(2)}, u32[]{:S(2)}) collective-permute-start(bf16[256,256]{1,0:T(8,128)(2,1)S(1)} %add_convert_fusion.1), channel_id=1, source_target_pairs={{0,2},{1,5},{4,0},{5,9},{8,4},{9,13},{12,8},{13,15},{14,12},{15,11... | collective-permute-start | bytes 393224 | tf_op jit(solution)/shard_map/ppermute | solution.py:51
  50.4 14.8 %collective-permute-start.22 = (bf16[256,256]{1,0:T(8,128)(2,1)S(1)}, bf16[256,256]{1,0:T(8,128)(2,1)S(1)}, u32[]{:S(2)}, u32[]{:S(2)}) collective-permute-start(bf16[256,256]{1,0:T(8,128)(2,1)S(1)} %add_convert_fusion.8), channel_id=1, source_target_pairs={{0,4},{1,3},{4,8},{5,1},{8,12},{9,5},{12,14},{13,9},{14,10},{15,13... | collective-permute-start | bytes 393224 | tf_op jit(solution)/shard_map/ppermute | solution.py:51
  51.0 7.8 %collective-permute-start.23 = (bf16[256,256]{1,0:T(8,128)(2,1)S(1)}, bf16[256,256]{1,0:T(8,128)(2,1)S(1)}, u32[]{:S(2)}, u32[]{:S(2)}) collective-permute-start(bf16[256,256]{1,0:T(8,128)(2,1)S(1)} %add_convert_fusion.5), channel_id=1, source_target_pairs={{0,2},{1,5},{4,0},{5,9},{8,4},{9,13},{12,8},{13,15},{14,12},{15,11... | collective-permute-start | bytes 393224 | tf_op jit(solution)/shard_map/ppermute | solution.py:51
  52.6 6.1 %collective-permute-start.25 = (bf16[256,256]{1,0:T(8,128)(2,1)S(1)}, bf16[256,256]{1,0:T(8,128)(2,1)S(1)}, u32[]{:S(2)}, u32[]{:S(2)}) collective-permute-start(bf16[256,256]{1,0:T(8,128)(2,1)S(1)} %add_convert_fusion.3), channel_id=1, source_target_pairs={{0,4},{1,3},{4,8},{5,1},{8,12},{9,5},{12,14},{13,9},{14,10},{15,13... | collective-permute-start | bytes 393224 | tf_op jit(solution)/shard_map/ppermute | solution.py:51
  53.2 7.7 %collective-permute-start.29 = (bf16[256,256]{1,0:T(8,128)(2,1)S(1)}, bf16[256,256]{1,0:T(8,128)(2,1)S(1)}, u32[]{:S(2)}, u32[]{:S(2)}) collective-permute-start(bf16[256,256]{1,0:T(8,128)(2,1)S(1)} %add_convert_fusion), channel_id=1, source_target_pairs={{0,2},{1,5},{4,0},{5,9},{8,4},{9,13},{12,8},{13,15},{14,12},{15,11... | collective-permute-start | bytes 393224 | tf_op jit(solution)/shard_map/ppermute | solution.py:51
  58.7 6.4 %collective-permute-start.26 = (bf16[256,256]{1,0:T(8,128)(2,1)S(1)}, bf16[256,256]{1,0:T(8,128)(2,1)S(1)}, u32[]{:S(2)}, u32[]{:S(2)}) collective-permute-start(bf16[256,256]{1,0:T(8,128)(2,1)S(1)} %add_convert_fusion.2), channel_id=1, source_target_pairs={{0,4},{1,3},{4,8},{5,1},{8,12},{9,5},{12,14},{13,9},{14,10},{15,13... | collective-permute-start | bytes 393224 | tf_op jit(solution)/shard_map/ppermute | solution.py:51
  58.9 6.4 %collective-permute-start.24 = (bf16[256,256]{1,0:T(8,128)(2,1)S(1)}, bf16[256,256]{1,0:T(8,128)(2,1)S(1)}, u32[]{:S(2)}, u32[]{:S(2)}) collective-permute-start(bf16[256,256]{1,0:T(8,128)(2,1)S(1)} %add_convert_fusion.4), channel_id=1, source_target_pairs={{0,2},{1,5},{4,0},{5,9},{8,4},{9,13},{12,8},{13,15},{14,12},{15,11... | collective-permute-start | bytes 393224 | tf_op jit(solution)/shard_map/ppermute | solution.py:51
  65.3 5.9 %collective-permute-start.34 = (bf16[256,256]{1,0:T(8,128)(2,1)S(1)}, bf16[256,256]{1,0:T(8,128)(2,1)S(1)}, u32[]{:S(2)}, u32[]{:S(2)}) collective-permute-start(bf16[256,256]{1,0:T(8,128)(2,1)S(1)} %multiply_convert_fusion.refs_1_), channel_id=1, source_target_pairs={{0,2},{1,5},{4,0},{5,9},{8,4},{9,13},{12,8},{13,15},{14,12},{15,11... | collective-permute-start | bytes 393224 | tf_op jit(solution)/shard_map/ppermute | solution.py:51
  67.4 6.4 %collective-permute-start.30 = (bf16[256,256]{1,0:T(8,128)(2,1)S(1)}, bf16[256,256]{1,0:T(8,128)(2,1)S(1)}, u32[]{:S(2)}, u32[]{:S(2)}) collective-permute-start(bf16[256,256]{1,0:T(8,128)(2,1)S(1)} %fusion.1.refs_0_), channel_id=1, source_target_pairs={{0,4},{1,3},{4,8},{5,1},{8,12},{9,5},{12,14},{13,9},{14,10},{15,13... | collective-permute-start | bytes 393224 | tf_op jit(solution)/shard_map/ppermute | solution.py:51
  67.4 7.4 %collective-permute-start.39 = (bf16[256,256]{1,0:T(8,128)(2,1)S(1)}, bf16[256,256]{1,0:T(8,128)(2,1)S(1)}, u32[]{:S(2)}, u32[]{:S(2)}) collective-permute-start(bf16[256,256]{1,0:T(8,128)(2,1)S(1)} %fusion.1.refs_0_), channel_id=1, source_target_pairs={{0,2},{1,5},{4,0},{5,9},{8,4},{9,13},{12,8},{13,15},{14,12},{15,11... | collective-permute-start | bytes 393224 | tf_op jit(solution)/shard_map/ppermute | solution.py:51
  69.4 7.5 %collective-permute-start.38 = (bf16[256,256]{1,0:T(8,128)(2,1)S(1)}, bf16[256,256]{1,0:T(8,128)(2,1)S(1)}, u32[]{:S(2)}, u32[]{:S(2)}) collective-permute-start(bf16[256,256]{1,0:T(8,128)(2,1)S(1)} %multiply_convert_fusion.refs_1_), channel_id=1, source_target_pairs={{0,4},{1,3},{4,8},{5,1},{8,12},{9,5},{12,14},{13,9},{14,10},{15,13... | collective-permute-start | bytes 393224 | tf_op jit(solution)/shard_map/ppermute | solution.py:51
  71.3 5.7 %collective-permute-start.35 = (bf16[256,256]{1,0:T(8,128)(2,1)S(1)}, bf16[256,256]{1,0:T(8,128)(2,1)S(1)}, u32[]{:S(2)}, u32[]{:S(2)}) collective-permute-start(bf16[256,256]{1,0:T(8,128)(2,1)S(1)} %collective-permute-done.34.refs_3_), channel_id=1, source_target_pairs={{0,2},{1,5},{4,0},{5,9},{8,4},{9,13},{12,8},{13,15},{14,12},{15,11... | collective-permute-start | bytes 393224 | tf_op jit(solution)/shard_map/ppermute | solution.py:51
  73.8 5.7 %collective-permute-start.31 = (bf16[256,256]{1,0:T(8,128)(2,1)S(1)}, bf16[256,256]{1,0:T(8,128)(2,1)S(1)}, u32[]{:S(2)}, u32[]{:S(2)}) collective-permute-start(bf16[256,256]{1,0:T(8,128)(2,1)S(1)} %collective-permute-done.30.refs_0_), channel_id=1, source_target_pairs={{0,4},{1,3},{4,8},{5,1},{8,12},{9,5},{12,14},{13,9},{14,10},{15,13... | collective-permute-start | bytes 393224 | tf_op jit(solution)/shard_map/ppermute | solution.py:51
  74.9 6.3 %collective-permute-start.41 = (bf16[256,256]{1,0:T(8,128)(2,1)S(1)}, bf16[256,256]{1,0:T(8,128)(2,1)S(1)}, u32[]{:S(2)}, u32[]{:S(2)}) collective-permute-start(bf16[256,256]{1,0:T(8,128)(2,1)S(1)} %collective-permute-done.39.refs_2_), channel_id=1, source_target_pairs={{0,2},{1,5},{4,0},{5,9},{8,4},{9,13},{12,8},{13,15},{14,12},{15,11... | collective-permute-start | bytes 393224 | tf_op jit(solution)/shard_map/ppermute | solution.py:51
  76.9 6.3 %collective-permute-start.36 = (bf16[256,256]{1,0:T(8,128)(2,1)S(1)}, bf16[256,256]{1,0:T(8,128)(2,1)S(1)}, u32[]{:S(2)}, u32[]{:S(2)}) collective-permute-start(bf16[256,256]{1,0:T(8,128)(2,1)S(1)} %collective-permute-done.35.refs_7_), channel_id=1, source_target_pairs={{0,2},{1,5},{4,0},{5,9},{8,4},{9,13},{12,8},{13,15},{14,12},{15,11... | collective-permute-start | bytes 393224 | tf_op jit(solution)/shard_map/ppermute | solution.py:51
  83.2 5.4 %collective-permute-start.37 = (bf16[256,256]{1,0:T(8,128)(2,1)S(1)}, bf16[256,256]{1,0:T(8,128)(2,1)S(1)}, u32[]{:S(2)}, u32[]{:S(2)}) collective-permute-start(bf16[256,256]{1,0:T(8,128)(2,1)S(1)} %collective-permute-done.36.refs_11_), channel_id=1, source_target_pairs={{0,2},{1,5},{4,0},{5,9},{8,4},{9,13},{12,8},{13,15},{14,12},{15,11... | collective-permute-start | bytes 393224 | tf_op jit(solution)/shard_map/ppermute | solution.py:51
  (16 other events, 121.0 us)

commit v13 on v12

--- a/solution.py
+++ b/solution.py
@@ -272,7 +272,7 @@
     inputs = [[part] + [None] * (size - 1) for part in halves(residual_in[0])]
     turned_own = []
     for chain in chains:
-        source = inputs[chain][0] if chain == 0 else after(inputs[chain][0], turned_own[0])
+        source = inputs[chain][0]
         turned_own += call(turn_own_kernel, [shape((wide, half), BF16)], 0, [starts, source])
     for s in range(1, reach + 1):
         gather_step(inputs, s, turned_own if s == 1 else None)
@@ -318,15 +318,15 @@
             if (chain, way) in moving:
                 total = total + moving[chain, way].astype(F32)
         if chain == 1:
-            wanted = after(wanted, errors[0][0])
+            wanted = after(wanted, codes)
         errors.append([((total - wanted.astype(F32)) * err_scale).astype(BF16)] + [None] * (size - 1))
 
-    def back(slots, before, decoders):
+    def back(slots, before):
         return call(
             functools.partial(back_kernel, slots, before is None),
             [shape((len(slots), 2 * lat, wide), F32), shape((2, half, 2 * lat), F32)],
             4 * unit * len(slots),
-            [starts] + both_chains(errors, slots) + [decoders] + both_t + ([] if before is None else [before]),
+            [starts] + both_chains(errors, slots) + [stacked] + both_t + ([] if before is None else [before]),
         )
 
     groups, outers, acc, pending = [], [], None, [0]
@@ -337,13 +337,13 @@
         0,
         [starts] + turned_own + arrived + both_chains(inputs, range(1, size))[1:],
     )[0]
-    groups = [(0,), tuple(range(1, far))] if reach > 1 else [(0,)]
-    outer, acc = back(groups[0], None, stacked)
-    outers = [outer]
     for s in range(1, reach + 1):
         gather_step(errors, s, (turned, turned) if s == 2 else None)
-    if reach > 1:
-        outer, acc = back(groups[1], acc, stacked)
+    cut = 1 + 2 * min(1, reach - 1)
+    groups = [group for group in (tuple(range(cut)), tuple(range(cut, far))) if group]
+    outers, acc = [], None
+    for group in groups:
+        outer, acc = back(group, acc)
         outers.append(outer)
     last_same, back_own, sent, high = call(
         functools.partial(last_back_kernel, groups, far),

time: 97.5 us -> 90.4 us (0.927)
  waiting for transfers between devices: 31.6 us -> 23.9 us
    ppermute x42, waiting for transfers between devices: 29.3 us -> 21.7 us  [hop(): return lax.ppermute(shard, ('latent', 'layer'), pairs)]
  transfers between devices with their start and end apart: 45 -> 45, of which waited for: 26 -> 25; matrix products, arithmetic and copies ran while one was open for 2% -> 2% of each run, Pallas kernels for 8% -> 10%
where the time goes in v13:
time: 90.4 us; the launch traced here: 90.1 us
  starting transfers between devices  48.6 us (54%)
  waiting for transfers between devices  23.9 us (26%)
  Pallas kernels  13.9 us (15%)
  other arithmetic  1.63 us (2%)
  local copies, waits for them, and re-layouts  1.15 us (1%)
  between operations  0.91 us (1%)
    ppermute x42, starting transfers between devices, hop(): return lax.ppermute(shard, ('latent', 'layer'), pairs)  44.7 us
    ppermute x42, waiting for transfers between devices, hop(): return lax.ppermute(shard, ('latent', 'layer'), pairs)  21.7 us
    pallas_call x12, Pallas kernels, call(): pl.pallas_call(kernel, out_shape=outs, in_specs=[spec(pltpu.SMEM)] + [spe...  13.9 us
    ppermute x3, starting transfers between devices, passed_along(): return lax.ppermute(shard, axis, pairs)  3.89 us
    ppermute x3, waiting for transfers between devices, passed_along(): return lax.ppermute(shard, axis, pairs)  2.27 us
  transfers between devices with their start and end apart: 45, of which 25 were waited for; matrix products, arithmetic and copies ran while one was open for 2% of the time, Pallas kernels for 10%

profile of v13, /device:TPU:0, one launch (start us, length us, event | category | flops | bytes accessed | tf_op | source)
XLA Modules:
  0.0 90.1 jit_solution(18200956349588138232)
XLA Ops:
  1.7 3.0 %collective-permute-start.4 = (bf16[256,256]{1,0:T(8,128)(2,1)S(1)}, bf16[256,256]{1,0:T(8,128)(2,1)S(1)}, u32[]{:S(2)}, u32[]{:S(2)}) collective-permute-start(bf16[256,256]{1,0:T(8,128)(2,1)S(1)} %get-tuple-element.47.shard.refs_1_), channel_id=1, source_target_pairs={{0,2},{1,5},{4,0},{5,9},{8,4},{9,13},{12,8},{13,15},{14,12},{15,11... | collective-permute-start | bytes 393224 | tf_op jit(solution)/shard_map/ppermute | solution.py:51
  5.6 1.9 %collective-permute-start.9 = (bf16[256,256]{1,0:T(8,128)(2,1)S(1)}, bf16[256,256]{1,0:T(8,128)(2,1)S(1)}, u32[]{:S(2)}, u32[]{:S(2)}) collective-permute-start(bf16[256,256]{1,0:T(8,128)(2,1)S(1)} %get-tuple-element.48.shard.refs_0_), channel_id=1, source_target_pairs={{0,2},{1,5},{4,0},{5,9},{8,4},{9,13},{12,8},{13,15},{14,12},{15,11... | collective-permute-start | bytes 393224 | tf_op jit(solution)/shard_map/ppermute | solution.py:51
  8.6 1.6 %collective-permute-start.5 = (bf16[256,256]{1,0:T(8,128)(2,1)S(1)}, bf16[256,256]{1,0:T(8,128)(2,1)S(1)}, u32[]{:S(2)}, u32[]{:S(2)}) collective-permute-start(bf16[256,256]{1,0:T(8,128)(2,1)S(1)} %collective-permute-done.4.refs_5_.refs_3_), channel_id=1, source_target_pairs={{0,2},{1,5},{4,0},{5,9},{8,4},{9,13},{12,8},{13,15},{14,12},{15,11... | collective-permute-start | bytes 393224 | tf_op jit(solution)/shard_map/ppermute | solution.py:51
  11.0 1.3 %collective-permute-start.14 = (bf16[128,1024]{1,0:T(8,128)(2,1)}, bf16[128,1024]{1,0:T(8,128)(2,1)S(1)}, u32[]{:S(2)}, u32[]{:S(2)}) collective-permute-start(bf16[128,1024]{1,0:T(8,128)(2,1)} %param.11), channel_id=1, source_target_pairs={{0,1},{2,3},{4,5},{6,7},{8,9},{10,11},{12,13},{14,15},{16,17},{18,... | collective-permute-start | bytes 786440 | tf_op jit(solution)/shard_map/ppermute | solution.py:23
  12.3 2.1 %collective-permute-start.11 = (bf16[256,256]{1,0:T(8,128)(2,1)S(1)}, bf16[256,256]{1,0:T(8,128)(2,1)S(1)}, u32[]{:S(2)}, u32[]{:S(2)}) collective-permute-start(bf16[256,256]{1,0:T(8,128)(2,1)S(1)} %collective-permute-done.9.refs_4_.refs_2_), channel_id=1, source_target_pairs={{0,2},{1,5},{4,0},{5,9},{8,4},{9,13},{12,8},{13,15},{14,12},{15,11... | collective-permute-start | bytes 393224 | tf_op jit(solution)/shard_map/ppermute | solution.py:51
  14.8 1.6 %collective-permute-start.6 = (bf16[256,256]{1,0:T(8,128)(2,1)S(1)}, bf16[256,256]{1,0:T(8,128)(2,1)S(1)}, u32[]{:S(2)}, u32[]{:S(2)}) collective-permute-start(bf16[256,256]{1,0:T(8,128)(2,1)S(1)} %collective-permute-done.5.refs_9_.refs_7_), channel_id=1, source_target_pairs={{0,2},{1,5},{4,0},{5,9},{8,4},{9,13},{12,8},{13,15},{14,12},{15,11... | collective-permute-start | bytes 393224 | tf_op jit(solution)/shard_map/ppermute | solution.py:51
  18.4 2.4 %collective-permute-start.13 = (bf16[256,256]{1,0:T(8,128)(2,1)S(1)}, bf16[256,256]{1,0:T(8,128)(2,1)S(1)}, u32[]{:S(2)}, u32[]{:S(2)}) collective-permute-start(bf16[256,256]{1,0:T(8,128)(2,1)S(1)} %collective-permute-done.11.refs_8_.refs_6_), channel_id=1, source_target_pairs={{0,2},{1,5},{4,0},{5,9},{8,4},{9,13},{12,8},{13,15},{14,12},{15,11... | collective-permute-start | bytes 393224 | tf_op jit(solution)/shard_map/ppermute | solution.py:51
  21.2 2.4 %collective-permute-start.7 = (bf16[256,256]{1,0:T(8,128)(2,1)S(1)}, bf16[256,256]{1,0:T(8,128)(2,1)S(1)}, u32[]{:S(2)}, u32[]{:S(2)}) collective-permute-start(bf16[256,256]{1,0:T(8,128)(2,1)S(1)} %collective-permute-done.6.refs_13_.refs_11_), channel_id=1, source_target_pairs={{0,2},{1,5},{4,0},{5,9},{8,4},{9,13},{12,8},{13,15},{14,12},{15,11... | collective-permute-start | bytes 393224 | tf_op jit(solution)/shard_map/ppermute | solution.py:51
  26.9 1.6 %collective-permute-done.3.refs_0_.refs_12_ = bf16[256,256]{1,0:T(8,128)(2,1)S(1)} collective-permute-done((bf16[256,256]{1,0:T(8,128)(2,1)S(1)}, bf16[256,256]{1,0:T(8,128)(2,1)S(1)}, u32[]{:S(2)}, u32[]{:S(2)}) %collective-permute-start.3) | collective-permute-done | bytes 131104 | tf_op jit(solution)/shard_map/ppermute | solution.py:51
  29.3 1.3 %collective-permute-start.15 = (bf16[512,128]{1,0:T(8,128)(2,1)S(1)}, bf16[512,128]{1,0:T(8,128)(2,1)S(1)}, u32[]{:S(2)}, u32[]{:S(2)}) collective-permute-start(bf16[512,128]{1,0:T(8,128)(2,1)S(1)} %get-tuple-element.51.codes), channel_id=1, source_target_pairs={{0,1},{2,3},{4,5},{6,7},{8,9},{10,11},{12,13},{14,15},{16,17},{18,... | collective-permute-start | bytes 393224 | tf_op jit(solution)/shard_map/ppermute | solution.py:23
  32.4 1.6 %collective-permute-start.18 = (bf16[256,256]{1,0:T(8,128)(2,1)S(1)}, bf16[256,256]{1,0:T(8,128)(2,1)S(1)}, u32[]{:S(2)}, u32[]{:S(2)}) collective-permute-start(bf16[256,256]{1,0:T(8,128)(2,1)S(1)} %get-tuple-element.57), channel_id=1, source_target_pairs={{0,2},{1,5},{4,0},{5,9},{8,4},{9,13},{12,8},{13,15},{14,12},{15,11... | collective-permute-start | bytes 393224 | tf_op jit(solution)/shard_map/ppermute | solution.py:51
  36.0 1.8 %collective-permute-start.27 = (bf16[256,256]{1,0:T(8,128)(2,1)S(1)}, bf16[256,256]{1,0:T(8,128)(2,1)S(1)}, u32[]{:S(2)}, u32[]{:S(2)}) collective-permute-start(bf16[256,256]{1,0:T(8,128)(2,1)S(1)} %get-tuple-element.72), channel_id=1, source_target_pairs={{0,2},{1,5},{4,0},{5,9},{8,4},{9,13},{12,8},{13,15},{14,12},{15,11... | collective-permute-start | bytes 393224 | tf_op jit(solution)/shard_map/ppermute | solution.py:51
  38.3 2.0 %collective-permute-start.21 = (bf16[256,256]{1,0:T(8,128)(2,1)S(1)}, bf16[256,256]{1,0:T(8,128)(2,1)S(1)}, u32[]{:S(2)}, u32[]{:S(2)}) collective-permute-start(bf16[256,256]{1,0:T(8,128)(2,1)S(1)} %add_convert_fusion.6), channel_id=1, source_target_pairs={{0,2},{1,5},{4,0},{5,9},{8,4},{9,13},{12,8},{13,15},{14,12},{15,11... | collective-permute-start | bytes 393224 | tf_op jit(solution)/shard_map/ppermute | solution.py:51
  40.5 1.5 %collective-permute-done.16 = bf16[256,256]{1,0:T(8,128)(2,1)S(1)} collective-permute-done((bf16[256,256]{1,0:T(8,128)(2,1)S(1)}, bf16[256,256]{1,0:T(8,128)(2,1)S(1)}, u32[]{:S(2)}, u32[]{:S(2)}) %collective-permute-start.16) | collective-permute-done | bytes 131104 | tf_op jit(solution)/shard_map/ppermute | solution.py:51
  42.2 2.0 %collective-permute-start.28 = (bf16[256,256]{1,0:T(8,128)(2,1)S(1)}, bf16[256,256]{1,0:T(8,128)(2,1)S(1)}, u32[]{:S(2)}, u32[]{:S(2)}) collective-permute-start(bf16[256,256]{1,0:T(8,128)(2,1)S(1)} %add_convert_fusion.1), channel_id=1, source_target_pairs={{0,2},{1,5},{4,0},{5,9},{8,4},{9,13},{12,8},{13,15},{14,12},{15,11... | collective-permute-start | bytes 393224 | tf_op jit(solution)/shard_map/ppermute | solution.py:51
  44.8 2.0 %collective-permute-start.23 = (bf16[256,256]{1,0:T(8,128)(2,1)S(1)}, bf16[256,256]{1,0:T(8,128)(2,1)S(1)}, u32[]{:S(2)}, u32[]{:S(2)}) collective-permute-start(bf16[256,256]{1,0:T(8,128)(2,1)S(1)} %add_convert_fusion.5), channel_id=1, source_target_pairs={{0,2},{1,5},{4,0},{5,9},{8,4},{9,13},{12,8},{13,15},{14,12},{15,11... | collective-permute-start | bytes 393224 | tf_op jit(solution)/shard_map/ppermute | solution.py:51
  47.0 1.7 %collective-permute-done.19 = bf16[256,256]{1,0:T(8,128)(2,1)S(1)} collective-permute-done((bf16[256,256]{1,0:T(8,128)(2,1)S(1)}, bf16[256,256]{1,0:T(8,128)(2,1)S(1)}, u32[]{:S(2)}, u32[]{:S(2)}) %collective-permute-start.19) | collective-permute-done | bytes 131104 | tf_op jit(solution)/shard_map/ppermute | solution.py:51
  48.8 2.1 %collective-permute-start.29 = (bf16[256,256]{1,0:T(8,128)(2,1)S(1)}, bf16[256,256]{1,0:T(8,128)(2,1)S(1)}, u32[]{:S(2)}, u32[]{:S(2)}) collective-permute-start(bf16[256,256]{1,0:T(8,128)(2,1)S(1)} %add_convert_fusion), channel_id=1, source_target_pairs={{0,2},{1,5},{4,0},{5,9},{8,4},{9,13},{12,8},{13,15},{14,12},{15,11... | collective-permute-start | bytes 393224 | tf_op jit(solution)/shard_map/ppermute | solution.py:51
  51.4 2.0 %collective-permute-start.24 = (bf16[256,256]{1,0:T(8,128)(2,1)S(1)}, bf16[256,256]{1,0:T(8,128)(2,1)S(1)}, u32[]{:S(2)}, u32[]{:S(2)}) collective-permute-start(bf16[256,256]{1,0:T(8,128)(2,1)S(1)} %add_convert_fusion.4), channel_id=1, source_target_pairs={{0,2},{1,5},{4,0},{5,9},{8,4},{9,13},{12,8},{13,15},{14,12},{15,11... | collective-permute-start | bytes 393224 | tf_op jit(solution)/shard_map/ppermute | solution.py:51
  53.5 2.6 %collective-permute-done.22 = bf16[256,256]{1,0:T(8,128)(2,1)S(1)} collective-permute-done((bf16[256,256]{1,0:T(8,128)(2,1)S(1)}, bf16[256,256]{1,0:T(8,128)(2,1)S(1)}, u32[]{:S(2)}, u32[]{:S(2)}) %collective-permute-start.22) | collective-permute-done | bytes 131104 | tf_op jit(solution)/shard_map/ppermute | solution.py:51
  56.7 1.9 %collective-permute-start.34 = (bf16[256,256]{1,0:T(8,128)(2,1)S(1)}, bf16[256,256]{1,0:T(8,128)(2,1)S(1)}, u32[]{:S(2)}, u32[]{:S(2)}) collective-permute-start(bf16[256,256]{1,0:T(8,128)(2,1)S(1)} %multiply_convert_fusion.refs_1_), channel_id=1, source_target_pairs={{0,2},{1,5},{4,0},{5,9},{8,4},{9,13},{12,8},{13,15},{14,12},{15,11... | collective-permute-start | bytes 393224 | tf_op jit(solution)/shard_map/ppermute | solution.py:51
  59.0 2.5 %collective-permute-start.38 = (bf16[256,256]{1,0:T(8,128)(2,1)S(1)}, bf16[256,256]{1,0:T(8,128)(2,1)S(1)}, u32[]{:S(2)}, u32[]{:S(2)}) collective-permute-start(bf16[256,256]{1,0:T(8,128)(2,1)S(1)} %multiply_convert_fusion.refs_1_), channel_id=1, source_target_pairs={{0,4},{1,3},{4,8},{5,1},{8,12},{9,5},{12,14},{13,9},{14,10},{15,13... | collective-permute-start | bytes 393224 | tf_op jit(solution)/shard_map/ppermute | solution.py:51
  61.4 1.7 %collective-permute-done.34.refs_5_ = bf16[256,256]{1,0:T(8,128)(2,1)S(1)} collective-permute-done((bf16[256,256]{1,0:T(8,128)(2,1)S(1)}, bf16[256,256]{1,0:T(8,128)(2,1)S(1)}, u32[]{:S(2)}, u32[]{:S(2)}) %collective-permute-start.34) | collective-permute-done | bytes 131104 | tf_op jit(solution)/shard_map/ppermute | solution.py:51
  63.1 1.8 %collective-permute-start.35 = (bf16[256,256]{1,0:T(8,128)(2,1)S(1)}, bf16[256,256]{1,0:T(8,128)(2,1)S(1)}, u32[]{:S(2)}, u32[]{:S(2)}) collective-permute-start(bf16[256,256]{1,0:T(8,128)(2,1)S(1)} %collective-permute-done.34.refs_5_), channel_id=1, source_target_pairs={{0,2},{1,5},{4,0},{5,9},{8,4},{9,13},{12,8},{13,15},{14,12},{15,11... | collective-permute-start | bytes 393224 | tf_op jit(solution)/shard_map/ppermute | solution.py:51
  68.0 1.3 %collective-permute-start.41 = (bf16[256,256]{1,0:T(8,128)(2,1)S(1)}, bf16[256,256]{1,0:T(8,128)(2,1)S(1)}, u32[]{:S(2)}, u32[]{:S(2)}) collective-permute-start(bf16[256,256]{1,0:T(8,128)(2,1)S(1)} %collective-permute-done.39.refs_4_), channel_id=1, source_target_pairs={{0,2},{1,5},{4,0},{5,9},{8,4},{9,13},{12,8},{13,15},{14,12},{15,11... | collective-permute-start | bytes 393224 | tf_op jit(solution)/shard_map/ppermute | solution.py:51
  69.4 1.5 %collective-permute-start.36 = (bf16[256,256]{1,0:T(8,128)(2,1)S(1)}, bf16[256,256]{1,0:T(8,128)(2,1)S(1)}, u32[]{:S(2)}, u32[]{:S(2)}) collective-permute-start(bf16[256,256]{1,0:T(8,128)(2,1)S(1)} %collective-permute-done.35.refs_3_), channel_id=1, source_target_pairs={{0,2},{1,5},{4,0},{5,9},{8,4},{9,13},{12,8},{13,15},{14,12},{15,11... | collective-permute-start | bytes 393224 | tf_op jit(solution)/shard_map/ppermute | solution.py:51
  71.4 2.4 %collective-permute-done.40.refs_1_ = bf16[256,256]{1,0:T(8,128)(2,1)S(1)} collective-permute-done((bf16[256,256]{1,0:T(8,128)(2,1)S(1)}, bf16[256,256]{1,0:T(8,128)(2,1)S(1)}, u32[]{:S(2)}, u32[]{:S(2)}) %collective-permute-start.40) | collective-permute-done | bytes 131104 | tf_op jit(solution)/shard_map/ppermute | solution.py:51
  74.4 1.5 %collective-permute-start.43 = (bf16[256,256]{1,0:T(8,128)(2,1)S(1)}, bf16[256,256]{1,0:T(8,128)(2,1)S(1)}, u32[]{:S(2)}, u32[]{:S(2)}) collective-permute-start(bf16[256,256]{1,0:T(8,128)(2,1)S(1)} %collective-permute-done.41.refs_2_), channel_id=1, source_target_pairs={{0,2},{1,5},{4,0},{5,9},{8,4},{9,13},{12,8},{13,15},{14,12},{15,11... | collective-permute-start | bytes 393224 | tf_op jit(solution)/shard_map/ppermute | solution.py:51
  83.3 1.3 %collective-permute-start.44 = (f32[1536,128]{1,0:T(8,128)S(1)}, f32[1536,128]{1,0:T(8,128)S(1)}, u32[]{:S(2)}, u32[]{:S(2)}) collective-permute-start(f32[1536,128]{1,0:T(8,128)S(1)} %get-tuple-element.84), channel_id=1, source_target_pairs={{1,0},{3,2},{5,4},{7,6},{9,8},{11,10},{13,12},{15,14},{17,16},{19,... | collective-permute-start | bytes 2359304 | tf_op jit(solution)/shard_map/ppermute | solution.py:23
  84.6 1.6 %shard_map.104 = f32[1,128,2048]{2,1,0:T(8,128)} custom-call(s32[9]{0:T(128)S(1)} %stack.39.starts, f32[128,256]{1,0:T(8,128)S(1)} %get-tuple-element.88.refs_0_, f32[3,256,256]{2,1,0:T(8,128)S(1)} %get-tuple-element.77.refs_5_.refs_1_, f32[4,256,256]{2,1,0:T(8,128)S(1)} %get-tuple-element.81.refs_6_.refs_2_), custom_call_target="tpu_custom_call" | custom-call | bytes 1024 | tf_op jit(solution)/shard_map/pallas_call | solution.py:64
  86.1 1.3 %collective-permute-done.44.arrived = f32[1536,128]{1,0:T(8,128)S(1)} collective-permute-done((f32[1536,128]{1,0:T(8,128)S(1)}, f32[1536,128]{1,0:T(8,128)S(1)}, u32[]{:S(2)}, u32[]{:S(2)}) %collective-permute-start.44) | collective-permute-done | bytes 786464 | tf_op jit(solution)/shard_map/ppermute | solution.py:23
  87.4 2.7 %shard_map.103 = (f32[1,2048,128]{2,1,0:T(8,128)}, f32[1,128]{1,0:T(1,128)}, f32[128,1024]{1,0:T(8,128)}) custom-call(s32[9]{0:T(128)S(1)} %stack.39.starts, bf16[2048,512]{1,0:T(8,128)(2,1)S(1)} %shard_map.99.turned, f32[512,128]{1,0:T(8,128)S(1)} %get-tuple-element.66.preact, f32[512,128]{1,0:T(8,128)S(1)} %get-tuple-element.83.back_own, ...), custom_call_target="tpu_custom_call" | custom-call | flops 268435456 | bytes 1024 | tf_op jit(solution)/shard_map/pallas_call | solution.py:64
  (92 shorter events, 29.3 us)
Async XLA Ops:
  1.7 6.9 %collective-permute-start.4 = (bf16[256,256]{1,0:T(8,128)(2,1)S(1)}, bf16[256,256]{1,0:T(8,128)(2,1)S(1)}, u32[]{:S(2)}, u32[]{:S(2)}) collective-permute-start(bf16[256,256]{1,0:T(8,128)(2,1)S(1)} %get-tuple-element.47.shard.refs_1_), channel_id=1, source_target_pairs={{0,2},{1,5},{4,0},{5,9},{8,4},{9,13},{12,8},{13,15},{14,12},{15,11... | collective-permute-start | bytes 393224 | tf_op jit(solution)/shard_map/ppermute | solution.py:51
  4.7 6.3 %collective-permute-start = (bf16[256,256]{1,0:T(8,128)(2,1)S(1)}, bf16[256,256]{1,0:T(8,128)(2,1)S(1)}, u32[]{:S(2)}, u32[]{:S(2)}) collective-permute-start(bf16[256,256]{1,0:T(8,128)(2,1)S(1)} %get-tuple-element.48.shard.refs_0_), channel_id=1, source_target_pairs={{0,4},{1,3},{4,8},{5,1},{8,12},{9,5},{12,14},{13,9},{14,10},{15,13... | collective-permute-start | bytes 393224 | tf_op jit(solution)/shard_map/ppermute | solution.py:51
  5.6 6.7 %collective-permute-start.9 = (bf16[256,256]{1,0:T(8,128)(2,1)S(1)}, bf16[256,256]{1,0:T(8,128)(2,1)S(1)}, u32[]{:S(2)}, u32[]{:S(2)}) collective-permute-start(bf16[256,256]{1,0:T(8,128)(2,1)S(1)} %get-tuple-element.48.shard.refs_0_), channel_id=1, source_target_pairs={{0,2},{1,5},{4,0},{5,9},{8,4},{9,13},{12,8},{13,15},{14,12},{15,11... | collective-permute-start | bytes 393224 | tf_op jit(solution)/shard_map/ppermute | solution.py:51
  8.1 6.3 %collective-permute-start.8 = (bf16[256,256]{1,0:T(8,128)(2,1)S(1)}, bf16[256,256]{1,0:T(8,128)(2,1)S(1)}, u32[]{:S(2)}, u32[]{:S(2)}) collective-permute-start(bf16[256,256]{1,0:T(8,128)(2,1)S(1)} %get-tuple-element.47.shard.refs_1_), channel_id=1, source_target_pairs={{0,4},{1,3},{4,8},{5,1},{8,12},{9,5},{12,14},{13,9},{14,10},{15,13... | collective-permute-start | bytes 393224 | tf_op jit(solution)/shard_map/ppermute | solution.py:51
  8.6 6.2 %collective-permute-start.5 = (bf16[256,256]{1,0:T(8,128)(2,1)S(1)}, bf16[256,256]{1,0:T(8,128)(2,1)S(1)}, u32[]{:S(2)}, u32[]{:S(2)}) collective-permute-start(bf16[256,256]{1,0:T(8,128)(2,1)S(1)} %collective-permute-done.4.refs_5_.refs_3_), channel_id=1, source_target_pairs={{0,2},{1,5},{4,0},{5,9},{8,4},{9,13},{12,8},{13,15},{14,12},{15,11... | collective-permute-start | bytes 393224 | tf_op jit(solution)/shard_map/ppermute | solution.py:51
  11.0 6.4 %collective-permute-start.1 = (bf16[256,256]{1,0:T(8,128)(2,1)S(1)}, bf16[256,256]{1,0:T(8,128)(2,1)S(1)}, u32[]{:S(2)}, u32[]{:S(2)}) collective-permute-start(bf16[256,256]{1,0:T(8,128)(2,1)S(1)} %collective-permute-done.refs_2_.refs_0_), channel_id=1, source_target_pairs={{0,4},{1,3},{4,8},{5,1},{8,12},{9,5},{12,14},{13,9},{14,10},{15,13... | collective-permute-start | bytes 393224 | tf_op jit(solution)/shard_map/ppermute | solution.py:51
  11.0 12.8 %collective-permute-start.14 = (bf16[128,1024]{1,0:T(8,128)(2,1)}, bf16[128,1024]{1,0:T(8,128)(2,1)S(1)}, u32[]{:S(2)}, u32[]{:S(2)}) collective-permute-start(bf16[128,1024]{1,0:T(8,128)(2,1)} %param.11), channel_id=1, source_target_pairs={{0,1},{2,3},{4,5},{6,7},{8,9},{10,11},{12,13},{14,15},{16,17},{18,... | collective-permute-start | bytes 786440 | tf_op jit(solution)/shard_map/ppermute | solution.py:23
  12.3 6.1 %collective-permute-start.11 = (bf16[256,256]{1,0:T(8,128)(2,1)S(1)}, bf16[256,256]{1,0:T(8,128)(2,1)S(1)}, u32[]{:S(2)}, u32[]{:S(2)}) collective-permute-start(bf16[256,256]{1,0:T(8,128)(2,1)S(1)} %collective-permute-done.9.refs_4_.refs_2_), channel_id=1, source_target_pairs={{0,2},{1,5},{4,0},{5,9},{8,4},{9,13},{12,8},{13,15},{14,12},{15,11... | collective-permute-start | bytes 393224 | tf_op jit(solution)/shard_map/ppermute | solution.py:51
  14.4 6.4 %collective-permute-start.10 = (bf16[256,256]{1,0:T(8,128)(2,1)S(1)}, bf16[256,256]{1,0:T(8,128)(2,1)S(1)}, u32[]{:S(2)}, u32[]{:S(2)}) collective-permute-start(bf16[256,256]{1,0:T(8,128)(2,1)S(1)} %collective-permute-done.8.refs_3_.refs_1_), channel_id=1, source_target_pairs={{0,4},{1,3},{4,8},{5,1},{8,12},{9,5},{12,14},{13,9},{14,10},{15,13... | collective-permute-start | bytes 393224 | tf_op jit(solution)/shard_map/ppermute | solution.py:51
  14.8 6.4 %collective-permute-start.6 = (bf16[256,256]{1,0:T(8,128)(2,1)S(1)}, bf16[256,256]{1,0:T(8,128)(2,1)S(1)}, u32[]{:S(2)}, u32[]{:S(2)}) collective-permute-start(bf16[256,256]{1,0:T(8,128)(2,1)S(1)} %collective-permute-done.5.refs_9_.refs_7_), channel_id=1, source_target_pairs={{0,2},{1,5},{4,0},{5,9},{8,4},{9,13},{12,8},{13,15},{14,12},{15,11... | collective-permute-start | bytes 393224 | tf_op jit(solution)/shard_map/ppermute | solution.py:51
  17.4 6.2 %collective-permute-start.2 = (bf16[256,256]{1,0:T(8,128)(2,1)S(1)}, bf16[256,256]{1,0:T(8,128)(2,1)S(1)}, u32[]{:S(2)}, u32[]{:S(2)}) collective-permute-start(bf16[256,256]{1,0:T(8,128)(2,1)S(1)} %collective-permute-done.1.refs_6_.refs_4_), channel_id=1, source_target_pairs={{0,4},{1,3},{4,8},{5,1},{8,12},{9,5},{12,14},{13,9},{14,10},{15,13... | collective-permute-start | bytes 393224 | tf_op jit(solution)/shard_map/ppermute | solution.py:51
  18.4 6.7 %collective-permute-start.13 = (bf16[256,256]{1,0:T(8,128)(2,1)S(1)}, bf16[256,256]{1,0:T(8,128)(2,1)S(1)}, u32[]{:S(2)}, u32[]{:S(2)}) collective-permute-start(bf16[256,256]{1,0:T(8,128)(2,1)S(1)} %collective-permute-done.11.refs_8_.refs_6_), channel_id=1, source_target_pairs={{0,2},{1,5},{4,0},{5,9},{8,4},{9,13},{12,8},{13,15},{14,12},{15,11... | collective-permute-start | bytes 393224 | tf_op jit(solution)/shard_map/ppermute | solution.py:51
  34.0 6.3 %collective-permute-start.17 = (bf16[256,256]{1,0:T(8,128)(2,1)S(1)}, bf16[256,256]{1,0:T(8,128)(2,1)S(1)}, u32[]{:S(2)}, u32[]{:S(2)}) collective-permute-start(bf16[256,256]{1,0:T(8,128)(2,1)S(1)} %get-tuple-element.56), channel_id=1, source_target_pairs={{0,4},{1,3},{4,8},{5,1},{8,12},{9,5},{12,14},{13,9},{14,10},{15,13... | collective-permute-start | bytes 393224 | tf_op jit(solution)/shard_map/ppermute | solution.py:51
  35.7 6.3 %collective-permute-start.16 = (bf16[256,256]{1,0:T(8,128)(2,1)S(1)}, bf16[256,256]{1,0:T(8,128)(2,1)S(1)}, u32[]{:S(2)}, u32[]{:S(2)}) collective-permute-start(bf16[256,256]{1,0:T(8,128)(2,1)S(1)} %get-tuple-element.55), channel_id=1, source_target_pairs={{0,4},{1,3},{4,8},{5,1},{8,12},{9,5},{12,14},{13,9},{14,10},{15,13... | collective-permute-start | bytes 393224 | tf_op jit(solution)/shard_map/ppermute | solution.py:51
  36.0 6.2 %collective-permute-start.27 = (bf16[256,256]{1,0:T(8,128)(2,1)S(1)}, bf16[256,256]{1,0:T(8,128)(2,1)S(1)}, u32[]{:S(2)}, u32[]{:S(2)}) collective-permute-start(bf16[256,256]{1,0:T(8,128)(2,1)S(1)} %get-tuple-element.72), channel_id=1, source_target_pairs={{0,2},{1,5},{4,0},{5,9},{8,4},{9,13},{12,8},{13,15},{14,12},{15,11... | collective-permute-start | bytes 393224 | tf_op jit(solution)/shard_map/ppermute | solution.py:51
  38.3 6.5 %collective-permute-start.21 = (bf16[256,256]{1,0:T(8,128)(2,1)S(1)}, bf16[256,256]{1,0:T(8,128)(2,1)S(1)}, u32[]{:S(2)}, u32[]{:S(2)}) collective-permute-start(bf16[256,256]{1,0:T(8,128)(2,1)S(1)} %add_convert_fusion.6), channel_id=1, source_target_pairs={{0,2},{1,5},{4,0},{5,9},{8,4},{9,13},{12,8},{13,15},{14,12},{15,11... | collective-permute-start | bytes 393224 | tf_op jit(solution)/shard_map/ppermute | solution.py:51
  40.4 6.5 %collective-permute-start.20 = (bf16[256,256]{1,0:T(8,128)(2,1)S(1)}, bf16[256,256]{1,0:T(8,128)(2,1)S(1)}, u32[]{:S(2)}, u32[]{:S(2)}) collective-permute-start(bf16[256,256]{1,0:T(8,128)(2,1)S(1)} %add_convert_fusion.7), channel_id=1, source_target_pairs={{0,4},{1,3},{4,8},{5,1},{8,12},{9,5},{12,14},{13,9},{14,10},{15,13... | collective-permute-start | bytes 393224 | tf_op jit(solution)/shard_map/ppermute | solution.py:51
  42.1 6.6 %collective-permute-start.19 = (bf16[256,256]{1,0:T(8,128)(2,1)S(1)}, bf16[256,256]{1,0:T(8,128)(2,1)S(1)}, u32[]{:S(2)}, u32[]{:S(2)}) collective-permute-start(bf16[256,256]{1,0:T(8,128)(2,1)S(1)} %add_convert_fusion.9), channel_id=1, source_target_pairs={{0,4},{1,3},{4,8},{5,1},{8,12},{9,5},{12,14},{13,9},{14,10},{15,13... | collective-permute-start | bytes 393224 | tf_op jit(solution)/shard_map/ppermute | solution.py:51
  42.2 6.5 %collective-permute-start.28 = (bf16[256,256]{1,0:T(8,128)(2,1)S(1)}, bf16[256,256]{1,0:T(8,128)(2,1)S(1)}, u32[]{:S(2)}, u32[]{:S(2)}) collective-permute-start(bf16[256,256]{1,0:T(8,128)(2,1)S(1)} %add_convert_fusion.1), channel_id=1, source_target_pairs={{0,2},{1,5},{4,0},{5,9},{8,4},{9,13},{12,8},{13,15},{14,12},{15,11... | collective-permute-start | bytes 393224 | tf_op jit(solution)/shard_map/ppermute | solution.py:51
  44.8 6.5 %collective-permute-start.23 = (bf16[256,256]{1,0:T(8,128)(2,1)S(1)}, bf16[256,256]{1,0:T(8,128)(2,1)S(1)}, u32[]{:S(2)}, u32[]{:S(2)}) collective-permute-start(bf16[256,256]{1,0:T(8,128)(2,1)S(1)} %add_convert_fusion.5), channel_id=1, source_target_pairs={{0,2},{1,5},{4,0},{5,9},{8,4},{9,13},{12,8},{13,15},{14,12},{15,11... | collective-permute-start | bytes 393224 | tf_op jit(solution)/shard_map/ppermute | solution.py:51
  46.9 6.5 %collective-permute-start.25 = (bf16[256,256]{1,0:T(8,128)(2,1)S(1)}, bf16[256,256]{1,0:T(8,128)(2,1)S(1)}, u32[]{:S(2)}, u32[]{:S(2)}) collective-permute-start(bf16[256,256]{1,0:T(8,128)(2,1)S(1)} %add_convert_fusion.3), channel_id=1, source_target_pairs={{0,4},{1,3},{4,8},{5,1},{8,12},{9,5},{12,14},{13,9},{14,10},{15,13... | collective-permute-start | bytes 393224 | tf_op jit(solution)/shard_map/ppermute | solution.py:51
  48.7 7.4 %collective-permute-start.22 = (bf16[256,256]{1,0:T(8,128)(2,1)S(1)}, bf16[256,256]{1,0:T(8,128)(2,1)S(1)}, u32[]{:S(2)}, u32[]{:S(2)}) collective-permute-start(bf16[256,256]{1,0:T(8,128)(2,1)S(1)} %add_convert_fusion.8), channel_id=1, source_target_pairs={{0,4},{1,3},{4,8},{5,1},{8,12},{9,5},{12,14},{13,9},{14,10},{15,13... | collective-permute-start | bytes 393224 | tf_op jit(solution)/shard_map/ppermute | solution.py:51
  48.8 9.8 %collective-permute-start.29 = (bf16[256,256]{1,0:T(8,128)(2,1)S(1)}, bf16[256,256]{1,0:T(8,128)(2,1)S(1)}, u32[]{:S(2)}, u32[]{:S(2)}) collective-permute-start(bf16[256,256]{1,0:T(8,128)(2,1)S(1)} %add_convert_fusion), channel_id=1, source_target_pairs={{0,2},{1,5},{4,0},{5,9},{8,4},{9,13},{12,8},{13,15},{14,12},{15,11... | collective-permute-start | bytes 393224 | tf_op jit(solution)/shard_map/ppermute | solution.py:51
  56.7 6.4 %collective-permute-start.34 = (bf16[256,256]{1,0:T(8,128)(2,1)S(1)}, bf16[256,256]{1,0:T(8,128)(2,1)S(1)}, u32[]{:S(2)}, u32[]{:S(2)}) collective-permute-start(bf16[256,256]{1,0:T(8,128)(2,1)S(1)} %multiply_convert_fusion.refs_1_), channel_id=1, source_target_pairs={{0,2},{1,5},{4,0},{5,9},{8,4},{9,13},{12,8},{13,15},{14,12},{15,11... | collective-permute-start | bytes 393224 | tf_op jit(solution)/shard_map/ppermute | solution.py:51
  58.6 6.4 %collective-permute-start.30 = (bf16[256,256]{1,0:T(8,128)(2,1)S(1)}, bf16[256,256]{1,0:T(8,128)(2,1)S(1)}, u32[]{:S(2)}, u32[]{:S(2)}) collective-permute-start(bf16[256,256]{1,0:T(8,128)(2,1)S(1)} %fusion.1.refs_0_), channel_id=1, source_target_pairs={{0,4},{1,3},{4,8},{5,1},{8,12},{9,5},{12,14},{13,9},{14,10},{15,13... | collective-permute-start | bytes 393224 | tf_op jit(solution)/shard_map/ppermute | solution.py:51
  59.0 8.4 %collective-permute-start.38 = (bf16[256,256]{1,0:T(8,128)(2,1)S(1)}, bf16[256,256]{1,0:T(8,128)(2,1)S(1)}, u32[]{:S(2)}, u32[]{:S(2)}) collective-permute-start(bf16[256,256]{1,0:T(8,128)(2,1)S(1)} %multiply_convert_fusion.refs_1_), channel_id=1, source_target_pairs={{0,4},{1,3},{4,8},{5,1},{8,12},{9,5},{12,14},{13,9},{14,10},{15,13... | collective-permute-start | bytes 393224 | tf_op jit(solution)/shard_map/ppermute | solution.py:51
  61.4 6.6 %collective-permute-start.39 = (bf16[256,256]{1,0:T(8,128)(2,1)S(1)}, bf16[256,256]{1,0:T(8,128)(2,1)S(1)}, u32[]{:S(2)}, u32[]{:S(2)}) collective-permute-start(bf16[256,256]{1,0:T(8,128)(2,1)S(1)} %fusion.1.refs_0_), channel_id=1, source_target_pairs={{0,2},{1,5},{4,0},{5,9},{8,4},{9,13},{12,8},{13,15},{14,12},{15,11... | collective-permute-start | bytes 393224 | tf_op jit(solution)/shard_map/ppermute | solution.py:51
  63.1 6.2 %collective-permute-start.35 = (bf16[256,256]{1,0:T(8,128)(2,1)S(1)}, bf16[256,256]{1,0:T(8,128)(2,1)S(1)}, u32[]{:S(2)}, u32[]{:S(2)}) collective-permute-start(bf16[256,256]{1,0:T(8,128)(2,1)S(1)} %collective-permute-done.34.refs_5_), channel_id=1, source_target_pairs={{0,2},{1,5},{4,0},{5,9},{8,4},{9,13},{12,8},{13,15},{14,12},{15,11... | collective-permute-start | bytes 393224 | tf_op jit(solution)/shard_map/ppermute | solution.py:51
  67.3 6.5 %collective-permute-start.40 = (bf16[256,256]{1,0:T(8,128)(2,1)S(1)}, bf16[256,256]{1,0:T(8,128)(2,1)S(1)}, u32[]{:S(2)}, u32[]{:S(2)}) collective-permute-start(bf16[256,256]{1,0:T(8,128)(2,1)S(1)} %collective-permute-done.38.refs_3_), channel_id=1, source_target_pairs={{0,4},{1,3},{4,8},{5,1},{8,12},{9,5},{12,14},{13,9},{14,10},{15,13... | collective-permute-start | bytes 393224 | tf_op jit(solution)/shard_map/ppermute | solution.py:51
  68.0 6.3 %collective-permute-start.41 = (bf16[256,256]{1,0:T(8,128)(2,1)S(1)}, bf16[256,256]{1,0:T(8,128)(2,1)S(1)}, u32[]{:S(2)}, u32[]{:S(2)}) collective-permute-start(bf16[256,256]{1,0:T(8,128)(2,1)S(1)} %collective-permute-done.39.refs_4_), channel_id=1, source_target_pairs={{0,2},{1,5},{4,0},{5,9},{8,4},{9,13},{12,8},{13,15},{14,12},{15,11... | collective-permute-start | bytes 393224 | tf_op jit(solution)/shard_map/ppermute | solution.py:51
  69.4 7.0 %collective-permute-start.36 = (bf16[256,256]{1,0:T(8,128)(2,1)S(1)}, bf16[256,256]{1,0:T(8,128)(2,1)S(1)}, u32[]{:S(2)}, u32[]{:S(2)}) collective-permute-start(bf16[256,256]{1,0:T(8,128)(2,1)S(1)} %collective-permute-done.35.refs_3_), channel_id=1, source_target_pairs={{0,2},{1,5},{4,0},{5,9},{8,4},{9,13},{12,8},{13,15},{14,12},{15,11... | collective-permute-start | bytes 393224 | tf_op jit(solution)/shard_map/ppermute | solution.py:51
  71.0 6.3 %collective-permute-start.32 = (bf16[256,256]{1,0:T(8,128)(2,1)S(1)}, bf16[256,256]{1,0:T(8,128)(2,1)S(1)}, u32[]{:S(2)}, u32[]{:S(2)}) collective-permute-start(bf16[256,256]{1,0:T(8,128)(2,1)S(1)} %collective-permute-done.31.refs_0_), channel_id=1, source_target_pairs={{0,4},{1,3},{4,8},{5,1},{8,12},{9,5},{12,14},{13,9},{14,10},{15,13... | collective-permute-start | bytes 393224 | tf_op jit(solution)/shard_map/ppermute | solution.py:51
  (16 other events, 124.5 us)

commit v14 on v13

--- a/solution.py
+++ b/solution.py
@@ -14,7 +14,7 @@
 OVER_COLS = (((1,), (1,)), ((), ()))
 RING_LIMIT = 16
 VMEM_BYTES = 24 * 1024 * 1024
-PIECES = 8
+PIECES = 4
 
 
 def passed_along(shard, axis, by):
@@ -155,7 +155,7 @@
     half_width = high.shape[0]
     for chain in range(2):
         back_own[chain * rows:(chain + 1) * rows, :] = totals[chain][:, :lat]
-        sent[chain * rows:(chain + 1) * rows, :] = totals[chain][:, lat:]
+        sent[chain * rows:(chain + 1) * rows, :] = totals[chain][:, lat:].astype(BF16)
     same[...] = block[:lat]
     pieces = [(far, block[lat:])]
     for group, outer in zip(slots, outers):
@@ -166,7 +166,7 @@
         @pl.when(start < half_width)
         def _():
             for c in range(0, wide, lat):
-                sent[pl.ds(2 * rows + start + c, lat), :] = piece[:, c:c + lat]
+                sent[pl.ds(2 * rows + start + c, lat), :] = piece[:, c:c + lat].astype(BF16)
 
         @pl.when(start >= half_width)
         def _():
@@ -188,26 +188,20 @@
         copy.wait()
 
 
-def finish_kernel(starts, turned, preact, back_own, arrived, high, grad, bias, cross, stage, grad_sems, cross_sems):
+def finish_kernel(
+    starts, turned, preact, back_own, arrived, high, grad, bias, cross, stage, cross_stage, grad_sems, cross_sems
+):
     pieces, height, lat = stage.shape
     rows = preact.shape[0]
     half_width = high.shape[0]
     copies = []
     first = starts[starts.shape[0] - 1] == 0
+    cross_stage[...] = jnp.where(first, arrived[rows:, :].astype(F32), high[...])
     for c in range(half_width // lat):
         at = pl.ds(c * lat, lat)
-
-        @pl.when(first)
-        def _():
-            source = arrived.at[pl.ds(rows + c * lat, lat), :]
-            pltpu.make_async_copy(source, cross.at[:, at], cross_sems.at[c]).start()
-
-        @pl.when(jnp.logical_not(first))
-        def _():
-            pltpu.make_async_copy(high.at[at, :], cross.at[:, at], cross_sems.at[c]).start()
-
-        copies.append(pltpu.make_async_copy(high.at[at, :], cross.at[:, at], cross_sems.at[c]))
-    value = jnp.where(preact[...] > 0, back_own[...] + arrived[:rows, :], 0.0).astype(BF16)
+        copies.append(pltpu.make_async_copy(cross_stage.at[at, :], cross.at[:, at], cross_sems.at[c]))
+        copies[-1].start()
+    value = jnp.where(preact[...] > 0, back_own[...] + arrived[:rows, :].astype(F32), 0.0).astype(BF16)
     for i in range(pieces):
         at = pl.ds(i * height, height)
         stage[i] = jnp.dot(turned[at, :], value, preferred_element_type=F32)
@@ -247,7 +241,7 @@
     starts = jnp.stack([ring_member(place + sign * offset, size) * wide for offset in offsets] + [layer])
     starts = starts.astype(jnp.int32)
 
-    urgent, later = ((0, 1), (1, -1)), ((0, -1), (1, 1))
+    urgent, later = ((0, -1), (1, 1)), ((0, 1), (1, -1))
 
     def gather_step(found, s, ready=None):
         for chain, way in urgent + later if s < reach else urgent:
@@ -293,9 +287,9 @@
         return found[:len(outs) // 2], found[len(outs) // 2:]
 
     rest = tuple(slot for slot in range(size) if slot != far)
-    instant = ({far: BF16, slot_p.get(reach - 1): BF16}, {far: BF16, slot_q.get(reach - 1): BF16})
+    instant = tuple({far: BF16, (slot_q if way == 1 else slot_p).get(reach - 1): BF16} for _, way in later)
     far_0, far_1 = spread((far,), instant, False)
-    moving = {(0, 1): hop(far_0[0], 1), (1, -1): hop(far_1[0], -1)}
+    moving = {loop: hop(message, loop[1]) for loop, message in zip(urgent, (far_0[0], far_1[0]))}
     partial, both_t = [], []
     for pieces in spread(rest, instant, True):
         partial.append(dict(zip(rest, pieces)))
@@ -350,7 +344,7 @@
         [
             shape((lat, wide), F32),
             shape((rows, lat), F32),
-            shape((rows + half_width, lat), F32),
+            shape((rows + half_width, lat), BF16),
             shape((half_width, lat), F32),
         ],
         4 * unit,
@@ -374,6 +368,7 @@
         out_spaces=[pl.ANY, pltpu.VMEM, pl.ANY],
         scratch=[
             pltpu.VMEM((PIECES, height, lat), F32),
+            pltpu.VMEM((half_width, lat), F32),
             pltpu.SemaphoreType.DMA((PIECES,)),
             pltpu.SemaphoreType.DMA((half_width // lat,)),
         ],

time: 90.4 us -> 89.4 us (0.989)
  starting transfers between devices: 48.6 us -> 47.4 us
    ppermute x42, starting transfers between devices: 44.7 us -> 43.5 us  [hop(): return lax.ppermute(shard, ('latent', 'layer'), pairs)]
  transfers between devices with their start and end apart: 45 -> 45, of which waited for: 25 -> 28; matrix products, arithmetic and copies ran while one was open for 2% -> 2% of each run, Pallas kernels for 10% -> 10%
where the time goes in v14:
time: 89.4 us; the launch traced here: 89.1 us
  starting transfers between devices  47.4 us (53%)
  waiting for transfers between devices  24 us (27%)
  Pallas kernels  14 us (16%)
  other arithmetic  1.63 us (2%)
  local copies, waits for them, and re-layouts  1.15 us (1%)
  between operations  0.96 us (1%)
    ppermute x42, starting transfers between devices, hop(): return lax.ppermute(shard, ('latent', 'layer'), pairs)  43.5 us
    ppermute x42, waiting for transfers between devices, hop(): return lax.ppermute(shard, ('latent', 'layer'), pairs)  22.3 us
    pallas_call x12, Pallas kernels, call(): pl.pallas_call(kernel, out_shape=outs, in_specs=[spec(pltpu.SMEM)] + [spe...  14 us
    ppermute x3, starting transfers between devices, passed_along(): return lax.ppermute(shard, axis, pairs)  3.89 us
  transfers between devices with their start and end apart: 45, of which 28 were waited for; matrix products, arithmetic and copies ran while one was open for 2% of the time, Pallas kernels for 10%

profile of v14, /device:TPU:0, one launch (start us, length us, event | category | flops | bytes accessed | tf_op | source)
XLA Modules:
  0.0 89.1 jit_solution(13898331750062703650)
XLA Ops:
  1.7 3.1 %collective-permute-start.5 = (bf16[256,256]{1,0:T(8,128)(2,1)S(1)}, bf16[256,256]{1,0:T(8,128)(2,1)S(1)}, u32[]{:S(2)}, u32[]{:S(2)}) collective-permute-start(bf16[256,256]{1,0:T(8,128)(2,1)S(1)} %get-tuple-element.48.shard.refs_1_), channel_id=1, source_target_pairs={{0,4},{1,3},{4,8},{5,1},{8,12},{9,5},{12,14},{13,9},{14,10},{15,13... | collective-permute-start | bytes 393224 | tf_op jit(solution)/shard_map/ppermute | solution.py:51
  5.5 2.1 %collective-permute-start = (bf16[256,256]{1,0:T(8,128)(2,1)S(1)}, bf16[256,256]{1,0:T(8,128)(2,1)S(1)}, u32[]{:S(2)}, u32[]{:S(2)}) collective-permute-start(bf16[256,256]{1,0:T(8,128)(2,1)S(1)} %get-tuple-element.47.shard.refs_0_), channel_id=1, source_target_pairs={{0,4},{1,3},{4,8},{5,1},{8,12},{9,5},{12,14},{13,9},{14,10},{15,13... | collective-permute-start | bytes 393224 | tf_op jit(solution)/shard_map/ppermute | solution.py:51
  8.5 1.8 %collective-permute-start.6 = (bf16[256,256]{1,0:T(8,128)(2,1)S(1)}, bf16[256,256]{1,0:T(8,128)(2,1)S(1)}, u32[]{:S(2)}, u32[]{:S(2)}) collective-permute-start(bf16[256,256]{1,0:T(8,128)(2,1)S(1)} %collective-permute-done.5.refs_3_.refs_1_), channel_id=1, source_target_pairs={{0,4},{1,3},{4,8},{5,1},{8,12},{9,5},{12,14},{13,9},{14,10},{15,13... | collective-permute-start | bytes 393224 | tf_op jit(solution)/shard_map/ppermute | solution.py:51
  11.5 1.3 %collective-permute-start.14 = (bf16[128,1024]{1,0:T(8,128)(2,1)}, bf16[128,1024]{1,0:T(8,128)(2,1)S(1)}, u32[]{:S(2)}, u32[]{:S(2)}) collective-permute-start(bf16[128,1024]{1,0:T(8,128)(2,1)} %param.11), channel_id=1, source_target_pairs={{0,1},{2,3},{4,5},{6,7},{8,9},{10,11},{12,13},{14,15},{16,17},{18,... | collective-permute-start | bytes 786440 | tf_op jit(solution)/shard_map/ppermute | solution.py:23
  12.8 2.5 %collective-permute-start.10 = (bf16[256,256]{1,0:T(8,128)(2,1)S(1)}, bf16[256,256]{1,0:T(8,128)(2,1)S(1)}, u32[]{:S(2)}, u32[]{:S(2)}) collective-permute-start(bf16[256,256]{1,0:T(8,128)(2,1)S(1)} %collective-permute-done.refs_2_.refs_0_), channel_id=1, source_target_pairs={{0,4},{1,3},{4,8},{5,1},{8,12},{9,5},{12,14},{13,9},{14,10},{15,13... | collective-permute-start | bytes 393224 | tf_op jit(solution)/shard_map/ppermute | solution.py:51
  15.3 2.0 %collective-permute-start.7 = (bf16[256,256]{1,0:T(8,128)(2,1)S(1)}, bf16[256,256]{1,0:T(8,128)(2,1)S(1)}, u32[]{:S(2)}, u32[]{:S(2)}) collective-permute-start(bf16[256,256]{1,0:T(8,128)(2,1)S(1)} %collective-permute-done.6.refs_7_.refs_5_), channel_id=1, source_target_pairs={{0,4},{1,3},{4,8},{5,1},{8,12},{9,5},{12,14},{13,9},{14,10},{15,13... | collective-permute-start | bytes 393224 | tf_op jit(solution)/shard_map/ppermute | solution.py:51
  17.4 1.5 %collective-permute-done.10.refs_6_.refs_4_ = bf16[256,256]{1,0:T(8,128)(2,1)S(1)} collective-permute-done((bf16[256,256]{1,0:T(8,128)(2,1)S(1)}, bf16[256,256]{1,0:T(8,128)(2,1)S(1)}, u32[]{:S(2)}, u32[]{:S(2)}) %collective-permute-start.10) | collective-permute-done | bytes 131104 | tf_op jit(solution)/shard_map/ppermute | solution.py:51
  18.9 1.4 %collective-permute-start.12 = (bf16[256,256]{1,0:T(8,128)(2,1)S(1)}, bf16[256,256]{1,0:T(8,128)(2,1)S(1)}, u32[]{:S(2)}, u32[]{:S(2)}) collective-permute-start(bf16[256,256]{1,0:T(8,128)(2,1)S(1)} %collective-permute-done.10.refs_6_.refs_4_), channel_id=1, source_target_pairs={{0,4},{1,3},{4,8},{5,1},{8,12},{9,5},{12,14},{13,9},{14,10},{15,13... | collective-permute-start | bytes 393224 | tf_op jit(solution)/shard_map/ppermute | solution.py:51
  21.8 1.8 %collective-permute-start.8 = (bf16[256,256]{1,0:T(8,128)(2,1)S(1)}, bf16[256,256]{1,0:T(8,128)(2,1)S(1)}, u32[]{:S(2)}, u32[]{:S(2)}) collective-permute-start(bf16[256,256]{1,0:T(8,128)(2,1)S(1)} %collective-permute-done.7.refs_11_.refs_9_), channel_id=1, source_target_pairs={{0,4},{1,3},{4,8},{5,1},{8,12},{9,5},{12,14},{13,9},{14,10},{15,13... | collective-permute-start | bytes 393224 | tf_op jit(solution)/shard_map/ppermute | solution.py:51
  27.5 1.6 %collective-permute-done.4.refs_0_.refs_12_ = bf16[256,256]{1,0:T(8,128)(2,1)S(1)} collective-permute-done((bf16[256,256]{1,0:T(8,128)(2,1)S(1)}, bf16[256,256]{1,0:T(8,128)(2,1)S(1)}, u32[]{:S(2)}, u32[]{:S(2)}) %collective-permute-start.4) | collective-permute-done | bytes 131104 | tf_op jit(solution)/shard_map/ppermute | solution.py:51
  29.9 1.3 %collective-permute-start.15 = (bf16[512,128]{1,0:T(8,128)(2,1)S(1)}, bf16[512,128]{1,0:T(8,128)(2,1)S(1)}, u32[]{:S(2)}, u32[]{:S(2)}) collective-permute-start(bf16[512,128]{1,0:T(8,128)(2,1)S(1)} %get-tuple-element.51.codes), channel_id=1, source_target_pairs={{0,1},{2,3},{4,5},{6,7},{8,9},{10,11},{12,13},{14,15},{16,17},{18,... | collective-permute-start | bytes 393224 | tf_op jit(solution)/shard_map/ppermute | solution.py:23
  33.0 2.1 %collective-permute-start.16 = (bf16[256,256]{1,0:T(8,128)(2,1)S(1)}, bf16[256,256]{1,0:T(8,128)(2,1)S(1)}, u32[]{:S(2)}, u32[]{:S(2)}) collective-permute-start(bf16[256,256]{1,0:T(8,128)(2,1)S(1)} %get-tuple-element.56), channel_id=1, source_target_pairs={{0,4},{1,3},{4,8},{5,1},{8,12},{9,5},{12,14},{13,9},{14,10},{15,13... | collective-permute-start | bytes 393224 | tf_op jit(solution)/shard_map/ppermute | solution.py:51
  36.4 2.0 %collective-permute-start.25 = (bf16[256,256]{1,0:T(8,128)(2,1)S(1)}, bf16[256,256]{1,0:T(8,128)(2,1)S(1)}, u32[]{:S(2)}, u32[]{:S(2)}) collective-permute-start(bf16[256,256]{1,0:T(8,128)(2,1)S(1)} %get-tuple-element.70), channel_id=1, source_target_pairs={{0,4},{1,3},{4,8},{5,1},{8,12},{9,5},{12,14},{13,9},{14,10},{15,13... | collective-permute-start | bytes 393224 | tf_op jit(solution)/shard_map/ppermute | solution.py:51
  39.1 2.1 %collective-permute-start.17 = (bf16[256,256]{1,0:T(8,128)(2,1)S(1)}, bf16[256,256]{1,0:T(8,128)(2,1)S(1)}, u32[]{:S(2)}, u32[]{:S(2)}) collective-permute-start(bf16[256,256]{1,0:T(8,128)(2,1)S(1)} %add_convert_fusion.9), channel_id=1, source_target_pairs={{0,4},{1,3},{4,8},{5,1},{8,12},{9,5},{12,14},{13,9},{14,10},{15,13... | collective-permute-start | bytes 393224 | tf_op jit(solution)/shard_map/ppermute | solution.py:51
  41.1 1.6 %collective-permute-done.20 = bf16[256,256]{1,0:T(8,128)(2,1)S(1)} collective-permute-done((bf16[256,256]{1,0:T(8,128)(2,1)S(1)}, bf16[256,256]{1,0:T(8,128)(2,1)S(1)}, u32[]{:S(2)}, u32[]{:S(2)}) %collective-permute-start.20) | collective-permute-done | bytes 131104 | tf_op jit(solution)/shard_map/ppermute | solution.py:51
  42.8 2.1 %collective-permute-start.26 = (bf16[256,256]{1,0:T(8,128)(2,1)S(1)}, bf16[256,256]{1,0:T(8,128)(2,1)S(1)}, u32[]{:S(2)}, u32[]{:S(2)}) collective-permute-start(bf16[256,256]{1,0:T(8,128)(2,1)S(1)} %add_convert_fusion.3), channel_id=1, source_target_pairs={{0,4},{1,3},{4,8},{5,1},{8,12},{9,5},{12,14},{13,9},{14,10},{15,13... | collective-permute-start | bytes 393224 | tf_op jit(solution)/shard_map/ppermute | solution.py:51
  45.7 2.1 %collective-permute-start.18 = (bf16[256,256]{1,0:T(8,128)(2,1)S(1)}, bf16[256,256]{1,0:T(8,128)(2,1)S(1)}, u32[]{:S(2)}, u32[]{:S(2)}) collective-permute-start(bf16[256,256]{1,0:T(8,128)(2,1)S(1)} %add_convert_fusion.8), channel_id=1, source_target_pairs={{0,4},{1,3},{4,8},{5,1},{8,12},{9,5},{12,14},{13,9},{14,10},{15,13... | collective-permute-start | bytes 393224 | tf_op jit(solution)/shard_map/ppermute | solution.py:51
  49.1 1.4 %collective-permute-start.27 = (bf16[256,256]{1,0:T(8,128)(2,1)S(1)}, bf16[256,256]{1,0:T(8,128)(2,1)S(1)}, u32[]{:S(2)}, u32[]{:S(2)}) collective-permute-start(bf16[256,256]{1,0:T(8,128)(2,1)S(1)} %add_convert_fusion.2), channel_id=1, source_target_pairs={{0,4},{1,3},{4,8},{5,1},{8,12},{9,5},{12,14},{13,9},{14,10},{15,13... | collective-permute-start | bytes 393224 | tf_op jit(solution)/shard_map/ppermute | solution.py:51
  51.6 1.3 %collective-permute-start.19 = (bf16[256,256]{1,0:T(8,128)(2,1)S(1)}, bf16[256,256]{1,0:T(8,128)(2,1)S(1)}, u32[]{:S(2)}, u32[]{:S(2)}) collective-permute-start(bf16[256,256]{1,0:T(8,128)(2,1)S(1)} %add_convert_fusion.7), channel_id=1, source_target_pairs={{0,4},{1,3},{4,8},{5,1},{8,12},{9,5},{12,14},{13,9},{14,10},{15,13... | collective-permute-start | bytes 393224 | tf_op jit(solution)/shard_map/ppermute | solution.py:51
  54.5 2.4 %collective-permute-done.19 = bf16[256,256]{1,0:T(8,128)(2,1)S(1)} collective-permute-done((bf16[256,256]{1,0:T(8,128)(2,1)S(1)}, bf16[256,256]{1,0:T(8,128)(2,1)S(1)}, u32[]{:S(2)}, u32[]{:S(2)}) %collective-permute-start.19) | collective-permute-done | bytes 131104 | tf_op jit(solution)/shard_map/ppermute | solution.py:51
  57.0 1.4 %collective-permute-start.34 = (bf16[256,256]{1,0:T(8,128)(2,1)S(1)}, bf16[256,256]{1,0:T(8,128)(2,1)S(1)}, u32[]{:S(2)}, u32[]{:S(2)}) collective-permute-start(bf16[256,256]{1,0:T(8,128)(2,1)S(1)} %multiply_convert_fusion.refs_1_), channel_id=1, source_target_pairs={{0,4},{1,3},{4,8},{5,1},{8,12},{9,5},{12,14},{13,9},{14,10},{15,13... | collective-permute-start | bytes 393224 | tf_op jit(solution)/shard_map/ppermute | solution.py:51
  61.3 1.9 %collective-permute-done.34.refs_3_ = bf16[256,256]{1,0:T(8,128)(2,1)S(1)} collective-permute-done((bf16[256,256]{1,0:T(8,128)(2,1)S(1)}, bf16[256,256]{1,0:T(8,128)(2,1)S(1)}, u32[]{:S(2)}, u32[]{:S(2)}) %collective-permute-start.34) | collective-permute-done | bytes 131104 | tf_op jit(solution)/shard_map/ppermute | solution.py:51
  63.1 1.4 %collective-permute-start.35 = (bf16[256,256]{1,0:T(8,128)(2,1)S(1)}, bf16[256,256]{1,0:T(8,128)(2,1)S(1)}, u32[]{:S(2)}, u32[]{:S(2)}) collective-permute-start(bf16[256,256]{1,0:T(8,128)(2,1)S(1)} %collective-permute-done.34.refs_3_), channel_id=1, source_target_pairs={{0,4},{1,3},{4,8},{5,1},{8,12},{9,5},{12,14},{13,9},{14,10},{15,13... | collective-permute-start | bytes 393224 | tf_op jit(solution)/shard_map/ppermute | solution.py:51
  67.5 1.4 %collective-permute-start.40 = (bf16[256,256]{1,0:T(8,128)(2,1)S(1)}, bf16[256,256]{1,0:T(8,128)(2,1)S(1)}, u32[]{:S(2)}, u32[]{:S(2)}) collective-permute-start(bf16[256,256]{1,0:T(8,128)(2,1)S(1)} %collective-permute-done.38.refs_2_), channel_id=1, source_target_pairs={{0,4},{1,3},{4,8},{5,1},{8,12},{9,5},{12,14},{13,9},{14,10},{15,13... | collective-permute-start | bytes 393224 | tf_op jit(solution)/shard_map/ppermute | solution.py:51
  68.9 1.5 %collective-permute-start.36 = (bf16[256,256]{1,0:T(8,128)(2,1)S(1)}, bf16[256,256]{1,0:T(8,128)(2,1)S(1)}, u32[]{:S(2)}, u32[]{:S(2)}) collective-permute-start(bf16[256,256]{1,0:T(8,128)(2,1)S(1)} %collective-permute-done.35.refs_1_), channel_id=1, source_target_pairs={{0,4},{1,3},{4,8},{5,1},{8,12},{9,5},{12,14},{13,9},{14,10},{15,13... | collective-permute-start | bytes 393224 | tf_op jit(solution)/shard_map/ppermute | solution.py:51
  71.3 2.0 %collective-permute-done.41.refs_3_ = bf16[256,256]{1,0:T(8,128)(2,1)S(1)} collective-permute-done((bf16[256,256]{1,0:T(8,128)(2,1)S(1)}, bf16[256,256]{1,0:T(8,128)(2,1)S(1)}, u32[]{:S(2)}, u32[]{:S(2)}) %collective-permute-start.41) | collective-permute-done | bytes 131104 | tf_op jit(solution)/shard_map/ppermute | solution.py:51
  73.6 1.7 %collective-permute-start.42 = (bf16[256,256]{1,0:T(8,128)(2,1)S(1)}, bf16[256,256]{1,0:T(8,128)(2,1)S(1)}, u32[]{:S(2)}, u32[]{:S(2)}) collective-permute-start(bf16[256,256]{1,0:T(8,128)(2,1)S(1)} %collective-permute-done.40.refs_0_), channel_id=1, source_target_pairs={{0,4},{1,3},{4,8},{5,1},{8,12},{9,5},{12,14},{13,9},{14,10},{15,13... | collective-permute-start | bytes 393224 | tf_op jit(solution)/shard_map/ppermute | solution.py:51
  75.3 1.4 %collective-permute-start.37 = (bf16[256,256]{1,0:T(8,128)(2,1)S(1)}, bf16[256,256]{1,0:T(8,128)(2,1)S(1)}, u32[]{:S(2)}, u32[]{:S(2)}) collective-permute-start(bf16[256,256]{1,0:T(8,128)(2,1)S(1)} %collective-permute-done.36.refs_5_), channel_id=1, source_target_pairs={{0,4},{1,3},{4,8},{5,1},{8,12},{9,5},{12,14},{13,9},{14,10},{15,13... | collective-permute-start | bytes 393224 | tf_op jit(solution)/shard_map/ppermute | solution.py:51
  80.3 1.4 %collective-permute-done.33.refs_0_ = bf16[256,256]{1,0:T(8,128)(2,1)S(1)} collective-permute-done((bf16[256,256]{1,0:T(8,128)(2,1)S(1)}, bf16[256,256]{1,0:T(8,128)(2,1)S(1)}, u32[]{:S(2)}, u32[]{:S(2)}) %collective-permute-start.33) | collective-permute-done | bytes 131104 | tf_op jit(solution)/shard_map/ppermute | solution.py:51
  82.7 1.3 %collective-permute-start.44 = (bf16[1536,128]{1,0:T(8,128)(2,1)S(1)}, bf16[1536,128]{1,0:T(8,128)(2,1)S(1)}, u32[]{:S(2)}, u32[]{:S(2)}) collective-permute-start(bf16[1536,128]{1,0:T(8,128)(2,1)S(1)} %get-tuple-element.84), channel_id=1, source_target_pairs={{1,0},{3,2},{5,4},{7,6},{9,8},{11,10},{13,12},{15,14},{17,16},{19,... | collective-permute-start | bytes 1179656 | tf_op jit(solution)/shard_map/ppermute | solution.py:23
  84.0 1.6 %shard_map.104 = f32[1,128,2048]{2,1,0:T(8,128)} custom-call(s32[9]{0:T(128)S(1)} %stack.39.starts, f32[128,256]{1,0:T(8,128)S(1)} %get-tuple-element.88.refs_0_, f32[3,256,256]{2,1,0:T(8,128)S(1)} %get-tuple-element.77.refs_5_.refs_1_, f32[4,256,256]{2,1,0:T(8,128)S(1)} %get-tuple-element.81.refs_6_.refs_2_), custom_call_target="tpu_custom_call" | custom-call | bytes 1024 | tf_op jit(solution)/shard_map/pallas_call | solution.py:64
  86.3 2.8 %shard_map.103 = (f32[1,2048,128]{2,1,0:T(8,128)}, f32[1,128]{1,0:T(1,128)}, f32[128,1024]{1,0:T(8,128)}) custom-call(s32[9]{0:T(128)S(1)} %stack.39.starts, bf16[2048,512]{1,0:T(8,128)(2,1)S(1)} %shard_map.99.turned, f32[512,128]{1,0:T(8,128)S(1)} %get-tuple-element.66.preact, f32[512,128]{1,0:T(8,128)S(1)} %get-tuple-element.83.back_own, ...), custom_call_target="tpu_custom_call" | custom-call | flops 268435456 | bytes 1024 | tf_op jit(solution)/shard_map/pallas_call | solution.py:64
  (92 shorter events, 31.1 us)
Async XLA Ops:
  1.7 6.8 %collective-permute-start.5 = (bf16[256,256]{1,0:T(8,128)(2,1)S(1)}, bf16[256,256]{1,0:T(8,128)(2,1)S(1)}, u32[]{:S(2)}, u32[]{:S(2)}) collective-permute-start(bf16[256,256]{1,0:T(8,128)(2,1)S(1)} %get-tuple-element.48.shard.refs_1_), channel_id=1, source_target_pairs={{0,4},{1,3},{4,8},{5,1},{8,12},{9,5},{12,14},{13,9},{14,10},{15,13... | collective-permute-start | bytes 393224 | tf_op jit(solution)/shard_map/ppermute | solution.py:51
  4.8 6.3 %collective-permute-start.1 = (bf16[256,256]{1,0:T(8,128)(2,1)S(1)}, bf16[256,256]{1,0:T(8,128)(2,1)S(1)}, u32[]{:S(2)}, u32[]{:S(2)}) collective-permute-start(bf16[256,256]{1,0:T(8,128)(2,1)S(1)} %get-tuple-element.47.shard.refs_0_), channel_id=1, source_target_pairs={{0,2},{1,5},{4,0},{5,9},{8,4},{9,13},{12,8},{13,15},{14,12},{15,11... | collective-permute-start | bytes 393224 | tf_op jit(solution)/shard_map/ppermute | solution.py:51
  5.5 6.0 %collective-permute-start = (bf16[256,256]{1,0:T(8,128)(2,1)S(1)}, bf16[256,256]{1,0:T(8,128)(2,1)S(1)}, u32[]{:S(2)}, u32[]{:S(2)}) collective-permute-start(bf16[256,256]{1,0:T(8,128)(2,1)S(1)} %get-tuple-element.47.shard.refs_0_), channel_id=1, source_target_pairs={{0,4},{1,3},{4,8},{5,1},{8,12},{9,5},{12,14},{13,9},{14,10},{15,13... | collective-permute-start | bytes 393224 | tf_op jit(solution)/shard_map/ppermute | solution.py:51
  8.2 7.1 %collective-permute-start.9 = (bf16[256,256]{1,0:T(8,128)(2,1)S(1)}, bf16[256,256]{1,0:T(8,128)(2,1)S(1)}, u32[]{:S(2)}, u32[]{:S(2)}) collective-permute-start(bf16[256,256]{1,0:T(8,128)(2,1)S(1)} %get-tuple-element.48.shard.refs_1_), channel_id=1, source_target_pairs={{0,2},{1,5},{4,0},{5,9},{8,4},{9,13},{12,8},{13,15},{14,12},{15,11... | collective-permute-start | bytes 393224 | tf_op jit(solution)/shard_map/ppermute | solution.py:51
  8.5 6.8 %collective-permute-start.6 = (bf16[256,256]{1,0:T(8,128)(2,1)S(1)}, bf16[256,256]{1,0:T(8,128)(2,1)S(1)}, u32[]{:S(2)}, u32[]{:S(2)}) collective-permute-start(bf16[256,256]{1,0:T(8,128)(2,1)S(1)} %collective-permute-done.5.refs_3_.refs_1_), channel_id=1, source_target_pairs={{0,4},{1,3},{4,8},{5,1},{8,12},{9,5},{12,14},{13,9},{14,10},{15,13... | collective-permute-start | bytes 393224 | tf_op jit(solution)/shard_map/ppermute | solution.py:51
  11.1 6.3 %collective-permute-start.2 = (bf16[256,256]{1,0:T(8,128)(2,1)S(1)}, bf16[256,256]{1,0:T(8,128)(2,1)S(1)}, u32[]{:S(2)}, u32[]{:S(2)}) collective-permute-start(bf16[256,256]{1,0:T(8,128)(2,1)S(1)} %collective-permute-done.1.refs_4_.refs_2_), channel_id=1, source_target_pairs={{0,2},{1,5},{4,0},{5,9},{8,4},{9,13},{12,8},{13,15},{14,12},{15,11... | collective-permute-start | bytes 393224 | tf_op jit(solution)/shard_map/ppermute | solution.py:51
  11.5 12.7 %collective-permute-start.14 = (bf16[128,1024]{1,0:T(8,128)(2,1)}, bf16[128,1024]{1,0:T(8,128)(2,1)S(1)}, u32[]{:S(2)}, u32[]{:S(2)}) collective-permute-start(bf16[128,1024]{1,0:T(8,128)(2,1)} %param.11), channel_id=1, source_target_pairs={{0,1},{2,3},{4,5},{6,7},{8,9},{10,11},{12,13},{14,15},{16,17},{18,... | collective-permute-start | bytes 786440 | tf_op jit(solution)/shard_map/ppermute | solution.py:23
  12.8 6.2 %collective-permute-start.10 = (bf16[256,256]{1,0:T(8,128)(2,1)S(1)}, bf16[256,256]{1,0:T(8,128)(2,1)S(1)}, u32[]{:S(2)}, u32[]{:S(2)}) collective-permute-start(bf16[256,256]{1,0:T(8,128)(2,1)S(1)} %collective-permute-done.refs_2_.refs_0_), channel_id=1, source_target_pairs={{0,4},{1,3},{4,8},{5,1},{8,12},{9,5},{12,14},{13,9},{14,10},{15,13... | collective-permute-start | bytes 393224 | tf_op jit(solution)/shard_map/ppermute | solution.py:51
  15.3 6.0 %collective-permute-start.11 = (bf16[256,256]{1,0:T(8,128)(2,1)S(1)}, bf16[256,256]{1,0:T(8,128)(2,1)S(1)}, u32[]{:S(2)}, u32[]{:S(2)}) collective-permute-start(bf16[256,256]{1,0:T(8,128)(2,1)S(1)} %collective-permute-done.9.refs_5_.refs_3_), channel_id=1, source_target_pairs={{0,2},{1,5},{4,0},{5,9},{8,4},{9,13},{12,8},{13,15},{14,12},{15,11... | collective-permute-start | bytes 393224 | tf_op jit(solution)/shard_map/ppermute | solution.py:51
  15.3 6.5 %collective-permute-start.7 = (bf16[256,256]{1,0:T(8,128)(2,1)S(1)}, bf16[256,256]{1,0:T(8,128)(2,1)S(1)}, u32[]{:S(2)}, u32[]{:S(2)}) collective-permute-start(bf16[256,256]{1,0:T(8,128)(2,1)S(1)} %collective-permute-done.6.refs_7_.refs_5_), channel_id=1, source_target_pairs={{0,4},{1,3},{4,8},{5,1},{8,12},{9,5},{12,14},{13,9},{14,10},{15,13... | collective-permute-start | bytes 393224 | tf_op jit(solution)/shard_map/ppermute | solution.py:51
  17.4 6.7 %collective-permute-start.3 = (bf16[256,256]{1,0:T(8,128)(2,1)S(1)}, bf16[256,256]{1,0:T(8,128)(2,1)S(1)}, u32[]{:S(2)}, u32[]{:S(2)}) collective-permute-start(bf16[256,256]{1,0:T(8,128)(2,1)S(1)} %collective-permute-done.2.refs_8_.refs_6_), channel_id=1, source_target_pairs={{0,2},{1,5},{4,0},{5,9},{8,4},{9,13},{12,8},{13,15},{14,12},{15,11... | collective-permute-start | bytes 393224 | tf_op jit(solution)/shard_map/ppermute | solution.py:51
  18.9 6.4 %collective-permute-start.12 = (bf16[256,256]{1,0:T(8,128)(2,1)S(1)}, bf16[256,256]{1,0:T(8,128)(2,1)S(1)}, u32[]{:S(2)}, u32[]{:S(2)}) collective-permute-start(bf16[256,256]{1,0:T(8,128)(2,1)S(1)} %collective-permute-done.10.refs_6_.refs_4_), channel_id=1, source_target_pairs={{0,4},{1,3},{4,8},{5,1},{8,12},{9,5},{12,14},{13,9},{14,10},{15,13... | collective-permute-start | bytes 393224 | tf_op jit(solution)/shard_map/ppermute | solution.py:51
  32.9 6.0 %collective-permute-start.21 = (bf16[256,256]{1,0:T(8,128)(2,1)S(1)}, bf16[256,256]{1,0:T(8,128)(2,1)S(1)}, u32[]{:S(2)}, u32[]{:S(2)}) collective-permute-start(bf16[256,256]{1,0:T(8,128)(2,1)S(1)} %get-tuple-element.60), channel_id=1, source_target_pairs={{0,2},{1,5},{4,0},{5,9},{8,4},{9,13},{12,8},{13,15},{14,12},{15,11... | collective-permute-start | bytes 393224 | tf_op jit(solution)/shard_map/ppermute | solution.py:51
  33.0 6.0 %collective-permute-start.16 = (bf16[256,256]{1,0:T(8,128)(2,1)S(1)}, bf16[256,256]{1,0:T(8,128)(2,1)S(1)}, u32[]{:S(2)}, u32[]{:S(2)}) collective-permute-start(bf16[256,256]{1,0:T(8,128)(2,1)S(1)} %get-tuple-element.56), channel_id=1, source_target_pairs={{0,4},{1,3},{4,8},{5,1},{8,12},{9,5},{12,14},{13,9},{14,10},{15,13... | collective-permute-start | bytes 393224 | tf_op jit(solution)/shard_map/ppermute | solution.py:51
  36.3 6.4 %collective-permute-start.20 = (bf16[256,256]{1,0:T(8,128)(2,1)S(1)}, bf16[256,256]{1,0:T(8,128)(2,1)S(1)}, u32[]{:S(2)}, u32[]{:S(2)}) collective-permute-start(bf16[256,256]{1,0:T(8,128)(2,1)S(1)} %get-tuple-element.59), channel_id=1, source_target_pairs={{0,2},{1,5},{4,0},{5,9},{8,4},{9,13},{12,8},{13,15},{14,12},{15,11... | collective-permute-start | bytes 393224 | tf_op jit(solution)/shard_map/ppermute | solution.py:51
  36.4 6.4 %collective-permute-start.25 = (bf16[256,256]{1,0:T(8,128)(2,1)S(1)}, bf16[256,256]{1,0:T(8,128)(2,1)S(1)}, u32[]{:S(2)}, u32[]{:S(2)}) collective-permute-start(bf16[256,256]{1,0:T(8,128)(2,1)S(1)} %get-tuple-element.70), channel_id=1, source_target_pairs={{0,4},{1,3},{4,8},{5,1},{8,12},{9,5},{12,14},{13,9},{14,10},{15,13... | collective-permute-start | bytes 393224 | tf_op jit(solution)/shard_map/ppermute | solution.py:51
  39.0 6.5 %collective-permute-start.23 = (bf16[256,256]{1,0:T(8,128)(2,1)S(1)}, bf16[256,256]{1,0:T(8,128)(2,1)S(1)}, u32[]{:S(2)}, u32[]{:S(2)}) collective-permute-start(bf16[256,256]{1,0:T(8,128)(2,1)S(1)} %add_convert_fusion.4), channel_id=1, source_target_pairs={{0,2},{1,5},{4,0},{5,9},{8,4},{9,13},{12,8},{13,15},{14,12},{15,11... | collective-permute-start | bytes 393224 | tf_op jit(solution)/shard_map/ppermute | solution.py:51
  39.1 6.5 %collective-permute-start.17 = (bf16[256,256]{1,0:T(8,128)(2,1)S(1)}, bf16[256,256]{1,0:T(8,128)(2,1)S(1)}, u32[]{:S(2)}, u32[]{:S(2)}) collective-permute-start(bf16[256,256]{1,0:T(8,128)(2,1)S(1)} %add_convert_fusion.9), channel_id=1, source_target_pairs={{0,4},{1,3},{4,8},{5,1},{8,12},{9,5},{12,14},{13,9},{14,10},{15,13... | collective-permute-start | bytes 393224 | tf_op jit(solution)/shard_map/ppermute | solution.py:51
  42.8 6.2 %collective-permute-start.26 = (bf16[256,256]{1,0:T(8,128)(2,1)S(1)}, bf16[256,256]{1,0:T(8,128)(2,1)S(1)}, u32[]{:S(2)}, u32[]{:S(2)}) collective-permute-start(bf16[256,256]{1,0:T(8,128)(2,1)S(1)} %add_convert_fusion.3), channel_id=1, source_target_pairs={{0,4},{1,3},{4,8},{5,1},{8,12},{9,5},{12,14},{13,9},{14,10},{15,13... | collective-permute-start | bytes 393224 | tf_op jit(solution)/shard_map/ppermute | solution.py:51
  45.5 7.3 %collective-permute-start.28 = (bf16[256,256]{1,0:T(8,128)(2,1)S(1)}, bf16[256,256]{1,0:T(8,128)(2,1)S(1)}, u32[]{:S(2)}, u32[]{:S(2)}) collective-permute-start(bf16[256,256]{1,0:T(8,128)(2,1)S(1)} %add_convert_fusion.1), channel_id=1, source_target_pairs={{0,2},{1,5},{4,0},{5,9},{8,4},{9,13},{12,8},{13,15},{14,12},{15,11... | collective-permute-start | bytes 393224 | tf_op jit(solution)/shard_map/ppermute | solution.py:51
  45.7 5.9 %collective-permute-start.18 = (bf16[256,256]{1,0:T(8,128)(2,1)S(1)}, bf16[256,256]{1,0:T(8,128)(2,1)S(1)}, u32[]{:S(2)}, u32[]{:S(2)}) collective-permute-start(bf16[256,256]{1,0:T(8,128)(2,1)S(1)} %add_convert_fusion.8), channel_id=1, source_target_pairs={{0,4},{1,3},{4,8},{5,1},{8,12},{9,5},{12,14},{13,9},{14,10},{15,13... | collective-permute-start | bytes 393224 | tf_op jit(solution)/shard_map/ppermute | solution.py:51
  48.3 6.2 %collective-permute-start.24 = (bf16[256,256]{1,0:T(8,128)(2,1)S(1)}, bf16[256,256]{1,0:T(8,128)(2,1)S(1)}, u32[]{:S(2)}, u32[]{:S(2)}) collective-permute-start(bf16[256,256]{1,0:T(8,128)(2,1)S(1)} %add_convert_fusion.5), channel_id=1, source_target_pairs={{0,2},{1,5},{4,0},{5,9},{8,4},{9,13},{12,8},{13,15},{14,12},{15,11... | collective-permute-start | bytes 393224 | tf_op jit(solution)/shard_map/ppermute | solution.py:51
  49.1 9.3 %collective-permute-start.27 = (bf16[256,256]{1,0:T(8,128)(2,1)S(1)}, bf16[256,256]{1,0:T(8,128)(2,1)S(1)}, u32[]{:S(2)}, u32[]{:S(2)}) collective-permute-start(bf16[256,256]{1,0:T(8,128)(2,1)S(1)} %add_convert_fusion.2), channel_id=1, source_target_pairs={{0,4},{1,3},{4,8},{5,1},{8,12},{9,5},{12,14},{13,9},{14,10},{15,13... | collective-permute-start | bytes 393224 | tf_op jit(solution)/shard_map/ppermute | solution.py:51
  57.0 6.2 %collective-permute-start.34 = (bf16[256,256]{1,0:T(8,128)(2,1)S(1)}, bf16[256,256]{1,0:T(8,128)(2,1)S(1)}, u32[]{:S(2)}, u32[]{:S(2)}) collective-permute-start(bf16[256,256]{1,0:T(8,128)(2,1)S(1)} %multiply_convert_fusion.refs_1_), channel_id=1, source_target_pairs={{0,4},{1,3},{4,8},{5,1},{8,12},{9,5},{12,14},{13,9},{14,10},{15,13... | collective-permute-start | bytes 393224 | tf_op jit(solution)/shard_map/ppermute | solution.py:51
  58.5 6.4 %collective-permute-start.30 = (bf16[256,256]{1,0:T(8,128)(2,1)S(1)}, bf16[256,256]{1,0:T(8,128)(2,1)S(1)}, u32[]{:S(2)}, u32[]{:S(2)}) collective-permute-start(bf16[256,256]{1,0:T(8,128)(2,1)S(1)} %fusion.1.refs_0_), channel_id=1, source_target_pairs={{0,2},{1,5},{4,0},{5,9},{8,4},{9,13},{12,8},{13,15},{14,12},{15,11... | collective-permute-start | bytes 393224 | tf_op jit(solution)/shard_map/ppermute | solution.py:51
  59.2 7.7 %collective-permute-start.39 = (bf16[256,256]{1,0:T(8,128)(2,1)S(1)}, bf16[256,256]{1,0:T(8,128)(2,1)S(1)}, u32[]{:S(2)}, u32[]{:S(2)}) collective-permute-start(bf16[256,256]{1,0:T(8,128)(2,1)S(1)} %multiply_convert_fusion.refs_1_), channel_id=1, source_target_pairs={{0,2},{1,5},{4,0},{5,9},{8,4},{9,13},{12,8},{13,15},{14,12},{15,11... | collective-permute-start | bytes 393224 | tf_op jit(solution)/shard_map/ppermute | solution.py:51
  60.3 7.2 %collective-permute-start.38 = (bf16[256,256]{1,0:T(8,128)(2,1)S(1)}, bf16[256,256]{1,0:T(8,128)(2,1)S(1)}, u32[]{:S(2)}, u32[]{:S(2)}) collective-permute-start(bf16[256,256]{1,0:T(8,128)(2,1)S(1)} %fusion.1.refs_0_), channel_id=1, source_target_pairs={{0,4},{1,3},{4,8},{5,1},{8,12},{9,5},{12,14},{13,9},{14,10},{15,13... | collective-permute-start | bytes 393224 | tf_op jit(solution)/shard_map/ppermute | solution.py:51
  64.9 5.9 %collective-permute-start.31 = (bf16[256,256]{1,0:T(8,128)(2,1)S(1)}, bf16[256,256]{1,0:T(8,128)(2,1)S(1)}, u32[]{:S(2)}, u32[]{:S(2)}) collective-permute-start(bf16[256,256]{1,0:T(8,128)(2,1)S(1)} %collective-permute-done.30.refs_4_), channel_id=1, source_target_pairs={{0,2},{1,5},{4,0},{5,9},{8,4},{9,13},{12,8},{13,15},{14,12},{15,11... | collective-permute-start | bytes 393224 | tf_op jit(solution)/shard_map/ppermute | solution.py:51
  66.9 6.4 %collective-permute-start.41 = (bf16[256,256]{1,0:T(8,128)(2,1)S(1)}, bf16[256,256]{1,0:T(8,128)(2,1)S(1)}, u32[]{:S(2)}, u32[]{:S(2)}) collective-permute-start(bf16[256,256]{1,0:T(8,128)(2,1)S(1)} %collective-permute-done.39.refs_5_), channel_id=1, source_target_pairs={{0,2},{1,5},{4,0},{5,9},{8,4},{9,13},{12,8},{13,15},{14,12},{15,11... | collective-permute-start | bytes 393224 | tf_op jit(solution)/shard_map/ppermute | solution.py:51
  67.5 6.1 %collective-permute-start.40 = (bf16[256,256]{1,0:T(8,128)(2,1)S(1)}, bf16[256,256]{1,0:T(8,128)(2,1)S(1)}, u32[]{:S(2)}, u32[]{:S(2)}) collective-permute-start(bf16[256,256]{1,0:T(8,128)(2,1)S(1)} %collective-permute-done.38.refs_2_), channel_id=1, source_target_pairs={{0,4},{1,3},{4,8},{5,1},{8,12},{9,5},{12,14},{13,9},{14,10},{15,13... | collective-permute-start | bytes 393224 | tf_op jit(solution)/shard_map/ppermute | solution.py:51
  68.9 6.4 %collective-permute-start.36 = (bf16[256,256]{1,0:T(8,128)(2,1)S(1)}, bf16[256,256]{1,0:T(8,128)(2,1)S(1)}, u32[]{:S(2)}, u32[]{:S(2)}) collective-permute-start(bf16[256,256]{1,0:T(8,128)(2,1)S(1)} %collective-permute-done.35.refs_1_), channel_id=1, source_target_pairs={{0,4},{1,3},{4,8},{5,1},{8,12},{9,5},{12,14},{13,9},{14,10},{15,13... | collective-permute-start | bytes 393224 | tf_op jit(solution)/shard_map/ppermute | solution.py:51
  70.8 5.9 %collective-permute-start.32 = (bf16[256,256]{1,0:T(8,128)(2,1)S(1)}, bf16[256,256]{1,0:T(8,128)(2,1)S(1)}, u32[]{:S(2)}, u32[]{:S(2)}) collective-permute-start(bf16[256,256]{1,0:T(8,128)(2,1)S(1)} %collective-permute-done.31.refs_2_), channel_id=1, source_target_pairs={{0,2},{1,5},{4,0},{5,9},{8,4},{9,13},{12,8},{13,15},{14,12},{15,11... | collective-permute-start | bytes 393224 | tf_op jit(solution)/shard_map/ppermute | solution.py:51
  (16 other events, 122.7 us)

commit v15 on v14

--- a/solution.py
+++ b/solution.py
@@ -14,7 +14,7 @@
 OVER_COLS = (((1,), (1,)), ((), ()))
 RING_LIMIT = 16
 VMEM_BYTES = 24 * 1024 * 1024
-PIECES = 4
+PIECES = 8
 
 
 def passed_along(shard, axis, by):
@@ -146,44 +146,60 @@
         back[chain] = totals[chain]
 
 
-def last_back_kernel(slots, far, starts, *refs):
-    near_refs, (before, same, back_own, sent, high) = refs[:-5], refs[-5:]
-    shards, (stacked, *both_t), outers = near_refs[:2], near_refs[2:5], near_refs[5:]
-    (block,), totals = back_products((far,), starts, shards, stacked, both_t, before)
+def cross_back_kernel(slots, far, starts, *refs):
+    shards, (stacked, *both_t), outers, (before, sent, high) = refs[:2], refs[2:5], refs[5:-3], refs[-3:]
     rows, wide = shards[0].shape
-    lat = high.shape[1]
-    half_width = high.shape[0]
-    for chain in range(2):
-        back_own[chain * rows:(chain + 1) * rows, :] = totals[chain][:, :lat]
-        sent[chain * rows:(chain + 1) * rows, :] = totals[chain][:, lat:].astype(BF16)
-    same[...] = block[:lat]
-    pieces = [(far, block[lat:])]
-    for group, outer in zip(slots, outers):
-        pieces += [(slot, outer[i, lat:]) for i, slot in enumerate(group)]
-    for slot, piece in pieces:
-        start = pl.multiple_of(starts[slot], wide)
-
-        @pl.when(start < half_width)
-        def _():
-            for c in range(0, wide, lat):
-                sent[pl.ds(2 * rows + start + c, lat), :] = piece[:, c:c + lat].astype(BF16)
-
-        @pl.when(start >= half_width)
-        def _():
-            for c in range(0, wide, lat):
-                high[pl.ds(start - half_width + c, lat), :] = piece[:, c:c + lat]
-
-
-def place_kernel(slots, far, starts, *refs):
-    last, *outers, same, sems = refs
-    lat, wide = last.shape
-    blocks = [(far, last)]
+    half_width, lat = high.shape
+
+    @pl.when(starts[starts.shape[0] - 1] != 0)
+    def _():
+        decoder = stacked[lat:, block_of(starts, far, wide)]
+        last = 0.0
+        for chain in range(2):
+            error = shards[chain][...]
+            last = last + jnp.dot(both_t[chain][lat:, :], error, preferred_element_type=F32)
+            term = lax.dot_general(error, decoder, OVER_COLS, preferred_element_type=F32)
+            sent[chain * rows:(chain + 1) * rows, :] = (before[chain, :, lat:] + term).astype(BF16)
+        pieces = [(far, last)]
+        for group, outer in zip(slots, outers):
+            pieces += [(slot, outer[i, lat:]) for i, slot in enumerate(group)]
+        for slot, piece in pieces:
+            start = pl.multiple_of(starts[slot], wide)
+
+            @pl.when(start < half_width)
+            def _():
+                for c in range(0, wide, lat):
+                    sent[pl.ds(2 * rows + start + c, lat), :] = piece[:, c:c + lat].astype(BF16)
+
+            @pl.when(start >= half_width)
+            def _():
+                for c in range(0, wide, lat):
+                    high[pl.ds(start - half_width + c, lat), :] = piece[:, c:c + lat]
+
+
+def own_back_kernel(slots, far, starts, *refs):
+    shards, (stacked, *both_t), refs = refs[:2], refs[2:5], refs[5:]
+    outers, (before, back_own, same, last, sems) = refs[:-5], refs[-5:]
+    rows, wide = shards[0].shape
+    lat = back_own.shape[1]
+    blocks = []
     for group, outer in zip(slots, outers):
         blocks += [(slot, outer.at[i, :lat, :]) for i, slot in enumerate(group)]
+    blocks.append((far, last))
     copies = []
     for i, (slot, block) in enumerate(blocks):
         copies.append(pltpu.make_async_copy(block, same.at[0, :, block_of(starts, slot, wide)], sems.at[i]))
-        copies[-1].start()
+    for copy in copies[:-1]:
+        copy.start()
+    decoder = stacked[:lat, block_of(starts, far, wide)]
+    total = 0.0
+    for chain in range(2):
+        error = shards[chain][...]
+        total = total + jnp.dot(both_t[chain][:lat, :], error, preferred_element_type=F32)
+        term = lax.dot_general(error, decoder, OVER_COLS, preferred_element_type=F32)
+        back_own[chain * rows:(chain + 1) * rows, :] = before[chain, :, :lat] + term
+    last[...] = total
+    copies[-1].start()
     for copy in copies:
         copy.wait()
 
@@ -196,7 +212,15 @@
     half_width = high.shape[0]
     copies = []
     first = starts[starts.shape[0] - 1] == 0
-    cross_stage[...] = jnp.where(first, arrived[rows:, :].astype(F32), high[...])
+
+    @pl.when(first)
+    def _():
+        cross_stage[...] = arrived[rows:, :].astype(F32)
+
+    @pl.when(jnp.logical_not(first))
+    def _():
+        cross_stage[...] = high[...]
+
     for c in range(half_width // lat):
         at = pl.ds(c * lat, lat)
         copies.append(pltpu.make_async_copy(cross_stage.at[at, :], cross.at[:, at], cross_sems.at[c]))
@@ -339,26 +363,22 @@
     for group in groups:
         outer, acc = back(group, acc)
         outers.append(outer)
-    last_same, back_own, sent, high = call(
-        functools.partial(last_back_kernel, groups, far),
-        [
-            shape((lat, wide), F32),
-            shape((rows, lat), F32),
-            shape((rows + half_width, lat), BF16),
-            shape((half_width, lat), F32),
-        ],
-        4 * unit,
-        [starts] + both_chains(errors, (far,)) + [stacked] + both_t + outers + [acc],
+    last = both_chains(errors, (far,)) + [stacked] + both_t + outers + [acc]
+    sent, high = call(
+        functools.partial(cross_back_kernel, groups, far),
+        [shape((rows + half_width, lat), BF16), shape((half_width, lat), F32)],
+        0,
+        [starts] + last,
     )
     returned = passed_along(sent, "layer", -1)
-    grad_same = call(
-        functools.partial(place_kernel, groups, far),
-        [shape((1, lat, deep), F32)],
+    back_own, grad_same = call(
+        functools.partial(own_back_kernel, groups, far),
+        [shape((rows, lat), F32), shape((1, lat, deep), F32)],
         0,
-        [starts, last_same] + outers,
-        out_spaces=[pl.ANY],
-        scratch=[pltpu.SemaphoreType.DMA((size,))],
-    )[0]
+        [starts] + last,
+        out_spaces=[pltpu.VMEM, pl.ANY],
+        scratch=[pltpu.VMEM((lat, wide), F32), pltpu.SemaphoreType.DMA((size,))],
+    )
     height = deep // PIECES
     grad_enc, grad_bias, grad_cross = call(
         finish_kernel,

time: 89.4 us -> 88.9 us (level)
  no operation moved by 1% of the time
where the time goes in v15:
time: 88.9 us; the launch traced here: 88.6 us
  starting transfers between devices  47.4 us (53%)
  waiting for transfers between devices  23.9 us (27%)
  Pallas kernels  13.5 us (15%)
  other arithmetic  1.63 us (2%)
  local copies, waits for them, and re-layouts  1.15 us (1%)
  between operations  0.96 us (1%)
    ppermute x42, starting transfers between devices, hop(): return lax.ppermute(shard, ('latent', 'layer'), pairs)  43.5 us
    ppermute x42, waiting for transfers between devices, hop(): return lax.ppermute(shard, ('latent', 'layer'), pairs)  22.3 us
    pallas_call x12, Pallas kernels, call(): pl.pallas_call(kernel, out_shape=outs, in_specs=[spec(pltpu.SMEM)] + [spe...  13.5 us
    ppermute x3, starting transfers between devices, passed_along(): return lax.ppermute(shard, axis, pairs)  3.89 us
  transfers between devices with their start and end apart: 45, of which 28 were waited for; matrix products, arithmetic and copies ran while one was open for 2% of the time, Pallas kernels for 10%

profile of v15, /device:TPU:0, one launch (start us, length us, event | category | flops | bytes accessed | tf_op | source)
XLA Modules:
  0.0 88.6 jit_solution(13074525942166901007)
XLA Ops:
  1.7 3.1 %collective-permute-start.5 = (bf16[256,256]{1,0:T(8,128)(2,1)S(1)}, bf16[256,256]{1,0:T(8,128)(2,1)S(1)}, u32[]{:S(2)}, u32[]{:S(2)}) collective-permute-start(bf16[256,256]{1,0:T(8,128)(2,1)S(1)} %get-tuple-element.48.shard.refs_1_), channel_id=1, source_target_pairs={{0,4},{1,3},{4,8},{5,1},{8,12},{9,5},{12,14},{13,9},{14,10},{15,13... | collective-permute-start | bytes 393224 | tf_op jit(solution)/shard_map/ppermute | solution.py:51
  5.5 2.1 %collective-permute-start = (bf16[256,256]{1,0:T(8,128)(2,1)S(1)}, bf16[256,256]{1,0:T(8,128)(2,1)S(1)}, u32[]{:S(2)}, u32[]{:S(2)}) collective-permute-start(bf16[256,256]{1,0:T(8,128)(2,1)S(1)} %get-tuple-element.47.shard.refs_0_), channel_id=1, source_target_pairs={{0,4},{1,3},{4,8},{5,1},{8,12},{9,5},{12,14},{13,9},{14,10},{15,13... | collective-permute-start | bytes 393224 | tf_op jit(solution)/shard_map/ppermute | solution.py:51
  8.5 1.8 %collective-permute-start.6 = (bf16[256,256]{1,0:T(8,128)(2,1)S(1)}, bf16[256,256]{1,0:T(8,128)(2,1)S(1)}, u32[]{:S(2)}, u32[]{:S(2)}) collective-permute-start(bf16[256,256]{1,0:T(8,128)(2,1)S(1)} %collective-permute-done.5.refs_3_.refs_1_), channel_id=1, source_target_pairs={{0,4},{1,3},{4,8},{5,1},{8,12},{9,5},{12,14},{13,9},{14,10},{15,13... | collective-permute-start | bytes 393224 | tf_op jit(solution)/shard_map/ppermute | solution.py:51
  11.5 1.3 %collective-permute-start.14 = (bf16[128,1024]{1,0:T(8,128)(2,1)}, bf16[128,1024]{1,0:T(8,128)(2,1)S(1)}, u32[]{:S(2)}, u32[]{:S(2)}) collective-permute-start(bf16[128,1024]{1,0:T(8,128)(2,1)} %param.11), channel_id=1, source_target_pairs={{0,1},{2,3},{4,5},{6,7},{8,9},{10,11},{12,13},{14,15},{16,17},{18,... | collective-permute-start | bytes 786440 | tf_op jit(solution)/shard_map/ppermute | solution.py:23
  12.8 2.5 %collective-permute-start.10 = (bf16[256,256]{1,0:T(8,128)(2,1)S(1)}, bf16[256,256]{1,0:T(8,128)(2,1)S(1)}, u32[]{:S(2)}, u32[]{:S(2)}) collective-permute-start(bf16[256,256]{1,0:T(8,128)(2,1)S(1)} %collective-permute-done.refs_2_.refs_0_), channel_id=1, source_target_pairs={{0,4},{1,3},{4,8},{5,1},{8,12},{9,5},{12,14},{13,9},{14,10},{15,13... | collective-permute-start | bytes 393224 | tf_op jit(solution)/shard_map/ppermute | solution.py:51
  15.3 2.0 %collective-permute-start.7 = (bf16[256,256]{1,0:T(8,128)(2,1)S(1)}, bf16[256,256]{1,0:T(8,128)(2,1)S(1)}, u32[]{:S(2)}, u32[]{:S(2)}) collective-permute-start(bf16[256,256]{1,0:T(8,128)(2,1)S(1)} %collective-permute-done.6.refs_7_.refs_5_), channel_id=1, source_target_pairs={{0,4},{1,3},{4,8},{5,1},{8,12},{9,5},{12,14},{13,9},{14,10},{15,13... | collective-permute-start | bytes 393224 | tf_op jit(solution)/shard_map/ppermute | solution.py:51
  17.4 1.5 %collective-permute-done.10.refs_6_.refs_4_ = bf16[256,256]{1,0:T(8,128)(2,1)S(1)} collective-permute-done((bf16[256,256]{1,0:T(8,128)(2,1)S(1)}, bf16[256,256]{1,0:T(8,128)(2,1)S(1)}, u32[]{:S(2)}, u32[]{:S(2)}) %collective-permute-start.10) | collective-permute-done | bytes 131104 | tf_op jit(solution)/shard_map/ppermute | solution.py:51
  18.9 1.4 %collective-permute-start.12 = (bf16[256,256]{1,0:T(8,128)(2,1)S(1)}, bf16[256,256]{1,0:T(8,128)(2,1)S(1)}, u32[]{:S(2)}, u32[]{:S(2)}) collective-permute-start(bf16[256,256]{1,0:T(8,128)(2,1)S(1)} %collective-permute-done.10.refs_6_.refs_4_), channel_id=1, source_target_pairs={{0,4},{1,3},{4,8},{5,1},{8,12},{9,5},{12,14},{13,9},{14,10},{15,13... | collective-permute-start | bytes 393224 | tf_op jit(solution)/shard_map/ppermute | solution.py:51
  21.8 1.8 %collective-permute-start.8 = (bf16[256,256]{1,0:T(8,128)(2,1)S(1)}, bf16[256,256]{1,0:T(8,128)(2,1)S(1)}, u32[]{:S(2)}, u32[]{:S(2)}) collective-permute-start(bf16[256,256]{1,0:T(8,128)(2,1)S(1)} %collective-permute-done.7.refs_11_.refs_9_), channel_id=1, source_target_pairs={{0,4},{1,3},{4,8},{5,1},{8,12},{9,5},{12,14},{13,9},{14,10},{15,13... | collective-permute-start | bytes 393224 | tf_op jit(solution)/shard_map/ppermute | solution.py:51
  27.5 1.6 %collective-permute-done.4.refs_0_.refs_12_ = bf16[256,256]{1,0:T(8,128)(2,1)S(1)} collective-permute-done((bf16[256,256]{1,0:T(8,128)(2,1)S(1)}, bf16[256,256]{1,0:T(8,128)(2,1)S(1)}, u32[]{:S(2)}, u32[]{:S(2)}) %collective-permute-start.4) | collective-permute-done | bytes 131104 | tf_op jit(solution)/shard_map/ppermute | solution.py:51
  29.9 1.3 %collective-permute-start.15 = (bf16[512,128]{1,0:T(8,128)(2,1)S(1)}, bf16[512,128]{1,0:T(8,128)(2,1)S(1)}, u32[]{:S(2)}, u32[]{:S(2)}) collective-permute-start(bf16[512,128]{1,0:T(8,128)(2,1)S(1)} %get-tuple-element.51.codes), channel_id=1, source_target_pairs={{0,1},{2,3},{4,5},{6,7},{8,9},{10,11},{12,13},{14,15},{16,17},{18,... | collective-permute-start | bytes 393224 | tf_op jit(solution)/shard_map/ppermute | solution.py:23
  33.0 2.1 %collective-permute-start.16 = (bf16[256,256]{1,0:T(8,128)(2,1)S(1)}, bf16[256,256]{1,0:T(8,128)(2,1)S(1)}, u32[]{:S(2)}, u32[]{:S(2)}) collective-permute-start(bf16[256,256]{1,0:T(8,128)(2,1)S(1)} %get-tuple-element.56), channel_id=1, source_target_pairs={{0,4},{1,3},{4,8},{5,1},{8,12},{9,5},{12,14},{13,9},{14,10},{15,13... | collective-permute-start | bytes 393224 | tf_op jit(solution)/shard_map/ppermute | solution.py:51
  36.4 2.0 %collective-permute-start.25 = (bf16[256,256]{1,0:T(8,128)(2,1)S(1)}, bf16[256,256]{1,0:T(8,128)(2,1)S(1)}, u32[]{:S(2)}, u32[]{:S(2)}) collective-permute-start(bf16[256,256]{1,0:T(8,128)(2,1)S(1)} %get-tuple-element.70), channel_id=1, source_target_pairs={{0,4},{1,3},{4,8},{5,1},{8,12},{9,5},{12,14},{13,9},{14,10},{15,13... | collective-permute-start | bytes 393224 | tf_op jit(solution)/shard_map/ppermute | solution.py:51
  39.1 2.1 %collective-permute-start.17 = (bf16[256,256]{1,0:T(8,128)(2,1)S(1)}, bf16[256,256]{1,0:T(8,128)(2,1)S(1)}, u32[]{:S(2)}, u32[]{:S(2)}) collective-permute-start(bf16[256,256]{1,0:T(8,128)(2,1)S(1)} %add_convert_fusion.9), channel_id=1, source_target_pairs={{0,4},{1,3},{4,8},{5,1},{8,12},{9,5},{12,14},{13,9},{14,10},{15,13... | collective-permute-start | bytes 393224 | tf_op jit(solution)/shard_map/ppermute | solution.py:51
  41.1 1.6 %collective-permute-done.20 = bf16[256,256]{1,0:T(8,128)(2,1)S(1)} collective-permute-done((bf16[256,256]{1,0:T(8,128)(2,1)S(1)}, bf16[256,256]{1,0:T(8,128)(2,1)S(1)}, u32[]{:S(2)}, u32[]{:S(2)}) %collective-permute-start.20) | collective-permute-done | bytes 131104 | tf_op jit(solution)/shard_map/ppermute | solution.py:51
  42.8 2.1 %collective-permute-start.26 = (bf16[256,256]{1,0:T(8,128)(2,1)S(1)}, bf16[256,256]{1,0:T(8,128)(2,1)S(1)}, u32[]{:S(2)}, u32[]{:S(2)}) collective-permute-start(bf16[256,256]{1,0:T(8,128)(2,1)S(1)} %add_convert_fusion.3), channel_id=1, source_target_pairs={{0,4},{1,3},{4,8},{5,1},{8,12},{9,5},{12,14},{13,9},{14,10},{15,13... | collective-permute-start | bytes 393224 | tf_op jit(solution)/shard_map/ppermute | solution.py:51
  45.7 2.1 %collective-permute-start.18 = (bf16[256,256]{1,0:T(8,128)(2,1)S(1)}, bf16[256,256]{1,0:T(8,128)(2,1)S(1)}, u32[]{:S(2)}, u32[]{:S(2)}) collective-permute-start(bf16[256,256]{1,0:T(8,128)(2,1)S(1)} %add_convert_fusion.8), channel_id=1, source_target_pairs={{0,4},{1,3},{4,8},{5,1},{8,12},{9,5},{12,14},{13,9},{14,10},{15,13... | collective-permute-start | bytes 393224 | tf_op jit(solution)/shard_map/ppermute | solution.py:51
  49.1 1.4 %collective-permute-start.27 = (bf16[256,256]{1,0:T(8,128)(2,1)S(1)}, bf16[256,256]{1,0:T(8,128)(2,1)S(1)}, u32[]{:S(2)}, u32[]{:S(2)}) collective-permute-start(bf16[256,256]{1,0:T(8,128)(2,1)S(1)} %add_convert_fusion.2), channel_id=1, source_target_pairs={{0,4},{1,3},{4,8},{5,1},{8,12},{9,5},{12,14},{13,9},{14,10},{15,13... | collective-permute-start | bytes 393224 | tf_op jit(solution)/shard_map/ppermute | solution.py:51
  51.6 1.3 %collective-permute-start.19 = (bf16[256,256]{1,0:T(8,128)(2,1)S(1)}, bf16[256,256]{1,0:T(8,128)(2,1)S(1)}, u32[]{:S(2)}, u32[]{:S(2)}) collective-permute-start(bf16[256,256]{1,0:T(8,128)(2,1)S(1)} %add_convert_fusion.7), channel_id=1, source_target_pairs={{0,4},{1,3},{4,8},{5,1},{8,12},{9,5},{12,14},{13,9},{14,10},{15,13... | collective-permute-start | bytes 393224 | tf_op jit(solution)/shard_map/ppermute | solution.py:51
  54.5 2.4 %collective-permute-done.19 = bf16[256,256]{1,0:T(8,128)(2,1)S(1)} collective-permute-done((bf16[256,256]{1,0:T(8,128)(2,1)S(1)}, bf16[256,256]{1,0:T(8,128)(2,1)S(1)}, u32[]{:S(2)}, u32[]{:S(2)}) %collective-permute-start.19) | collective-permute-done | bytes 131104 | tf_op jit(solution)/shard_map/ppermute | solution.py:51
  57.0 1.4 %collective-permute-start.34 = (bf16[256,256]{1,0:T(8,128)(2,1)S(1)}, bf16[256,256]{1,0:T(8,128)(2,1)S(1)}, u32[]{:S(2)}, u32[]{:S(2)}) collective-permute-start(bf16[256,256]{1,0:T(8,128)(2,1)S(1)} %multiply_convert_fusion.refs_1_), channel_id=1, source_target_pairs={{0,4},{1,3},{4,8},{5,1},{8,12},{9,5},{12,14},{13,9},{14,10},{15,13... | collective-permute-start | bytes 393224 | tf_op jit(solution)/shard_map/ppermute | solution.py:51
  61.3 1.9 %collective-permute-done.34.refs_3_ = bf16[256,256]{1,0:T(8,128)(2,1)S(1)} collective-permute-done((bf16[256,256]{1,0:T(8,128)(2,1)S(1)}, bf16[256,256]{1,0:T(8,128)(2,1)S(1)}, u32[]{:S(2)}, u32[]{:S(2)}) %collective-permute-start.34) | collective-permute-done | bytes 131104 | tf_op jit(solution)/shard_map/ppermute | solution.py:51
  63.1 1.4 %collective-permute-start.35 = (bf16[256,256]{1,0:T(8,128)(2,1)S(1)}, bf16[256,256]{1,0:T(8,128)(2,1)S(1)}, u32[]{:S(2)}, u32[]{:S(2)}) collective-permute-start(bf16[256,256]{1,0:T(8,128)(2,1)S(1)} %collective-permute-done.34.refs_3_), channel_id=1, source_target_pairs={{0,4},{1,3},{4,8},{5,1},{8,12},{9,5},{12,14},{13,9},{14,10},{15,13... | collective-permute-start | bytes 393224 | tf_op jit(solution)/shard_map/ppermute | solution.py:51
  67.5 1.4 %collective-permute-start.40 = (bf16[256,256]{1,0:T(8,128)(2,1)S(1)}, bf16[256,256]{1,0:T(8,128)(2,1)S(1)}, u32[]{:S(2)}, u32[]{:S(2)}) collective-permute-start(bf16[256,256]{1,0:T(8,128)(2,1)S(1)} %collective-permute-done.38.refs_2_), channel_id=1, source_target_pairs={{0,4},{1,3},{4,8},{5,1},{8,12},{9,5},{12,14},{13,9},{14,10},{15,13... | collective-permute-start | bytes 393224 | tf_op jit(solution)/shard_map/ppermute | solution.py:51
  68.9 1.5 %collective-permute-start.36 = (bf16[256,256]{1,0:T(8,128)(2,1)S(1)}, bf16[256,256]{1,0:T(8,128)(2,1)S(1)}, u32[]{:S(2)}, u32[]{:S(2)}) collective-permute-start(bf16[256,256]{1,0:T(8,128)(2,1)S(1)} %collective-permute-done.35.refs_1_), channel_id=1, source_target_pairs={{0,4},{1,3},{4,8},{5,1},{8,12},{9,5},{12,14},{13,9},{14,10},{15,13... | collective-permute-start | bytes 393224 | tf_op jit(solution)/shard_map/ppermute | solution.py:51
  71.3 2.0 %collective-permute-done.41.refs_3_ = bf16[256,256]{1,0:T(8,128)(2,1)S(1)} collective-permute-done((bf16[256,256]{1,0:T(8,128)(2,1)S(1)}, bf16[256,256]{1,0:T(8,128)(2,1)S(1)}, u32[]{:S(2)}, u32[]{:S(2)}) %collective-permute-start.41) | collective-permute-done | bytes 131104 | tf_op jit(solution)/shard_map/ppermute | solution.py:51
  73.6 1.7 %collective-permute-start.42 = (bf16[256,256]{1,0:T(8,128)(2,1)S(1)}, bf16[256,256]{1,0:T(8,128)(2,1)S(1)}, u32[]{:S(2)}, u32[]{:S(2)}) collective-permute-start(bf16[256,256]{1,0:T(8,128)(2,1)S(1)} %collective-permute-done.40.refs_0_), channel_id=1, source_target_pairs={{0,4},{1,3},{4,8},{5,1},{8,12},{9,5},{12,14},{13,9},{14,10},{15,13... | collective-permute-start | bytes 393224 | tf_op jit(solution)/shard_map/ppermute | solution.py:51
  75.3 1.4 %collective-permute-start.37 = (bf16[256,256]{1,0:T(8,128)(2,1)S(1)}, bf16[256,256]{1,0:T(8,128)(2,1)S(1)}, u32[]{:S(2)}, u32[]{:S(2)}) collective-permute-start(bf16[256,256]{1,0:T(8,128)(2,1)S(1)} %collective-permute-done.36.refs_5_), channel_id=1, source_target_pairs={{0,4},{1,3},{4,8},{5,1},{8,12},{9,5},{12,14},{13,9},{14,10},{15,13... | collective-permute-start | bytes 393224 | tf_op jit(solution)/shard_map/ppermute | solution.py:51
  80.3 1.4 %collective-permute-done.33.refs_0_ = bf16[256,256]{1,0:T(8,128)(2,1)S(1)} collective-permute-done((bf16[256,256]{1,0:T(8,128)(2,1)S(1)}, bf16[256,256]{1,0:T(8,128)(2,1)S(1)}, u32[]{:S(2)}, u32[]{:S(2)}) %collective-permute-start.33) | collective-permute-done | bytes 131104 | tf_op jit(solution)/shard_map/ppermute | solution.py:51
  82.2 1.3 %collective-permute-start.44 = (bf16[1536,128]{1,0:T(8,128)(2,1)S(1)}, bf16[1536,128]{1,0:T(8,128)(2,1)S(1)}, u32[]{:S(2)}, u32[]{:S(2)}) collective-permute-start(bf16[1536,128]{1,0:T(8,128)(2,1)S(1)} %get-tuple-element.84), channel_id=1, source_target_pairs={{1,0},{3,2},{5,4},{7,6},{9,8},{11,10},{13,12},{15,14},{17,16},{19,... | collective-permute-start | bytes 1179656 | tf_op jit(solution)/shard_map/ppermute | solution.py:23
  83.5 1.6 %shard_map.102 = (f32[512,128]{1,0:T(8,128)S(1)}, f32[1,128,2048]{2,1,0:T(8,128)}) custom-call(s32[9]{0:T(128)S(1)} %stack.39.starts, bf16[256,256]{1,0:T(8,128)(2,1)S(1)} %collective-permute-done.33.refs_0_, bf16[256,256]{1,0:T(8,128)(2,1)S(1)} %collective-permute-done.37.refs_1_, bf16[256,2048]{1,0:T(8,128)(2,1)S(1)} %maximum_maximum_fusion.stacked.refs_6_.refs_8_.refs_2_, ...), custom_call_target="tpu_custom_call" | custom-call | bytes 1024 | tf_op jit(solution)/shard_map/pallas_call | solution.py:64
  85.9 2.7 %shard_map.104 = (f32[1,2048,128]{2,1,0:T(8,128)}, f32[1,128]{1,0:T(1,128)}, f32[128,1024]{1,0:T(8,128)}) custom-call(s32[9]{0:T(128)S(1)} %stack.39.starts, bf16[2048,512]{1,0:T(8,128)(2,1)S(1)} %shard_map.99.turned, f32[512,128]{1,0:T(8,128)S(1)} %get-tuple-element.66.preact, f32[512,128]{1,0:T(8,128)S(1)} %get-tuple-element.83.back_own, ...), custom_call_target="tpu_custom_call" | custom-call | flops 268435456 | bytes 1024 | tf_op jit(solution)/shard_map/pallas_call | solution.py:64
  (92 shorter events, 30.6 us)
Async XLA Ops:
  1.7 6.8 %collective-permute-start.5 = (bf16[256,256]{1,0:T(8,128)(2,1)S(1)}, bf16[256,256]{1,0:T(8,128)(2,1)S(1)}, u32[]{:S(2)}, u32[]{:S(2)}) collective-permute-start(bf16[256,256]{1,0:T(8,128)(2,1)S(1)} %get-tuple-element.48.shard.refs_1_), channel_id=1, source_target_pairs={{0,4},{1,3},{4,8},{5,1},{8,12},{9,5},{12,14},{13,9},{14,10},{15,13... | collective-permute-start | bytes 393224 | tf_op jit(solution)/shard_map/ppermute | solution.py:51
  4.8 6.3 %collective-permute-start.1 = (bf16[256,256]{1,0:T(8,128)(2,1)S(1)}, bf16[256,256]{1,0:T(8,128)(2,1)S(1)}, u32[]{:S(2)}, u32[]{:S(2)}) collective-permute-start(bf16[256,256]{1,0:T(8,128)(2,1)S(1)} %get-tuple-element.47.shard.refs_0_), channel_id=1, source_target_pairs={{0,2},{1,5},{4,0},{5,9},{8,4},{9,13},{12,8},{13,15},{14,12},{15,11... | collective-permute-start | bytes 393224 | tf_op jit(solution)/shard_map/ppermute | solution.py:51
  5.5 6.0 %collective-permute-start = (bf16[256,256]{1,0:T(8,128)(2,1)S(1)}, bf16[256,256]{1,0:T(8,128)(2,1)S(1)}, u32[]{:S(2)}, u32[]{:S(2)}) collective-permute-start(bf16[256,256]{1,0:T(8,128)(2,1)S(1)} %get-tuple-element.47.shard.refs_0_), channel_id=1, source_target_pairs={{0,4},{1,3},{4,8},{5,1},{8,12},{9,5},{12,14},{13,9},{14,10},{15,13... | collective-permute-start | bytes 393224 | tf_op jit(solution)/shard_map/ppermute | solution.py:51
  8.2 7.1 %collective-permute-start.9 = (bf16[256,256]{1,0:T(8,128)(2,1)S(1)}, bf16[256,256]{1,0:T(8,128)(2,1)S(1)}, u32[]{:S(2)}, u32[]{:S(2)}) collective-permute-start(bf16[256,256]{1,0:T(8,128)(2,1)S(1)} %get-tuple-element.48.shard.refs_1_), channel_id=1, source_target_pairs={{0,2},{1,5},{4,0},{5,9},{8,4},{9,13},{12,8},{13,15},{14,12},{15,11... | collective-permute-start | bytes 393224 | tf_op jit(solution)/shard_map/ppermute | solution.py:51
  8.5 6.8 %collective-permute-start.6 = (bf16[256,256]{1,0:T(8,128)(2,1)S(1)}, bf16[256,256]{1,0:T(8,128)(2,1)S(1)}, u32[]{:S(2)}, u32[]{:S(2)}) collective-permute-start(bf16[256,256]{1,0:T(8,128)(2,1)S(1)} %collective-permute-done.5.refs_3_.refs_1_), channel_id=1, source_target_pairs={{0,4},{1,3},{4,8},{5,1},{8,12},{9,5},{12,14},{13,9},{14,10},{15,13... | collective-permute-start | bytes 393224 | tf_op jit(solution)/shard_map/ppermute | solution.py:51
  11.1 6.3 %collective-permute-start.2 = (bf16[256,256]{1,0:T(8,128)(2,1)S(1)}, bf16[256,256]{1,0:T(8,128)(2,1)S(1)}, u32[]{:S(2)}, u32[]{:S(2)}) collective-permute-start(bf16[256,256]{1,0:T(8,128)(2,1)S(1)} %collective-permute-done.1.refs_4_.refs_2_), channel_id=1, source_target_pairs={{0,2},{1,5},{4,0},{5,9},{8,4},{9,13},{12,8},{13,15},{14,12},{15,11... | collective-permute-start | bytes 393224 | tf_op jit(solution)/shard_map/ppermute | solution.py:51
  11.5 12.7 %collective-permute-start.14 = (bf16[128,1024]{1,0:T(8,128)(2,1)}, bf16[128,1024]{1,0:T(8,128)(2,1)S(1)}, u32[]{:S(2)}, u32[]{:S(2)}) collective-permute-start(bf16[128,1024]{1,0:T(8,128)(2,1)} %param.11), channel_id=1, source_target_pairs={{0,1},{2,3},{4,5},{6,7},{8,9},{10,11},{12,13},{14,15},{16,17},{18,... | collective-permute-start | bytes 786440 | tf_op jit(solution)/shard_map/ppermute | solution.py:23
  12.8 6.2 %collective-permute-start.10 = (bf16[256,256]{1,0:T(8,128)(2,1)S(1)}, bf16[256,256]{1,0:T(8,128)(2,1)S(1)}, u32[]{:S(2)}, u32[]{:S(2)}) collective-permute-start(bf16[256,256]{1,0:T(8,128)(2,1)S(1)} %collective-permute-done.refs_2_.refs_0_), channel_id=1, source_target_pairs={{0,4},{1,3},{4,8},{5,1},{8,12},{9,5},{12,14},{13,9},{14,10},{15,13... | collective-permute-start | bytes 393224 | tf_op jit(solution)/shard_map/ppermute | solution.py:51
  15.3 6.0 %collective-permute-start.11 = (bf16[256,256]{1,0:T(8,128)(2,1)S(1)}, bf16[256,256]{1,0:T(8,128)(2,1)S(1)}, u32[]{:S(2)}, u32[]{:S(2)}) collective-permute-start(bf16[256,256]{1,0:T(8,128)(2,1)S(1)} %collective-permute-done.9.refs_5_.refs_3_), channel_id=1, source_target_pairs={{0,2},{1,5},{4,0},{5,9},{8,4},{9,13},{12,8},{13,15},{14,12},{15,11... | collective-permute-start | bytes 393224 | tf_op jit(solution)/shard_map/ppermute | solution.py:51
  15.3 6.5 %collective-permute-start.7 = (bf16[256,256]{1,0:T(8,128)(2,1)S(1)}, bf16[256,256]{1,0:T(8,128)(2,1)S(1)}, u32[]{:S(2)}, u32[]{:S(2)}) collective-permute-start(bf16[256,256]{1,0:T(8,128)(2,1)S(1)} %collective-permute-done.6.refs_7_.refs_5_), channel_id=1, source_target_pairs={{0,4},{1,3},{4,8},{5,1},{8,12},{9,5},{12,14},{13,9},{14,10},{15,13... | collective-permute-start | bytes 393224 | tf_op jit(solution)/shard_map/ppermute | solution.py:51
  17.4 6.7 %collective-permute-start.3 = (bf16[256,256]{1,0:T(8,128)(2,1)S(1)}, bf16[256,256]{1,0:T(8,128)(2,1)S(1)}, u32[]{:S(2)}, u32[]{:S(2)}) collective-permute-start(bf16[256,256]{1,0:T(8,128)(2,1)S(1)} %collective-permute-done.2.refs_8_.refs_6_), channel_id=1, source_target_pairs={{0,2},{1,5},{4,0},{5,9},{8,4},{9,13},{12,8},{13,15},{14,12},{15,11... | collective-permute-start | bytes 393224 | tf_op jit(solution)/shard_map/ppermute | solution.py:51
  18.9 6.4 %collective-permute-start.12 = (bf16[256,256]{1,0:T(8,128)(2,1)S(1)}, bf16[256,256]{1,0:T(8,128)(2,1)S(1)}, u32[]{:S(2)}, u32[]{:S(2)}) collective-permute-start(bf16[256,256]{1,0:T(8,128)(2,1)S(1)} %collective-permute-done.10.refs_6_.refs_4_), channel_id=1, source_target_pairs={{0,4},{1,3},{4,8},{5,1},{8,12},{9,5},{12,14},{13,9},{14,10},{15,13... | collective-permute-start | bytes 393224 | tf_op jit(solution)/shard_map/ppermute | solution.py:51
  32.9 6.0 %collective-permute-start.21 = (bf16[256,256]{1,0:T(8,128)(2,1)S(1)}, bf16[256,256]{1,0:T(8,128)(2,1)S(1)}, u32[]{:S(2)}, u32[]{:S(2)}) collective-permute-start(bf16[256,256]{1,0:T(8,128)(2,1)S(1)} %get-tuple-element.60), channel_id=1, source_target_pairs={{0,2},{1,5},{4,0},{5,9},{8,4},{9,13},{12,8},{13,15},{14,12},{15,11... | collective-permute-start | bytes 393224 | tf_op jit(solution)/shard_map/ppermute | solution.py:51
  33.0 6.0 %collective-permute-start.16 = (bf16[256,256]{1,0:T(8,128)(2,1)S(1)}, bf16[256,256]{1,0:T(8,128)(2,1)S(1)}, u32[]{:S(2)}, u32[]{:S(2)}) collective-permute-start(bf16[256,256]{1,0:T(8,128)(2,1)S(1)} %get-tuple-element.56), channel_id=1, source_target_pairs={{0,4},{1,3},{4,8},{5,1},{8,12},{9,5},{12,14},{13,9},{14,10},{15,13... | collective-permute-start | bytes 393224 | tf_op jit(solution)/shard_map/ppermute | solution.py:51
  36.3 6.4 %collective-permute-start.20 = (bf16[256,256]{1,0:T(8,128)(2,1)S(1)}, bf16[256,256]{1,0:T(8,128)(2,1)S(1)}, u32[]{:S(2)}, u32[]{:S(2)}) collective-permute-start(bf16[256,256]{1,0:T(8,128)(2,1)S(1)} %get-tuple-element.59), channel_id=1, source_target_pairs={{0,2},{1,5},{4,0},{5,9},{8,4},{9,13},{12,8},{13,15},{14,12},{15,11... | collective-permute-start | bytes 393224 | tf_op jit(solution)/shard_map/ppermute | solution.py:51
  36.4 6.4 %collective-permute-start.25 = (bf16[256,256]{1,0:T(8,128)(2,1)S(1)}, bf16[256,256]{1,0:T(8,128)(2,1)S(1)}, u32[]{:S(2)}, u32[]{:S(2)}) collective-permute-start(bf16[256,256]{1,0:T(8,128)(2,1)S(1)} %get-tuple-element.70), channel_id=1, source_target_pairs={{0,4},{1,3},{4,8},{5,1},{8,12},{9,5},{12,14},{13,9},{14,10},{15,13... | collective-permute-start | bytes 393224 | tf_op jit(solution)/shard_map/ppermute | solution.py:51
  39.0 6.5 %collective-permute-start.23 = (bf16[256,256]{1,0:T(8,128)(2,1)S(1)}, bf16[256,256]{1,0:T(8,128)(2,1)S(1)}, u32[]{:S(2)}, u32[]{:S(2)}) collective-permute-start(bf16[256,256]{1,0:T(8,128)(2,1)S(1)} %add_convert_fusion.4), channel_id=1, source_target_pairs={{0,2},{1,5},{4,0},{5,9},{8,4},{9,13},{12,8},{13,15},{14,12},{15,11... | collective-permute-start | bytes 393224 | tf_op jit(solution)/shard_map/ppermute | solution.py:51
  39.1 6.5 %collective-permute-start.17 = (bf16[256,256]{1,0:T(8,128)(2,1)S(1)}, bf16[256,256]{1,0:T(8,128)(2,1)S(1)}, u32[]{:S(2)}, u32[]{:S(2)}) collective-permute-start(bf16[256,256]{1,0:T(8,128)(2,1)S(1)} %add_convert_fusion.9), channel_id=1, source_target_pairs={{0,4},{1,3},{4,8},{5,1},{8,12},{9,5},{12,14},{13,9},{14,10},{15,13... | collective-permute-start | bytes 393224 | tf_op jit(solution)/shard_map/ppermute | solution.py:51
  42.8 6.2 %collective-permute-start.26 = (bf16[256,256]{1,0:T(8,128)(2,1)S(1)}, bf16[256,256]{1,0:T(8,128)(2,1)S(1)}, u32[]{:S(2)}, u32[]{:S(2)}) collective-permute-start(bf16[256,256]{1,0:T(8,128)(2,1)S(1)} %add_convert_fusion.3), channel_id=1, source_target_pairs={{0,4},{1,3},{4,8},{5,1},{8,12},{9,5},{12,14},{13,9},{14,10},{15,13... | collective-permute-start | bytes 393224 | tf_op jit(solution)/shard_map/ppermute | solution.py:51
  45.5 7.3 %collective-permute-start.28 = (bf16[256,256]{1,0:T(8,128)(2,1)S(1)}, bf16[256,256]{1,0:T(8,128)(2,1)S(1)}, u32[]{:S(2)}, u32[]{:S(2)}) collective-permute-start(bf16[256,256]{1,0:T(8,128)(2,1)S(1)} %add_convert_fusion.1), channel_id=1, source_target_pairs={{0,2},{1,5},{4,0},{5,9},{8,4},{9,13},{12,8},{13,15},{14,12},{15,11... | collective-permute-start | bytes 393224 | tf_op jit(solution)/shard_map/ppermute | solution.py:51
  45.7 5.9 %collective-permute-start.18 = (bf16[256,256]{1,0:T(8,128)(2,1)S(1)}, bf16[256,256]{1,0:T(8,128)(2,1)S(1)}, u32[]{:S(2)}, u32[]{:S(2)}) collective-permute-start(bf16[256,256]{1,0:T(8,128)(2,1)S(1)} %add_convert_fusion.8), channel_id=1, source_target_pairs={{0,4},{1,3},{4,8},{5,1},{8,12},{9,5},{12,14},{13,9},{14,10},{15,13... | collective-permute-start | bytes 393224 | tf_op jit(solution)/shard_map/ppermute | solution.py:51
  48.3 6.2 %collective-permute-start.24 = (bf16[256,256]{1,0:T(8,128)(2,1)S(1)}, bf16[256,256]{1,0:T(8,128)(2,1)S(1)}, u32[]{:S(2)}, u32[]{:S(2)}) collective-permute-start(bf16[256,256]{1,0:T(8,128)(2,1)S(1)} %add_convert_fusion.5), channel_id=1, source_target_pairs={{0,2},{1,5},{4,0},{5,9},{8,4},{9,13},{12,8},{13,15},{14,12},{15,11... | collective-permute-start | bytes 393224 | tf_op jit(solution)/shard_map/ppermute | solution.py:51
  49.1 9.3 %collective-permute-start.27 = (bf16[256,256]{1,0:T(8,128)(2,1)S(1)}, bf16[256,256]{1,0:T(8,128)(2,1)S(1)}, u32[]{:S(2)}, u32[]{:S(2)}) collective-permute-start(bf16[256,256]{1,0:T(8,128)(2,1)S(1)} %add_convert_fusion.2), channel_id=1, source_target_pairs={{0,4},{1,3},{4,8},{5,1},{8,12},{9,5},{12,14},{13,9},{14,10},{15,13... | collective-permute-start | bytes 393224 | tf_op jit(solution)/shard_map/ppermute | solution.py:51
  57.0 6.2 %collective-permute-start.34 = (bf16[256,256]{1,0:T(8,128)(2,1)S(1)}, bf16[256,256]{1,0:T(8,128)(2,1)S(1)}, u32[]{:S(2)}, u32[]{:S(2)}) collective-permute-start(bf16[256,256]{1,0:T(8,128)(2,1)S(1)} %multiply_convert_fusion.refs_1_), channel_id=1, source_target_pairs={{0,4},{1,3},{4,8},{5,1},{8,12},{9,5},{12,14},{13,9},{14,10},{15,13... | collective-permute-start | bytes 393224 | tf_op jit(solution)/shard_map/ppermute | solution.py:51
  58.5 6.4 %collective-permute-start.30 = (bf16[256,256]{1,0:T(8,128)(2,1)S(1)}, bf16[256,256]{1,0:T(8,128)(2,1)S(1)}, u32[]{:S(2)}, u32[]{:S(2)}) collective-permute-start(bf16[256,256]{1,0:T(8,128)(2,1)S(1)} %fusion.1.refs_0_), channel_id=1, source_target_pairs={{0,2},{1,5},{4,0},{5,9},{8,4},{9,13},{12,8},{13,15},{14,12},{15,11... | collective-permute-start | bytes 393224 | tf_op jit(solution)/shard_map/ppermute | solution.py:51
  59.2 7.7 %collective-permute-start.39 = (bf16[256,256]{1,0:T(8,128)(2,1)S(1)}, bf16[256,256]{1,0:T(8,128)(2,1)S(1)}, u32[]{:S(2)}, u32[]{:S(2)}) collective-permute-start(bf16[256,256]{1,0:T(8,128)(2,1)S(1)} %multiply_convert_fusion.refs_1_), channel_id=1, source_target_pairs={{0,2},{1,5},{4,0},{5,9},{8,4},{9,13},{12,8},{13,15},{14,12},{15,11... | collective-permute-start | bytes 393224 | tf_op jit(solution)/shard_map/ppermute | solution.py:51
  60.3 7.2 %collective-permute-start.38 = (bf16[256,256]{1,0:T(8,128)(2,1)S(1)}, bf16[256,256]{1,0:T(8,128)(2,1)S(1)}, u32[]{:S(2)}, u32[]{:S(2)}) collective-permute-start(bf16[256,256]{1,0:T(8,128)(2,1)S(1)} %fusion.1.refs_0_), channel_id=1, source_target_pairs={{0,4},{1,3},{4,8},{5,1},{8,12},{9,5},{12,14},{13,9},{14,10},{15,13... | collective-permute-start | bytes 393224 | tf_op jit(solution)/shard_map/ppermute | solution.py:51
  64.9 5.9 %collective-permute-start.31 = (bf16[256,256]{1,0:T(8,128)(2,1)S(1)}, bf16[256,256]{1,0:T(8,128)(2,1)S(1)}, u32[]{:S(2)}, u32[]{:S(2)}) collective-permute-start(bf16[256,256]{1,0:T(8,128)(2,1)S(1)} %collective-permute-done.30.refs_4_), channel_id=1, source_target_pairs={{0,2},{1,5},{4,0},{5,9},{8,4},{9,13},{12,8},{13,15},{14,12},{15,11... | collective-permute-start | bytes 393224 | tf_op jit(solution)/shard_map/ppermute | solution.py:51
  66.9 6.4 %collective-permute-start.41 = (bf16[256,256]{1,0:T(8,128)(2,1)S(1)}, bf16[256,256]{1,0:T(8,128)(2,1)S(1)}, u32[]{:S(2)}, u32[]{:S(2)}) collective-permute-start(bf16[256,256]{1,0:T(8,128)(2,1)S(1)} %collective-permute-done.39.refs_5_), channel_id=1, source_target_pairs={{0,2},{1,5},{4,0},{5,9},{8,4},{9,13},{12,8},{13,15},{14,12},{15,11... | collective-permute-start | bytes 393224 | tf_op jit(solution)/shard_map/ppermute | solution.py:51
  67.5 6.1 %collective-permute-start.40 = (bf16[256,256]{1,0:T(8,128)(2,1)S(1)}, bf16[256,256]{1,0:T(8,128)(2,1)S(1)}, u32[]{:S(2)}, u32[]{:S(2)}) collective-permute-start(bf16[256,256]{1,0:T(8,128)(2,1)S(1)} %collective-permute-done.38.refs_2_), channel_id=1, source_target_pairs={{0,4},{1,3},{4,8},{5,1},{8,12},{9,5},{12,14},{13,9},{14,10},{15,13... | collective-permute-start | bytes 393224 | tf_op jit(solution)/shard_map/ppermute | solution.py:51
  68.9 6.4 %collective-permute-start.36 = (bf16[256,256]{1,0:T(8,128)(2,1)S(1)}, bf16[256,256]{1,0:T(8,128)(2,1)S(1)}, u32[]{:S(2)}, u32[]{:S(2)}) collective-permute-start(bf16[256,256]{1,0:T(8,128)(2,1)S(1)} %collective-permute-done.35.refs_1_), channel_id=1, source_target_pairs={{0,4},{1,3},{4,8},{5,1},{8,12},{9,5},{12,14},{13,9},{14,10},{15,13... | collective-permute-start | bytes 393224 | tf_op jit(solution)/shard_map/ppermute | solution.py:51
  70.8 5.9 %collective-permute-start.32 = (bf16[256,256]{1,0:T(8,128)(2,1)S(1)}, bf16[256,256]{1,0:T(8,128)(2,1)S(1)}, u32[]{:S(2)}, u32[]{:S(2)}) collective-permute-start(bf16[256,256]{1,0:T(8,128)(2,1)S(1)} %collective-permute-done.31.refs_2_), channel_id=1, source_target_pairs={{0,2},{1,5},{4,0},{5,9},{8,4},{9,13},{12,8},{13,15},{14,12},{15,11... | collective-permute-start | bytes 393224 | tf_op jit(solution)/shard_map/ppermute | solution.py:51
  (16 other events, 122.7 us)

commit v16 on v15

--- a/solution.py
+++ b/solution.py
@@ -355,12 +355,12 @@
         0,
         [starts] + turned_own + arrived + both_chains(inputs, range(1, size))[1:],
     )[0]
+    groups = [group for group in ((0,), tuple(range(1, far))) if group]
+    outer, acc = back(groups[0], None)
+    outers = [outer]
     for s in range(1, reach + 1):
-        gather_step(errors, s, (turned, turned) if s == 2 else None)
-    cut = 1 + 2 * min(1, reach - 1)
-    groups = [group for group in (tuple(range(cut)), tuple(range(cut, far))) if group]
-    outers, acc = [], None
-    for group in groups:
+        gather_step(errors, s, (turned, acc) if s == 1 else None)
+    for group in groups[1:]:
         outer, acc = back(group, acc)
         outers.append(outer)
     last = both_chains(errors, (far,)) + [stacked] + both_t + outers + [acc]

time: 88.9 us -> 89.3 us (level)
  transfers between devices with their start and end apart: 45 -> 45, of which waited for: 28 -> 30; matrix products, arithmetic and copies ran while one was open for 2% -> 2% of each run, Pallas kernels for 10% -> 10%
where the time goes in v16:
time: 89.3 us; the launch traced here: 89.1 us
  starting transfers between devices  47.2 us (53%)
  waiting for transfers between devices  24.7 us (28%)
  Pallas kernels  13.5 us (15%)
  other arithmetic  1.63 us (2%)
  local copies, waits for them, and re-layouts  1.15 us (1%)
  between operations  0.96 us (1%)
    ppermute x42, starting transfers between devices, hop(): return lax.ppermute(shard, ('latent', 'layer'), pairs)  43.3 us
    ppermute x42, waiting for transfers between devices, hop(): return lax.ppermute(shard, ('latent', 'layer'), pairs)  23 us
    pallas_call x12, Pallas kernels, call(): pl.pallas_call(kernel, out_shape=outs, in_specs=[spec(pltpu.SMEM)] + [spe...  13.5 us
    ppermute x3, starting transfers between devices, passed_along(): return lax.ppermute(shard, axis, pairs)  3.89 us
  transfers between devices with their start and end apart: 45, of which 30 were waited for; matrix products, arithmetic and copies ran while one was open for 2% of the time, Pallas kernels for 10%

profile of v16, /device:TPU:0, one launch (start us, length us, event | category | flops | bytes accessed | tf_op | source)
XLA Modules:
  0.0 89.1 jit_solution(7720230376261333499)
XLA Ops:
  1.7 3.1 %collective-permute-start.5 = (bf16[256,256]{1,0:T(8,128)(2,1)S(1)}, bf16[256,256]{1,0:T(8,128)(2,1)S(1)}, u32[]{:S(2)}, u32[]{:S(2)}) collective-permute-start(bf16[256,256]{1,0:T(8,128)(2,1)S(1)} %get-tuple-element.48.shard.refs_1_), channel_id=1, source_target_pairs={{0,4},{1,3},{4,8},{5,1},{8,12},{9,5},{12,14},{13,9},{14,10},{15,13... | collective-permute-start | bytes 393224 | tf_op jit(solution)/shard_map/ppermute | solution.py:51
  5.5 2.1 %collective-permute-start = (bf16[256,256]{1,0:T(8,128)(2,1)S(1)}, bf16[256,256]{1,0:T(8,128)(2,1)S(1)}, u32[]{:S(2)}, u32[]{:S(2)}) collective-permute-start(bf16[256,256]{1,0:T(8,128)(2,1)S(1)} %get-tuple-element.47.shard.refs_0_), channel_id=1, source_target_pairs={{0,4},{1,3},{4,8},{5,1},{8,12},{9,5},{12,14},{13,9},{14,10},{15,13... | collective-permute-start | bytes 393224 | tf_op jit(solution)/shard_map/ppermute | solution.py:51
  8.5 1.8 %collective-permute-start.6 = (bf16[256,256]{1,0:T(8,128)(2,1)S(1)}, bf16[256,256]{1,0:T(8,128)(2,1)S(1)}, u32[]{:S(2)}, u32[]{:S(2)}) collective-permute-start(bf16[256,256]{1,0:T(8,128)(2,1)S(1)} %collective-permute-done.5.refs_3_.refs_1_), channel_id=1, source_target_pairs={{0,4},{1,3},{4,8},{5,1},{8,12},{9,5},{12,14},{13,9},{14,10},{15,13... | collective-permute-start | bytes 393224 | tf_op jit(solution)/shard_map/ppermute | solution.py:51
  11.5 1.3 %collective-permute-start.14 = (bf16[128,1024]{1,0:T(8,128)(2,1)}, bf16[128,1024]{1,0:T(8,128)(2,1)S(1)}, u32[]{:S(2)}, u32[]{:S(2)}) collective-permute-start(bf16[128,1024]{1,0:T(8,128)(2,1)} %param.11), channel_id=1, source_target_pairs={{0,1},{2,3},{4,5},{6,7},{8,9},{10,11},{12,13},{14,15},{16,17},{18,... | collective-permute-start | bytes 786440 | tf_op jit(solution)/shard_map/ppermute | solution.py:23
  12.8 2.5 %collective-permute-start.10 = (bf16[256,256]{1,0:T(8,128)(2,1)S(1)}, bf16[256,256]{1,0:T(8,128)(2,1)S(1)}, u32[]{:S(2)}, u32[]{:S(2)}) collective-permute-start(bf16[256,256]{1,0:T(8,128)(2,1)S(1)} %collective-permute-done.refs_2_.refs_0_), channel_id=1, source_target_pairs={{0,4},{1,3},{4,8},{5,1},{8,12},{9,5},{12,14},{13,9},{14,10},{15,13... | collective-permute-start | bytes 393224 | tf_op jit(solution)/shard_map/ppermute | solution.py:51
  15.3 2.0 %collective-permute-start.7 = (bf16[256,256]{1,0:T(8,128)(2,1)S(1)}, bf16[256,256]{1,0:T(8,128)(2,1)S(1)}, u32[]{:S(2)}, u32[]{:S(2)}) collective-permute-start(bf16[256,256]{1,0:T(8,128)(2,1)S(1)} %collective-permute-done.6.refs_7_.refs_5_), channel_id=1, source_target_pairs={{0,4},{1,3},{4,8},{5,1},{8,12},{9,5},{12,14},{13,9},{14,10},{15,13... | collective-permute-start | bytes 393224 | tf_op jit(solution)/shard_map/ppermute | solution.py:51
  17.4 1.5 %collective-permute-done.10.refs_6_.refs_4_ = bf16[256,256]{1,0:T(8,128)(2,1)S(1)} collective-permute-done((bf16[256,256]{1,0:T(8,128)(2,1)S(1)}, bf16[256,256]{1,0:T(8,128)(2,1)S(1)}, u32[]{:S(2)}, u32[]{:S(2)}) %collective-permute-start.10) | collective-permute-done | bytes 131104 | tf_op jit(solution)/shard_map/ppermute | solution.py:51
  18.9 1.4 %collective-permute-start.12 = (bf16[256,256]{1,0:T(8,128)(2,1)S(1)}, bf16[256,256]{1,0:T(8,128)(2,1)S(1)}, u32[]{:S(2)}, u32[]{:S(2)}) collective-permute-start(bf16[256,256]{1,0:T(8,128)(2,1)S(1)} %collective-permute-done.10.refs_6_.refs_4_), channel_id=1, source_target_pairs={{0,4},{1,3},{4,8},{5,1},{8,12},{9,5},{12,14},{13,9},{14,10},{15,13... | collective-permute-start | bytes 393224 | tf_op jit(solution)/shard_map/ppermute | solution.py:51
  21.8 1.8 %collective-permute-start.8 = (bf16[256,256]{1,0:T(8,128)(2,1)S(1)}, bf16[256,256]{1,0:T(8,128)(2,1)S(1)}, u32[]{:S(2)}, u32[]{:S(2)}) collective-permute-start(bf16[256,256]{1,0:T(8,128)(2,1)S(1)} %collective-permute-done.7.refs_11_.refs_9_), channel_id=1, source_target_pairs={{0,4},{1,3},{4,8},{5,1},{8,12},{9,5},{12,14},{13,9},{14,10},{15,13... | collective-permute-start | bytes 393224 | tf_op jit(solution)/shard_map/ppermute | solution.py:51
  27.5 1.6 %collective-permute-done.4.refs_0_.refs_12_ = bf16[256,256]{1,0:T(8,128)(2,1)S(1)} collective-permute-done((bf16[256,256]{1,0:T(8,128)(2,1)S(1)}, bf16[256,256]{1,0:T(8,128)(2,1)S(1)}, u32[]{:S(2)}, u32[]{:S(2)}) %collective-permute-start.4) | collective-permute-done | bytes 131104 | tf_op jit(solution)/shard_map/ppermute | solution.py:51
  29.9 1.3 %collective-permute-start.15 = (bf16[512,128]{1,0:T(8,128)(2,1)S(1)}, bf16[512,128]{1,0:T(8,128)(2,1)S(1)}, u32[]{:S(2)}, u32[]{:S(2)}) collective-permute-start(bf16[512,128]{1,0:T(8,128)(2,1)S(1)} %get-tuple-element.51.codes), channel_id=1, source_target_pairs={{0,1},{2,3},{4,5},{6,7},{8,9},{10,11},{12,13},{14,15},{16,17},{18,... | collective-permute-start | bytes 393224 | tf_op jit(solution)/shard_map/ppermute | solution.py:23
  33.0 2.1 %collective-permute-start.16 = (bf16[256,256]{1,0:T(8,128)(2,1)S(1)}, bf16[256,256]{1,0:T(8,128)(2,1)S(1)}, u32[]{:S(2)}, u32[]{:S(2)}) collective-permute-start(bf16[256,256]{1,0:T(8,128)(2,1)S(1)} %get-tuple-element.56), channel_id=1, source_target_pairs={{0,4},{1,3},{4,8},{5,1},{8,12},{9,5},{12,14},{13,9},{14,10},{15,13... | collective-permute-start | bytes 393224 | tf_op jit(solution)/shard_map/ppermute | solution.py:51
  36.4 2.0 %collective-permute-start.25 = (bf16[256,256]{1,0:T(8,128)(2,1)S(1)}, bf16[256,256]{1,0:T(8,128)(2,1)S(1)}, u32[]{:S(2)}, u32[]{:S(2)}) collective-permute-start(bf16[256,256]{1,0:T(8,128)(2,1)S(1)} %get-tuple-element.70), channel_id=1, source_target_pairs={{0,4},{1,3},{4,8},{5,1},{8,12},{9,5},{12,14},{13,9},{14,10},{15,13... | collective-permute-start | bytes 393224 | tf_op jit(solution)/shard_map/ppermute | solution.py:51
  39.1 2.1 %collective-permute-start.17 = (bf16[256,256]{1,0:T(8,128)(2,1)S(1)}, bf16[256,256]{1,0:T(8,128)(2,1)S(1)}, u32[]{:S(2)}, u32[]{:S(2)}) collective-permute-start(bf16[256,256]{1,0:T(8,128)(2,1)S(1)} %add_convert_fusion.9), channel_id=1, source_target_pairs={{0,4},{1,3},{4,8},{5,1},{8,12},{9,5},{12,14},{13,9},{14,10},{15,13... | collective-permute-start | bytes 393224 | tf_op jit(solution)/shard_map/ppermute | solution.py:51
  41.1 1.6 %collective-permute-done.20 = bf16[256,256]{1,0:T(8,128)(2,1)S(1)} collective-permute-done((bf16[256,256]{1,0:T(8,128)(2,1)S(1)}, bf16[256,256]{1,0:T(8,128)(2,1)S(1)}, u32[]{:S(2)}, u32[]{:S(2)}) %collective-permute-start.20) | collective-permute-done | bytes 131104 | tf_op jit(solution)/shard_map/ppermute | solution.py:51
  42.8 2.1 %collective-permute-start.26 = (bf16[256,256]{1,0:T(8,128)(2,1)S(1)}, bf16[256,256]{1,0:T(8,128)(2,1)S(1)}, u32[]{:S(2)}, u32[]{:S(2)}) collective-permute-start(bf16[256,256]{1,0:T(8,128)(2,1)S(1)} %add_convert_fusion.3), channel_id=1, source_target_pairs={{0,4},{1,3},{4,8},{5,1},{8,12},{9,5},{12,14},{13,9},{14,10},{15,13... | collective-permute-start | bytes 393224 | tf_op jit(solution)/shard_map/ppermute | solution.py:51
  45.6 2.1 %collective-permute-start.18 = (bf16[256,256]{1,0:T(8,128)(2,1)S(1)}, bf16[256,256]{1,0:T(8,128)(2,1)S(1)}, u32[]{:S(2)}, u32[]{:S(2)}) collective-permute-start(bf16[256,256]{1,0:T(8,128)(2,1)S(1)} %add_convert_fusion.8), channel_id=1, source_target_pairs={{0,4},{1,3},{4,8},{5,1},{8,12},{9,5},{12,14},{13,9},{14,10},{15,13... | collective-permute-start | bytes 393224 | tf_op jit(solution)/shard_map/ppermute | solution.py:51
  49.1 1.4 %collective-permute-start.27 = (bf16[256,256]{1,0:T(8,128)(2,1)S(1)}, bf16[256,256]{1,0:T(8,128)(2,1)S(1)}, u32[]{:S(2)}, u32[]{:S(2)}) collective-permute-start(bf16[256,256]{1,0:T(8,128)(2,1)S(1)} %add_convert_fusion.2), channel_id=1, source_target_pairs={{0,4},{1,3},{4,8},{5,1},{8,12},{9,5},{12,14},{13,9},{14,10},{15,13... | collective-permute-start | bytes 393224 | tf_op jit(solution)/shard_map/ppermute | solution.py:51
  51.6 1.3 %collective-permute-start.19 = (bf16[256,256]{1,0:T(8,128)(2,1)S(1)}, bf16[256,256]{1,0:T(8,128)(2,1)S(1)}, u32[]{:S(2)}, u32[]{:S(2)}) collective-permute-start(bf16[256,256]{1,0:T(8,128)(2,1)S(1)} %add_convert_fusion.7), channel_id=1, source_target_pairs={{0,4},{1,3},{4,8},{5,1},{8,12},{9,5},{12,14},{13,9},{14,10},{15,13... | collective-permute-start | bytes 393224 | tf_op jit(solution)/shard_map/ppermute | solution.py:51
  54.5 2.4 %collective-permute-done.19 = bf16[256,256]{1,0:T(8,128)(2,1)S(1)} collective-permute-done((bf16[256,256]{1,0:T(8,128)(2,1)S(1)}, bf16[256,256]{1,0:T(8,128)(2,1)S(1)}, u32[]{:S(2)}, u32[]{:S(2)}) %collective-permute-start.19) | collective-permute-done | bytes 131104 | tf_op jit(solution)/shard_map/ppermute | solution.py:51
  57.0 1.4 %collective-permute-start.34 = (bf16[256,256]{1,0:T(8,128)(2,1)S(1)}, bf16[256,256]{1,0:T(8,128)(2,1)S(1)}, u32[]{:S(2)}, u32[]{:S(2)}) collective-permute-start(bf16[256,256]{1,0:T(8,128)(2,1)S(1)} %multiply_convert_fusion.refs_1_), channel_id=1, source_target_pairs={{0,4},{1,3},{4,8},{5,1},{8,12},{9,5},{12,14},{13,9},{14,10},{15,13... | collective-permute-start | bytes 393224 | tf_op jit(solution)/shard_map/ppermute | solution.py:51
  60.3 1.4 %collective-permute-start.38 = (bf16[256,256]{1,0:T(8,128)(2,1)S(1)}, bf16[256,256]{1,0:T(8,128)(2,1)S(1)}, u32[]{:S(2)}, u32[]{:S(2)}) collective-permute-start(bf16[256,256]{1,0:T(8,128)(2,1)S(1)} %fusion.1.refs_0_), channel_id=1, source_target_pairs={{0,4},{1,3},{4,8},{5,1},{8,12},{9,5},{12,14},{13,9},{14,10},{15,13... | collective-permute-start | bytes 393224 | tf_op jit(solution)/shard_map/ppermute | solution.py:51
  63.3 1.3 %collective-permute-start.35 = (bf16[256,256]{1,0:T(8,128)(2,1)S(1)}, bf16[256,256]{1,0:T(8,128)(2,1)S(1)}, u32[]{:S(2)}, u32[]{:S(2)}) collective-permute-start(bf16[256,256]{1,0:T(8,128)(2,1)S(1)} %collective-permute-done.34.refs_1_), channel_id=1, source_target_pairs={{0,4},{1,3},{4,8},{5,1},{8,12},{9,5},{12,14},{13,9},{14,10},{15,13... | collective-permute-start | bytes 393224 | tf_op jit(solution)/shard_map/ppermute | solution.py:51
  66.4 1.4 %collective-permute-start.40 = (bf16[256,256]{1,0:T(8,128)(2,1)S(1)}, bf16[256,256]{1,0:T(8,128)(2,1)S(1)}, u32[]{:S(2)}, u32[]{:S(2)}) collective-permute-start(bf16[256,256]{1,0:T(8,128)(2,1)S(1)} %collective-permute-done.38.refs_0_), channel_id=1, source_target_pairs={{0,4},{1,3},{4,8},{5,1},{8,12},{9,5},{12,14},{13,9},{14,10},{15,13... | collective-permute-start | bytes 393224 | tf_op jit(solution)/shard_map/ppermute | solution.py:51
  69.5 1.4 %collective-permute-start.36 = (bf16[256,256]{1,0:T(8,128)(2,1)S(1)}, bf16[256,256]{1,0:T(8,128)(2,1)S(1)}, u32[]{:S(2)}, u32[]{:S(2)}) collective-permute-start(bf16[256,256]{1,0:T(8,128)(2,1)S(1)} %collective-permute-done.35.refs_5_), channel_id=1, source_target_pairs={{0,4},{1,3},{4,8},{5,1},{8,12},{9,5},{12,14},{13,9},{14,10},{15,13... | collective-permute-start | bytes 393224 | tf_op jit(solution)/shard_map/ppermute | solution.py:51
  74.5 1.3 %collective-permute-done.36.refs_9_ = bf16[256,256]{1,0:T(8,128)(2,1)S(1)} collective-permute-done((bf16[256,256]{1,0:T(8,128)(2,1)S(1)}, bf16[256,256]{1,0:T(8,128)(2,1)S(1)}, u32[]{:S(2)}, u32[]{:S(2)}) %collective-permute-start.36) | collective-permute-done | bytes 131104 | tf_op jit(solution)/shard_map/ppermute | solution.py:51
  75.8 1.4 %collective-permute-start.37 = (bf16[256,256]{1,0:T(8,128)(2,1)S(1)}, bf16[256,256]{1,0:T(8,128)(2,1)S(1)}, u32[]{:S(2)}, u32[]{:S(2)}) collective-permute-start(bf16[256,256]{1,0:T(8,128)(2,1)S(1)} %collective-permute-done.36.refs_9_), channel_id=1, source_target_pairs={{0,4},{1,3},{4,8},{5,1},{8,12},{9,5},{12,14},{13,9},{14,10},{15,13... | collective-permute-start | bytes 393224 | tf_op jit(solution)/shard_map/ppermute | solution.py:51
  78.8 1.5 %shard_map.101 = (f32[6,256,256]{2,1,0:T(8,128)S(1)}, f32[2,256,256]{2,1,0:T(8,128)S(1)}) custom-call(s32[9]{0:T(128)S(1)} %stack.39.starts, bf16[256,256]{1,0:T(8,128)(2,1)S(1)} %collective-permute-done.38.refs_0_, bf16[256,256]{1,0:T(8,128)(2,1)S(1)} %collective-permute-done.34.refs_1_, bf16[256,256]{1,0:T(8,128)(2,1)S(1)} %collective-permute-done.30.refs_2_, ...), custom_call_target="tpu_custom_call" | custom-call | flops 402653184 | bytes 1024 | tf_op jit(solution)/shard_map/pallas_call | solution.py:64
  80.8 1.4 %collective-permute-done.33.refs_0_ = bf16[256,256]{1,0:T(8,128)(2,1)S(1)} collective-permute-done((bf16[256,256]{1,0:T(8,128)(2,1)S(1)}, bf16[256,256]{1,0:T(8,128)(2,1)S(1)}, u32[]{:S(2)}, u32[]{:S(2)}) %collective-permute-start.33) | collective-permute-done | bytes 131104 | tf_op jit(solution)/shard_map/ppermute | solution.py:51
  82.8 1.3 %collective-permute-start.44 = (bf16[1536,128]{1,0:T(8,128)(2,1)S(1)}, bf16[1536,128]{1,0:T(8,128)(2,1)S(1)}, u32[]{:S(2)}, u32[]{:S(2)}) collective-permute-start(bf16[1536,128]{1,0:T(8,128)(2,1)S(1)} %get-tuple-element.84), channel_id=1, source_target_pairs={{1,0},{3,2},{5,4},{7,6},{9,8},{11,10},{13,12},{15,14},{17,16},{19,... | collective-permute-start | bytes 1179656 | tf_op jit(solution)/shard_map/ppermute | solution.py:23
  84.1 1.6 %shard_map.102 = (f32[512,128]{1,0:T(8,128)S(1)}, f32[1,128,2048]{2,1,0:T(8,128)}) custom-call(s32[9]{0:T(128)S(1)} %stack.39.starts, bf16[256,256]{1,0:T(8,128)(2,1)S(1)} %collective-permute-done.33.refs_0_, bf16[256,256]{1,0:T(8,128)(2,1)S(1)} %collective-permute-done.37.refs_1_, bf16[256,2048]{1,0:T(8,128)(2,1)S(1)} %maximum_maximum_fusion.stacked.refs_2_.refs_12_, ...), custom_call_target="tpu_custom_call" | custom-call | bytes 1024 | tf_op jit(solution)/shard_map/pallas_call | solution.py:64
  86.4 2.7 %shard_map.104 = (f32[1,2048,128]{2,1,0:T(8,128)}, f32[1,128]{1,0:T(1,128)}, f32[128,1024]{1,0:T(8,128)}) custom-call(s32[9]{0:T(128)S(1)} %stack.39.starts, bf16[2048,512]{1,0:T(8,128)(2,1)S(1)} %shard_map.99.turned, f32[512,128]{1,0:T(8,128)S(1)} %get-tuple-element.66.preact, f32[512,128]{1,0:T(8,128)S(1)} %get-tuple-element.83.back_own, ...), custom_call_target="tpu_custom_call" | custom-call | flops 268435456 | bytes 1024 | tf_op jit(solution)/shard_map/pallas_call | solution.py:64
  (92 shorter events, 32.6 us)
Async XLA Ops:
  1.7 6.8 %collective-permute-start.5 = (bf16[256,256]{1,0:T(8,128)(2,1)S(1)}, bf16[256,256]{1,0:T(8,128)(2,1)S(1)}, u32[]{:S(2)}, u32[]{:S(2)}) collective-permute-start(bf16[256,256]{1,0:T(8,128)(2,1)S(1)} %get-tuple-element.48.shard.refs_1_), channel_id=1, source_target_pairs={{0,4},{1,3},{4,8},{5,1},{8,12},{9,5},{12,14},{13,9},{14,10},{15,13... | collective-permute-start | bytes 393224 | tf_op jit(solution)/shard_map/ppermute | solution.py:51
  4.8 6.3 %collective-permute-start.1 = (bf16[256,256]{1,0:T(8,128)(2,1)S(1)}, bf16[256,256]{1,0:T(8,128)(2,1)S(1)}, u32[]{:S(2)}, u32[]{:S(2)}) collective-permute-start(bf16[256,256]{1,0:T(8,128)(2,1)S(1)} %get-tuple-element.47.shard.refs_0_), channel_id=1, source_target_pairs={{0,2},{1,5},{4,0},{5,9},{8,4},{9,13},{12,8},{13,15},{14,12},{15,11... | collective-permute-start | bytes 393224 | tf_op jit(solution)/shard_map/ppermute | solution.py:51
  5.5 6.0 %collective-permute-start = (bf16[256,256]{1,0:T(8,128)(2,1)S(1)}, bf16[256,256]{1,0:T(8,128)(2,1)S(1)}, u32[]{:S(2)}, u32[]{:S(2)}) collective-permute-start(bf16[256,256]{1,0:T(8,128)(2,1)S(1)} %get-tuple-element.47.shard.refs_0_), channel_id=1, source_target_pairs={{0,4},{1,3},{4,8},{5,1},{8,12},{9,5},{12,14},{13,9},{14,10},{15,13... | collective-permute-start | bytes 393224 | tf_op jit(solution)/shard_map/ppermute | solution.py:51
  8.2 7.1 %collective-permute-start.9 = (bf16[256,256]{1,0:T(8,128)(2,1)S(1)}, bf16[256,256]{1,0:T(8,128)(2,1)S(1)}, u32[]{:S(2)}, u32[]{:S(2)}) collective-permute-start(bf16[256,256]{1,0:T(8,128)(2,1)S(1)} %get-tuple-element.48.shard.refs_1_), channel_id=1, source_target_pairs={{0,2},{1,5},{4,0},{5,9},{8,4},{9,13},{12,8},{13,15},{14,12},{15,11... | collective-permute-start | bytes 393224 | tf_op jit(solution)/shard_map/ppermute | solution.py:51
  8.5 6.8 %collective-permute-start.6 = (bf16[256,256]{1,0:T(8,128)(2,1)S(1)}, bf16[256,256]{1,0:T(8,128)(2,1)S(1)}, u32[]{:S(2)}, u32[]{:S(2)}) collective-permute-start(bf16[256,256]{1,0:T(8,128)(2,1)S(1)} %collective-permute-done.5.refs_3_.refs_1_), channel_id=1, source_target_pairs={{0,4},{1,3},{4,8},{5,1},{8,12},{9,5},{12,14},{13,9},{14,10},{15,13... | collective-permute-start | bytes 393224 | tf_op jit(solution)/shard_map/ppermute | solution.py:51
  11.1 6.3 %collective-permute-start.2 = (bf16[256,256]{1,0:T(8,128)(2,1)S(1)}, bf16[256,256]{1,0:T(8,128)(2,1)S(1)}, u32[]{:S(2)}, u32[]{:S(2)}) collective-permute-start(bf16[256,256]{1,0:T(8,128)(2,1)S(1)} %collective-permute-done.1.refs_4_.refs_2_), channel_id=1, source_target_pairs={{0,2},{1,5},{4,0},{5,9},{8,4},{9,13},{12,8},{13,15},{14,12},{15,11... | collective-permute-start | bytes 393224 | tf_op jit(solution)/shard_map/ppermute | solution.py:51
  11.5 12.7 %collective-permute-start.14 = (bf16[128,1024]{1,0:T(8,128)(2,1)}, bf16[128,1024]{1,0:T(8,128)(2,1)S(1)}, u32[]{:S(2)}, u32[]{:S(2)}) collective-permute-start(bf16[128,1024]{1,0:T(8,128)(2,1)} %param.11), channel_id=1, source_target_pairs={{0,1},{2,3},{4,5},{6,7},{8,9},{10,11},{12,13},{14,15},{16,17},{18,... | collective-permute-start | bytes 786440 | tf_op jit(solution)/shard_map/ppermute | solution.py:23
  12.8 6.2 %collective-permute-start.10 = (bf16[256,256]{1,0:T(8,128)(2,1)S(1)}, bf16[256,256]{1,0:T(8,128)(2,1)S(1)}, u32[]{:S(2)}, u32[]{:S(2)}) collective-permute-start(bf16[256,256]{1,0:T(8,128)(2,1)S(1)} %collective-permute-done.refs_2_.refs_0_), channel_id=1, source_target_pairs={{0,4},{1,3},{4,8},{5,1},{8,12},{9,5},{12,14},{13,9},{14,10},{15,13... | collective-permute-start | bytes 393224 | tf_op jit(solution)/shard_map/ppermute | solution.py:51
  15.3 6.0 %collective-permute-start.11 = (bf16[256,256]{1,0:T(8,128)(2,1)S(1)}, bf16[256,256]{1,0:T(8,128)(2,1)S(1)}, u32[]{:S(2)}, u32[]{:S(2)}) collective-permute-start(bf16[256,256]{1,0:T(8,128)(2,1)S(1)} %collective-permute-done.9.refs_5_.refs_3_), channel_id=1, source_target_pairs={{0,2},{1,5},{4,0},{5,9},{8,4},{9,13},{12,8},{13,15},{14,12},{15,11... | collective-permute-start | bytes 393224 | tf_op jit(solution)/shard_map/ppermute | solution.py:51
  15.3 6.5 %collective-permute-start.7 = (bf16[256,256]{1,0:T(8,128)(2,1)S(1)}, bf16[256,256]{1,0:T(8,128)(2,1)S(1)}, u32[]{:S(2)}, u32[]{:S(2)}) collective-permute-start(bf16[256,256]{1,0:T(8,128)(2,1)S(1)} %collective-permute-done.6.refs_7_.refs_5_), channel_id=1, source_target_pairs={{0,4},{1,3},{4,8},{5,1},{8,12},{9,5},{12,14},{13,9},{14,10},{15,13... | collective-permute-start | bytes 393224 | tf_op jit(solution)/shard_map/ppermute | solution.py:51
  17.4 6.7 %collective-permute-start.3 = (bf16[256,256]{1,0:T(8,128)(2,1)S(1)}, bf16[256,256]{1,0:T(8,128)(2,1)S(1)}, u32[]{:S(2)}, u32[]{:S(2)}) collective-permute-start(bf16[256,256]{1,0:T(8,128)(2,1)S(1)} %collective-permute-done.2.refs_8_.refs_6_), channel_id=1, source_target_pairs={{0,2},{1,5},{4,0},{5,9},{8,4},{9,13},{12,8},{13,15},{14,12},{15,11... | collective-permute-start | bytes 393224 | tf_op jit(solution)/shard_map/ppermute | solution.py:51
  18.9 6.4 %collective-permute-start.12 = (bf16[256,256]{1,0:T(8,128)(2,1)S(1)}, bf16[256,256]{1,0:T(8,128)(2,1)S(1)}, u32[]{:S(2)}, u32[]{:S(2)}) collective-permute-start(bf16[256,256]{1,0:T(8,128)(2,1)S(1)} %collective-permute-done.10.refs_6_.refs_4_), channel_id=1, source_target_pairs={{0,4},{1,3},{4,8},{5,1},{8,12},{9,5},{12,14},{13,9},{14,10},{15,13... | collective-permute-start | bytes 393224 | tf_op jit(solution)/shard_map/ppermute | solution.py:51
  32.9 6.0 %collective-permute-start.21 = (bf16[256,256]{1,0:T(8,128)(2,1)S(1)}, bf16[256,256]{1,0:T(8,128)(2,1)S(1)}, u32[]{:S(2)}, u32[]{:S(2)}) collective-permute-start(bf16[256,256]{1,0:T(8,128)(2,1)S(1)} %get-tuple-element.60), channel_id=1, source_target_pairs={{0,2},{1,5},{4,0},{5,9},{8,4},{9,13},{12,8},{13,15},{14,12},{15,11... | collective-permute-start | bytes 393224 | tf_op jit(solution)/shard_map/ppermute | solution.py:51
  33.0 6.0 %collective-permute-start.16 = (bf16[256,256]{1,0:T(8,128)(2,1)S(1)}, bf16[256,256]{1,0:T(8,128)(2,1)S(1)}, u32[]{:S(2)}, u32[]{:S(2)}) collective-permute-start(bf16[256,256]{1,0:T(8,128)(2,1)S(1)} %get-tuple-element.56), channel_id=1, source_target_pairs={{0,4},{1,3},{4,8},{5,1},{8,12},{9,5},{12,14},{13,9},{14,10},{15,13... | collective-permute-start | bytes 393224 | tf_op jit(solution)/shard_map/ppermute | solution.py:51
  36.3 6.4 %collective-permute-start.20 = (bf16[256,256]{1,0:T(8,128)(2,1)S(1)}, bf16[256,256]{1,0:T(8,128)(2,1)S(1)}, u32[]{:S(2)}, u32[]{:S(2)}) collective-permute-start(bf16[256,256]{1,0:T(8,128)(2,1)S(1)} %get-tuple-element.59), channel_id=1, source_target_pairs={{0,2},{1,5},{4,0},{5,9},{8,4},{9,13},{12,8},{13,15},{14,12},{15,11... | collective-permute-start | bytes 393224 | tf_op jit(solution)/shard_map/ppermute | solution.py:51
  36.4 6.4 %collective-permute-start.25 = (bf16[256,256]{1,0:T(8,128)(2,1)S(1)}, bf16[256,256]{1,0:T(8,128)(2,1)S(1)}, u32[]{:S(2)}, u32[]{:S(2)}) collective-permute-start(bf16[256,256]{1,0:T(8,128)(2,1)S(1)} %get-tuple-element.70), channel_id=1, source_target_pairs={{0,4},{1,3},{4,8},{5,1},{8,12},{9,5},{12,14},{13,9},{14,10},{15,13... | collective-permute-start | bytes 393224 | tf_op jit(solution)/shard_map/ppermute | solution.py:51
  39.0 6.5 %collective-permute-start.23 = (bf16[256,256]{1,0:T(8,128)(2,1)S(1)}, bf16[256,256]{1,0:T(8,128)(2,1)S(1)}, u32[]{:S(2)}, u32[]{:S(2)}) collective-permute-start(bf16[256,256]{1,0:T(8,128)(2,1)S(1)} %add_convert_fusion.4), channel_id=1, source_target_pairs={{0,2},{1,5},{4,0},{5,9},{8,4},{9,13},{12,8},{13,15},{14,12},{15,11... | collective-permute-start | bytes 393224 | tf_op jit(solution)/shard_map/ppermute | solution.py:51
  39.1 6.5 %collective-permute-start.17 = (bf16[256,256]{1,0:T(8,128)(2,1)S(1)}, bf16[256,256]{1,0:T(8,128)(2,1)S(1)}, u32[]{:S(2)}, u32[]{:S(2)}) collective-permute-start(bf16[256,256]{1,0:T(8,128)(2,1)S(1)} %add_convert_fusion.9), channel_id=1, source_target_pairs={{0,4},{1,3},{4,8},{5,1},{8,12},{9,5},{12,14},{13,9},{14,10},{15,13... | collective-permute-start | bytes 393224 | tf_op jit(solution)/shard_map/ppermute | solution.py:51
  42.8 6.2 %collective-permute-start.26 = (bf16[256,256]{1,0:T(8,128)(2,1)S(1)}, bf16[256,256]{1,0:T(8,128)(2,1)S(1)}, u32[]{:S(2)}, u32[]{:S(2)}) collective-permute-start(bf16[256,256]{1,0:T(8,128)(2,1)S(1)} %add_convert_fusion.3), channel_id=1, source_target_pairs={{0,4},{1,3},{4,8},{5,1},{8,12},{9,5},{12,14},{13,9},{14,10},{15,13... | collective-permute-start | bytes 393224 | tf_op jit(solution)/shard_map/ppermute | solution.py:51
  45.5 7.4 %collective-permute-start.28 = (bf16[256,256]{1,0:T(8,128)(2,1)S(1)}, bf16[256,256]{1,0:T(8,128)(2,1)S(1)}, u32[]{:S(2)}, u32[]{:S(2)}) collective-permute-start(bf16[256,256]{1,0:T(8,128)(2,1)S(1)} %add_convert_fusion.1), channel_id=1, source_target_pairs={{0,2},{1,5},{4,0},{5,9},{8,4},{9,13},{12,8},{13,15},{14,12},{15,11... | collective-permute-start | bytes 393224 | tf_op jit(solution)/shard_map/ppermute | solution.py:51
  45.6 5.9 %collective-permute-start.18 = (bf16[256,256]{1,0:T(8,128)(2,1)S(1)}, bf16[256,256]{1,0:T(8,128)(2,1)S(1)}, u32[]{:S(2)}, u32[]{:S(2)}) collective-permute-start(bf16[256,256]{1,0:T(8,128)(2,1)S(1)} %add_convert_fusion.8), channel_id=1, source_target_pairs={{0,4},{1,3},{4,8},{5,1},{8,12},{9,5},{12,14},{13,9},{14,10},{15,13... | collective-permute-start | bytes 393224 | tf_op jit(solution)/shard_map/ppermute | solution.py:51
  48.3 6.2 %collective-permute-start.24 = (bf16[256,256]{1,0:T(8,128)(2,1)S(1)}, bf16[256,256]{1,0:T(8,128)(2,1)S(1)}, u32[]{:S(2)}, u32[]{:S(2)}) collective-permute-start(bf16[256,256]{1,0:T(8,128)(2,1)S(1)} %add_convert_fusion.5), channel_id=1, source_target_pairs={{0,2},{1,5},{4,0},{5,9},{8,4},{9,13},{12,8},{13,15},{14,12},{15,11... | collective-permute-start | bytes 393224 | tf_op jit(solution)/shard_map/ppermute | solution.py:51
  49.1 9.3 %collective-permute-start.27 = (bf16[256,256]{1,0:T(8,128)(2,1)S(1)}, bf16[256,256]{1,0:T(8,128)(2,1)S(1)}, u32[]{:S(2)}, u32[]{:S(2)}) collective-permute-start(bf16[256,256]{1,0:T(8,128)(2,1)S(1)} %add_convert_fusion.2), channel_id=1, source_target_pairs={{0,4},{1,3},{4,8},{5,1},{8,12},{9,5},{12,14},{13,9},{14,10},{15,13... | collective-permute-start | bytes 393224 | tf_op jit(solution)/shard_map/ppermute | solution.py:51
  57.0 6.3 %collective-permute-start.34 = (bf16[256,256]{1,0:T(8,128)(2,1)S(1)}, bf16[256,256]{1,0:T(8,128)(2,1)S(1)}, u32[]{:S(2)}, u32[]{:S(2)}) collective-permute-start(bf16[256,256]{1,0:T(8,128)(2,1)S(1)} %multiply_convert_fusion.refs_1_), channel_id=1, source_target_pairs={{0,4},{1,3},{4,8},{5,1},{8,12},{9,5},{12,14},{13,9},{14,10},{15,13... | collective-permute-start | bytes 393224 | tf_op jit(solution)/shard_map/ppermute | solution.py:51
  58.4 6.1 %collective-permute-start.30 = (bf16[256,256]{1,0:T(8,128)(2,1)S(1)}, bf16[256,256]{1,0:T(8,128)(2,1)S(1)}, u32[]{:S(2)}, u32[]{:S(2)}) collective-permute-start(bf16[256,256]{1,0:T(8,128)(2,1)S(1)} %fusion.1.refs_0_), channel_id=1, source_target_pairs={{0,2},{1,5},{4,0},{5,9},{8,4},{9,13},{12,8},{13,15},{14,12},{15,11... | collective-permute-start | bytes 393224 | tf_op jit(solution)/shard_map/ppermute | solution.py:51
  60.3 6.2 %collective-permute-start.38 = (bf16[256,256]{1,0:T(8,128)(2,1)S(1)}, bf16[256,256]{1,0:T(8,128)(2,1)S(1)}, u32[]{:S(2)}, u32[]{:S(2)}) collective-permute-start(bf16[256,256]{1,0:T(8,128)(2,1)S(1)} %fusion.1.refs_0_), channel_id=1, source_target_pairs={{0,4},{1,3},{4,8},{5,1},{8,12},{9,5},{12,14},{13,9},{14,10},{15,13... | collective-permute-start | bytes 393224 | tf_op jit(solution)/shard_map/ppermute | solution.py:51
  63.3 6.2 %collective-permute-start.35 = (bf16[256,256]{1,0:T(8,128)(2,1)S(1)}, bf16[256,256]{1,0:T(8,128)(2,1)S(1)}, u32[]{:S(2)}, u32[]{:S(2)}) collective-permute-start(bf16[256,256]{1,0:T(8,128)(2,1)S(1)} %collective-permute-done.34.refs_1_), channel_id=1, source_target_pairs={{0,4},{1,3},{4,8},{5,1},{8,12},{9,5},{12,14},{13,9},{14,10},{15,13... | collective-permute-start | bytes 393224 | tf_op jit(solution)/shard_map/ppermute | solution.py:51
  64.6 6.4 %collective-permute-start.31 = (bf16[256,256]{1,0:T(8,128)(2,1)S(1)}, bf16[256,256]{1,0:T(8,128)(2,1)S(1)}, u32[]{:S(2)}, u32[]{:S(2)}) collective-permute-start(bf16[256,256]{1,0:T(8,128)(2,1)S(1)} %collective-permute-done.30.refs_2_), channel_id=1, source_target_pairs={{0,2},{1,5},{4,0},{5,9},{8,4},{9,13},{12,8},{13,15},{14,12},{15,11... | collective-permute-start | bytes 393224 | tf_op jit(solution)/shard_map/ppermute | solution.py:51
  66.4 6.0 %collective-permute-start.40 = (bf16[256,256]{1,0:T(8,128)(2,1)S(1)}, bf16[256,256]{1,0:T(8,128)(2,1)S(1)}, u32[]{:S(2)}, u32[]{:S(2)}) collective-permute-start(bf16[256,256]{1,0:T(8,128)(2,1)S(1)} %collective-permute-done.38.refs_0_), channel_id=1, source_target_pairs={{0,4},{1,3},{4,8},{5,1},{8,12},{9,5},{12,14},{13,9},{14,10},{15,13... | collective-permute-start | bytes 393224 | tf_op jit(solution)/shard_map/ppermute | solution.py:51
  68.0 5.8 %collective-permute-start.41 = (bf16[256,256]{1,0:T(8,128)(2,1)S(1)}, bf16[256,256]{1,0:T(8,128)(2,1)S(1)}, u32[]{:S(2)}, u32[]{:S(2)}) collective-permute-start(bf16[256,256]{1,0:T(8,128)(2,1)S(1)} %collective-permute-done.39.refs_3_), channel_id=1, source_target_pairs={{0,2},{1,5},{4,0},{5,9},{8,4},{9,13},{12,8},{13,15},{14,12},{15,11... | collective-permute-start | bytes 393224 | tf_op jit(solution)/shard_map/ppermute | solution.py:51
  69.5 6.3 %collective-permute-start.36 = (bf16[256,256]{1,0:T(8,128)(2,1)S(1)}, bf16[256,256]{1,0:T(8,128)(2,1)S(1)}, u32[]{:S(2)}, u32[]{:S(2)}) collective-permute-start(bf16[256,256]{1,0:T(8,128)(2,1)S(1)} %collective-permute-done.35.refs_5_), channel_id=1, source_target_pairs={{0,4},{1,3},{4,8},{5,1},{8,12},{9,5},{12,14},{13,9},{14,10},{15,13... | collective-permute-start | bytes 393224 | tf_op jit(solution)/shard_map/ppermute | solution.py:51
  71.0 6.3 %collective-permute-start.32 = (bf16[256,256]{1,0:T(8,128)(2,1)S(1)}, bf16[256,256]{1,0:T(8,128)(2,1)S(1)}, u32[]{:S(2)}, u32[]{:S(2)}) collective-permute-start(bf16[256,256]{1,0:T(8,128)(2,1)S(1)} %collective-permute-done.31.refs_6_), channel_id=1, source_target_pairs={{0,2},{1,5},{4,0},{5,9},{8,4},{9,13},{12,8},{13,15},{14,12},{15,11... | collective-permute-start | bytes 393224 | tf_op jit(solution)/shard_map/ppermute | solution.py:51
  (16 other events, 122.5 us)

commit v17 on v15

--- a/solution.py
+++ b/solution.py
@@ -15,6 +15,7 @@
 RING_LIMIT = 16
 VMEM_BYTES = 24 * 1024 * 1024
 PIECES = 8
+URGENT = 5 * 10**9
 
 
 def passed_along(shard, axis, by):
@@ -40,12 +41,12 @@
     return jnp.where(member % 2 == 0, member // 2, size - 1 - member // 2)
 
 
-def hop(shard, way):
+def hop(shard, way, only=None):
     size, layers = lax.axis_size("latent"), lax.axis_size("layer")
     order = ring_order(size)
     pairs = []
     for p in range(size):
-        for layer in range(layers):
+        for layer in only or range(layers):
             by = way if layer % 2 == 0 else -way
             pairs.append((order[p] * layers + layer, order[(p + by) % size] * layers + layer))
     return lax.ppermute(shard, ("latent", "layer"), pairs)
@@ -55,7 +56,7 @@
     return lax.optimization_barrier((value,) + others)[0]
 
 
-def call(kernel, outs, flops, operands, spaces=None, out_spaces=None, scratch=(), aliases=None):
+def call(kernel, outs, flops, operands, spaces=None, out_spaces=None, scratch=(), aliases=None, weight=0):
     def spec(space):
         return pl.BlockSpec(memory_space=space)
 
@@ -69,7 +70,7 @@
         scratch_shapes=list(scratch),
         input_output_aliases=aliases or {},
         compiler_params=pltpu.CompilerParams(vmem_limit_bytes=VMEM_BYTES),
-        cost_estimate=pl.CostEstimate(flops=flops, bytes_accessed=1024, transcendentals=0),
+        cost_estimate=pl.CostEstimate(flops=flops + weight, bytes_accessed=1024, transcendentals=0),
     )(*operands)
 
 
@@ -178,10 +179,11 @@
 
 
 def own_back_kernel(slots, far, starts, *refs):
-    shards, (stacked, *both_t), refs = refs[:2], refs[2:5], refs[5:]
+    firsts, laters, (stacked, *both_t), refs = refs[:2], refs[2:4], refs[4:7], refs[7:]
     outers, (before, back_own, same, last, sems) = refs[:-5], refs[-5:]
-    rows, wide = shards[0].shape
+    rows, wide = firsts[0].shape
     lat = back_own.shape[1]
+    first = starts[starts.shape[0] - 1] == 0
     blocks = []
     for group, outer in zip(slots, outers):
         blocks += [(slot, outer.at[i, :lat, :]) for i, slot in enumerate(group)]
@@ -194,7 +196,7 @@
     decoder = stacked[:lat, block_of(starts, far, wide)]
     total = 0.0
     for chain in range(2):
-        error = shards[chain][...]
+        error = jnp.where(first, firsts[chain][...], laters[chain][...])
         total = total + jnp.dot(both_t[chain][:lat, :], error, preferred_element_type=F32)
         term = lax.dot_general(error, decoder, OVER_COLS, preferred_element_type=F32)
         back_own[chain * rows:(chain + 1) * rows, :] = before[chain, :, :lat] + term
@@ -267,13 +269,16 @@
 
     urgent, later = ((0, -1), (1, 1)), ((0, 1), (1, -1))
 
-    def gather_step(found, s, ready=None):
+    def gather_step(found, s, ready=None, split=None):
         for chain, way in urgent + later if s < reach else urgent:
             slots = slot_p if way == 1 else slot_q
             shard = found[chain][slots[s - 1] if s > 1 else 0]
             if ready is not None and (chain, way) in later:
                 shard = after(shard, ready[chain])
-            found[chain][slots[s] if s < reach else far] = hop(shard, way)
+            if split and s == reach:
+                found[chain][far] = hop(shard, way, (0,)), hop(shard, way, split)
+            else:
+                found[chain][slots[s] if s < reach else far] = hop(shard, way)
 
     def both_chains(found, slots):
         return [found[chain][slot] for slot in slots for chain in chains]
@@ -355,29 +360,32 @@
         0,
         [starts] + turned_own + arrived + both_chains(inputs, range(1, size))[1:],
     )[0]
+    later_layers = tuple(range(1, lax.axis_size("layer")))
     for s in range(1, reach + 1):
-        gather_step(errors, s, (turned, turned) if s == 2 else None)
+        gather_step(errors, s, (turned, turned) if s == 2 else None, later_layers)
     cut = 1 + 2 * min(1, reach - 1)
     groups = [group for group in (tuple(range(cut)), tuple(range(cut, far))) if group]
     outers, acc = [], None
     for group in groups:
         outer, acc = back(group, acc)
         outers.append(outer)
-    last = both_chains(errors, (far,)) + [stacked] + both_t + outers + [acc]
+    far_first, far_later = zip(errors[0][far], errors[1][far])
+    others = [stacked] + both_t + outers + [acc]
     sent, high = call(
         functools.partial(cross_back_kernel, groups, far),
         [shape((rows + half_width, lat), BF16), shape((half_width, lat), F32)],
         0,
-        [starts] + last,
+        [starts] + list(far_later) + others,
     )
     returned = passed_along(sent, "layer", -1)
     back_own, grad_same = call(
         functools.partial(own_back_kernel, groups, far),
         [shape((rows, lat), F32), shape((1, lat, deep), F32)],
         0,
-        [starts] + last,
+        [starts] + list(far_first) + list(far_later) + others,
         out_spaces=[pltpu.VMEM, pl.ANY],
         scratch=[pltpu.VMEM((lat, wide), F32), pltpu.SemaphoreType.DMA((size,))],
+        weight=URGENT,
     )
     height = deep // PIECES
     grad_enc, grad_bias, grad_cross = call(

time: 88.9 us -> 102 us (1.15)
  starting transfers between devices: 47.4 us -> 57.6 us
  waiting for transfers between devices: 23.9 us -> 26.4 us
    ppermute x42 -> x44, starting transfers between devices: 43.5 us -> 53.7 us  [hop(): return lax.ppermute(shard, ('latent', 'layer'), pairs)]
    ppermute x42 -> x44, waiting for transfers between devices: 22.3 us -> 24.8 us  [hop(): return lax.ppermute(shard, ('latent', 'layer'), pairs)]
  transfers between devices with their start and end apart: 45 -> 47, of which waited for: 28 -> 23; matrix products, arithmetic and copies ran while one was open for 2% -> 2% of each run, Pallas kernels for 10% -> 9%
where the time goes in v17:
time: 102 us; the launch traced here: 101 us
  starting transfers between devices  57.6 us (56%)
  waiting for transfers between devices  26.4 us (26%)
  Pallas kernels  13.6 us (13%)
  other arithmetic  1.63 us (2%)
  local copies, waits for them, and re-layouts  1.15 us (1%)
    ppermute x44, starting transfers between devices, hop(): return lax.ppermute(shard, ('latent', 'layer'), pairs)  53.7 us
    ppermute x44, waiting for transfers between devices, hop(): return lax.ppermute(shard, ('latent', 'layer'), pairs)  24.8 us
    pallas_call x12, Pallas kernels, call(): pl.pallas_call(kernel, out_shape=outs, in_specs=[spec(pltpu.SMEM)] + [spe...  13.6 us
    ppermute x3, starting transfers between devices, passed_along(): return lax.ppermute(shard, axis, pairs)  3.89 us
  transfers between devices with their start and end apart: 47, of which 23 were waited for; matrix products, arithmetic and copies ran while one was open for 2% of the time, Pallas kernels for 9%

profile of v17, /device:TPU:0, one launch (start us, length us, event | category | flops | bytes accessed | tf_op | source)
XLA Modules:
  0.0 101.4 jit_solution(17073117816722884298)
XLA Ops:
  1.7 3.0 %collective-permute-start.1 = (bf16[256,256]{1,0:T(8,128)(2,1)S(1)}, bf16[256,256]{1,0:T(8,128)(2,1)S(1)}, u32[]{:S(2)}, u32[]{:S(2)}) collective-permute-start(bf16[256,256]{1,0:T(8,128)(2,1)S(1)} %get-tuple-element.47.shard.refs_0_), channel_id=1, source_target_pairs={{0,2},{1,5},{4,0},{5,9},{8,4},{9,13},{12,8},{13,15},{14,12},{15,11... | collective-permute-start | bytes 393224 | tf_op jit(solution)/shard_map/ppermute | solution.py:52
  5.6 2.0 %collective-permute-start = (bf16[256,256]{1,0:T(8,128)(2,1)S(1)}, bf16[256,256]{1,0:T(8,128)(2,1)S(1)}, u32[]{:S(2)}, u32[]{:S(2)}) collective-permute-start(bf16[256,256]{1,0:T(8,128)(2,1)S(1)} %get-tuple-element.47.shard.refs_0_), channel_id=1, source_target_pairs={{0,4},{1,3},{4,8},{5,1},{8,12},{9,5},{12,14},{13,9},{14,10},{15,13... | collective-permute-start | bytes 393224 | tf_op jit(solution)/shard_map/ppermute | solution.py:52
  8.6 2.1 %collective-permute-start.2 = (bf16[256,256]{1,0:T(8,128)(2,1)S(1)}, bf16[256,256]{1,0:T(8,128)(2,1)S(1)}, u32[]{:S(2)}, u32[]{:S(2)}) collective-permute-start(bf16[256,256]{1,0:T(8,128)(2,1)S(1)} %collective-permute-done.1.refs_4_.refs_2_), channel_id=1, source_target_pairs={{0,2},{1,5},{4,0},{5,9},{8,4},{9,13},{12,8},{13,15},{14,12},{15,11... | collective-permute-start | bytes 393224 | tf_op jit(solution)/shard_map/ppermute | solution.py:52
  11.0 1.3 %collective-permute-done.refs_2_.refs_0_ = bf16[256,256]{1,0:T(8,128)(2,1)S(1)} collective-permute-done((bf16[256,256]{1,0:T(8,128)(2,1)S(1)}, bf16[256,256]{1,0:T(8,128)(2,1)S(1)}, u32[]{:S(2)}, u32[]{:S(2)}) %collective-permute-start) | collective-permute-done | bytes 131104 | tf_op jit(solution)/shard_map/ppermute | solution.py:52
  12.3 1.3 %collective-permute-start.14 = (bf16[128,1024]{1,0:T(8,128)(2,1)}, bf16[128,1024]{1,0:T(8,128)(2,1)S(1)}, u32[]{:S(2)}, u32[]{:S(2)}) collective-permute-start(bf16[128,1024]{1,0:T(8,128)(2,1)} %param.11), channel_id=1, source_target_pairs={{0,1},{2,3},{4,5},{6,7},{8,9},{10,11},{12,13},{14,15},{16,17},{18,... | collective-permute-start | bytes 786440 | tf_op jit(solution)/shard_map/ppermute | solution.py:24
  13.6 1.7 %collective-permute-start.10 = (bf16[256,256]{1,0:T(8,128)(2,1)S(1)}, bf16[256,256]{1,0:T(8,128)(2,1)S(1)}, u32[]{:S(2)}, u32[]{:S(2)}) collective-permute-start(bf16[256,256]{1,0:T(8,128)(2,1)S(1)} %collective-permute-done.refs_2_.refs_0_), channel_id=1, source_target_pairs={{0,4},{1,3},{4,8},{5,1},{8,12},{9,5},{12,14},{13,9},{14,10},{15,13... | collective-permute-start | bytes 393224 | tf_op jit(solution)/shard_map/ppermute | solution.py:52
  15.7 1.4 %collective-permute-done.2.refs_8_.refs_6_ = bf16[256,256]{1,0:T(8,128)(2,1)S(1)} collective-permute-done((bf16[256,256]{1,0:T(8,128)(2,1)S(1)}, bf16[256,256]{1,0:T(8,128)(2,1)S(1)}, u32[]{:S(2)}, u32[]{:S(2)}) %collective-permute-start.2) | collective-permute-done | bytes 131104 | tf_op jit(solution)/shard_map/ppermute | solution.py:52
  17.3 1.9 %collective-permute-start.7 = (bf16[256,256]{1,0:T(8,128)(2,1)S(1)}, bf16[256,256]{1,0:T(8,128)(2,1)S(1)}, u32[]{:S(2)}, u32[]{:S(2)}) collective-permute-start(bf16[256,256]{1,0:T(8,128)(2,1)S(1)} %collective-permute-done.6.refs_7_.refs_5_), channel_id=1, source_target_pairs={{0,4},{1,3},{4,8},{5,1},{8,12},{9,5},{12,14},{13,9},{14,10},{15,13... | collective-permute-start | bytes 393224 | tf_op jit(solution)/shard_map/ppermute | solution.py:52
  21.9 1.9 %collective-permute-done.3.refs_12_.refs_10_ = bf16[256,256]{1,0:T(8,128)(2,1)S(1)} collective-permute-done((bf16[256,256]{1,0:T(8,128)(2,1)S(1)}, bf16[256,256]{1,0:T(8,128)(2,1)S(1)}, u32[]{:S(2)}, u32[]{:S(2)}) %collective-permute-start.3) | collective-permute-done | bytes 131104 | tf_op jit(solution)/shard_map/ppermute | solution.py:52
  24.0 1.9 %collective-permute-start.8 = (bf16[256,256]{1,0:T(8,128)(2,1)S(1)}, bf16[256,256]{1,0:T(8,128)(2,1)S(1)}, u32[]{:S(2)}, u32[]{:S(2)}) collective-permute-start(bf16[256,256]{1,0:T(8,128)(2,1)S(1)} %collective-permute-done.7.refs_11_.refs_9_), channel_id=1, source_target_pairs={{0,4},{1,3},{4,8},{5,1},{8,12},{9,5},{12,14},{13,9},{14,10},{15,13... | collective-permute-start | bytes 393224 | tf_op jit(solution)/shard_map/ppermute | solution.py:52
  29.7 1.3 %collective-permute-start.15 = (bf16[512,128]{1,0:T(8,128)(2,1)S(1)}, bf16[512,128]{1,0:T(8,128)(2,1)S(1)}, u32[]{:S(2)}, u32[]{:S(2)}) collective-permute-start(bf16[512,128]{1,0:T(8,128)(2,1)S(1)} %get-tuple-element.51.codes), channel_id=1, source_target_pairs={{0,1},{2,3},{4,5},{6,7},{8,9},{10,11},{12,13},{14,15},{16,17},{18,... | collective-permute-start | bytes 393224 | tf_op jit(solution)/shard_map/ppermute | solution.py:24
  33.2 1.6 %collective-permute-start.20 = (bf16[256,256]{1,0:T(8,128)(2,1)S(1)}, bf16[256,256]{1,0:T(8,128)(2,1)S(1)}, u32[]{:S(2)}, u32[]{:S(2)}) collective-permute-start(bf16[256,256]{1,0:T(8,128)(2,1)S(1)} %get-tuple-element.59), channel_id=1, source_target_pairs={{0,2},{1,5},{4,0},{5,9},{8,4},{9,13},{12,8},{13,15},{14,12},{15,11... | collective-permute-start | bytes 393224 | tf_op jit(solution)/shard_map/ppermute | solution.py:52
  35.6 1.6 %collective-permute-start.21 = (bf16[256,256]{1,0:T(8,128)(2,1)S(1)}, bf16[256,256]{1,0:T(8,128)(2,1)S(1)}, u32[]{:S(2)}, u32[]{:S(2)}) collective-permute-start(bf16[256,256]{1,0:T(8,128)(2,1)S(1)} %get-tuple-element.60), channel_id=1, source_target_pairs={{0,2},{1,5},{4,0},{5,9},{8,4},{9,13},{12,8},{13,15},{14,12},{15,11... | collective-permute-start | bytes 393224 | tf_op jit(solution)/shard_map/ppermute | solution.py:52
  38.2 3.1 %collective-permute-done.21 = bf16[256,256]{1,0:T(8,128)(2,1)S(1)} collective-permute-done((bf16[256,256]{1,0:T(8,128)(2,1)S(1)}, bf16[256,256]{1,0:T(8,128)(2,1)S(1)}, u32[]{:S(2)}, u32[]{:S(2)}) %collective-permute-start.21) | collective-permute-done | bytes 131104 | tf_op jit(solution)/shard_map/ppermute | solution.py:52
  42.2 1.6 %collective-permute-start.22 = (bf16[256,256]{1,0:T(8,128)(2,1)S(1)}, bf16[256,256]{1,0:T(8,128)(2,1)S(1)}, u32[]{:S(2)}, u32[]{:S(2)}) collective-permute-start(bf16[256,256]{1,0:T(8,128)(2,1)S(1)} %add_convert_fusion.6), channel_id=1, source_target_pairs={{0,2},{1,5},{4,0},{5,9},{8,4},{9,13},{12,8},{13,15},{14,12},{15,11... | collective-permute-start | bytes 393224 | tf_op jit(solution)/shard_map/ppermute | solution.py:52
  43.8 1.9 %collective-permute-start.23 = (bf16[256,256]{1,0:T(8,128)(2,1)S(1)}, bf16[256,256]{1,0:T(8,128)(2,1)S(1)}, u32[]{:S(2)}, u32[]{:S(2)}) collective-permute-start(bf16[256,256]{1,0:T(8,128)(2,1)S(1)} %add_convert_fusion.4), channel_id=1, source_target_pairs={{0,2},{1,5},{4,0},{5,9},{8,4},{9,13},{12,8},{13,15},{14,12},{15,11... | collective-permute-start | bytes 393224 | tf_op jit(solution)/shard_map/ppermute | solution.py:52
  47.7 2.8 %collective-permute-done.23 = bf16[256,256]{1,0:T(8,128)(2,1)S(1)} collective-permute-done((bf16[256,256]{1,0:T(8,128)(2,1)S(1)}, bf16[256,256]{1,0:T(8,128)(2,1)S(1)}, u32[]{:S(2)}, u32[]{:S(2)}) %collective-permute-start.23) | collective-permute-done | bytes 131104 | tf_op jit(solution)/shard_map/ppermute | solution.py:52
  50.8 2.2 %collective-permute-start.24 = (bf16[256,256]{1,0:T(8,128)(2,1)S(1)}, bf16[256,256]{1,0:T(8,128)(2,1)S(1)}, u32[]{:S(2)}, u32[]{:S(2)}) collective-permute-start(bf16[256,256]{1,0:T(8,128)(2,1)S(1)} %add_convert_fusion.5), channel_id=1, source_target_pairs={{0,2},{1,5},{4,0},{5,9},{8,4},{9,13},{12,8},{13,15},{14,12},{15,11... | collective-permute-start | bytes 393224 | tf_op jit(solution)/shard_map/ppermute | solution.py:52
  53.1 2.1 %collective-permute-start.28 = (bf16[256,256]{1,0:T(8,128)(2,1)S(1)}, bf16[256,256]{1,0:T(8,128)(2,1)S(1)}, u32[]{:S(2)}, u32[]{:S(2)}) collective-permute-start(bf16[256,256]{1,0:T(8,128)(2,1)S(1)} %add_convert_fusion.1), channel_id=1, source_target_pairs={{0,2},{1,5},{4,0},{5,9},{8,4},{9,13},{12,8},{13,15},{14,12},{15,11... | collective-permute-start | bytes 393224 | tf_op jit(solution)/shard_map/ppermute | solution.py:52
  55.2 3.7 %collective-permute-done.28 = bf16[256,256]{1,0:T(8,128)(2,1)S(1)} collective-permute-done((bf16[256,256]{1,0:T(8,128)(2,1)S(1)}, bf16[256,256]{1,0:T(8,128)(2,1)S(1)}, u32[]{:S(2)}, u32[]{:S(2)}) %collective-permute-start.28) | collective-permute-done | bytes 131104 | tf_op jit(solution)/shard_map/ppermute | solution.py:52
  61.2 2.9 %collective-permute-done.29 = bf16[256,256]{1,0:T(8,128)(2,1)S(1)} collective-permute-done((bf16[256,256]{1,0:T(8,128)(2,1)S(1)}, bf16[256,256]{1,0:T(8,128)(2,1)S(1)}, u32[]{:S(2)}, u32[]{:S(2)}) %collective-permute-start.29) | collective-permute-done | bytes 131104 | tf_op jit(solution)/shard_map/ppermute | solution.py:52
  64.1 2.7 %collective-permute-start.30 = (bf16[256,256]{1,0:T(8,128)(2,1)S(1)}, bf16[256,256]{1,0:T(8,128)(2,1)S(1)}, u32[]{:S(2)}, u32[]{:S(2)}) collective-permute-start(bf16[256,256]{1,0:T(8,128)(2,1)S(1)} %fusion.1.refs_0_), channel_id=1, source_target_pairs={{0,2},{1,5},{4,0},{5,9},{8,4},{9,13},{12,8},{13,15},{14,12},{15,11... | collective-permute-start | bytes 393224 | tf_op jit(solution)/shard_map/ppermute | solution.py:52
  68.0 1.5 %collective-permute-start.41 = (bf16[256,256]{1,0:T(8,128)(2,1)S(1)}, bf16[256,256]{1,0:T(8,128)(2,1)S(1)}, u32[]{:S(2)}, u32[]{:S(2)}) collective-permute-start(bf16[256,256]{1,0:T(8,128)(2,1)S(1)} %multiply_convert_fusion.refs_1_), channel_id=1, source_target_pairs={{0,2},{1,5},{4,0},{5,9},{8,4},{9,13},{12,8},{13,15},{14,12},{15,11... | collective-permute-start | bytes 393224 | tf_op jit(solution)/shard_map/ppermute | solution.py:52
  70.1 3.0 %collective-permute-start.31 = (bf16[256,256]{1,0:T(8,128)(2,1)S(1)}, bf16[256,256]{1,0:T(8,128)(2,1)S(1)}, u32[]{:S(2)}, u32[]{:S(2)}) collective-permute-start(bf16[256,256]{1,0:T(8,128)(2,1)S(1)} %collective-permute-done.30.refs_4_), channel_id=1, source_target_pairs={{0,2},{1,5},{4,0},{5,9},{8,4},{9,13},{12,8},{13,15},{14,12},{15,11... | collective-permute-start | bytes 393224 | tf_op jit(solution)/shard_map/ppermute | solution.py:52
  75.1 3.4 %collective-permute-start.43 = (bf16[256,256]{1,0:T(8,128)(2,1)S(1)}, bf16[256,256]{1,0:T(8,128)(2,1)S(1)}, u32[]{:S(2)}, u32[]{:S(2)}) collective-permute-start(bf16[256,256]{1,0:T(8,128)(2,1)S(1)} %collective-permute-done.41.refs_5_), channel_id=1, source_target_pairs={{0,2},{1,5},{4,0},{5,9},{8,4},{9,13},{12,8},{13,15},{14,12},{15,11... | collective-permute-start | bytes 393224 | tf_op jit(solution)/shard_map/ppermute | solution.py:52
  78.5 2.0 %collective-permute-start.32 = (bf16[256,256]{1,0:T(8,128)(2,1)S(1)}, bf16[256,256]{1,0:T(8,128)(2,1)S(1)}, u32[]{:S(2)}, u32[]{:S(2)}) collective-permute-start(bf16[256,256]{1,0:T(8,128)(2,1)S(1)} %collective-permute-done.31.refs_2_), channel_id=1, source_target_pairs={{0,2},{1,5},{4,0},{5,9},{8,4},{9,13},{12,8},{13,15},{14,12},{15,11... | collective-permute-start | bytes 393224 | tf_op jit(solution)/shard_map/ppermute | solution.py:52
  81.4 2.3 %collective-permute-start.45 = (bf16[256,256]{1,0:T(8,128)(2,1)S(1)}, bf16[256,256]{1,0:T(8,128)(2,1)S(1)}, u32[]{:S(2)}, u32[]{:S(2)}) collective-permute-start(bf16[256,256]{1,0:T(8,128)(2,1)S(1)} %collective-permute-done.43.refs_3_), channel_id=1, source_target_pairs={{0,2},{1,5},{4,0},{5,9},{8,4},{9,13},{12,8},{13,15},{14,12},{15,11... | collective-permute-start | bytes 393224 | tf_op jit(solution)/shard_map/ppermute | solution.py:52
  86.1 3.2 %collective-permute-start.33 = (bf16[256,256]{1,0:T(8,128)(2,1)S(1)}, bf16[256,256]{1,0:T(8,128)(2,1)S(1)}, u32[]{:S(2)}, u32[]{:S(2)}) collective-permute-start(bf16[256,256]{1,0:T(8,128)(2,1)S(1)} %collective-permute-done.32.refs_6_), channel_id=1, source_target_pairs={{0,2},{4,0},{8,4},{12,8},{14,12},{10,14},{6,10},{2,6},{16,18},{20,... | collective-permute-start | bytes 393224 | tf_op jit(solution)/shard_map/ppermute | solution.py:52
  89.3 2.7 %collective-permute-start.37 = (bf16[256,256]{1,0:T(8,128)(2,1)S(1)}, bf16[256,256]{1,0:T(8,128)(2,1)S(1)}, u32[]{:S(2)}, u32[]{:S(2)}) collective-permute-start(bf16[256,256]{1,0:T(8,128)(2,1)S(1)} %collective-permute-done.36.refs_5_), channel_id=1, source_target_pairs={{0,4},{4,8},{8,12},{12,14},{14,10},{10,6},{6,2},{2,0},{16,20},{20,... | collective-permute-start | bytes 393224 | tf_op jit(solution)/shard_map/ppermute | solution.py:52
  95.0 1.3 %collective-permute-start.46 = (bf16[1536,128]{1,0:T(8,128)(2,1)S(1)}, bf16[1536,128]{1,0:T(8,128)(2,1)S(1)}, u32[]{:S(2)}, u32[]{:S(2)}) collective-permute-start(bf16[1536,128]{1,0:T(8,128)(2,1)S(1)} %get-tuple-element.84), channel_id=1, source_target_pairs={{1,0},{3,2},{5,4},{7,6},{9,8},{11,10},{13,12},{15,14},{17,16},{19,... | collective-permute-start | bytes 1179656 | tf_op jit(solution)/shard_map/ppermute | solution.py:24
  96.3 1.6 %shard_map.102 = (f32[512,128]{1,0:T(8,128)S(1)}, f32[1,128,2048]{2,1,0:T(8,128)}) custom-call(s32[9]{0:T(128)S(1)} %stack.39.starts, bf16[256,256]{1,0:T(8,128)(2,1)S(1)} %collective-permute-done.33.refs_0_, bf16[256,256]{1,0:T(8,128)(2,1)S(1)} %collective-permute-done.37.refs_1_, bf16[256,256]{1,0:T(8,128)(2,1)S(1)} %collective-permute-done.38.refs_2_.refs_0_, ...), custom_call_target="tpu_custom_call" | custom-call | flops 5000000000 | bytes 1024 | tf_op jit(solution)/shard_map/pallas_call | solution.py:65
  98.6 2.7 %shard_map.104 = (f32[1,2048,128]{2,1,0:T(8,128)}, f32[1,128]{1,0:T(1,128)}, f32[128,1024]{1,0:T(8,128)}) custom-call(s32[9]{0:T(128)S(1)} %stack.39.starts, bf16[2048,512]{1,0:T(8,128)(2,1)S(1)} %shard_map.99.turned, f32[512,128]{1,0:T(8,128)S(1)} %get-tuple-element.66.preact, f32[512,128]{1,0:T(8,128)S(1)} %get-tuple-element.83.back_own, ...), custom_call_target="tpu_custom_call" | custom-call | flops 268435456 | bytes 1024 | tf_op jit(solution)/shard_map/pallas_call | solution.py:65
  (96 shorter events, 30.7 us)
Async XLA Ops:
  1.7 6.9 %collective-permute-start.1 = (bf16[256,256]{1,0:T(8,128)(2,1)S(1)}, bf16[256,256]{1,0:T(8,128)(2,1)S(1)}, u32[]{:S(2)}, u32[]{:S(2)}) collective-permute-start(bf16[256,256]{1,0:T(8,128)(2,1)S(1)} %get-tuple-element.47.shard.refs_0_), channel_id=1, source_target_pairs={{0,2},{1,5},{4,0},{5,9},{8,4},{9,13},{12,8},{13,15},{14,12},{15,11... | collective-permute-start | bytes 393224 | tf_op jit(solution)/shard_map/ppermute | solution.py:52
  5.6 6.7 %collective-permute-start = (bf16[256,256]{1,0:T(8,128)(2,1)S(1)}, bf16[256,256]{1,0:T(8,128)(2,1)S(1)}, u32[]{:S(2)}, u32[]{:S(2)}) collective-permute-start(bf16[256,256]{1,0:T(8,128)(2,1)S(1)} %get-tuple-element.47.shard.refs_0_), channel_id=1, source_target_pairs={{0,4},{1,3},{4,8},{5,1},{8,12},{9,5},{12,14},{13,9},{14,10},{15,13... | collective-permute-start | bytes 393224 | tf_op jit(solution)/shard_map/ppermute | solution.py:52
  8.2 7.1 %collective-permute-start.9 = (bf16[256,256]{1,0:T(8,128)(2,1)S(1)}, bf16[256,256]{1,0:T(8,128)(2,1)S(1)}, u32[]{:S(2)}, u32[]{:S(2)}) collective-permute-start(bf16[256,256]{1,0:T(8,128)(2,1)S(1)} %get-tuple-element.48.shard.refs_1_), channel_id=1, source_target_pairs={{0,2},{1,5},{4,0},{5,9},{8,4},{9,13},{12,8},{13,15},{14,12},{15,11... | collective-permute-start | bytes 393224 | tf_op jit(solution)/shard_map/ppermute | solution.py:52
  8.6 8.6 %collective-permute-start.2 = (bf16[256,256]{1,0:T(8,128)(2,1)S(1)}, bf16[256,256]{1,0:T(8,128)(2,1)S(1)}, u32[]{:S(2)}, u32[]{:S(2)}) collective-permute-start(bf16[256,256]{1,0:T(8,128)(2,1)S(1)} %collective-permute-done.1.refs_4_.refs_2_), channel_id=1, source_target_pairs={{0,2},{1,5},{4,0},{5,9},{8,4},{9,13},{12,8},{13,15},{14,12},{15,11... | collective-permute-start | bytes 393224 | tf_op jit(solution)/shard_map/ppermute | solution.py:52
  10.7 6.6 %collective-permute-start.6 = (bf16[256,256]{1,0:T(8,128)(2,1)S(1)}, bf16[256,256]{1,0:T(8,128)(2,1)S(1)}, u32[]{:S(2)}, u32[]{:S(2)}) collective-permute-start(bf16[256,256]{1,0:T(8,128)(2,1)S(1)} %collective-permute-done.5.refs_3_.refs_1_), channel_id=1, source_target_pairs={{0,4},{1,3},{4,8},{5,1},{8,12},{9,5},{12,14},{13,9},{14,10},{15,13... | collective-permute-start | bytes 393224 | tf_op jit(solution)/shard_map/ppermute | solution.py:52
  12.3 13.6 %collective-permute-start.14 = (bf16[128,1024]{1,0:T(8,128)(2,1)}, bf16[128,1024]{1,0:T(8,128)(2,1)S(1)}, u32[]{:S(2)}, u32[]{:S(2)}) collective-permute-start(bf16[128,1024]{1,0:T(8,128)(2,1)} %param.11), channel_id=1, source_target_pairs={{0,1},{2,3},{4,5},{6,7},{8,9},{10,11},{12,13},{14,15},{16,17},{18,... | collective-permute-start | bytes 786440 | tf_op jit(solution)/shard_map/ppermute | solution.py:24
  13.6 6.2 %collective-permute-start.10 = (bf16[256,256]{1,0:T(8,128)(2,1)S(1)}, bf16[256,256]{1,0:T(8,128)(2,1)S(1)}, u32[]{:S(2)}, u32[]{:S(2)}) collective-permute-start(bf16[256,256]{1,0:T(8,128)(2,1)S(1)} %collective-permute-done.refs_2_.refs_0_), channel_id=1, source_target_pairs={{0,4},{1,3},{4,8},{5,1},{8,12},{9,5},{12,14},{13,9},{14,10},{15,13... | collective-permute-start | bytes 393224 | tf_op jit(solution)/shard_map/ppermute | solution.py:52
  17.1 6.7 %collective-permute-start.3 = (bf16[256,256]{1,0:T(8,128)(2,1)S(1)}, bf16[256,256]{1,0:T(8,128)(2,1)S(1)}, u32[]{:S(2)}, u32[]{:S(2)}) collective-permute-start(bf16[256,256]{1,0:T(8,128)(2,1)S(1)} %collective-permute-done.2.refs_8_.refs_6_), channel_id=1, source_target_pairs={{0,2},{1,5},{4,0},{5,9},{8,4},{9,13},{12,8},{13,15},{14,12},{15,11... | collective-permute-start | bytes 393224 | tf_op jit(solution)/shard_map/ppermute | solution.py:52
  17.3 6.7 %collective-permute-start.7 = (bf16[256,256]{1,0:T(8,128)(2,1)S(1)}, bf16[256,256]{1,0:T(8,128)(2,1)S(1)}, u32[]{:S(2)}, u32[]{:S(2)}) collective-permute-start(bf16[256,256]{1,0:T(8,128)(2,1)S(1)} %collective-permute-done.6.refs_7_.refs_5_), channel_id=1, source_target_pairs={{0,4},{1,3},{4,8},{5,1},{8,12},{9,5},{12,14},{13,9},{14,10},{15,13... | collective-permute-start | bytes 393224 | tf_op jit(solution)/shard_map/ppermute | solution.py:52
  19.8 7.3 %collective-permute-start.12 = (bf16[256,256]{1,0:T(8,128)(2,1)S(1)}, bf16[256,256]{1,0:T(8,128)(2,1)S(1)}, u32[]{:S(2)}, u32[]{:S(2)}) collective-permute-start(bf16[256,256]{1,0:T(8,128)(2,1)S(1)} %collective-permute-done.10.refs_6_.refs_4_), channel_id=1, source_target_pairs={{0,4},{1,3},{4,8},{5,1},{8,12},{9,5},{12,14},{13,9},{14,10},{15,13... | collective-permute-start | bytes 393224 | tf_op jit(solution)/shard_map/ppermute | solution.py:52
  21.0 6.1 %collective-permute-start.13 = (bf16[256,256]{1,0:T(8,128)(2,1)S(1)}, bf16[256,256]{1,0:T(8,128)(2,1)S(1)}, u32[]{:S(2)}, u32[]{:S(2)}) collective-permute-start(bf16[256,256]{1,0:T(8,128)(2,1)S(1)} %collective-permute-done.11.refs_9_.refs_7_), channel_id=1, source_target_pairs={{0,2},{1,5},{4,0},{5,9},{8,4},{9,13},{12,8},{13,15},{14,12},{15,11... | collective-permute-start | bytes 393224 | tf_op jit(solution)/shard_map/ppermute | solution.py:52
  37.7 8.3 %collective-permute-start.25 = (bf16[256,256]{1,0:T(8,128)(2,1)S(1)}, bf16[256,256]{1,0:T(8,128)(2,1)S(1)}, u32[]{:S(2)}, u32[]{:S(2)}) collective-permute-start(bf16[256,256]{1,0:T(8,128)(2,1)S(1)} %get-tuple-element.70), channel_id=1, source_target_pairs={{0,4},{1,3},{4,8},{5,1},{8,12},{9,5},{12,14},{13,9},{14,10},{15,13... | collective-permute-start | bytes 393224 | tf_op jit(solution)/shard_map/ppermute | solution.py:52
  43.8 6.7 %collective-permute-start.23 = (bf16[256,256]{1,0:T(8,128)(2,1)S(1)}, bf16[256,256]{1,0:T(8,128)(2,1)S(1)}, u32[]{:S(2)}, u32[]{:S(2)}) collective-permute-start(bf16[256,256]{1,0:T(8,128)(2,1)S(1)} %add_convert_fusion.4), channel_id=1, source_target_pairs={{0,2},{1,5},{4,0},{5,9},{8,4},{9,13},{12,8},{13,15},{14,12},{15,11... | collective-permute-start | bytes 393224 | tf_op jit(solution)/shard_map/ppermute | solution.py:52
  46.0 9.1 %collective-permute-start.26 = (bf16[256,256]{1,0:T(8,128)(2,1)S(1)}, bf16[256,256]{1,0:T(8,128)(2,1)S(1)}, u32[]{:S(2)}, u32[]{:S(2)}) collective-permute-start(bf16[256,256]{1,0:T(8,128)(2,1)S(1)} %add_convert_fusion.3), channel_id=1, source_target_pairs={{0,4},{1,3},{4,8},{5,1},{8,12},{9,5},{12,14},{13,9},{14,10},{15,13... | collective-permute-start | bytes 393224 | tf_op jit(solution)/shard_map/ppermute | solution.py:52
  50.8 16.0 %collective-permute-start.24 = (bf16[256,256]{1,0:T(8,128)(2,1)S(1)}, bf16[256,256]{1,0:T(8,128)(2,1)S(1)}, u32[]{:S(2)}, u32[]{:S(2)}) collective-permute-start(bf16[256,256]{1,0:T(8,128)(2,1)S(1)} %add_convert_fusion.5), channel_id=1, source_target_pairs={{0,2},{1,5},{4,0},{5,9},{8,4},{9,13},{12,8},{13,15},{14,12},{15,11... | collective-permute-start | bytes 393224 | tf_op jit(solution)/shard_map/ppermute | solution.py:52
  53.0 7.3 %collective-permute-start.18 = (bf16[256,256]{1,0:T(8,128)(2,1)S(1)}, bf16[256,256]{1,0:T(8,128)(2,1)S(1)}, u32[]{:S(2)}, u32[]{:S(2)}) collective-permute-start(bf16[256,256]{1,0:T(8,128)(2,1)S(1)} %add_convert_fusion.8), channel_id=1, source_target_pairs={{0,4},{1,3},{4,8},{5,1},{8,12},{9,5},{12,14},{13,9},{14,10},{15,13... | collective-permute-start | bytes 393224 | tf_op jit(solution)/shard_map/ppermute | solution.py:52
  55.2 6.0 %collective-permute-start.27 = (bf16[256,256]{1,0:T(8,128)(2,1)S(1)}, bf16[256,256]{1,0:T(8,128)(2,1)S(1)}, u32[]{:S(2)}, u32[]{:S(2)}) collective-permute-start(bf16[256,256]{1,0:T(8,128)(2,1)S(1)} %add_convert_fusion.2), channel_id=1, source_target_pairs={{0,4},{1,3},{4,8},{5,1},{8,12},{9,5},{12,14},{13,9},{14,10},{15,13... | collective-permute-start | bytes 393224 | tf_op jit(solution)/shard_map/ppermute | solution.py:52
  60.3 6.5 %collective-permute-start.19 = (bf16[256,256]{1,0:T(8,128)(2,1)S(1)}, bf16[256,256]{1,0:T(8,128)(2,1)S(1)}, u32[]{:S(2)}, u32[]{:S(2)}) collective-permute-start(bf16[256,256]{1,0:T(8,128)(2,1)S(1)} %add_convert_fusion.7), channel_id=1, source_target_pairs={{0,4},{1,3},{4,8},{5,1},{8,12},{9,5},{12,14},{13,9},{14,10},{15,13... | collective-permute-start | bytes 393224 | tf_op jit(solution)/shard_map/ppermute | solution.py:52
  64.1 6.1 %collective-permute-start.30 = (bf16[256,256]{1,0:T(8,128)(2,1)S(1)}, bf16[256,256]{1,0:T(8,128)(2,1)S(1)}, u32[]{:S(2)}, u32[]{:S(2)}) collective-permute-start(bf16[256,256]{1,0:T(8,128)(2,1)S(1)} %fusion.1.refs_0_), channel_id=1, source_target_pairs={{0,2},{1,5},{4,0},{5,9},{8,4},{9,13},{12,8},{13,15},{14,12},{15,11... | collective-permute-start | bytes 393224 | tf_op jit(solution)/shard_map/ppermute | solution.py:52
  66.9 6.3 %collective-permute-start.34 = (bf16[256,256]{1,0:T(8,128)(2,1)S(1)}, bf16[256,256]{1,0:T(8,128)(2,1)S(1)}, u32[]{:S(2)}, u32[]{:S(2)}) collective-permute-start(bf16[256,256]{1,0:T(8,128)(2,1)S(1)} %multiply_convert_fusion.refs_1_), channel_id=1, source_target_pairs={{0,4},{1,3},{4,8},{5,1},{8,12},{9,5},{12,14},{13,9},{14,10},{15,13... | collective-permute-start | bytes 393224 | tf_op jit(solution)/shard_map/ppermute | solution.py:52
  67.2 7.8 %collective-permute-start.40 = (bf16[256,256]{1,0:T(8,128)(2,1)S(1)}, bf16[256,256]{1,0:T(8,128)(2,1)S(1)}, u32[]{:S(2)}, u32[]{:S(2)}) collective-permute-start(bf16[256,256]{1,0:T(8,128)(2,1)S(1)} %fusion.1.refs_0_), channel_id=1, source_target_pairs={{0,4},{1,3},{4,8},{5,1},{8,12},{9,5},{12,14},{13,9},{14,10},{15,13... | collective-permute-start | bytes 393224 | tf_op jit(solution)/shard_map/ppermute | solution.py:52
  68.0 7.1 %collective-permute-start.41 = (bf16[256,256]{1,0:T(8,128)(2,1)S(1)}, bf16[256,256]{1,0:T(8,128)(2,1)S(1)}, u32[]{:S(2)}, u32[]{:S(2)}) collective-permute-start(bf16[256,256]{1,0:T(8,128)(2,1)S(1)} %multiply_convert_fusion.refs_1_), channel_id=1, source_target_pairs={{0,2},{1,5},{4,0},{5,9},{8,4},{9,13},{12,8},{13,15},{14,12},{15,11... | collective-permute-start | bytes 393224 | tf_op jit(solution)/shard_map/ppermute | solution.py:52
  70.1 8.3 %collective-permute-start.31 = (bf16[256,256]{1,0:T(8,128)(2,1)S(1)}, bf16[256,256]{1,0:T(8,128)(2,1)S(1)}, u32[]{:S(2)}, u32[]{:S(2)}) collective-permute-start(bf16[256,256]{1,0:T(8,128)(2,1)S(1)} %collective-permute-done.30.refs_4_), channel_id=1, source_target_pairs={{0,2},{1,5},{4,0},{5,9},{8,4},{9,13},{12,8},{13,15},{14,12},{15,11... | collective-permute-start | bytes 393224 | tf_op jit(solution)/shard_map/ppermute | solution.py:52
  73.1 7.4 %collective-permute-start.35 = (bf16[256,256]{1,0:T(8,128)(2,1)S(1)}, bf16[256,256]{1,0:T(8,128)(2,1)S(1)}, u32[]{:S(2)}, u32[]{:S(2)}) collective-permute-start(bf16[256,256]{1,0:T(8,128)(2,1)S(1)} %collective-permute-done.34.refs_3_), channel_id=1, source_target_pairs={{0,4},{1,3},{4,8},{5,1},{8,12},{9,5},{12,14},{13,9},{14,10},{15,13... | collective-permute-start | bytes 393224 | tf_op jit(solution)/shard_map/ppermute | solution.py:52
  75.0 6.4 %collective-permute-start.42 = (bf16[256,256]{1,0:T(8,128)(2,1)S(1)}, bf16[256,256]{1,0:T(8,128)(2,1)S(1)}, u32[]{:S(2)}, u32[]{:S(2)}) collective-permute-start(bf16[256,256]{1,0:T(8,128)(2,1)S(1)} %collective-permute-done.40.refs_2_), channel_id=1, source_target_pairs={{0,4},{1,3},{4,8},{5,1},{8,12},{9,5},{12,14},{13,9},{14,10},{15,13... | collective-permute-start | bytes 393224 | tf_op jit(solution)/shard_map/ppermute | solution.py:52
  75.1 6.4 %collective-permute-start.43 = (bf16[256,256]{1,0:T(8,128)(2,1)S(1)}, bf16[256,256]{1,0:T(8,128)(2,1)S(1)}, u32[]{:S(2)}, u32[]{:S(2)}) collective-permute-start(bf16[256,256]{1,0:T(8,128)(2,1)S(1)} %collective-permute-done.41.refs_5_), channel_id=1, source_target_pairs={{0,2},{1,5},{4,0},{5,9},{8,4},{9,13},{12,8},{13,15},{14,12},{15,11... | collective-permute-start | bytes 393224 | tf_op jit(solution)/shard_map/ppermute | solution.py:52
  81.4 7.9 %collective-permute-start.44 = (bf16[256,256]{1,0:T(8,128)(2,1)S(1)}, bf16[256,256]{1,0:T(8,128)(2,1)S(1)}, u32[]{:S(2)}, u32[]{:S(2)}) collective-permute-start(bf16[256,256]{1,0:T(8,128)(2,1)S(1)} %collective-permute-done.42.refs_0_), channel_id=1, source_target_pairs={{0,4},{1,3},{4,8},{5,1},{8,12},{9,5},{12,14},{13,9},{14,10},{15,13... | collective-permute-start | bytes 393224 | tf_op jit(solution)/shard_map/ppermute | solution.py:52
  81.4 11.7 %collective-permute-start.45 = (bf16[256,256]{1,0:T(8,128)(2,1)S(1)}, bf16[256,256]{1,0:T(8,128)(2,1)S(1)}, u32[]{:S(2)}, u32[]{:S(2)}) collective-permute-start(bf16[256,256]{1,0:T(8,128)(2,1)S(1)} %collective-permute-done.43.refs_3_), channel_id=1, source_target_pairs={{0,2},{1,5},{4,0},{5,9},{8,4},{9,13},{12,8},{13,15},{14,12},{15,11... | collective-permute-start | bytes 393224 | tf_op jit(solution)/shard_map/ppermute | solution.py:52
  83.9 10.6 %collective-permute-start.38 = (bf16[256,256]{1,0:T(8,128)(2,1)S(1)}, bf16[256,256]{1,0:T(8,128)(2,1)S(1)}, u32[]{:S(2)}, u32[]{:S(2)}) collective-permute-start(bf16[256,256]{1,0:T(8,128)(2,1)S(1)} %collective-permute-done.32.refs_6_), channel_id=1, source_target_pairs={{1,5},{5,9},{9,13},{13,15},{15,11},{11,7},{7,3},{3,1},{17,21},{21,... | collective-permute-start | bytes 393224 | tf_op jit(solution)/shard_map/ppermute | solution.py:52
  85.5 9.0 %collective-permute-start.39 = (bf16[256,256]{1,0:T(8,128)(2,1)S(1)}, bf16[256,256]{1,0:T(8,128)(2,1)S(1)}, u32[]{:S(2)}, u32[]{:S(2)}) collective-permute-start(bf16[256,256]{1,0:T(8,128)(2,1)S(1)} %collective-permute-done.36.refs_5_), channel_id=1, source_target_pairs={{1,3},{5,1},{9,5},{13,9},{15,13},{11,15},{7,11},{3,7},{17,19},{21,... | collective-permute-start | bytes 393224 | tf_op jit(solution)/shard_map/ppermute | solution.py:52
  86.1 10.2 %collective-permute-start.33 = (bf16[256,256]{1,0:T(8,128)(2,1)S(1)}, bf16[256,256]{1,0:T(8,128)(2,1)S(1)}, u32[]{:S(2)}, u32[]{:S(2)}) collective-permute-start(bf16[256,256]{1,0:T(8,128)(2,1)S(1)} %collective-permute-done.32.refs_6_), channel_id=1, source_target_pairs={{0,2},{4,0},{8,4},{12,8},{14,12},{10,14},{6,10},{2,6},{16,18},{20,... | collective-permute-start | bytes 393224 | tf_op jit(solution)/shard_map/ppermute | solution.py:52
  89.3 7.0 %collective-permute-start.37 = (bf16[256,256]{1,0:T(8,128)(2,1)S(1)}, bf16[256,256]{1,0:T(8,128)(2,1)S(1)}, u32[]{:S(2)}, u32[]{:S(2)}) collective-permute-start(bf16[256,256]{1,0:T(8,128)(2,1)S(1)} %collective-permute-done.36.refs_5_), channel_id=1, source_target_pairs={{0,4},{4,8},{8,12},{12,14},{14,10},{10,6},{6,2},{2,0},{16,20},{20,... | collective-permute-start | bytes 393224 | tf_op jit(solution)/shard_map/ppermute | solution.py:52
  (18 other events, 135.6 us)

commit v18 on v16

--- a/solution.py
+++ b/solution.py
@@ -312,7 +312,11 @@
 
     rest = tuple(slot for slot in range(size) if slot != far)
     instant = tuple({far: BF16, (slot_q if way == 1 else slot_p).get(reach - 1): BF16} for _, way in later)
-    far_0, far_1 = spread((far,), instant, False)
+    block = lax.dynamic_slice_in_dim(stacked, starts[far], wide, 1)
+    far_0, far_1 = [
+        [(matmul(now, block[:lat]) + matmul(before, block[lat:])).astype(BF16)]
+        for now, before in zip(halves(codes), halves(earlier))
+    ]
     moving = {loop: hop(message, loop[1]) for loop, message in zip(urgent, (far_0[0], far_1[0]))}
     partial, both_t = [], []
     for pieces in spread(rest, instant, True):

time: 89.3 us -> 89.3 us (level)
  waiting for transfers between devices: 24.7 us -> 23.7 us
  starting transfers between devices: 47.2 us -> 48.1 us
    ppermute x42, starting transfers between devices: 43.3 us -> 44.3 us  [hop(): return lax.ppermute(shard, ('latent', 'layer'), pairs)]
    ppermute x42, waiting for transfers between devices: 23 us -> 22.1 us  [hop(): return lax.ppermute(shard, ('latent', 'layer'), pairs)]
    pallas_call x12 -> x11, Pallas kernels: 13.5 us -> 12.7 us  [call(): pl.pallas_call(kernel, out_shape=outs, in_specs=[spec(pltpu.SMEM)] + [spe...]
  transfers between devices with their start and end apart: 45 -> 45, of which waited for: 30 -> 28; matrix products, arithmetic and copies ran while one was open for 2% -> 2% of each run, Pallas kernels for 10% -> 10%
where the time goes in v18:
time: 89.3 us; the launch traced here: 89 us
  starting transfers between devices  48.1 us (54%)
  waiting for transfers between devices  23.7 us (27%)
  Pallas kernels  12.7 us (14%)
  other arithmetic  1.63 us (2%)
  local copies, waits for them, and re-layouts  1.15 us (1%)
  between operations  0.96 us (1%)
    ppermute x42, starting transfers between devices, hop(): return lax.ppermute(shard, ('latent', 'layer'), pairs)  44.3 us
    ppermute x42, waiting for transfers between devices, hop(): return lax.ppermute(shard, ('latent', 'layer'), pairs)  22.1 us
    pallas_call x11, Pallas kernels, call(): pl.pallas_call(kernel, out_shape=outs, in_specs=[spec(pltpu.SMEM)] + [spe...  12.7 us
    ppermute x3, starting transfers between devices, passed_along(): return lax.ppermute(shard, axis, pairs)  3.89 us
  transfers between devices with their start and end apart: 45, of which 28 were waited for; matrix products, arithmetic and copies ran while one was open for 2% of the time, Pallas kernels for 10%

profile of v18, /device:TPU:0, one launch (start us, length us, event | category | flops | bytes accessed | tf_op | source)
XLA Modules:
  0.0 89.0 jit_solution(4887157022186916666)
XLA Ops:
  1.7 3.1 %collective-permute-start.5 = (bf16[256,256]{1,0:T(8,128)(2,1)S(1)}, bf16[256,256]{1,0:T(8,128)(2,1)S(1)}, u32[]{:S(2)}, u32[]{:S(2)}) collective-permute-start(bf16[256,256]{1,0:T(8,128)(2,1)S(1)} %get-tuple-element.46.shard.refs_1_), channel_id=1, source_target_pairs={{0,4},{1,3},{4,8},{5,1},{8,12},{9,5},{12,14},{13,9},{14,10},{15,13... | collective-permute-start | bytes 393224 | tf_op jit(solution)/shard_map/ppermute | solution.py:51
  5.5 2.1 %collective-permute-start = (bf16[256,256]{1,0:T(8,128)(2,1)S(1)}, bf16[256,256]{1,0:T(8,128)(2,1)S(1)}, u32[]{:S(2)}, u32[]{:S(2)}) collective-permute-start(bf16[256,256]{1,0:T(8,128)(2,1)S(1)} %get-tuple-element.45.shard.refs_0_), channel_id=1, source_target_pairs={{0,4},{1,3},{4,8},{5,1},{8,12},{9,5},{12,14},{13,9},{14,10},{15,13... | collective-permute-start | bytes 393224 | tf_op jit(solution)/shard_map/ppermute | solution.py:51
  8.5 1.8 %collective-permute-start.6 = (bf16[256,256]{1,0:T(8,128)(2,1)S(1)}, bf16[256,256]{1,0:T(8,128)(2,1)S(1)}, u32[]{:S(2)}, u32[]{:S(2)}) collective-permute-start(bf16[256,256]{1,0:T(8,128)(2,1)S(1)} %collective-permute-done.5.refs_3_.refs_1_), channel_id=1, source_target_pairs={{0,4},{1,3},{4,8},{5,1},{8,12},{9,5},{12,14},{13,9},{14,10},{15,13... | collective-permute-start | bytes 393224 | tf_op jit(solution)/shard_map/ppermute | solution.py:51
  11.5 1.3 %collective-permute-start.14 = (bf16[128,1024]{1,0:T(8,128)(2,1)}, bf16[128,1024]{1,0:T(8,128)(2,1)S(1)}, u32[]{:S(2)}, u32[]{:S(2)}) collective-permute-start(bf16[128,1024]{1,0:T(8,128)(2,1)} %param.11), channel_id=1, source_target_pairs={{0,1},{2,3},{4,5},{6,7},{8,9},{10,11},{12,13},{14,15},{16,17},{18,... | collective-permute-start | bytes 786440 | tf_op jit(solution)/shard_map/ppermute | solution.py:23
  12.8 2.5 %collective-permute-start.10 = (bf16[256,256]{1,0:T(8,128)(2,1)S(1)}, bf16[256,256]{1,0:T(8,128)(2,1)S(1)}, u32[]{:S(2)}, u32[]{:S(2)}) collective-permute-start(bf16[256,256]{1,0:T(8,128)(2,1)S(1)} %collective-permute-done.refs_2_.refs_0_), channel_id=1, source_target_pairs={{0,4},{1,3},{4,8},{5,1},{8,12},{9,5},{12,14},{13,9},{14,10},{15,13... | collective-permute-start | bytes 393224 | tf_op jit(solution)/shard_map/ppermute | solution.py:51
  15.3 2.0 %collective-permute-start.7 = (bf16[256,256]{1,0:T(8,128)(2,1)S(1)}, bf16[256,256]{1,0:T(8,128)(2,1)S(1)}, u32[]{:S(2)}, u32[]{:S(2)}) collective-permute-start(bf16[256,256]{1,0:T(8,128)(2,1)S(1)} %collective-permute-done.6.refs_7_.refs_5_), channel_id=1, source_target_pairs={{0,4},{1,3},{4,8},{5,1},{8,12},{9,5},{12,14},{13,9},{14,10},{15,13... | collective-permute-start | bytes 393224 | tf_op jit(solution)/shard_map/ppermute | solution.py:51
  17.4 1.5 %collective-permute-done.10.refs_6_.refs_4_ = bf16[256,256]{1,0:T(8,128)(2,1)S(1)} collective-permute-done((bf16[256,256]{1,0:T(8,128)(2,1)S(1)}, bf16[256,256]{1,0:T(8,128)(2,1)S(1)}, u32[]{:S(2)}, u32[]{:S(2)}) %collective-permute-start.10) | collective-permute-done | bytes 131104 | tf_op jit(solution)/shard_map/ppermute | solution.py:51
  18.9 1.4 %collective-permute-start.12 = (bf16[256,256]{1,0:T(8,128)(2,1)S(1)}, bf16[256,256]{1,0:T(8,128)(2,1)S(1)}, u32[]{:S(2)}, u32[]{:S(2)}) collective-permute-start(bf16[256,256]{1,0:T(8,128)(2,1)S(1)} %collective-permute-done.10.refs_6_.refs_4_), channel_id=1, source_target_pairs={{0,4},{1,3},{4,8},{5,1},{8,12},{9,5},{12,14},{13,9},{14,10},{15,13... | collective-permute-start | bytes 393224 | tf_op jit(solution)/shard_map/ppermute | solution.py:51
  21.8 1.8 %collective-permute-start.8 = (bf16[256,256]{1,0:T(8,128)(2,1)S(1)}, bf16[256,256]{1,0:T(8,128)(2,1)S(1)}, u32[]{:S(2)}, u32[]{:S(2)}) collective-permute-start(bf16[256,256]{1,0:T(8,128)(2,1)S(1)} %collective-permute-done.7.refs_11_.refs_9_), channel_id=1, source_target_pairs={{0,4},{1,3},{4,8},{5,1},{8,12},{9,5},{12,14},{13,9},{14,10},{15,13... | collective-permute-start | bytes 393224 | tf_op jit(solution)/shard_map/ppermute | solution.py:51
  24.1 1.2 %maximum_maximum_fusion.stacked.refs_2_.refs_12_ = bf16[256,2048]{1,0:T(8,128)(2,1)S(1)} fusion(bf16[128,1024]{1,0:T(8,128)(2,1)} %param.11, bf16[128,1024]{1,0:T(8,128)(2,1)S(1)} %collective-permute-done.14, bf16[128,2048]{1,0:T(8,128)(2,1)} %bitcast.19), kind=kLoop, calls=%fused_computation.4 | loop fusion | flops 3145728 | bytes 2097152 | tf_op jit(solution)/shard_map/concatenate | solution.py:298
  27.5 1.6 %collective-permute-done.4.refs_0_.refs_12_ = bf16[256,256]{1,0:T(8,128)(2,1)S(1)} collective-permute-done((bf16[256,256]{1,0:T(8,128)(2,1)S(1)}, bf16[256,256]{1,0:T(8,128)(2,1)S(1)}, u32[]{:S(2)}, u32[]{:S(2)}) %collective-permute-start.4) | collective-permute-done | bytes 131104 | tf_op jit(solution)/shard_map/ppermute | solution.py:51
  29.9 1.3 %collective-permute-start.15 = (bf16[512,128]{1,0:T(8,128)(2,1)S(1)}, bf16[512,128]{1,0:T(8,128)(2,1)S(1)}, u32[]{:S(2)}, u32[]{:S(2)}) collective-permute-start(bf16[512,128]{1,0:T(8,128)(2,1)S(1)} %get-tuple-element.49.codes), channel_id=1, source_target_pairs={{0,1},{2,3},{4,5},{6,7},{8,9},{10,11},{12,13},{14,15},{16,17},{18,... | collective-permute-start | bytes 393224 | tf_op jit(solution)/shard_map/ppermute | solution.py:23
  32.9 2.1 %collective-permute-start.16 = (bf16[256,256]{1,0:T(8,128)(2,1)S(1)}, bf16[256,256]{1,0:T(8,128)(2,1)S(1)}, u32[]{:S(2)}, u32[]{:S(2)}) collective-permute-start(bf16[256,256]{1,0:T(8,128)(2,1)S(1)} %fusion), channel_id=1, source_target_pairs={{0,4},{1,3},{4,8},{5,1},{8,12},{9,5},{12,14},{13,9},{14,10},{15,13... | collective-permute-start | bytes 393224 | tf_op jit(solution)/shard_map/ppermute | solution.py:51
  35.0 1.2 %shard_map.97 = (f32[256,256]{1,0:T(8,128)S(1)}, f32[256,256]{1,0:T(8,128)S(1)}, f32[256,256]{1,0:T(8,128)S(1)}, f32[256,256]{1,0:T(8,128)S(1)}, f32[256,256]{1,...) custom-call(s32[9]{0:T(128)S(1)} %stack.39.starts, ...), custom_call_target="tpu_custom_call" | custom-call | flops 469762048 | bytes 1024 | tf_op jit(solution)/shard_map/pallas_call | solution.py:64
  36.3 2.0 %collective-permute-start.25 = (bf16[256,256]{1,0:T(8,128)(2,1)S(1)}, bf16[256,256]{1,0:T(8,128)(2,1)S(1)}, u32[]{:S(2)}, u32[]{:S(2)}) collective-permute-start(bf16[256,256]{1,0:T(8,128)(2,1)S(1)} %get-tuple-element.66), channel_id=1, source_target_pairs={{0,4},{1,3},{4,8},{5,1},{8,12},{9,5},{12,14},{13,9},{14,10},{15,13... | collective-permute-start | bytes 393224 | tf_op jit(solution)/shard_map/ppermute | solution.py:51
  38.5 2.0 %collective-permute-start.17 = (bf16[256,256]{1,0:T(8,128)(2,1)S(1)}, bf16[256,256]{1,0:T(8,128)(2,1)S(1)}, u32[]{:S(2)}, u32[]{:S(2)}) collective-permute-start(bf16[256,256]{1,0:T(8,128)(2,1)S(1)} %add_convert_fusion.9), channel_id=1, source_target_pairs={{0,4},{1,3},{4,8},{5,1},{8,12},{9,5},{12,14},{13,9},{14,10},{15,13... | collective-permute-start | bytes 393224 | tf_op jit(solution)/shard_map/ppermute | solution.py:51
  40.5 2.1 %collective-permute-done.20 = bf16[256,256]{1,0:T(8,128)(2,1)S(1)} collective-permute-done((bf16[256,256]{1,0:T(8,128)(2,1)S(1)}, bf16[256,256]{1,0:T(8,128)(2,1)S(1)}, u32[]{:S(2)}, u32[]{:S(2)}) %collective-permute-start.20) | collective-permute-done | bytes 131104 | tf_op jit(solution)/shard_map/ppermute | solution.py:51
  42.8 2.1 %collective-permute-start.26 = (bf16[256,256]{1,0:T(8,128)(2,1)S(1)}, bf16[256,256]{1,0:T(8,128)(2,1)S(1)}, u32[]{:S(2)}, u32[]{:S(2)}) collective-permute-start(bf16[256,256]{1,0:T(8,128)(2,1)S(1)} %add_convert_fusion.3), channel_id=1, source_target_pairs={{0,4},{1,3},{4,8},{5,1},{8,12},{9,5},{12,14},{13,9},{14,10},{15,13... | collective-permute-start | bytes 393224 | tf_op jit(solution)/shard_map/ppermute | solution.py:51
  45.6 2.1 %collective-permute-start.18 = (bf16[256,256]{1,0:T(8,128)(2,1)S(1)}, bf16[256,256]{1,0:T(8,128)(2,1)S(1)}, u32[]{:S(2)}, u32[]{:S(2)}) collective-permute-start(bf16[256,256]{1,0:T(8,128)(2,1)S(1)} %add_convert_fusion.8), channel_id=1, source_target_pairs={{0,4},{1,3},{4,8},{5,1},{8,12},{9,5},{12,14},{13,9},{14,10},{15,13... | collective-permute-start | bytes 393224 | tf_op jit(solution)/shard_map/ppermute | solution.py:51
  49.1 1.3 %collective-permute-start.27 = (bf16[256,256]{1,0:T(8,128)(2,1)S(1)}, bf16[256,256]{1,0:T(8,128)(2,1)S(1)}, u32[]{:S(2)}, u32[]{:S(2)}) collective-permute-start(bf16[256,256]{1,0:T(8,128)(2,1)S(1)} %add_convert_fusion.2), channel_id=1, source_target_pairs={{0,4},{1,3},{4,8},{5,1},{8,12},{9,5},{12,14},{13,9},{14,10},{15,13... | collective-permute-start | bytes 393224 | tf_op jit(solution)/shard_map/ppermute | solution.py:51
  51.4 1.4 %collective-permute-start.19 = (bf16[256,256]{1,0:T(8,128)(2,1)S(1)}, bf16[256,256]{1,0:T(8,128)(2,1)S(1)}, u32[]{:S(2)}, u32[]{:S(2)}) collective-permute-start(bf16[256,256]{1,0:T(8,128)(2,1)S(1)} %add_convert_fusion.7), channel_id=1, source_target_pairs={{0,4},{1,3},{4,8},{5,1},{8,12},{9,5},{12,14},{13,9},{14,10},{15,13... | collective-permute-start | bytes 393224 | tf_op jit(solution)/shard_map/ppermute | solution.py:51
  54.4 2.5 %collective-permute-done.19 = bf16[256,256]{1,0:T(8,128)(2,1)S(1)} collective-permute-done((bf16[256,256]{1,0:T(8,128)(2,1)S(1)}, bf16[256,256]{1,0:T(8,128)(2,1)S(1)}, u32[]{:S(2)}, u32[]{:S(2)}) %collective-permute-start.19) | collective-permute-done | bytes 131104 | tf_op jit(solution)/shard_map/ppermute | solution.py:51
  57.0 1.3 %collective-permute-start.34 = (bf16[256,256]{1,0:T(8,128)(2,1)S(1)}, bf16[256,256]{1,0:T(8,128)(2,1)S(1)}, u32[]{:S(2)}, u32[]{:S(2)}) collective-permute-start(bf16[256,256]{1,0:T(8,128)(2,1)S(1)} %multiply_convert_fusion.refs_1_), channel_id=1, source_target_pairs={{0,4},{1,3},{4,8},{5,1},{8,12},{9,5},{12,14},{13,9},{14,10},{15,13... | collective-permute-start | bytes 393224 | tf_op jit(solution)/shard_map/ppermute | solution.py:51
  60.3 1.3 %collective-permute-start.38 = (bf16[256,256]{1,0:T(8,128)(2,1)S(1)}, bf16[256,256]{1,0:T(8,128)(2,1)S(1)}, u32[]{:S(2)}, u32[]{:S(2)}) collective-permute-start(bf16[256,256]{1,0:T(8,128)(2,1)S(1)} %fusion.3.refs_0_), channel_id=1, source_target_pairs={{0,4},{1,3},{4,8},{5,1},{8,12},{9,5},{12,14},{13,9},{14,10},{15,13... | collective-permute-start | bytes 393224 | tf_op jit(solution)/shard_map/ppermute | solution.py:51
  63.3 1.2 %collective-permute-start.35 = (bf16[256,256]{1,0:T(8,128)(2,1)S(1)}, bf16[256,256]{1,0:T(8,128)(2,1)S(1)}, u32[]{:S(2)}, u32[]{:S(2)}) collective-permute-start(bf16[256,256]{1,0:T(8,128)(2,1)S(1)} %collective-permute-done.34.refs_1_), channel_id=1, source_target_pairs={{0,4},{1,3},{4,8},{5,1},{8,12},{9,5},{12,14},{13,9},{14,10},{15,13... | collective-permute-start | bytes 393224 | tf_op jit(solution)/shard_map/ppermute | solution.py:51
  65.3 1.4 %collective-permute-done.38.refs_0_ = bf16[256,256]{1,0:T(8,128)(2,1)S(1)} collective-permute-done((bf16[256,256]{1,0:T(8,128)(2,1)S(1)}, bf16[256,256]{1,0:T(8,128)(2,1)S(1)}, u32[]{:S(2)}, u32[]{:S(2)}) %collective-permute-start.38) | collective-permute-done | bytes 131104 | tf_op jit(solution)/shard_map/ppermute | solution.py:51
  69.6 1.3 %collective-permute-start.36 = (bf16[256,256]{1,0:T(8,128)(2,1)S(1)}, bf16[256,256]{1,0:T(8,128)(2,1)S(1)}, u32[]{:S(2)}, u32[]{:S(2)}) collective-permute-start(bf16[256,256]{1,0:T(8,128)(2,1)S(1)} %collective-permute-done.35.refs_5_), channel_id=1, source_target_pairs={{0,4},{1,3},{4,8},{5,1},{8,12},{9,5},{12,14},{13,9},{14,10},{15,13... | collective-permute-start | bytes 393224 | tf_op jit(solution)/shard_map/ppermute | solution.py:51
  74.6 1.3 %collective-permute-done.36.refs_9_ = bf16[256,256]{1,0:T(8,128)(2,1)S(1)} collective-permute-done((bf16[256,256]{1,0:T(8,128)(2,1)S(1)}, bf16[256,256]{1,0:T(8,128)(2,1)S(1)}, u32[]{:S(2)}, u32[]{:S(2)}) %collective-permute-start.36) | collective-permute-done | bytes 131104 | tf_op jit(solution)/shard_map/ppermute | solution.py:51
  78.7 1.5 %shard_map.100 = (f32[6,256,256]{2,1,0:T(8,128)S(1)}, f32[2,256,256]{2,1,0:T(8,128)S(1)}) custom-call(s32[9]{0:T(128)S(1)} %stack.39.starts, bf16[256,256]{1,0:T(8,128)(2,1)S(1)} %collective-permute-done.38.refs_0_, bf16[256,256]{1,0:T(8,128)(2,1)S(1)} %collective-permute-done.34.refs_1_, bf16[256,256]{1,0:T(8,128)(2,1)S(1)} %collective-permute-done.30.refs_2_, ...), custom_call_target="tpu_custom_call" | custom-call | flops 402653184 | bytes 1024 | tf_op jit(solution)/shard_map/pallas_call | solution.py:64
  82.7 1.3 %collective-permute-start.44 = (bf16[1536,128]{1,0:T(8,128)(2,1)S(1)}, bf16[1536,128]{1,0:T(8,128)(2,1)S(1)}, u32[]{:S(2)}, u32[]{:S(2)}) collective-permute-start(bf16[1536,128]{1,0:T(8,128)(2,1)S(1)} %get-tuple-element.80), channel_id=1, source_target_pairs={{1,0},{3,2},{5,4},{7,6},{9,8},{11,10},{13,12},{15,14},{17,16},{19,... | collective-permute-start | bytes 1179656 | tf_op jit(solution)/shard_map/ppermute | solution.py:23
  84.0 1.6 %shard_map.101 = (f32[512,128]{1,0:T(8,128)S(1)}, f32[1,128,2048]{2,1,0:T(8,128)}) custom-call(s32[9]{0:T(128)S(1)} %stack.39.starts, bf16[256,256]{1,0:T(8,128)(2,1)S(1)} %collective-permute-done.33.refs_0_, bf16[256,256]{1,0:T(8,128)(2,1)S(1)} %collective-permute-done.37.refs_1_, bf16[256,2048]{1,0:T(8,128)(2,1)S(1)} %maximum_maximum_fusion.stacked.refs_2_.refs_12_, ...), custom_call_target="tpu_custom_call" | custom-call | bytes 1024 | tf_op jit(solution)/shard_map/pallas_call | solution.py:64
  86.3 2.7 %shard_map.103 = (f32[1,2048,128]{2,1,0:T(8,128)}, f32[1,128]{1,0:T(1,128)}, f32[128,1024]{1,0:T(8,128)}) custom-call(s32[9]{0:T(128)S(1)} %stack.39.starts, bf16[2048,512]{1,0:T(8,128)(2,1)S(1)} %shard_map.98.turned, f32[512,128]{1,0:T(8,128)S(1)} %get-tuple-element.62.preact, f32[512,128]{1,0:T(8,128)S(1)} %get-tuple-element.79.back_own, ...), custom_call_target="tpu_custom_call" | custom-call | flops 268435456 | bytes 1024 | tf_op jit(solution)/shard_map/pallas_call | solution.py:64
  (95 shorter events, 32.8 us)
Async XLA Ops:
  1.7 6.8 %collective-permute-start.5 = (bf16[256,256]{1,0:T(8,128)(2,1)S(1)}, bf16[256,256]{1,0:T(8,128)(2,1)S(1)}, u32[]{:S(2)}, u32[]{:S(2)}) collective-permute-start(bf16[256,256]{1,0:T(8,128)(2,1)S(1)} %get-tuple-element.46.shard.refs_1_), channel_id=1, source_target_pairs={{0,4},{1,3},{4,8},{5,1},{8,12},{9,5},{12,14},{13,9},{14,10},{15,13... | collective-permute-start | bytes 393224 | tf_op jit(solution)/shard_map/ppermute | solution.py:51
  4.8 6.3 %collective-permute-start.1 = (bf16[256,256]{1,0:T(8,128)(2,1)S(1)}, bf16[256,256]{1,0:T(8,128)(2,1)S(1)}, u32[]{:S(2)}, u32[]{:S(2)}) collective-permute-start(bf16[256,256]{1,0:T(8,128)(2,1)S(1)} %get-tuple-element.45.shard.refs_0_), channel_id=1, source_target_pairs={{0,2},{1,5},{4,0},{5,9},{8,4},{9,13},{12,8},{13,15},{14,12},{15,11... | collective-permute-start | bytes 393224 | tf_op jit(solution)/shard_map/ppermute | solution.py:51
  5.5 6.0 %collective-permute-start = (bf16[256,256]{1,0:T(8,128)(2,1)S(1)}, bf16[256,256]{1,0:T(8,128)(2,1)S(1)}, u32[]{:S(2)}, u32[]{:S(2)}) collective-permute-start(bf16[256,256]{1,0:T(8,128)(2,1)S(1)} %get-tuple-element.45.shard.refs_0_), channel_id=1, source_target_pairs={{0,4},{1,3},{4,8},{5,1},{8,12},{9,5},{12,14},{13,9},{14,10},{15,13... | collective-permute-start | bytes 393224 | tf_op jit(solution)/shard_map/ppermute | solution.py:51
  8.2 7.1 %collective-permute-start.9 = (bf16[256,256]{1,0:T(8,128)(2,1)S(1)}, bf16[256,256]{1,0:T(8,128)(2,1)S(1)}, u32[]{:S(2)}, u32[]{:S(2)}) collective-permute-start(bf16[256,256]{1,0:T(8,128)(2,1)S(1)} %get-tuple-element.46.shard.refs_1_), channel_id=1, source_target_pairs={{0,2},{1,5},{4,0},{5,9},{8,4},{9,13},{12,8},{13,15},{14,12},{15,11... | collective-permute-start | bytes 393224 | tf_op jit(solution)/shard_map/ppermute | solution.py:51
  8.5 6.8 %collective-permute-start.6 = (bf16[256,256]{1,0:T(8,128)(2,1)S(1)}, bf16[256,256]{1,0:T(8,128)(2,1)S(1)}, u32[]{:S(2)}, u32[]{:S(2)}) collective-permute-start(bf16[256,256]{1,0:T(8,128)(2,1)S(1)} %collective-permute-done.5.refs_3_.refs_1_), channel_id=1, source_target_pairs={{0,4},{1,3},{4,8},{5,1},{8,12},{9,5},{12,14},{13,9},{14,10},{15,13... | collective-permute-start | bytes 393224 | tf_op jit(solution)/shard_map/ppermute | solution.py:51
  11.1 6.3 %collective-permute-start.2 = (bf16[256,256]{1,0:T(8,128)(2,1)S(1)}, bf16[256,256]{1,0:T(8,128)(2,1)S(1)}, u32[]{:S(2)}, u32[]{:S(2)}) collective-permute-start(bf16[256,256]{1,0:T(8,128)(2,1)S(1)} %collective-permute-done.1.refs_4_.refs_2_), channel_id=1, source_target_pairs={{0,2},{1,5},{4,0},{5,9},{8,4},{9,13},{12,8},{13,15},{14,12},{15,11... | collective-permute-start | bytes 393224 | tf_op jit(solution)/shard_map/ppermute | solution.py:51
  11.5 12.7 %collective-permute-start.14 = (bf16[128,1024]{1,0:T(8,128)(2,1)}, bf16[128,1024]{1,0:T(8,128)(2,1)S(1)}, u32[]{:S(2)}, u32[]{:S(2)}) collective-permute-start(bf16[128,1024]{1,0:T(8,128)(2,1)} %param.11), channel_id=1, source_target_pairs={{0,1},{2,3},{4,5},{6,7},{8,9},{10,11},{12,13},{14,15},{16,17},{18,... | collective-permute-start | bytes 786440 | tf_op jit(solution)/shard_map/ppermute | solution.py:23
  12.8 6.2 %collective-permute-start.10 = (bf16[256,256]{1,0:T(8,128)(2,1)S(1)}, bf16[256,256]{1,0:T(8,128)(2,1)S(1)}, u32[]{:S(2)}, u32[]{:S(2)}) collective-permute-start(bf16[256,256]{1,0:T(8,128)(2,1)S(1)} %collective-permute-done.refs_2_.refs_0_), channel_id=1, source_target_pairs={{0,4},{1,3},{4,8},{5,1},{8,12},{9,5},{12,14},{13,9},{14,10},{15,13... | collective-permute-start | bytes 393224 | tf_op jit(solution)/shard_map/ppermute | solution.py:51
  15.3 6.0 %collective-permute-start.11 = (bf16[256,256]{1,0:T(8,128)(2,1)S(1)}, bf16[256,256]{1,0:T(8,128)(2,1)S(1)}, u32[]{:S(2)}, u32[]{:S(2)}) collective-permute-start(bf16[256,256]{1,0:T(8,128)(2,1)S(1)} %collective-permute-done.9.refs_5_.refs_3_), channel_id=1, source_target_pairs={{0,2},{1,5},{4,0},{5,9},{8,4},{9,13},{12,8},{13,15},{14,12},{15,11... | collective-permute-start | bytes 393224 | tf_op jit(solution)/shard_map/ppermute | solution.py:51
  15.3 6.5 %collective-permute-start.7 = (bf16[256,256]{1,0:T(8,128)(2,1)S(1)}, bf16[256,256]{1,0:T(8,128)(2,1)S(1)}, u32[]{:S(2)}, u32[]{:S(2)}) collective-permute-start(bf16[256,256]{1,0:T(8,128)(2,1)S(1)} %collective-permute-done.6.refs_7_.refs_5_), channel_id=1, source_target_pairs={{0,4},{1,3},{4,8},{5,1},{8,12},{9,5},{12,14},{13,9},{14,10},{15,13... | collective-permute-start | bytes 393224 | tf_op jit(solution)/shard_map/ppermute | solution.py:51
  17.4 6.7 %collective-permute-start.3 = (bf16[256,256]{1,0:T(8,128)(2,1)S(1)}, bf16[256,256]{1,0:T(8,128)(2,1)S(1)}, u32[]{:S(2)}, u32[]{:S(2)}) collective-permute-start(bf16[256,256]{1,0:T(8,128)(2,1)S(1)} %collective-permute-done.2.refs_8_.refs_6_), channel_id=1, source_target_pairs={{0,2},{1,5},{4,0},{5,9},{8,4},{9,13},{12,8},{13,15},{14,12},{15,11... | collective-permute-start | bytes 393224 | tf_op jit(solution)/shard_map/ppermute | solution.py:51
  18.9 6.4 %collective-permute-start.12 = (bf16[256,256]{1,0:T(8,128)(2,1)S(1)}, bf16[256,256]{1,0:T(8,128)(2,1)S(1)}, u32[]{:S(2)}, u32[]{:S(2)}) collective-permute-start(bf16[256,256]{1,0:T(8,128)(2,1)S(1)} %collective-permute-done.10.refs_6_.refs_4_), channel_id=1, source_target_pairs={{0,4},{1,3},{4,8},{5,1},{8,12},{9,5},{12,14},{13,9},{14,10},{15,13... | collective-permute-start | bytes 393224 | tf_op jit(solution)/shard_map/ppermute | solution.py:51
  21.8 5.7 %collective-permute-start.8 = (bf16[256,256]{1,0:T(8,128)(2,1)S(1)}, bf16[256,256]{1,0:T(8,128)(2,1)S(1)}, u32[]{:S(2)}, u32[]{:S(2)}) collective-permute-start(bf16[256,256]{1,0:T(8,128)(2,1)S(1)} %collective-permute-done.7.refs_11_.refs_9_), channel_id=1, source_target_pairs={{0,4},{1,3},{4,8},{5,1},{8,12},{9,5},{12,14},{13,9},{14,10},{15,13... | collective-permute-start | bytes 393224 | tf_op jit(solution)/shard_map/ppermute | solution.py:51
  32.5 5.8 %collective-permute-start.21 = (bf16[256,256]{1,0:T(8,128)(2,1)S(1)}, bf16[256,256]{1,0:T(8,128)(2,1)S(1)}, u32[]{:S(2)}, u32[]{:S(2)}) collective-permute-start(bf16[256,256]{1,0:T(8,128)(2,1)S(1)} %fusion.1), channel_id=1, source_target_pairs={{0,2},{1,5},{4,0},{5,9},{8,4},{9,13},{12,8},{13,15},{14,12},{15,11... | collective-permute-start | bytes 393224 | tf_op jit(solution)/shard_map/ppermute | solution.py:51
  36.2 6.4 %collective-permute-start.20 = (bf16[256,256]{1,0:T(8,128)(2,1)S(1)}, bf16[256,256]{1,0:T(8,128)(2,1)S(1)}, u32[]{:S(2)}, u32[]{:S(2)}) collective-permute-start(bf16[256,256]{1,0:T(8,128)(2,1)S(1)} %get-tuple-element.56), channel_id=1, source_target_pairs={{0,2},{1,5},{4,0},{5,9},{8,4},{9,13},{12,8},{13,15},{14,12},{15,11... | collective-permute-start | bytes 393224 | tf_op jit(solution)/shard_map/ppermute | solution.py:51
  36.3 6.4 %collective-permute-start.25 = (bf16[256,256]{1,0:T(8,128)(2,1)S(1)}, bf16[256,256]{1,0:T(8,128)(2,1)S(1)}, u32[]{:S(2)}, u32[]{:S(2)}) collective-permute-start(bf16[256,256]{1,0:T(8,128)(2,1)S(1)} %get-tuple-element.66), channel_id=1, source_target_pairs={{0,4},{1,3},{4,8},{5,1},{8,12},{9,5},{12,14},{13,9},{14,10},{15,13... | collective-permute-start | bytes 393224 | tf_op jit(solution)/shard_map/ppermute | solution.py:51
  38.3 7.1 %collective-permute-start.23 = (bf16[256,256]{1,0:T(8,128)(2,1)S(1)}, bf16[256,256]{1,0:T(8,128)(2,1)S(1)}, u32[]{:S(2)}, u32[]{:S(2)}) collective-permute-start(bf16[256,256]{1,0:T(8,128)(2,1)S(1)} %add_convert_fusion.4), channel_id=1, source_target_pairs={{0,2},{1,5},{4,0},{5,9},{8,4},{9,13},{12,8},{13,15},{14,12},{15,11... | collective-permute-start | bytes 393224 | tf_op jit(solution)/shard_map/ppermute | solution.py:51
  38.5 7.1 %collective-permute-start.17 = (bf16[256,256]{1,0:T(8,128)(2,1)S(1)}, bf16[256,256]{1,0:T(8,128)(2,1)S(1)}, u32[]{:S(2)}, u32[]{:S(2)}) collective-permute-start(bf16[256,256]{1,0:T(8,128)(2,1)S(1)} %add_convert_fusion.9), channel_id=1, source_target_pairs={{0,4},{1,3},{4,8},{5,1},{8,12},{9,5},{12,14},{13,9},{14,10},{15,13... | collective-permute-start | bytes 393224 | tf_op jit(solution)/shard_map/ppermute | solution.py:51
  42.8 6.3 %collective-permute-start.26 = (bf16[256,256]{1,0:T(8,128)(2,1)S(1)}, bf16[256,256]{1,0:T(8,128)(2,1)S(1)}, u32[]{:S(2)}, u32[]{:S(2)}) collective-permute-start(bf16[256,256]{1,0:T(8,128)(2,1)S(1)} %add_convert_fusion.3), channel_id=1, source_target_pairs={{0,4},{1,3},{4,8},{5,1},{8,12},{9,5},{12,14},{13,9},{14,10},{15,13... | collective-permute-start | bytes 393224 | tf_op jit(solution)/shard_map/ppermute | solution.py:51
  45.5 7.4 %collective-permute-start.28 = (bf16[256,256]{1,0:T(8,128)(2,1)S(1)}, bf16[256,256]{1,0:T(8,128)(2,1)S(1)}, u32[]{:S(2)}, u32[]{:S(2)}) collective-permute-start(bf16[256,256]{1,0:T(8,128)(2,1)S(1)} %add_convert_fusion.1), channel_id=1, source_target_pairs={{0,2},{1,5},{4,0},{5,9},{8,4},{9,13},{12,8},{13,15},{14,12},{15,11... | collective-permute-start | bytes 393224 | tf_op jit(solution)/shard_map/ppermute | solution.py:51
  45.6 5.8 %collective-permute-start.18 = (bf16[256,256]{1,0:T(8,128)(2,1)S(1)}, bf16[256,256]{1,0:T(8,128)(2,1)S(1)}, u32[]{:S(2)}, u32[]{:S(2)}) collective-permute-start(bf16[256,256]{1,0:T(8,128)(2,1)S(1)} %add_convert_fusion.8), channel_id=1, source_target_pairs={{0,4},{1,3},{4,8},{5,1},{8,12},{9,5},{12,14},{13,9},{14,10},{15,13... | collective-permute-start | bytes 393224 | tf_op jit(solution)/shard_map/ppermute | solution.py:51
  48.2 6.2 %collective-permute-start.24 = (bf16[256,256]{1,0:T(8,128)(2,1)S(1)}, bf16[256,256]{1,0:T(8,128)(2,1)S(1)}, u32[]{:S(2)}, u32[]{:S(2)}) collective-permute-start(bf16[256,256]{1,0:T(8,128)(2,1)S(1)} %add_convert_fusion.5), channel_id=1, source_target_pairs={{0,2},{1,5},{4,0},{5,9},{8,4},{9,13},{12,8},{13,15},{14,12},{15,11... | collective-permute-start | bytes 393224 | tf_op jit(solution)/shard_map/ppermute | solution.py:51
  49.1 9.2 %collective-permute-start.27 = (bf16[256,256]{1,0:T(8,128)(2,1)S(1)}, bf16[256,256]{1,0:T(8,128)(2,1)S(1)}, u32[]{:S(2)}, u32[]{:S(2)}) collective-permute-start(bf16[256,256]{1,0:T(8,128)(2,1)S(1)} %add_convert_fusion.2), channel_id=1, source_target_pairs={{0,4},{1,3},{4,8},{5,1},{8,12},{9,5},{12,14},{13,9},{14,10},{15,13... | collective-permute-start | bytes 393224 | tf_op jit(solution)/shard_map/ppermute | solution.py:51
  57.0 6.3 %collective-permute-start.34 = (bf16[256,256]{1,0:T(8,128)(2,1)S(1)}, bf16[256,256]{1,0:T(8,128)(2,1)S(1)}, u32[]{:S(2)}, u32[]{:S(2)}) collective-permute-start(bf16[256,256]{1,0:T(8,128)(2,1)S(1)} %multiply_convert_fusion.refs_1_), channel_id=1, source_target_pairs={{0,4},{1,3},{4,8},{5,1},{8,12},{9,5},{12,14},{13,9},{14,10},{15,13... | collective-permute-start | bytes 393224 | tf_op jit(solution)/shard_map/ppermute | solution.py:51
  58.4 6.1 %collective-permute-start.30 = (bf16[256,256]{1,0:T(8,128)(2,1)S(1)}, bf16[256,256]{1,0:T(8,128)(2,1)S(1)}, u32[]{:S(2)}, u32[]{:S(2)}) collective-permute-start(bf16[256,256]{1,0:T(8,128)(2,1)S(1)} %fusion.3.refs_0_), channel_id=1, source_target_pairs={{0,2},{1,5},{4,0},{5,9},{8,4},{9,13},{12,8},{13,15},{14,12},{15,11... | collective-permute-start | bytes 393224 | tf_op jit(solution)/shard_map/ppermute | solution.py:51
  60.3 6.4 %collective-permute-start.38 = (bf16[256,256]{1,0:T(8,128)(2,1)S(1)}, bf16[256,256]{1,0:T(8,128)(2,1)S(1)}, u32[]{:S(2)}, u32[]{:S(2)}) collective-permute-start(bf16[256,256]{1,0:T(8,128)(2,1)S(1)} %fusion.3.refs_0_), channel_id=1, source_target_pairs={{0,4},{1,3},{4,8},{5,1},{8,12},{9,5},{12,14},{13,9},{14,10},{15,13... | collective-permute-start | bytes 393224 | tf_op jit(solution)/shard_map/ppermute | solution.py:51
  63.3 6.3 %collective-permute-start.35 = (bf16[256,256]{1,0:T(8,128)(2,1)S(1)}, bf16[256,256]{1,0:T(8,128)(2,1)S(1)}, u32[]{:S(2)}, u32[]{:S(2)}) collective-permute-start(bf16[256,256]{1,0:T(8,128)(2,1)S(1)} %collective-permute-done.34.refs_1_), channel_id=1, source_target_pairs={{0,4},{1,3},{4,8},{5,1},{8,12},{9,5},{12,14},{13,9},{14,10},{15,13... | collective-permute-start | bytes 393224 | tf_op jit(solution)/shard_map/ppermute | solution.py:51
  64.5 6.4 %collective-permute-start.31 = (bf16[256,256]{1,0:T(8,128)(2,1)S(1)}, bf16[256,256]{1,0:T(8,128)(2,1)S(1)}, u32[]{:S(2)}, u32[]{:S(2)}) collective-permute-start(bf16[256,256]{1,0:T(8,128)(2,1)S(1)} %collective-permute-done.30.refs_2_), channel_id=1, source_target_pairs={{0,2},{1,5},{4,0},{5,9},{8,4},{9,13},{12,8},{13,15},{14,12},{15,11... | collective-permute-start | bytes 393224 | tf_op jit(solution)/shard_map/ppermute | solution.py:51
  66.7 5.9 %collective-permute-start.40 = (bf16[256,256]{1,0:T(8,128)(2,1)S(1)}, bf16[256,256]{1,0:T(8,128)(2,1)S(1)}, u32[]{:S(2)}, u32[]{:S(2)}) collective-permute-start(bf16[256,256]{1,0:T(8,128)(2,1)S(1)} %collective-permute-done.38.refs_0_), channel_id=1, source_target_pairs={{0,4},{1,3},{4,8},{5,1},{8,12},{9,5},{12,14},{13,9},{14,10},{15,13... | collective-permute-start | bytes 393224 | tf_op jit(solution)/shard_map/ppermute | solution.py:51
  67.9 5.9 %collective-permute-start.41 = (bf16[256,256]{1,0:T(8,128)(2,1)S(1)}, bf16[256,256]{1,0:T(8,128)(2,1)S(1)}, u32[]{:S(2)}, u32[]{:S(2)}) collective-permute-start(bf16[256,256]{1,0:T(8,128)(2,1)S(1)} %collective-permute-done.39.refs_3_), channel_id=1, source_target_pairs={{0,2},{1,5},{4,0},{5,9},{8,4},{9,13},{12,8},{13,15},{14,12},{15,11... | collective-permute-start | bytes 393224 | tf_op jit(solution)/shard_map/ppermute | solution.py:51
  69.6 6.4 %collective-permute-start.36 = (bf16[256,256]{1,0:T(8,128)(2,1)S(1)}, bf16[256,256]{1,0:T(8,128)(2,1)S(1)}, u32[]{:S(2)}, u32[]{:S(2)}) collective-permute-start(bf16[256,256]{1,0:T(8,128)(2,1)S(1)} %collective-permute-done.35.refs_5_), channel_id=1, source_target_pairs={{0,4},{1,3},{4,8},{5,1},{8,12},{9,5},{12,14},{13,9},{14,10},{15,13... | collective-permute-start | bytes 393224 | tf_op jit(solution)/shard_map/ppermute | solution.py:51
  70.9 6.3 %collective-permute-start.32 = (bf16[256,256]{1,0:T(8,128)(2,1)S(1)}, bf16[256,256]{1,0:T(8,128)(2,1)S(1)}, u32[]{:S(2)}, u32[]{:S(2)}) collective-permute-start(bf16[256,256]{1,0:T(8,128)(2,1)S(1)} %collective-permute-done.31.refs_6_), channel_id=1, source_target_pairs={{0,2},{1,5},{4,0},{5,9},{8,4},{9,13},{12,8},{13,15},{14,12},{15,11... | collective-permute-start | bytes 393224 | tf_op jit(solution)/shard_map/ppermute | solution.py:51
  (16 other events, 120.7 us)

commit v19 on v15

--- a/solution.py
+++ b/solution.py
@@ -205,32 +205,25 @@
 
 
 def finish_kernel(
-    starts, turned, preact, back_own, arrived, high, grad, bias, cross, stage, cross_stage, grad_sems, cross_sems
+    starts, turned, preact, back_own, arrived, high, grad, bias, cross, stage, cross_stage, grad_sems, cross_sem
 ):
     pieces, height, lat = stage.shape
     rows = preact.shape[0]
     half_width = high.shape[0]
+    first = starts[starts.shape[0] - 1] == 0
+    value = jnp.where(preact[...] > 0, back_own[...] + arrived[:rows, :].astype(F32), 0.0).astype(BF16)
     copies = []
-    first = starts[starts.shape[0] - 1] == 0
-
-    @pl.when(first)
-    def _():
-        cross_stage[...] = arrived[rows:, :].astype(F32)
-
-    @pl.when(jnp.logical_not(first))
-    def _():
-        cross_stage[...] = high[...]
-
-    for c in range(half_width // lat):
-        at = pl.ds(c * lat, lat)
-        copies.append(pltpu.make_async_copy(cross_stage.at[at, :], cross.at[:, at], cross_sems.at[c]))
-        copies[-1].start()
-    value = jnp.where(preact[...] > 0, back_own[...] + arrived[:rows, :].astype(F32), 0.0).astype(BF16)
     for i in range(pieces):
         at = pl.ds(i * height, height)
         stage[i] = jnp.dot(turned[at, :], value, preferred_element_type=F32)
         copies.append(pltpu.make_async_copy(stage.at[i], grad.at[0, at, :], grad_sems.at[i]))
         copies[-1].start()
+        if i == 0:
+            for c in range(0, half_width, lat):
+                source = arrived[rows + c:rows + c + lat, :].astype(F32)
+                cross_stage[:, c:c + lat] = jnp.where(first, source, high[c:c + lat, :])
+            copies.append(pltpu.make_async_copy(cross_stage, cross, cross_sem))
+            copies[-1].start()
     bias[...] = jnp.sum(value.astype(F32), axis=0, keepdims=True)
     for copy in copies:
         copy.wait()
@@ -388,9 +381,9 @@
         out_spaces=[pl.ANY, pltpu.VMEM, pl.ANY],
         scratch=[
             pltpu.VMEM((PIECES, height, lat), F32),
-            pltpu.VMEM((half_width, lat), F32),
+            pltpu.VMEM((lat, half_width), F32),
             pltpu.SemaphoreType.DMA((PIECES,)),
-            pltpu.SemaphoreType.DMA((half_width // lat,)),
+            pltpu.SemaphoreType.DMA,
         ],
     )
     return (grad_enc, grad_bias, grad_same, grad_cross)

time: 88.9 us -> 88.8 us (level)
  no operation moved by 1% of the time
where the time goes in v19:
time: 88.8 us; the launch traced here: 88.6 us
  starting transfers between devices  47.4 us (53%)
  waiting for transfers between devices  23.9 us (27%)
  Pallas kernels  13.5 us (15%)
  other arithmetic  1.63 us (2%)
  local copies, waits for them, and re-layouts  1.15 us (1%)
  between operations  0.96 us (1%)
    ppermute x42, starting transfers between devices, hop(): return lax.ppermute(shard, ('latent', 'layer'), pairs)  43.5 us
    ppermute x42, waiting for transfers between devices, hop(): return lax.ppermute(shard, ('latent', 'layer'), pairs)  22.3 us
    pallas_call x12, Pallas kernels, call(): pl.pallas_call(kernel, out_shape=outs, in_specs=[spec(pltpu.SMEM)] + [spe...  13.5 us
    ppermute x3, starting transfers between devices, passed_along(): return lax.ppermute(shard, axis, pairs)  3.89 us
  transfers between devices with their start and end apart: 45, of which 28 were waited for; matrix products, arithmetic and copies ran while one was open for 2% of the time, Pallas kernels for 10%

profile of v19, /device:TPU:0, one launch (start us, length us, event | category | flops | bytes accessed | tf_op | source)
XLA Modules:
  0.0 88.6 jit_solution(14960422383333440027)
XLA Ops:
  1.7 3.1 %collective-permute-start.5 = (bf16[256,256]{1,0:T(8,128)(2,1)S(1)}, bf16[256,256]{1,0:T(8,128)(2,1)S(1)}, u32[]{:S(2)}, u32[]{:S(2)}) collective-permute-start(bf16[256,256]{1,0:T(8,128)(2,1)S(1)} %get-tuple-element.48.shard.refs_1_), channel_id=1, source_target_pairs={{0,4},{1,3},{4,8},{5,1},{8,12},{9,5},{12,14},{13,9},{14,10},{15,13... | collective-permute-start | bytes 393224 | tf_op jit(solution)/shard_map/ppermute | solution.py:51
  5.5 2.1 %collective-permute-start = (bf16[256,256]{1,0:T(8,128)(2,1)S(1)}, bf16[256,256]{1,0:T(8,128)(2,1)S(1)}, u32[]{:S(2)}, u32[]{:S(2)}) collective-permute-start(bf16[256,256]{1,0:T(8,128)(2,1)S(1)} %get-tuple-element.47.shard.refs_0_), channel_id=1, source_target_pairs={{0,4},{1,3},{4,8},{5,1},{8,12},{9,5},{12,14},{13,9},{14,10},{15,13... | collective-permute-start | bytes 393224 | tf_op jit(solution)/shard_map/ppermute | solution.py:51
  8.5 1.8 %collective-permute-start.6 = (bf16[256,256]{1,0:T(8,128)(2,1)S(1)}, bf16[256,256]{1,0:T(8,128)(2,1)S(1)}, u32[]{:S(2)}, u32[]{:S(2)}) collective-permute-start(bf16[256,256]{1,0:T(8,128)(2,1)S(1)} %collective-permute-done.5.refs_3_.refs_1_), channel_id=1, source_target_pairs={{0,4},{1,3},{4,8},{5,1},{8,12},{9,5},{12,14},{13,9},{14,10},{15,13... | collective-permute-start | bytes 393224 | tf_op jit(solution)/shard_map/ppermute | solution.py:51
  11.5 1.3 %collective-permute-start.14 = (bf16[128,1024]{1,0:T(8,128)(2,1)}, bf16[128,1024]{1,0:T(8,128)(2,1)S(1)}, u32[]{:S(2)}, u32[]{:S(2)}) collective-permute-start(bf16[128,1024]{1,0:T(8,128)(2,1)} %param.11), channel_id=1, source_target_pairs={{0,1},{2,3},{4,5},{6,7},{8,9},{10,11},{12,13},{14,15},{16,17},{18,... | collective-permute-start | bytes 786440 | tf_op jit(solution)/shard_map/ppermute | solution.py:23
  12.8 2.5 %collective-permute-start.10 = (bf16[256,256]{1,0:T(8,128)(2,1)S(1)}, bf16[256,256]{1,0:T(8,128)(2,1)S(1)}, u32[]{:S(2)}, u32[]{:S(2)}) collective-permute-start(bf16[256,256]{1,0:T(8,128)(2,1)S(1)} %collective-permute-done.refs_2_.refs_0_), channel_id=1, source_target_pairs={{0,4},{1,3},{4,8},{5,1},{8,12},{9,5},{12,14},{13,9},{14,10},{15,13... | collective-permute-start | bytes 393224 | tf_op jit(solution)/shard_map/ppermute | solution.py:51
  15.3 2.0 %collective-permute-start.7 = (bf16[256,256]{1,0:T(8,128)(2,1)S(1)}, bf16[256,256]{1,0:T(8,128)(2,1)S(1)}, u32[]{:S(2)}, u32[]{:S(2)}) collective-permute-start(bf16[256,256]{1,0:T(8,128)(2,1)S(1)} %collective-permute-done.6.refs_7_.refs_5_), channel_id=1, source_target_pairs={{0,4},{1,3},{4,8},{5,1},{8,12},{9,5},{12,14},{13,9},{14,10},{15,13... | collective-permute-start | bytes 393224 | tf_op jit(solution)/shard_map/ppermute | solution.py:51
  17.4 1.5 %collective-permute-done.10.refs_6_.refs_4_ = bf16[256,256]{1,0:T(8,128)(2,1)S(1)} collective-permute-done((bf16[256,256]{1,0:T(8,128)(2,1)S(1)}, bf16[256,256]{1,0:T(8,128)(2,1)S(1)}, u32[]{:S(2)}, u32[]{:S(2)}) %collective-permute-start.10) | collective-permute-done | bytes 131104 | tf_op jit(solution)/shard_map/ppermute | solution.py:51
  18.9 1.4 %collective-permute-start.12 = (bf16[256,256]{1,0:T(8,128)(2,1)S(1)}, bf16[256,256]{1,0:T(8,128)(2,1)S(1)}, u32[]{:S(2)}, u32[]{:S(2)}) collective-permute-start(bf16[256,256]{1,0:T(8,128)(2,1)S(1)} %collective-permute-done.10.refs_6_.refs_4_), channel_id=1, source_target_pairs={{0,4},{1,3},{4,8},{5,1},{8,12},{9,5},{12,14},{13,9},{14,10},{15,13... | collective-permute-start | bytes 393224 | tf_op jit(solution)/shard_map/ppermute | solution.py:51
  21.8 1.8 %collective-permute-start.8 = (bf16[256,256]{1,0:T(8,128)(2,1)S(1)}, bf16[256,256]{1,0:T(8,128)(2,1)S(1)}, u32[]{:S(2)}, u32[]{:S(2)}) collective-permute-start(bf16[256,256]{1,0:T(8,128)(2,1)S(1)} %collective-permute-done.7.refs_11_.refs_9_), channel_id=1, source_target_pairs={{0,4},{1,3},{4,8},{5,1},{8,12},{9,5},{12,14},{13,9},{14,10},{15,13... | collective-permute-start | bytes 393224 | tf_op jit(solution)/shard_map/ppermute | solution.py:51
  27.5 1.6 %collective-permute-done.4.refs_0_.refs_12_ = bf16[256,256]{1,0:T(8,128)(2,1)S(1)} collective-permute-done((bf16[256,256]{1,0:T(8,128)(2,1)S(1)}, bf16[256,256]{1,0:T(8,128)(2,1)S(1)}, u32[]{:S(2)}, u32[]{:S(2)}) %collective-permute-start.4) | collective-permute-done | bytes 131104 | tf_op jit(solution)/shard_map/ppermute | solution.py:51
  29.9 1.3 %collective-permute-start.15 = (bf16[512,128]{1,0:T(8,128)(2,1)S(1)}, bf16[512,128]{1,0:T(8,128)(2,1)S(1)}, u32[]{:S(2)}, u32[]{:S(2)}) collective-permute-start(bf16[512,128]{1,0:T(8,128)(2,1)S(1)} %get-tuple-element.51.codes), channel_id=1, source_target_pairs={{0,1},{2,3},{4,5},{6,7},{8,9},{10,11},{12,13},{14,15},{16,17},{18,... | collective-permute-start | bytes 393224 | tf_op jit(solution)/shard_map/ppermute | solution.py:23
  33.0 2.1 %collective-permute-start.16 = (bf16[256,256]{1,0:T(8,128)(2,1)S(1)}, bf16[256,256]{1,0:T(8,128)(2,1)S(1)}, u32[]{:S(2)}, u32[]{:S(2)}) collective-permute-start(bf16[256,256]{1,0:T(8,128)(2,1)S(1)} %get-tuple-element.56), channel_id=1, source_target_pairs={{0,4},{1,3},{4,8},{5,1},{8,12},{9,5},{12,14},{13,9},{14,10},{15,13... | collective-permute-start | bytes 393224 | tf_op jit(solution)/shard_map/ppermute | solution.py:51
  36.4 2.0 %collective-permute-start.25 = (bf16[256,256]{1,0:T(8,128)(2,1)S(1)}, bf16[256,256]{1,0:T(8,128)(2,1)S(1)}, u32[]{:S(2)}, u32[]{:S(2)}) collective-permute-start(bf16[256,256]{1,0:T(8,128)(2,1)S(1)} %get-tuple-element.70), channel_id=1, source_target_pairs={{0,4},{1,3},{4,8},{5,1},{8,12},{9,5},{12,14},{13,9},{14,10},{15,13... | collective-permute-start | bytes 393224 | tf_op jit(solution)/shard_map/ppermute | solution.py:51
  39.1 2.1 %collective-permute-start.17 = (bf16[256,256]{1,0:T(8,128)(2,1)S(1)}, bf16[256,256]{1,0:T(8,128)(2,1)S(1)}, u32[]{:S(2)}, u32[]{:S(2)}) collective-permute-start(bf16[256,256]{1,0:T(8,128)(2,1)S(1)} %add_convert_fusion.9), channel_id=1, source_target_pairs={{0,4},{1,3},{4,8},{5,1},{8,12},{9,5},{12,14},{13,9},{14,10},{15,13... | collective-permute-start | bytes 393224 | tf_op jit(solution)/shard_map/ppermute | solution.py:51
  41.1 1.6 %collective-permute-done.20 = bf16[256,256]{1,0:T(8,128)(2,1)S(1)} collective-permute-done((bf16[256,256]{1,0:T(8,128)(2,1)S(1)}, bf16[256,256]{1,0:T(8,128)(2,1)S(1)}, u32[]{:S(2)}, u32[]{:S(2)}) %collective-permute-start.20) | collective-permute-done | bytes 131104 | tf_op jit(solution)/shard_map/ppermute | solution.py:51
  42.8 2.1 %collective-permute-start.26 = (bf16[256,256]{1,0:T(8,128)(2,1)S(1)}, bf16[256,256]{1,0:T(8,128)(2,1)S(1)}, u32[]{:S(2)}, u32[]{:S(2)}) collective-permute-start(bf16[256,256]{1,0:T(8,128)(2,1)S(1)} %add_convert_fusion.3), channel_id=1, source_target_pairs={{0,4},{1,3},{4,8},{5,1},{8,12},{9,5},{12,14},{13,9},{14,10},{15,13... | collective-permute-start | bytes 393224 | tf_op jit(solution)/shard_map/ppermute | solution.py:51
  45.7 2.1 %collective-permute-start.18 = (bf16[256,256]{1,0:T(8,128)(2,1)S(1)}, bf16[256,256]{1,0:T(8,128)(2,1)S(1)}, u32[]{:S(2)}, u32[]{:S(2)}) collective-permute-start(bf16[256,256]{1,0:T(8,128)(2,1)S(1)} %add_convert_fusion.8), channel_id=1, source_target_pairs={{0,4},{1,3},{4,8},{5,1},{8,12},{9,5},{12,14},{13,9},{14,10},{15,13... | collective-permute-start | bytes 393224 | tf_op jit(solution)/shard_map/ppermute | solution.py:51
  49.1 1.4 %collective-permute-start.27 = (bf16[256,256]{1,0:T(8,128)(2,1)S(1)}, bf16[256,256]{1,0:T(8,128)(2,1)S(1)}, u32[]{:S(2)}, u32[]{:S(2)}) collective-permute-start(bf16[256,256]{1,0:T(8,128)(2,1)S(1)} %add_convert_fusion.2), channel_id=1, source_target_pairs={{0,4},{1,3},{4,8},{5,1},{8,12},{9,5},{12,14},{13,9},{14,10},{15,13... | collective-permute-start | bytes 393224 | tf_op jit(solution)/shard_map/ppermute | solution.py:51
  51.6 1.3 %collective-permute-start.19 = (bf16[256,256]{1,0:T(8,128)(2,1)S(1)}, bf16[256,256]{1,0:T(8,128)(2,1)S(1)}, u32[]{:S(2)}, u32[]{:S(2)}) collective-permute-start(bf16[256,256]{1,0:T(8,128)(2,1)S(1)} %add_convert_fusion.7), channel_id=1, source_target_pairs={{0,4},{1,3},{4,8},{5,1},{8,12},{9,5},{12,14},{13,9},{14,10},{15,13... | collective-permute-start | bytes 393224 | tf_op jit(solution)/shard_map/ppermute | solution.py:51
  54.5 2.4 %collective-permute-done.19 = bf16[256,256]{1,0:T(8,128)(2,1)S(1)} collective-permute-done((bf16[256,256]{1,0:T(8,128)(2,1)S(1)}, bf16[256,256]{1,0:T(8,128)(2,1)S(1)}, u32[]{:S(2)}, u32[]{:S(2)}) %collective-permute-start.19) | collective-permute-done | bytes 131104 | tf_op jit(solution)/shard_map/ppermute | solution.py:51
  57.0 1.4 %collective-permute-start.34 = (bf16[256,256]{1,0:T(8,128)(2,1)S(1)}, bf16[256,256]{1,0:T(8,128)(2,1)S(1)}, u32[]{:S(2)}, u32[]{:S(2)}) collective-permute-start(bf16[256,256]{1,0:T(8,128)(2,1)S(1)} %multiply_convert_fusion.refs_1_), channel_id=1, source_target_pairs={{0,4},{1,3},{4,8},{5,1},{8,12},{9,5},{12,14},{13,9},{14,10},{15,13... | collective-permute-start | bytes 393224 | tf_op jit(solution)/shard_map/ppermute | solution.py:51
  61.3 1.9 %collective-permute-done.34.refs_3_ = bf16[256,256]{1,0:T(8,128)(2,1)S(1)} collective-permute-done((bf16[256,256]{1,0:T(8,128)(2,1)S(1)}, bf16[256,256]{1,0:T(8,128)(2,1)S(1)}, u32[]{:S(2)}, u32[]{:S(2)}) %collective-permute-start.34) | collective-permute-done | bytes 131104 | tf_op jit(solution)/shard_map/ppermute | solution.py:51
  63.1 1.4 %collective-permute-start.35 = (bf16[256,256]{1,0:T(8,128)(2,1)S(1)}, bf16[256,256]{1,0:T(8,128)(2,1)S(1)}, u32[]{:S(2)}, u32[]{:S(2)}) collective-permute-start(bf16[256,256]{1,0:T(8,128)(2,1)S(1)} %collective-permute-done.34.refs_3_), channel_id=1, source_target_pairs={{0,4},{1,3},{4,8},{5,1},{8,12},{9,5},{12,14},{13,9},{14,10},{15,13... | collective-permute-start | bytes 393224 | tf_op jit(solution)/shard_map/ppermute | solution.py:51
  67.5 1.4 %collective-permute-start.40 = (bf16[256,256]{1,0:T(8,128)(2,1)S(1)}, bf16[256,256]{1,0:T(8,128)(2,1)S(1)}, u32[]{:S(2)}, u32[]{:S(2)}) collective-permute-start(bf16[256,256]{1,0:T(8,128)(2,1)S(1)} %collective-permute-done.38.refs_2_), channel_id=1, source_target_pairs={{0,4},{1,3},{4,8},{5,1},{8,12},{9,5},{12,14},{13,9},{14,10},{15,13... | collective-permute-start | bytes 393224 | tf_op jit(solution)/shard_map/ppermute | solution.py:51
  68.9 1.5 %collective-permute-start.36 = (bf16[256,256]{1,0:T(8,128)(2,1)S(1)}, bf16[256,256]{1,0:T(8,128)(2,1)S(1)}, u32[]{:S(2)}, u32[]{:S(2)}) collective-permute-start(bf16[256,256]{1,0:T(8,128)(2,1)S(1)} %collective-permute-done.35.refs_1_), channel_id=1, source_target_pairs={{0,4},{1,3},{4,8},{5,1},{8,12},{9,5},{12,14},{13,9},{14,10},{15,13... | collective-permute-start | bytes 393224 | tf_op jit(solution)/shard_map/ppermute | solution.py:51
  71.3 2.0 %collective-permute-done.41.refs_3_ = bf16[256,256]{1,0:T(8,128)(2,1)S(1)} collective-permute-done((bf16[256,256]{1,0:T(8,128)(2,1)S(1)}, bf16[256,256]{1,0:T(8,128)(2,1)S(1)}, u32[]{:S(2)}, u32[]{:S(2)}) %collective-permute-start.41) | collective-permute-done | bytes 131104 | tf_op jit(solution)/shard_map/ppermute | solution.py:51
  73.6 1.7 %collective-permute-start.42 = (bf16[256,256]{1,0:T(8,128)(2,1)S(1)}, bf16[256,256]{1,0:T(8,128)(2,1)S(1)}, u32[]{:S(2)}, u32[]{:S(2)}) collective-permute-start(bf16[256,256]{1,0:T(8,128)(2,1)S(1)} %collective-permute-done.40.refs_0_), channel_id=1, source_target_pairs={{0,4},{1,3},{4,8},{5,1},{8,12},{9,5},{12,14},{13,9},{14,10},{15,13... | collective-permute-start | bytes 393224 | tf_op jit(solution)/shard_map/ppermute | solution.py:51
  75.3 1.4 %collective-permute-start.37 = (bf16[256,256]{1,0:T(8,128)(2,1)S(1)}, bf16[256,256]{1,0:T(8,128)(2,1)S(1)}, u32[]{:S(2)}, u32[]{:S(2)}) collective-permute-start(bf16[256,256]{1,0:T(8,128)(2,1)S(1)} %collective-permute-done.36.refs_5_), channel_id=1, source_target_pairs={{0,4},{1,3},{4,8},{5,1},{8,12},{9,5},{12,14},{13,9},{14,10},{15,13... | collective-permute-start | bytes 393224 | tf_op jit(solution)/shard_map/ppermute | solution.py:51
  80.3 1.4 %collective-permute-done.33.refs_0_ = bf16[256,256]{1,0:T(8,128)(2,1)S(1)} collective-permute-done((bf16[256,256]{1,0:T(8,128)(2,1)S(1)}, bf16[256,256]{1,0:T(8,128)(2,1)S(1)}, u32[]{:S(2)}, u32[]{:S(2)}) %collective-permute-start.33) | collective-permute-done | bytes 131104 | tf_op jit(solution)/shard_map/ppermute | solution.py:51
  82.2 1.3 %collective-permute-start.44 = (bf16[1536,128]{1,0:T(8,128)(2,1)S(1)}, bf16[1536,128]{1,0:T(8,128)(2,1)S(1)}, u32[]{:S(2)}, u32[]{:S(2)}) collective-permute-start(bf16[1536,128]{1,0:T(8,128)(2,1)S(1)} %get-tuple-element.84), channel_id=1, source_target_pairs={{1,0},{3,2},{5,4},{7,6},{9,8},{11,10},{13,12},{15,14},{17,16},{19,... | collective-permute-start | bytes 1179656 | tf_op jit(solution)/shard_map/ppermute | solution.py:23
  83.5 1.6 %shard_map.102 = (f32[512,128]{1,0:T(8,128)S(1)}, f32[1,128,2048]{2,1,0:T(8,128)}) custom-call(s32[9]{0:T(128)S(1)} %stack.39.starts, bf16[256,256]{1,0:T(8,128)(2,1)S(1)} %collective-permute-done.33.refs_0_, bf16[256,256]{1,0:T(8,128)(2,1)S(1)} %collective-permute-done.37.refs_1_, bf16[256,2048]{1,0:T(8,128)(2,1)S(1)} %maximum_maximum_fusion.stacked.refs_6_.refs_8_.refs_2_, ...), custom_call_target="tpu_custom_call" | custom-call | bytes 1024 | tf_op jit(solution)/shard_map/pallas_call | solution.py:64
  85.9 2.7 %shard_map.104 = (f32[1,2048,128]{2,1,0:T(8,128)}, f32[1,128]{1,0:T(1,128)}, f32[128,1024]{1,0:T(8,128)}) custom-call(s32[9]{0:T(128)S(1)} %stack.39.starts, bf16[2048,512]{1,0:T(8,128)(2,1)S(1)} %shard_map.99.turned, f32[512,128]{1,0:T(8,128)S(1)} %get-tuple-element.66.preact, f32[512,128]{1,0:T(8,128)S(1)} %get-tuple-element.83.back_own, ...), custom_call_target="tpu_custom_call" | custom-call | flops 268435456 | bytes 1024 | tf_op jit(solution)/shard_map/pallas_call | solution.py:64
  (92 shorter events, 30.6 us)
Async XLA Ops:
  1.7 6.8 %collective-permute-start.5 = (bf16[256,256]{1,0:T(8,128)(2,1)S(1)}, bf16[256,256]{1,0:T(8,128)(2,1)S(1)}, u32[]{:S(2)}, u32[]{:S(2)}) collective-permute-start(bf16[256,256]{1,0:T(8,128)(2,1)S(1)} %get-tuple-element.48.shard.refs_1_), channel_id=1, source_target_pairs={{0,4},{1,3},{4,8},{5,1},{8,12},{9,5},{12,14},{13,9},{14,10},{15,13... | collective-permute-start | bytes 393224 | tf_op jit(solution)/shard_map/ppermute | solution.py:51
  4.8 6.3 %collective-permute-start.1 = (bf16[256,256]{1,0:T(8,128)(2,1)S(1)}, bf16[256,256]{1,0:T(8,128)(2,1)S(1)}, u32[]{:S(2)}, u32[]{:S(2)}) collective-permute-start(bf16[256,256]{1,0:T(8,128)(2,1)S(1)} %get-tuple-element.47.shard.refs_0_), channel_id=1, source_target_pairs={{0,2},{1,5},{4,0},{5,9},{8,4},{9,13},{12,8},{13,15},{14,12},{15,11... | collective-permute-start | bytes 393224 | tf_op jit(solution)/shard_map/ppermute | solution.py:51
  5.5 6.0 %collective-permute-start = (bf16[256,256]{1,0:T(8,128)(2,1)S(1)}, bf16[256,256]{1,0:T(8,128)(2,1)S(1)}, u32[]{:S(2)}, u32[]{:S(2)}) collective-permute-start(bf16[256,256]{1,0:T(8,128)(2,1)S(1)} %get-tuple-element.47.shard.refs_0_), channel_id=1, source_target_pairs={{0,4},{1,3},{4,8},{5,1},{8,12},{9,5},{12,14},{13,9},{14,10},{15,13... | collective-permute-start | bytes 393224 | tf_op jit(solution)/shard_map/ppermute | solution.py:51
  8.2 7.1 %collective-permute-start.9 = (bf16[256,256]{1,0:T(8,128)(2,1)S(1)}, bf16[256,256]{1,0:T(8,128)(2,1)S(1)}, u32[]{:S(2)}, u32[]{:S(2)}) collective-permute-start(bf16[256,256]{1,0:T(8,128)(2,1)S(1)} %get-tuple-element.48.shard.refs_1_), channel_id=1, source_target_pairs={{0,2},{1,5},{4,0},{5,9},{8,4},{9,13},{12,8},{13,15},{14,12},{15,11... | collective-permute-start | bytes 393224 | tf_op jit(solution)/shard_map/ppermute | solution.py:51
  8.5 6.8 %collective-permute-start.6 = (bf16[256,256]{1,0:T(8,128)(2,1)S(1)}, bf16[256,256]{1,0:T(8,128)(2,1)S(1)}, u32[]{:S(2)}, u32[]{:S(2)}) collective-permute-start(bf16[256,256]{1,0:T(8,128)(2,1)S(1)} %collective-permute-done.5.refs_3_.refs_1_), channel_id=1, source_target_pairs={{0,4},{1,3},{4,8},{5,1},{8,12},{9,5},{12,14},{13,9},{14,10},{15,13... | collective-permute-start | bytes 393224 | tf_op jit(solution)/shard_map/ppermute | solution.py:51
  11.1 6.3 %collective-permute-start.2 = (bf16[256,256]{1,0:T(8,128)(2,1)S(1)}, bf16[256,256]{1,0:T(8,128)(2,1)S(1)}, u32[]{:S(2)}, u32[]{:S(2)}) collective-permute-start(bf16[256,256]{1,0:T(8,128)(2,1)S(1)} %collective-permute-done.1.refs_4_.refs_2_), channel_id=1, source_target_pairs={{0,2},{1,5},{4,0},{5,9},{8,4},{9,13},{12,8},{13,15},{14,12},{15,11... | collective-permute-start | bytes 393224 | tf_op jit(solution)/shard_map/ppermute | solution.py:51
  11.5 12.7 %collective-permute-start.14 = (bf16[128,1024]{1,0:T(8,128)(2,1)}, bf16[128,1024]{1,0:T(8,128)(2,1)S(1)}, u32[]{:S(2)}, u32[]{:S(2)}) collective-permute-start(bf16[128,1024]{1,0:T(8,128)(2,1)} %param.11), channel_id=1, source_target_pairs={{0,1},{2,3},{4,5},{6,7},{8,9},{10,11},{12,13},{14,15},{16,17},{18,... | collective-permute-start | bytes 786440 | tf_op jit(solution)/shard_map/ppermute | solution.py:23
  12.8 6.2 %collective-permute-start.10 = (bf16[256,256]{1,0:T(8,128)(2,1)S(1)}, bf16[256,256]{1,0:T(8,128)(2,1)S(1)}, u32[]{:S(2)}, u32[]{:S(2)}) collective-permute-start(bf16[256,256]{1,0:T(8,128)(2,1)S(1)} %collective-permute-done.refs_2_.refs_0_), channel_id=1, source_target_pairs={{0,4},{1,3},{4,8},{5,1},{8,12},{9,5},{12,14},{13,9},{14,10},{15,13... | collective-permute-start | bytes 393224 | tf_op jit(solution)/shard_map/ppermute | solution.py:51
  15.3 6.0 %collective-permute-start.11 = (bf16[256,256]{1,0:T(8,128)(2,1)S(1)}, bf16[256,256]{1,0:T(8,128)(2,1)S(1)}, u32[]{:S(2)}, u32[]{:S(2)}) collective-permute-start(bf16[256,256]{1,0:T(8,128)(2,1)S(1)} %collective-permute-done.9.refs_5_.refs_3_), channel_id=1, source_target_pairs={{0,2},{1,5},{4,0},{5,9},{8,4},{9,13},{12,8},{13,15},{14,12},{15,11... | collective-permute-start | bytes 393224 | tf_op jit(solution)/shard_map/ppermute | solution.py:51
  15.3 6.5 %collective-permute-start.7 = (bf16[256,256]{1,0:T(8,128)(2,1)S(1)}, bf16[256,256]{1,0:T(8,128)(2,1)S(1)}, u32[]{:S(2)}, u32[]{:S(2)}) collective-permute-start(bf16[256,256]{1,0:T(8,128)(2,1)S(1)} %collective-permute-done.6.refs_7_.refs_5_), channel_id=1, source_target_pairs={{0,4},{1,3},{4,8},{5,1},{8,12},{9,5},{12,14},{13,9},{14,10},{15,13... | collective-permute-start | bytes 393224 | tf_op jit(solution)/shard_map/ppermute | solution.py:51
  17.4 6.7 %collective-permute-start.3 = (bf16[256,256]{1,0:T(8,128)(2,1)S(1)}, bf16[256,256]{1,0:T(8,128)(2,1)S(1)}, u32[]{:S(2)}, u32[]{:S(2)}) collective-permute-start(bf16[256,256]{1,0:T(8,128)(2,1)S(1)} %collective-permute-done.2.refs_8_.refs_6_), channel_id=1, source_target_pairs={{0,2},{1,5},{4,0},{5,9},{8,4},{9,13},{12,8},{13,15},{14,12},{15,11... | collective-permute-start | bytes 393224 | tf_op jit(solution)/shard_map/ppermute | solution.py:51
  18.9 6.4 %collective-permute-start.12 = (bf16[256,256]{1,0:T(8,128)(2,1)S(1)}, bf16[256,256]{1,0:T(8,128)(2,1)S(1)}, u32[]{:S(2)}, u32[]{:S(2)}) collective-permute-start(bf16[256,256]{1,0:T(8,128)(2,1)S(1)} %collective-permute-done.10.refs_6_.refs_4_), channel_id=1, source_target_pairs={{0,4},{1,3},{4,8},{5,1},{8,12},{9,5},{12,14},{13,9},{14,10},{15,13... | collective-permute-start | bytes 393224 | tf_op jit(solution)/shard_map/ppermute | solution.py:51
  32.9 6.0 %collective-permute-start.21 = (bf16[256,256]{1,0:T(8,128)(2,1)S(1)}, bf16[256,256]{1,0:T(8,128)(2,1)S(1)}, u32[]{:S(2)}, u32[]{:S(2)}) collective-permute-start(bf16[256,256]{1,0:T(8,128)(2,1)S(1)} %get-tuple-element.60), channel_id=1, source_target_pairs={{0,2},{1,5},{4,0},{5,9},{8,4},{9,13},{12,8},{13,15},{14,12},{15,11... | collective-permute-start | bytes 393224 | tf_op jit(solution)/shard_map/ppermute | solution.py:51
  33.0 6.0 %collective-permute-start.16 = (bf16[256,256]{1,0:T(8,128)(2,1)S(1)}, bf16[256,256]{1,0:T(8,128)(2,1)S(1)}, u32[]{:S(2)}, u32[]{:S(2)}) collective-permute-start(bf16[256,256]{1,0:T(8,128)(2,1)S(1)} %get-tuple-element.56), channel_id=1, source_target_pairs={{0,4},{1,3},{4,8},{5,1},{8,12},{9,5},{12,14},{13,9},{14,10},{15,13... | collective-permute-start | bytes 393224 | tf_op jit(solution)/shard_map/ppermute | solution.py:51
  36.3 6.4 %collective-permute-start.20 = (bf16[256,256]{1,0:T(8,128)(2,1)S(1)}, bf16[256,256]{1,0:T(8,128)(2,1)S(1)}, u32[]{:S(2)}, u32[]{:S(2)}) collective-permute-start(bf16[256,256]{1,0:T(8,128)(2,1)S(1)} %get-tuple-element.59), channel_id=1, source_target_pairs={{0,2},{1,5},{4,0},{5,9},{8,4},{9,13},{12,8},{13,15},{14,12},{15,11... | collective-permute-start | bytes 393224 | tf_op jit(solution)/shard_map/ppermute | solution.py:51
  36.4 6.4 %collective-permute-start.25 = (bf16[256,256]{1,0:T(8,128)(2,1)S(1)}, bf16[256,256]{1,0:T(8,128)(2,1)S(1)}, u32[]{:S(2)}, u32[]{:S(2)}) collective-permute-start(bf16[256,256]{1,0:T(8,128)(2,1)S(1)} %get-tuple-element.70), channel_id=1, source_target_pairs={{0,4},{1,3},{4,8},{5,1},{8,12},{9,5},{12,14},{13,9},{14,10},{15,13... | collective-permute-start | bytes 393224 | tf_op jit(solution)/shard_map/ppermute | solution.py:51
  39.0 6.5 %collective-permute-start.23 = (bf16[256,256]{1,0:T(8,128)(2,1)S(1)}, bf16[256,256]{1,0:T(8,128)(2,1)S(1)}, u32[]{:S(2)}, u32[]{:S(2)}) collective-permute-start(bf16[256,256]{1,0:T(8,128)(2,1)S(1)} %add_convert_fusion.4), channel_id=1, source_target_pairs={{0,2},{1,5},{4,0},{5,9},{8,4},{9,13},{12,8},{13,15},{14,12},{15,11... | collective-permute-start | bytes 393224 | tf_op jit(solution)/shard_map/ppermute | solution.py:51
  39.1 6.5 %collective-permute-start.17 = (bf16[256,256]{1,0:T(8,128)(2,1)S(1)}, bf16[256,256]{1,0:T(8,128)(2,1)S(1)}, u32[]{:S(2)}, u32[]{:S(2)}) collective-permute-start(bf16[256,256]{1,0:T(8,128)(2,1)S(1)} %add_convert_fusion.9), channel_id=1, source_target_pairs={{0,4},{1,3},{4,8},{5,1},{8,12},{9,5},{12,14},{13,9},{14,10},{15,13... | collective-permute-start | bytes 393224 | tf_op jit(solution)/shard_map/ppermute | solution.py:51
  42.8 6.2 %collective-permute-start.26 = (bf16[256,256]{1,0:T(8,128)(2,1)S(1)}, bf16[256,256]{1,0:T(8,128)(2,1)S(1)}, u32[]{:S(2)}, u32[]{:S(2)}) collective-permute-start(bf16[256,256]{1,0:T(8,128)(2,1)S(1)} %add_convert_fusion.3), channel_id=1, source_target_pairs={{0,4},{1,3},{4,8},{5,1},{8,12},{9,5},{12,14},{13,9},{14,10},{15,13... | collective-permute-start | bytes 393224 | tf_op jit(solution)/shard_map/ppermute | solution.py:51
  45.5 7.3 %collective-permute-start.28 = (bf16[256,256]{1,0:T(8,128)(2,1)S(1)}, bf16[256,256]{1,0:T(8,128)(2,1)S(1)}, u32[]{:S(2)}, u32[]{:S(2)}) collective-permute-start(bf16[256,256]{1,0:T(8,128)(2,1)S(1)} %add_convert_fusion.1), channel_id=1, source_target_pairs={{0,2},{1,5},{4,0},{5,9},{8,4},{9,13},{12,8},{13,15},{14,12},{15,11... | collective-permute-start | bytes 393224 | tf_op jit(solution)/shard_map/ppermute | solution.py:51
  45.7 5.9 %collective-permute-start.18 = (bf16[256,256]{1,0:T(8,128)(2,1)S(1)}, bf16[256,256]{1,0:T(8,128)(2,1)S(1)}, u32[]{:S(2)}, u32[]{:S(2)}) collective-permute-start(bf16[256,256]{1,0:T(8,128)(2,1)S(1)} %add_convert_fusion.8), channel_id=1, source_target_pairs={{0,4},{1,3},{4,8},{5,1},{8,12},{9,5},{12,14},{13,9},{14,10},{15,13... | collective-permute-start | bytes 393224 | tf_op jit(solution)/shard_map/ppermute | solution.py:51
  48.3 6.2 %collective-permute-start.24 = (bf16[256,256]{1,0:T(8,128)(2,1)S(1)}, bf16[256,256]{1,0:T(8,128)(2,1)S(1)}, u32[]{:S(2)}, u32[]{:S(2)}) collective-permute-start(bf16[256,256]{1,0:T(8,128)(2,1)S(1)} %add_convert_fusion.5), channel_id=1, source_target_pairs={{0,2},{1,5},{4,0},{5,9},{8,4},{9,13},{12,8},{13,15},{14,12},{15,11... | collective-permute-start | bytes 393224 | tf_op jit(solution)/shard_map/ppermute | solution.py:51
  49.1 9.3 %collective-permute-start.27 = (bf16[256,256]{1,0:T(8,128)(2,1)S(1)}, bf16[256,256]{1,0:T(8,128)(2,1)S(1)}, u32[]{:S(2)}, u32[]{:S(2)}) collective-permute-start(bf16[256,256]{1,0:T(8,128)(2,1)S(1)} %add_convert_fusion.2), channel_id=1, source_target_pairs={{0,4},{1,3},{4,8},{5,1},{8,12},{9,5},{12,14},{13,9},{14,10},{15,13... | collective-permute-start | bytes 393224 | tf_op jit(solution)/shard_map/ppermute | solution.py:51
  57.0 6.2 %collective-permute-start.34 = (bf16[256,256]{1,0:T(8,128)(2,1)S(1)}, bf16[256,256]{1,0:T(8,128)(2,1)S(1)}, u32[]{:S(2)}, u32[]{:S(2)}) collective-permute-start(bf16[256,256]{1,0:T(8,128)(2,1)S(1)} %multiply_convert_fusion.refs_1_), channel_id=1, source_target_pairs={{0,4},{1,3},{4,8},{5,1},{8,12},{9,5},{12,14},{13,9},{14,10},{15,13... | collective-permute-start | bytes 393224 | tf_op jit(solution)/shard_map/ppermute | solution.py:51
  58.5 6.4 %collective-permute-start.30 = (bf16[256,256]{1,0:T(8,128)(2,1)S(1)}, bf16[256,256]{1,0:T(8,128)(2,1)S(1)}, u32[]{:S(2)}, u32[]{:S(2)}) collective-permute-start(bf16[256,256]{1,0:T(8,128)(2,1)S(1)} %fusion.1.refs_0_), channel_id=1, source_target_pairs={{0,2},{1,5},{4,0},{5,9},{8,4},{9,13},{12,8},{13,15},{14,12},{15,11... | collective-permute-start | bytes 393224 | tf_op jit(solution)/shard_map/ppermute | solution.py:51
  59.2 7.7 %collective-permute-start.39 = (bf16[256,256]{1,0:T(8,128)(2,1)S(1)}, bf16[256,256]{1,0:T(8,128)(2,1)S(1)}, u32[]{:S(2)}, u32[]{:S(2)}) collective-permute-start(bf16[256,256]{1,0:T(8,128)(2,1)S(1)} %multiply_convert_fusion.refs_1_), channel_id=1, source_target_pairs={{0,2},{1,5},{4,0},{5,9},{8,4},{9,13},{12,8},{13,15},{14,12},{15,11... | collective-permute-start | bytes 393224 | tf_op jit(solution)/shard_map/ppermute | solution.py:51
  60.3 7.2 %collective-permute-start.38 = (bf16[256,256]{1,0:T(8,128)(2,1)S(1)}, bf16[256,256]{1,0:T(8,128)(2,1)S(1)}, u32[]{:S(2)}, u32[]{:S(2)}) collective-permute-start(bf16[256,256]{1,0:T(8,128)(2,1)S(1)} %fusion.1.refs_0_), channel_id=1, source_target_pairs={{0,4},{1,3},{4,8},{5,1},{8,12},{9,5},{12,14},{13,9},{14,10},{15,13... | collective-permute-start | bytes 393224 | tf_op jit(solution)/shard_map/ppermute | solution.py:51
  64.9 5.9 %collective-permute-start.31 = (bf16[256,256]{1,0:T(8,128)(2,1)S(1)}, bf16[256,256]{1,0:T(8,128)(2,1)S(1)}, u32[]{:S(2)}, u32[]{:S(2)}) collective-permute-start(bf16[256,256]{1,0:T(8,128)(2,1)S(1)} %collective-permute-done.30.refs_4_), channel_id=1, source_target_pairs={{0,2},{1,5},{4,0},{5,9},{8,4},{9,13},{12,8},{13,15},{14,12},{15,11... | collective-permute-start | bytes 393224 | tf_op jit(solution)/shard_map/ppermute | solution.py:51
  66.9 6.4 %collective-permute-start.41 = (bf16[256,256]{1,0:T(8,128)(2,1)S(1)}, bf16[256,256]{1,0:T(8,128)(2,1)S(1)}, u32[]{:S(2)}, u32[]{:S(2)}) collective-permute-start(bf16[256,256]{1,0:T(8,128)(2,1)S(1)} %collective-permute-done.39.refs_5_), channel_id=1, source_target_pairs={{0,2},{1,5},{4,0},{5,9},{8,4},{9,13},{12,8},{13,15},{14,12},{15,11... | collective-permute-start | bytes 393224 | tf_op jit(solution)/shard_map/ppermute | solution.py:51
  67.5 6.1 %collective-permute-start.40 = (bf16[256,256]{1,0:T(8,128)(2,1)S(1)}, bf16[256,256]{1,0:T(8,128)(2,1)S(1)}, u32[]{:S(2)}, u32[]{:S(2)}) collective-permute-start(bf16[256,256]{1,0:T(8,128)(2,1)S(1)} %collective-permute-done.38.refs_2_), channel_id=1, source_target_pairs={{0,4},{1,3},{4,8},{5,1},{8,12},{9,5},{12,14},{13,9},{14,10},{15,13... | collective-permute-start | bytes 393224 | tf_op jit(solution)/shard_map/ppermute | solution.py:51
  68.9 6.4 %collective-permute-start.36 = (bf16[256,256]{1,0:T(8,128)(2,1)S(1)}, bf16[256,256]{1,0:T(8,128)(2,1)S(1)}, u32[]{:S(2)}, u32[]{:S(2)}) collective-permute-start(bf16[256,256]{1,0:T(8,128)(2,1)S(1)} %collective-permute-done.35.refs_1_), channel_id=1, source_target_pairs={{0,4},{1,3},{4,8},{5,1},{8,12},{9,5},{12,14},{13,9},{14,10},{15,13... | collective-permute-start | bytes 393224 | tf_op jit(solution)/shard_map/ppermute | solution.py:51
  70.8 5.9 %collective-permute-start.32 = (bf16[256,256]{1,0:T(8,128)(2,1)S(1)}, bf16[256,256]{1,0:T(8,128)(2,1)S(1)}, u32[]{:S(2)}, u32[]{:S(2)}) collective-permute-start(bf16[256,256]{1,0:T(8,128)(2,1)S(1)} %collective-permute-done.31.refs_2_), channel_id=1, source_target_pairs={{0,2},{1,5},{4,0},{5,9},{8,4},{9,13},{12,8},{13,15},{14,12},{15,11... | collective-permute-start | bytes 393224 | tf_op jit(solution)/shard_map/ppermute | solution.py:51
  (16 other events, 122.7 us)

commit v20 on v19

--- a/solution.py
+++ b/solution.py
@@ -21,6 +21,11 @@
     size = lax.axis_size(axis)
     pairs = [(i, i + by) for i in range(size) if 0 <= i + by < size]
     return lax.ppermute(shard, axis, pairs)
+
+
+def swapped(shard):
+    size = lax.axis_size("layer")
+    return lax.ppermute(shard, "layer", [(i, size - 1 - i) for i in range(size)])
 
 
 def matmul(a, b, dims=(((1,), (0,)), ((), ()))):
@@ -211,7 +216,8 @@
     rows = preact.shape[0]
     half_width = high.shape[0]
     first = starts[starts.shape[0] - 1] == 0
-    value = jnp.where(preact[...] > 0, back_own[...] + arrived[:rows, :].astype(F32), 0.0).astype(BF16)
+    later = jnp.where(first, arrived[:rows, :].astype(F32), 0.0)
+    value = jnp.where(preact[...] > 0, back_own[...] + later, 0.0).astype(BF16)
     copies = []
     for i in range(pieces):
         at = pl.ds(i * height, height)
@@ -287,11 +293,12 @@
         turned_own += call(turn_own_kernel, [shape((wide, half), BF16)], 0, [starts, source])
     for s in range(1, reach + 1):
         gather_step(inputs, s, turned_own if s == 1 else None)
-    low_cross = passed_along(after(dec_cross, inputs[0][slot_p.get(1, far)]), "layer", 1)
-    stacked = jnp.concatenate([dec_same[0], jnp.concatenate([low_cross, dec_cross], axis=1)], axis=0)
+    low_cross = swapped(after(dec_cross, inputs[0][slot_p.get(1, far)]))
+    cross = jnp.where(layer > 0, jnp.concatenate([low_cross, dec_cross], axis=1), jnp.zeros((), BF16))
+    stacked = jnp.concatenate([dec_same[0], cross], axis=0)
     part = encode(tuple(range(far)), after(enc_bias, stacked))[0]
     preact, codes = encode((far,), part)
-    earlier = passed_along(codes, "layer", 1)
+    earlier = swapped(codes)
 
     def spread(slots, dtypes, turned):
         outs = []
@@ -363,7 +370,7 @@
         0,
         [starts] + last,
     )
-    returned = passed_along(sent, "layer", -1)
+    returned = swapped(sent)
     back_own, grad_same = call(
         functools.partial(own_back_kernel, groups, far),
         [shape((rows, lat), F32), shape((1, lat, deep), F32)],

time: 88.8 us -> 85.9 us (0.967)
  starting transfers between devices: 47.4 us -> 46 us
  waiting for transfers between devices: 23.9 us -> 22.6 us
    ppermute x3, starting transfers between devices: 3.89 us -> 0.14 us  [swapped(): lax.ppermute(shard, 'layer', [(i, size - 1 - i) for i in range(size)])]
    ppermute x42, starting transfers between devices: 43.5 us -> 45.9 us  [hop(): return lax.ppermute(shard, ('latent', 'layer'), pairs)]
    ppermute x42, waiting for transfers between devices: 22.3 us -> 21.2 us  [hop(): return lax.ppermute(shard, ('latent', 'layer'), pairs)]
    concatenate x1, other arithmetic: 1.22 us -> 0.09 us  [ring_shards(): stacked = jnp.concatenate([dec_same[0], cross], axis=0)]
    select_n x0 -> x1, other arithmetic: none -> 1.06 us  [ring_shards(): jnp.where(layer > 0, jnp.concatenate([low_cross, dec_cross], axis=1), jnp...]
where the time goes in v20:
time: 85.9 us; the launch traced here: 85.7 us
  starting transfers between devices  46 us (54%)
  waiting for transfers between devices  22.6 us (26%)
  Pallas kernels  13.5 us (16%)
  other arithmetic  1.56 us (2%)
  local copies, waits for them, and re-layouts  1.16 us (1%)
  between operations  0.92 us (1%)
    ppermute x42, starting transfers between devices, hop(): return lax.ppermute(shard, ('latent', 'layer'), pairs)  45.9 us
    ppermute x42, waiting for transfers between devices, hop(): return lax.ppermute(shard, ('latent', 'layer'), pairs)  21.2 us
    pallas_call x12, Pallas kernels, call(): pl.pallas_call(kernel, out_shape=outs, in_specs=[spec(pltpu.SMEM)] + [spe...  13.5 us
  transfers between devices with their start and end apart: 45, of which 28 were waited for; matrix products, arithmetic and copies ran while one was open for 2% of the time, Pallas kernels for 10%

profile of v20, /device:TPU:0, one launch (start us, length us, event | category | flops | bytes accessed | tf_op | source)
XLA Modules:
  0.0 85.7 jit_solution(7056853505126253069)
XLA Ops:
  1.7 3.1 %collective-permute-start.5 = (bf16[256,256]{1,0:T(8,128)(2,1)S(1)}, bf16[256,256]{1,0:T(8,128)(2,1)S(1)}, u32[]{:S(2)}, u32[]{:S(2)}) collective-permute-start(bf16[256,256]{1,0:T(8,128)(2,1)S(1)} %get-tuple-element.48.shard.refs_1_), channel_id=1, source_target_pairs={{0,4},{1,3},{4,8},{5,1},{8,12},{9,5},{12,14},{13,9},{14,10},{15,13... | collective-permute-start | bytes 393224 | tf_op jit(solution)/shard_map/ppermute | solution.py:56
  5.5 2.1 %collective-permute-start = (bf16[256,256]{1,0:T(8,128)(2,1)S(1)}, bf16[256,256]{1,0:T(8,128)(2,1)S(1)}, u32[]{:S(2)}, u32[]{:S(2)}) collective-permute-start(bf16[256,256]{1,0:T(8,128)(2,1)S(1)} %get-tuple-element.47.shard.refs_0_), channel_id=1, source_target_pairs={{0,4},{1,3},{4,8},{5,1},{8,12},{9,5},{12,14},{13,9},{14,10},{15,13... | collective-permute-start | bytes 393224 | tf_op jit(solution)/shard_map/ppermute | solution.py:56
  8.5 1.8 %collective-permute-start.6 = (bf16[256,256]{1,0:T(8,128)(2,1)S(1)}, bf16[256,256]{1,0:T(8,128)(2,1)S(1)}, u32[]{:S(2)}, u32[]{:S(2)}) collective-permute-start(bf16[256,256]{1,0:T(8,128)(2,1)S(1)} %collective-permute-done.5.refs_3_.refs_1_), channel_id=1, source_target_pairs={{0,4},{1,3},{4,8},{5,1},{8,12},{9,5},{12,14},{13,9},{14,10},{15,13... | collective-permute-start | bytes 393224 | tf_op jit(solution)/shard_map/ppermute | solution.py:56
  11.5 2.5 %collective-permute-start.10 = (bf16[256,256]{1,0:T(8,128)(2,1)S(1)}, bf16[256,256]{1,0:T(8,128)(2,1)S(1)}, u32[]{:S(2)}, u32[]{:S(2)}) collective-permute-start(bf16[256,256]{1,0:T(8,128)(2,1)S(1)} %collective-permute-done.refs_2_.refs_0_), channel_id=1, source_target_pairs={{0,4},{1,3},{4,8},{5,1},{8,12},{9,5},{12,14},{13,9},{14,10},{15,13... | collective-permute-start | bytes 393224 | tf_op jit(solution)/shard_map/ppermute | solution.py:56
  14.7 1.3 %collective-permute-start.7 = (bf16[256,256]{1,0:T(8,128)(2,1)S(1)}, bf16[256,256]{1,0:T(8,128)(2,1)S(1)}, u32[]{:S(2)}, u32[]{:S(2)}) collective-permute-start(bf16[256,256]{1,0:T(8,128)(2,1)S(1)} %collective-permute-done.6.refs_7_.refs_5_), channel_id=1, source_target_pairs={{0,4},{1,3},{4,8},{5,1},{8,12},{9,5},{12,14},{13,9},{14,10},{15,13... | collective-permute-start | bytes 393224 | tf_op jit(solution)/shard_map/ppermute | solution.py:56
  17.8 2.5 %collective-permute-start.12 = (bf16[256,256]{1,0:T(8,128)(2,1)S(1)}, bf16[256,256]{1,0:T(8,128)(2,1)S(1)}, u32[]{:S(2)}, u32[]{:S(2)}) collective-permute-start(bf16[256,256]{1,0:T(8,128)(2,1)S(1)} %collective-permute-done.10.refs_6_.refs_4_), channel_id=1, source_target_pairs={{0,4},{1,3},{4,8},{5,1},{8,12},{9,5},{12,14},{13,9},{14,10},{15,13... | collective-permute-start | bytes 393224 | tf_op jit(solution)/shard_map/ppermute | solution.py:56
  20.8 2.3 %collective-permute-start.8 = (bf16[256,256]{1,0:T(8,128)(2,1)S(1)}, bf16[256,256]{1,0:T(8,128)(2,1)S(1)}, u32[]{:S(2)}, u32[]{:S(2)}) collective-permute-start(bf16[256,256]{1,0:T(8,128)(2,1)S(1)} %collective-permute-done.7.refs_11_.refs_9_), channel_id=1, source_target_pairs={{0,4},{1,3},{4,8},{5,1},{8,12},{9,5},{12,14},{13,9},{14,10},{15,13... | collective-permute-start | bytes 393224 | tf_op jit(solution)/shard_map/ppermute | solution.py:56
  24.7 1.2 %collective-permute-done.13.refs_13_.refs_11_ = bf16[256,256]{1,0:T(8,128)(2,1)S(1)} collective-permute-done((bf16[256,256]{1,0:T(8,128)(2,1)S(1)}, bf16[256,256]{1,0:T(8,128)(2,1)S(1)}, u32[]{:S(2)}, u32[]{:S(2)}) %collective-permute-start.13) | collective-permute-done | bytes 131104 | tf_op jit(solution)/shard_map/ppermute | solution.py:56
  27.1 1.2 %collective-permute-done.4.refs_0_.refs_12_ = bf16[256,256]{1,0:T(8,128)(2,1)S(1)} collective-permute-done((bf16[256,256]{1,0:T(8,128)(2,1)S(1)}, bf16[256,256]{1,0:T(8,128)(2,1)S(1)}, u32[]{:S(2)}, u32[]{:S(2)}) %collective-permute-start.4) | collective-permute-done | bytes 131104 | tf_op jit(solution)/shard_map/ppermute | solution.py:56
  29.1 1.3 %collective-permute-done.15.earlier = bf16[512,128]{1,0:T(8,128)(2,1)S(1)} collective-permute-done((bf16[512,128]{1,0:T(8,128)(2,1)S(1)}, bf16[512,128]{1,0:T(8,128)(2,1)S(1)}, u32[]{:S(2)}, u32[]{:S(2)}) %collective-permute-start.15) | collective-permute-done | bytes 131104 | tf_op jit(solution)/shard_map/ppermute | solution.py:28
  31.5 1.9 %collective-permute-start.16 = (bf16[256,256]{1,0:T(8,128)(2,1)S(1)}, bf16[256,256]{1,0:T(8,128)(2,1)S(1)}, u32[]{:S(2)}, u32[]{:S(2)}) collective-permute-start(bf16[256,256]{1,0:T(8,128)(2,1)S(1)} %get-tuple-element.56), channel_id=1, source_target_pairs={{0,4},{1,3},{4,8},{5,1},{8,12},{9,5},{12,14},{13,9},{14,10},{15,13... | collective-permute-start | bytes 393224 | tf_op jit(solution)/shard_map/ppermute | solution.py:56
  33.4 1.2 %shard_map.97 = (f32[256,256]{1,0:T(8,128)S(1)}, f32[256,256]{1,0:T(8,128)S(1)}, f32[256,256]{1,0:T(8,128)S(1)}, f32[256,256]{1,0:T(8,128)S(1)}, f32[256,256]{1,...) custom-call(s32[9]{0:T(128)S(1)} %stack.39.starts, ...), custom_call_target="tpu_custom_call" | custom-call | flops 469762048 | bytes 1024 | tf_op jit(solution)/shard_map/pallas_call | solution.py:69
  34.9 1.8 %collective-permute-start.25 = (bf16[256,256]{1,0:T(8,128)(2,1)S(1)}, bf16[256,256]{1,0:T(8,128)(2,1)S(1)}, u32[]{:S(2)}, u32[]{:S(2)}) collective-permute-start(bf16[256,256]{1,0:T(8,128)(2,1)S(1)} %get-tuple-element.70), channel_id=1, source_target_pairs={{0,4},{1,3},{4,8},{5,1},{8,12},{9,5},{12,14},{13,9},{14,10},{15,13... | collective-permute-start | bytes 393224 | tf_op jit(solution)/shard_map/ppermute | solution.py:56
  37.5 2.1 %collective-permute-start.17 = (bf16[256,256]{1,0:T(8,128)(2,1)S(1)}, bf16[256,256]{1,0:T(8,128)(2,1)S(1)}, u32[]{:S(2)}, u32[]{:S(2)}) collective-permute-start(bf16[256,256]{1,0:T(8,128)(2,1)S(1)} %add_convert_fusion.9), channel_id=1, source_target_pairs={{0,4},{1,3},{4,8},{5,1},{8,12},{9,5},{12,14},{13,9},{14,10},{15,13... | collective-permute-start | bytes 393224 | tf_op jit(solution)/shard_map/ppermute | solution.py:56
  39.6 1.5 %collective-permute-done.20 = bf16[256,256]{1,0:T(8,128)(2,1)S(1)} collective-permute-done((bf16[256,256]{1,0:T(8,128)(2,1)S(1)}, bf16[256,256]{1,0:T(8,128)(2,1)S(1)}, u32[]{:S(2)}, u32[]{:S(2)}) %collective-permute-start.20) | collective-permute-done | bytes 131104 | tf_op jit(solution)/shard_map/ppermute | solution.py:56
  41.2 2.0 %collective-permute-start.26 = (bf16[256,256]{1,0:T(8,128)(2,1)S(1)}, bf16[256,256]{1,0:T(8,128)(2,1)S(1)}, u32[]{:S(2)}, u32[]{:S(2)}) collective-permute-start(bf16[256,256]{1,0:T(8,128)(2,1)S(1)} %add_convert_fusion.3), channel_id=1, source_target_pairs={{0,4},{1,3},{4,8},{5,1},{8,12},{9,5},{12,14},{13,9},{14,10},{15,13... | collective-permute-start | bytes 393224 | tf_op jit(solution)/shard_map/ppermute | solution.py:56
  44.0 1.9 %collective-permute-start.18 = (bf16[256,256]{1,0:T(8,128)(2,1)S(1)}, bf16[256,256]{1,0:T(8,128)(2,1)S(1)}, u32[]{:S(2)}, u32[]{:S(2)}) collective-permute-start(bf16[256,256]{1,0:T(8,128)(2,1)S(1)} %add_convert_fusion.8), channel_id=1, source_target_pairs={{0,4},{1,3},{4,8},{5,1},{8,12},{9,5},{12,14},{13,9},{14,10},{15,13... | collective-permute-start | bytes 393224 | tf_op jit(solution)/shard_map/ppermute | solution.py:56
  47.2 1.6 %collective-permute-start.27 = (bf16[256,256]{1,0:T(8,128)(2,1)S(1)}, bf16[256,256]{1,0:T(8,128)(2,1)S(1)}, u32[]{:S(2)}, u32[]{:S(2)}) collective-permute-start(bf16[256,256]{1,0:T(8,128)(2,1)S(1)} %add_convert_fusion.2), channel_id=1, source_target_pairs={{0,4},{1,3},{4,8},{5,1},{8,12},{9,5},{12,14},{13,9},{14,10},{15,13... | collective-permute-start | bytes 393224 | tf_op jit(solution)/shard_map/ppermute | solution.py:56
  49.7 1.4 %collective-permute-start.19 = (bf16[256,256]{1,0:T(8,128)(2,1)S(1)}, bf16[256,256]{1,0:T(8,128)(2,1)S(1)}, u32[]{:S(2)}, u32[]{:S(2)}) collective-permute-start(bf16[256,256]{1,0:T(8,128)(2,1)S(1)} %add_convert_fusion.7), channel_id=1, source_target_pairs={{0,4},{1,3},{4,8},{5,1},{8,12},{9,5},{12,14},{13,9},{14,10},{15,13... | collective-permute-start | bytes 393224 | tf_op jit(solution)/shard_map/ppermute | solution.py:56
  53.1 2.0 %collective-permute-done.19 = bf16[256,256]{1,0:T(8,128)(2,1)S(1)} collective-permute-done((bf16[256,256]{1,0:T(8,128)(2,1)S(1)}, bf16[256,256]{1,0:T(8,128)(2,1)S(1)}, u32[]{:S(2)}, u32[]{:S(2)}) %collective-permute-start.19) | collective-permute-done | bytes 131104 | tf_op jit(solution)/shard_map/ppermute | solution.py:56
  55.1 1.6 %collective-permute-start.34 = (bf16[256,256]{1,0:T(8,128)(2,1)S(1)}, bf16[256,256]{1,0:T(8,128)(2,1)S(1)}, u32[]{:S(2)}, u32[]{:S(2)}) collective-permute-start(bf16[256,256]{1,0:T(8,128)(2,1)S(1)} %multiply_convert_fusion.refs_1_), channel_id=1, source_target_pairs={{0,4},{1,3},{4,8},{5,1},{8,12},{9,5},{12,14},{13,9},{14,10},{15,13... | collective-permute-start | bytes 393224 | tf_op jit(solution)/shard_map/ppermute | solution.py:56
  57.3 1.5 %collective-permute-start.39 = (bf16[256,256]{1,0:T(8,128)(2,1)S(1)}, bf16[256,256]{1,0:T(8,128)(2,1)S(1)}, u32[]{:S(2)}, u32[]{:S(2)}) collective-permute-start(bf16[256,256]{1,0:T(8,128)(2,1)S(1)} %multiply_convert_fusion.refs_1_), channel_id=1, source_target_pairs={{0,2},{1,5},{4,0},{5,9},{8,4},{9,13},{12,8},{13,15},{14,12},{15,11... | collective-permute-start | bytes 393224 | tf_op jit(solution)/shard_map/ppermute | solution.py:56
  59.4 1.9 %collective-permute-done.34.refs_3_ = bf16[256,256]{1,0:T(8,128)(2,1)S(1)} collective-permute-done((bf16[256,256]{1,0:T(8,128)(2,1)S(1)}, bf16[256,256]{1,0:T(8,128)(2,1)S(1)}, u32[]{:S(2)}, u32[]{:S(2)}) %collective-permute-start.34) | collective-permute-done | bytes 131104 | tf_op jit(solution)/shard_map/ppermute | solution.py:56
  61.2 1.6 %collective-permute-start.35 = (bf16[256,256]{1,0:T(8,128)(2,1)S(1)}, bf16[256,256]{1,0:T(8,128)(2,1)S(1)}, u32[]{:S(2)}, u32[]{:S(2)}) collective-permute-start(bf16[256,256]{1,0:T(8,128)(2,1)S(1)} %collective-permute-done.34.refs_3_), channel_id=1, source_target_pairs={{0,4},{1,3},{4,8},{5,1},{8,12},{9,5},{12,14},{13,9},{14,10},{15,13... | collective-permute-start | bytes 393224 | tf_op jit(solution)/shard_map/ppermute | solution.py:56
  67.1 1.9 %collective-permute-start.36 = (bf16[256,256]{1,0:T(8,128)(2,1)S(1)}, bf16[256,256]{1,0:T(8,128)(2,1)S(1)}, u32[]{:S(2)}, u32[]{:S(2)}) collective-permute-start(bf16[256,256]{1,0:T(8,128)(2,1)S(1)} %collective-permute-done.35.refs_1_), channel_id=1, source_target_pairs={{0,4},{1,3},{4,8},{5,1},{8,12},{9,5},{12,14},{13,9},{14,10},{15,13... | collective-permute-start | bytes 393224 | tf_op jit(solution)/shard_map/ppermute | solution.py:56
  69.7 2.2 %collective-permute-done.41.refs_3_ = bf16[256,256]{1,0:T(8,128)(2,1)S(1)} collective-permute-done((bf16[256,256]{1,0:T(8,128)(2,1)S(1)}, bf16[256,256]{1,0:T(8,128)(2,1)S(1)}, u32[]{:S(2)}, u32[]{:S(2)}) %collective-permute-start.41) | collective-permute-done | bytes 131104 | tf_op jit(solution)/shard_map/ppermute | solution.py:56
  72.2 1.7 %collective-permute-start.42 = (bf16[256,256]{1,0:T(8,128)(2,1)S(1)}, bf16[256,256]{1,0:T(8,128)(2,1)S(1)}, u32[]{:S(2)}, u32[]{:S(2)}) collective-permute-start(bf16[256,256]{1,0:T(8,128)(2,1)S(1)} %collective-permute-done.40.refs_0_), channel_id=1, source_target_pairs={{0,4},{1,3},{4,8},{5,1},{8,12},{9,5},{12,14},{13,9},{14,10},{15,13... | collective-permute-start | bytes 393224 | tf_op jit(solution)/shard_map/ppermute | solution.py:56
  73.9 1.8 %collective-permute-start.37 = (bf16[256,256]{1,0:T(8,128)(2,1)S(1)}, bf16[256,256]{1,0:T(8,128)(2,1)S(1)}, u32[]{:S(2)}, u32[]{:S(2)}) collective-permute-start(bf16[256,256]{1,0:T(8,128)(2,1)S(1)} %collective-permute-done.36.refs_5_), channel_id=1, source_target_pairs={{0,4},{1,3},{4,8},{5,1},{8,12},{9,5},{12,14},{13,9},{14,10},{15,13... | collective-permute-start | bytes 393224 | tf_op jit(solution)/shard_map/ppermute | solution.py:56
  77.2 1.3 %shard_map.101 = (f32[4,256,256]{2,1,0:T(8,128)S(1)}, f32[2,256,256]{2,1,0:T(8,128)S(1)}) custom-call(s32[9]{0:T(128)S(1)} %stack.39.starts, bf16[256,256]{1,0:T(8,128)(2,1)S(1)} %collective-permute-done.40.refs_0_, bf16[256,256]{1,0:T(8,128)(2,1)S(1)} %collective-permute-done.35.refs_1_, bf16[256,256]{1,0:T(8,128)(2,1)S(1)} %collective-permute-done.31.refs_2_, ...), custom_call_target="tpu_custom_call" | custom-call | flops 268435456 | bytes 1024 | tf_op jit(solution)/shard_map/pallas_call | solution.py:69
  78.9 1.8 %collective-permute-done.33.refs_0_ = bf16[256,256]{1,0:T(8,128)(2,1)S(1)} collective-permute-done((bf16[256,256]{1,0:T(8,128)(2,1)S(1)}, bf16[256,256]{1,0:T(8,128)(2,1)S(1)}, u32[]{:S(2)}, u32[]{:S(2)}) %collective-permute-start.33) | collective-permute-done | bytes 131104 | tf_op jit(solution)/shard_map/ppermute | solution.py:56
  81.3 1.6 %shard_map.102 = (f32[512,128]{1,0:T(8,128)S(1)}, f32[1,128,2048]{2,1,0:T(8,128)}) custom-call(s32[9]{0:T(128)S(1)} %stack.39.starts, bf16[256,256]{1,0:T(8,128)(2,1)S(1)} %collective-permute-done.33.refs_0_, bf16[256,256]{1,0:T(8,128)(2,1)S(1)} %collective-permute-done.37.refs_1_, bf16[256,2048]{1,0:T(8,128)(2,1)S(1)} %pad_maximum_fusion.stacked.refs_6_.refs_8_.refs_2_, ...), custom_call_target="tpu_custom_call" | custom-call | bytes 1024 | tf_op jit(solution)/shard_map/pallas_call | solution.py:69
  83.0 2.7 %shard_map.104 = (f32[1,2048,128]{2,1,0:T(8,128)}, f32[1,128]{1,0:T(1,128)}, f32[128,1024]{1,0:T(8,128)}) custom-call(s32[9]{0:T(128)S(1)} %stack.39.starts, bf16[2048,512]{1,0:T(8,128)(2,1)S(1)} %shard_map.99.turned, f32[512,128]{1,0:T(8,128)S(1)} %get-tuple-element.66.preact, f32[512,128]{1,0:T(8,128)S(1)} %get-tuple-element.83.back_own, ...), custom_call_target="tpu_custom_call" | custom-call | flops 268435456 | bytes 1024 | tf_op jit(solution)/shard_map/pallas_call | solution.py:69
  (95 shorter events, 26.8 us)
Async XLA Ops:
  1.7 6.8 %collective-permute-start.5 = (bf16[256,256]{1,0:T(8,128)(2,1)S(1)}, bf16[256,256]{1,0:T(8,128)(2,1)S(1)}, u32[]{:S(2)}, u32[]{:S(2)}) collective-permute-start(bf16[256,256]{1,0:T(8,128)(2,1)S(1)} %get-tuple-element.48.shard.refs_1_), channel_id=1, source_target_pairs={{0,4},{1,3},{4,8},{5,1},{8,12},{9,5},{12,14},{13,9},{14,10},{15,13... | collective-permute-start | bytes 393224 | tf_op jit(solution)/shard_map/ppermute | solution.py:56
  4.8 6.3 %collective-permute-start.1 = (bf16[256,256]{1,0:T(8,128)(2,1)S(1)}, bf16[256,256]{1,0:T(8,128)(2,1)S(1)}, u32[]{:S(2)}, u32[]{:S(2)}) collective-permute-start(bf16[256,256]{1,0:T(8,128)(2,1)S(1)} %get-tuple-element.47.shard.refs_0_), channel_id=1, source_target_pairs={{0,2},{1,5},{4,0},{5,9},{8,4},{9,13},{12,8},{13,15},{14,12},{15,11... | collective-permute-start | bytes 393224 | tf_op jit(solution)/shard_map/ppermute | solution.py:56
  5.5 6.0 %collective-permute-start = (bf16[256,256]{1,0:T(8,128)(2,1)S(1)}, bf16[256,256]{1,0:T(8,128)(2,1)S(1)}, u32[]{:S(2)}, u32[]{:S(2)}) collective-permute-start(bf16[256,256]{1,0:T(8,128)(2,1)S(1)} %get-tuple-element.47.shard.refs_0_), channel_id=1, source_target_pairs={{0,4},{1,3},{4,8},{5,1},{8,12},{9,5},{12,14},{13,9},{14,10},{15,13... | collective-permute-start | bytes 393224 | tf_op jit(solution)/shard_map/ppermute | solution.py:56
  8.5 6.2 %collective-permute-start.6 = (bf16[256,256]{1,0:T(8,128)(2,1)S(1)}, bf16[256,256]{1,0:T(8,128)(2,1)S(1)}, u32[]{:S(2)}, u32[]{:S(2)}) collective-permute-start(bf16[256,256]{1,0:T(8,128)(2,1)S(1)} %collective-permute-done.5.refs_3_.refs_1_), channel_id=1, source_target_pairs={{0,4},{1,3},{4,8},{5,1},{8,12},{9,5},{12,14},{13,9},{14,10},{15,13... | collective-permute-start | bytes 393224 | tf_op jit(solution)/shard_map/ppermute | solution.py:56
  11.1 5.8 %collective-permute-start.2 = (bf16[256,256]{1,0:T(8,128)(2,1)S(1)}, bf16[256,256]{1,0:T(8,128)(2,1)S(1)}, u32[]{:S(2)}, u32[]{:S(2)}) collective-permute-start(bf16[256,256]{1,0:T(8,128)(2,1)S(1)} %collective-permute-done.1.refs_4_.refs_2_), channel_id=1, source_target_pairs={{0,2},{1,5},{4,0},{5,9},{8,4},{9,13},{12,8},{13,15},{14,12},{15,11... | collective-permute-start | bytes 393224 | tf_op jit(solution)/shard_map/ppermute | solution.py:56
  11.5 12.0 %collective-permute-start.14 = (bf16[128,1024]{1,0:T(8,128)(2,1)}, bf16[128,1024]{1,0:T(8,128)(2,1)S(1)}, u32[]{:S(2)}, u32[]{:S(2)}) collective-permute-start(bf16[128,1024]{1,0:T(8,128)(2,1)} %param.11), channel_id=1, source_target_pairs={{0,1},{1,0},{2,3},{3,2},{4,5},{5,4},{6,7},{7,6},{8,9},{9,8},{10,11... | collective-permute-start | bytes 786440 | tf_op jit(solution)/shard_map/ppermute | solution.py:28
  11.5 6.3 %collective-permute-start.10 = (bf16[256,256]{1,0:T(8,128)(2,1)S(1)}, bf16[256,256]{1,0:T(8,128)(2,1)S(1)}, u32[]{:S(2)}, u32[]{:S(2)}) collective-permute-start(bf16[256,256]{1,0:T(8,128)(2,1)S(1)} %collective-permute-done.refs_2_.refs_0_), channel_id=1, source_target_pairs={{0,4},{1,3},{4,8},{5,1},{8,12},{9,5},{12,14},{13,9},{14,10},{15,13... | collective-permute-start | bytes 393224 | tf_op jit(solution)/shard_map/ppermute | solution.py:56
  14.0 6.4 %collective-permute-start.11 = (bf16[256,256]{1,0:T(8,128)(2,1)S(1)}, bf16[256,256]{1,0:T(8,128)(2,1)S(1)}, u32[]{:S(2)}, u32[]{:S(2)}) collective-permute-start(bf16[256,256]{1,0:T(8,128)(2,1)S(1)} %collective-permute-done.9.refs_5_.refs_3_), channel_id=1, source_target_pairs={{0,2},{1,5},{4,0},{5,9},{8,4},{9,13},{12,8},{13,15},{14,12},{15,11... | collective-permute-start | bytes 393224 | tf_op jit(solution)/shard_map/ppermute | solution.py:56
  14.7 6.0 %collective-permute-start.7 = (bf16[256,256]{1,0:T(8,128)(2,1)S(1)}, bf16[256,256]{1,0:T(8,128)(2,1)S(1)}, u32[]{:S(2)}, u32[]{:S(2)}) collective-permute-start(bf16[256,256]{1,0:T(8,128)(2,1)S(1)} %collective-permute-done.6.refs_7_.refs_5_), channel_id=1, source_target_pairs={{0,4},{1,3},{4,8},{5,1},{8,12},{9,5},{12,14},{13,9},{14,10},{15,13... | collective-permute-start | bytes 393224 | tf_op jit(solution)/shard_map/ppermute | solution.py:56
  16.9 6.4 %collective-permute-start.3 = (bf16[256,256]{1,0:T(8,128)(2,1)S(1)}, bf16[256,256]{1,0:T(8,128)(2,1)S(1)}, u32[]{:S(2)}, u32[]{:S(2)}) collective-permute-start(bf16[256,256]{1,0:T(8,128)(2,1)S(1)} %collective-permute-done.2.refs_8_.refs_6_), channel_id=1, source_target_pairs={{0,2},{1,5},{4,0},{5,9},{8,4},{9,13},{12,8},{13,15},{14,12},{15,11... | collective-permute-start | bytes 393224 | tf_op jit(solution)/shard_map/ppermute | solution.py:56
  17.8 6.9 %collective-permute-start.12 = (bf16[256,256]{1,0:T(8,128)(2,1)S(1)}, bf16[256,256]{1,0:T(8,128)(2,1)S(1)}, u32[]{:S(2)}, u32[]{:S(2)}) collective-permute-start(bf16[256,256]{1,0:T(8,128)(2,1)S(1)} %collective-permute-done.10.refs_6_.refs_4_), channel_id=1, source_target_pairs={{0,4},{1,3},{4,8},{5,1},{8,12},{9,5},{12,14},{13,9},{14,10},{15,13... | collective-permute-start | bytes 393224 | tf_op jit(solution)/shard_map/ppermute | solution.py:56
  20.8 6.3 %collective-permute-start.8 = (bf16[256,256]{1,0:T(8,128)(2,1)S(1)}, bf16[256,256]{1,0:T(8,128)(2,1)S(1)}, u32[]{:S(2)}, u32[]{:S(2)}) collective-permute-start(bf16[256,256]{1,0:T(8,128)(2,1)S(1)} %collective-permute-done.7.refs_11_.refs_9_), channel_id=1, source_target_pairs={{0,4},{1,3},{4,8},{5,1},{8,12},{9,5},{12,14},{13,9},{14,10},{15,13... | collective-permute-start | bytes 393224 | tf_op jit(solution)/shard_map/ppermute | solution.py:56
  31.3 6.1 %collective-permute-start.21 = (bf16[256,256]{1,0:T(8,128)(2,1)S(1)}, bf16[256,256]{1,0:T(8,128)(2,1)S(1)}, u32[]{:S(2)}, u32[]{:S(2)}) collective-permute-start(bf16[256,256]{1,0:T(8,128)(2,1)S(1)} %get-tuple-element.60), channel_id=1, source_target_pairs={{0,2},{1,5},{4,0},{5,9},{8,4},{9,13},{12,8},{13,15},{14,12},{15,11... | collective-permute-start | bytes 393224 | tf_op jit(solution)/shard_map/ppermute | solution.py:56
  31.5 5.9 %collective-permute-start.16 = (bf16[256,256]{1,0:T(8,128)(2,1)S(1)}, bf16[256,256]{1,0:T(8,128)(2,1)S(1)}, u32[]{:S(2)}, u32[]{:S(2)}) collective-permute-start(bf16[256,256]{1,0:T(8,128)(2,1)S(1)} %get-tuple-element.56), channel_id=1, source_target_pairs={{0,4},{1,3},{4,8},{5,1},{8,12},{9,5},{12,14},{13,9},{14,10},{15,13... | collective-permute-start | bytes 393224 | tf_op jit(solution)/shard_map/ppermute | solution.py:56
  34.6 6.4 %collective-permute-start.20 = (bf16[256,256]{1,0:T(8,128)(2,1)S(1)}, bf16[256,256]{1,0:T(8,128)(2,1)S(1)}, u32[]{:S(2)}, u32[]{:S(2)}) collective-permute-start(bf16[256,256]{1,0:T(8,128)(2,1)S(1)} %get-tuple-element.59), channel_id=1, source_target_pairs={{0,2},{1,5},{4,0},{5,9},{8,4},{9,13},{12,8},{13,15},{14,12},{15,11... | collective-permute-start | bytes 393224 | tf_op jit(solution)/shard_map/ppermute | solution.py:56
  34.9 6.3 %collective-permute-start.25 = (bf16[256,256]{1,0:T(8,128)(2,1)S(1)}, bf16[256,256]{1,0:T(8,128)(2,1)S(1)}, u32[]{:S(2)}, u32[]{:S(2)}) collective-permute-start(bf16[256,256]{1,0:T(8,128)(2,1)S(1)} %get-tuple-element.70), channel_id=1, source_target_pairs={{0,4},{1,3},{4,8},{5,1},{8,12},{9,5},{12,14},{13,9},{14,10},{15,13... | collective-permute-start | bytes 393224 | tf_op jit(solution)/shard_map/ppermute | solution.py:56
  37.4 6.4 %collective-permute-start.23 = (bf16[256,256]{1,0:T(8,128)(2,1)S(1)}, bf16[256,256]{1,0:T(8,128)(2,1)S(1)}, u32[]{:S(2)}, u32[]{:S(2)}) collective-permute-start(bf16[256,256]{1,0:T(8,128)(2,1)S(1)} %add_convert_fusion.4), channel_id=1, source_target_pairs={{0,2},{1,5},{4,0},{5,9},{8,4},{9,13},{12,8},{13,15},{14,12},{15,11... | collective-permute-start | bytes 393224 | tf_op jit(solution)/shard_map/ppermute | solution.py:56
  37.5 6.5 %collective-permute-start.17 = (bf16[256,256]{1,0:T(8,128)(2,1)S(1)}, bf16[256,256]{1,0:T(8,128)(2,1)S(1)}, u32[]{:S(2)}, u32[]{:S(2)}) collective-permute-start(bf16[256,256]{1,0:T(8,128)(2,1)S(1)} %add_convert_fusion.9), channel_id=1, source_target_pairs={{0,4},{1,3},{4,8},{5,1},{8,12},{9,5},{12,14},{13,9},{14,10},{15,13... | collective-permute-start | bytes 393224 | tf_op jit(solution)/shard_map/ppermute | solution.py:56
  41.2 6.0 %collective-permute-start.26 = (bf16[256,256]{1,0:T(8,128)(2,1)S(1)}, bf16[256,256]{1,0:T(8,128)(2,1)S(1)}, u32[]{:S(2)}, u32[]{:S(2)}) collective-permute-start(bf16[256,256]{1,0:T(8,128)(2,1)S(1)} %add_convert_fusion.3), channel_id=1, source_target_pairs={{0,4},{1,3},{4,8},{5,1},{8,12},{9,5},{12,14},{13,9},{14,10},{15,13... | collective-permute-start | bytes 393224 | tf_op jit(solution)/shard_map/ppermute | solution.py:56
  43.8 7.3 %collective-permute-start.28 = (bf16[256,256]{1,0:T(8,128)(2,1)S(1)}, bf16[256,256]{1,0:T(8,128)(2,1)S(1)}, u32[]{:S(2)}, u32[]{:S(2)}) collective-permute-start(bf16[256,256]{1,0:T(8,128)(2,1)S(1)} %add_convert_fusion.1), channel_id=1, source_target_pairs={{0,2},{1,5},{4,0},{5,9},{8,4},{9,13},{12,8},{13,15},{14,12},{15,11... | collective-permute-start | bytes 393224 | tf_op jit(solution)/shard_map/ppermute | solution.py:56
  46.6 6.5 %collective-permute-start.24 = (bf16[256,256]{1,0:T(8,128)(2,1)S(1)}, bf16[256,256]{1,0:T(8,128)(2,1)S(1)}, u32[]{:S(2)}, u32[]{:S(2)}) collective-permute-start(bf16[256,256]{1,0:T(8,128)(2,1)S(1)} %add_convert_fusion.5), channel_id=1, source_target_pairs={{0,2},{1,5},{4,0},{5,9},{8,4},{9,13},{12,8},{13,15},{14,12},{15,11... | collective-permute-start | bytes 393224 | tf_op jit(solution)/shard_map/ppermute | solution.py:56
  47.2 9.5 %collective-permute-start.27 = (bf16[256,256]{1,0:T(8,128)(2,1)S(1)}, bf16[256,256]{1,0:T(8,128)(2,1)S(1)}, u32[]{:S(2)}, u32[]{:S(2)}) collective-permute-start(bf16[256,256]{1,0:T(8,128)(2,1)S(1)} %add_convert_fusion.2), channel_id=1, source_target_pairs={{0,4},{1,3},{4,8},{5,1},{8,12},{9,5},{12,14},{13,9},{14,10},{15,13... | collective-permute-start | bytes 393224 | tf_op jit(solution)/shard_map/ppermute | solution.py:56
  55.1 6.1 %collective-permute-start.34 = (bf16[256,256]{1,0:T(8,128)(2,1)S(1)}, bf16[256,256]{1,0:T(8,128)(2,1)S(1)}, u32[]{:S(2)}, u32[]{:S(2)}) collective-permute-start(bf16[256,256]{1,0:T(8,128)(2,1)S(1)} %multiply_convert_fusion.refs_1_), channel_id=1, source_target_pairs={{0,4},{1,3},{4,8},{5,1},{8,12},{9,5},{12,14},{13,9},{14,10},{15,13... | collective-permute-start | bytes 393224 | tf_op jit(solution)/shard_map/ppermute | solution.py:56
  56.8 6.5 %collective-permute-start.30 = (bf16[256,256]{1,0:T(8,128)(2,1)S(1)}, bf16[256,256]{1,0:T(8,128)(2,1)S(1)}, u32[]{:S(2)}, u32[]{:S(2)}) collective-permute-start(bf16[256,256]{1,0:T(8,128)(2,1)S(1)} %fusion.1.refs_0_), channel_id=1, source_target_pairs={{0,2},{1,5},{4,0},{5,9},{8,4},{9,13},{12,8},{13,15},{14,12},{15,11... | collective-permute-start | bytes 393224 | tf_op jit(solution)/shard_map/ppermute | solution.py:56
  57.3 7.8 %collective-permute-start.39 = (bf16[256,256]{1,0:T(8,128)(2,1)S(1)}, bf16[256,256]{1,0:T(8,128)(2,1)S(1)}, u32[]{:S(2)}, u32[]{:S(2)}) collective-permute-start(bf16[256,256]{1,0:T(8,128)(2,1)S(1)} %multiply_convert_fusion.refs_1_), channel_id=1, source_target_pairs={{0,2},{1,5},{4,0},{5,9},{8,4},{9,13},{12,8},{13,15},{14,12},{15,11... | collective-permute-start | bytes 393224 | tf_op jit(solution)/shard_map/ppermute | solution.py:56
  58.8 7.1 %collective-permute-start.38 = (bf16[256,256]{1,0:T(8,128)(2,1)S(1)}, bf16[256,256]{1,0:T(8,128)(2,1)S(1)}, u32[]{:S(2)}, u32[]{:S(2)}) collective-permute-start(bf16[256,256]{1,0:T(8,128)(2,1)S(1)} %fusion.1.refs_0_), channel_id=1, source_target_pairs={{0,4},{1,3},{4,8},{5,1},{8,12},{9,5},{12,14},{13,9},{14,10},{15,13... | collective-permute-start | bytes 393224 | tf_op jit(solution)/shard_map/ppermute | solution.py:56
  61.2 5.9 %collective-permute-start.35 = (bf16[256,256]{1,0:T(8,128)(2,1)S(1)}, bf16[256,256]{1,0:T(8,128)(2,1)S(1)}, u32[]{:S(2)}, u32[]{:S(2)}) collective-permute-start(bf16[256,256]{1,0:T(8,128)(2,1)S(1)} %collective-permute-done.34.refs_3_), channel_id=1, source_target_pairs={{0,4},{1,3},{4,8},{5,1},{8,12},{9,5},{12,14},{13,9},{14,10},{15,13... | collective-permute-start | bytes 393224 | tf_op jit(solution)/shard_map/ppermute | solution.py:56
  63.2 6.1 %collective-permute-start.31 = (bf16[256,256]{1,0:T(8,128)(2,1)S(1)}, bf16[256,256]{1,0:T(8,128)(2,1)S(1)}, u32[]{:S(2)}, u32[]{:S(2)}) collective-permute-start(bf16[256,256]{1,0:T(8,128)(2,1)S(1)} %collective-permute-done.30.refs_4_), channel_id=1, source_target_pairs={{0,2},{1,5},{4,0},{5,9},{8,4},{9,13},{12,8},{13,15},{14,12},{15,11... | collective-permute-start | bytes 393224 | tf_op jit(solution)/shard_map/ppermute | solution.py:56
  65.1 6.8 %collective-permute-start.41 = (bf16[256,256]{1,0:T(8,128)(2,1)S(1)}, bf16[256,256]{1,0:T(8,128)(2,1)S(1)}, u32[]{:S(2)}, u32[]{:S(2)}) collective-permute-start(bf16[256,256]{1,0:T(8,128)(2,1)S(1)} %collective-permute-done.39.refs_5_), channel_id=1, source_target_pairs={{0,2},{1,5},{4,0},{5,9},{8,4},{9,13},{12,8},{13,15},{14,12},{15,11... | collective-permute-start | bytes 393224 | tf_op jit(solution)/shard_map/ppermute | solution.py:56
  66.0 6.2 %collective-permute-start.40 = (bf16[256,256]{1,0:T(8,128)(2,1)S(1)}, bf16[256,256]{1,0:T(8,128)(2,1)S(1)}, u32[]{:S(2)}, u32[]{:S(2)}) collective-permute-start(bf16[256,256]{1,0:T(8,128)(2,1)S(1)} %collective-permute-done.38.refs_2_), channel_id=1, source_target_pairs={{0,4},{1,3},{4,8},{5,1},{8,12},{9,5},{12,14},{13,9},{14,10},{15,13... | collective-permute-start | bytes 393224 | tf_op jit(solution)/shard_map/ppermute | solution.py:56
  67.1 6.8 %collective-permute-start.36 = (bf16[256,256]{1,0:T(8,128)(2,1)S(1)}, bf16[256,256]{1,0:T(8,128)(2,1)S(1)}, u32[]{:S(2)}, u32[]{:S(2)}) collective-permute-start(bf16[256,256]{1,0:T(8,128)(2,1)S(1)} %collective-permute-done.35.refs_1_), channel_id=1, source_target_pairs={{0,4},{1,3},{4,8},{5,1},{8,12},{9,5},{12,14},{13,9},{14,10},{15,13... | collective-permute-start | bytes 393224 | tf_op jit(solution)/shard_map/ppermute | solution.py:56
  69.3 6.4 %collective-permute-start.32 = (bf16[256,256]{1,0:T(8,128)(2,1)S(1)}, bf16[256,256]{1,0:T(8,128)(2,1)S(1)}, u32[]{:S(2)}, u32[]{:S(2)}) collective-permute-start(bf16[256,256]{1,0:T(8,128)(2,1)S(1)} %collective-permute-done.31.refs_2_), channel_id=1, source_target_pairs={{0,2},{1,5},{4,0},{5,9},{8,4},{9,13},{12,8},{13,15},{14,12},{15,11... | collective-permute-start | bytes 393224 | tf_op jit(solution)/shard_map/ppermute | solution.py:56
  (17 other events, 140.8 us)

commit v21 on v20

--- a/solution.py
+++ b/solution.py
@@ -312,7 +312,11 @@
 
     rest = tuple(slot for slot in range(size) if slot != far)
     instant = tuple({far: BF16, (slot_q if way == 1 else slot_p).get(reach - 1): BF16} for _, way in later)
-    far_0, far_1 = spread((far,), instant, False)
+    block = lax.dynamic_slice_in_dim(stacked, starts[far], wide, 1)
+    far_0, far_1 = [
+        [(matmul(now, block[:lat]) + matmul(before, block[lat:])).astype(BF16)]
+        for now, before in zip(halves(codes), halves(earlier))
+    ]
     moving = {loop: hop(message, loop[1]) for loop, message in zip(urgent, (far_0[0], far_1[0]))}
     partial, both_t = [], []
     for pieces in spread(rest, instant, True):
@@ -355,12 +359,12 @@
         0,
         [starts] + turned_own + arrived + both_chains(inputs, range(1, size))[1:],
     )[0]
+    groups = [group for group in ((0,), tuple(range(1, far))) if group]
+    outer, acc = back(groups[0], None)
+    outers = [outer]
     for s in range(1, reach + 1):
-        gather_step(errors, s, (turned, turned) if s == 2 else None)
-    cut = 1 + 2 * min(1, reach - 1)
-    groups = [group for group in (tuple(range(cut)), tuple(range(cut, far))) if group]
-    outers, acc = [], None
-    for group in groups:
+        gather_step(errors, s, (turned, acc) if s == 1 else None)
+    for group in groups[1:]:
         outer, acc = back(group, acc)
         outers.append(outer)
     last = both_chains(errors, (far,)) + [stacked] + both_t + outers + [acc]

time: 85.9 us -> 88.8 us (1.034)
  waiting for transfers between devices: 22.6 us -> 17.7 us
  matrix products: 0 us -> 2.35 us
  other arithmetic: 1.56 us -> 3.66 us
  starting transfers between devices: 46 us -> 47.6 us
  local copies, waits for them, and re-layouts: 1.16 us -> 2.44 us
    ppermute x42, waiting for transfers between devices: 21.2 us -> 17.6 us  [hop(): return lax.ppermute(shard, ('latent', 'layer'), pairs)]
    dot_general x0 -> x4, matrix products: none -> 2.35 us  [matmul(): return lax.dot_general(a, b, dims, preferred_element_type=F32)]
    concatenate x1 -> x2, other arithmetic: 0.09 us -> 2.18 us  [ring_shards(): stacked = jnp.concatenate([dec_same[0], cross], axis=0)]
    ppermute x42, starting transfers between devices: 45.9 us -> 47.6 us  [hop(): return lax.ppermute(shard, ('latent', 'layer'), pairs)]
    ppermute x3, waiting for transfers between devices: 1.39 us -> 0.12 us  [swapped(): lax.ppermute(shard, 'layer', [(i, size - 1 - i) for i in range(size)])]
    pallas_call x12 -> x11, Pallas kernels: 13.5 us -> 13.7 us  [call(): pl.pallas_call(kernel, out_shape=outs, in_specs=[spec(pltpu.SMEM)] + [spe...]
  transfers between devices with their start and end apart: 45 -> 45, of which waited for: 28 -> 23; matrix products, arithmetic and copies ran while one was open for 2% -> 6% of each run, Pallas kernels for 10% -> 10%
where the time goes in v21:
time: 88.8 us; the launch traced here: 88.5 us
  starting transfers between devices  47.6 us (54%)
  waiting for transfers between devices  17.7 us (20%)
  Pallas kernels  13.7 us (15%)
  other arithmetic  3.66 us (4%)
  local copies, waits for them, and re-layouts  2.44 us (3%)
  matrix products  2.35 us (3%)
  between operations  0.97 us (1%)
    ppermute x42, starting transfers between devices, hop(): return lax.ppermute(shard, ('latent', 'layer'), pairs)  47.6 us
    ppermute x42, waiting for transfers between devices, hop(): return lax.ppermute(shard, ('latent', 'layer'), pairs)  17.6 us
    pallas_call x11, Pallas kernels, call(): pl.pallas_call(kernel, out_shape=outs, in_specs=[spec(pltpu.SMEM)] + [spe...  13.7 us
    dot_general x4, matrix products, matmul(): return lax.dot_general(a, b, dims, preferred_element_type=F32)  2.35 us
    concatenate x2, other arithmetic, ring_shards(): stacked = jnp.concatenate([dec_same[0], cross], axis=0)  2.18 us
  transfers between devices with their start and end apart: 45, of which 23 were waited for; matrix products, arithmetic and copies ran while one was open for 6% of the time, Pallas kernels for 10%

profile of v21, /device:TPU:0, one launch (start us, length us, event | category | flops | bytes accessed | tf_op | source)
XLA Modules:
  0.0 88.5 jit_solution(11270187914478289024)
XLA Ops:
  1.6 3.1 %collective-permute-start.5 = (bf16[256,256]{1,0:T(8,128)(2,1)S(1)}, bf16[256,256]{1,0:T(8,128)(2,1)S(1)}, u32[]{:S(2)}, u32[]{:S(2)}) collective-permute-start(bf16[256,256]{1,0:T(8,128)(2,1)S(1)} %get-tuple-element.46.shard.refs_1_), channel_id=1, source_target_pairs={{0,4},{1,3},{4,8},{5,1},{8,12},{9,5},{12,14},{13,9},{14,10},{15,13... | collective-permute-start | bytes 393224 | tf_op jit(solution)/shard_map/ppermute | solution.py:56
  5.4 2.1 %collective-permute-start = (bf16[256,256]{1,0:T(8,128)(2,1)S(1)}, bf16[256,256]{1,0:T(8,128)(2,1)S(1)}, u32[]{:S(2)}, u32[]{:S(2)}) collective-permute-start(bf16[256,256]{1,0:T(8,128)(2,1)S(1)} %get-tuple-element.45.shard.refs_0_), channel_id=1, source_target_pairs={{0,4},{1,3},{4,8},{5,1},{8,12},{9,5},{12,14},{13,9},{14,10},{15,13... | collective-permute-start | bytes 393224 | tf_op jit(solution)/shard_map/ppermute | solution.py:56
  8.8 2.0 %collective-permute-start.6 = (bf16[256,256]{1,0:T(8,128)(2,1)S(1)}, bf16[256,256]{1,0:T(8,128)(2,1)S(1)}, u32[]{:S(2)}, u32[]{:S(2)}) collective-permute-start(bf16[256,256]{1,0:T(8,128)(2,1)S(1)} %collective-permute-done.5.refs_3_.refs_1_), channel_id=1, source_target_pairs={{0,4},{1,3},{4,8},{5,1},{8,12},{9,5},{12,14},{13,9},{14,10},{15,13... | collective-permute-start | bytes 393224 | tf_op jit(solution)/shard_map/ppermute | solution.py:56
  11.3 2.5 %collective-permute-start.10 = (bf16[256,256]{1,0:T(8,128)(2,1)S(1)}, bf16[256,256]{1,0:T(8,128)(2,1)S(1)}, u32[]{:S(2)}, u32[]{:S(2)}) collective-permute-start(bf16[256,256]{1,0:T(8,128)(2,1)S(1)} %collective-permute-done.refs_2_.refs_0_), channel_id=1, source_target_pairs={{0,4},{1,3},{4,8},{5,1},{8,12},{9,5},{12,14},{13,9},{14,10},{15,13... | collective-permute-start | bytes 393224 | tf_op jit(solution)/shard_map/ppermute | solution.py:56
  14.9 1.5 %collective-permute-start.7 = (bf16[256,256]{1,0:T(8,128)(2,1)S(1)}, bf16[256,256]{1,0:T(8,128)(2,1)S(1)}, u32[]{:S(2)}, u32[]{:S(2)}) collective-permute-start(bf16[256,256]{1,0:T(8,128)(2,1)S(1)} %collective-permute-done.6.refs_7_.refs_5_), channel_id=1, source_target_pairs={{0,4},{1,3},{4,8},{5,1},{8,12},{9,5},{12,14},{13,9},{14,10},{15,13... | collective-permute-start | bytes 393224 | tf_op jit(solution)/shard_map/ppermute | solution.py:56
  17.6 2.5 %collective-permute-start.12 = (bf16[256,256]{1,0:T(8,128)(2,1)S(1)}, bf16[256,256]{1,0:T(8,128)(2,1)S(1)}, u32[]{:S(2)}, u32[]{:S(2)}) collective-permute-start(bf16[256,256]{1,0:T(8,128)(2,1)S(1)} %collective-permute-done.10.refs_6_.refs_4_), channel_id=1, source_target_pairs={{0,4},{1,3},{4,8},{5,1},{8,12},{9,5},{12,14},{13,9},{14,10},{15,13... | collective-permute-start | bytes 393224 | tf_op jit(solution)/shard_map/ppermute | solution.py:56
  20.6 2.4 %collective-permute-start.8 = (bf16[256,256]{1,0:T(8,128)(2,1)S(1)}, bf16[256,256]{1,0:T(8,128)(2,1)S(1)}, u32[]{:S(2)}, u32[]{:S(2)}) collective-permute-start(bf16[256,256]{1,0:T(8,128)(2,1)S(1)} %collective-permute-done.7.refs_11_.refs_9_), channel_id=1, source_target_pairs={{0,4},{1,3},{4,8},{5,1},{8,12},{9,5},{12,14},{13,9},{14,10},{15,13... | collective-permute-start | bytes 393224 | tf_op jit(solution)/shard_map/ppermute | solution.py:56
  24.4 1.3 %pad_maximum_fusion.stacked.refs_2_.refs_12_ = bf16[256,2048]{1,0:T(8,128)(2,1)S(1)} fusion(bf16[128,2048]{1,0:T(8,128)(2,1)S(1)} %maximum_select_fusion, bf16[128,2048]{1,0:T(8,128)(2,1)} %bitcast.19), kind=kLoop, calls=%fused_computation.1 | loop fusion | flops 2097152 | bytes 2097152 | tf_op jit(solution)/shard_map/concatenate | solution.py:298
  25.8 1.2 %shard_map.95.refs_3_ = f32[512,128]{1,0:T(8,128)S(1)} custom-call(s32[9]{0:T(128)S(1)} %stack.39.starts, bf16[256,256]{1,0:T(8,128)(2,1)S(1)} %get-tuple-element.45.shard.refs_0_, bf16[256,256]{1,0:T(8,128)(2,1)S(1)} %get-tuple-element.46.shard.refs_1_, bf16[256,256]{1,0:T(8,128)(2,1)S(1)} %collective-permute-done.refs_2_.refs_0_, ...), custom_call_target="tpu_custom_call" | custom-call | flops 234881024 | bytes 1024 | tf_op jit(solution)/shard_map/pallas_call | solution.py:69
  27.0 1.1 %collective-permute-done.4.refs_0_.refs_12_ = bf16[256,256]{1,0:T(8,128)(2,1)S(1)} collective-permute-done((bf16[256,256]{1,0:T(8,128)(2,1)S(1)}, bf16[256,256]{1,0:T(8,128)(2,1)S(1)}, u32[]{:S(2)}, u32[]{:S(2)}) %collective-permute-start.4) | collective-permute-done | bytes 131104 | tf_op jit(solution)/shard_map/ppermute | solution.py:56
  28.0 1.4 %shard_map.96 = (f32[512,128]{1,0:T(8,128)S(1)}, bf16[512,128]{1,0:T(8,128)(2,1)}) custom-call(s32[9]{0:T(128)S(1)} %stack.39.starts, bf16[256,256]{1,0:T(8,128)(2,1)S(1)} %collective-permute-done.4.refs_0_.refs_12_, bf16[256,256]{1,0:T(8,128)(2,1)S(1)} %collective-permute-done.8.refs_1_.refs_13_, bf16[1,2048,128]{2,1,0:T(8,128)(2,1)S(1)} %copy-done, ...), custom_call_target="tpu_custom_call" | custom-call | flops 33554432 | bytes 1024 | tf_op jit(solution)/shard_map/pallas_call | solution.py:69
  34.1 1.4 %collective-permute-start.16 = (bf16[256,256]{1,0:T(8,128)(2,1)S(1)}, bf16[256,256]{1,0:T(8,128)(2,1)S(1)}, u32[]{:S(2)}, u32[]{:S(2)}) collective-permute-start(bf16[256,256]{1,0:T(8,128)(2,1)S(1)} %fusion), channel_id=1, source_target_pairs={{0,4},{1,3},{4,8},{5,1},{8,12},{9,5},{12,14},{13,9},{14,10},{15,13... | collective-permute-start | bytes 393224 | tf_op jit(solution)/shard_map/ppermute | solution.py:56
  35.6 1.6 %shard_map.97 = (f32[256,256]{1,0:T(8,128)S(1)}, f32[256,256]{1,0:T(8,128)S(1)}, f32[256,256]{1,0:T(8,128)S(1)}, f32[256,256]{1,0:T(8,128)S(1)}, f32[256,256]{1,...) custom-call(s32[9]{0:T(128)S(1)} %stack.39.starts, ...), custom_call_target="tpu_custom_call" | custom-call | flops 469762048 | bytes 1024 | tf_op jit(solution)/shard_map/pallas_call | solution.py:69
  38.0 1.2 %collective-permute-start.25 = (bf16[256,256]{1,0:T(8,128)(2,1)S(1)}, bf16[256,256]{1,0:T(8,128)(2,1)S(1)}, u32[]{:S(2)}, u32[]{:S(2)}) collective-permute-start(bf16[256,256]{1,0:T(8,128)(2,1)S(1)} %get-tuple-element.66), channel_id=1, source_target_pairs={{0,4},{1,3},{4,8},{5,1},{8,12},{9,5},{12,14},{13,9},{14,10},{15,13... | collective-permute-start | bytes 393224 | tf_op jit(solution)/shard_map/ppermute | solution.py:56
  40.2 1.2 %collective-permute-start.17 = (bf16[256,256]{1,0:T(8,128)(2,1)S(1)}, bf16[256,256]{1,0:T(8,128)(2,1)S(1)}, u32[]{:S(2)}, u32[]{:S(2)}) collective-permute-start(bf16[256,256]{1,0:T(8,128)(2,1)S(1)} %add_convert_fusion.9), channel_id=1, source_target_pairs={{0,4},{1,3},{4,8},{5,1},{8,12},{9,5},{12,14},{13,9},{14,10},{15,13... | collective-permute-start | bytes 393224 | tf_op jit(solution)/shard_map/ppermute | solution.py:56
  41.4 2.0 %collective-permute-done.20 = bf16[256,256]{1,0:T(8,128)(2,1)S(1)} collective-permute-done((bf16[256,256]{1,0:T(8,128)(2,1)S(1)}, bf16[256,256]{1,0:T(8,128)(2,1)S(1)}, u32[]{:S(2)}, u32[]{:S(2)}) %collective-permute-start.20) | collective-permute-done | bytes 131104 | tf_op jit(solution)/shard_map/ppermute | solution.py:56
  44.5 1.2 %collective-permute-start.26 = (bf16[256,256]{1,0:T(8,128)(2,1)S(1)}, bf16[256,256]{1,0:T(8,128)(2,1)S(1)}, u32[]{:S(2)}, u32[]{:S(2)}) collective-permute-start(bf16[256,256]{1,0:T(8,128)(2,1)S(1)} %add_convert_fusion.3), channel_id=1, source_target_pairs={{0,4},{1,3},{4,8},{5,1},{8,12},{9,5},{12,14},{13,9},{14,10},{15,13... | collective-permute-start | bytes 393224 | tf_op jit(solution)/shard_map/ppermute | solution.py:56
  47.3 1.1 %collective-permute-start.18 = (bf16[256,256]{1,0:T(8,128)(2,1)S(1)}, bf16[256,256]{1,0:T(8,128)(2,1)S(1)}, u32[]{:S(2)}, u32[]{:S(2)}) collective-permute-start(bf16[256,256]{1,0:T(8,128)(2,1)S(1)} %add_convert_fusion.8), channel_id=1, source_target_pairs={{0,4},{1,3},{4,8},{5,1},{8,12},{9,5},{12,14},{13,9},{14,10},{15,13... | collective-permute-start | bytes 393224 | tf_op jit(solution)/shard_map/ppermute | solution.py:56
  50.4 1.2 %collective-permute-start.27 = (bf16[256,256]{1,0:T(8,128)(2,1)S(1)}, bf16[256,256]{1,0:T(8,128)(2,1)S(1)}, u32[]{:S(2)}, u32[]{:S(2)}) collective-permute-start(bf16[256,256]{1,0:T(8,128)(2,1)S(1)} %add_convert_fusion.2), channel_id=1, source_target_pairs={{0,4},{1,3},{4,8},{5,1},{8,12},{9,5},{12,14},{13,9},{14,10},{15,13... | collective-permute-start | bytes 393224 | tf_op jit(solution)/shard_map/ppermute | solution.py:56
  52.5 1.5 %collective-permute-start.19 = (bf16[256,256]{1,0:T(8,128)(2,1)S(1)}, bf16[256,256]{1,0:T(8,128)(2,1)S(1)}, u32[]{:S(2)}, u32[]{:S(2)}) collective-permute-start(bf16[256,256]{1,0:T(8,128)(2,1)S(1)} %add_convert_fusion.7), channel_id=1, source_target_pairs={{0,4},{1,3},{4,8},{5,1},{8,12},{9,5},{12,14},{13,9},{14,10},{15,13... | collective-permute-start | bytes 393224 | tf_op jit(solution)/shard_map/ppermute | solution.py:56
  55.4 3.3 %collective-permute-done.19 = bf16[256,256]{1,0:T(8,128)(2,1)S(1)} collective-permute-done((bf16[256,256]{1,0:T(8,128)(2,1)S(1)}, bf16[256,256]{1,0:T(8,128)(2,1)S(1)}, u32[]{:S(2)}, u32[]{:S(2)}) %collective-permute-start.19) | collective-permute-done | bytes 131104 | tf_op jit(solution)/shard_map/ppermute | solution.py:56
  59.6 1.4 %collective-permute-start.30 = (bf16[256,256]{1,0:T(8,128)(2,1)S(1)}, bf16[256,256]{1,0:T(8,128)(2,1)S(1)}, u32[]{:S(2)}, u32[]{:S(2)}) collective-permute-start(bf16[256,256]{1,0:T(8,128)(2,1)S(1)} %fusion.3.refs_0_), channel_id=1, source_target_pairs={{0,2},{1,5},{4,0},{5,9},{8,4},{9,13},{12,8},{13,15},{14,12},{15,11... | collective-permute-start | bytes 393224 | tf_op jit(solution)/shard_map/ppermute | solution.py:56
  61.0 1.1 %shard_map.98.turned = bf16[2048,512]{1,0:T(8,128)(2,1)S(1)} custom-call(s32[9]{0:T(128)S(1)} %stack.39.starts, bf16[256,256]{1,0:T(8,128)(2,1)S(1)} %shard_map.93.own_0, bf16[256,256]{1,0:T(8,128)(2,1)S(1)} %copy-done.2, bf16[256,256]{1,0:T(8,128)(2,1)S(1)} %collective-permute-done.refs_2_.refs_0_, ...), custom_call_target="tpu_custom_call" | custom-call | bytes 1024 | tf_op jit(solution)/shard_map/pallas_call | solution.py:69
  63.7 1.4 %collective-permute-start.39 = (bf16[256,256]{1,0:T(8,128)(2,1)S(1)}, bf16[256,256]{1,0:T(8,128)(2,1)S(1)}, u32[]{:S(2)}, u32[]{:S(2)}) collective-permute-start(bf16[256,256]{1,0:T(8,128)(2,1)S(1)} %multiply_convert_fusion.refs_1_), channel_id=1, source_target_pairs={{0,2},{1,5},{4,0},{5,9},{8,4},{9,13},{12,8},{13,15},{14,12},{15,11... | collective-permute-start | bytes 393224 | tf_op jit(solution)/shard_map/ppermute | solution.py:56
  65.8 1.3 %collective-permute-start.31 = (bf16[256,256]{1,0:T(8,128)(2,1)S(1)}, bf16[256,256]{1,0:T(8,128)(2,1)S(1)}, u32[]{:S(2)}, u32[]{:S(2)}) collective-permute-start(bf16[256,256]{1,0:T(8,128)(2,1)S(1)} %collective-permute-done.30.refs_2_), channel_id=1, source_target_pairs={{0,2},{1,5},{4,0},{5,9},{8,4},{9,13},{12,8},{13,15},{14,12},{15,11... | collective-permute-start | bytes 393224 | tf_op jit(solution)/shard_map/ppermute | solution.py:56
  69.2 1.4 %collective-permute-start.41 = (bf16[256,256]{1,0:T(8,128)(2,1)S(1)}, bf16[256,256]{1,0:T(8,128)(2,1)S(1)}, u32[]{:S(2)}, u32[]{:S(2)}) collective-permute-start(bf16[256,256]{1,0:T(8,128)(2,1)S(1)} %collective-permute-done.39.refs_3_), channel_id=1, source_target_pairs={{0,2},{1,5},{4,0},{5,9},{8,4},{9,13},{12,8},{13,15},{14,12},{15,11... | collective-permute-start | bytes 393224 | tf_op jit(solution)/shard_map/ppermute | solution.py:56
  72.1 1.3 %collective-permute-start.32 = (bf16[256,256]{1,0:T(8,128)(2,1)S(1)}, bf16[256,256]{1,0:T(8,128)(2,1)S(1)}, u32[]{:S(2)}, u32[]{:S(2)}) collective-permute-start(bf16[256,256]{1,0:T(8,128)(2,1)S(1)} %collective-permute-done.31.refs_6_), channel_id=1, source_target_pairs={{0,2},{1,5},{4,0},{5,9},{8,4},{9,13},{12,8},{13,15},{14,12},{15,11... | collective-permute-start | bytes 393224 | tf_op jit(solution)/shard_map/ppermute | solution.py:56
  75.0 1.4 %collective-permute-start.43 = (bf16[256,256]{1,0:T(8,128)(2,1)S(1)}, bf16[256,256]{1,0:T(8,128)(2,1)S(1)}, u32[]{:S(2)}, u32[]{:S(2)}) collective-permute-start(bf16[256,256]{1,0:T(8,128)(2,1)S(1)} %collective-permute-done.41.refs_7_), channel_id=1, source_target_pairs={{0,2},{1,5},{4,0},{5,9},{8,4},{9,13},{12,8},{13,15},{14,12},{15,11... | collective-permute-start | bytes 393224 | tf_op jit(solution)/shard_map/ppermute | solution.py:56
  76.3 1.1 %collective-permute-done.36.refs_9_ = bf16[256,256]{1,0:T(8,128)(2,1)S(1)} collective-permute-done((bf16[256,256]{1,0:T(8,128)(2,1)S(1)}, bf16[256,256]{1,0:T(8,128)(2,1)S(1)}, u32[]{:S(2)}, u32[]{:S(2)}) %collective-permute-start.36) | collective-permute-done | bytes 131104 | tf_op jit(solution)/shard_map/ppermute | solution.py:56
  80.0 1.5 %shard_map.100 = (f32[6,256,256]{2,1,0:T(8,128)S(1)}, f32[2,256,256]{2,1,0:T(8,128)S(1)}) custom-call(s32[9]{0:T(128)S(1)} %stack.39.starts, bf16[256,256]{1,0:T(8,128)(2,1)S(1)} %collective-permute-done.38.refs_0_, bf16[256,256]{1,0:T(8,128)(2,1)S(1)} %collective-permute-done.34.refs_1_, bf16[256,256]{1,0:T(8,128)(2,1)S(1)} %collective-permute-done.30.refs_2_, ...), custom_call_target="tpu_custom_call" | custom-call | flops 402653184 | bytes 1024 | tf_op jit(solution)/shard_map/pallas_call | solution.py:69
  84.0 1.6 %shard_map.101 = (f32[512,128]{1,0:T(8,128)S(1)}, f32[1,128,2048]{2,1,0:T(8,128)}) custom-call(s32[9]{0:T(128)S(1)} %stack.39.starts, bf16[256,256]{1,0:T(8,128)(2,1)S(1)} %collective-permute-done.33.refs_0_, bf16[256,256]{1,0:T(8,128)(2,1)S(1)} %collective-permute-done.37.refs_1_, bf16[256,2048]{1,0:T(8,128)(2,1)S(1)} %pad_maximum_fusion.stacked.refs_2_.refs_12_, ...), custom_call_target="tpu_custom_call" | custom-call | bytes 1024 | tf_op jit(solution)/shard_map/pallas_call | solution.py:69
  85.7 2.7 %shard_map.103 = (f32[1,2048,128]{2,1,0:T(8,128)}, f32[1,128]{1,0:T(1,128)}, f32[128,1024]{1,0:T(8,128)}) custom-call(s32[9]{0:T(128)S(1)} %stack.39.starts, bf16[2048,512]{1,0:T(8,128)(2,1)S(1)} %shard_map.98.turned, f32[512,128]{1,0:T(8,128)S(1)} %get-tuple-element.62.preact, f32[512,128]{1,0:T(8,128)S(1)} %get-tuple-element.79.back_own, ...), custom_call_target="tpu_custom_call" | custom-call | flops 268435456 | bytes 1024 | tf_op jit(solution)/shard_map/pallas_call | solution.py:69
  (115 shorter events, 34.6 us)
Async XLA Ops:
  1.6 7.2 %collective-permute-start.5 = (bf16[256,256]{1,0:T(8,128)(2,1)S(1)}, bf16[256,256]{1,0:T(8,128)(2,1)S(1)}, u32[]{:S(2)}, u32[]{:S(2)}) collective-permute-start(bf16[256,256]{1,0:T(8,128)(2,1)S(1)} %get-tuple-element.46.shard.refs_1_), channel_id=1, source_target_pairs={{0,4},{1,3},{4,8},{5,1},{8,12},{9,5},{12,14},{13,9},{14,10},{15,13... | collective-permute-start | bytes 393224 | tf_op jit(solution)/shard_map/ppermute | solution.py:56
  4.7 6.1 %collective-permute-start.1 = (bf16[256,256]{1,0:T(8,128)(2,1)S(1)}, bf16[256,256]{1,0:T(8,128)(2,1)S(1)}, u32[]{:S(2)}, u32[]{:S(2)}) collective-permute-start(bf16[256,256]{1,0:T(8,128)(2,1)S(1)} %get-tuple-element.45.shard.refs_0_), channel_id=1, source_target_pairs={{0,2},{1,5},{4,0},{5,9},{8,4},{9,13},{12,8},{13,15},{14,12},{15,11... | collective-permute-start | bytes 393224 | tf_op jit(solution)/shard_map/ppermute | solution.py:56
  5.4 5.9 %collective-permute-start = (bf16[256,256]{1,0:T(8,128)(2,1)S(1)}, bf16[256,256]{1,0:T(8,128)(2,1)S(1)}, u32[]{:S(2)}, u32[]{:S(2)}) collective-permute-start(bf16[256,256]{1,0:T(8,128)(2,1)S(1)} %get-tuple-element.45.shard.refs_0_), channel_id=1, source_target_pairs={{0,4},{1,3},{4,8},{5,1},{8,12},{9,5},{12,14},{13,9},{14,10},{15,13... | collective-permute-start | bytes 393224 | tf_op jit(solution)/shard_map/ppermute | solution.py:56
  8.8 6.0 %collective-permute-start.6 = (bf16[256,256]{1,0:T(8,128)(2,1)S(1)}, bf16[256,256]{1,0:T(8,128)(2,1)S(1)}, u32[]{:S(2)}, u32[]{:S(2)}) collective-permute-start(bf16[256,256]{1,0:T(8,128)(2,1)S(1)} %collective-permute-done.5.refs_3_.refs_1_), channel_id=1, source_target_pairs={{0,4},{1,3},{4,8},{5,1},{8,12},{9,5},{12,14},{13,9},{14,10},{15,13... | collective-permute-start | bytes 393224 | tf_op jit(solution)/shard_map/ppermute | solution.py:56
  11.3 12.0 %collective-permute-start.14 = (bf16[128,1024]{1,0:T(8,128)(2,1)}, bf16[128,1024]{1,0:T(8,128)(2,1)S(1)}, u32[]{:S(2)}, u32[]{:S(2)}) collective-permute-start(bf16[128,1024]{1,0:T(8,128)(2,1)} %param.11), channel_id=1, source_target_pairs={{0,1},{1,0},{2,3},{3,2},{4,5},{5,4},{6,7},{7,6},{8,9},{9,8},{10,11... | collective-permute-start | bytes 786440 | tf_op jit(solution)/shard_map/ppermute | solution.py:28
  11.3 6.3 %collective-permute-start.10 = (bf16[256,256]{1,0:T(8,128)(2,1)S(1)}, bf16[256,256]{1,0:T(8,128)(2,1)S(1)}, u32[]{:S(2)}, u32[]{:S(2)}) collective-permute-start(bf16[256,256]{1,0:T(8,128)(2,1)S(1)} %collective-permute-done.refs_2_.refs_0_), channel_id=1, source_target_pairs={{0,4},{1,3},{4,8},{5,1},{8,12},{9,5},{12,14},{13,9},{14,10},{15,13... | collective-permute-start | bytes 393224 | tf_op jit(solution)/shard_map/ppermute | solution.py:56
  13.8 6.4 %collective-permute-start.11 = (bf16[256,256]{1,0:T(8,128)(2,1)S(1)}, bf16[256,256]{1,0:T(8,128)(2,1)S(1)}, u32[]{:S(2)}, u32[]{:S(2)}) collective-permute-start(bf16[256,256]{1,0:T(8,128)(2,1)S(1)} %collective-permute-done.9.refs_5_.refs_3_), channel_id=1, source_target_pairs={{0,2},{1,5},{4,0},{5,9},{8,4},{9,13},{12,8},{13,15},{14,12},{15,11... | collective-permute-start | bytes 393224 | tf_op jit(solution)/shard_map/ppermute | solution.py:56
  14.9 5.7 %collective-permute-start.7 = (bf16[256,256]{1,0:T(8,128)(2,1)S(1)}, bf16[256,256]{1,0:T(8,128)(2,1)S(1)}, u32[]{:S(2)}, u32[]{:S(2)}) collective-permute-start(bf16[256,256]{1,0:T(8,128)(2,1)S(1)} %collective-permute-done.6.refs_7_.refs_5_), channel_id=1, source_target_pairs={{0,4},{1,3},{4,8},{5,1},{8,12},{9,5},{12,14},{13,9},{14,10},{15,13... | collective-permute-start | bytes 393224 | tf_op jit(solution)/shard_map/ppermute | solution.py:56
  16.5 6.6 %collective-permute-start.3 = (bf16[256,256]{1,0:T(8,128)(2,1)S(1)}, bf16[256,256]{1,0:T(8,128)(2,1)S(1)}, u32[]{:S(2)}, u32[]{:S(2)}) collective-permute-start(bf16[256,256]{1,0:T(8,128)(2,1)S(1)} %collective-permute-done.2.refs_8_.refs_6_), channel_id=1, source_target_pairs={{0,2},{1,5},{4,0},{5,9},{8,4},{9,13},{12,8},{13,15},{14,12},{15,11... | collective-permute-start | bytes 393224 | tf_op jit(solution)/shard_map/ppermute | solution.py:56
  17.6 8.1 %collective-permute-start.12 = (bf16[256,256]{1,0:T(8,128)(2,1)S(1)}, bf16[256,256]{1,0:T(8,128)(2,1)S(1)}, u32[]{:S(2)}, u32[]{:S(2)}) collective-permute-start(bf16[256,256]{1,0:T(8,128)(2,1)S(1)} %collective-permute-done.10.refs_6_.refs_4_), channel_id=1, source_target_pairs={{0,4},{1,3},{4,8},{5,1},{8,12},{9,5},{12,14},{13,9},{14,10},{15,13... | collective-permute-start | bytes 393224 | tf_op jit(solution)/shard_map/ppermute | solution.py:56
  20.6 6.4 %collective-permute-start.8 = (bf16[256,256]{1,0:T(8,128)(2,1)S(1)}, bf16[256,256]{1,0:T(8,128)(2,1)S(1)}, u32[]{:S(2)}, u32[]{:S(2)}) collective-permute-start(bf16[256,256]{1,0:T(8,128)(2,1)S(1)} %collective-permute-done.7.refs_11_.refs_9_), channel_id=1, source_target_pairs={{0,4},{1,3},{4,8},{5,1},{8,12},{9,5},{12,14},{13,9},{14,10},{15,13... | collective-permute-start | bytes 393224 | tf_op jit(solution)/shard_map/ppermute | solution.py:56
  32.2 7.0 %collective-permute-start.21 = (bf16[256,256]{1,0:T(8,128)(2,1)S(1)}, bf16[256,256]{1,0:T(8,128)(2,1)S(1)}, u32[]{:S(2)}, u32[]{:S(2)}) collective-permute-start(bf16[256,256]{1,0:T(8,128)(2,1)S(1)} %fusion.1), channel_id=1, source_target_pairs={{0,2},{1,5},{4,0},{5,9},{8,4},{9,13},{12,8},{13,15},{14,12},{15,11... | collective-permute-start | bytes 393224 | tf_op jit(solution)/shard_map/ppermute | solution.py:56
  34.1 6.0 %collective-permute-start.16 = (bf16[256,256]{1,0:T(8,128)(2,1)S(1)}, bf16[256,256]{1,0:T(8,128)(2,1)S(1)}, u32[]{:S(2)}, u32[]{:S(2)}) collective-permute-start(bf16[256,256]{1,0:T(8,128)(2,1)S(1)} %fusion), channel_id=1, source_target_pairs={{0,4},{1,3},{4,8},{5,1},{8,12},{9,5},{12,14},{13,9},{14,10},{15,13... | collective-permute-start | bytes 393224 | tf_op jit(solution)/shard_map/ppermute | solution.py:56
  37.1 6.3 %collective-permute-start.20 = (bf16[256,256]{1,0:T(8,128)(2,1)S(1)}, bf16[256,256]{1,0:T(8,128)(2,1)S(1)}, u32[]{:S(2)}, u32[]{:S(2)}) collective-permute-start(bf16[256,256]{1,0:T(8,128)(2,1)S(1)} %get-tuple-element.56), channel_id=1, source_target_pairs={{0,2},{1,5},{4,0},{5,9},{8,4},{9,13},{12,8},{13,15},{14,12},{15,11... | collective-permute-start | bytes 393224 | tf_op jit(solution)/shard_map/ppermute | solution.py:56
  38.0 6.5 %collective-permute-start.25 = (bf16[256,256]{1,0:T(8,128)(2,1)S(1)}, bf16[256,256]{1,0:T(8,128)(2,1)S(1)}, u32[]{:S(2)}, u32[]{:S(2)}) collective-permute-start(bf16[256,256]{1,0:T(8,128)(2,1)S(1)} %get-tuple-element.66), channel_id=1, source_target_pairs={{0,4},{1,3},{4,8},{5,1},{8,12},{9,5},{12,14},{13,9},{14,10},{15,13... | collective-permute-start | bytes 393224 | tf_op jit(solution)/shard_map/ppermute | solution.py:56
  39.2 7.0 %collective-permute-start.23 = (bf16[256,256]{1,0:T(8,128)(2,1)S(1)}, bf16[256,256]{1,0:T(8,128)(2,1)S(1)}, u32[]{:S(2)}, u32[]{:S(2)}) collective-permute-start(bf16[256,256]{1,0:T(8,128)(2,1)S(1)} %add_convert_fusion.4), channel_id=1, source_target_pairs={{0,2},{1,5},{4,0},{5,9},{8,4},{9,13},{12,8},{13,15},{14,12},{15,11... | collective-permute-start | bytes 393224 | tf_op jit(solution)/shard_map/ppermute | solution.py:56
  40.2 7.1 %collective-permute-start.17 = (bf16[256,256]{1,0:T(8,128)(2,1)S(1)}, bf16[256,256]{1,0:T(8,128)(2,1)S(1)}, u32[]{:S(2)}, u32[]{:S(2)}) collective-permute-start(bf16[256,256]{1,0:T(8,128)(2,1)S(1)} %add_convert_fusion.9), channel_id=1, source_target_pairs={{0,4},{1,3},{4,8},{5,1},{8,12},{9,5},{12,14},{13,9},{14,10},{15,13... | collective-permute-start | bytes 393224 | tf_op jit(solution)/shard_map/ppermute | solution.py:56
  43.4 6.0 %collective-permute-start.22 = (bf16[256,256]{1,0:T(8,128)(2,1)S(1)}, bf16[256,256]{1,0:T(8,128)(2,1)S(1)}, u32[]{:S(2)}, u32[]{:S(2)}) collective-permute-start(bf16[256,256]{1,0:T(8,128)(2,1)S(1)} %add_convert_fusion.6), channel_id=1, source_target_pairs={{0,2},{1,5},{4,0},{5,9},{8,4},{9,13},{12,8},{13,15},{14,12},{15,11... | collective-permute-start | bytes 393224 | tf_op jit(solution)/shard_map/ppermute | solution.py:56
  44.5 5.9 %collective-permute-start.26 = (bf16[256,256]{1,0:T(8,128)(2,1)S(1)}, bf16[256,256]{1,0:T(8,128)(2,1)S(1)}, u32[]{:S(2)}, u32[]{:S(2)}) collective-permute-start(bf16[256,256]{1,0:T(8,128)(2,1)S(1)} %add_convert_fusion.3), channel_id=1, source_target_pairs={{0,4},{1,3},{4,8},{5,1},{8,12},{9,5},{12,14},{13,9},{14,10},{15,13... | collective-permute-start | bytes 393224 | tf_op jit(solution)/shard_map/ppermute | solution.py:56
  46.2 7.8 %collective-permute-start.28 = (bf16[256,256]{1,0:T(8,128)(2,1)S(1)}, bf16[256,256]{1,0:T(8,128)(2,1)S(1)}, u32[]{:S(2)}, u32[]{:S(2)}) collective-permute-start(bf16[256,256]{1,0:T(8,128)(2,1)S(1)} %add_convert_fusion.1), channel_id=1, source_target_pairs={{0,2},{1,5},{4,0},{5,9},{8,4},{9,13},{12,8},{13,15},{14,12},{15,11... | collective-permute-start | bytes 393224 | tf_op jit(solution)/shard_map/ppermute | solution.py:56
  49.5 5.9 %collective-permute-start.24 = (bf16[256,256]{1,0:T(8,128)(2,1)S(1)}, bf16[256,256]{1,0:T(8,128)(2,1)S(1)}, u32[]{:S(2)}, u32[]{:S(2)}) collective-permute-start(bf16[256,256]{1,0:T(8,128)(2,1)S(1)} %add_convert_fusion.5), channel_id=1, source_target_pairs={{0,2},{1,5},{4,0},{5,9},{8,4},{9,13},{12,8},{13,15},{14,12},{15,11... | collective-permute-start | bytes 393224 | tf_op jit(solution)/shard_map/ppermute | solution.py:56
  50.4 9.1 %collective-permute-start.27 = (bf16[256,256]{1,0:T(8,128)(2,1)S(1)}, bf16[256,256]{1,0:T(8,128)(2,1)S(1)}, u32[]{:S(2)}, u32[]{:S(2)}) collective-permute-start(bf16[256,256]{1,0:T(8,128)(2,1)S(1)} %add_convert_fusion.2), channel_id=1, source_target_pairs={{0,4},{1,3},{4,8},{5,1},{8,12},{9,5},{12,14},{13,9},{14,10},{15,13... | collective-permute-start | bytes 393224 | tf_op jit(solution)/shard_map/ppermute | solution.py:56
  52.5 6.2 %collective-permute-start.19 = (bf16[256,256]{1,0:T(8,128)(2,1)S(1)}, bf16[256,256]{1,0:T(8,128)(2,1)S(1)}, u32[]{:S(2)}, u32[]{:S(2)}) collective-permute-start(bf16[256,256]{1,0:T(8,128)(2,1)S(1)} %add_convert_fusion.7), channel_id=1, source_target_pairs={{0,4},{1,3},{4,8},{5,1},{8,12},{9,5},{12,14},{13,9},{14,10},{15,13... | collective-permute-start | bytes 393224 | tf_op jit(solution)/shard_map/ppermute | solution.py:56
  58.8 6.3 %collective-permute-start.34 = (bf16[256,256]{1,0:T(8,128)(2,1)S(1)}, bf16[256,256]{1,0:T(8,128)(2,1)S(1)}, u32[]{:S(2)}, u32[]{:S(2)}) collective-permute-start(bf16[256,256]{1,0:T(8,128)(2,1)S(1)} %multiply_convert_fusion.refs_1_), channel_id=1, source_target_pairs={{0,4},{1,3},{4,8},{5,1},{8,12},{9,5},{12,14},{13,9},{14,10},{15,13... | collective-permute-start | bytes 393224 | tf_op jit(solution)/shard_map/ppermute | solution.py:56
  59.6 6.2 %collective-permute-start.30 = (bf16[256,256]{1,0:T(8,128)(2,1)S(1)}, bf16[256,256]{1,0:T(8,128)(2,1)S(1)}, u32[]{:S(2)}, u32[]{:S(2)}) collective-permute-start(bf16[256,256]{1,0:T(8,128)(2,1)S(1)} %fusion.3.refs_0_), channel_id=1, source_target_pairs={{0,2},{1,5},{4,0},{5,9},{8,4},{9,13},{12,8},{13,15},{14,12},{15,11... | collective-permute-start | bytes 393224 | tf_op jit(solution)/shard_map/ppermute | solution.py:56
  62.1 6.0 %collective-permute-start.38 = (bf16[256,256]{1,0:T(8,128)(2,1)S(1)}, bf16[256,256]{1,0:T(8,128)(2,1)S(1)}, u32[]{:S(2)}, u32[]{:S(2)}) collective-permute-start(bf16[256,256]{1,0:T(8,128)(2,1)S(1)} %fusion.3.refs_0_), channel_id=1, source_target_pairs={{0,4},{1,3},{4,8},{5,1},{8,12},{9,5},{12,14},{13,9},{14,10},{15,13... | collective-permute-start | bytes 393224 | tf_op jit(solution)/shard_map/ppermute | solution.py:56
  65.1 6.3 %collective-permute-start.35 = (bf16[256,256]{1,0:T(8,128)(2,1)S(1)}, bf16[256,256]{1,0:T(8,128)(2,1)S(1)}, u32[]{:S(2)}, u32[]{:S(2)}) collective-permute-start(bf16[256,256]{1,0:T(8,128)(2,1)S(1)} %collective-permute-done.34.refs_1_), channel_id=1, source_target_pairs={{0,4},{1,3},{4,8},{5,1},{8,12},{9,5},{12,14},{13,9},{14,10},{15,13... | collective-permute-start | bytes 393224 | tf_op jit(solution)/shard_map/ppermute | solution.py:56
  65.8 6.4 %collective-permute-start.31 = (bf16[256,256]{1,0:T(8,128)(2,1)S(1)}, bf16[256,256]{1,0:T(8,128)(2,1)S(1)}, u32[]{:S(2)}, u32[]{:S(2)}) collective-permute-start(bf16[256,256]{1,0:T(8,128)(2,1)S(1)} %collective-permute-done.30.refs_2_), channel_id=1, source_target_pairs={{0,2},{1,5},{4,0},{5,9},{8,4},{9,13},{12,8},{13,15},{14,12},{15,11... | collective-permute-start | bytes 393224 | tf_op jit(solution)/shard_map/ppermute | solution.py:56
  68.0 6.2 %collective-permute-start.40 = (bf16[256,256]{1,0:T(8,128)(2,1)S(1)}, bf16[256,256]{1,0:T(8,128)(2,1)S(1)}, u32[]{:S(2)}, u32[]{:S(2)}) collective-permute-start(bf16[256,256]{1,0:T(8,128)(2,1)S(1)} %collective-permute-done.38.refs_0_), channel_id=1, source_target_pairs={{0,4},{1,3},{4,8},{5,1},{8,12},{9,5},{12,14},{13,9},{14,10},{15,13... | collective-permute-start | bytes 393224 | tf_op jit(solution)/shard_map/ppermute | solution.py:56
  69.2 5.8 %collective-permute-start.41 = (bf16[256,256]{1,0:T(8,128)(2,1)S(1)}, bf16[256,256]{1,0:T(8,128)(2,1)S(1)}, u32[]{:S(2)}, u32[]{:S(2)}) collective-permute-start(bf16[256,256]{1,0:T(8,128)(2,1)S(1)} %collective-permute-done.39.refs_3_), channel_id=1, source_target_pairs={{0,2},{1,5},{4,0},{5,9},{8,4},{9,13},{12,8},{13,15},{14,12},{15,11... | collective-permute-start | bytes 393224 | tf_op jit(solution)/shard_map/ppermute | solution.py:56
  71.4 6.1 %collective-permute-start.36 = (bf16[256,256]{1,0:T(8,128)(2,1)S(1)}, bf16[256,256]{1,0:T(8,128)(2,1)S(1)}, u32[]{:S(2)}, u32[]{:S(2)}) collective-permute-start(bf16[256,256]{1,0:T(8,128)(2,1)S(1)} %collective-permute-done.35.refs_5_), channel_id=1, source_target_pairs={{0,4},{1,3},{4,8},{5,1},{8,12},{9,5},{12,14},{13,9},{14,10},{15,13... | collective-permute-start | bytes 393224 | tf_op jit(solution)/shard_map/ppermute | solution.py:56
  72.1 6.3 %collective-permute-start.32 = (bf16[256,256]{1,0:T(8,128)(2,1)S(1)}, bf16[256,256]{1,0:T(8,128)(2,1)S(1)}, u32[]{:S(2)}, u32[]{:S(2)}) collective-permute-start(bf16[256,256]{1,0:T(8,128)(2,1)S(1)} %collective-permute-done.31.refs_6_), channel_id=1, source_target_pairs={{0,2},{1,5},{4,0},{5,9},{8,4},{9,13},{12,8},{13,15},{14,12},{15,11... | collective-permute-start | bytes 393224 | tf_op jit(solution)/shard_map/ppermute | solution.py:56
  (25 other events, 190.2 us)

commit v22 on v20

--- a/solution.py
+++ b/solution.py
@@ -14,7 +14,7 @@
 OVER_COLS = (((1,), (1,)), ((), ()))
 RING_LIMIT = 16
 VMEM_BYTES = 24 * 1024 * 1024
-PIECES = 8
+PIECES = 16
 
 
 def passed_along(shard, axis, by):
@@ -117,7 +117,8 @@
     outs = list(outs)
     for chain in range(2):
         at = slice(chain * rows, (chain + 1) * rows)
-        both = jnp.concatenate([codes[at, :], earlier[at, :]], axis=1)
+        before = jnp.where(starts[starts.shape[0] - 1] > 0, earlier[at, :], jnp.zeros((), BF16))
+        both = jnp.concatenate([codes[at, :], before], axis=1)
         for slot in slots:
             partial = outs.pop(0)
             block = stacked[:, block_of(starts, slot, partial.shape[1])]
@@ -294,8 +295,7 @@
     for s in range(1, reach + 1):
         gather_step(inputs, s, turned_own if s == 1 else None)
     low_cross = swapped(after(dec_cross, inputs[0][slot_p.get(1, far)]))
-    cross = jnp.where(layer > 0, jnp.concatenate([low_cross, dec_cross], axis=1), jnp.zeros((), BF16))
-    stacked = jnp.concatenate([dec_same[0], cross], axis=0)
+    stacked = jnp.concatenate([dec_same[0], jnp.concatenate([low_cross, dec_cross], axis=1)], axis=0)
     part = encode(tuple(range(far)), after(enc_bias, stacked))[0]
     preact, codes = encode((far,), part)
     earlier = swapped(codes)

time: 85.9 us -> 85.9 us (level)
    concatenate x1, other arithmetic: 0.09 us -> 1.21 us  [ring_shards(): jnp.concatenate([dec_same[0], jnp.concatenate([low_cross, dec_cross], axi...]
    select_n x1 -> x0, other arithmetic: 1.06 us -> none  [ring_shards(): jnp.where(layer > 0, jnp.concatenate([low_cross, dec_cross], axis=1), jnp...]
where the time goes in v22:
time: 85.9 us; the launch traced here: 85.8 us
  starting transfers between devices  46.2 us (54%)
  waiting for transfers between devices  22.3 us (26%)
  Pallas kernels  13.6 us (16%)
  other arithmetic  1.63 us (2%)
  local copies, waits for them, and re-layouts  1.15 us (1%)
  between operations  0.9 us (1%)
    ppermute x42, starting transfers between devices, hop(): return lax.ppermute(shard, ('latent', 'layer'), pairs)  46 us
    ppermute x42, waiting for transfers between devices, hop(): return lax.ppermute(shard, ('latent', 'layer'), pairs)  20.9 us
    pallas_call x12, Pallas kernels, call(): pl.pallas_call(kernel, out_shape=outs, in_specs=[spec(pltpu.SMEM)] + [spe...  13.6 us
  transfers between devices with their start and end apart: 45, of which 28 were waited for; matrix products, arithmetic and copies ran while one was open for 2% of the time, Pallas kernels for 10%

profile of v22, /device:TPU:0, one launch (start us, length us, event | category | flops | bytes accessed | tf_op | source)
XLA Modules:
  0.0 85.8 jit_solution(82516962725496540)
XLA Ops:
  1.7 3.1 %collective-permute-start.5 = (bf16[256,256]{1,0:T(8,128)(2,1)S(1)}, bf16[256,256]{1,0:T(8,128)(2,1)S(1)}, u32[]{:S(2)}, u32[]{:S(2)}) collective-permute-start(bf16[256,256]{1,0:T(8,128)(2,1)S(1)} %get-tuple-element.48.shard.refs_1_), channel_id=1, source_target_pairs={{0,4},{1,3},{4,8},{5,1},{8,12},{9,5},{12,14},{13,9},{14,10},{15,13... | collective-permute-start | bytes 393224 | tf_op jit(solution)/shard_map/ppermute | solution.py:56
  5.5 2.1 %collective-permute-start = (bf16[256,256]{1,0:T(8,128)(2,1)S(1)}, bf16[256,256]{1,0:T(8,128)(2,1)S(1)}, u32[]{:S(2)}, u32[]{:S(2)}) collective-permute-start(bf16[256,256]{1,0:T(8,128)(2,1)S(1)} %get-tuple-element.47.shard.refs_0_), channel_id=1, source_target_pairs={{0,4},{1,3},{4,8},{5,1},{8,12},{9,5},{12,14},{13,9},{14,10},{15,13... | collective-permute-start | bytes 393224 | tf_op jit(solution)/shard_map/ppermute | solution.py:56
  8.5 1.8 %collective-permute-start.6 = (bf16[256,256]{1,0:T(8,128)(2,1)S(1)}, bf16[256,256]{1,0:T(8,128)(2,1)S(1)}, u32[]{:S(2)}, u32[]{:S(2)}) collective-permute-start(bf16[256,256]{1,0:T(8,128)(2,1)S(1)} %collective-permute-done.5.refs_3_.refs_1_), channel_id=1, source_target_pairs={{0,4},{1,3},{4,8},{5,1},{8,12},{9,5},{12,14},{13,9},{14,10},{15,13... | collective-permute-start | bytes 393224 | tf_op jit(solution)/shard_map/ppermute | solution.py:56
  11.5 2.5 %collective-permute-start.10 = (bf16[256,256]{1,0:T(8,128)(2,1)S(1)}, bf16[256,256]{1,0:T(8,128)(2,1)S(1)}, u32[]{:S(2)}, u32[]{:S(2)}) collective-permute-start(bf16[256,256]{1,0:T(8,128)(2,1)S(1)} %collective-permute-done.refs_2_.refs_0_), channel_id=1, source_target_pairs={{0,4},{1,3},{4,8},{5,1},{8,12},{9,5},{12,14},{13,9},{14,10},{15,13... | collective-permute-start | bytes 393224 | tf_op jit(solution)/shard_map/ppermute | solution.py:56
  14.7 1.3 %collective-permute-start.7 = (bf16[256,256]{1,0:T(8,128)(2,1)S(1)}, bf16[256,256]{1,0:T(8,128)(2,1)S(1)}, u32[]{:S(2)}, u32[]{:S(2)}) collective-permute-start(bf16[256,256]{1,0:T(8,128)(2,1)S(1)} %collective-permute-done.6.refs_7_.refs_5_), channel_id=1, source_target_pairs={{0,4},{1,3},{4,8},{5,1},{8,12},{9,5},{12,14},{13,9},{14,10},{15,13... | collective-permute-start | bytes 393224 | tf_op jit(solution)/shard_map/ppermute | solution.py:56
  17.8 2.5 %collective-permute-start.12 = (bf16[256,256]{1,0:T(8,128)(2,1)S(1)}, bf16[256,256]{1,0:T(8,128)(2,1)S(1)}, u32[]{:S(2)}, u32[]{:S(2)}) collective-permute-start(bf16[256,256]{1,0:T(8,128)(2,1)S(1)} %collective-permute-done.10.refs_6_.refs_4_), channel_id=1, source_target_pairs={{0,4},{1,3},{4,8},{5,1},{8,12},{9,5},{12,14},{13,9},{14,10},{15,13... | collective-permute-start | bytes 393224 | tf_op jit(solution)/shard_map/ppermute | solution.py:56
  20.8 2.3 %collective-permute-start.8 = (bf16[256,256]{1,0:T(8,128)(2,1)S(1)}, bf16[256,256]{1,0:T(8,128)(2,1)S(1)}, u32[]{:S(2)}, u32[]{:S(2)}) collective-permute-start(bf16[256,256]{1,0:T(8,128)(2,1)S(1)} %collective-permute-done.7.refs_11_.refs_9_), channel_id=1, source_target_pairs={{0,4},{1,3},{4,8},{5,1},{8,12},{9,5},{12,14},{13,9},{14,10},{15,13... | collective-permute-start | bytes 393224 | tf_op jit(solution)/shard_map/ppermute | solution.py:56
  23.5 1.2 %maximum_maximum_fusion.stacked.refs_6_.refs_8_.refs_2_ = bf16[256,2048]{1,0:T(8,128)(2,1)S(1)} fusion(bf16[128,1024]{1,0:T(8,128)(2,1)} %param.11, bf16[128,1024]{1,0:T(8,128)(2,1)S(1)} %collective-permute-done.14, bf16[128,2048]{1,0:T(8,128)(2,1)} %bitcast.19), kind=kLoop, calls=%fused_computation | loop fusion | flops 3145728 | bytes 2097152 | tf_op jit(solution)/shard_map/concatenate | solution.py:298
  29.1 1.3 %collective-permute-done.15.earlier = bf16[512,128]{1,0:T(8,128)(2,1)S(1)} collective-permute-done((bf16[512,128]{1,0:T(8,128)(2,1)S(1)}, bf16[512,128]{1,0:T(8,128)(2,1)S(1)}, u32[]{:S(2)}, u32[]{:S(2)}) %collective-permute-start.15) | collective-permute-done | bytes 131104 | tf_op jit(solution)/shard_map/ppermute | solution.py:28
  31.5 1.9 %collective-permute-start.16 = (bf16[256,256]{1,0:T(8,128)(2,1)S(1)}, bf16[256,256]{1,0:T(8,128)(2,1)S(1)}, u32[]{:S(2)}, u32[]{:S(2)}) collective-permute-start(bf16[256,256]{1,0:T(8,128)(2,1)S(1)} %get-tuple-element.56), channel_id=1, source_target_pairs={{0,4},{1,3},{4,8},{5,1},{8,12},{9,5},{12,14},{13,9},{14,10},{15,13... | collective-permute-start | bytes 393224 | tf_op jit(solution)/shard_map/ppermute | solution.py:56
  33.4 1.2 %shard_map.97 = (f32[256,256]{1,0:T(8,128)S(1)}, f32[256,256]{1,0:T(8,128)S(1)}, f32[256,256]{1,0:T(8,128)S(1)}, f32[256,256]{1,0:T(8,128)S(1)}, f32[256,256]{1,...) custom-call(s32[9]{0:T(128)S(1)} %stack.39.starts, ...), custom_call_target="tpu_custom_call" | custom-call | flops 469762048 | bytes 1024 | tf_op jit(solution)/shard_map/pallas_call | solution.py:69
  34.9 1.8 %collective-permute-start.25 = (bf16[256,256]{1,0:T(8,128)(2,1)S(1)}, bf16[256,256]{1,0:T(8,128)(2,1)S(1)}, u32[]{:S(2)}, u32[]{:S(2)}) collective-permute-start(bf16[256,256]{1,0:T(8,128)(2,1)S(1)} %get-tuple-element.70), channel_id=1, source_target_pairs={{0,4},{1,3},{4,8},{5,1},{8,12},{9,5},{12,14},{13,9},{14,10},{15,13... | collective-permute-start | bytes 393224 | tf_op jit(solution)/shard_map/ppermute | solution.py:56
  37.5 2.1 %collective-permute-start.17 = (bf16[256,256]{1,0:T(8,128)(2,1)S(1)}, bf16[256,256]{1,0:T(8,128)(2,1)S(1)}, u32[]{:S(2)}, u32[]{:S(2)}) collective-permute-start(bf16[256,256]{1,0:T(8,128)(2,1)S(1)} %add_convert_fusion.9), channel_id=1, source_target_pairs={{0,4},{1,3},{4,8},{5,1},{8,12},{9,5},{12,14},{13,9},{14,10},{15,13... | collective-permute-start | bytes 393224 | tf_op jit(solution)/shard_map/ppermute | solution.py:56
  39.5 1.5 %collective-permute-done.20 = bf16[256,256]{1,0:T(8,128)(2,1)S(1)} collective-permute-done((bf16[256,256]{1,0:T(8,128)(2,1)S(1)}, bf16[256,256]{1,0:T(8,128)(2,1)S(1)}, u32[]{:S(2)}, u32[]{:S(2)}) %collective-permute-start.20) | collective-permute-done | bytes 131104 | tf_op jit(solution)/shard_map/ppermute | solution.py:56
  41.2 2.1 %collective-permute-start.26 = (bf16[256,256]{1,0:T(8,128)(2,1)S(1)}, bf16[256,256]{1,0:T(8,128)(2,1)S(1)}, u32[]{:S(2)}, u32[]{:S(2)}) collective-permute-start(bf16[256,256]{1,0:T(8,128)(2,1)S(1)} %add_convert_fusion.3), channel_id=1, source_target_pairs={{0,4},{1,3},{4,8},{5,1},{8,12},{9,5},{12,14},{13,9},{14,10},{15,13... | collective-permute-start | bytes 393224 | tf_op jit(solution)/shard_map/ppermute | solution.py:56
  44.0 1.9 %collective-permute-start.18 = (bf16[256,256]{1,0:T(8,128)(2,1)S(1)}, bf16[256,256]{1,0:T(8,128)(2,1)S(1)}, u32[]{:S(2)}, u32[]{:S(2)}) collective-permute-start(bf16[256,256]{1,0:T(8,128)(2,1)S(1)} %add_convert_fusion.8), channel_id=1, source_target_pairs={{0,4},{1,3},{4,8},{5,1},{8,12},{9,5},{12,14},{13,9},{14,10},{15,13... | collective-permute-start | bytes 393224 | tf_op jit(solution)/shard_map/ppermute | solution.py:56
  47.2 1.5 %collective-permute-start.27 = (bf16[256,256]{1,0:T(8,128)(2,1)S(1)}, bf16[256,256]{1,0:T(8,128)(2,1)S(1)}, u32[]{:S(2)}, u32[]{:S(2)}) collective-permute-start(bf16[256,256]{1,0:T(8,128)(2,1)S(1)} %add_convert_fusion.2), channel_id=1, source_target_pairs={{0,4},{1,3},{4,8},{5,1},{8,12},{9,5},{12,14},{13,9},{14,10},{15,13... | collective-permute-start | bytes 393224 | tf_op jit(solution)/shard_map/ppermute | solution.py:56
  49.7 1.4 %collective-permute-start.19 = (bf16[256,256]{1,0:T(8,128)(2,1)S(1)}, bf16[256,256]{1,0:T(8,128)(2,1)S(1)}, u32[]{:S(2)}, u32[]{:S(2)}) collective-permute-start(bf16[256,256]{1,0:T(8,128)(2,1)S(1)} %add_convert_fusion.7), channel_id=1, source_target_pairs={{0,4},{1,3},{4,8},{5,1},{8,12},{9,5},{12,14},{13,9},{14,10},{15,13... | collective-permute-start | bytes 393224 | tf_op jit(solution)/shard_map/ppermute | solution.py:56
  53.0 2.0 %collective-permute-done.19 = bf16[256,256]{1,0:T(8,128)(2,1)S(1)} collective-permute-done((bf16[256,256]{1,0:T(8,128)(2,1)S(1)}, bf16[256,256]{1,0:T(8,128)(2,1)S(1)}, u32[]{:S(2)}, u32[]{:S(2)}) %collective-permute-start.19) | collective-permute-done | bytes 131104 | tf_op jit(solution)/shard_map/ppermute | solution.py:56
  55.1 1.5 %collective-permute-start.34 = (bf16[256,256]{1,0:T(8,128)(2,1)S(1)}, bf16[256,256]{1,0:T(8,128)(2,1)S(1)}, u32[]{:S(2)}, u32[]{:S(2)}) collective-permute-start(bf16[256,256]{1,0:T(8,128)(2,1)S(1)} %multiply_convert_fusion.refs_1_), channel_id=1, source_target_pairs={{0,4},{1,3},{4,8},{5,1},{8,12},{9,5},{12,14},{13,9},{14,10},{15,13... | collective-permute-start | bytes 393224 | tf_op jit(solution)/shard_map/ppermute | solution.py:56
  57.3 1.5 %collective-permute-start.39 = (bf16[256,256]{1,0:T(8,128)(2,1)S(1)}, bf16[256,256]{1,0:T(8,128)(2,1)S(1)}, u32[]{:S(2)}, u32[]{:S(2)}) collective-permute-start(bf16[256,256]{1,0:T(8,128)(2,1)S(1)} %multiply_convert_fusion.refs_1_), channel_id=1, source_target_pairs={{0,2},{1,5},{4,0},{5,9},{8,4},{9,13},{12,8},{13,15},{14,12},{15,11... | collective-permute-start | bytes 393224 | tf_op jit(solution)/shard_map/ppermute | solution.py:56
  59.4 1.9 %collective-permute-done.34.refs_3_ = bf16[256,256]{1,0:T(8,128)(2,1)S(1)} collective-permute-done((bf16[256,256]{1,0:T(8,128)(2,1)S(1)}, bf16[256,256]{1,0:T(8,128)(2,1)S(1)}, u32[]{:S(2)}, u32[]{:S(2)}) %collective-permute-start.34) | collective-permute-done | bytes 131104 | tf_op jit(solution)/shard_map/ppermute | solution.py:56
  61.3 1.5 %collective-permute-start.35 = (bf16[256,256]{1,0:T(8,128)(2,1)S(1)}, bf16[256,256]{1,0:T(8,128)(2,1)S(1)}, u32[]{:S(2)}, u32[]{:S(2)}) collective-permute-start(bf16[256,256]{1,0:T(8,128)(2,1)S(1)} %collective-permute-done.34.refs_3_), channel_id=1, source_target_pairs={{0,4},{1,3},{4,8},{5,1},{8,12},{9,5},{12,14},{13,9},{14,10},{15,13... | collective-permute-start | bytes 393224 | tf_op jit(solution)/shard_map/ppermute | solution.py:56
  65.9 1.2 %collective-permute-start.40 = (bf16[256,256]{1,0:T(8,128)(2,1)S(1)}, bf16[256,256]{1,0:T(8,128)(2,1)S(1)}, u32[]{:S(2)}, u32[]{:S(2)}) collective-permute-start(bf16[256,256]{1,0:T(8,128)(2,1)S(1)} %collective-permute-done.38.refs_2_), channel_id=1, source_target_pairs={{0,4},{1,3},{4,8},{5,1},{8,12},{9,5},{12,14},{13,9},{14,10},{15,13... | collective-permute-start | bytes 393224 | tf_op jit(solution)/shard_map/ppermute | solution.py:56
  67.1 1.9 %collective-permute-start.36 = (bf16[256,256]{1,0:T(8,128)(2,1)S(1)}, bf16[256,256]{1,0:T(8,128)(2,1)S(1)}, u32[]{:S(2)}, u32[]{:S(2)}) collective-permute-start(bf16[256,256]{1,0:T(8,128)(2,1)S(1)} %collective-permute-done.35.refs_1_), channel_id=1, source_target_pairs={{0,4},{1,3},{4,8},{5,1},{8,12},{9,5},{12,14},{13,9},{14,10},{15,13... | collective-permute-start | bytes 393224 | tf_op jit(solution)/shard_map/ppermute | solution.py:56
  69.7 1.9 %collective-permute-done.41.refs_3_ = bf16[256,256]{1,0:T(8,128)(2,1)S(1)} collective-permute-done((bf16[256,256]{1,0:T(8,128)(2,1)S(1)}, bf16[256,256]{1,0:T(8,128)(2,1)S(1)}, u32[]{:S(2)}, u32[]{:S(2)}) %collective-permute-start.41) | collective-permute-done | bytes 131104 | tf_op jit(solution)/shard_map/ppermute | solution.py:56
  72.2 1.5 %collective-permute-start.42 = (bf16[256,256]{1,0:T(8,128)(2,1)S(1)}, bf16[256,256]{1,0:T(8,128)(2,1)S(1)}, u32[]{:S(2)}, u32[]{:S(2)}) collective-permute-start(bf16[256,256]{1,0:T(8,128)(2,1)S(1)} %collective-permute-done.40.refs_0_), channel_id=1, source_target_pairs={{0,4},{1,3},{4,8},{5,1},{8,12},{9,5},{12,14},{13,9},{14,10},{15,13... | collective-permute-start | bytes 393224 | tf_op jit(solution)/shard_map/ppermute | solution.py:56
  73.6 2.0 %collective-permute-start.37 = (bf16[256,256]{1,0:T(8,128)(2,1)S(1)}, bf16[256,256]{1,0:T(8,128)(2,1)S(1)}, u32[]{:S(2)}, u32[]{:S(2)}) collective-permute-start(bf16[256,256]{1,0:T(8,128)(2,1)S(1)} %collective-permute-done.36.refs_5_), channel_id=1, source_target_pairs={{0,4},{1,3},{4,8},{5,1},{8,12},{9,5},{12,14},{13,9},{14,10},{15,13... | collective-permute-start | bytes 393224 | tf_op jit(solution)/shard_map/ppermute | solution.py:56
  77.1 1.3 %shard_map.101 = (f32[4,256,256]{2,1,0:T(8,128)S(1)}, f32[2,256,256]{2,1,0:T(8,128)S(1)}) custom-call(s32[9]{0:T(128)S(1)} %stack.39.starts, bf16[256,256]{1,0:T(8,128)(2,1)S(1)} %collective-permute-done.40.refs_0_, bf16[256,256]{1,0:T(8,128)(2,1)S(1)} %collective-permute-done.35.refs_1_, bf16[256,256]{1,0:T(8,128)(2,1)S(1)} %collective-permute-done.31.refs_2_, ...), custom_call_target="tpu_custom_call" | custom-call | flops 268435456 | bytes 1024 | tf_op jit(solution)/shard_map/pallas_call | solution.py:69
  78.6 2.0 %collective-permute-done.33.refs_0_ = bf16[256,256]{1,0:T(8,128)(2,1)S(1)} collective-permute-done((bf16[256,256]{1,0:T(8,128)(2,1)S(1)}, bf16[256,256]{1,0:T(8,128)(2,1)S(1)}, u32[]{:S(2)}, u32[]{:S(2)}) %collective-permute-start.33) | collective-permute-done | bytes 131104 | tf_op jit(solution)/shard_map/ppermute | solution.py:56
  81.3 1.6 %shard_map.102 = (f32[512,128]{1,0:T(8,128)S(1)}, f32[1,128,2048]{2,1,0:T(8,128)}) custom-call(s32[9]{0:T(128)S(1)} %stack.39.starts, bf16[256,256]{1,0:T(8,128)(2,1)S(1)} %collective-permute-done.33.refs_0_, bf16[256,256]{1,0:T(8,128)(2,1)S(1)} %collective-permute-done.37.refs_1_, bf16[256,2048]{1,0:T(8,128)(2,1)S(1)} %maximum_maximum_fusion.stacked.refs_6_.refs_8_.refs_2_, ...), custom_call_target="tpu_custom_call" | custom-call | bytes 1024 | tf_op jit(solution)/shard_map/pallas_call | solution.py:69
  83.0 2.8 %shard_map.104 = (f32[1,2048,128]{2,1,0:T(8,128)}, f32[1,128]{1,0:T(1,128)}, f32[128,1024]{1,0:T(8,128)}) custom-call(s32[9]{0:T(128)S(1)} %stack.39.starts, bf16[2048,512]{1,0:T(8,128)(2,1)S(1)} %shard_map.99.turned, f32[512,128]{1,0:T(8,128)S(1)} %get-tuple-element.66.preact, f32[512,128]{1,0:T(8,128)S(1)} %get-tuple-element.83.back_own, ...), custom_call_target="tpu_custom_call" | custom-call | flops 268435456 | bytes 1024 | tf_op jit(solution)/shard_map/pallas_call | solution.py:69
  (92 shorter events, 26.8 us)
Async XLA Ops:
  1.7 6.8 %collective-permute-start.5 = (bf16[256,256]{1,0:T(8,128)(2,1)S(1)}, bf16[256,256]{1,0:T(8,128)(2,1)S(1)}, u32[]{:S(2)}, u32[]{:S(2)}) collective-permute-start(bf16[256,256]{1,0:T(8,128)(2,1)S(1)} %get-tuple-element.48.shard.refs_1_), channel_id=1, source_target_pairs={{0,4},{1,3},{4,8},{5,1},{8,12},{9,5},{12,14},{13,9},{14,10},{15,13... | collective-permute-start | bytes 393224 | tf_op jit(solution)/shard_map/ppermute | solution.py:56
  4.8 6.3 %collective-permute-start.1 = (bf16[256,256]{1,0:T(8,128)(2,1)S(1)}, bf16[256,256]{1,0:T(8,128)(2,1)S(1)}, u32[]{:S(2)}, u32[]{:S(2)}) collective-permute-start(bf16[256,256]{1,0:T(8,128)(2,1)S(1)} %get-tuple-element.47.shard.refs_0_), channel_id=1, source_target_pairs={{0,2},{1,5},{4,0},{5,9},{8,4},{9,13},{12,8},{13,15},{14,12},{15,11... | collective-permute-start | bytes 393224 | tf_op jit(solution)/shard_map/ppermute | solution.py:56
  5.5 6.0 %collective-permute-start = (bf16[256,256]{1,0:T(8,128)(2,1)S(1)}, bf16[256,256]{1,0:T(8,128)(2,1)S(1)}, u32[]{:S(2)}, u32[]{:S(2)}) collective-permute-start(bf16[256,256]{1,0:T(8,128)(2,1)S(1)} %get-tuple-element.47.shard.refs_0_), channel_id=1, source_target_pairs={{0,4},{1,3},{4,8},{5,1},{8,12},{9,5},{12,14},{13,9},{14,10},{15,13... | collective-permute-start | bytes 393224 | tf_op jit(solution)/shard_map/ppermute | solution.py:56
  8.5 6.2 %collective-permute-start.6 = (bf16[256,256]{1,0:T(8,128)(2,1)S(1)}, bf16[256,256]{1,0:T(8,128)(2,1)S(1)}, u32[]{:S(2)}, u32[]{:S(2)}) collective-permute-start(bf16[256,256]{1,0:T(8,128)(2,1)S(1)} %collective-permute-done.5.refs_3_.refs_1_), channel_id=1, source_target_pairs={{0,4},{1,3},{4,8},{5,1},{8,12},{9,5},{12,14},{13,9},{14,10},{15,13... | collective-permute-start | bytes 393224 | tf_op jit(solution)/shard_map/ppermute | solution.py:56
  11.1 5.8 %collective-permute-start.2 = (bf16[256,256]{1,0:T(8,128)(2,1)S(1)}, bf16[256,256]{1,0:T(8,128)(2,1)S(1)}, u32[]{:S(2)}, u32[]{:S(2)}) collective-permute-start(bf16[256,256]{1,0:T(8,128)(2,1)S(1)} %collective-permute-done.1.refs_4_.refs_2_), channel_id=1, source_target_pairs={{0,2},{1,5},{4,0},{5,9},{8,4},{9,13},{12,8},{13,15},{14,12},{15,11... | collective-permute-start | bytes 393224 | tf_op jit(solution)/shard_map/ppermute | solution.py:56
  11.5 12.0 %collective-permute-start.14 = (bf16[128,1024]{1,0:T(8,128)(2,1)}, bf16[128,1024]{1,0:T(8,128)(2,1)S(1)}, u32[]{:S(2)}, u32[]{:S(2)}) collective-permute-start(bf16[128,1024]{1,0:T(8,128)(2,1)} %param.11), channel_id=1, source_target_pairs={{0,1},{1,0},{2,3},{3,2},{4,5},{5,4},{6,7},{7,6},{8,9},{9,8},{10,11... | collective-permute-start | bytes 786440 | tf_op jit(solution)/shard_map/ppermute | solution.py:28
  11.5 6.3 %collective-permute-start.10 = (bf16[256,256]{1,0:T(8,128)(2,1)S(1)}, bf16[256,256]{1,0:T(8,128)(2,1)S(1)}, u32[]{:S(2)}, u32[]{:S(2)}) collective-permute-start(bf16[256,256]{1,0:T(8,128)(2,1)S(1)} %collective-permute-done.refs_2_.refs_0_), channel_id=1, source_target_pairs={{0,4},{1,3},{4,8},{5,1},{8,12},{9,5},{12,14},{13,9},{14,10},{15,13... | collective-permute-start | bytes 393224 | tf_op jit(solution)/shard_map/ppermute | solution.py:56
  14.0 6.4 %collective-permute-start.11 = (bf16[256,256]{1,0:T(8,128)(2,1)S(1)}, bf16[256,256]{1,0:T(8,128)(2,1)S(1)}, u32[]{:S(2)}, u32[]{:S(2)}) collective-permute-start(bf16[256,256]{1,0:T(8,128)(2,1)S(1)} %collective-permute-done.9.refs_5_.refs_3_), channel_id=1, source_target_pairs={{0,2},{1,5},{4,0},{5,9},{8,4},{9,13},{12,8},{13,15},{14,12},{15,11... | collective-permute-start | bytes 393224 | tf_op jit(solution)/shard_map/ppermute | solution.py:56
  14.7 6.0 %collective-permute-start.7 = (bf16[256,256]{1,0:T(8,128)(2,1)S(1)}, bf16[256,256]{1,0:T(8,128)(2,1)S(1)}, u32[]{:S(2)}, u32[]{:S(2)}) collective-permute-start(bf16[256,256]{1,0:T(8,128)(2,1)S(1)} %collective-permute-done.6.refs_7_.refs_5_), channel_id=1, source_target_pairs={{0,4},{1,3},{4,8},{5,1},{8,12},{9,5},{12,14},{13,9},{14,10},{15,13... | collective-permute-start | bytes 393224 | tf_op jit(solution)/shard_map/ppermute | solution.py:56
  16.9 6.4 %collective-permute-start.3 = (bf16[256,256]{1,0:T(8,128)(2,1)S(1)}, bf16[256,256]{1,0:T(8,128)(2,1)S(1)}, u32[]{:S(2)}, u32[]{:S(2)}) collective-permute-start(bf16[256,256]{1,0:T(8,128)(2,1)S(1)} %collective-permute-done.2.refs_8_.refs_6_), channel_id=1, source_target_pairs={{0,2},{1,5},{4,0},{5,9},{8,4},{9,13},{12,8},{13,15},{14,12},{15,11... | collective-permute-start | bytes 393224 | tf_op jit(solution)/shard_map/ppermute | solution.py:56
  17.8 7.0 %collective-permute-start.12 = (bf16[256,256]{1,0:T(8,128)(2,1)S(1)}, bf16[256,256]{1,0:T(8,128)(2,1)S(1)}, u32[]{:S(2)}, u32[]{:S(2)}) collective-permute-start(bf16[256,256]{1,0:T(8,128)(2,1)S(1)} %collective-permute-done.10.refs_6_.refs_4_), channel_id=1, source_target_pairs={{0,4},{1,3},{4,8},{5,1},{8,12},{9,5},{12,14},{13,9},{14,10},{15,13... | collective-permute-start | bytes 393224 | tf_op jit(solution)/shard_map/ppermute | solution.py:56
  20.8 6.3 %collective-permute-start.8 = (bf16[256,256]{1,0:T(8,128)(2,1)S(1)}, bf16[256,256]{1,0:T(8,128)(2,1)S(1)}, u32[]{:S(2)}, u32[]{:S(2)}) collective-permute-start(bf16[256,256]{1,0:T(8,128)(2,1)S(1)} %collective-permute-done.7.refs_11_.refs_9_), channel_id=1, source_target_pairs={{0,4},{1,3},{4,8},{5,1},{8,12},{9,5},{12,14},{13,9},{14,10},{15,13... | collective-permute-start | bytes 393224 | tf_op jit(solution)/shard_map/ppermute | solution.py:56
  31.3 6.1 %collective-permute-start.21 = (bf16[256,256]{1,0:T(8,128)(2,1)S(1)}, bf16[256,256]{1,0:T(8,128)(2,1)S(1)}, u32[]{:S(2)}, u32[]{:S(2)}) collective-permute-start(bf16[256,256]{1,0:T(8,128)(2,1)S(1)} %get-tuple-element.60), channel_id=1, source_target_pairs={{0,2},{1,5},{4,0},{5,9},{8,4},{9,13},{12,8},{13,15},{14,12},{15,11... | collective-permute-start | bytes 393224 | tf_op jit(solution)/shard_map/ppermute | solution.py:56
  31.5 5.9 %collective-permute-start.16 = (bf16[256,256]{1,0:T(8,128)(2,1)S(1)}, bf16[256,256]{1,0:T(8,128)(2,1)S(1)}, u32[]{:S(2)}, u32[]{:S(2)}) collective-permute-start(bf16[256,256]{1,0:T(8,128)(2,1)S(1)} %get-tuple-element.56), channel_id=1, source_target_pairs={{0,4},{1,3},{4,8},{5,1},{8,12},{9,5},{12,14},{13,9},{14,10},{15,13... | collective-permute-start | bytes 393224 | tf_op jit(solution)/shard_map/ppermute | solution.py:56
  34.6 6.4 %collective-permute-start.20 = (bf16[256,256]{1,0:T(8,128)(2,1)S(1)}, bf16[256,256]{1,0:T(8,128)(2,1)S(1)}, u32[]{:S(2)}, u32[]{:S(2)}) collective-permute-start(bf16[256,256]{1,0:T(8,128)(2,1)S(1)} %get-tuple-element.59), channel_id=1, source_target_pairs={{0,2},{1,5},{4,0},{5,9},{8,4},{9,13},{12,8},{13,15},{14,12},{15,11... | collective-permute-start | bytes 393224 | tf_op jit(solution)/shard_map/ppermute | solution.py:56
  34.9 6.3 %collective-permute-start.25 = (bf16[256,256]{1,0:T(8,128)(2,1)S(1)}, bf16[256,256]{1,0:T(8,128)(2,1)S(1)}, u32[]{:S(2)}, u32[]{:S(2)}) collective-permute-start(bf16[256,256]{1,0:T(8,128)(2,1)S(1)} %get-tuple-element.70), channel_id=1, source_target_pairs={{0,4},{1,3},{4,8},{5,1},{8,12},{9,5},{12,14},{13,9},{14,10},{15,13... | collective-permute-start | bytes 393224 | tf_op jit(solution)/shard_map/ppermute | solution.py:56
  37.4 6.4 %collective-permute-start.23 = (bf16[256,256]{1,0:T(8,128)(2,1)S(1)}, bf16[256,256]{1,0:T(8,128)(2,1)S(1)}, u32[]{:S(2)}, u32[]{:S(2)}) collective-permute-start(bf16[256,256]{1,0:T(8,128)(2,1)S(1)} %add_convert_fusion.4), channel_id=1, source_target_pairs={{0,2},{1,5},{4,0},{5,9},{8,4},{9,13},{12,8},{13,15},{14,12},{15,11... | collective-permute-start | bytes 393224 | tf_op jit(solution)/shard_map/ppermute | solution.py:56
  37.5 6.5 %collective-permute-start.17 = (bf16[256,256]{1,0:T(8,128)(2,1)S(1)}, bf16[256,256]{1,0:T(8,128)(2,1)S(1)}, u32[]{:S(2)}, u32[]{:S(2)}) collective-permute-start(bf16[256,256]{1,0:T(8,128)(2,1)S(1)} %add_convert_fusion.9), channel_id=1, source_target_pairs={{0,4},{1,3},{4,8},{5,1},{8,12},{9,5},{12,14},{13,9},{14,10},{15,13... | collective-permute-start | bytes 393224 | tf_op jit(solution)/shard_map/ppermute | solution.py:56
  41.2 6.0 %collective-permute-start.26 = (bf16[256,256]{1,0:T(8,128)(2,1)S(1)}, bf16[256,256]{1,0:T(8,128)(2,1)S(1)}, u32[]{:S(2)}, u32[]{:S(2)}) collective-permute-start(bf16[256,256]{1,0:T(8,128)(2,1)S(1)} %add_convert_fusion.3), channel_id=1, source_target_pairs={{0,4},{1,3},{4,8},{5,1},{8,12},{9,5},{12,14},{13,9},{14,10},{15,13... | collective-permute-start | bytes 393224 | tf_op jit(solution)/shard_map/ppermute | solution.py:56
  43.8 7.3 %collective-permute-start.28 = (bf16[256,256]{1,0:T(8,128)(2,1)S(1)}, bf16[256,256]{1,0:T(8,128)(2,1)S(1)}, u32[]{:S(2)}, u32[]{:S(2)}) collective-permute-start(bf16[256,256]{1,0:T(8,128)(2,1)S(1)} %add_convert_fusion.1), channel_id=1, source_target_pairs={{0,2},{1,5},{4,0},{5,9},{8,4},{9,13},{12,8},{13,15},{14,12},{15,11... | collective-permute-start | bytes 393224 | tf_op jit(solution)/shard_map/ppermute | solution.py:56
  46.6 6.5 %collective-permute-start.24 = (bf16[256,256]{1,0:T(8,128)(2,1)S(1)}, bf16[256,256]{1,0:T(8,128)(2,1)S(1)}, u32[]{:S(2)}, u32[]{:S(2)}) collective-permute-start(bf16[256,256]{1,0:T(8,128)(2,1)S(1)} %add_convert_fusion.5), channel_id=1, source_target_pairs={{0,2},{1,5},{4,0},{5,9},{8,4},{9,13},{12,8},{13,15},{14,12},{15,11... | collective-permute-start | bytes 393224 | tf_op jit(solution)/shard_map/ppermute | solution.py:56
  47.2 9.4 %collective-permute-start.27 = (bf16[256,256]{1,0:T(8,128)(2,1)S(1)}, bf16[256,256]{1,0:T(8,128)(2,1)S(1)}, u32[]{:S(2)}, u32[]{:S(2)}) collective-permute-start(bf16[256,256]{1,0:T(8,128)(2,1)S(1)} %add_convert_fusion.2), channel_id=1, source_target_pairs={{0,4},{1,3},{4,8},{5,1},{8,12},{9,5},{12,14},{13,9},{14,10},{15,13... | collective-permute-start | bytes 393224 | tf_op jit(solution)/shard_map/ppermute | solution.py:56
  55.1 6.2 %collective-permute-start.34 = (bf16[256,256]{1,0:T(8,128)(2,1)S(1)}, bf16[256,256]{1,0:T(8,128)(2,1)S(1)}, u32[]{:S(2)}, u32[]{:S(2)}) collective-permute-start(bf16[256,256]{1,0:T(8,128)(2,1)S(1)} %multiply_convert_fusion.refs_1_), channel_id=1, source_target_pairs={{0,4},{1,3},{4,8},{5,1},{8,12},{9,5},{12,14},{13,9},{14,10},{15,13... | collective-permute-start | bytes 393224 | tf_op jit(solution)/shard_map/ppermute | solution.py:56
  56.7 6.5 %collective-permute-start.30 = (bf16[256,256]{1,0:T(8,128)(2,1)S(1)}, bf16[256,256]{1,0:T(8,128)(2,1)S(1)}, u32[]{:S(2)}, u32[]{:S(2)}) collective-permute-start(bf16[256,256]{1,0:T(8,128)(2,1)S(1)} %fusion.1.refs_0_), channel_id=1, source_target_pairs={{0,2},{1,5},{4,0},{5,9},{8,4},{9,13},{12,8},{13,15},{14,12},{15,11... | collective-permute-start | bytes 393224 | tf_op jit(solution)/shard_map/ppermute | solution.py:56
  57.3 7.7 %collective-permute-start.39 = (bf16[256,256]{1,0:T(8,128)(2,1)S(1)}, bf16[256,256]{1,0:T(8,128)(2,1)S(1)}, u32[]{:S(2)}, u32[]{:S(2)}) collective-permute-start(bf16[256,256]{1,0:T(8,128)(2,1)S(1)} %multiply_convert_fusion.refs_1_), channel_id=1, source_target_pairs={{0,2},{1,5},{4,0},{5,9},{8,4},{9,13},{12,8},{13,15},{14,12},{15,11... | collective-permute-start | bytes 393224 | tf_op jit(solution)/shard_map/ppermute | solution.py:56
  58.8 7.0 %collective-permute-start.38 = (bf16[256,256]{1,0:T(8,128)(2,1)S(1)}, bf16[256,256]{1,0:T(8,128)(2,1)S(1)}, u32[]{:S(2)}, u32[]{:S(2)}) collective-permute-start(bf16[256,256]{1,0:T(8,128)(2,1)S(1)} %fusion.1.refs_0_), channel_id=1, source_target_pairs={{0,4},{1,3},{4,8},{5,1},{8,12},{9,5},{12,14},{13,9},{14,10},{15,13... | collective-permute-start | bytes 393224 | tf_op jit(solution)/shard_map/ppermute | solution.py:56
  61.3 5.8 %collective-permute-start.35 = (bf16[256,256]{1,0:T(8,128)(2,1)S(1)}, bf16[256,256]{1,0:T(8,128)(2,1)S(1)}, u32[]{:S(2)}, u32[]{:S(2)}) collective-permute-start(bf16[256,256]{1,0:T(8,128)(2,1)S(1)} %collective-permute-done.34.refs_3_), channel_id=1, source_target_pairs={{0,4},{1,3},{4,8},{5,1},{8,12},{9,5},{12,14},{13,9},{14,10},{15,13... | collective-permute-start | bytes 393224 | tf_op jit(solution)/shard_map/ppermute | solution.py:56
  63.2 5.9 %collective-permute-start.31 = (bf16[256,256]{1,0:T(8,128)(2,1)S(1)}, bf16[256,256]{1,0:T(8,128)(2,1)S(1)}, u32[]{:S(2)}, u32[]{:S(2)}) collective-permute-start(bf16[256,256]{1,0:T(8,128)(2,1)S(1)} %collective-permute-done.30.refs_4_), channel_id=1, source_target_pairs={{0,2},{1,5},{4,0},{5,9},{8,4},{9,13},{12,8},{13,15},{14,12},{15,11... | collective-permute-start | bytes 393224 | tf_op jit(solution)/shard_map/ppermute | solution.py:56
  65.1 6.5 %collective-permute-start.41 = (bf16[256,256]{1,0:T(8,128)(2,1)S(1)}, bf16[256,256]{1,0:T(8,128)(2,1)S(1)}, u32[]{:S(2)}, u32[]{:S(2)}) collective-permute-start(bf16[256,256]{1,0:T(8,128)(2,1)S(1)} %collective-permute-done.39.refs_5_), channel_id=1, source_target_pairs={{0,2},{1,5},{4,0},{5,9},{8,4},{9,13},{12,8},{13,15},{14,12},{15,11... | collective-permute-start | bytes 393224 | tf_op jit(solution)/shard_map/ppermute | solution.py:56
  65.9 6.3 %collective-permute-start.40 = (bf16[256,256]{1,0:T(8,128)(2,1)S(1)}, bf16[256,256]{1,0:T(8,128)(2,1)S(1)}, u32[]{:S(2)}, u32[]{:S(2)}) collective-permute-start(bf16[256,256]{1,0:T(8,128)(2,1)S(1)} %collective-permute-done.38.refs_2_), channel_id=1, source_target_pairs={{0,4},{1,3},{4,8},{5,1},{8,12},{9,5},{12,14},{13,9},{14,10},{15,13... | collective-permute-start | bytes 393224 | tf_op jit(solution)/shard_map/ppermute | solution.py:56
  67.1 6.5 %collective-permute-start.36 = (bf16[256,256]{1,0:T(8,128)(2,1)S(1)}, bf16[256,256]{1,0:T(8,128)(2,1)S(1)}, u32[]{:S(2)}, u32[]{:S(2)}) collective-permute-start(bf16[256,256]{1,0:T(8,128)(2,1)S(1)} %collective-permute-done.35.refs_1_), channel_id=1, source_target_pairs={{0,4},{1,3},{4,8},{5,1},{8,12},{9,5},{12,14},{13,9},{14,10},{15,13... | collective-permute-start | bytes 393224 | tf_op jit(solution)/shard_map/ppermute | solution.py:56
  69.1 6.6 %collective-permute-start.32 = (bf16[256,256]{1,0:T(8,128)(2,1)S(1)}, bf16[256,256]{1,0:T(8,128)(2,1)S(1)}, u32[]{:S(2)}, u32[]{:S(2)}) collective-permute-start(bf16[256,256]{1,0:T(8,128)(2,1)S(1)} %collective-permute-done.31.refs_2_), channel_id=1, source_target_pairs={{0,2},{1,5},{4,0},{5,9},{8,4},{9,13},{12,8},{13,15},{14,12},{15,11... | collective-permute-start | bytes 393224 | tf_op jit(solution)/shard_map/ppermute | solution.py:56
  (16 other events, 119.0 us)

commit v23 on v20

--- a/solution.py
+++ b/solution.py
@@ -46,14 +46,9 @@
 
 
 def hop(shard, way):
-    size, layers = lax.axis_size("latent"), lax.axis_size("layer")
+    size = lax.axis_size("latent")
     order = ring_order(size)
-    pairs = []
-    for p in range(size):
-        for layer in range(layers):
-            by = way if layer % 2 == 0 else -way
-            pairs.append((order[p] * layers + layer, order[(p + by) % size] * layers + layer))
-    return lax.ppermute(shard, ("latent", "layer"), pairs)
+    return lax.ppermute(shard, "latent", [(order[p], order[(p + way) % size]) for p in range(size)])
 
 
 def after(value, *others):
@@ -240,7 +235,6 @@
     reach = size // 2
     place = ring_place(lax.axis_index("latent"), size)
     layer = lax.axis_index("layer")
-    sign = jnp.where(layer % 2 == 0, 1, -1)
     rows, wide = residual_in.shape[1:]
     half = rows // 2
     deep, lat = enc_weight.shape[1:]
@@ -261,7 +255,7 @@
     for s in range(1, reach):
         offsets[slot_p[s]] = -s
         offsets[slot_q[s]] = s
-    starts = jnp.stack([ring_member(place + sign * offset, size) * wide for offset in offsets] + [layer])
+    starts = jnp.stack([ring_member(place + offset, size) * wide for offset in offsets] + [layer])
     starts = starts.astype(jnp.int32)
 
     urgent, later = ((0, -1), (1, 1)), ((0, 1), (1, -1))

time: 85.9 us -> 86.6 us (level)
  transfers between devices with their start and end apart: 45 -> 45, of which waited for: 28 -> 26; matrix products, arithmetic and copies ran while one was open for 2% -> 2% of each run, Pallas kernels for 10% -> 10%
where the time goes in v23:
time: 86.6 us; the launch traced here: 86.4 us
  starting transfers between devices  46 us (53%)
  waiting for transfers between devices  23.3 us (27%)
  Pallas kernels  13.5 us (16%)
  other arithmetic  1.56 us (2%)
  local copies, waits for them, and re-layouts  1.16 us (1%)
  between operations  0.91 us (1%)
    ppermute x42, starting transfers between devices, hop(): lax.ppermute(shard, 'latent', [(order[p], order[(p + way) % size]) for p...  45.8 us
    ppermute x42, waiting for transfers between devices, hop(): lax.ppermute(shard, 'latent', [(order[p], order[(p + way) % size]) for p...  21.9 us
    pallas_call x12, Pallas kernels, call(): pl.pallas_call(kernel, out_shape=outs, in_specs=[spec(pltpu.SMEM)] + [spe...  13.5 us
  transfers between devices with their start and end apart: 45, of which 26 were waited for; matrix products, arithmetic and copies ran while one was open for 2% of the time, Pallas kernels for 10%

profile of v23, /device:TPU:0, one launch (start us, length us, event | category | flops | bytes accessed | tf_op | source)
XLA Modules:
  0.0 86.4 jit_solution(4928117737456506441)
XLA Ops:
  1.7 3.1 %collective-permute-start.5 = (bf16[256,256]{1,0:T(8,128)(2,1)S(1)}, bf16[256,256]{1,0:T(8,128)(2,1)S(1)}, u32[]{:S(2)}, u32[]{:S(2)}) collective-permute-start(bf16[256,256]{1,0:T(8,128)(2,1)S(1)} %get-tuple-element.48.shard.refs_1_), channel_id=1, source_target_pairs={{0,4},{4,8},{8,12},{12,14},{14,10},{10,6},{6,2},{2,0},{1,5},{5,9},... | collective-permute-start | bytes 393224 | tf_op jit(solution)/shard_map/ppermute | solution.py:51
  5.5 2.1 %collective-permute-start = (bf16[256,256]{1,0:T(8,128)(2,1)S(1)}, bf16[256,256]{1,0:T(8,128)(2,1)S(1)}, u32[]{:S(2)}, u32[]{:S(2)}) collective-permute-start(bf16[256,256]{1,0:T(8,128)(2,1)S(1)} %get-tuple-element.47.shard.refs_0_), channel_id=1, source_target_pairs={{0,4},{4,8},{8,12},{12,14},{14,10},{10,6},{6,2},{2,0},{1,5},{5,9},... | collective-permute-start | bytes 393224 | tf_op jit(solution)/shard_map/ppermute | solution.py:51
  8.6 2.0 %collective-permute-start.6 = (bf16[256,256]{1,0:T(8,128)(2,1)S(1)}, bf16[256,256]{1,0:T(8,128)(2,1)S(1)}, u32[]{:S(2)}, u32[]{:S(2)}) collective-permute-start(bf16[256,256]{1,0:T(8,128)(2,1)S(1)} %collective-permute-done.5.refs_3_.refs_1_), channel_id=1, source_target_pairs={{0,4},{4,8},{8,12},{12,14},{14,10},{10,6},{6,2},{2,0},{1,5},{5,9},... | collective-permute-start | bytes 393224 | tf_op jit(solution)/shard_map/ppermute | solution.py:51
  10.7 1.3 %collective-permute-done.refs_2_.refs_0_ = bf16[256,256]{1,0:T(8,128)(2,1)S(1)} collective-permute-done((bf16[256,256]{1,0:T(8,128)(2,1)S(1)}, bf16[256,256]{1,0:T(8,128)(2,1)S(1)}, u32[]{:S(2)}, u32[]{:S(2)}) %collective-permute-start) | collective-permute-done | bytes 131104 | tf_op jit(solution)/shard_map/ppermute | solution.py:51
  12.0 2.1 %collective-permute-start.10 = (bf16[256,256]{1,0:T(8,128)(2,1)S(1)}, bf16[256,256]{1,0:T(8,128)(2,1)S(1)}, u32[]{:S(2)}, u32[]{:S(2)}) collective-permute-start(bf16[256,256]{1,0:T(8,128)(2,1)S(1)} %collective-permute-done.refs_2_.refs_0_), channel_id=1, source_target_pairs={{0,4},{4,8},{8,12},{12,14},{14,10},{10,6},{6,2},{2,0},{1,5},{5,9},... | collective-permute-start | bytes 393224 | tf_op jit(solution)/shard_map/ppermute | solution.py:51
  14.6 1.5 %collective-permute-start.7 = (bf16[256,256]{1,0:T(8,128)(2,1)S(1)}, bf16[256,256]{1,0:T(8,128)(2,1)S(1)}, u32[]{:S(2)}, u32[]{:S(2)}) collective-permute-start(bf16[256,256]{1,0:T(8,128)(2,1)S(1)} %collective-permute-done.6.refs_7_.refs_5_), channel_id=1, source_target_pairs={{0,4},{4,8},{8,12},{12,14},{14,10},{10,6},{6,2},{2,0},{1,5},{5,9},... | collective-permute-start | bytes 393224 | tf_op jit(solution)/shard_map/ppermute | solution.py:51
  16.7 1.7 %collective-permute-done.10.refs_6_.refs_4_ = bf16[256,256]{1,0:T(8,128)(2,1)S(1)} collective-permute-done((bf16[256,256]{1,0:T(8,128)(2,1)S(1)}, bf16[256,256]{1,0:T(8,128)(2,1)S(1)}, u32[]{:S(2)}, u32[]{:S(2)}) %collective-permute-start.10) | collective-permute-done | bytes 131104 | tf_op jit(solution)/shard_map/ppermute | solution.py:51
  18.3 2.0 %collective-permute-start.12 = (bf16[256,256]{1,0:T(8,128)(2,1)S(1)}, bf16[256,256]{1,0:T(8,128)(2,1)S(1)}, u32[]{:S(2)}, u32[]{:S(2)}) collective-permute-start(bf16[256,256]{1,0:T(8,128)(2,1)S(1)} %collective-permute-done.10.refs_6_.refs_4_), channel_id=1, source_target_pairs={{0,4},{4,8},{8,12},{12,14},{14,10},{10,6},{6,2},{2,0},{1,5},{5,9},... | collective-permute-start | bytes 393224 | tf_op jit(solution)/shard_map/ppermute | solution.py:51
  21.1 2.0 %collective-permute-start.8 = (bf16[256,256]{1,0:T(8,128)(2,1)S(1)}, bf16[256,256]{1,0:T(8,128)(2,1)S(1)}, u32[]{:S(2)}, u32[]{:S(2)}) collective-permute-start(bf16[256,256]{1,0:T(8,128)(2,1)S(1)} %collective-permute-done.7.refs_11_.refs_9_), channel_id=1, source_target_pairs={{0,4},{4,8},{8,12},{12,14},{14,10},{10,6},{6,2},{2,0},{1,5},{5,9},... | collective-permute-start | bytes 393224 | tf_op jit(solution)/shard_map/ppermute | solution.py:51
  24.4 1.8 %collective-permute-done.13.refs_13_.refs_11_ = bf16[256,256]{1,0:T(8,128)(2,1)S(1)} collective-permute-done((bf16[256,256]{1,0:T(8,128)(2,1)S(1)}, bf16[256,256]{1,0:T(8,128)(2,1)S(1)}, u32[]{:S(2)}, u32[]{:S(2)}) %collective-permute-start.13) | collective-permute-done | bytes 131104 | tf_op jit(solution)/shard_map/ppermute | solution.py:51
  29.1 1.3 %collective-permute-done.15.earlier = bf16[512,128]{1,0:T(8,128)(2,1)S(1)} collective-permute-done((bf16[512,128]{1,0:T(8,128)(2,1)S(1)}, bf16[512,128]{1,0:T(8,128)(2,1)S(1)}, u32[]{:S(2)}, u32[]{:S(2)}) %collective-permute-start.15) | collective-permute-done | bytes 131104 | tf_op jit(solution)/shard_map/ppermute | solution.py:28
  31.8 1.6 %collective-permute-start.16 = (bf16[256,256]{1,0:T(8,128)(2,1)S(1)}, bf16[256,256]{1,0:T(8,128)(2,1)S(1)}, u32[]{:S(2)}, u32[]{:S(2)}) collective-permute-start(bf16[256,256]{1,0:T(8,128)(2,1)S(1)} %get-tuple-element.56), channel_id=1, source_target_pairs={{0,4},{4,8},{8,12},{12,14},{14,10},{10,6},{6,2},{2,0},{1,5},{5,9},... | collective-permute-start | bytes 393224 | tf_op jit(solution)/shard_map/ppermute | solution.py:51
  35.2 1.5 %collective-permute-start.25 = (bf16[256,256]{1,0:T(8,128)(2,1)S(1)}, bf16[256,256]{1,0:T(8,128)(2,1)S(1)}, u32[]{:S(2)}, u32[]{:S(2)}) collective-permute-start(bf16[256,256]{1,0:T(8,128)(2,1)S(1)} %get-tuple-element.70), channel_id=1, source_target_pairs={{0,4},{4,8},{8,12},{12,14},{14,10},{10,6},{6,2},{2,0},{1,5},{5,9},... | collective-permute-start | bytes 393224 | tf_op jit(solution)/shard_map/ppermute | solution.py:51
  37.5 1.6 %collective-permute-start.17 = (bf16[256,256]{1,0:T(8,128)(2,1)S(1)}, bf16[256,256]{1,0:T(8,128)(2,1)S(1)}, u32[]{:S(2)}, u32[]{:S(2)}) collective-permute-start(bf16[256,256]{1,0:T(8,128)(2,1)S(1)} %add_convert_fusion.9), channel_id=1, source_target_pairs={{0,4},{4,8},{8,12},{12,14},{14,10},{10,6},{6,2},{2,0},{1,5},{5,9},... | collective-permute-start | bytes 393224 | tf_op jit(solution)/shard_map/ppermute | solution.py:51
  39.0 1.5 %collective-permute-done.20 = bf16[256,256]{1,0:T(8,128)(2,1)S(1)} collective-permute-done((bf16[256,256]{1,0:T(8,128)(2,1)S(1)}, bf16[256,256]{1,0:T(8,128)(2,1)S(1)}, u32[]{:S(2)}, u32[]{:S(2)}) %collective-permute-start.20) | collective-permute-done | bytes 131104 | tf_op jit(solution)/shard_map/ppermute | solution.py:51
  41.2 1.6 %collective-permute-start.26 = (bf16[256,256]{1,0:T(8,128)(2,1)S(1)}, bf16[256,256]{1,0:T(8,128)(2,1)S(1)}, u32[]{:S(2)}, u32[]{:S(2)}) collective-permute-start(bf16[256,256]{1,0:T(8,128)(2,1)S(1)} %add_convert_fusion.3), channel_id=1, source_target_pairs={{0,4},{4,8},{8,12},{12,14},{14,10},{10,6},{6,2},{2,0},{1,5},{5,9},... | collective-permute-start | bytes 393224 | tf_op jit(solution)/shard_map/ppermute | solution.py:51
  44.0 1.6 %collective-permute-start.18 = (bf16[256,256]{1,0:T(8,128)(2,1)S(1)}, bf16[256,256]{1,0:T(8,128)(2,1)S(1)}, u32[]{:S(2)}, u32[]{:S(2)}) collective-permute-start(bf16[256,256]{1,0:T(8,128)(2,1)S(1)} %add_convert_fusion.8), channel_id=1, source_target_pairs={{0,4},{4,8},{8,12},{12,14},{14,10},{10,6},{6,2},{2,0},{1,5},{5,9},... | collective-permute-start | bytes 393224 | tf_op jit(solution)/shard_map/ppermute | solution.py:51
  47.6 1.6 %collective-permute-start.27 = (bf16[256,256]{1,0:T(8,128)(2,1)S(1)}, bf16[256,256]{1,0:T(8,128)(2,1)S(1)}, u32[]{:S(2)}, u32[]{:S(2)}) collective-permute-start(bf16[256,256]{1,0:T(8,128)(2,1)S(1)} %add_convert_fusion.2), channel_id=1, source_target_pairs={{0,4},{4,8},{8,12},{12,14},{14,10},{10,6},{6,2},{2,0},{1,5},{5,9},... | collective-permute-start | bytes 393224 | tf_op jit(solution)/shard_map/ppermute | solution.py:51
  50.4 1.6 %collective-permute-start.19 = (bf16[256,256]{1,0:T(8,128)(2,1)S(1)}, bf16[256,256]{1,0:T(8,128)(2,1)S(1)}, u32[]{:S(2)}, u32[]{:S(2)}) collective-permute-start(bf16[256,256]{1,0:T(8,128)(2,1)S(1)} %add_convert_fusion.7), channel_id=1, source_target_pairs={{0,4},{4,8},{8,12},{12,14},{14,10},{10,6},{6,2},{2,0},{1,5},{5,9},... | collective-permute-start | bytes 393224 | tf_op jit(solution)/shard_map/ppermute | solution.py:51
  52.6 3.3 %collective-permute-done.19 = bf16[256,256]{1,0:T(8,128)(2,1)S(1)} collective-permute-done((bf16[256,256]{1,0:T(8,128)(2,1)S(1)}, bf16[256,256]{1,0:T(8,128)(2,1)S(1)}, u32[]{:S(2)}, u32[]{:S(2)}) %collective-permute-start.19) | collective-permute-done | bytes 131104 | tf_op jit(solution)/shard_map/ppermute | solution.py:51
  55.9 1.6 %collective-permute-start.34 = (bf16[256,256]{1,0:T(8,128)(2,1)S(1)}, bf16[256,256]{1,0:T(8,128)(2,1)S(1)}, u32[]{:S(2)}, u32[]{:S(2)}) collective-permute-start(bf16[256,256]{1,0:T(8,128)(2,1)S(1)} %multiply_convert_fusion.refs_1_), channel_id=1, source_target_pairs={{0,4},{4,8},{8,12},{12,14},{14,10},{10,6},{6,2},{2,0},{1,5},{5,9},... | collective-permute-start | bytes 393224 | tf_op jit(solution)/shard_map/ppermute | solution.py:51
  58.4 1.4 %collective-permute-start.39 = (bf16[256,256]{1,0:T(8,128)(2,1)S(1)}, bf16[256,256]{1,0:T(8,128)(2,1)S(1)}, u32[]{:S(2)}, u32[]{:S(2)}) collective-permute-start(bf16[256,256]{1,0:T(8,128)(2,1)S(1)} %multiply_convert_fusion.refs_1_), channel_id=1, source_target_pairs={{0,2},{4,0},{8,4},{12,8},{14,12},{10,14},{6,10},{2,6},{1,3},{5,1},... | collective-permute-start | bytes 393224 | tf_op jit(solution)/shard_map/ppermute | solution.py:51
  60.4 2.0 %collective-permute-done.34.refs_3_ = bf16[256,256]{1,0:T(8,128)(2,1)S(1)} collective-permute-done((bf16[256,256]{1,0:T(8,128)(2,1)S(1)}, bf16[256,256]{1,0:T(8,128)(2,1)S(1)}, u32[]{:S(2)}, u32[]{:S(2)}) %collective-permute-start.34) | collective-permute-done | bytes 131104 | tf_op jit(solution)/shard_map/ppermute | solution.py:51
  62.4 1.5 %collective-permute-start.35 = (bf16[256,256]{1,0:T(8,128)(2,1)S(1)}, bf16[256,256]{1,0:T(8,128)(2,1)S(1)}, u32[]{:S(2)}, u32[]{:S(2)}) collective-permute-start(bf16[256,256]{1,0:T(8,128)(2,1)S(1)} %collective-permute-done.34.refs_3_), channel_id=1, source_target_pairs={{0,4},{4,8},{8,12},{12,14},{14,10},{10,6},{6,2},{2,0},{1,5},{5,9},... | collective-permute-start | bytes 393224 | tf_op jit(solution)/shard_map/ppermute | solution.py:51
  67.2 1.5 %collective-permute-start.40 = (bf16[256,256]{1,0:T(8,128)(2,1)S(1)}, bf16[256,256]{1,0:T(8,128)(2,1)S(1)}, u32[]{:S(2)}, u32[]{:S(2)}) collective-permute-start(bf16[256,256]{1,0:T(8,128)(2,1)S(1)} %collective-permute-done.38.refs_2_), channel_id=1, source_target_pairs={{0,4},{4,8},{8,12},{12,14},{14,10},{10,6},{6,2},{2,0},{1,5},{5,9},... | collective-permute-start | bytes 393224 | tf_op jit(solution)/shard_map/ppermute | solution.py:51
  71.0 1.5 %collective-permute-done.41.refs_3_ = bf16[256,256]{1,0:T(8,128)(2,1)S(1)} collective-permute-done((bf16[256,256]{1,0:T(8,128)(2,1)S(1)}, bf16[256,256]{1,0:T(8,128)(2,1)S(1)}, u32[]{:S(2)}, u32[]{:S(2)}) %collective-permute-start.41) | collective-permute-done | bytes 131104 | tf_op jit(solution)/shard_map/ppermute | solution.py:51
  72.6 2.1 %collective-permute-start.42 = (bf16[256,256]{1,0:T(8,128)(2,1)S(1)}, bf16[256,256]{1,0:T(8,128)(2,1)S(1)}, u32[]{:S(2)}, u32[]{:S(2)}) collective-permute-start(bf16[256,256]{1,0:T(8,128)(2,1)S(1)} %collective-permute-done.40.refs_0_), channel_id=1, source_target_pairs={{0,4},{4,8},{8,12},{12,14},{14,10},{10,6},{6,2},{2,0},{1,5},{5,9},... | collective-permute-start | bytes 393224 | tf_op jit(solution)/shard_map/ppermute | solution.py:51
  74.9 1.4 %collective-permute-start.37 = (bf16[256,256]{1,0:T(8,128)(2,1)S(1)}, bf16[256,256]{1,0:T(8,128)(2,1)S(1)}, u32[]{:S(2)}, u32[]{:S(2)}) collective-permute-start(bf16[256,256]{1,0:T(8,128)(2,1)S(1)} %collective-permute-done.36.refs_5_), channel_id=1, source_target_pairs={{0,4},{4,8},{8,12},{12,14},{14,10},{10,6},{6,2},{2,0},{1,5},{5,9},... | collective-permute-start | bytes 393224 | tf_op jit(solution)/shard_map/ppermute | solution.py:51
  78.1 1.3 %shard_map.101 = (f32[4,256,256]{2,1,0:T(8,128)S(1)}, f32[2,256,256]{2,1,0:T(8,128)S(1)}) custom-call(s32[9]{0:T(128)S(1)} %stack.39.starts, bf16[256,256]{1,0:T(8,128)(2,1)S(1)} %collective-permute-done.40.refs_0_, bf16[256,256]{1,0:T(8,128)(2,1)S(1)} %collective-permute-done.35.refs_1_, bf16[256,256]{1,0:T(8,128)(2,1)S(1)} %collective-permute-done.31.refs_2_, ...), custom_call_target="tpu_custom_call" | custom-call | flops 268435456 | bytes 1024 | tf_op jit(solution)/shard_map/pallas_call | solution.py:64
  79.9 1.4 %collective-permute-done.33.refs_0_ = bf16[256,256]{1,0:T(8,128)(2,1)S(1)} collective-permute-done((bf16[256,256]{1,0:T(8,128)(2,1)S(1)}, bf16[256,256]{1,0:T(8,128)(2,1)S(1)}, u32[]{:S(2)}, u32[]{:S(2)}) %collective-permute-start.33) | collective-permute-done | bytes 131104 | tf_op jit(solution)/shard_map/ppermute | solution.py:51
  82.0 1.6 %shard_map.102 = (f32[512,128]{1,0:T(8,128)S(1)}, f32[1,128,2048]{2,1,0:T(8,128)}) custom-call(s32[9]{0:T(128)S(1)} %stack.39.starts, bf16[256,256]{1,0:T(8,128)(2,1)S(1)} %collective-permute-done.33.refs_0_, bf16[256,256]{1,0:T(8,128)(2,1)S(1)} %collective-permute-done.37.refs_1_, bf16[256,2048]{1,0:T(8,128)(2,1)S(1)} %pad_maximum_fusion.stacked.refs_6_.refs_8_.refs_2_, ...), custom_call_target="tpu_custom_call" | custom-call | bytes 1024 | tf_op jit(solution)/shard_map/pallas_call | solution.py:64
  83.7 2.7 %shard_map.104 = (f32[1,2048,128]{2,1,0:T(8,128)}, f32[1,128]{1,0:T(1,128)}, f32[128,1024]{1,0:T(8,128)}) custom-call(s32[9]{0:T(128)S(1)} %stack.39.starts, bf16[2048,512]{1,0:T(8,128)(2,1)S(1)} %shard_map.99.turned, f32[512,128]{1,0:T(8,128)S(1)} %get-tuple-element.66.preact, f32[512,128]{1,0:T(8,128)S(1)} %get-tuple-element.83.back_own, ...), custom_call_target="tpu_custom_call" | custom-call | flops 268435456 | bytes 1024 | tf_op jit(solution)/shard_map/pallas_call | solution.py:64
  (95 shorter events, 29.1 us)
Async XLA Ops:
  1.7 6.9 %collective-permute-start.5 = (bf16[256,256]{1,0:T(8,128)(2,1)S(1)}, bf16[256,256]{1,0:T(8,128)(2,1)S(1)}, u32[]{:S(2)}, u32[]{:S(2)}) collective-permute-start(bf16[256,256]{1,0:T(8,128)(2,1)S(1)} %get-tuple-element.48.shard.refs_1_), channel_id=1, source_target_pairs={{0,4},{4,8},{8,12},{12,14},{14,10},{10,6},{6,2},{2,0},{1,5},{5,9},... | collective-permute-start | bytes 393224 | tf_op jit(solution)/shard_map/ppermute | solution.py:51
  4.8 5.8 %collective-permute-start.1 = (bf16[256,256]{1,0:T(8,128)(2,1)S(1)}, bf16[256,256]{1,0:T(8,128)(2,1)S(1)}, u32[]{:S(2)}, u32[]{:S(2)}) collective-permute-start(bf16[256,256]{1,0:T(8,128)(2,1)S(1)} %get-tuple-element.47.shard.refs_0_), channel_id=1, source_target_pairs={{0,2},{4,0},{8,4},{12,8},{14,12},{10,14},{6,10},{2,6},{1,3},{5,1},... | collective-permute-start | bytes 393224 | tf_op jit(solution)/shard_map/ppermute | solution.py:51
  5.5 6.4 %collective-permute-start = (bf16[256,256]{1,0:T(8,128)(2,1)S(1)}, bf16[256,256]{1,0:T(8,128)(2,1)S(1)}, u32[]{:S(2)}, u32[]{:S(2)}) collective-permute-start(bf16[256,256]{1,0:T(8,128)(2,1)S(1)} %get-tuple-element.47.shard.refs_0_), channel_id=1, source_target_pairs={{0,4},{4,8},{8,12},{12,14},{14,10},{10,6},{6,2},{2,0},{1,5},{5,9},... | collective-permute-start | bytes 393224 | tf_op jit(solution)/shard_map/ppermute | solution.py:51
  8.2 5.9 %collective-permute-start.9 = (bf16[256,256]{1,0:T(8,128)(2,1)S(1)}, bf16[256,256]{1,0:T(8,128)(2,1)S(1)}, u32[]{:S(2)}, u32[]{:S(2)}) collective-permute-start(bf16[256,256]{1,0:T(8,128)(2,1)S(1)} %get-tuple-element.48.shard.refs_1_), channel_id=1, source_target_pairs={{0,2},{4,0},{8,4},{12,8},{14,12},{10,14},{6,10},{2,6},{1,3},{5,1},... | collective-permute-start | bytes 393224 | tf_op jit(solution)/shard_map/ppermute | solution.py:51
  8.6 6.0 %collective-permute-start.6 = (bf16[256,256]{1,0:T(8,128)(2,1)S(1)}, bf16[256,256]{1,0:T(8,128)(2,1)S(1)}, u32[]{:S(2)}, u32[]{:S(2)}) collective-permute-start(bf16[256,256]{1,0:T(8,128)(2,1)S(1)} %collective-permute-done.5.refs_3_.refs_1_), channel_id=1, source_target_pairs={{0,4},{4,8},{8,12},{12,14},{14,10},{10,6},{6,2},{2,0},{1,5},{5,9},... | collective-permute-start | bytes 393224 | tf_op jit(solution)/shard_map/ppermute | solution.py:51
  12.0 11.2 %collective-permute-start.14 = (bf16[128,1024]{1,0:T(8,128)(2,1)}, bf16[128,1024]{1,0:T(8,128)(2,1)S(1)}, u32[]{:S(2)}, u32[]{:S(2)}) collective-permute-start(bf16[128,1024]{1,0:T(8,128)(2,1)} %param.11), channel_id=1, source_target_pairs={{0,1},{1,0},{2,3},{3,2},{4,5},{5,4},{6,7},{7,6},{8,9},{9,8},{10,11... | collective-permute-start | bytes 786440 | tf_op jit(solution)/shard_map/ppermute | solution.py:28
  12.0 6.4 %collective-permute-start.10 = (bf16[256,256]{1,0:T(8,128)(2,1)S(1)}, bf16[256,256]{1,0:T(8,128)(2,1)S(1)}, u32[]{:S(2)}, u32[]{:S(2)}) collective-permute-start(bf16[256,256]{1,0:T(8,128)(2,1)S(1)} %collective-permute-done.refs_2_.refs_0_), channel_id=1, source_target_pairs={{0,4},{4,8},{8,12},{12,14},{14,10},{10,6},{6,2},{2,0},{1,5},{5,9},... | collective-permute-start | bytes 393224 | tf_op jit(solution)/shard_map/ppermute | solution.py:51
  14.1 6.3 %collective-permute-start.11 = (bf16[256,256]{1,0:T(8,128)(2,1)S(1)}, bf16[256,256]{1,0:T(8,128)(2,1)S(1)}, u32[]{:S(2)}, u32[]{:S(2)}) collective-permute-start(bf16[256,256]{1,0:T(8,128)(2,1)S(1)} %collective-permute-done.9.refs_5_.refs_3_), channel_id=1, source_target_pairs={{0,2},{4,0},{8,4},{12,8},{14,12},{10,14},{6,10},{2,6},{1,3},{5,1},... | collective-permute-start | bytes 393224 | tf_op jit(solution)/shard_map/ppermute | solution.py:51
  14.6 6.5 %collective-permute-start.7 = (bf16[256,256]{1,0:T(8,128)(2,1)S(1)}, bf16[256,256]{1,0:T(8,128)(2,1)S(1)}, u32[]{:S(2)}, u32[]{:S(2)}) collective-permute-start(bf16[256,256]{1,0:T(8,128)(2,1)S(1)} %collective-permute-done.6.refs_7_.refs_5_), channel_id=1, source_target_pairs={{0,4},{4,8},{8,12},{12,14},{14,10},{10,6},{6,2},{2,0},{1,5},{5,9},... | collective-permute-start | bytes 393224 | tf_op jit(solution)/shard_map/ppermute | solution.py:51
  16.2 7.0 %collective-permute-start.3 = (bf16[256,256]{1,0:T(8,128)(2,1)S(1)}, bf16[256,256]{1,0:T(8,128)(2,1)S(1)}, u32[]{:S(2)}, u32[]{:S(2)}) collective-permute-start(bf16[256,256]{1,0:T(8,128)(2,1)S(1)} %collective-permute-done.2.refs_8_.refs_6_), channel_id=1, source_target_pairs={{0,2},{4,0},{8,4},{12,8},{14,12},{10,14},{6,10},{2,6},{1,3},{5,1},... | collective-permute-start | bytes 393224 | tf_op jit(solution)/shard_map/ppermute | solution.py:51
  18.3 6.0 %collective-permute-start.12 = (bf16[256,256]{1,0:T(8,128)(2,1)S(1)}, bf16[256,256]{1,0:T(8,128)(2,1)S(1)}, u32[]{:S(2)}, u32[]{:S(2)}) collective-permute-start(bf16[256,256]{1,0:T(8,128)(2,1)S(1)} %collective-permute-done.10.refs_6_.refs_4_), channel_id=1, source_target_pairs={{0,4},{4,8},{8,12},{12,14},{14,10},{10,6},{6,2},{2,0},{1,5},{5,9},... | collective-permute-start | bytes 393224 | tf_op jit(solution)/shard_map/ppermute | solution.py:51
  21.1 6.2 %collective-permute-start.8 = (bf16[256,256]{1,0:T(8,128)(2,1)S(1)}, bf16[256,256]{1,0:T(8,128)(2,1)S(1)}, u32[]{:S(2)}, u32[]{:S(2)}) collective-permute-start(bf16[256,256]{1,0:T(8,128)(2,1)S(1)} %collective-permute-done.7.refs_11_.refs_9_), channel_id=1, source_target_pairs={{0,4},{4,8},{8,12},{12,14},{14,10},{10,6},{6,2},{2,0},{1,5},{5,9},... | collective-permute-start | bytes 393224 | tf_op jit(solution)/shard_map/ppermute | solution.py:51
  34.6 5.9 %collective-permute-start.20 = (bf16[256,256]{1,0:T(8,128)(2,1)S(1)}, bf16[256,256]{1,0:T(8,128)(2,1)S(1)}, u32[]{:S(2)}, u32[]{:S(2)}) collective-permute-start(bf16[256,256]{1,0:T(8,128)(2,1)S(1)} %get-tuple-element.59), channel_id=1, source_target_pairs={{0,2},{4,0},{8,4},{12,8},{14,12},{10,14},{6,10},{2,6},{1,3},{5,1},... | collective-permute-start | bytes 393224 | tf_op jit(solution)/shard_map/ppermute | solution.py:51
  35.2 6.0 %collective-permute-start.25 = (bf16[256,256]{1,0:T(8,128)(2,1)S(1)}, bf16[256,256]{1,0:T(8,128)(2,1)S(1)}, u32[]{:S(2)}, u32[]{:S(2)}) collective-permute-start(bf16[256,256]{1,0:T(8,128)(2,1)S(1)} %get-tuple-element.70), channel_id=1, source_target_pairs={{0,4},{4,8},{8,12},{12,14},{14,10},{10,6},{6,2},{2,0},{1,5},{5,9},... | collective-permute-start | bytes 393224 | tf_op jit(solution)/shard_map/ppermute | solution.py:51
  36.9 6.5 %collective-permute-start.23 = (bf16[256,256]{1,0:T(8,128)(2,1)S(1)}, bf16[256,256]{1,0:T(8,128)(2,1)S(1)}, u32[]{:S(2)}, u32[]{:S(2)}) collective-permute-start(bf16[256,256]{1,0:T(8,128)(2,1)S(1)} %add_convert_fusion.4), channel_id=1, source_target_pairs={{0,2},{4,0},{8,4},{12,8},{14,12},{10,14},{6,10},{2,6},{1,3},{5,1},... | collective-permute-start | bytes 393224 | tf_op jit(solution)/shard_map/ppermute | solution.py:51
  37.5 6.5 %collective-permute-start.17 = (bf16[256,256]{1,0:T(8,128)(2,1)S(1)}, bf16[256,256]{1,0:T(8,128)(2,1)S(1)}, u32[]{:S(2)}, u32[]{:S(2)}) collective-permute-start(bf16[256,256]{1,0:T(8,128)(2,1)S(1)} %add_convert_fusion.9), channel_id=1, source_target_pairs={{0,4},{4,8},{8,12},{12,14},{14,10},{10,6},{6,2},{2,0},{1,5},{5,9},... | collective-permute-start | bytes 393224 | tf_op jit(solution)/shard_map/ppermute | solution.py:51
  40.5 6.2 %collective-permute-start.22 = (bf16[256,256]{1,0:T(8,128)(2,1)S(1)}, bf16[256,256]{1,0:T(8,128)(2,1)S(1)}, u32[]{:S(2)}, u32[]{:S(2)}) collective-permute-start(bf16[256,256]{1,0:T(8,128)(2,1)S(1)} %add_convert_fusion.6), channel_id=1, source_target_pairs={{0,2},{4,0},{8,4},{12,8},{14,12},{10,14},{6,10},{2,6},{1,3},{5,1},... | collective-permute-start | bytes 393224 | tf_op jit(solution)/shard_map/ppermute | solution.py:51
  41.2 6.4 %collective-permute-start.26 = (bf16[256,256]{1,0:T(8,128)(2,1)S(1)}, bf16[256,256]{1,0:T(8,128)(2,1)S(1)}, u32[]{:S(2)}, u32[]{:S(2)}) collective-permute-start(bf16[256,256]{1,0:T(8,128)(2,1)S(1)} %add_convert_fusion.3), channel_id=1, source_target_pairs={{0,4},{4,8},{8,12},{12,14},{14,10},{10,6},{6,2},{2,0},{1,5},{5,9},... | collective-permute-start | bytes 393224 | tf_op jit(solution)/shard_map/ppermute | solution.py:51
  43.4 8.6 %collective-permute-start.28 = (bf16[256,256]{1,0:T(8,128)(2,1)S(1)}, bf16[256,256]{1,0:T(8,128)(2,1)S(1)}, u32[]{:S(2)}, u32[]{:S(2)}) collective-permute-start(bf16[256,256]{1,0:T(8,128)(2,1)S(1)} %add_convert_fusion.1), channel_id=1, source_target_pairs={{0,2},{4,0},{8,4},{12,8},{14,12},{10,14},{6,10},{2,6},{1,3},{5,1},... | collective-permute-start | bytes 393224 | tf_op jit(solution)/shard_map/ppermute | solution.py:51
  44.0 6.4 %collective-permute-start.18 = (bf16[256,256]{1,0:T(8,128)(2,1)S(1)}, bf16[256,256]{1,0:T(8,128)(2,1)S(1)}, u32[]{:S(2)}, u32[]{:S(2)}) collective-permute-start(bf16[256,256]{1,0:T(8,128)(2,1)S(1)} %add_convert_fusion.8), channel_id=1, source_target_pairs={{0,4},{4,8},{8,12},{12,14},{14,10},{10,6},{6,2},{2,0},{1,5},{5,9},... | collective-permute-start | bytes 393224 | tf_op jit(solution)/shard_map/ppermute | solution.py:51
  46.8 5.8 %collective-permute-start.24 = (bf16[256,256]{1,0:T(8,128)(2,1)S(1)}, bf16[256,256]{1,0:T(8,128)(2,1)S(1)}, u32[]{:S(2)}, u32[]{:S(2)}) collective-permute-start(bf16[256,256]{1,0:T(8,128)(2,1)S(1)} %add_convert_fusion.5), channel_id=1, source_target_pairs={{0,2},{4,0},{8,4},{12,8},{14,12},{10,14},{6,10},{2,6},{1,3},{5,1},... | collective-permute-start | bytes 393224 | tf_op jit(solution)/shard_map/ppermute | solution.py:51
  47.6 9.9 %collective-permute-start.27 = (bf16[256,256]{1,0:T(8,128)(2,1)S(1)}, bf16[256,256]{1,0:T(8,128)(2,1)S(1)}, u32[]{:S(2)}, u32[]{:S(2)}) collective-permute-start(bf16[256,256]{1,0:T(8,128)(2,1)S(1)} %add_convert_fusion.2), channel_id=1, source_target_pairs={{0,4},{4,8},{8,12},{12,14},{14,10},{10,6},{6,2},{2,0},{1,5},{5,9},... | collective-permute-start | bytes 393224 | tf_op jit(solution)/shard_map/ppermute | solution.py:51
  52.0 5.7 %collective-permute-start.29 = (bf16[256,256]{1,0:T(8,128)(2,1)S(1)}, bf16[256,256]{1,0:T(8,128)(2,1)S(1)}, u32[]{:S(2)}, u32[]{:S(2)}) collective-permute-start(bf16[256,256]{1,0:T(8,128)(2,1)S(1)} %add_convert_fusion), channel_id=1, source_target_pairs={{0,2},{4,0},{8,4},{12,8},{14,12},{10,14},{6,10},{2,6},{1,3},{5,1},... | collective-permute-start | bytes 393224 | tf_op jit(solution)/shard_map/ppermute | solution.py:51
  55.9 6.4 %collective-permute-start.34 = (bf16[256,256]{1,0:T(8,128)(2,1)S(1)}, bf16[256,256]{1,0:T(8,128)(2,1)S(1)}, u32[]{:S(2)}, u32[]{:S(2)}) collective-permute-start(bf16[256,256]{1,0:T(8,128)(2,1)S(1)} %multiply_convert_fusion.refs_1_), channel_id=1, source_target_pairs={{0,4},{4,8},{8,12},{12,14},{14,10},{10,6},{6,2},{2,0},{1,5},{5,9},... | collective-permute-start | bytes 393224 | tf_op jit(solution)/shard_map/ppermute | solution.py:51
  57.8 6.4 %collective-permute-start.30 = (bf16[256,256]{1,0:T(8,128)(2,1)S(1)}, bf16[256,256]{1,0:T(8,128)(2,1)S(1)}, u32[]{:S(2)}, u32[]{:S(2)}) collective-permute-start(bf16[256,256]{1,0:T(8,128)(2,1)S(1)} %fusion.1.refs_0_), channel_id=1, source_target_pairs={{0,2},{4,0},{8,4},{12,8},{14,12},{10,14},{6,10},{2,6},{1,3},{5,1},... | collective-permute-start | bytes 393224 | tf_op jit(solution)/shard_map/ppermute | solution.py:51
  58.4 8.2 %collective-permute-start.39 = (bf16[256,256]{1,0:T(8,128)(2,1)S(1)}, bf16[256,256]{1,0:T(8,128)(2,1)S(1)}, u32[]{:S(2)}, u32[]{:S(2)}) collective-permute-start(bf16[256,256]{1,0:T(8,128)(2,1)S(1)} %multiply_convert_fusion.refs_1_), channel_id=1, source_target_pairs={{0,2},{4,0},{8,4},{12,8},{14,12},{10,14},{6,10},{2,6},{1,3},{5,1},... | collective-permute-start | bytes 393224 | tf_op jit(solution)/shard_map/ppermute | solution.py:51
  59.8 7.4 %collective-permute-start.38 = (bf16[256,256]{1,0:T(8,128)(2,1)S(1)}, bf16[256,256]{1,0:T(8,128)(2,1)S(1)}, u32[]{:S(2)}, u32[]{:S(2)}) collective-permute-start(bf16[256,256]{1,0:T(8,128)(2,1)S(1)} %fusion.1.refs_0_), channel_id=1, source_target_pairs={{0,4},{4,8},{8,12},{12,14},{14,10},{10,6},{6,2},{2,0},{1,5},{5,9},... | collective-permute-start | bytes 393224 | tf_op jit(solution)/shard_map/ppermute | solution.py:51
  62.4 6.6 %collective-permute-start.35 = (bf16[256,256]{1,0:T(8,128)(2,1)S(1)}, bf16[256,256]{1,0:T(8,128)(2,1)S(1)}, u32[]{:S(2)}, u32[]{:S(2)}) collective-permute-start(bf16[256,256]{1,0:T(8,128)(2,1)S(1)} %collective-permute-done.34.refs_3_), channel_id=1, source_target_pairs={{0,4},{4,8},{8,12},{12,14},{14,10},{10,6},{6,2},{2,0},{1,5},{5,9},... | collective-permute-start | bytes 393224 | tf_op jit(solution)/shard_map/ppermute | solution.py:51
  64.2 6.0 %collective-permute-start.31 = (bf16[256,256]{1,0:T(8,128)(2,1)S(1)}, bf16[256,256]{1,0:T(8,128)(2,1)S(1)}, u32[]{:S(2)}, u32[]{:S(2)}) collective-permute-start(bf16[256,256]{1,0:T(8,128)(2,1)S(1)} %collective-permute-done.30.refs_4_), channel_id=1, source_target_pairs={{0,2},{4,0},{8,4},{12,8},{14,12},{10,14},{6,10},{2,6},{1,3},{5,1},... | collective-permute-start | bytes 393224 | tf_op jit(solution)/shard_map/ppermute | solution.py:51
  66.6 5.8 %collective-permute-start.41 = (bf16[256,256]{1,0:T(8,128)(2,1)S(1)}, bf16[256,256]{1,0:T(8,128)(2,1)S(1)}, u32[]{:S(2)}, u32[]{:S(2)}) collective-permute-start(bf16[256,256]{1,0:T(8,128)(2,1)S(1)} %collective-permute-done.39.refs_5_), channel_id=1, source_target_pairs={{0,2},{4,0},{8,4},{12,8},{14,12},{10,14},{6,10},{2,6},{1,3},{5,1},... | collective-permute-start | bytes 393224 | tf_op jit(solution)/shard_map/ppermute | solution.py:51
  68.9 6.0 %collective-permute-start.36 = (bf16[256,256]{1,0:T(8,128)(2,1)S(1)}, bf16[256,256]{1,0:T(8,128)(2,1)S(1)}, u32[]{:S(2)}, u32[]{:S(2)}) collective-permute-start(bf16[256,256]{1,0:T(8,128)(2,1)S(1)} %collective-permute-done.35.refs_1_), channel_id=1, source_target_pairs={{0,4},{4,8},{8,12},{12,14},{14,10},{10,6},{6,2},{2,0},{1,5},{5,9},... | collective-permute-start | bytes 393224 | tf_op jit(solution)/shard_map/ppermute | solution.py:51
  70.2 6.2 %collective-permute-start.32 = (bf16[256,256]{1,0:T(8,128)(2,1)S(1)}, bf16[256,256]{1,0:T(8,128)(2,1)S(1)}, u32[]{:S(2)}, u32[]{:S(2)}) collective-permute-start(bf16[256,256]{1,0:T(8,128)(2,1)S(1)} %collective-permute-done.31.refs_2_), channel_id=1, source_target_pairs={{0,2},{4,0},{8,4},{12,8},{14,12},{10,14},{6,10},{2,6},{1,3},{5,1},... | collective-permute-start | bytes 393224 | tf_op jit(solution)/shard_map/ppermute | solution.py:51
  (17 other events, 142.8 us)

commit v24 on v20

--- a/solution.py
+++ b/solution.py
@@ -149,6 +149,32 @@
         outer[i] = block
     for chain in range(2):
         back[chain] = totals[chain]
+
+
+def near_back_kernel(groups, starts, *refs):
+    count = 2 * len(groups[-1])
+    shards, (stacked, *both_t), refs = refs[:count], refs[count:count + 3], refs[count + 3:]
+    *outers, before, outer, back, same, sems = refs
+    wide = shards[0].shape[1]
+    lat = stacked.shape[0] // 2
+    copies = []
+
+    def send(slots, blocks):
+        for i, slot in enumerate(slots):
+            there = same.at[0, :, block_of(starts, slot, wide)]
+            copies.append(pltpu.make_async_copy(blocks.at[i, :lat, :], there, sems.at[len(copies)]))
+            copies[-1].start()
+
+    for slots, blocks in zip(groups[:-1], outers):
+        send(slots, blocks)
+    found, totals = back_products(groups[-1], starts, shards, stacked, both_t, before)
+    for i, block in enumerate(found):
+        outer[i] = block
+    send(groups[-1], outer)
+    for chain in range(2):
+        back[chain] = totals[chain]
+    for copy in copies:
+        copy.wait()
 
 
 def cross_back_kernel(slots, far, starts, *refs):
@@ -182,20 +208,10 @@
                     high[pl.ds(start - half_width + c, lat), :] = piece[:, c:c + lat]
 
 
-def own_back_kernel(slots, far, starts, *refs):
-    shards, (stacked, *both_t), refs = refs[:2], refs[2:5], refs[5:]
-    outers, (before, back_own, same, last, sems) = refs[:-5], refs[-5:]
+def own_back_kernel(far, starts, *refs):
+    shards, (stacked, *both_t), (before, back_own, last) = refs[:2], refs[2:5], refs[5:]
     rows, wide = shards[0].shape
     lat = back_own.shape[1]
-    blocks = []
-    for group, outer in zip(slots, outers):
-        blocks += [(slot, outer.at[i, :lat, :]) for i, slot in enumerate(group)]
-    blocks.append((far, last))
-    copies = []
-    for i, (slot, block) in enumerate(blocks):
-        copies.append(pltpu.make_async_copy(block, same.at[0, :, block_of(starts, slot, wide)], sems.at[i]))
-    for copy in copies[:-1]:
-        copy.start()
     decoder = stacked[:lat, block_of(starts, far, wide)]
     total = 0.0
     for chain in range(2):
@@ -204,14 +220,14 @@
         term = lax.dot_general(error, decoder, OVER_COLS, preferred_element_type=F32)
         back_own[chain * rows:(chain + 1) * rows, :] = before[chain, :, :lat] + term
     last[...] = total
-    copies[-1].start()
-    for copy in copies:
-        copy.wait()
 
 
 def finish_kernel(
-    starts, turned, preact, back_own, arrived, high, grad, bias, cross, stage, cross_stage, grad_sems, cross_sem
+    far, starts, turned, preact, back_own, arrived, high, last, same_before, grad, bias, cross, same,
+    stage, cross_stage, grad_sems, cross_sem, same_sem
 ):
+    same_copy = pltpu.make_async_copy(last, same.at[0, :, block_of(starts, far, last.shape[1])], same_sem)
+    same_copy.start()
     pieces, height, lat = stage.shape
     rows = preact.shape[0]
     half_width = high.shape[0]
@@ -231,6 +247,7 @@
             copies.append(pltpu.make_async_copy(cross_stage, cross, cross_sem))
             copies[-1].start()
     bias[...] = jnp.sum(value.astype(F32), axis=0, keepdims=True)
+    same_copy.wait()
     for copy in copies:
         copy.wait()
 
@@ -356,13 +373,27 @@
         [starts] + turned_own + arrived + both_chains(inputs, range(1, size))[1:],
     )[0]
     for s in range(1, reach + 1):
-        gather_step(errors, s, (turned, turned) if s == 2 else None)
+        gather_step(errors, s, (turned, turned) if s == 1 else None)
     cut = 1 + 2 * min(1, reach - 1)
     groups = [group for group in (tuple(range(cut)), tuple(range(cut, far))) if group]
     outers, acc = [], None
-    for group in groups:
+    for group in groups[:-1]:
         outer, acc = back(group, acc)
         outers.append(outer)
+    before = [jnp.zeros((2, half, 2 * lat), F32)] if acc is None else [acc]
+    outer, acc, same = call(
+        functools.partial(near_back_kernel, groups),
+        [
+            shape((len(groups[-1]), 2 * lat, wide), F32),
+            shape((2, half, 2 * lat), F32),
+            shape((1, lat, deep), F32),
+        ],
+        0,
+        [starts] + both_chains(errors, groups[-1]) + [stacked] + both_t + outers + before,
+        out_spaces=[pltpu.VMEM, pltpu.VMEM, pl.ANY],
+        scratch=[pltpu.SemaphoreType.DMA((far,))],
+    )
+    outers.append(outer)
     last = both_chains(errors, (far,)) + [stacked] + both_t + outers + [acc]
     sent, high = call(
         functools.partial(cross_back_kernel, groups, far),
@@ -371,25 +402,26 @@
         [starts] + last,
     )
     returned = swapped(sent)
-    back_own, grad_same = call(
-        functools.partial(own_back_kernel, groups, far),
-        [shape((rows, lat), F32), shape((1, lat, deep), F32)],
+    back_own, last_same = call(
+        functools.partial(own_back_kernel, far),
+        [shape((rows, lat), F32), shape((lat, wide), F32)],
         0,
-        [starts] + last,
-        out_spaces=[pltpu.VMEM, pl.ANY],
-        scratch=[pltpu.VMEM((lat, wide), F32), pltpu.SemaphoreType.DMA((size,))],
+        [starts] + both_chains(errors, (far,)) + [stacked] + both_t + [acc],
     )
     height = deep // PIECES
-    grad_enc, grad_bias, grad_cross = call(
-        finish_kernel,
-        [shape((1, deep, lat), F32), shape((1, lat), F32), shape((lat, half_width), F32)],
+    grad_enc, grad_bias, grad_cross, grad_same = call(
+        functools.partial(finish_kernel, far),
+        [shape((1, deep, lat), F32), shape((1, lat), F32), shape((lat, half_width), F32), shape((1, lat, deep), F32)],
         2 * unit * size,
-        [starts, turned, preact, back_own, returned, high],
-        out_spaces=[pl.ANY, pltpu.VMEM, pl.ANY],
+        [starts, turned, preact, back_own, returned, high, last_same, same],
+        spaces=[pltpu.VMEM] * 6 + [pl.ANY],
+        out_spaces=[pl.ANY, pltpu.VMEM, pl.ANY, pl.ANY],
+        aliases={7: 3},
         scratch=[
             pltpu.VMEM((PIECES, height, lat), F32),
             pltpu.VMEM((lat, half_width), F32),
             pltpu.SemaphoreType.DMA((PIECES,)),
+            pltpu.SemaphoreType.DMA,
             pltpu.SemaphoreType.DMA,
         ],
     )

time: 85.9 us -> 90.5 us (1.054)
  waiting for transfers between devices: 22.6 us -> 29.6 us
  starting transfers between devices: 46 us -> 43.6 us
    ppermute x42, waiting for transfers between devices: 21.2 us -> 27.4 us  [hop(): return lax.ppermute(shard, ('latent', 'layer'), pairs)]
    ppermute x42, starting transfers between devices: 45.9 us -> 43.4 us  [hop(): return lax.ppermute(shard, ('latent', 'layer'), pairs)]
  transfers between devices with their start and end apart: 45 -> 45, of which waited for: 28 -> 26; matrix products, arithmetic and copies ran while one was open for 2% -> 2% of each run, Pallas kernels for 10% -> 10%
where the time goes in v24:
time: 90.5 us; the launch traced here: 90.3 us
  starting transfers between devices  43.6 us (48%)
  waiting for transfers between devices  29.6 us (33%)
  Pallas kernels  13.5 us (15%)
  other arithmetic  1.56 us (2%)
  local copies, waits for them, and re-layouts  1.16 us (1%)
    ppermute x42, starting transfers between devices, hop(): return lax.ppermute(shard, ('latent', 'layer'), pairs)  43.4 us
    ppermute x42, waiting for transfers between devices, hop(): return lax.ppermute(shard, ('latent', 'layer'), pairs)  27.4 us
    pallas_call x12, Pallas kernels, call(): pl.pallas_call(kernel, out_shape=outs, in_specs=[spec(pltpu.SMEM)] + [spe...  13.5 us
    ppermute x3, waiting for transfers between devices, swapped(): lax.ppermute(shard, 'layer', [(i, size - 1 - i) for i in range(size)])  2.22 us
  transfers between devices with their start and end apart: 45, of which 26 were waited for; matrix products, arithmetic and copies ran while one was open for 2% of the time, Pallas kernels for 10%

profile of v24, /device:TPU:0, one launch (start us, length us, event | category | flops | bytes accessed | tf_op | source)
XLA Modules:
  0.0 90.3 jit_solution(4659966237139709717)
XLA Ops:
  1.7 3.0 %collective-permute-start.1 = (bf16[256,256]{1,0:T(8,128)(2,1)S(1)}, bf16[256,256]{1,0:T(8,128)(2,1)S(1)}, u32[]{:S(2)}, u32[]{:S(2)}) collective-permute-start(bf16[256,256]{1,0:T(8,128)(2,1)S(1)} %get-tuple-element.49.shard.refs_0_), channel_id=1, source_target_pairs={{0,2},{1,5},{4,0},{5,9},{8,4},{9,13},{12,8},{13,15},{14,12},{15,11... | collective-permute-start | bytes 393224 | tf_op jit(solution)/shard_map/ppermute | solution.py:56
  5.6 2.0 %collective-permute-start = (bf16[256,256]{1,0:T(8,128)(2,1)S(1)}, bf16[256,256]{1,0:T(8,128)(2,1)S(1)}, u32[]{:S(2)}, u32[]{:S(2)}) collective-permute-start(bf16[256,256]{1,0:T(8,128)(2,1)S(1)} %get-tuple-element.49.shard.refs_0_), channel_id=1, source_target_pairs={{0,4},{1,3},{4,8},{5,1},{8,12},{9,5},{12,14},{13,9},{14,10},{15,13... | collective-permute-start | bytes 393224 | tf_op jit(solution)/shard_map/ppermute | solution.py:56
  8.6 2.1 %collective-permute-start.2 = (bf16[256,256]{1,0:T(8,128)(2,1)S(1)}, bf16[256,256]{1,0:T(8,128)(2,1)S(1)}, u32[]{:S(2)}, u32[]{:S(2)}) collective-permute-start(bf16[256,256]{1,0:T(8,128)(2,1)S(1)} %collective-permute-done.1.refs_4_.refs_2_), channel_id=1, source_target_pairs={{0,2},{1,5},{4,0},{5,9},{8,4},{9,13},{12,8},{13,15},{14,12},{15,11... | collective-permute-start | bytes 393224 | tf_op jit(solution)/shard_map/ppermute | solution.py:56
  11.0 1.3 %collective-permute-done.refs_2_.refs_0_ = bf16[256,256]{1,0:T(8,128)(2,1)S(1)} collective-permute-done((bf16[256,256]{1,0:T(8,128)(2,1)S(1)}, bf16[256,256]{1,0:T(8,128)(2,1)S(1)}, u32[]{:S(2)}, u32[]{:S(2)}) %collective-permute-start) | collective-permute-done | bytes 131104 | tf_op jit(solution)/shard_map/ppermute | solution.py:56
  12.3 2.0 %collective-permute-done.9.refs_5_.refs_3_ = bf16[256,256]{1,0:T(8,128)(2,1)S(1)} collective-permute-done((bf16[256,256]{1,0:T(8,128)(2,1)S(1)}, bf16[256,256]{1,0:T(8,128)(2,1)S(1)}, u32[]{:S(2)}, u32[]{:S(2)}) %collective-permute-start.9) | collective-permute-done | bytes 131104 | tf_op jit(solution)/shard_map/ppermute | solution.py:56
  14.5 1.9 %collective-permute-start.10 = (bf16[256,256]{1,0:T(8,128)(2,1)S(1)}, bf16[256,256]{1,0:T(8,128)(2,1)S(1)}, u32[]{:S(2)}, u32[]{:S(2)}) collective-permute-start(bf16[256,256]{1,0:T(8,128)(2,1)S(1)} %collective-permute-done.refs_2_.refs_0_), channel_id=1, source_target_pairs={{0,4},{1,3},{4,8},{5,1},{8,12},{9,5},{12,14},{13,9},{14,10},{15,13... | collective-permute-start | bytes 393224 | tf_op jit(solution)/shard_map/ppermute | solution.py:56
  16.5 1.9 %collective-permute-start.7 = (bf16[256,256]{1,0:T(8,128)(2,1)S(1)}, bf16[256,256]{1,0:T(8,128)(2,1)S(1)}, u32[]{:S(2)}, u32[]{:S(2)}) collective-permute-start(bf16[256,256]{1,0:T(8,128)(2,1)S(1)} %collective-permute-done.6.refs_7_.refs_5_), channel_id=1, source_target_pairs={{0,4},{1,3},{4,8},{5,1},{8,12},{9,5},{12,14},{13,9},{14,10},{15,13... | collective-permute-start | bytes 393224 | tf_op jit(solution)/shard_map/ppermute | solution.py:56
  18.4 2.3 %collective-permute-done.11.refs_9_.refs_7_ = bf16[256,256]{1,0:T(8,128)(2,1)S(1)} collective-permute-done((bf16[256,256]{1,0:T(8,128)(2,1)S(1)}, bf16[256,256]{1,0:T(8,128)(2,1)S(1)}, u32[]{:S(2)}, u32[]{:S(2)}) %collective-permute-start.11) | collective-permute-done | bytes 131104 | tf_op jit(solution)/shard_map/ppermute | solution.py:56
  20.8 1.9 %collective-permute-start.12 = (bf16[256,256]{1,0:T(8,128)(2,1)S(1)}, bf16[256,256]{1,0:T(8,128)(2,1)S(1)}, u32[]{:S(2)}, u32[]{:S(2)}) collective-permute-start(bf16[256,256]{1,0:T(8,128)(2,1)S(1)} %collective-permute-done.10.refs_6_.refs_4_), channel_id=1, source_target_pairs={{0,4},{1,3},{4,8},{5,1},{8,12},{9,5},{12,14},{13,9},{14,10},{15,13... | collective-permute-start | bytes 393224 | tf_op jit(solution)/shard_map/ppermute | solution.py:56
  23.6 1.9 %collective-permute-start.8 = (bf16[256,256]{1,0:T(8,128)(2,1)S(1)}, bf16[256,256]{1,0:T(8,128)(2,1)S(1)}, u32[]{:S(2)}, u32[]{:S(2)}) collective-permute-start(bf16[256,256]{1,0:T(8,128)(2,1)S(1)} %collective-permute-done.7.refs_11_.refs_9_), channel_id=1, source_target_pairs={{0,4},{1,3},{4,8},{5,1},{8,12},{9,5},{12,14},{13,9},{14,10},{15,13... | collective-permute-start | bytes 393224 | tf_op jit(solution)/shard_map/ppermute | solution.py:56
  26.8 1.2 %shard_map.95.refs_3_ = f32[512,128]{1,0:T(8,128)S(1)} custom-call(s32[9]{0:T(128)S(1)} %stack.39.starts, bf16[256,256]{1,0:T(8,128)(2,1)S(1)} %get-tuple-element.49.shard.refs_0_, bf16[256,256]{1,0:T(8,128)(2,1)S(1)} %get-tuple-element.50.shard.refs_1_, bf16[256,256]{1,0:T(8,128)(2,1)S(1)} %collective-permute-done.refs_2_.refs_0_, ...), custom_call_target="tpu_custom_call" | custom-call | flops 234881024 | bytes 1024 | tf_op jit(solution)/shard_map/pallas_call | solution.py:69
  29.4 1.3 %collective-permute-done.15.earlier = bf16[512,128]{1,0:T(8,128)(2,1)S(1)} collective-permute-done((bf16[512,128]{1,0:T(8,128)(2,1)S(1)}, bf16[512,128]{1,0:T(8,128)(2,1)S(1)}, u32[]{:S(2)}, u32[]{:S(2)}) %collective-permute-start.15) | collective-permute-done | bytes 131104 | tf_op jit(solution)/shard_map/ppermute | solution.py:28
  31.6 2.0 %collective-permute-start.16 = (bf16[256,256]{1,0:T(8,128)(2,1)S(1)}, bf16[256,256]{1,0:T(8,128)(2,1)S(1)}, u32[]{:S(2)}, u32[]{:S(2)}) collective-permute-start(bf16[256,256]{1,0:T(8,128)(2,1)S(1)} %get-tuple-element.58), channel_id=1, source_target_pairs={{0,4},{1,3},{4,8},{5,1},{8,12},{9,5},{12,14},{13,9},{14,10},{15,13... | collective-permute-start | bytes 393224 | tf_op jit(solution)/shard_map/ppermute | solution.py:56
  33.7 1.2 %shard_map.97 = (f32[256,256]{1,0:T(8,128)S(1)}, f32[256,256]{1,0:T(8,128)S(1)}, f32[256,256]{1,0:T(8,128)S(1)}, f32[256,256]{1,0:T(8,128)S(1)}, f32[256,256]{1,...) custom-call(s32[9]{0:T(128)S(1)} %stack.39.starts, ...), custom_call_target="tpu_custom_call" | custom-call | flops 469762048 | bytes 1024 | tf_op jit(solution)/shard_map/pallas_call | solution.py:69
  34.9 1.9 %collective-permute-start.20 = (bf16[256,256]{1,0:T(8,128)(2,1)S(1)}, bf16[256,256]{1,0:T(8,128)(2,1)S(1)}, u32[]{:S(2)}, u32[]{:S(2)}) collective-permute-start(bf16[256,256]{1,0:T(8,128)(2,1)S(1)} %get-tuple-element.61), channel_id=1, source_target_pairs={{0,2},{1,5},{4,0},{5,9},{8,4},{9,13},{12,8},{13,15},{14,12},{15,11... | collective-permute-start | bytes 393224 | tf_op jit(solution)/shard_map/ppermute | solution.py:56
  37.3 2.1 %collective-permute-start.17 = (bf16[256,256]{1,0:T(8,128)(2,1)S(1)}, bf16[256,256]{1,0:T(8,128)(2,1)S(1)}, u32[]{:S(2)}, u32[]{:S(2)}) collective-permute-start(bf16[256,256]{1,0:T(8,128)(2,1)S(1)} %add_convert_fusion.9), channel_id=1, source_target_pairs={{0,4},{1,3},{4,8},{5,1},{8,12},{9,5},{12,14},{13,9},{14,10},{15,13... | collective-permute-start | bytes 393224 | tf_op jit(solution)/shard_map/ppermute | solution.py:56
  39.5 1.6 %collective-permute-done.20 = bf16[256,256]{1,0:T(8,128)(2,1)S(1)} collective-permute-done((bf16[256,256]{1,0:T(8,128)(2,1)S(1)}, bf16[256,256]{1,0:T(8,128)(2,1)S(1)}, u32[]{:S(2)}, u32[]{:S(2)}) %collective-permute-start.20) | collective-permute-done | bytes 131104 | tf_op jit(solution)/shard_map/ppermute | solution.py:56
  41.1 2.1 %collective-permute-start.22 = (bf16[256,256]{1,0:T(8,128)(2,1)S(1)}, bf16[256,256]{1,0:T(8,128)(2,1)S(1)}, u32[]{:S(2)}, u32[]{:S(2)}) collective-permute-start(bf16[256,256]{1,0:T(8,128)(2,1)S(1)} %add_convert_fusion.6), channel_id=1, source_target_pairs={{0,2},{1,5},{4,0},{5,9},{8,4},{9,13},{12,8},{13,15},{14,12},{15,11... | collective-permute-start | bytes 393224 | tf_op jit(solution)/shard_map/ppermute | solution.py:56
  43.5 2.1 %collective-permute-done.17 = bf16[256,256]{1,0:T(8,128)(2,1)S(1)} collective-permute-done((bf16[256,256]{1,0:T(8,128)(2,1)S(1)}, bf16[256,256]{1,0:T(8,128)(2,1)S(1)}, u32[]{:S(2)}, u32[]{:S(2)}) %collective-permute-start.17) | collective-permute-done | bytes 131104 | tf_op jit(solution)/shard_map/ppermute | solution.py:56
  45.8 1.8 %collective-permute-done.22 = bf16[256,256]{1,0:T(8,128)(2,1)S(1)} collective-permute-done((bf16[256,256]{1,0:T(8,128)(2,1)S(1)}, bf16[256,256]{1,0:T(8,128)(2,1)S(1)}, u32[]{:S(2)}, u32[]{:S(2)}) %collective-permute-start.22) | collective-permute-done | bytes 131104 | tf_op jit(solution)/shard_map/ppermute | solution.py:56
  47.7 1.5 %collective-permute-start.24 = (bf16[256,256]{1,0:T(8,128)(2,1)S(1)}, bf16[256,256]{1,0:T(8,128)(2,1)S(1)}, u32[]{:S(2)}, u32[]{:S(2)}) collective-permute-start(bf16[256,256]{1,0:T(8,128)(2,1)S(1)} %add_convert_fusion.5), channel_id=1, source_target_pairs={{0,2},{1,5},{4,0},{5,9},{8,4},{9,13},{12,8},{13,15},{14,12},{15,11... | collective-permute-start | bytes 393224 | tf_op jit(solution)/shard_map/ppermute | solution.py:56
  49.2 1.7 %collective-permute-start.28 = (bf16[256,256]{1,0:T(8,128)(2,1)S(1)}, bf16[256,256]{1,0:T(8,128)(2,1)S(1)}, u32[]{:S(2)}, u32[]{:S(2)}) collective-permute-start(bf16[256,256]{1,0:T(8,128)(2,1)S(1)} %add_convert_fusion.1), channel_id=1, source_target_pairs={{0,2},{1,5},{4,0},{5,9},{8,4},{9,13},{12,8},{13,15},{14,12},{15,11... | collective-permute-start | bytes 393224 | tf_op jit(solution)/shard_map/ppermute | solution.py:56
  51.4 3.3 %collective-permute-done.28 = bf16[256,256]{1,0:T(8,128)(2,1)S(1)} collective-permute-done((bf16[256,256]{1,0:T(8,128)(2,1)S(1)}, bf16[256,256]{1,0:T(8,128)(2,1)S(1)}, u32[]{:S(2)}, u32[]{:S(2)}) %collective-permute-start.28) | collective-permute-done | bytes 131104 | tf_op jit(solution)/shard_map/ppermute | solution.py:56
  54.7 1.2 %collective-permute-start.29 = (bf16[256,256]{1,0:T(8,128)(2,1)S(1)}, bf16[256,256]{1,0:T(8,128)(2,1)S(1)}, u32[]{:S(2)}, u32[]{:S(2)}) collective-permute-start(bf16[256,256]{1,0:T(8,128)(2,1)S(1)} %add_convert_fusion), channel_id=1, source_target_pairs={{0,2},{1,5},{4,0},{5,9},{8,4},{9,13},{12,8},{13,15},{14,12},{15,11... | collective-permute-start | bytes 393224 | tf_op jit(solution)/shard_map/ppermute | solution.py:56
  56.9 2.9 %collective-permute-done.29 = bf16[256,256]{1,0:T(8,128)(2,1)S(1)} collective-permute-done((bf16[256,256]{1,0:T(8,128)(2,1)S(1)}, bf16[256,256]{1,0:T(8,128)(2,1)S(1)}, u32[]{:S(2)}, u32[]{:S(2)}) %collective-permute-start.29) | collective-permute-done | bytes 131104 | tf_op jit(solution)/shard_map/ppermute | solution.py:56
  59.8 1.2 %collective-permute-start.30 = (bf16[256,256]{1,0:T(8,128)(2,1)S(1)}, bf16[256,256]{1,0:T(8,128)(2,1)S(1)}, u32[]{:S(2)}, u32[]{:S(2)}) collective-permute-start(bf16[256,256]{1,0:T(8,128)(2,1)S(1)} %fusion.1.refs_0_), channel_id=1, source_target_pairs={{0,2},{1,5},{4,0},{5,9},{8,4},{9,13},{12,8},{13,15},{14,12},{15,11... | collective-permute-start | bytes 393224 | tf_op jit(solution)/shard_map/ppermute | solution.py:56
  67.4 1.1 %collective-permute-done.34.refs_3_ = bf16[256,256]{1,0:T(8,128)(2,1)S(1)} collective-permute-done((bf16[256,256]{1,0:T(8,128)(2,1)S(1)}, bf16[256,256]{1,0:T(8,128)(2,1)S(1)}, u32[]{:S(2)}, u32[]{:S(2)}) %collective-permute-start.34) | collective-permute-done | bytes 131104 | tf_op jit(solution)/shard_map/ppermute | solution.py:56
  71.5 1.3 %collective-permute-start.39 = (bf16[256,256]{1,0:T(8,128)(2,1)S(1)}, bf16[256,256]{1,0:T(8,128)(2,1)S(1)}, u32[]{:S(2)}, u32[]{:S(2)}) collective-permute-start(bf16[256,256]{1,0:T(8,128)(2,1)S(1)} %collective-permute-done.38.refs_2_), channel_id=1, source_target_pairs={{0,4},{1,3},{4,8},{5,1},{8,12},{9,5},{12,14},{13,9},{14,10},{15,13... | collective-permute-start | bytes 393224 | tf_op jit(solution)/shard_map/ppermute | solution.py:56
  78.8 1.4 %collective-permute-start.33 = (bf16[256,256]{1,0:T(8,128)(2,1)S(1)}, bf16[256,256]{1,0:T(8,128)(2,1)S(1)}, u32[]{:S(2)}, u32[]{:S(2)}) collective-permute-start(bf16[256,256]{1,0:T(8,128)(2,1)S(1)} %collective-permute-done.32.refs_6_), channel_id=1, source_target_pairs={{0,2},{1,5},{4,0},{5,9},{8,4},{9,13},{12,8},{13,15},{14,12},{15,11... | collective-permute-start | bytes 393224 | tf_op jit(solution)/shard_map/ppermute | solution.py:56
  80.8 1.1 %shard_map.100 = (f32[3,256,256]{2,1,0:T(8,128)S(1)}, f32[2,256,256]{2,1,0:T(8,128)S(1)}) custom-call(s32[9]{0:T(128)S(1)} %stack.39.starts, bf16[256,256]{1,0:T(8,128)(2,1)S(1)} %fusion.1.refs_0_, bf16[256,256]{1,0:T(8,128)(2,1)S(1)} %multiply_convert_fusion.refs_1_, bf16[256,256]{1,0:T(8,128)(2,1)S(1)} %collective-permute-done.38.refs_2_, ...), custom_call_target="tpu_custom_call" | custom-call | flops 201326592 | bytes 1024 | tf_op jit(solution)/shard_map/pallas_call | solution.py:69
  82.6 2.1 %shard_map.101 = (f32[4,256,256]{2,1,0:T(8,128)S(1)}, f32[2,256,256]{2,1,0:T(8,128)S(1)}, f32[1,128,2048]{2,1,0:T(8,128)}) custom-call(s32[9]{0:T(128)S(1)} %stack.39.starts, bf16[256,256]{1,0:T(8,128)(2,1)S(1)} %collective-permute-done.39.refs_0_, bf16[256,256]{1,0:T(8,128)(2,1)S(1)} %collective-permute-done.35.refs_1_, ...), custom_call_target="tpu_custom_call" | custom-call | bytes 1024 | tf_op jit(solution)/shard_map/pallas_call | solution.py:69
  87.6 2.7 %shard_map.104 = (f32[1,2048,128]{2,1,0:T(8,128)}, f32[1,128]{1,0:T(1,128)}, f32[128,1024]{1,0:T(8,128)}, f32[1,128,2048]{2,1,0:T(8,128)}) custom-call(s32[9]{0:T(128)S(1)} %stack.39.starts, bf16[2048,512]{1,0:T(8,128)(2,1)S(1)} %shard_map.99.turned, f32[512,128]{1,0:T(8,128)S(1)} %get-tuple-element.68.preact, ...), custom_call_target="tpu_custom_call", output_to_operand_aliasing={{3}: (7, {})} | custom-call | flops 268435456 | bytes 1024 | tf_op jit(solution)/shard_map/pallas_call | solution.py:69
  (95 shorter events, 30.2 us)
Async XLA Ops:
  1.7 6.9 %collective-permute-start.1 = (bf16[256,256]{1,0:T(8,128)(2,1)S(1)}, bf16[256,256]{1,0:T(8,128)(2,1)S(1)}, u32[]{:S(2)}, u32[]{:S(2)}) collective-permute-start(bf16[256,256]{1,0:T(8,128)(2,1)S(1)} %get-tuple-element.49.shard.refs_0_), channel_id=1, source_target_pairs={{0,2},{1,5},{4,0},{5,9},{8,4},{9,13},{12,8},{13,15},{14,12},{15,11... | collective-permute-start | bytes 393224 | tf_op jit(solution)/shard_map/ppermute | solution.py:56
  4.7 6.0 %collective-permute-start.5 = (bf16[256,256]{1,0:T(8,128)(2,1)S(1)}, bf16[256,256]{1,0:T(8,128)(2,1)S(1)}, u32[]{:S(2)}, u32[]{:S(2)}) collective-permute-start(bf16[256,256]{1,0:T(8,128)(2,1)S(1)} %get-tuple-element.50.shard.refs_1_), channel_id=1, source_target_pairs={{0,4},{1,3},{4,8},{5,1},{8,12},{9,5},{12,14},{13,9},{14,10},{15,13... | collective-permute-start | bytes 393224 | tf_op jit(solution)/shard_map/ppermute | solution.py:56
  5.6 6.7 %collective-permute-start = (bf16[256,256]{1,0:T(8,128)(2,1)S(1)}, bf16[256,256]{1,0:T(8,128)(2,1)S(1)}, u32[]{:S(2)}, u32[]{:S(2)}) collective-permute-start(bf16[256,256]{1,0:T(8,128)(2,1)S(1)} %get-tuple-element.49.shard.refs_0_), channel_id=1, source_target_pairs={{0,4},{1,3},{4,8},{5,1},{8,12},{9,5},{12,14},{13,9},{14,10},{15,13... | collective-permute-start | bytes 393224 | tf_op jit(solution)/shard_map/ppermute | solution.py:56
  8.2 6.1 %collective-permute-start.9 = (bf16[256,256]{1,0:T(8,128)(2,1)S(1)}, bf16[256,256]{1,0:T(8,128)(2,1)S(1)}, u32[]{:S(2)}, u32[]{:S(2)}) collective-permute-start(bf16[256,256]{1,0:T(8,128)(2,1)S(1)} %get-tuple-element.50.shard.refs_1_), channel_id=1, source_target_pairs={{0,2},{1,5},{4,0},{5,9},{8,4},{9,13},{12,8},{13,15},{14,12},{15,11... | collective-permute-start | bytes 393224 | tf_op jit(solution)/shard_map/ppermute | solution.py:56
  8.6 7.8 %collective-permute-start.2 = (bf16[256,256]{1,0:T(8,128)(2,1)S(1)}, bf16[256,256]{1,0:T(8,128)(2,1)S(1)}, u32[]{:S(2)}, u32[]{:S(2)}) collective-permute-start(bf16[256,256]{1,0:T(8,128)(2,1)S(1)} %collective-permute-done.1.refs_4_.refs_2_), channel_id=1, source_target_pairs={{0,2},{1,5},{4,0},{5,9},{8,4},{9,13},{12,8},{13,15},{14,12},{15,11... | collective-permute-start | bytes 393224 | tf_op jit(solution)/shard_map/ppermute | solution.py:56
  10.7 5.8 %collective-permute-start.6 = (bf16[256,256]{1,0:T(8,128)(2,1)S(1)}, bf16[256,256]{1,0:T(8,128)(2,1)S(1)}, u32[]{:S(2)}, u32[]{:S(2)}) collective-permute-start(bf16[256,256]{1,0:T(8,128)(2,1)S(1)} %collective-permute-done.5.refs_3_.refs_1_), channel_id=1, source_target_pairs={{0,4},{1,3},{4,8},{5,1},{8,12},{9,5},{12,14},{13,9},{14,10},{15,13... | collective-permute-start | bytes 393224 | tf_op jit(solution)/shard_map/ppermute | solution.py:56
  12.3 13.2 %collective-permute-start.14 = (bf16[128,1024]{1,0:T(8,128)(2,1)}, bf16[128,1024]{1,0:T(8,128)(2,1)S(1)}, u32[]{:S(2)}, u32[]{:S(2)}) collective-permute-start(bf16[128,1024]{1,0:T(8,128)(2,1)} %param.11), channel_id=1, source_target_pairs={{0,1},{1,0},{2,3},{3,2},{4,5},{5,4},{6,7},{7,6},{8,9},{9,8},{10,11... | collective-permute-start | bytes 786440 | tf_op jit(solution)/shard_map/ppermute | solution.py:28
  14.3 6.4 %collective-permute-start.11 = (bf16[256,256]{1,0:T(8,128)(2,1)S(1)}, bf16[256,256]{1,0:T(8,128)(2,1)S(1)}, u32[]{:S(2)}, u32[]{:S(2)}) collective-permute-start(bf16[256,256]{1,0:T(8,128)(2,1)S(1)} %collective-permute-done.9.refs_5_.refs_3_), channel_id=1, source_target_pairs={{0,2},{1,5},{4,0},{5,9},{8,4},{9,13},{12,8},{13,15},{14,12},{15,11... | collective-permute-start | bytes 393224 | tf_op jit(solution)/shard_map/ppermute | solution.py:56
  14.5 6.3 %collective-permute-start.10 = (bf16[256,256]{1,0:T(8,128)(2,1)S(1)}, bf16[256,256]{1,0:T(8,128)(2,1)S(1)}, u32[]{:S(2)}, u32[]{:S(2)}) collective-permute-start(bf16[256,256]{1,0:T(8,128)(2,1)S(1)} %collective-permute-done.refs_2_.refs_0_), channel_id=1, source_target_pairs={{0,4},{1,3},{4,8},{5,1},{8,12},{9,5},{12,14},{13,9},{14,10},{15,13... | collective-permute-start | bytes 393224 | tf_op jit(solution)/shard_map/ppermute | solution.py:56
  16.4 7.2 %collective-permute-start.3 = (bf16[256,256]{1,0:T(8,128)(2,1)S(1)}, bf16[256,256]{1,0:T(8,128)(2,1)S(1)}, u32[]{:S(2)}, u32[]{:S(2)}) collective-permute-start(bf16[256,256]{1,0:T(8,128)(2,1)S(1)} %collective-permute-done.2.refs_8_.refs_6_), channel_id=1, source_target_pairs={{0,2},{1,5},{4,0},{5,9},{8,4},{9,13},{12,8},{13,15},{14,12},{15,11... | collective-permute-start | bytes 393224 | tf_op jit(solution)/shard_map/ppermute | solution.py:56
  16.5 7.1 %collective-permute-start.7 = (bf16[256,256]{1,0:T(8,128)(2,1)S(1)}, bf16[256,256]{1,0:T(8,128)(2,1)S(1)}, u32[]{:S(2)}, u32[]{:S(2)}) collective-permute-start(bf16[256,256]{1,0:T(8,128)(2,1)S(1)} %collective-permute-done.6.refs_7_.refs_5_), channel_id=1, source_target_pairs={{0,4},{1,3},{4,8},{5,1},{8,12},{9,5},{12,14},{13,9},{14,10},{15,13... | collective-permute-start | bytes 393224 | tf_op jit(solution)/shard_map/ppermute | solution.py:56
  20.7 6.1 %collective-permute-start.13 = (bf16[256,256]{1,0:T(8,128)(2,1)S(1)}, bf16[256,256]{1,0:T(8,128)(2,1)S(1)}, u32[]{:S(2)}, u32[]{:S(2)}) collective-permute-start(bf16[256,256]{1,0:T(8,128)(2,1)S(1)} %collective-permute-done.11.refs_9_.refs_7_), channel_id=1, source_target_pairs={{0,2},{1,5},{4,0},{5,9},{8,4},{9,13},{12,8},{13,15},{14,12},{15,11... | collective-permute-start | bytes 393224 | tf_op jit(solution)/shard_map/ppermute | solution.py:56
  20.8 6.0 %collective-permute-start.12 = (bf16[256,256]{1,0:T(8,128)(2,1)S(1)}, bf16[256,256]{1,0:T(8,128)(2,1)S(1)}, u32[]{:S(2)}, u32[]{:S(2)}) collective-permute-start(bf16[256,256]{1,0:T(8,128)(2,1)S(1)} %collective-permute-done.10.refs_6_.refs_4_), channel_id=1, source_target_pairs={{0,4},{1,3},{4,8},{5,1},{8,12},{9,5},{12,14},{13,9},{14,10},{15,13... | collective-permute-start | bytes 393224 | tf_op jit(solution)/shard_map/ppermute | solution.py:56
  33.6 5.8 %collective-permute-start.21 = (bf16[256,256]{1,0:T(8,128)(2,1)S(1)}, bf16[256,256]{1,0:T(8,128)(2,1)S(1)}, u32[]{:S(2)}, u32[]{:S(2)}) collective-permute-start(bf16[256,256]{1,0:T(8,128)(2,1)S(1)} %get-tuple-element.62), channel_id=1, source_target_pairs={{0,2},{1,5},{4,0},{5,9},{8,4},{9,13},{12,8},{13,15},{14,12},{15,11... | collective-permute-start | bytes 393224 | tf_op jit(solution)/shard_map/ppermute | solution.py:56
  34.9 6.2 %collective-permute-start.20 = (bf16[256,256]{1,0:T(8,128)(2,1)S(1)}, bf16[256,256]{1,0:T(8,128)(2,1)S(1)}, u32[]{:S(2)}, u32[]{:S(2)}) collective-permute-start(bf16[256,256]{1,0:T(8,128)(2,1)S(1)} %get-tuple-element.61), channel_id=1, source_target_pairs={{0,2},{1,5},{4,0},{5,9},{8,4},{9,13},{12,8},{13,15},{14,12},{15,11... | collective-permute-start | bytes 393224 | tf_op jit(solution)/shard_map/ppermute | solution.py:56
  36.8 6.5 %collective-permute-start.25 = (bf16[256,256]{1,0:T(8,128)(2,1)S(1)}, bf16[256,256]{1,0:T(8,128)(2,1)S(1)}, u32[]{:S(2)}, u32[]{:S(2)}) collective-permute-start(bf16[256,256]{1,0:T(8,128)(2,1)S(1)} %get-tuple-element.72), channel_id=1, source_target_pairs={{0,4},{1,3},{4,8},{5,1},{8,12},{9,5},{12,14},{13,9},{14,10},{15,13... | collective-permute-start | bytes 393224 | tf_op jit(solution)/shard_map/ppermute | solution.py:56
  37.3 8.3 %collective-permute-start.17 = (bf16[256,256]{1,0:T(8,128)(2,1)S(1)}, bf16[256,256]{1,0:T(8,128)(2,1)S(1)}, u32[]{:S(2)}, u32[]{:S(2)}) collective-permute-start(bf16[256,256]{1,0:T(8,128)(2,1)S(1)} %add_convert_fusion.9), channel_id=1, source_target_pairs={{0,4},{1,3},{4,8},{5,1},{8,12},{9,5},{12,14},{13,9},{14,10},{15,13... | collective-permute-start | bytes 393224 | tf_op jit(solution)/shard_map/ppermute | solution.py:56
  39.4 8.3 %collective-permute-start.23 = (bf16[256,256]{1,0:T(8,128)(2,1)S(1)}, bf16[256,256]{1,0:T(8,128)(2,1)S(1)}, u32[]{:S(2)}, u32[]{:S(2)}) collective-permute-start(bf16[256,256]{1,0:T(8,128)(2,1)S(1)} %add_convert_fusion.4), channel_id=1, source_target_pairs={{0,2},{1,5},{4,0},{5,9},{8,4},{9,13},{12,8},{13,15},{14,12},{15,11... | collective-permute-start | bytes 393224 | tf_op jit(solution)/shard_map/ppermute | solution.py:56
  41.1 6.5 %collective-permute-start.22 = (bf16[256,256]{1,0:T(8,128)(2,1)S(1)}, bf16[256,256]{1,0:T(8,128)(2,1)S(1)}, u32[]{:S(2)}, u32[]{:S(2)}) collective-permute-start(bf16[256,256]{1,0:T(8,128)(2,1)S(1)} %add_convert_fusion.6), channel_id=1, source_target_pairs={{0,2},{1,5},{4,0},{5,9},{8,4},{9,13},{12,8},{13,15},{14,12},{15,11... | collective-permute-start | bytes 393224 | tf_op jit(solution)/shard_map/ppermute | solution.py:56
  43.3 7.6 %collective-permute-start.26 = (bf16[256,256]{1,0:T(8,128)(2,1)S(1)}, bf16[256,256]{1,0:T(8,128)(2,1)S(1)}, u32[]{:S(2)}, u32[]{:S(2)}) collective-permute-start(bf16[256,256]{1,0:T(8,128)(2,1)S(1)} %add_convert_fusion.3), channel_id=1, source_target_pairs={{0,4},{1,3},{4,8},{5,1},{8,12},{9,5},{12,14},{13,9},{14,10},{15,13... | collective-permute-start | bytes 393224 | tf_op jit(solution)/shard_map/ppermute | solution.py:56
  45.6 10.3 %collective-permute-start.18 = (bf16[256,256]{1,0:T(8,128)(2,1)S(1)}, bf16[256,256]{1,0:T(8,128)(2,1)S(1)}, u32[]{:S(2)}, u32[]{:S(2)}) collective-permute-start(bf16[256,256]{1,0:T(8,128)(2,1)S(1)} %add_convert_fusion.8), channel_id=1, source_target_pairs={{0,4},{1,3},{4,8},{5,1},{8,12},{9,5},{12,14},{13,9},{14,10},{15,13... | collective-permute-start | bytes 393224 | tf_op jit(solution)/shard_map/ppermute | solution.py:56
  47.7 13.3 %collective-permute-start.24 = (bf16[256,256]{1,0:T(8,128)(2,1)S(1)}, bf16[256,256]{1,0:T(8,128)(2,1)S(1)}, u32[]{:S(2)}, u32[]{:S(2)}) collective-permute-start(bf16[256,256]{1,0:T(8,128)(2,1)S(1)} %add_convert_fusion.5), channel_id=1, source_target_pairs={{0,2},{1,5},{4,0},{5,9},{8,4},{9,13},{12,8},{13,15},{14,12},{15,11... | collective-permute-start | bytes 393224 | tf_op jit(solution)/shard_map/ppermute | solution.py:56
  50.9 6.0 %collective-permute-start.27 = (bf16[256,256]{1,0:T(8,128)(2,1)S(1)}, bf16[256,256]{1,0:T(8,128)(2,1)S(1)}, u32[]{:S(2)}, u32[]{:S(2)}) collective-permute-start(bf16[256,256]{1,0:T(8,128)(2,1)S(1)} %add_convert_fusion.2), channel_id=1, source_target_pairs={{0,4},{1,3},{4,8},{5,1},{8,12},{9,5},{12,14},{13,9},{14,10},{15,13... | collective-permute-start | bytes 393224 | tf_op jit(solution)/shard_map/ppermute | solution.py:56
  56.0 6.1 %collective-permute-start.19 = (bf16[256,256]{1,0:T(8,128)(2,1)S(1)}, bf16[256,256]{1,0:T(8,128)(2,1)S(1)}, u32[]{:S(2)}, u32[]{:S(2)}) collective-permute-start(bf16[256,256]{1,0:T(8,128)(2,1)S(1)} %add_convert_fusion.7), channel_id=1, source_target_pairs={{0,4},{1,3},{4,8},{5,1},{8,12},{9,5},{12,14},{13,9},{14,10},{15,13... | collective-permute-start | bytes 393224 | tf_op jit(solution)/shard_map/ppermute | solution.py:56
  59.8 6.6 %collective-permute-start.30 = (bf16[256,256]{1,0:T(8,128)(2,1)S(1)}, bf16[256,256]{1,0:T(8,128)(2,1)S(1)}, u32[]{:S(2)}, u32[]{:S(2)}) collective-permute-start(bf16[256,256]{1,0:T(8,128)(2,1)S(1)} %fusion.1.refs_0_), channel_id=1, source_target_pairs={{0,2},{1,5},{4,0},{5,9},{8,4},{9,13},{12,8},{13,15},{14,12},{15,11... | collective-permute-start | bytes 393224 | tf_op jit(solution)/shard_map/ppermute | solution.py:56
  62.2 6.4 %collective-permute-start.34 = (bf16[256,256]{1,0:T(8,128)(2,1)S(1)}, bf16[256,256]{1,0:T(8,128)(2,1)S(1)}, u32[]{:S(2)}, u32[]{:S(2)}) collective-permute-start(bf16[256,256]{1,0:T(8,128)(2,1)S(1)} %multiply_convert_fusion.refs_1_), channel_id=1, source_target_pairs={{0,4},{1,3},{4,8},{5,1},{8,12},{9,5},{12,14},{13,9},{14,10},{15,13... | collective-permute-start | bytes 393224 | tf_op jit(solution)/shard_map/ppermute | solution.py:56
  64.3 6.4 %collective-permute-start.40 = (bf16[256,256]{1,0:T(8,128)(2,1)S(1)}, bf16[256,256]{1,0:T(8,128)(2,1)S(1)}, u32[]{:S(2)}, u32[]{:S(2)}) collective-permute-start(bf16[256,256]{1,0:T(8,128)(2,1)S(1)} %multiply_convert_fusion.refs_1_), channel_id=1, source_target_pairs={{0,2},{1,5},{4,0},{5,9},{8,4},{9,13},{12,8},{13,15},{14,12},{15,11... | collective-permute-start | bytes 393224 | tf_op jit(solution)/shard_map/ppermute | solution.py:56
  65.4 6.1 %collective-permute-start.38 = (bf16[256,256]{1,0:T(8,128)(2,1)S(1)}, bf16[256,256]{1,0:T(8,128)(2,1)S(1)}, u32[]{:S(2)}, u32[]{:S(2)}) collective-permute-start(bf16[256,256]{1,0:T(8,128)(2,1)S(1)} %fusion.1.refs_0_), channel_id=1, source_target_pairs={{0,4},{1,3},{4,8},{5,1},{8,12},{9,5},{12,14},{13,9},{14,10},{15,13... | collective-permute-start | bytes 393224 | tf_op jit(solution)/shard_map/ppermute | solution.py:56
  66.4 7.2 %collective-permute-start.31 = (bf16[256,256]{1,0:T(8,128)(2,1)S(1)}, bf16[256,256]{1,0:T(8,128)(2,1)S(1)}, u32[]{:S(2)}, u32[]{:S(2)}) collective-permute-start(bf16[256,256]{1,0:T(8,128)(2,1)S(1)} %collective-permute-done.30.refs_4_), channel_id=1, source_target_pairs={{0,2},{1,5},{4,0},{5,9},{8,4},{9,13},{12,8},{13,15},{14,12},{15,11... | collective-permute-start | bytes 393224 | tf_op jit(solution)/shard_map/ppermute | solution.py:56
  68.5 6.1 %collective-permute-start.35 = (bf16[256,256]{1,0:T(8,128)(2,1)S(1)}, bf16[256,256]{1,0:T(8,128)(2,1)S(1)}, u32[]{:S(2)}, u32[]{:S(2)}) collective-permute-start(bf16[256,256]{1,0:T(8,128)(2,1)S(1)} %collective-permute-done.34.refs_3_), channel_id=1, source_target_pairs={{0,4},{1,3},{4,8},{5,1},{8,12},{9,5},{12,14},{13,9},{14,10},{15,13... | collective-permute-start | bytes 393224 | tf_op jit(solution)/shard_map/ppermute | solution.py:56
  71.5 6.1 %collective-permute-start.39 = (bf16[256,256]{1,0:T(8,128)(2,1)S(1)}, bf16[256,256]{1,0:T(8,128)(2,1)S(1)}, u32[]{:S(2)}, u32[]{:S(2)}) collective-permute-start(bf16[256,256]{1,0:T(8,128)(2,1)S(1)} %collective-permute-done.38.refs_2_), channel_id=1, source_target_pairs={{0,4},{1,3},{4,8},{5,1},{8,12},{9,5},{12,14},{13,9},{14,10},{15,13... | collective-permute-start | bytes 393224 | tf_op jit(solution)/shard_map/ppermute | solution.py:56
  78.8 5.9 %collective-permute-start.33 = (bf16[256,256]{1,0:T(8,128)(2,1)S(1)}, bf16[256,256]{1,0:T(8,128)(2,1)S(1)}, u32[]{:S(2)}, u32[]{:S(2)}) collective-permute-start(bf16[256,256]{1,0:T(8,128)(2,1)S(1)} %collective-permute-done.32.refs_6_), channel_id=1, source_target_pairs={{0,2},{1,5},{4,0},{5,9},{8,4},{9,13},{12,8},{13,15},{14,12},{15,11... | collective-permute-start | bytes 393224 | tf_op jit(solution)/shard_map/ppermute | solution.py:56
  (17 other events, 144.4 us)

commit v25 on v20

--- a/solution.py
+++ b/solution.py
@@ -336,7 +336,7 @@
             if (chain, way) in moving:
                 total = total + moving[chain, way].astype(F32)
         if chain == 1:
-            wanted = after(wanted, codes)
+            wanted = after(wanted, errors[0][0])
         errors.append([((total - wanted.astype(F32)) * err_scale).astype(BF16)] + [None] * (size - 1))
 
     def back(slots, before):
@@ -356,7 +356,7 @@
         [starts] + turned_own + arrived + both_chains(inputs, range(1, size))[1:],
     )[0]
     for s in range(1, reach + 1):
-        gather_step(errors, s, (turned, turned) if s == 2 else None)
+        gather_step(errors, s, (turned, turned) if s == 1 else None)
     cut = 1 + 2 * min(1, reach - 1)
     groups = [group for group in (tuple(range(cut)), tuple(range(cut, far))) if group]
     outers, acc = [], None

time: 85.9 us -> 86 us (level)
  transfers between devices with their start and end apart: 45 -> 45, of which waited for: 28 -> 27; matrix products, arithmetic and copies ran while one was open for 2% -> 2% of each run, Pallas kernels for 10% -> 10%
where the time goes in v25:
time: 86 us; the launch traced here: 85.8 us
  starting transfers between devices  46.2 us (54%)
  waiting for transfers between devices  22.4 us (26%)
  Pallas kernels  13.5 us (16%)
  other arithmetic  1.56 us (2%)
  local copies, waits for them, and re-layouts  1.16 us (1%)
  between operations  0.95 us (1%)
    ppermute x42, starting transfers between devices, hop(): return lax.ppermute(shard, ('latent', 'layer'), pairs)  46.1 us
    ppermute x42, waiting for transfers between devices, hop(): return lax.ppermute(shard, ('latent', 'layer'), pairs)  21 us
    pallas_call x12, Pallas kernels, call(): pl.pallas_call(kernel, out_shape=outs, in_specs=[spec(pltpu.SMEM)] + [spe...  13.5 us
  transfers between devices with their start and end apart: 45, of which 27 were waited for; matrix products, arithmetic and copies ran while one was open for 2% of the time, Pallas kernels for 10%

profile of v25, /device:TPU:0, one launch (start us, length us, event | category | flops | bytes accessed | tf_op | source)
XLA Modules:
  0.0 85.8 jit_solution(17144905184094814741)
XLA Ops:
  1.7 3.1 %collective-permute-start.5 = (bf16[256,256]{1,0:T(8,128)(2,1)S(1)}, bf16[256,256]{1,0:T(8,128)(2,1)S(1)}, u32[]{:S(2)}, u32[]{:S(2)}) collective-permute-start(bf16[256,256]{1,0:T(8,128)(2,1)S(1)} %get-tuple-element.48.shard.refs_1_), channel_id=1, source_target_pairs={{0,4},{1,3},{4,8},{5,1},{8,12},{9,5},{12,14},{13,9},{14,10},{15,13... | collective-permute-start | bytes 393224 | tf_op jit(solution)/shard_map/ppermute | solution.py:56
  5.5 2.1 %collective-permute-start = (bf16[256,256]{1,0:T(8,128)(2,1)S(1)}, bf16[256,256]{1,0:T(8,128)(2,1)S(1)}, u32[]{:S(2)}, u32[]{:S(2)}) collective-permute-start(bf16[256,256]{1,0:T(8,128)(2,1)S(1)} %get-tuple-element.47.shard.refs_0_), channel_id=1, source_target_pairs={{0,4},{1,3},{4,8},{5,1},{8,12},{9,5},{12,14},{13,9},{14,10},{15,13... | collective-permute-start | bytes 393224 | tf_op jit(solution)/shard_map/ppermute | solution.py:56
  8.5 1.8 %collective-permute-start.6 = (bf16[256,256]{1,0:T(8,128)(2,1)S(1)}, bf16[256,256]{1,0:T(8,128)(2,1)S(1)}, u32[]{:S(2)}, u32[]{:S(2)}) collective-permute-start(bf16[256,256]{1,0:T(8,128)(2,1)S(1)} %collective-permute-done.5.refs_3_.refs_1_), channel_id=1, source_target_pairs={{0,4},{1,3},{4,8},{5,1},{8,12},{9,5},{12,14},{13,9},{14,10},{15,13... | collective-permute-start | bytes 393224 | tf_op jit(solution)/shard_map/ppermute | solution.py:56
  11.5 2.5 %collective-permute-start.10 = (bf16[256,256]{1,0:T(8,128)(2,1)S(1)}, bf16[256,256]{1,0:T(8,128)(2,1)S(1)}, u32[]{:S(2)}, u32[]{:S(2)}) collective-permute-start(bf16[256,256]{1,0:T(8,128)(2,1)S(1)} %collective-permute-done.refs_2_.refs_0_), channel_id=1, source_target_pairs={{0,4},{1,3},{4,8},{5,1},{8,12},{9,5},{12,14},{13,9},{14,10},{15,13... | collective-permute-start | bytes 393224 | tf_op jit(solution)/shard_map/ppermute | solution.py:56
  14.7 1.3 %collective-permute-start.7 = (bf16[256,256]{1,0:T(8,128)(2,1)S(1)}, bf16[256,256]{1,0:T(8,128)(2,1)S(1)}, u32[]{:S(2)}, u32[]{:S(2)}) collective-permute-start(bf16[256,256]{1,0:T(8,128)(2,1)S(1)} %collective-permute-done.6.refs_7_.refs_5_), channel_id=1, source_target_pairs={{0,4},{1,3},{4,8},{5,1},{8,12},{9,5},{12,14},{13,9},{14,10},{15,13... | collective-permute-start | bytes 393224 | tf_op jit(solution)/shard_map/ppermute | solution.py:56
  17.8 2.5 %collective-permute-start.12 = (bf16[256,256]{1,0:T(8,128)(2,1)S(1)}, bf16[256,256]{1,0:T(8,128)(2,1)S(1)}, u32[]{:S(2)}, u32[]{:S(2)}) collective-permute-start(bf16[256,256]{1,0:T(8,128)(2,1)S(1)} %collective-permute-done.10.refs_6_.refs_4_), channel_id=1, source_target_pairs={{0,4},{1,3},{4,8},{5,1},{8,12},{9,5},{12,14},{13,9},{14,10},{15,13... | collective-permute-start | bytes 393224 | tf_op jit(solution)/shard_map/ppermute | solution.py:56
  20.8 2.3 %collective-permute-start.8 = (bf16[256,256]{1,0:T(8,128)(2,1)S(1)}, bf16[256,256]{1,0:T(8,128)(2,1)S(1)}, u32[]{:S(2)}, u32[]{:S(2)}) collective-permute-start(bf16[256,256]{1,0:T(8,128)(2,1)S(1)} %collective-permute-done.7.refs_11_.refs_9_), channel_id=1, source_target_pairs={{0,4},{1,3},{4,8},{5,1},{8,12},{9,5},{12,14},{13,9},{14,10},{15,13... | collective-permute-start | bytes 393224 | tf_op jit(solution)/shard_map/ppermute | solution.py:56
  24.7 1.2 %collective-permute-done.13.refs_13_.refs_11_ = bf16[256,256]{1,0:T(8,128)(2,1)S(1)} collective-permute-done((bf16[256,256]{1,0:T(8,128)(2,1)S(1)}, bf16[256,256]{1,0:T(8,128)(2,1)S(1)}, u32[]{:S(2)}, u32[]{:S(2)}) %collective-permute-start.13) | collective-permute-done | bytes 131104 | tf_op jit(solution)/shard_map/ppermute | solution.py:56
  27.1 1.2 %collective-permute-done.4.refs_0_.refs_12_ = bf16[256,256]{1,0:T(8,128)(2,1)S(1)} collective-permute-done((bf16[256,256]{1,0:T(8,128)(2,1)S(1)}, bf16[256,256]{1,0:T(8,128)(2,1)S(1)}, u32[]{:S(2)}, u32[]{:S(2)}) %collective-permute-start.4) | collective-permute-done | bytes 131104 | tf_op jit(solution)/shard_map/ppermute | solution.py:56
  29.1 1.3 %collective-permute-done.15.earlier = bf16[512,128]{1,0:T(8,128)(2,1)S(1)} collective-permute-done((bf16[512,128]{1,0:T(8,128)(2,1)S(1)}, bf16[512,128]{1,0:T(8,128)(2,1)S(1)}, u32[]{:S(2)}, u32[]{:S(2)}) %collective-permute-start.15) | collective-permute-done | bytes 131104 | tf_op jit(solution)/shard_map/ppermute | solution.py:28
  31.5 1.9 %collective-permute-start.16 = (bf16[256,256]{1,0:T(8,128)(2,1)S(1)}, bf16[256,256]{1,0:T(8,128)(2,1)S(1)}, u32[]{:S(2)}, u32[]{:S(2)}) collective-permute-start(bf16[256,256]{1,0:T(8,128)(2,1)S(1)} %get-tuple-element.56), channel_id=1, source_target_pairs={{0,4},{1,3},{4,8},{5,1},{8,12},{9,5},{12,14},{13,9},{14,10},{15,13... | collective-permute-start | bytes 393224 | tf_op jit(solution)/shard_map/ppermute | solution.py:56
  33.4 1.2 %shard_map.97 = (f32[256,256]{1,0:T(8,128)S(1)}, f32[256,256]{1,0:T(8,128)S(1)}, f32[256,256]{1,0:T(8,128)S(1)}, f32[256,256]{1,0:T(8,128)S(1)}, f32[256,256]{1,...) custom-call(s32[9]{0:T(128)S(1)} %stack.39.starts, ...), custom_call_target="tpu_custom_call" | custom-call | flops 469762048 | bytes 1024 | tf_op jit(solution)/shard_map/pallas_call | solution.py:69
  34.9 1.8 %collective-permute-start.25 = (bf16[256,256]{1,0:T(8,128)(2,1)S(1)}, bf16[256,256]{1,0:T(8,128)(2,1)S(1)}, u32[]{:S(2)}, u32[]{:S(2)}) collective-permute-start(bf16[256,256]{1,0:T(8,128)(2,1)S(1)} %get-tuple-element.67), channel_id=1, source_target_pairs={{0,4},{1,3},{4,8},{5,1},{8,12},{9,5},{12,14},{13,9},{14,10},{15,13... | collective-permute-start | bytes 393224 | tf_op jit(solution)/shard_map/ppermute | solution.py:56
  37.5 2.1 %collective-permute-start.17 = (bf16[256,256]{1,0:T(8,128)(2,1)S(1)}, bf16[256,256]{1,0:T(8,128)(2,1)S(1)}, u32[]{:S(2)}, u32[]{:S(2)}) collective-permute-start(bf16[256,256]{1,0:T(8,128)(2,1)S(1)} %add_convert_fusion.9), channel_id=1, source_target_pairs={{0,4},{1,3},{4,8},{5,1},{8,12},{9,5},{12,14},{13,9},{14,10},{15,13... | collective-permute-start | bytes 393224 | tf_op jit(solution)/shard_map/ppermute | solution.py:56
  39.6 1.5 %collective-permute-done.20 = bf16[256,256]{1,0:T(8,128)(2,1)S(1)} collective-permute-done((bf16[256,256]{1,0:T(8,128)(2,1)S(1)}, bf16[256,256]{1,0:T(8,128)(2,1)S(1)}, u32[]{:S(2)}, u32[]{:S(2)}) %collective-permute-start.20) | collective-permute-done | bytes 131104 | tf_op jit(solution)/shard_map/ppermute | solution.py:56
  41.2 2.0 %collective-permute-start.26 = (bf16[256,256]{1,0:T(8,128)(2,1)S(1)}, bf16[256,256]{1,0:T(8,128)(2,1)S(1)}, u32[]{:S(2)}, u32[]{:S(2)}) collective-permute-start(bf16[256,256]{1,0:T(8,128)(2,1)S(1)} %add_convert_fusion.3), channel_id=1, source_target_pairs={{0,4},{1,3},{4,8},{5,1},{8,12},{9,5},{12,14},{13,9},{14,10},{15,13... | collective-permute-start | bytes 393224 | tf_op jit(solution)/shard_map/ppermute | solution.py:56
  44.0 1.9 %collective-permute-start.18 = (bf16[256,256]{1,0:T(8,128)(2,1)S(1)}, bf16[256,256]{1,0:T(8,128)(2,1)S(1)}, u32[]{:S(2)}, u32[]{:S(2)}) collective-permute-start(bf16[256,256]{1,0:T(8,128)(2,1)S(1)} %add_convert_fusion.8), channel_id=1, source_target_pairs={{0,4},{1,3},{4,8},{5,1},{8,12},{9,5},{12,14},{13,9},{14,10},{15,13... | collective-permute-start | bytes 393224 | tf_op jit(solution)/shard_map/ppermute | solution.py:56
  47.2 1.6 %collective-permute-start.27 = (bf16[256,256]{1,0:T(8,128)(2,1)S(1)}, bf16[256,256]{1,0:T(8,128)(2,1)S(1)}, u32[]{:S(2)}, u32[]{:S(2)}) collective-permute-start(bf16[256,256]{1,0:T(8,128)(2,1)S(1)} %add_convert_fusion.2), channel_id=1, source_target_pairs={{0,4},{1,3},{4,8},{5,1},{8,12},{9,5},{12,14},{13,9},{14,10},{15,13... | collective-permute-start | bytes 393224 | tf_op jit(solution)/shard_map/ppermute | solution.py:56
  48.8 1.5 %collective-permute-done.28 = bf16[256,256]{1,0:T(8,128)(2,1)S(1)} collective-permute-done((bf16[256,256]{1,0:T(8,128)(2,1)S(1)}, bf16[256,256]{1,0:T(8,128)(2,1)S(1)}, u32[]{:S(2)}, u32[]{:S(2)}) %collective-permute-start.28) | collective-permute-done | bytes 131104 | tf_op jit(solution)/shard_map/ppermute | solution.py:56
  50.4 2.1 %collective-permute-start.19 = (bf16[256,256]{1,0:T(8,128)(2,1)S(1)}, bf16[256,256]{1,0:T(8,128)(2,1)S(1)}, u32[]{:S(2)}, u32[]{:S(2)}) collective-permute-start(bf16[256,256]{1,0:T(8,128)(2,1)S(1)} %add_convert_fusion.7), channel_id=1, source_target_pairs={{0,4},{1,3},{4,8},{5,1},{8,12},{9,5},{12,14},{13,9},{14,10},{15,13... | collective-permute-start | bytes 393224 | tf_op jit(solution)/shard_map/ppermute | solution.py:56
  52.5 2.8 %collective-permute-done.29 = bf16[256,256]{1,0:T(8,128)(2,1)S(1)} collective-permute-done((bf16[256,256]{1,0:T(8,128)(2,1)S(1)}, bf16[256,256]{1,0:T(8,128)(2,1)S(1)}, u32[]{:S(2)}, u32[]{:S(2)}) %collective-permute-start.29) | collective-permute-done | bytes 131104 | tf_op jit(solution)/shard_map/ppermute | solution.py:56
  55.5 2.1 %collective-permute-start.34 = (bf16[256,256]{1,0:T(8,128)(2,1)S(1)}, bf16[256,256]{1,0:T(8,128)(2,1)S(1)}, u32[]{:S(2)}, u32[]{:S(2)}) collective-permute-start(bf16[256,256]{1,0:T(8,128)(2,1)S(1)} %multiply_convert_fusion.refs_1_), channel_id=1, source_target_pairs={{0,4},{1,3},{4,8},{5,1},{8,12},{9,5},{12,14},{13,9},{14,10},{15,13... | collective-permute-start | bytes 393224 | tf_op jit(solution)/shard_map/ppermute | solution.py:56
  58.6 2.1 %collective-permute-start.38 = (bf16[256,256]{1,0:T(8,128)(2,1)S(1)}, bf16[256,256]{1,0:T(8,128)(2,1)S(1)}, u32[]{:S(2)}, u32[]{:S(2)}) collective-permute-start(bf16[256,256]{1,0:T(8,128)(2,1)S(1)} %fusion.1.refs_0_), channel_id=1, source_target_pairs={{0,4},{1,3},{4,8},{5,1},{8,12},{9,5},{12,14},{13,9},{14,10},{15,13... | collective-permute-start | bytes 393224 | tf_op jit(solution)/shard_map/ppermute | solution.py:56
  61.8 2.1 %collective-permute-start.35 = (bf16[256,256]{1,0:T(8,128)(2,1)S(1)}, bf16[256,256]{1,0:T(8,128)(2,1)S(1)}, u32[]{:S(2)}, u32[]{:S(2)}) collective-permute-start(bf16[256,256]{1,0:T(8,128)(2,1)S(1)} %collective-permute-done.34.refs_3_), channel_id=1, source_target_pairs={{0,4},{1,3},{4,8},{5,1},{8,12},{9,5},{12,14},{13,9},{14,10},{15,13... | collective-permute-start | bytes 393224 | tf_op jit(solution)/shard_map/ppermute | solution.py:56
  64.8 2.1 %collective-permute-start.40 = (bf16[256,256]{1,0:T(8,128)(2,1)S(1)}, bf16[256,256]{1,0:T(8,128)(2,1)S(1)}, u32[]{:S(2)}, u32[]{:S(2)}) collective-permute-start(bf16[256,256]{1,0:T(8,128)(2,1)S(1)} %collective-permute-done.38.refs_2_), channel_id=1, source_target_pairs={{0,4},{1,3},{4,8},{5,1},{8,12},{9,5},{12,14},{13,9},{14,10},{15,13... | collective-permute-start | bytes 393224 | tf_op jit(solution)/shard_map/ppermute | solution.py:56
  68.0 2.3 %collective-permute-start.36 = (bf16[256,256]{1,0:T(8,128)(2,1)S(1)}, bf16[256,256]{1,0:T(8,128)(2,1)S(1)}, u32[]{:S(2)}, u32[]{:S(2)}) collective-permute-start(bf16[256,256]{1,0:T(8,128)(2,1)S(1)} %collective-permute-done.35.refs_1_), channel_id=1, source_target_pairs={{0,4},{1,3},{4,8},{5,1},{8,12},{9,5},{12,14},{13,9},{14,10},{15,13... | collective-permute-start | bytes 393224 | tf_op jit(solution)/shard_map/ppermute | solution.py:56
  71.0 2.1 %collective-permute-start.42 = (bf16[256,256]{1,0:T(8,128)(2,1)S(1)}, bf16[256,256]{1,0:T(8,128)(2,1)S(1)}, u32[]{:S(2)}, u32[]{:S(2)}) collective-permute-start(bf16[256,256]{1,0:T(8,128)(2,1)S(1)} %collective-permute-done.40.refs_0_), channel_id=1, source_target_pairs={{0,4},{1,3},{4,8},{5,1},{8,12},{9,5},{12,14},{13,9},{14,10},{15,13... | collective-permute-start | bytes 393224 | tf_op jit(solution)/shard_map/ppermute | solution.py:56
  74.1 1.6 %collective-permute-start.37 = (bf16[256,256]{1,0:T(8,128)(2,1)S(1)}, bf16[256,256]{1,0:T(8,128)(2,1)S(1)}, u32[]{:S(2)}, u32[]{:S(2)}) collective-permute-start(bf16[256,256]{1,0:T(8,128)(2,1)S(1)} %collective-permute-done.36.refs_5_), channel_id=1, source_target_pairs={{0,4},{1,3},{4,8},{5,1},{8,12},{9,5},{12,14},{13,9},{14,10},{15,13... | collective-permute-start | bytes 393224 | tf_op jit(solution)/shard_map/ppermute | solution.py:56
  78.1 1.3 %shard_map.101 = (f32[4,256,256]{2,1,0:T(8,128)S(1)}, f32[2,256,256]{2,1,0:T(8,128)S(1)}) custom-call(s32[9]{0:T(128)S(1)} %stack.39.starts, bf16[256,256]{1,0:T(8,128)(2,1)S(1)} %collective-permute-done.40.refs_0_, bf16[256,256]{1,0:T(8,128)(2,1)S(1)} %collective-permute-done.35.refs_1_, bf16[256,256]{1,0:T(8,128)(2,1)S(1)} %collective-permute-done.31.refs_2_, ...), custom_call_target="tpu_custom_call" | custom-call | flops 268435456 | bytes 1024 | tf_op jit(solution)/shard_map/pallas_call | solution.py:69
  79.4 1.4 %collective-permute-done.33.refs_0_ = bf16[256,256]{1,0:T(8,128)(2,1)S(1)} collective-permute-done((bf16[256,256]{1,0:T(8,128)(2,1)S(1)}, bf16[256,256]{1,0:T(8,128)(2,1)S(1)}, u32[]{:S(2)}, u32[]{:S(2)}) %collective-permute-start.33) | collective-permute-done | bytes 131104 | tf_op jit(solution)/shard_map/ppermute | solution.py:56
  81.4 1.6 %shard_map.102 = (f32[512,128]{1,0:T(8,128)S(1)}, f32[1,128,2048]{2,1,0:T(8,128)}) custom-call(s32[9]{0:T(128)S(1)} %stack.39.starts, bf16[256,256]{1,0:T(8,128)(2,1)S(1)} %collective-permute-done.33.refs_0_, bf16[256,256]{1,0:T(8,128)(2,1)S(1)} %collective-permute-done.37.refs_1_, bf16[256,2048]{1,0:T(8,128)(2,1)S(1)} %pad_maximum_fusion.stacked.refs_6_.refs_8_.refs_2_, ...), custom_call_target="tpu_custom_call" | custom-call | bytes 1024 | tf_op jit(solution)/shard_map/pallas_call | solution.py:69
  83.1 2.7 %shard_map.104 = (f32[1,2048,128]{2,1,0:T(8,128)}, f32[1,128]{1,0:T(1,128)}, f32[128,1024]{1,0:T(8,128)}) custom-call(s32[9]{0:T(128)S(1)} %stack.39.starts, bf16[2048,512]{1,0:T(8,128)(2,1)S(1)} %shard_map.99.turned, f32[512,128]{1,0:T(8,128)S(1)} %get-tuple-element.74.preact, f32[512,128]{1,0:T(8,128)S(1)} %get-tuple-element.83.back_own, ...), custom_call_target="tpu_custom_call" | custom-call | flops 268435456 | bytes 1024 | tf_op jit(solution)/shard_map/pallas_call | solution.py:69
  (95 shorter events, 23.9 us)
Async XLA Ops:
  1.7 6.8 %collective-permute-start.5 = (bf16[256,256]{1,0:T(8,128)(2,1)S(1)}, bf16[256,256]{1,0:T(8,128)(2,1)S(1)}, u32[]{:S(2)}, u32[]{:S(2)}) collective-permute-start(bf16[256,256]{1,0:T(8,128)(2,1)S(1)} %get-tuple-element.48.shard.refs_1_), channel_id=1, source_target_pairs={{0,4},{1,3},{4,8},{5,1},{8,12},{9,5},{12,14},{13,9},{14,10},{15,13... | collective-permute-start | bytes 393224 | tf_op jit(solution)/shard_map/ppermute | solution.py:56
  4.8 6.3 %collective-permute-start.1 = (bf16[256,256]{1,0:T(8,128)(2,1)S(1)}, bf16[256,256]{1,0:T(8,128)(2,1)S(1)}, u32[]{:S(2)}, u32[]{:S(2)}) collective-permute-start(bf16[256,256]{1,0:T(8,128)(2,1)S(1)} %get-tuple-element.47.shard.refs_0_), channel_id=1, source_target_pairs={{0,2},{1,5},{4,0},{5,9},{8,4},{9,13},{12,8},{13,15},{14,12},{15,11... | collective-permute-start | bytes 393224 | tf_op jit(solution)/shard_map/ppermute | solution.py:56
  5.5 6.0 %collective-permute-start = (bf16[256,256]{1,0:T(8,128)(2,1)S(1)}, bf16[256,256]{1,0:T(8,128)(2,1)S(1)}, u32[]{:S(2)}, u32[]{:S(2)}) collective-permute-start(bf16[256,256]{1,0:T(8,128)(2,1)S(1)} %get-tuple-element.47.shard.refs_0_), channel_id=1, source_target_pairs={{0,4},{1,3},{4,8},{5,1},{8,12},{9,5},{12,14},{13,9},{14,10},{15,13... | collective-permute-start | bytes 393224 | tf_op jit(solution)/shard_map/ppermute | solution.py:56
  8.5 6.2 %collective-permute-start.6 = (bf16[256,256]{1,0:T(8,128)(2,1)S(1)}, bf16[256,256]{1,0:T(8,128)(2,1)S(1)}, u32[]{:S(2)}, u32[]{:S(2)}) collective-permute-start(bf16[256,256]{1,0:T(8,128)(2,1)S(1)} %collective-permute-done.5.refs_3_.refs_1_), channel_id=1, source_target_pairs={{0,4},{1,3},{4,8},{5,1},{8,12},{9,5},{12,14},{13,9},{14,10},{15,13... | collective-permute-start | bytes 393224 | tf_op jit(solution)/shard_map/ppermute | solution.py:56
  11.1 5.8 %collective-permute-start.2 = (bf16[256,256]{1,0:T(8,128)(2,1)S(1)}, bf16[256,256]{1,0:T(8,128)(2,1)S(1)}, u32[]{:S(2)}, u32[]{:S(2)}) collective-permute-start(bf16[256,256]{1,0:T(8,128)(2,1)S(1)} %collective-permute-done.1.refs_4_.refs_2_), channel_id=1, source_target_pairs={{0,2},{1,5},{4,0},{5,9},{8,4},{9,13},{12,8},{13,15},{14,12},{15,11... | collective-permute-start | bytes 393224 | tf_op jit(solution)/shard_map/ppermute | solution.py:56
  11.5 12.0 %collective-permute-start.14 = (bf16[128,1024]{1,0:T(8,128)(2,1)}, bf16[128,1024]{1,0:T(8,128)(2,1)S(1)}, u32[]{:S(2)}, u32[]{:S(2)}) collective-permute-start(bf16[128,1024]{1,0:T(8,128)(2,1)} %param.11), channel_id=1, source_target_pairs={{0,1},{1,0},{2,3},{3,2},{4,5},{5,4},{6,7},{7,6},{8,9},{9,8},{10,11... | collective-permute-start | bytes 786440 | tf_op jit(solution)/shard_map/ppermute | solution.py:28
  11.5 6.3 %collective-permute-start.10 = (bf16[256,256]{1,0:T(8,128)(2,1)S(1)}, bf16[256,256]{1,0:T(8,128)(2,1)S(1)}, u32[]{:S(2)}, u32[]{:S(2)}) collective-permute-start(bf16[256,256]{1,0:T(8,128)(2,1)S(1)} %collective-permute-done.refs_2_.refs_0_), channel_id=1, source_target_pairs={{0,4},{1,3},{4,8},{5,1},{8,12},{9,5},{12,14},{13,9},{14,10},{15,13... | collective-permute-start | bytes 393224 | tf_op jit(solution)/shard_map/ppermute | solution.py:56
  14.0 6.4 %collective-permute-start.11 = (bf16[256,256]{1,0:T(8,128)(2,1)S(1)}, bf16[256,256]{1,0:T(8,128)(2,1)S(1)}, u32[]{:S(2)}, u32[]{:S(2)}) collective-permute-start(bf16[256,256]{1,0:T(8,128)(2,1)S(1)} %collective-permute-done.9.refs_5_.refs_3_), channel_id=1, source_target_pairs={{0,2},{1,5},{4,0},{5,9},{8,4},{9,13},{12,8},{13,15},{14,12},{15,11... | collective-permute-start | bytes 393224 | tf_op jit(solution)/shard_map/ppermute | solution.py:56
  14.7 6.0 %collective-permute-start.7 = (bf16[256,256]{1,0:T(8,128)(2,1)S(1)}, bf16[256,256]{1,0:T(8,128)(2,1)S(1)}, u32[]{:S(2)}, u32[]{:S(2)}) collective-permute-start(bf16[256,256]{1,0:T(8,128)(2,1)S(1)} %collective-permute-done.6.refs_7_.refs_5_), channel_id=1, source_target_pairs={{0,4},{1,3},{4,8},{5,1},{8,12},{9,5},{12,14},{13,9},{14,10},{15,13... | collective-permute-start | bytes 393224 | tf_op jit(solution)/shard_map/ppermute | solution.py:56
  16.9 6.4 %collective-permute-start.3 = (bf16[256,256]{1,0:T(8,128)(2,1)S(1)}, bf16[256,256]{1,0:T(8,128)(2,1)S(1)}, u32[]{:S(2)}, u32[]{:S(2)}) collective-permute-start(bf16[256,256]{1,0:T(8,128)(2,1)S(1)} %collective-permute-done.2.refs_8_.refs_6_), channel_id=1, source_target_pairs={{0,2},{1,5},{4,0},{5,9},{8,4},{9,13},{12,8},{13,15},{14,12},{15,11... | collective-permute-start | bytes 393224 | tf_op jit(solution)/shard_map/ppermute | solution.py:56
  17.8 6.9 %collective-permute-start.12 = (bf16[256,256]{1,0:T(8,128)(2,1)S(1)}, bf16[256,256]{1,0:T(8,128)(2,1)S(1)}, u32[]{:S(2)}, u32[]{:S(2)}) collective-permute-start(bf16[256,256]{1,0:T(8,128)(2,1)S(1)} %collective-permute-done.10.refs_6_.refs_4_), channel_id=1, source_target_pairs={{0,4},{1,3},{4,8},{5,1},{8,12},{9,5},{12,14},{13,9},{14,10},{15,13... | collective-permute-start | bytes 393224 | tf_op jit(solution)/shard_map/ppermute | solution.py:56
  20.8 6.3 %collective-permute-start.8 = (bf16[256,256]{1,0:T(8,128)(2,1)S(1)}, bf16[256,256]{1,0:T(8,128)(2,1)S(1)}, u32[]{:S(2)}, u32[]{:S(2)}) collective-permute-start(bf16[256,256]{1,0:T(8,128)(2,1)S(1)} %collective-permute-done.7.refs_11_.refs_9_), channel_id=1, source_target_pairs={{0,4},{1,3},{4,8},{5,1},{8,12},{9,5},{12,14},{13,9},{14,10},{15,13... | collective-permute-start | bytes 393224 | tf_op jit(solution)/shard_map/ppermute | solution.py:56
  31.3 6.1 %collective-permute-start.21 = (bf16[256,256]{1,0:T(8,128)(2,1)S(1)}, bf16[256,256]{1,0:T(8,128)(2,1)S(1)}, u32[]{:S(2)}, u32[]{:S(2)}) collective-permute-start(bf16[256,256]{1,0:T(8,128)(2,1)S(1)} %get-tuple-element.60), channel_id=1, source_target_pairs={{0,2},{1,5},{4,0},{5,9},{8,4},{9,13},{12,8},{13,15},{14,12},{15,11... | collective-permute-start | bytes 393224 | tf_op jit(solution)/shard_map/ppermute | solution.py:56
  31.5 5.9 %collective-permute-start.16 = (bf16[256,256]{1,0:T(8,128)(2,1)S(1)}, bf16[256,256]{1,0:T(8,128)(2,1)S(1)}, u32[]{:S(2)}, u32[]{:S(2)}) collective-permute-start(bf16[256,256]{1,0:T(8,128)(2,1)S(1)} %get-tuple-element.56), channel_id=1, source_target_pairs={{0,4},{1,3},{4,8},{5,1},{8,12},{9,5},{12,14},{13,9},{14,10},{15,13... | collective-permute-start | bytes 393224 | tf_op jit(solution)/shard_map/ppermute | solution.py:56
  34.6 6.4 %collective-permute-start.20 = (bf16[256,256]{1,0:T(8,128)(2,1)S(1)}, bf16[256,256]{1,0:T(8,128)(2,1)S(1)}, u32[]{:S(2)}, u32[]{:S(2)}) collective-permute-start(bf16[256,256]{1,0:T(8,128)(2,1)S(1)} %get-tuple-element.59), channel_id=1, source_target_pairs={{0,2},{1,5},{4,0},{5,9},{8,4},{9,13},{12,8},{13,15},{14,12},{15,11... | collective-permute-start | bytes 393224 | tf_op jit(solution)/shard_map/ppermute | solution.py:56
  34.9 6.3 %collective-permute-start.25 = (bf16[256,256]{1,0:T(8,128)(2,1)S(1)}, bf16[256,256]{1,0:T(8,128)(2,1)S(1)}, u32[]{:S(2)}, u32[]{:S(2)}) collective-permute-start(bf16[256,256]{1,0:T(8,128)(2,1)S(1)} %get-tuple-element.67), channel_id=1, source_target_pairs={{0,4},{1,3},{4,8},{5,1},{8,12},{9,5},{12,14},{13,9},{14,10},{15,13... | collective-permute-start | bytes 393224 | tf_op jit(solution)/shard_map/ppermute | solution.py:56
  37.4 6.4 %collective-permute-start.23 = (bf16[256,256]{1,0:T(8,128)(2,1)S(1)}, bf16[256,256]{1,0:T(8,128)(2,1)S(1)}, u32[]{:S(2)}, u32[]{:S(2)}) collective-permute-start(bf16[256,256]{1,0:T(8,128)(2,1)S(1)} %add_convert_fusion.4), channel_id=1, source_target_pairs={{0,2},{1,5},{4,0},{5,9},{8,4},{9,13},{12,8},{13,15},{14,12},{15,11... | collective-permute-start | bytes 393224 | tf_op jit(solution)/shard_map/ppermute | solution.py:56
  37.5 6.5 %collective-permute-start.17 = (bf16[256,256]{1,0:T(8,128)(2,1)S(1)}, bf16[256,256]{1,0:T(8,128)(2,1)S(1)}, u32[]{:S(2)}, u32[]{:S(2)}) collective-permute-start(bf16[256,256]{1,0:T(8,128)(2,1)S(1)} %add_convert_fusion.9), channel_id=1, source_target_pairs={{0,4},{1,3},{4,8},{5,1},{8,12},{9,5},{12,14},{13,9},{14,10},{15,13... | collective-permute-start | bytes 393224 | tf_op jit(solution)/shard_map/ppermute | solution.py:56
  41.2 6.0 %collective-permute-start.26 = (bf16[256,256]{1,0:T(8,128)(2,1)S(1)}, bf16[256,256]{1,0:T(8,128)(2,1)S(1)}, u32[]{:S(2)}, u32[]{:S(2)}) collective-permute-start(bf16[256,256]{1,0:T(8,128)(2,1)S(1)} %add_convert_fusion.3), channel_id=1, source_target_pairs={{0,4},{1,3},{4,8},{5,1},{8,12},{9,5},{12,14},{13,9},{14,10},{15,13... | collective-permute-start | bytes 393224 | tf_op jit(solution)/shard_map/ppermute | solution.py:56
  43.8 6.5 %collective-permute-start.28 = (bf16[256,256]{1,0:T(8,128)(2,1)S(1)}, bf16[256,256]{1,0:T(8,128)(2,1)S(1)}, u32[]{:S(2)}, u32[]{:S(2)}) collective-permute-start(bf16[256,256]{1,0:T(8,128)(2,1)S(1)} %add_convert_fusion.1), channel_id=1, source_target_pairs={{0,2},{1,5},{4,0},{5,9},{8,4},{9,13},{12,8},{13,15},{14,12},{15,11... | collective-permute-start | bytes 393224 | tf_op jit(solution)/shard_map/ppermute | solution.py:56
  44.0 6.3 %collective-permute-start.18 = (bf16[256,256]{1,0:T(8,128)(2,1)S(1)}, bf16[256,256]{1,0:T(8,128)(2,1)S(1)}, u32[]{:S(2)}, u32[]{:S(2)}) collective-permute-start(bf16[256,256]{1,0:T(8,128)(2,1)S(1)} %add_convert_fusion.8), channel_id=1, source_target_pairs={{0,4},{1,3},{4,8},{5,1},{8,12},{9,5},{12,14},{13,9},{14,10},{15,13... | collective-permute-start | bytes 393224 | tf_op jit(solution)/shard_map/ppermute | solution.py:56
  46.6 8.8 %collective-permute-start.24 = (bf16[256,256]{1,0:T(8,128)(2,1)S(1)}, bf16[256,256]{1,0:T(8,128)(2,1)S(1)}, u32[]{:S(2)}, u32[]{:S(2)}) collective-permute-start(bf16[256,256]{1,0:T(8,128)(2,1)S(1)} %add_convert_fusion.5), channel_id=1, source_target_pairs={{0,2},{1,5},{4,0},{5,9},{8,4},{9,13},{12,8},{13,15},{14,12},{15,11... | collective-permute-start | bytes 393224 | tf_op jit(solution)/shard_map/ppermute | solution.py:56
  55.5 6.3 %collective-permute-start.34 = (bf16[256,256]{1,0:T(8,128)(2,1)S(1)}, bf16[256,256]{1,0:T(8,128)(2,1)S(1)}, u32[]{:S(2)}, u32[]{:S(2)}) collective-permute-start(bf16[256,256]{1,0:T(8,128)(2,1)S(1)} %multiply_convert_fusion.refs_1_), channel_id=1, source_target_pairs={{0,4},{1,3},{4,8},{5,1},{8,12},{9,5},{12,14},{13,9},{14,10},{15,13... | collective-permute-start | bytes 393224 | tf_op jit(solution)/shard_map/ppermute | solution.py:56
  57.5 6.4 %collective-permute-start.30 = (bf16[256,256]{1,0:T(8,128)(2,1)S(1)}, bf16[256,256]{1,0:T(8,128)(2,1)S(1)}, u32[]{:S(2)}, u32[]{:S(2)}) collective-permute-start(bf16[256,256]{1,0:T(8,128)(2,1)S(1)} %fusion.1.refs_0_), channel_id=1, source_target_pairs={{0,2},{1,5},{4,0},{5,9},{8,4},{9,13},{12,8},{13,15},{14,12},{15,11... | collective-permute-start | bytes 393224 | tf_op jit(solution)/shard_map/ppermute | solution.py:56
  58.6 6.1 %collective-permute-start.38 = (bf16[256,256]{1,0:T(8,128)(2,1)S(1)}, bf16[256,256]{1,0:T(8,128)(2,1)S(1)}, u32[]{:S(2)}, u32[]{:S(2)}) collective-permute-start(bf16[256,256]{1,0:T(8,128)(2,1)S(1)} %fusion.1.refs_0_), channel_id=1, source_target_pairs={{0,4},{1,3},{4,8},{5,1},{8,12},{9,5},{12,14},{13,9},{14,10},{15,13... | collective-permute-start | bytes 393224 | tf_op jit(solution)/shard_map/ppermute | solution.py:56
  60.7 6.2 %collective-permute-start.39 = (bf16[256,256]{1,0:T(8,128)(2,1)S(1)}, bf16[256,256]{1,0:T(8,128)(2,1)S(1)}, u32[]{:S(2)}, u32[]{:S(2)}) collective-permute-start(bf16[256,256]{1,0:T(8,128)(2,1)S(1)} %multiply_convert_fusion.refs_1_), channel_id=1, source_target_pairs={{0,2},{1,5},{4,0},{5,9},{8,4},{9,13},{12,8},{13,15},{14,12},{15,11... | collective-permute-start | bytes 393224 | tf_op jit(solution)/shard_map/ppermute | solution.py:56
  61.8 6.2 %collective-permute-start.35 = (bf16[256,256]{1,0:T(8,128)(2,1)S(1)}, bf16[256,256]{1,0:T(8,128)(2,1)S(1)}, u32[]{:S(2)}, u32[]{:S(2)}) collective-permute-start(bf16[256,256]{1,0:T(8,128)(2,1)S(1)} %collective-permute-done.34.refs_3_), channel_id=1, source_target_pairs={{0,4},{1,3},{4,8},{5,1},{8,12},{9,5},{12,14},{13,9},{14,10},{15,13... | collective-permute-start | bytes 393224 | tf_op jit(solution)/shard_map/ppermute | solution.py:56
  63.9 6.4 %collective-permute-start.31 = (bf16[256,256]{1,0:T(8,128)(2,1)S(1)}, bf16[256,256]{1,0:T(8,128)(2,1)S(1)}, u32[]{:S(2)}, u32[]{:S(2)}) collective-permute-start(bf16[256,256]{1,0:T(8,128)(2,1)S(1)} %collective-permute-done.30.refs_4_), channel_id=1, source_target_pairs={{0,2},{1,5},{4,0},{5,9},{8,4},{9,13},{12,8},{13,15},{14,12},{15,11... | collective-permute-start | bytes 393224 | tf_op jit(solution)/shard_map/ppermute | solution.py:56
  64.8 6.2 %collective-permute-start.40 = (bf16[256,256]{1,0:T(8,128)(2,1)S(1)}, bf16[256,256]{1,0:T(8,128)(2,1)S(1)}, u32[]{:S(2)}, u32[]{:S(2)}) collective-permute-start(bf16[256,256]{1,0:T(8,128)(2,1)S(1)} %collective-permute-done.38.refs_2_), channel_id=1, source_target_pairs={{0,4},{1,3},{4,8},{5,1},{8,12},{9,5},{12,14},{13,9},{14,10},{15,13... | collective-permute-start | bytes 393224 | tf_op jit(solution)/shard_map/ppermute | solution.py:56
  66.8 6.3 %collective-permute-start.41 = (bf16[256,256]{1,0:T(8,128)(2,1)S(1)}, bf16[256,256]{1,0:T(8,128)(2,1)S(1)}, u32[]{:S(2)}, u32[]{:S(2)}) collective-permute-start(bf16[256,256]{1,0:T(8,128)(2,1)S(1)} %collective-permute-done.39.refs_5_), channel_id=1, source_target_pairs={{0,2},{1,5},{4,0},{5,9},{8,4},{9,13},{12,8},{13,15},{14,12},{15,11... | collective-permute-start | bytes 393224 | tf_op jit(solution)/shard_map/ppermute | solution.py:56
  68.0 6.1 %collective-permute-start.36 = (bf16[256,256]{1,0:T(8,128)(2,1)S(1)}, bf16[256,256]{1,0:T(8,128)(2,1)S(1)}, u32[]{:S(2)}, u32[]{:S(2)}) collective-permute-start(bf16[256,256]{1,0:T(8,128)(2,1)S(1)} %collective-permute-done.35.refs_1_), channel_id=1, source_target_pairs={{0,4},{1,3},{4,8},{5,1},{8,12},{9,5},{12,14},{13,9},{14,10},{15,13... | collective-permute-start | bytes 393224 | tf_op jit(solution)/shard_map/ppermute | solution.py:56
  71.0 6.3 %collective-permute-start.42 = (bf16[256,256]{1,0:T(8,128)(2,1)S(1)}, bf16[256,256]{1,0:T(8,128)(2,1)S(1)}, u32[]{:S(2)}, u32[]{:S(2)}) collective-permute-start(bf16[256,256]{1,0:T(8,128)(2,1)S(1)} %collective-permute-done.40.refs_0_), channel_id=1, source_target_pairs={{0,4},{1,3},{4,8},{5,1},{8,12},{9,5},{12,14},{13,9},{14,10},{15,13... | collective-permute-start | bytes 393224 | tf_op jit(solution)/shard_map/ppermute | solution.py:56
  (17 other events, 140.2 us)

commit v26 on v20

--- a/solution.py
+++ b/solution.py
@@ -164,7 +164,7 @@
             error = shards[chain][...]
             last = last + jnp.dot(both_t[chain][lat:, :], error, preferred_element_type=F32)
             term = lax.dot_general(error, decoder, OVER_COLS, preferred_element_type=F32)
-            sent[chain * rows:(chain + 1) * rows, :] = (before[chain, :, lat:] + term).astype(BF16)
+            sent[chain * rows:(chain + 1) * rows, :] = before[chain, :, lat:] + term
         pieces = [(far, last)]
         for group, outer in zip(slots, outers):
             pieces += [(slot, outer[i, lat:]) for i, slot in enumerate(group)]
@@ -174,7 +174,7 @@
             @pl.when(start < half_width)
             def _():
                 for c in range(0, wide, lat):
-                    sent[pl.ds(2 * rows + start + c, lat), :] = piece[:, c:c + lat].astype(BF16)
+                    sent[pl.ds(2 * rows + start + c, lat), :] = piece[:, c:c + lat]
 
             @pl.when(start >= half_width)
             def _():
@@ -366,7 +366,7 @@
     last = both_chains(errors, (far,)) + [stacked] + both_t + outers + [acc]
     sent, high = call(
         functools.partial(cross_back_kernel, groups, far),
-        [shape((rows + half_width, lat), BF16), shape((half_width, lat), F32)],
+        [shape((rows + half_width, lat), F32), shape((half_width, lat), F32)],
         0,
         [starts] + last,
     )

time: 85.9 us -> 86.4 us (level)
  no operation moved by 1% of the time
where the time goes in v26:
time: 86.4 us; the launch traced here: 86.3 us
  starting transfers between devices  46 us (53%)
  waiting for transfers between devices  23.1 us (27%)
  Pallas kernels  13.5 us (16%)
  other arithmetic  1.56 us (2%)
  local copies, waits for them, and re-layouts  1.16 us (1%)
  between operations  0.92 us (1%)
    ppermute x42, starting transfers between devices, hop(): return lax.ppermute(shard, ('latent', 'layer'), pairs)  45.9 us
    ppermute x42, waiting for transfers between devices, hop(): return lax.ppermute(shard, ('latent', 'layer'), pairs)  21.2 us
    pallas_call x12, Pallas kernels, call(): pl.pallas_call(kernel, out_shape=outs, in_specs=[spec(pltpu.SMEM)] + [spe...  13.5 us
    ppermute x3, waiting for transfers between devices, swapped(): lax.ppermute(shard, 'layer', [(i, size - 1 - i) for i in range(size)])  1.96 us
  transfers between devices with their start and end apart: 45, of which 28 were waited for; matrix products, arithmetic and copies ran while one was open for 2% of the time, Pallas kernels for 10%

profile of v26, /device:TPU:0, one launch (start us, length us, event | category | flops | bytes accessed | tf_op | source)
XLA Modules:
  0.0 86.3 jit_solution(3829102816669507131)
XLA Ops:
  1.7 3.1 %collective-permute-start.5 = (bf16[256,256]{1,0:T(8,128)(2,1)S(1)}, bf16[256,256]{1,0:T(8,128)(2,1)S(1)}, u32[]{:S(2)}, u32[]{:S(2)}) collective-permute-start(bf16[256,256]{1,0:T(8,128)(2,1)S(1)} %get-tuple-element.48.shard.refs_1_), channel_id=1, source_target_pairs={{0,4},{1,3},{4,8},{5,1},{8,12},{9,5},{12,14},{13,9},{14,10},{15,13... | collective-permute-start | bytes 393224 | tf_op jit(solution)/shard_map/ppermute | solution.py:56
  5.5 2.1 %collective-permute-start = (bf16[256,256]{1,0:T(8,128)(2,1)S(1)}, bf16[256,256]{1,0:T(8,128)(2,1)S(1)}, u32[]{:S(2)}, u32[]{:S(2)}) collective-permute-start(bf16[256,256]{1,0:T(8,128)(2,1)S(1)} %get-tuple-element.47.shard.refs_0_), channel_id=1, source_target_pairs={{0,4},{1,3},{4,8},{5,1},{8,12},{9,5},{12,14},{13,9},{14,10},{15,13... | collective-permute-start | bytes 393224 | tf_op jit(solution)/shard_map/ppermute | solution.py:56
  8.5 1.8 %collective-permute-start.6 = (bf16[256,256]{1,0:T(8,128)(2,1)S(1)}, bf16[256,256]{1,0:T(8,128)(2,1)S(1)}, u32[]{:S(2)}, u32[]{:S(2)}) collective-permute-start(bf16[256,256]{1,0:T(8,128)(2,1)S(1)} %collective-permute-done.5.refs_3_.refs_1_), channel_id=1, source_target_pairs={{0,4},{1,3},{4,8},{5,1},{8,12},{9,5},{12,14},{13,9},{14,10},{15,13... | collective-permute-start | bytes 393224 | tf_op jit(solution)/shard_map/ppermute | solution.py:56
  11.5 2.5 %collective-permute-start.10 = (bf16[256,256]{1,0:T(8,128)(2,1)S(1)}, bf16[256,256]{1,0:T(8,128)(2,1)S(1)}, u32[]{:S(2)}, u32[]{:S(2)}) collective-permute-start(bf16[256,256]{1,0:T(8,128)(2,1)S(1)} %collective-permute-done.refs_2_.refs_0_), channel_id=1, source_target_pairs={{0,4},{1,3},{4,8},{5,1},{8,12},{9,5},{12,14},{13,9},{14,10},{15,13... | collective-permute-start | bytes 393224 | tf_op jit(solution)/shard_map/ppermute | solution.py:56
  14.7 1.3 %collective-permute-start.7 = (bf16[256,256]{1,0:T(8,128)(2,1)S(1)}, bf16[256,256]{1,0:T(8,128)(2,1)S(1)}, u32[]{:S(2)}, u32[]{:S(2)}) collective-permute-start(bf16[256,256]{1,0:T(8,128)(2,1)S(1)} %collective-permute-done.6.refs_7_.refs_5_), channel_id=1, source_target_pairs={{0,4},{1,3},{4,8},{5,1},{8,12},{9,5},{12,14},{13,9},{14,10},{15,13... | collective-permute-start | bytes 393224 | tf_op jit(solution)/shard_map/ppermute | solution.py:56
  17.8 2.5 %collective-permute-start.12 = (bf16[256,256]{1,0:T(8,128)(2,1)S(1)}, bf16[256,256]{1,0:T(8,128)(2,1)S(1)}, u32[]{:S(2)}, u32[]{:S(2)}) collective-permute-start(bf16[256,256]{1,0:T(8,128)(2,1)S(1)} %collective-permute-done.10.refs_6_.refs_4_), channel_id=1, source_target_pairs={{0,4},{1,3},{4,8},{5,1},{8,12},{9,5},{12,14},{13,9},{14,10},{15,13... | collective-permute-start | bytes 393224 | tf_op jit(solution)/shard_map/ppermute | solution.py:56
  20.8 2.3 %collective-permute-start.8 = (bf16[256,256]{1,0:T(8,128)(2,1)S(1)}, bf16[256,256]{1,0:T(8,128)(2,1)S(1)}, u32[]{:S(2)}, u32[]{:S(2)}) collective-permute-start(bf16[256,256]{1,0:T(8,128)(2,1)S(1)} %collective-permute-done.7.refs_11_.refs_9_), channel_id=1, source_target_pairs={{0,4},{1,3},{4,8},{5,1},{8,12},{9,5},{12,14},{13,9},{14,10},{15,13... | collective-permute-start | bytes 393224 | tf_op jit(solution)/shard_map/ppermute | solution.py:56
  24.7 1.2 %collective-permute-done.13.refs_13_.refs_11_ = bf16[256,256]{1,0:T(8,128)(2,1)S(1)} collective-permute-done((bf16[256,256]{1,0:T(8,128)(2,1)S(1)}, bf16[256,256]{1,0:T(8,128)(2,1)S(1)}, u32[]{:S(2)}, u32[]{:S(2)}) %collective-permute-start.13) | collective-permute-done | bytes 131104 | tf_op jit(solution)/shard_map/ppermute | solution.py:56
  27.1 1.2 %collective-permute-done.4.refs_0_.refs_12_ = bf16[256,256]{1,0:T(8,128)(2,1)S(1)} collective-permute-done((bf16[256,256]{1,0:T(8,128)(2,1)S(1)}, bf16[256,256]{1,0:T(8,128)(2,1)S(1)}, u32[]{:S(2)}, u32[]{:S(2)}) %collective-permute-start.4) | collective-permute-done | bytes 131104 | tf_op jit(solution)/shard_map/ppermute | solution.py:56
  29.1 1.3 %collective-permute-done.15.earlier = bf16[512,128]{1,0:T(8,128)(2,1)S(1)} collective-permute-done((bf16[512,128]{1,0:T(8,128)(2,1)S(1)}, bf16[512,128]{1,0:T(8,128)(2,1)S(1)}, u32[]{:S(2)}, u32[]{:S(2)}) %collective-permute-start.15) | collective-permute-done | bytes 131104 | tf_op jit(solution)/shard_map/ppermute | solution.py:28
  31.5 1.9 %collective-permute-start.16 = (bf16[256,256]{1,0:T(8,128)(2,1)S(1)}, bf16[256,256]{1,0:T(8,128)(2,1)S(1)}, u32[]{:S(2)}, u32[]{:S(2)}) collective-permute-start(bf16[256,256]{1,0:T(8,128)(2,1)S(1)} %get-tuple-element.56), channel_id=1, source_target_pairs={{0,4},{1,3},{4,8},{5,1},{8,12},{9,5},{12,14},{13,9},{14,10},{15,13... | collective-permute-start | bytes 393224 | tf_op jit(solution)/shard_map/ppermute | solution.py:56
  33.4 1.2 %shard_map.97 = (f32[256,256]{1,0:T(8,128)S(1)}, f32[256,256]{1,0:T(8,128)S(1)}, f32[256,256]{1,0:T(8,128)S(1)}, f32[256,256]{1,0:T(8,128)S(1)}, f32[256,256]{1,...) custom-call(s32[9]{0:T(128)S(1)} %stack.39.starts, ...), custom_call_target="tpu_custom_call" | custom-call | flops 469762048 | bytes 1024 | tf_op jit(solution)/shard_map/pallas_call | solution.py:69
  34.9 1.8 %collective-permute-start.25 = (bf16[256,256]{1,0:T(8,128)(2,1)S(1)}, bf16[256,256]{1,0:T(8,128)(2,1)S(1)}, u32[]{:S(2)}, u32[]{:S(2)}) collective-permute-start(bf16[256,256]{1,0:T(8,128)(2,1)S(1)} %get-tuple-element.70), channel_id=1, source_target_pairs={{0,4},{1,3},{4,8},{5,1},{8,12},{9,5},{12,14},{13,9},{14,10},{15,13... | collective-permute-start | bytes 393224 | tf_op jit(solution)/shard_map/ppermute | solution.py:56
  37.5 2.1 %collective-permute-start.17 = (bf16[256,256]{1,0:T(8,128)(2,1)S(1)}, bf16[256,256]{1,0:T(8,128)(2,1)S(1)}, u32[]{:S(2)}, u32[]{:S(2)}) collective-permute-start(bf16[256,256]{1,0:T(8,128)(2,1)S(1)} %add_convert_fusion.9), channel_id=1, source_target_pairs={{0,4},{1,3},{4,8},{5,1},{8,12},{9,5},{12,14},{13,9},{14,10},{15,13... | collective-permute-start | bytes 393224 | tf_op jit(solution)/shard_map/ppermute | solution.py:56
  39.6 1.5 %collective-permute-done.20 = bf16[256,256]{1,0:T(8,128)(2,1)S(1)} collective-permute-done((bf16[256,256]{1,0:T(8,128)(2,1)S(1)}, bf16[256,256]{1,0:T(8,128)(2,1)S(1)}, u32[]{:S(2)}, u32[]{:S(2)}) %collective-permute-start.20) | collective-permute-done | bytes 131104 | tf_op jit(solution)/shard_map/ppermute | solution.py:56
  41.2 2.0 %collective-permute-start.26 = (bf16[256,256]{1,0:T(8,128)(2,1)S(1)}, bf16[256,256]{1,0:T(8,128)(2,1)S(1)}, u32[]{:S(2)}, u32[]{:S(2)}) collective-permute-start(bf16[256,256]{1,0:T(8,128)(2,1)S(1)} %add_convert_fusion.3), channel_id=1, source_target_pairs={{0,4},{1,3},{4,8},{5,1},{8,12},{9,5},{12,14},{13,9},{14,10},{15,13... | collective-permute-start | bytes 393224 | tf_op jit(solution)/shard_map/ppermute | solution.py:56
  44.0 1.9 %collective-permute-start.18 = (bf16[256,256]{1,0:T(8,128)(2,1)S(1)}, bf16[256,256]{1,0:T(8,128)(2,1)S(1)}, u32[]{:S(2)}, u32[]{:S(2)}) collective-permute-start(bf16[256,256]{1,0:T(8,128)(2,1)S(1)} %add_convert_fusion.8), channel_id=1, source_target_pairs={{0,4},{1,3},{4,8},{5,1},{8,12},{9,5},{12,14},{13,9},{14,10},{15,13... | collective-permute-start | bytes 393224 | tf_op jit(solution)/shard_map/ppermute | solution.py:56
  47.2 1.6 %collective-permute-start.27 = (bf16[256,256]{1,0:T(8,128)(2,1)S(1)}, bf16[256,256]{1,0:T(8,128)(2,1)S(1)}, u32[]{:S(2)}, u32[]{:S(2)}) collective-permute-start(bf16[256,256]{1,0:T(8,128)(2,1)S(1)} %add_convert_fusion.2), channel_id=1, source_target_pairs={{0,4},{1,3},{4,8},{5,1},{8,12},{9,5},{12,14},{13,9},{14,10},{15,13... | collective-permute-start | bytes 393224 | tf_op jit(solution)/shard_map/ppermute | solution.py:56
  49.7 1.4 %collective-permute-start.19 = (bf16[256,256]{1,0:T(8,128)(2,1)S(1)}, bf16[256,256]{1,0:T(8,128)(2,1)S(1)}, u32[]{:S(2)}, u32[]{:S(2)}) collective-permute-start(bf16[256,256]{1,0:T(8,128)(2,1)S(1)} %add_convert_fusion.7), channel_id=1, source_target_pairs={{0,4},{1,3},{4,8},{5,1},{8,12},{9,5},{12,14},{13,9},{14,10},{15,13... | collective-permute-start | bytes 393224 | tf_op jit(solution)/shard_map/ppermute | solution.py:56
  53.1 2.0 %collective-permute-done.19 = bf16[256,256]{1,0:T(8,128)(2,1)S(1)} collective-permute-done((bf16[256,256]{1,0:T(8,128)(2,1)S(1)}, bf16[256,256]{1,0:T(8,128)(2,1)S(1)}, u32[]{:S(2)}, u32[]{:S(2)}) %collective-permute-start.19) | collective-permute-done | bytes 131104 | tf_op jit(solution)/shard_map/ppermute | solution.py:56
  55.1 1.6 %collective-permute-start.34 = (bf16[256,256]{1,0:T(8,128)(2,1)S(1)}, bf16[256,256]{1,0:T(8,128)(2,1)S(1)}, u32[]{:S(2)}, u32[]{:S(2)}) collective-permute-start(bf16[256,256]{1,0:T(8,128)(2,1)S(1)} %multiply_convert_fusion.refs_1_), channel_id=1, source_target_pairs={{0,4},{1,3},{4,8},{5,1},{8,12},{9,5},{12,14},{13,9},{14,10},{15,13... | collective-permute-start | bytes 393224 | tf_op jit(solution)/shard_map/ppermute | solution.py:56
  57.3 1.5 %collective-permute-start.39 = (bf16[256,256]{1,0:T(8,128)(2,1)S(1)}, bf16[256,256]{1,0:T(8,128)(2,1)S(1)}, u32[]{:S(2)}, u32[]{:S(2)}) collective-permute-start(bf16[256,256]{1,0:T(8,128)(2,1)S(1)} %multiply_convert_fusion.refs_1_), channel_id=1, source_target_pairs={{0,2},{1,5},{4,0},{5,9},{8,4},{9,13},{12,8},{13,15},{14,12},{15,11... | collective-permute-start | bytes 393224 | tf_op jit(solution)/shard_map/ppermute | solution.py:56
  59.4 1.9 %collective-permute-done.34.refs_3_ = bf16[256,256]{1,0:T(8,128)(2,1)S(1)} collective-permute-done((bf16[256,256]{1,0:T(8,128)(2,1)S(1)}, bf16[256,256]{1,0:T(8,128)(2,1)S(1)}, u32[]{:S(2)}, u32[]{:S(2)}) %collective-permute-start.34) | collective-permute-done | bytes 131104 | tf_op jit(solution)/shard_map/ppermute | solution.py:56
  61.2 1.6 %collective-permute-start.35 = (bf16[256,256]{1,0:T(8,128)(2,1)S(1)}, bf16[256,256]{1,0:T(8,128)(2,1)S(1)}, u32[]{:S(2)}, u32[]{:S(2)}) collective-permute-start(bf16[256,256]{1,0:T(8,128)(2,1)S(1)} %collective-permute-done.34.refs_3_), channel_id=1, source_target_pairs={{0,4},{1,3},{4,8},{5,1},{8,12},{9,5},{12,14},{13,9},{14,10},{15,13... | collective-permute-start | bytes 393224 | tf_op jit(solution)/shard_map/ppermute | solution.py:56
  67.1 1.9 %collective-permute-start.36 = (bf16[256,256]{1,0:T(8,128)(2,1)S(1)}, bf16[256,256]{1,0:T(8,128)(2,1)S(1)}, u32[]{:S(2)}, u32[]{:S(2)}) collective-permute-start(bf16[256,256]{1,0:T(8,128)(2,1)S(1)} %collective-permute-done.35.refs_1_), channel_id=1, source_target_pairs={{0,4},{1,3},{4,8},{5,1},{8,12},{9,5},{12,14},{13,9},{14,10},{15,13... | collective-permute-start | bytes 393224 | tf_op jit(solution)/shard_map/ppermute | solution.py:56
  69.7 2.2 %collective-permute-done.41.refs_3_ = bf16[256,256]{1,0:T(8,128)(2,1)S(1)} collective-permute-done((bf16[256,256]{1,0:T(8,128)(2,1)S(1)}, bf16[256,256]{1,0:T(8,128)(2,1)S(1)}, u32[]{:S(2)}, u32[]{:S(2)}) %collective-permute-start.41) | collective-permute-done | bytes 131104 | tf_op jit(solution)/shard_map/ppermute | solution.py:56
  72.2 1.7 %collective-permute-start.42 = (bf16[256,256]{1,0:T(8,128)(2,1)S(1)}, bf16[256,256]{1,0:T(8,128)(2,1)S(1)}, u32[]{:S(2)}, u32[]{:S(2)}) collective-permute-start(bf16[256,256]{1,0:T(8,128)(2,1)S(1)} %collective-permute-done.40.refs_0_), channel_id=1, source_target_pairs={{0,4},{1,3},{4,8},{5,1},{8,12},{9,5},{12,14},{13,9},{14,10},{15,13... | collective-permute-start | bytes 393224 | tf_op jit(solution)/shard_map/ppermute | solution.py:56
  73.9 1.8 %collective-permute-start.37 = (bf16[256,256]{1,0:T(8,128)(2,1)S(1)}, bf16[256,256]{1,0:T(8,128)(2,1)S(1)}, u32[]{:S(2)}, u32[]{:S(2)}) collective-permute-start(bf16[256,256]{1,0:T(8,128)(2,1)S(1)} %collective-permute-done.36.refs_5_), channel_id=1, source_target_pairs={{0,4},{1,3},{4,8},{5,1},{8,12},{9,5},{12,14},{13,9},{14,10},{15,13... | collective-permute-start | bytes 393224 | tf_op jit(solution)/shard_map/ppermute | solution.py:56
  77.2 1.3 %shard_map.101 = (f32[4,256,256]{2,1,0:T(8,128)S(1)}, f32[2,256,256]{2,1,0:T(8,128)S(1)}) custom-call(s32[9]{0:T(128)S(1)} %stack.39.starts, bf16[256,256]{1,0:T(8,128)(2,1)S(1)} %collective-permute-done.40.refs_0_, bf16[256,256]{1,0:T(8,128)(2,1)S(1)} %collective-permute-done.35.refs_1_, bf16[256,256]{1,0:T(8,128)(2,1)S(1)} %collective-permute-done.31.refs_2_, ...), custom_call_target="tpu_custom_call" | custom-call | flops 268435456 | bytes 1024 | tf_op jit(solution)/shard_map/pallas_call | solution.py:69
  78.9 1.8 %collective-permute-done.33.refs_0_ = bf16[256,256]{1,0:T(8,128)(2,1)S(1)} collective-permute-done((bf16[256,256]{1,0:T(8,128)(2,1)S(1)}, bf16[256,256]{1,0:T(8,128)(2,1)S(1)}, u32[]{:S(2)}, u32[]{:S(2)}) %collective-permute-start.33) | collective-permute-done | bytes 131104 | tf_op jit(solution)/shard_map/ppermute | solution.py:56
  81.3 1.6 %shard_map.102 = (f32[512,128]{1,0:T(8,128)S(1)}, f32[1,128,2048]{2,1,0:T(8,128)}) custom-call(s32[9]{0:T(128)S(1)} %stack.39.starts, bf16[256,256]{1,0:T(8,128)(2,1)S(1)} %collective-permute-done.33.refs_0_, bf16[256,256]{1,0:T(8,128)(2,1)S(1)} %collective-permute-done.37.refs_1_, bf16[256,2048]{1,0:T(8,128)(2,1)S(1)} %pad_maximum_fusion.stacked.refs_6_.refs_8_.refs_2_, ...), custom_call_target="tpu_custom_call" | custom-call | bytes 1024 | tf_op jit(solution)/shard_map/pallas_call | solution.py:69
  83.6 2.7 %shard_map.104 = (f32[1,2048,128]{2,1,0:T(8,128)}, f32[1,128]{1,0:T(1,128)}, f32[128,1024]{1,0:T(8,128)}) custom-call(s32[9]{0:T(128)S(1)} %stack.39.starts, bf16[2048,512]{1,0:T(8,128)(2,1)S(1)} %shard_map.99.turned, f32[512,128]{1,0:T(8,128)S(1)} %get-tuple-element.66.preact, f32[512,128]{1,0:T(8,128)S(1)} %get-tuple-element.83.back_own, ...), custom_call_target="tpu_custom_call" | custom-call | flops 268435456 | bytes 1024 | tf_op jit(solution)/shard_map/pallas_call | solution.py:69
  (95 shorter events, 27.3 us)
Async XLA Ops:
  1.7 6.8 %collective-permute-start.5 = (bf16[256,256]{1,0:T(8,128)(2,1)S(1)}, bf16[256,256]{1,0:T(8,128)(2,1)S(1)}, u32[]{:S(2)}, u32[]{:S(2)}) collective-permute-start(bf16[256,256]{1,0:T(8,128)(2,1)S(1)} %get-tuple-element.48.shard.refs_1_), channel_id=1, source_target_pairs={{0,4},{1,3},{4,8},{5,1},{8,12},{9,5},{12,14},{13,9},{14,10},{15,13... | collective-permute-start | bytes 393224 | tf_op jit(solution)/shard_map/ppermute | solution.py:56
  4.8 6.3 %collective-permute-start.1 = (bf16[256,256]{1,0:T(8,128)(2,1)S(1)}, bf16[256,256]{1,0:T(8,128)(2,1)S(1)}, u32[]{:S(2)}, u32[]{:S(2)}) collective-permute-start(bf16[256,256]{1,0:T(8,128)(2,1)S(1)} %get-tuple-element.47.shard.refs_0_), channel_id=1, source_target_pairs={{0,2},{1,5},{4,0},{5,9},{8,4},{9,13},{12,8},{13,15},{14,12},{15,11... | collective-permute-start | bytes 393224 | tf_op jit(solution)/shard_map/ppermute | solution.py:56
  5.5 6.0 %collective-permute-start = (bf16[256,256]{1,0:T(8,128)(2,1)S(1)}, bf16[256,256]{1,0:T(8,128)(2,1)S(1)}, u32[]{:S(2)}, u32[]{:S(2)}) collective-permute-start(bf16[256,256]{1,0:T(8,128)(2,1)S(1)} %get-tuple-element.47.shard.refs_0_), channel_id=1, source_target_pairs={{0,4},{1,3},{4,8},{5,1},{8,12},{9,5},{12,14},{13,9},{14,10},{15,13... | collective-permute-start | bytes 393224 | tf_op jit(solution)/shard_map/ppermute | solution.py:56
  8.5 6.2 %collective-permute-start.6 = (bf16[256,256]{1,0:T(8,128)(2,1)S(1)}, bf16[256,256]{1,0:T(8,128)(2,1)S(1)}, u32[]{:S(2)}, u32[]{:S(2)}) collective-permute-start(bf16[256,256]{1,0:T(8,128)(2,1)S(1)} %collective-permute-done.5.refs_3_.refs_1_), channel_id=1, source_target_pairs={{0,4},{1,3},{4,8},{5,1},{8,12},{9,5},{12,14},{13,9},{14,10},{15,13... | collective-permute-start | bytes 393224 | tf_op jit(solution)/shard_map/ppermute | solution.py:56
  11.1 5.8 %collective-permute-start.2 = (bf16[256,256]{1,0:T(8,128)(2,1)S(1)}, bf16[256,256]{1,0:T(8,128)(2,1)S(1)}, u32[]{:S(2)}, u32[]{:S(2)}) collective-permute-start(bf16[256,256]{1,0:T(8,128)(2,1)S(1)} %collective-permute-done.1.refs_4_.refs_2_), channel_id=1, source_target_pairs={{0,2},{1,5},{4,0},{5,9},{8,4},{9,13},{12,8},{13,15},{14,12},{15,11... | collective-permute-start | bytes 393224 | tf_op jit(solution)/shard_map/ppermute | solution.py:56
  11.5 12.0 %collective-permute-start.14 = (bf16[128,1024]{1,0:T(8,128)(2,1)}, bf16[128,1024]{1,0:T(8,128)(2,1)S(1)}, u32[]{:S(2)}, u32[]{:S(2)}) collective-permute-start(bf16[128,1024]{1,0:T(8,128)(2,1)} %param.11), channel_id=1, source_target_pairs={{0,1},{1,0},{2,3},{3,2},{4,5},{5,4},{6,7},{7,6},{8,9},{9,8},{10,11... | collective-permute-start | bytes 786440 | tf_op jit(solution)/shard_map/ppermute | solution.py:28
  11.5 6.3 %collective-permute-start.10 = (bf16[256,256]{1,0:T(8,128)(2,1)S(1)}, bf16[256,256]{1,0:T(8,128)(2,1)S(1)}, u32[]{:S(2)}, u32[]{:S(2)}) collective-permute-start(bf16[256,256]{1,0:T(8,128)(2,1)S(1)} %collective-permute-done.refs_2_.refs_0_), channel_id=1, source_target_pairs={{0,4},{1,3},{4,8},{5,1},{8,12},{9,5},{12,14},{13,9},{14,10},{15,13... | collective-permute-start | bytes 393224 | tf_op jit(solution)/shard_map/ppermute | solution.py:56
  14.0 6.4 %collective-permute-start.11 = (bf16[256,256]{1,0:T(8,128)(2,1)S(1)}, bf16[256,256]{1,0:T(8,128)(2,1)S(1)}, u32[]{:S(2)}, u32[]{:S(2)}) collective-permute-start(bf16[256,256]{1,0:T(8,128)(2,1)S(1)} %collective-permute-done.9.refs_5_.refs_3_), channel_id=1, source_target_pairs={{0,2},{1,5},{4,0},{5,9},{8,4},{9,13},{12,8},{13,15},{14,12},{15,11... | collective-permute-start | bytes 393224 | tf_op jit(solution)/shard_map/ppermute | solution.py:56
  14.7 6.0 %collective-permute-start.7 = (bf16[256,256]{1,0:T(8,128)(2,1)S(1)}, bf16[256,256]{1,0:T(8,128)(2,1)S(1)}, u32[]{:S(2)}, u32[]{:S(2)}) collective-permute-start(bf16[256,256]{1,0:T(8,128)(2,1)S(1)} %collective-permute-done.6.refs_7_.refs_5_), channel_id=1, source_target_pairs={{0,4},{1,3},{4,8},{5,1},{8,12},{9,5},{12,14},{13,9},{14,10},{15,13... | collective-permute-start | bytes 393224 | tf_op jit(solution)/shard_map/ppermute | solution.py:56
  16.9 6.4 %collective-permute-start.3 = (bf16[256,256]{1,0:T(8,128)(2,1)S(1)}, bf16[256,256]{1,0:T(8,128)(2,1)S(1)}, u32[]{:S(2)}, u32[]{:S(2)}) collective-permute-start(bf16[256,256]{1,0:T(8,128)(2,1)S(1)} %collective-permute-done.2.refs_8_.refs_6_), channel_id=1, source_target_pairs={{0,2},{1,5},{4,0},{5,9},{8,4},{9,13},{12,8},{13,15},{14,12},{15,11... | collective-permute-start | bytes 393224 | tf_op jit(solution)/shard_map/ppermute | solution.py:56
  17.8 6.9 %collective-permute-start.12 = (bf16[256,256]{1,0:T(8,128)(2,1)S(1)}, bf16[256,256]{1,0:T(8,128)(2,1)S(1)}, u32[]{:S(2)}, u32[]{:S(2)}) collective-permute-start(bf16[256,256]{1,0:T(8,128)(2,1)S(1)} %collective-permute-done.10.refs_6_.refs_4_), channel_id=1, source_target_pairs={{0,4},{1,3},{4,8},{5,1},{8,12},{9,5},{12,14},{13,9},{14,10},{15,13... | collective-permute-start | bytes 393224 | tf_op jit(solution)/shard_map/ppermute | solution.py:56
  20.8 6.3 %collective-permute-start.8 = (bf16[256,256]{1,0:T(8,128)(2,1)S(1)}, bf16[256,256]{1,0:T(8,128)(2,1)S(1)}, u32[]{:S(2)}, u32[]{:S(2)}) collective-permute-start(bf16[256,256]{1,0:T(8,128)(2,1)S(1)} %collective-permute-done.7.refs_11_.refs_9_), channel_id=1, source_target_pairs={{0,4},{1,3},{4,8},{5,1},{8,12},{9,5},{12,14},{13,9},{14,10},{15,13... | collective-permute-start | bytes 393224 | tf_op jit(solution)/shard_map/ppermute | solution.py:56
  31.3 6.1 %collective-permute-start.21 = (bf16[256,256]{1,0:T(8,128)(2,1)S(1)}, bf16[256,256]{1,0:T(8,128)(2,1)S(1)}, u32[]{:S(2)}, u32[]{:S(2)}) collective-permute-start(bf16[256,256]{1,0:T(8,128)(2,1)S(1)} %get-tuple-element.60), channel_id=1, source_target_pairs={{0,2},{1,5},{4,0},{5,9},{8,4},{9,13},{12,8},{13,15},{14,12},{15,11... | collective-permute-start | bytes 393224 | tf_op jit(solution)/shard_map/ppermute | solution.py:56
  31.5 5.9 %collective-permute-start.16 = (bf16[256,256]{1,0:T(8,128)(2,1)S(1)}, bf16[256,256]{1,0:T(8,128)(2,1)S(1)}, u32[]{:S(2)}, u32[]{:S(2)}) collective-permute-start(bf16[256,256]{1,0:T(8,128)(2,1)S(1)} %get-tuple-element.56), channel_id=1, source_target_pairs={{0,4},{1,3},{4,8},{5,1},{8,12},{9,5},{12,14},{13,9},{14,10},{15,13... | collective-permute-start | bytes 393224 | tf_op jit(solution)/shard_map/ppermute | solution.py:56
  34.6 6.4 %collective-permute-start.20 = (bf16[256,256]{1,0:T(8,128)(2,1)S(1)}, bf16[256,256]{1,0:T(8,128)(2,1)S(1)}, u32[]{:S(2)}, u32[]{:S(2)}) collective-permute-start(bf16[256,256]{1,0:T(8,128)(2,1)S(1)} %get-tuple-element.59), channel_id=1, source_target_pairs={{0,2},{1,5},{4,0},{5,9},{8,4},{9,13},{12,8},{13,15},{14,12},{15,11... | collective-permute-start | bytes 393224 | tf_op jit(solution)/shard_map/ppermute | solution.py:56
  34.9 6.3 %collective-permute-start.25 = (bf16[256,256]{1,0:T(8,128)(2,1)S(1)}, bf16[256,256]{1,0:T(8,128)(2,1)S(1)}, u32[]{:S(2)}, u32[]{:S(2)}) collective-permute-start(bf16[256,256]{1,0:T(8,128)(2,1)S(1)} %get-tuple-element.70), channel_id=1, source_target_pairs={{0,4},{1,3},{4,8},{5,1},{8,12},{9,5},{12,14},{13,9},{14,10},{15,13... | collective-permute-start | bytes 393224 | tf_op jit(solution)/shard_map/ppermute | solution.py:56
  37.4 6.4 %collective-permute-start.23 = (bf16[256,256]{1,0:T(8,128)(2,1)S(1)}, bf16[256,256]{1,0:T(8,128)(2,1)S(1)}, u32[]{:S(2)}, u32[]{:S(2)}) collective-permute-start(bf16[256,256]{1,0:T(8,128)(2,1)S(1)} %add_convert_fusion.4), channel_id=1, source_target_pairs={{0,2},{1,5},{4,0},{5,9},{8,4},{9,13},{12,8},{13,15},{14,12},{15,11... | collective-permute-start | bytes 393224 | tf_op jit(solution)/shard_map/ppermute | solution.py:56
  37.5 6.5 %collective-permute-start.17 = (bf16[256,256]{1,0:T(8,128)(2,1)S(1)}, bf16[256,256]{1,0:T(8,128)(2,1)S(1)}, u32[]{:S(2)}, u32[]{:S(2)}) collective-permute-start(bf16[256,256]{1,0:T(8,128)(2,1)S(1)} %add_convert_fusion.9), channel_id=1, source_target_pairs={{0,4},{1,3},{4,8},{5,1},{8,12},{9,5},{12,14},{13,9},{14,10},{15,13... | collective-permute-start | bytes 393224 | tf_op jit(solution)/shard_map/ppermute | solution.py:56
  41.2 6.0 %collective-permute-start.26 = (bf16[256,256]{1,0:T(8,128)(2,1)S(1)}, bf16[256,256]{1,0:T(8,128)(2,1)S(1)}, u32[]{:S(2)}, u32[]{:S(2)}) collective-permute-start(bf16[256,256]{1,0:T(8,128)(2,1)S(1)} %add_convert_fusion.3), channel_id=1, source_target_pairs={{0,4},{1,3},{4,8},{5,1},{8,12},{9,5},{12,14},{13,9},{14,10},{15,13... | collective-permute-start | bytes 393224 | tf_op jit(solution)/shard_map/ppermute | solution.py:56
  43.8 7.3 %collective-permute-start.28 = (bf16[256,256]{1,0:T(8,128)(2,1)S(1)}, bf16[256,256]{1,0:T(8,128)(2,1)S(1)}, u32[]{:S(2)}, u32[]{:S(2)}) collective-permute-start(bf16[256,256]{1,0:T(8,128)(2,1)S(1)} %add_convert_fusion.1), channel_id=1, source_target_pairs={{0,2},{1,5},{4,0},{5,9},{8,4},{9,13},{12,8},{13,15},{14,12},{15,11... | collective-permute-start | bytes 393224 | tf_op jit(solution)/shard_map/ppermute | solution.py:56
  46.6 6.5 %collective-permute-start.24 = (bf16[256,256]{1,0:T(8,128)(2,1)S(1)}, bf16[256,256]{1,0:T(8,128)(2,1)S(1)}, u32[]{:S(2)}, u32[]{:S(2)}) collective-permute-start(bf16[256,256]{1,0:T(8,128)(2,1)S(1)} %add_convert_fusion.5), channel_id=1, source_target_pairs={{0,2},{1,5},{4,0},{5,9},{8,4},{9,13},{12,8},{13,15},{14,12},{15,11... | collective-permute-start | bytes 393224 | tf_op jit(solution)/shard_map/ppermute | solution.py:56
  47.2 9.5 %collective-permute-start.27 = (bf16[256,256]{1,0:T(8,128)(2,1)S(1)}, bf16[256,256]{1,0:T(8,128)(2,1)S(1)}, u32[]{:S(2)}, u32[]{:S(2)}) collective-permute-start(bf16[256,256]{1,0:T(8,128)(2,1)S(1)} %add_convert_fusion.2), channel_id=1, source_target_pairs={{0,4},{1,3},{4,8},{5,1},{8,12},{9,5},{12,14},{13,9},{14,10},{15,13... | collective-permute-start | bytes 393224 | tf_op jit(solution)/shard_map/ppermute | solution.py:56
  55.1 6.1 %collective-permute-start.34 = (bf16[256,256]{1,0:T(8,128)(2,1)S(1)}, bf16[256,256]{1,0:T(8,128)(2,1)S(1)}, u32[]{:S(2)}, u32[]{:S(2)}) collective-permute-start(bf16[256,256]{1,0:T(8,128)(2,1)S(1)} %multiply_convert_fusion.refs_1_), channel_id=1, source_target_pairs={{0,4},{1,3},{4,8},{5,1},{8,12},{9,5},{12,14},{13,9},{14,10},{15,13... | collective-permute-start | bytes 393224 | tf_op jit(solution)/shard_map/ppermute | solution.py:56
  56.8 6.5 %collective-permute-start.30 = (bf16[256,256]{1,0:T(8,128)(2,1)S(1)}, bf16[256,256]{1,0:T(8,128)(2,1)S(1)}, u32[]{:S(2)}, u32[]{:S(2)}) collective-permute-start(bf16[256,256]{1,0:T(8,128)(2,1)S(1)} %fusion.1.refs_0_), channel_id=1, source_target_pairs={{0,2},{1,5},{4,0},{5,9},{8,4},{9,13},{12,8},{13,15},{14,12},{15,11... | collective-permute-start | bytes 393224 | tf_op jit(solution)/shard_map/ppermute | solution.py:56
  57.3 7.8 %collective-permute-start.39 = (bf16[256,256]{1,0:T(8,128)(2,1)S(1)}, bf16[256,256]{1,0:T(8,128)(2,1)S(1)}, u32[]{:S(2)}, u32[]{:S(2)}) collective-permute-start(bf16[256,256]{1,0:T(8,128)(2,1)S(1)} %multiply_convert_fusion.refs_1_), channel_id=1, source_target_pairs={{0,2},{1,5},{4,0},{5,9},{8,4},{9,13},{12,8},{13,15},{14,12},{15,11... | collective-permute-start | bytes 393224 | tf_op jit(solution)/shard_map/ppermute | solution.py:56
  58.8 7.1 %collective-permute-start.38 = (bf16[256,256]{1,0:T(8,128)(2,1)S(1)}, bf16[256,256]{1,0:T(8,128)(2,1)S(1)}, u32[]{:S(2)}, u32[]{:S(2)}) collective-permute-start(bf16[256,256]{1,0:T(8,128)(2,1)S(1)} %fusion.1.refs_0_), channel_id=1, source_target_pairs={{0,4},{1,3},{4,8},{5,1},{8,12},{9,5},{12,14},{13,9},{14,10},{15,13... | collective-permute-start | bytes 393224 | tf_op jit(solution)/shard_map/ppermute | solution.py:56
  61.2 5.9 %collective-permute-start.35 = (bf16[256,256]{1,0:T(8,128)(2,1)S(1)}, bf16[256,256]{1,0:T(8,128)(2,1)S(1)}, u32[]{:S(2)}, u32[]{:S(2)}) collective-permute-start(bf16[256,256]{1,0:T(8,128)(2,1)S(1)} %collective-permute-done.34.refs_3_), channel_id=1, source_target_pairs={{0,4},{1,3},{4,8},{5,1},{8,12},{9,5},{12,14},{13,9},{14,10},{15,13... | collective-permute-start | bytes 393224 | tf_op jit(solution)/shard_map/ppermute | solution.py:56
  63.2 6.1 %collective-permute-start.31 = (bf16[256,256]{1,0:T(8,128)(2,1)S(1)}, bf16[256,256]{1,0:T(8,128)(2,1)S(1)}, u32[]{:S(2)}, u32[]{:S(2)}) collective-permute-start(bf16[256,256]{1,0:T(8,128)(2,1)S(1)} %collective-permute-done.30.refs_4_), channel_id=1, source_target_pairs={{0,2},{1,5},{4,0},{5,9},{8,4},{9,13},{12,8},{13,15},{14,12},{15,11... | collective-permute-start | bytes 393224 | tf_op jit(solution)/shard_map/ppermute | solution.py:56
  65.1 6.8 %collective-permute-start.41 = (bf16[256,256]{1,0:T(8,128)(2,1)S(1)}, bf16[256,256]{1,0:T(8,128)(2,1)S(1)}, u32[]{:S(2)}, u32[]{:S(2)}) collective-permute-start(bf16[256,256]{1,0:T(8,128)(2,1)S(1)} %collective-permute-done.39.refs_5_), channel_id=1, source_target_pairs={{0,2},{1,5},{4,0},{5,9},{8,4},{9,13},{12,8},{13,15},{14,12},{15,11... | collective-permute-start | bytes 393224 | tf_op jit(solution)/shard_map/ppermute | solution.py:56
  66.0 6.2 %collective-permute-start.40 = (bf16[256,256]{1,0:T(8,128)(2,1)S(1)}, bf16[256,256]{1,0:T(8,128)(2,1)S(1)}, u32[]{:S(2)}, u32[]{:S(2)}) collective-permute-start(bf16[256,256]{1,0:T(8,128)(2,1)S(1)} %collective-permute-done.38.refs_2_), channel_id=1, source_target_pairs={{0,4},{1,3},{4,8},{5,1},{8,12},{9,5},{12,14},{13,9},{14,10},{15,13... | collective-permute-start | bytes 393224 | tf_op jit(solution)/shard_map/ppermute | solution.py:56
  67.1 6.8 %collective-permute-start.36 = (bf16[256,256]{1,0:T(8,128)(2,1)S(1)}, bf16[256,256]{1,0:T(8,128)(2,1)S(1)}, u32[]{:S(2)}, u32[]{:S(2)}) collective-permute-start(bf16[256,256]{1,0:T(8,128)(2,1)S(1)} %collective-permute-done.35.refs_1_), channel_id=1, source_target_pairs={{0,4},{1,3},{4,8},{5,1},{8,12},{9,5},{12,14},{13,9},{14,10},{15,13... | collective-permute-start | bytes 393224 | tf_op jit(solution)/shard_map/ppermute | solution.py:56
  69.3 6.4 %collective-permute-start.32 = (bf16[256,256]{1,0:T(8,128)(2,1)S(1)}, bf16[256,256]{1,0:T(8,128)(2,1)S(1)}, u32[]{:S(2)}, u32[]{:S(2)}) collective-permute-start(bf16[256,256]{1,0:T(8,128)(2,1)S(1)} %collective-permute-done.31.refs_2_), channel_id=1, source_target_pairs={{0,2},{1,5},{4,0},{5,9},{8,4},{9,13},{12,8},{13,15},{14,12},{15,11... | collective-permute-start | bytes 393224 | tf_op jit(solution)/shard_map/ppermute | solution.py:56
  (17 other events, 141.4 us)
